TPU v7x, 32 devices: a whole 2x2x4 slice. The times are simulated.
32 devices in a mesh: groups: 2 (over y), cells: 4 (over z), slots: 2 (over x), mp: 2 (over core).
Axes of the slice: x: 2, y: 2, z: 4, core: 2. Of those that a mesh axis runs over, the one named last changes fastest.
Arguments:
- obs_feat: bfloat16 [16384, 768], P(('groups', 'cells', 'slots', 'mp')), parts along dimension 0, may hold values from -6 to 6
- obs_cell: int32 [16384], P(('groups', 'cells', 'slots', 'mp')), parts along dimension 0, may hold values from 0 to 1023, as said below
- obs_slot: int32 [16384], P(('groups', 'cells', 'slots', 'mp')), parts along dimension 0, may hold values from 0 to 3
- obs_count: int32 [32], P(('groups', 'cells', 'slots', 'mp')), parts along dimension 0, may hold values from 256 to 512
- time_embed: bfloat16 [8, 768], replicated, may hold values from -6 to 6
- w_qkv: bfloat16 [768, 3, 768], P('cells', None, 'mp'), may hold values from -0.21875 to 0.21875
- w_out: bfloat16 [768, 768], P('mp', 'cells'), may hold values from -0.21875 to 0.21875
- w_gate_up: bfloat16 [768, 2, 3072], P('cells', None, 'mp'), may hold values from -0.21875 to 0.21875
- w_down: bfloat16 [3072, 768], P('mp', 'cells'), may hold values from -0.109375 to 0.109375
Outputs:
- mixed: bfloat16 [2048, 8, 768], P(('groups', 'cells', 'slots', 'mp')), parts along dimension 0
There are 2 independent parts, one for each index of `groups`. A program takes and returns all parts, laid end to end along the dimension named above; an argument that names none is the same for every part. Nothing has to cross between parts.
Inputs may be any that keep to these rules, and one draw needn't show every extreme that they name: `obs_cell`: call the block of cell g the pair (g // 256, (g // 64) % 2). Among the live rows of one device at most 192 lie in any one block, and one block, the same for all devices of a part, gets exactly 192 live rows from every device.
All inputs are finite; a program needn't handle non-finite values.
Results may differ from a plain program's by a relative error of at most 0.0057.
Values may be sent and summed in bfloat16 or wider, within the bound.
No kernel may reach another device: no remote copies, remote signals or barrier semaphores. Data moves between devices by JAX's collectives and lax.ppermute only.
A program may use at most 128 MiB of HBM per device.

v0:
```python
import jax
import jax.numpy as jnp
from jax import lax
from jax.sharding import PartitionSpec as P

HD = 64
TSTEPS = 8
CB = 128


EPS = 1e-06


def rms_scale(values):
    return values * lax.rsqrt(jnp.mean(values * values, axis=-1, keepdims=True) + EPS)


def on_device(obs_feat, obs_cell, obs_slot, obs_count, time_embed, w_qkv, w_out, w_gate_up, w_down):
    n_cells = lax.axis_size("cells")
    n_slots = lax.axis_size("slots")
    n_mp = lax.axis_size("mp")
    n_owners = n_cells * n_mp
    obs_rows = obs_feat.shape[0]
    feat_width = obs_feat.shape[1]
    capacity = 3 * obs_rows // n_owners
    quarter = CB // n_slots
    slot_dev = TSTEPS // n_slots
    full_qkv, full_out, full_gate_up, full_down = (
        lax.all_gather(w_qkv, "cells", axis=0, tiled=True),
        lax.all_gather(w_out, "cells", axis=1, tiled=True),
        lax.all_gather(w_gate_up, "cells", axis=0, tiled=True),
        lax.all_gather(w_down, "cells", axis=1, tiled=True),
    )
    row_ids = jnp.arange(obs_rows, dtype=jnp.int32)
    valid_row = row_ids < obs_count[0]
    local_part = obs_cell % quarter
    mp_part = obs_cell // quarter % n_mp
    slot_part = obs_cell // (quarter * n_mp) % n_slots
    cell_part = obs_cell // (quarter * n_mp * n_slots)
    owner_idx = jnp.where(valid_row, cell_part * n_mp + mp_part, n_owners)
    local_idx = slot_part * quarter + local_part
    owner_hot = (owner_idx[:, None] == jnp.arange(n_owners, dtype=jnp.int32)[None, :]).astype(
        jnp.bfloat16
    )
    lower_tri = (row_ids[None, :] <= row_ids[:, None]).astype(jnp.bfloat16)
    running = jnp.dot(lower_tri, owner_hot, preferred_element_type=jnp.float32)
    slot_rank = jnp.sum(running * owner_hot.astype(jnp.float32), axis=1).astype(jnp.int32) - 1
    dest_slot = jnp.where(valid_row, owner_idx * capacity + slot_rank, n_owners * capacity)
    place_ids = jnp.arange(n_owners * capacity, dtype=jnp.int32)
    placement = (place_ids[:, None] == dest_slot[None, :]).astype(jnp.bfloat16)
    send_feat = jnp.dot(placement, obs_feat, preferred_element_type=jnp.float32).astype(
        jnp.bfloat16
    )
    side_cols = jnp.stack(
        [(local_idx + 1).astype(jnp.float32), obs_slot.astype(jnp.float32)], axis=1
    )
    side_sent = jnp.dot(placement.astype(jnp.float32), side_cols, precision=lax.Precision.HIGHEST)
    send_feat = send_feat.reshape(n_owners, capacity, feat_width)
    send_cell = (side_sent[:, 0] - 1.0).astype(jnp.bfloat16).reshape(n_owners, capacity)
    send_slot = side_sent[:, 1].astype(jnp.bfloat16).reshape(n_owners, capacity)
    recv_feat, recv_cell, recv_slot = (
        lax.all_to_all(send_feat, ("cells", "mp"), split_axis=0, concat_axis=0, tiled=True),
        lax.all_to_all(send_cell, ("cells", "mp"), split_axis=0, concat_axis=0, tiled=True),
        lax.all_to_all(send_slot, ("cells", "mp"), split_axis=0, concat_axis=0, tiled=True),
    )
    got_feat = recv_feat.reshape(-1, feat_width)
    got_cell = recv_cell.reshape(-1).astype(jnp.int32)
    got_slot = recv_slot.reshape(-1).astype(jnp.int32)
    position = jnp.where(got_cell >= 0, got_cell * slot_dev + got_slot, -1)
    onehot_tab = (jnp.arange(CB * slot_dev, dtype=jnp.int32)[:, None] == position[None, :]).astype(
        jnp.bfloat16
    )
    pooled_sum = jnp.dot(onehot_tab, got_feat, preferred_element_type=jnp.float32)
    cell_count = jnp.sum(onehot_tab.astype(jnp.float32), axis=1)
    pooled = pooled_sum / jnp.maximum(cell_count, 1.0)[:, None]
    slot_embed = lax.dynamic_slice_in_dim(
        time_embed, lax.axis_index("slots") * slot_dev, slot_dev, 0
    )
    tokens = (
        pooled.reshape(CB, slot_dev, feat_width) + slot_embed.astype(jnp.float32)[None]
    ).astype(jnp.bfloat16)
    token_grid = tokens.reshape(n_slots, quarter, slot_dev, feat_width)
    token_block = lax.all_to_all(token_grid, "slots", split_axis=0, concat_axis=2, tiled=True)
    item_count = token_block.shape[1]
    resid = token_block.reshape(item_count, TSTEPS, feat_width).astype(jnp.float32)
    normed = rms_scale(resid).astype(jnp.bfloat16)
    together = lax.all_gather(normed, "mp", axis=0, tiled=True)
    flat_rows = together.reshape(-1, feat_width)
    row_items = together.shape[0]
    head_count = full_qkv.shape[2] // HD
    projected = jnp.dot(
        flat_rows, full_qkv.reshape(feat_width, -1), preferred_element_type=jnp.float32
    )
    projected = projected.reshape(row_items, TSTEPS, 3, head_count, HD)
    queries = rms_scale(projected[:, :, 0]).astype(jnp.bfloat16)
    keys_att = rms_scale(projected[:, :, 1]).astype(jnp.bfloat16)
    values_att = projected[:, :, 2].astype(jnp.bfloat16)
    scores = jnp.einsum(
        "cthe,cshe->chts", queries, keys_att, preferred_element_type=jnp.float32
    ) * HD ** (-0.5)
    expo = jnp.exp(scores)
    attn_probs = (expo / jnp.sum(expo, axis=-1, keepdims=True)).astype(jnp.bfloat16)
    context = jnp.einsum(
        "chts,cshe->cthe", attn_probs, values_att, preferred_element_type=jnp.float32
    )
    context = context.astype(jnp.bfloat16).reshape(-1, head_count * HD)
    attn_out = jnp.dot(context, full_out, preferred_element_type=jnp.float32)
    gate_up = jnp.dot(
        flat_rows, full_gate_up.reshape(feat_width, -1), preferred_element_type=jnp.float32
    )
    gate_up = gate_up.reshape(flat_rows.shape[0], 2, -1)
    hidden = (jax.nn.silu(gate_up[:, 0]) * gate_up[:, 1]).astype(jnp.bfloat16)
    mlp_out = jnp.dot(hidden, full_down, preferred_element_type=jnp.float32)
    partial_value = (attn_out + mlp_out).reshape(row_items, TSTEPS, feat_width)
    summed = lax.psum_scatter(partial_value, "mp", scatter_dimension=0, tiled=True)
    mixed = (resid + summed).astype(jnp.bfloat16).reshape(1, item_count, TSTEPS, feat_width)
    return mixed.reshape(quarter, TSTEPS, feat_width)


def solution(mesh):
    placed = (
        P(("groups", "cells", "slots", "mp"), None),
        P(("groups", "cells", "slots", "mp")),
        P(("groups", "cells", "slots", "mp")),
        P(("groups", "cells", "slots", "mp")),
        P(),
        P("cells", None, "mp"),
        P("mp", "cells"),
        P("cells", None, "mp"),
        P("mp", "cells"),
    )
    return jax.shard_map(
        on_device,
        mesh=mesh,
        in_specs=placed,
        out_specs=P(("groups", "cells", "slots", "mp"), None, None),
        check_vma=False,
    )
```

profile of v0, /device:TPU:0, one launch (start us, length us, event | category | flops | bytes accessed | tf_op | source)
XLA Modules:
  0.0 320.4 jit_solution(1449691355339979950)
XLA Ops:
  7.3 0.7 fusion.43
  8.2 0.7 convert_element_type.125
  8.9 1.5 fusion.4
  10.5 0.7 convert_element_type.153
  11.1 6.3 %all-to-all-start = ((bf16[8,1,192]{2,1,0:T(2,128)(2,1)}), bf16[8,1,192]{2,1,0:T(2,128)(2,1)S(1)}, u32[]{:S(2)}, u32[]{:S(2)}) async-start(bf16[8,1,192]{2,1,0:T(2,128)(2,1)} %convert_element_type.153), calls=%async_computation | async-start | bytes 16384 | tf_op jit(solution)/shard_map/all_to_all | solution.py:63
  17.5 0.7 convert_element_type.154
  18.1 4.9 %all-to-all-done = bf16[8,1,192]{2,1,0:T(2,128)(2,1)S(1)} async-done(((bf16[8,1,192]{2,1,0:T(2,128)(2,1)}), bf16[8,1,192]{2,1,0:T(2,128)(2,1)S(1)}, u32[]{:S(2)}, u32[]{:S(2)}) %all-to-all-start) | async-done | bytes 3104 | tf_op jit(solution)/shard_map/all_to_all | solution.py:63
  23.1 3.3 %all-to-all-start.1 = ((bf16[8,1,192]{2,1,0:T(2,128)(2,1)}), bf16[8,1,192]{2,1,0:T(2,128)(2,1)S(1)}, u32[]{:S(2)}, u32[]{:S(2)}) async-start(bf16[8,1,192]{2,1,0:T(2,128)(2,1)} %convert_element_type.154), calls=%async_computation.1 | async-start | bytes 16384 | tf_op jit(solution)/shard_map/all_to_all | solution.py:64
  26.4 2.9 convolution_convert_fusion
  29.3 2.6 all-to-all-done.1
  31.9 3.7 %all-to-all-start.2 = ((bf16[8,192,768]{2,1,0:T(8,128)(2,1)}), bf16[8,192,768]{2,1,0:T(8,128)(2,1)S(1)}, u32[]{:S(2)}, u32[]{:S(2)}) async-start(bf16[8,192,768]{2,1,0:T(8,128)(2,1)} %bitcast.3), calls=%async_computation.2 | async-start | bytes 4718592 | tf_op jit(solution)/shard_map/all_to_all | solution.py:62
  35.7 0.7 all-gather.7.cloned.1.call-update
  36.6 0.4 convert_reduce_fusion
  37.0 81.7 %all-to-all-done.2 = bf16[8,192,768]{2,1,0:T(8,128)(2,1)S(1)} async-done(((bf16[8,192,768]{2,1,0:T(8,128)(2,1)}), bf16[8,192,768]{2,1,0:T(8,128)(2,1)S(1)}, u32[]{:S(2)}, u32[]{:S(2)}) %all-to-all-start.2) | async-done | bytes 2359328 | tf_op jit(solution)/shard_map/all_to_all | solution.py:62
  118.7 2.7 fusion.20
  121.4 1.8 reshape.145
  123.5 13.3 %all_to_all.26 = bf16[2,64,4,768]{3,2,1,0:T(4,128)(2,1)S(1)} all-to-all(bf16[2,64,4,768]{3,2,1,0:T(4,128)(2,1)S(1)} %add_convert_fusion), channel_id=1, replica_groups=mesh['groups'=2,'cells'=4,'slots'=2,'mp'=2] {'slots'}, dimensions={0} | all-to-all | bytes 1572864 | tf_op jit(solution)/shard_map/all_to_all | solution.py:83
  137.0 0.3 copy.71
  137.3 0.5 fusion.9
  137.9 1.0 fusion.13
  139.0 0.7 all-gather.9.cloned.1.call-update
  139.7 0.5 all-gather.11.cloned.1.call-update
  140.3 17.0 %all_gather.17 = bf16[384,768]{0,1:T(8,128)(2,1)} all-gather(bf16[384,192]{0,1:T(8,128)(2,1)S(1)} %copy-done.4), channel_id=1, replica_groups=mesh['groups'=2,'cells'=4,'slots'=2,'mp'=2] {'cells'}, dimensions={1}, use_global_device_ids=true | all-gather | bytes 737280 | tf_op jit(solution)/shard_map/all_gather | solution.py:30
  157.3 3.9 %copy.73 = bf16[768,3,384]{0,2,1:T(8,128)(2,1)} copy(bf16[768,3,384]{2,0,1:T(8,128)(2,1)} %all-gather.7.cloned.1.call-done) | data formatting | bytes 3538944 | tf_op jit(solution)/shard_map/all_gather | solution.py:29
  161.2 4.0 %fusion.11 = f32[128,8,3,6,64]{0,4,3,2,1:T(8,128)S(1)} fusion(bf16[3,6,64,768,1]{3,2,1,0,4:T(8,128)(2,1)} %bitcast.86, bf16[128,8,768]{2,0,1:T(8,128)(2,1)} %all-gather.5.cloned.1.call-done), kind=kOutput, calls=%fused_computation.23 | convolution fusion | flops 1811939328 | bytes 8060928 | tf_op jit(solution)/shard_map/dot_general | solution.py:91
  165.3 0.6 multiply_reduce_fusion
  165.8 0.5 multiply_convert_fusion
  166.4 1.0 copy-done.2
  167.4 1.8 copy.74
  169.2 1.8 copy.75
  170.9 4.5 %fusion.47 = f32[128,6,8,8]{2,3,1,0:T(8,128)} fusion(bf16[128,8,6,64]{3,1,2,0:T(8,128)(2,1)} %copy.74, bf16[128,8,6,64]{3,1,2,0:T(8,128)(2,1)} %copy.75), kind=kOutput, calls=%fused_computation.99 | convolution fusion | flops 6291456 | bytes 1769472 | tf_op jit(solution)/shard_map/cthe,cshe->chts/dot_general | solution.py:98
  175.4 2.4 copy.76
  177.9 1.7 copy.78
  179.6 1.5 fusion.22
  181.2 1.8 copy.77
  183.0 2.9 fusion.19
  185.8 2.0 copy.79
  187.8 3.1 reshape.147
  190.9 48.6 %all-gather.9.cloned.1.call-done = bf16[768,2,1536]{2,1,0:T(2,128)(2,1)} async-done(((bf16[192,2,1536]{2,1,0:T(2,128)(2,1)}), bf16[768,2,1536]{2,1,0:T(2,128)(2,1)}) %all-gather.9.cloned.1.call-update) | async-done | bytes 4718608 | tf_op jit(solution)/shard_map/all_gather | solution.py:31
  239.5 12.5 %copy.85 = bf16[768,2,1536]{0,2,1:T(8,128)(2,1)} copy(bf16[768,2,1536]{2,1,0:T(2,128)(2,1)} %all-gather.9.cloned.1.call-done) | data formatting | bytes 9437184 | tf_op jit(solution)/shard_map/reshape | solution.py:109
  252.0 10.5 %fusion.2 = f32[1024,2,1536]{2,0,1:T(8,128)} fusion(bf16[768,2,1536]{0,2,1:T(8,128)(2,1)} %copy.85, bf16[128,8,768]{2,0,1:T(8,128)(2,1)} %all-gather.5.cloned.1.call-done), kind=kOutput, calls=%fused_computation.4 | convolution fusion | flops 4831838208 | bytes 18874368 | tf_op jit(solution)/shard_map/dot_general | solution.py:108
  262.5 27.4 %all-gather.11.cloned.1.call-done = bf16[1536,768]{0,1:T(8,128)(2,1)} async-done(((bf16[1536,192]{0,1:T(8,128)(2,1)}), bf16[1536,768]{0,1:T(8,128)(2,1)}) %all-gather.11.cloned.1.call-update) | async-done | bytes 2359312 | tf_op jit(solution)/shard_map/all_gather | solution.py:32
  289.9 7.4 %fusion.7 = f32[1024,768]{1,0:T(8,128)S(1)} fusion(bf16[1536,768]{0,1:T(8,128)(2,1)} %all-gather.11.cloned.1.call-done, f32[1024,2,1536]{2,0,1:T(8,128)} %fusion.2), kind=kOutput, calls=%fused_computation.14 | convolution fusion | flops 2425356288 | bytes 18087936 | tf_op jit(solution)/shard_map/dot_general | solution.py:113
  297.3 1.0 add_bitcast_fusion
  298.3 2.6 copy.82
  301.0 9.9 %reduce-scatter.2.cloned.1.call-done = f32[64,8,768]{2,0,1:T(8,128)} async-done(((f32[128,8,768]{2,0,1:T(8,128)}), f32[64,8,768]{2,0,1:T(8,128)}) %reduce-scatter.2.cloned.1.call-update) | async-done | bytes 1572880 | tf_op jit(solution)/shard_map/reduce_scatter | solution.py:115
  310.9 1.7 fusion.14
  312.5 1.3 copy.83
  (34 shorter events, 1.4 us)
Async XLA Ops:
  6.5 19.9 %copy-start = (bf16[512,768]{1,0:T(8,128)(2,1)S(1)}, bf16[512,768]{1,0:T(8,128)(2,1)}, u32[]{:S(2)}) copy-start(bf16[512,768]{1,0:T(8,128)(2,1)} %param.9) | copy-start | bytes 2359300
  11.1 11.9 %all-to-all-start = ((bf16[8,1,192]{2,1,0:T(2,128)(2,1)}), bf16[8,1,192]{2,1,0:T(2,128)(2,1)S(1)}, u32[]{:S(2)}, u32[]{:S(2)}) async-start(bf16[8,1,192]{2,1,0:T(2,128)(2,1)} %convert_element_type.153), calls=%async_computation | async-start | bytes 16384 | tf_op jit(solution)/shard_map/all_to_all | solution.py:63
  23.1 8.9 %all-to-all-start.1 = ((bf16[8,1,192]{2,1,0:T(2,128)(2,1)}), bf16[8,1,192]{2,1,0:T(2,128)(2,1)S(1)}, u32[]{:S(2)}, u32[]{:S(2)}) async-start(bf16[8,1,192]{2,1,0:T(2,128)(2,1)} %convert_element_type.154), calls=%async_computation.1 | async-start | bytes 16384 | tf_op jit(solution)/shard_map/all_to_all | solution.py:64
  31.9 4.5 %copy-start.5 = (bf16[8,768]{1,0:T(8,128)(2,1)S(1)}, bf16[8,768]{1,0:T(8,128)(2,1)}, u32[]{:S(2)}) copy-start(bf16[8,768]{1,0:T(8,128)(2,1)} %param.13) | copy-start | bytes 36868
  31.9 86.8 %all-to-all-start.2 = ((bf16[8,192,768]{2,1,0:T(8,128)(2,1)}), bf16[8,192,768]{2,1,0:T(8,128)(2,1)S(1)}, u32[]{:S(2)}, u32[]{:S(2)}) async-start(bf16[8,192,768]{2,1,0:T(8,128)(2,1)} %bitcast.3), calls=%async_computation.2 | async-start | bytes 4718592 | tf_op jit(solution)/shard_map/all_to_all | solution.py:62
  35.7 121.6 %all-gather.7.cloned.1.call-start = ((), (), s32[]{:S(2)}) async-start(), calls=%async_computation.6 | async-start | bytes 2211840 | tf_op jit(solution)/shard_map/all_gather | solution.py:29
  36.4 124.8 %all-gather.5.cloned.1.call-start = ((), (), s32[]{:S(2)}) async-start(), calls=%async_computation.5 | async-start | bytes 2359296 | tf_op jit(solution)/shard_map/all_gather | solution.py:87
  138.9 1.4 copy-start.4
  138.9 100.5 %all-gather.9.cloned.1.call-start = ((), (), s32[]{:S(2)}) async-start(), calls=%async_computation.7 | async-start | bytes 5898240 | tf_op jit(solution)/shard_map/all_gather | solution.py:31
  139.7 150.2 %all-gather.11.cloned.1.call-start = ((), (), s32[]{:S(2)}) async-start(), calls=%async_computation.8 | async-start | bytes 2949120 | tf_op jit(solution)/shard_map/all_gather | solution.py:32
  140.2 170.6 %reduce-scatter.2.cloned.1.call-start = ((), (), s32[]{:S(2)}) async-start(), calls=%async_computation.9 | async-start | bytes 4718592 | tf_op jit(solution)/shard_map/reduce_scatter | solution.py:115
  165.2 2.2 copy-start.2
  262.5 34.9 %copy-start.3 = (bf16[384,768]{0,1:T(8,128)(2,1)S(1)}, bf16[384,768]{0,1:T(8,128)(2,1)}, u32[]{:S(2)}) copy-start(bf16[384,768]{0,1:T(8,128)(2,1)} %all_gather.17) | copy-start | bytes 1769476
  310.9 3.0 copy-start.1
Sparse Core Ops, SparseCore 0:
  38.1 76.3 all-gather.6
  139.1 8.1 all-gather.4
  148.9 90.5 all-gather.8
  240.9 48.9 all-gather.10
  301.1 9.7 reduce-scatter.1
where the time goes:
time: 321 us; the launch traced here: 320 us
  waiting for transfers between devices  177 us (55%)
  local copies, waits for them, and re-layouts  41 us (13%)
  matrix products  37.6 us (12%)
  blocking collectives  30.3 us (9%)
  between operations  14.1 us (4%)
  starting transfers between devices  13.6 us (4%)
  other arithmetic  6.81 us (2%)
    all_to_all x1, waiting for transfers between devices, on_device(): lax.all_to_all(send_feat, ('cells', 'mp'), split_axis=0, concat_axis=0, t...  81.7 us
    all_gather x1, waiting for transfers between devices, on_device(): lax.all_gather(w_gate_up, 'cells', axis=0, tiled=True)  48.6 us
    all_gather x1, waiting for transfers between devices, on_device(): lax.all_gather(w_down, 'cells', axis=1, tiled=True)  27.4 us
    all_gather x1, blocking collectives, on_device(): lax.all_gather(w_out, 'cells', axis=1, tiled=True)  17 us
    all_to_all x1, blocking collectives, on_device(): lax.all_to_all(token_grid, 'slots', split_axis=0, concat_axis=2, tiled=True)  13.3 us
    reshape x1, local copies, waits for them, and re-layouts, on_device(): full_gate_up.reshape(feat_width, -1)  12.5 us
    dot_general x1, matrix products, on_device(): jnp.dot(flat_rows, full_gate_up.reshape(feat_width, -1), preferred_elemen...  10.5 us
    reduce_scatter x1, waiting for transfers between devices, on_device(): lax.psum_scatter(partial_value, 'mp', scatter_dimension=0, tiled=True)  9.88 us
  transfers between devices with their start and end apart: 8, of which 6 were waited for; matrix products, arithmetic and copies ran while one was open for 21% of the time, Pallas kernels for 0%

commit v1 on v0

v1 whole, which is shorter than its diff:
```python
import jax
import jax.numpy as jnp
from jax import lax
from jax.sharding import PartitionSpec as P

HD = 64
TSTEPS = 8
CB = 128


EPS = 1e-06


def rms_scale(values):
    return values * lax.rsqrt(jnp.mean(values * values, axis=-1, keepdims=True) + EPS)


def gather_weights(local_rows):
    n_share = lax.axis_size("groups") * lax.axis_size("slots")
    share = local_rows.shape[0] // n_share
    which = lax.axis_index("groups") * lax.axis_size("slots") + lax.axis_index("slots")
    mine = lax.dynamic_slice_in_dim(local_rows, which * share, share, 0)
    mine = mine.reshape(share, -1)
    return lax.all_gather(mine, ("mp", "cells", "groups", "slots"), axis=0, tiled=True)


def on_device(obs_feat, obs_cell, obs_slot, obs_count, time_embed, w_qkv, w_out, w_gate_up, w_down):
    n_cells = lax.axis_size("cells")
    n_slots = lax.axis_size("slots")
    n_mp = lax.axis_size("mp")
    n_owners = n_cells * n_mp
    obs_rows = obs_feat.shape[0]
    feat_width = obs_feat.shape[1]
    capacity = 3 * obs_rows // n_owners
    quarter = CB // n_slots
    slot_dev = TSTEPS // n_slots
    my_owner = lax.axis_index("cells") * n_mp + lax.axis_index("mp")
    my_slot = lax.axis_index("slots")
    full_qkv = gather_weights(w_qkv)
    full_out = gather_weights(w_out.T)
    full_gate_up = gather_weights(w_gate_up)
    full_down = gather_weights(w_down.T)

    row_ids = jnp.arange(obs_rows, dtype=jnp.int32)
    valid_row = row_ids < obs_count[0]
    local_part = obs_cell % quarter
    mp_part = obs_cell // quarter % n_mp
    slot_part = obs_cell // (quarter * n_mp) % n_slots
    cell_part = obs_cell // (quarter * n_mp * n_slots)
    ahead = jnp.where(
        valid_row, (cell_part * n_mp + mp_part - my_owner + n_owners) % n_owners, n_owners
    )
    position = (slot_part * quarter + local_part) * slot_dev + obs_slot
    owner_hot = (ahead[:, None] == jnp.arange(n_owners, dtype=jnp.int32)[None, :]).astype(
        jnp.bfloat16
    )
    lower_tri = (row_ids[None, :] <= row_ids[:, None]).astype(jnp.bfloat16)
    running = jnp.dot(lower_tri, owner_hot, preferred_element_type=jnp.float32)
    slot_rank = jnp.sum(running * owner_hot.astype(jnp.float32), axis=1).astype(jnp.int32) - 1
    place = jnp.where(valid_row, ahead * capacity + slot_rank, n_owners * capacity)
    place_ids = jnp.arange(n_owners * capacity, dtype=jnp.int32)
    taken = place_ids[:, None] == place[None, :]
    send_pos = jnp.sum(jnp.where(taken, position[None, :] + 1, 0), axis=1) - 1
    send_pos = send_pos.reshape(n_owners, capacity)

    def shift(values, step):
        pairs = [(j, (j + step) % n_owners) for j in range(n_owners)]
        return lax.ppermute(values, ("cells", "mp"), pairs)

    got_feat, got_pos = [], []
    for step in range(n_owners):
        hot = taken[step * capacity : (step + 1) * capacity].astype(jnp.bfloat16)
        block = jnp.dot(hot, obs_feat, preferred_element_type=jnp.float32).astype(jnp.bfloat16)
        got_feat.append(shift(block, step) if step else block)
        got_pos.append(shift(send_pos[step], step) if step else send_pos[step])
    got_feat = jnp.concatenate(got_feat, axis=0)
    got_pos = jnp.concatenate(got_pos, axis=0)
    onehot_tab = (jnp.arange(CB * slot_dev, dtype=jnp.int32)[:, None] == got_pos[None, :]).astype(
        jnp.bfloat16
    )
    pooled_sum = jnp.dot(onehot_tab, got_feat, preferred_element_type=jnp.float32)
    cell_count = jnp.sum(onehot_tab.astype(jnp.float32), axis=1)
    pooled = pooled_sum / jnp.maximum(cell_count, 1.0)[:, None]
    slot_embed = lax.dynamic_slice_in_dim(time_embed, my_slot * slot_dev, slot_dev, 0)
    tokens = (
        pooled.reshape(CB, slot_dev, feat_width) + slot_embed.astype(jnp.float32)[None]
    ).astype(jnp.bfloat16)
    token_grid = tokens.reshape(n_slots, quarter, slot_dev, feat_width)
    token_block = lax.all_to_all(token_grid, "slots", split_axis=0, concat_axis=2, tiled=True)
    resid = token_block.reshape(quarter, TSTEPS, feat_width).astype(jnp.float32)
    normed = rms_scale(resid).astype(jnp.bfloat16)
    flat_rows = normed.reshape(-1, feat_width)
    n_rows = flat_rows.shape[0]
    head_count = w_qkv.shape[2] // HD

    total = resid.reshape(n_rows, feat_width)
    for part in range(n_mp):
        rows = slice(part * feat_width, (part + 1) * feat_width)
        projected = jnp.dot(flat_rows, full_qkv[rows], preferred_element_type=jnp.float32)
        projected = projected.reshape(quarter, TSTEPS, 3, head_count, HD)
        queries = rms_scale(projected[:, :, 0]).astype(jnp.bfloat16)
        keys_att = rms_scale(projected[:, :, 1]).astype(jnp.bfloat16)
        values_att = projected[:, :, 2].astype(jnp.bfloat16)
        scores = jnp.einsum(
            "cthe,cshe->chts", queries, keys_att, preferred_element_type=jnp.float32
        ) * HD ** (-0.5)
        expo = jnp.exp(scores)
        attn_probs = (expo / jnp.sum(expo, axis=-1, keepdims=True)).astype(jnp.bfloat16)
        context = jnp.einsum(
            "chts,cshe->cthe", attn_probs, values_att, preferred_element_type=jnp.float32
        )
        context = context.astype(jnp.bfloat16).reshape(n_rows, head_count * HD)
        total += jnp.dot(context, full_out[rows].T, preferred_element_type=jnp.float32)
        gate_up = jnp.dot(flat_rows, full_gate_up[rows], preferred_element_type=jnp.float32)
        hidden_width = gate_up.shape[1] // 2
        hidden = jax.nn.silu(gate_up[:, :hidden_width]) * gate_up[:, hidden_width:]
        total += jnp.dot(
            hidden.astype(jnp.bfloat16), full_down[rows].T, preferred_element_type=jnp.float32
        )
    return total.astype(jnp.bfloat16).reshape(quarter, TSTEPS, feat_width)


def solution(mesh):
    placed = (
        P(("groups", "cells", "slots", "mp"), None),
        P(("groups", "cells", "slots", "mp")),
        P(("groups", "cells", "slots", "mp")),
        P(("groups", "cells", "slots", "mp")),
        P(),
        P("cells", None, "mp"),
        P("mp", "cells"),
        P("cells", None, "mp"),
        P("mp", "cells"),
    )
    return jax.shard_map(
        on_device,
        mesh=mesh,
        in_specs=placed,
        out_specs=P(("groups", "cells", "slots", "mp"), None, None),
        check_vma=False,
    )
```

time: 321 us -> 325 us (1.012)
  matrix products: 37.6 us -> 53.1 us
  local copies, waits for them, and re-layouts: 41 us -> 28.7 us
  blocking collectives: 30.3 us -> 18.6 us
  starting transfers between devices: 13.6 us -> 23.9 us
    all_to_all x3 -> x0, waiting for transfers between devices: 89.3 us -> none  [the longest x1 81.7 us: on_device(): lax.all_to_all(send_feat, ('cells', 'mp'), split_axis=0, concat_axis=0, t...]
    all_gather x4, waiting for transfers between devices: 76 us -> 149 us  [gather_weights(): lax.all_gather(mine, ('mp', 'cells', 'groups', 'slots'), axis=0, tiled=True)]
    ppermute x0 -> x14, waiting for transfers between devices: none -> 26.5 us  [shift(): return lax.ppermute(values, ('cells', 'mp'), pairs)]
    ppermute x0 -> x14, starting transfers between devices: none -> 23.8 us  [shift(): return lax.ppermute(values, ('cells', 'mp'), pairs)]
    all_gather x1 -> x0, blocking collectives: 17 us -> none  [on_device(): lax.all_gather(w_out, 'cells', axis=1, tiled=True)]
    reshape x3, local copies, waits for them, and re-layouts: 18.2 us -> 2.63 us  [the longest x2 1.97 us: on_device(): context = context.astype(jnp.bfloat16).reshape(n_rows, head_count * HD)]
    all_to_all x3 -> x0, starting transfers between devices: 13.4 us -> none  [the longest x1 6.33 us: on_device(): lax.all_to_all(send_cell, ('cells', 'mp'), split_axis=0, concat_axis=0, t...]
    dot_general x6 -> x16, matrix products: 27.3 us -> 39.9 us  [the longest x2 11.7 us: on_device(): jnp.dot(flat_rows, full_qkv[rows], preferred_element_type=jnp.float32)]
  transfers between devices with their start and end apart: 8 -> 18, of which waited for: 6 -> 6; matrix products, arithmetic and copies ran while one was open for 21% -> 25% of each run, Pallas kernels for 0% -> 0%
where the time goes in v1:
time: 325 us; the launch traced here: 324 us
  waiting for transfers between devices  176 us (54%)
  matrix products  53.1 us (16%)
  local copies, waits for them, and re-layouts  28.7 us (9%)
  starting transfers between devices  23.9 us (7%)
  blocking collectives  18.6 us (6%)
  between operations  14.2 us (4%)
  other arithmetic  9.85 us (3%)
    all_gather x4, waiting for transfers between devices, gather_weights(): lax.all_gather(mine, ('mp', 'cells', 'groups', 'slots'), axis=0, tiled=True)  149 us
    ppermute x14, waiting for transfers between devices, shift(): return lax.ppermute(values, ('cells', 'mp'), pairs)  26.5 us
    ppermute x14, starting transfers between devices, shift(): return lax.ppermute(values, ('cells', 'mp'), pairs)  23.8 us
    all_to_all x1, blocking collectives, on_device(): lax.all_to_all(token_grid, 'slots', split_axis=0, concat_axis=2, tiled=True)  18.6 us
    dot_general x2, matrix products, on_device(): jnp.dot(flat_rows, full_qkv[rows], preferred_element_type=jnp.float32)  11.7 us
    dot_general x2, matrix products, on_device(): jnp.dot(flat_rows, full_gate_up[rows], preferred_element_type=jnp.float32)  11.7 us
    unnamed x30, local copies, waits for them, and re-layouts  7.55 us
    dot_general x2, matrix products, on_device(): jnp.dot(hidden.astype(jnp.bfloat16), full_down[rows].T, preferred_element...  7.32 us
  transfers between devices with their start and end apart: 18, of which 6 were waited for; matrix products, arithmetic and copies ran while one was open for 25% of the time, Pallas kernels for 0%

profile of v1, /device:TPU:0, one launch (start us, length us, event | category | flops | bytes accessed | tf_op | source)
XLA Modules:
  0.0 324.1 jit_solution(7655698336143107831)
XLA Ops:
  6.5 1.0 dynamic-slice_bitcast_fusion.1
  8.3 1.4 dynamic-slice_bitcast_fusion.2
  10.0 0.8 copy.113
  13.5 2.6 collective-permute-start.1
  16.1 2.5 collective-permute-start.2
  18.6 1.2 collective-permute-start.3
  19.9 1.2 collective-permute-start.4
  21.1 1.6 dynamic-slice_bitcast_fusion
  23.3 1.1 fusion.20
  24.4 1.0 convolution_convert_fusion.8
  25.4 1.1 convolution_convert_fusion.7
  28.2 1.4 collective-permute-start.5
  29.6 1.4 collective-permute-start.6
  32.1 3.5 %collective-permute-start.10 = (bf16[192,768]{1,0:T(8,128)(2,1)S(1)}, bf16[192,768]{1,0:T(8,128)(2,1)S(1)}, u32[]{:S(2)}, u32[]{:S(2)}) collective-permute-start(bf16[192,768]{1,0:T(8,128)(2,1)S(1)} %convolution_convert_fusion.5), channel_id=1, source_target_pairs={{0,8},{1,9},{4,12},{5,13},{8,0},{9,1},{12,4},{13,5},{2,10},{3,11},... | collective-permute-start | bytes 884744 | tf_op jit(solution)/shard_map/ppermute | solution.py:68
  36.1 5.9 %collective-permute-done.7 = bf16[192,768]{1,0:T(8,128)(2,1)S(1)} collective-permute-done((bf16[192,768]{1,0:T(8,128)(2,1)}, bf16[192,768]{1,0:T(8,128)(2,1)S(1)}, u32[]{:S(2)}, u32[]{:S(2)}) %collective-permute-start.7) | collective-permute-done | bytes 294944 | tf_op jit(solution)/shard_map/ppermute | solution.py:68
  42.8 1.2 collective-permute-done.8
  44.0 8.4 %collective-permute-start.13 = (bf16[192,768]{1,0:T(8,128)(2,1)S(1)}, bf16[192,768]{1,0:T(8,128)(2,1)S(1)}, u32[]{:S(2)}, u32[]{:S(2)}) collective-permute-start(bf16[192,768]{1,0:T(8,128)(2,1)S(1)} %convolution_convert_fusion.2), channel_id=1, source_target_pairs={{0,13},{1,0},{4,1},{5,4},{8,5},{9,8},{12,9},{13,12},{2,15},{3,2},{... | collective-permute-start | bytes 884744 | tf_op jit(solution)/shard_map/ppermute | solution.py:68
  53.1 19.3 %collective-permute-done.9 = bf16[192,768]{1,0:T(8,128)(2,1)S(1)} collective-permute-done((bf16[192,768]{1,0:T(8,128)(2,1)S(1)}, bf16[192,768]{1,0:T(8,128)(2,1)S(1)}, u32[]{:S(2)}, u32[]{:S(2)}) %collective-permute-start.9) | collective-permute-done | bytes 294944 | tf_op jit(solution)/shard_map/ppermute | solution.py:68
  74.6 0.8 constant_dynamic-update-slice_fusion.1
  76.1 3.1 fusion.19
  80.0 18.6 %all_to_all.4 = bf16[2,64,4,768]{3,1,2,0:T(8,128)(2,1)S(1)} all-to-all(bf16[2,64,4,768]{3,1,2,0:T(8,128)(2,1)S(1)} %fusion.12), channel_id=1, replica_groups=mesh['groups'=2,'cells'=4,'slots'=2,'mp'=2] {'slots'}, dimensions={0} | all-to-all | bytes 1572864 | tf_op jit(solution)/shard_map/all_to_all | solution.py:89
  98.8 1.0 copy.82
  99.8 1.7 reshape.152
  102.0 1.1 multiply_convert_fusion.5
  103.1 2.3 slice_bitcast_fusion.1
  105.3 2.3 copy.96
  107.6 6.2 %fusion.32 = f32[64,8,3,6,64]{4,1,3,2,0:T(8,128)} fusion(bf16[3,6,64,768,1]{3,2,1,0,4:T(8,128)(2,1)} %bitcast.93, bf16[64,8,768,1,1]{2,0,1,4,3:T(8,128)(2,1)} %bitcast.96), kind=kOutput, calls=%fused_computation.68 | convolution fusion | flops 905969664 | bytes 4915200 | tf_op jit(solution)/shard_map/dot_general | solution.py:99
  113.9 2.8 multiply_reduce_fusion.1
  116.8 0.9 copy.101
  117.8 0.9 copy.99
  118.7 3.0 fusion.23
  123.0 2.0 fusion.17
  125.3 1.4 reshape.150
  126.7 0.9 copy.86
  127.6 5.5 %fusion.34 = f32[64,8,3,6,64]{4,1,3,2,0:T(8,128)} fusion(bf16[3,6,64,768,1]{3,2,1,0,4:T(8,128)(2,1)S(1)} %bitcast.92, bf16[64,8,768,1,1]{2,0,1,4,3:T(8,128)(2,1)} %bitcast.97), kind=kOutput, calls=%fused_computation.70 | convolution fusion | flops 905969664 | bytes 4915200 | tf_op jit(solution)/shard_map/dot_general | solution.py:99
  133.1 2.8 multiply_reduce_fusion.3
  136.5 2.9 fusion.22
  140.8 2.0 fusion.16
  143.7 14.9 %all-gather.7.cloned.1.call-done = bf16[1536,384]{1,0:T(8,128)(2,1)} async-done(((bf16[48,384]{1,0:T(8,128)(2,1)}), bf16[1536,384]{1,0:T(8,128)(2,1)}) %all-gather.7.cloned.1.call-update) | async-done | bytes 1179664 | tf_op jit(solution)/shard_map/all_gather | solution.py:24
  158.6 2.8 fusion.37
  161.4 81.1 %all-gather.9.cloned.1.call-done = bf16[1536,3072]{1,0:T(8,128)(2,1)} async-done(((bf16[48,3072]{1,0:T(8,128)(2,1)}), bf16[1536,3072]{1,0:T(8,128)(2,1)}) %all-gather.9.cloned.1.call-update) | async-done | bytes 9437200 | tf_op jit(solution)/shard_map/all_gather | solution.py:24
  242.5 7.1 %fusion = f32[512,3072]{1,0:T(8,128)} fusion(bf16[1536,3072]{1,0:T(8,128)(2,1)} %all-gather.9.cloned.1.call-done, f32[512,768]{1,0:T(8,128)S(1)} %copy-done.3, f32[512]{0:T(512)S(1)} %rsqrt.48), kind=kOutput, calls=%fused_computation | convolution fusion | flops 2416705536 | bytes 12584960 | tf_op jit(solution)/shard_map/dot_general | solution.py:114
  249.6 4.6 %fusion.2 = f32[512,3072]{1,0:T(8,128)} fusion(bf16[1536,3072]{1,0:T(8,128)(2,1)S(1)} %copy-done.8, f32[512,768]{1,0:T(8,128)S(1)} %copy-done.3, f32[512]{0:T(512)S(1)} %rsqrt.48), kind=kOutput, calls=%fused_computation.2 | convolution fusion | flops 2416705536 | bytes 12584960 | tf_op jit(solution)/shard_map/dot_general | solution.py:114
  254.2 53.2 %all-gather.11.cloned.1.call-done = bf16[1536,1536]{1,0:T(8,128)(2,1)} async-done(((bf16[48,1536]{1,0:T(8,128)(2,1)}), bf16[1536,1536]{1,0:T(8,128)(2,1)}) %all-gather.11.cloned.1.call-update) | async-done | bytes 4718608 | tf_op jit(solution)/shard_map/all_gather | solution.py:24
  307.4 5.5 %fusion.8 = f32[512,768]{1,0:T(8,128)S(1)} fusion(bf16[1536,1536]{1,0:T(8,128)(2,1)} %all-gather.11.cloned.1.call-done, f32[512,3072]{1,0:T(8,128)} %fusion), kind=kOutput, calls=%fused_computation.14 | convolution fusion | flops 1212678144 | bytes 10223616 | tf_op jit(solution)/shard_map/dot_general | solution.py:117
  312.9 1.2 copy-done.10
  314.2 1.8 fusion.10
  316.0 1.5 fusion.18
  (99 shorter events, 17.4 us)
Async XLA Ops:
  6.5 3.3 %copy-start = (bf16[192,2,1536]{2,1,0:T(2,128)(2,1)S(1)}, bf16[192,2,1536]{2,1,0:T(2,128)(2,1)}, u32[]{:S(2)}) copy-start(bf16[192,2,1536]{2,1,0:T(2,128)(2,1)} %param.16) | copy-start | bytes 3538948
  6.5 16.7 %copy-start.2 = (bf16[512,768]{1,0:T(8,128)(2,1)S(1)}, bf16[512,768]{1,0:T(8,128)(2,1)}, u32[]{:S(2)}) copy-start(bf16[512,768]{1,0:T(8,128)(2,1)} %param.9) | copy-start | bytes 2359300
  6.5 96.5 %all-gather.5.cloned.1.call-start = ((), (), s32[]{:S(2)}) async-start(), calls=%async_computation.1 | async-start | bytes 3649536 | tf_op jit(solution)/shard_map/all_gather | solution.py:24
  8.3 150.3 %all-gather.7.cloned.1.call-start = ((), (), s32[]{:S(2)}) async-start(), calls=%async_computation.2 | async-start | bytes 1216512 | tf_op jit(solution)/shard_map/all_gather | solution.py:24
  9.7 232.7 %all-gather.9.cloned.1.call-start = ((), (), s32[]{:S(2)}) async-start(), calls=%async_computation.3 | async-start | bytes 9732096 | tf_op jit(solution)/shard_map/all_gather | solution.py:24
  10.8 296.6 %all-gather.11.cloned.1.call-start = ((), (), s32[]{:S(2)}) async-start(), calls=%async_computation.4 | async-start | bytes 4866048 | tf_op jit(solution)/shard_map/all_gather | solution.py:24
  13.0 15.2 %collective-permute-start = (s32[192]{0:T(256)S(1)}, s32[192]{0:T(256)S(1)}, u32[]{:S(2)}, u32[]{:S(2)}) collective-permute-start(s32[192]{0:T(256)S(1)} %get-tuple-element.17), channel_id=1, source_target_pairs={{0,1},{1,4},{4,5},{5,8},{8,9},{9,12},{12,13},{13,0},{2,3},{3,6},{6... | collective-permute-start | bytes 2312 | tf_op jit(solution)/shard_map/ppermute | solution.py:68
  13.5 16.2 %collective-permute-start.1 = (s32[192]{0:T(256)S(1)}, s32[192]{0:T(256)S(1)}, u32[]{:S(2)}, u32[]{:S(2)}) collective-permute-start(s32[192]{0:T(256)S(1)} %get-tuple-element.16), channel_id=1, source_target_pairs={{0,4},{1,5},{4,8},{5,9},{8,12},{9,13},{12,0},{13,1},{2,6},{3,7},{6... | collective-permute-start | bytes 2312 | tf_op jit(solution)/shard_map/ppermute | solution.py:68
  16.1 14.9 %collective-permute-start.2 = (s32[192]{0:T(256)S(1)}, s32[192]{0:T(256)S(1)}, u32[]{:S(2)}, u32[]{:S(2)}) collective-permute-start(s32[192]{0:T(256)S(1)} %get-tuple-element.15), channel_id=1, source_target_pairs={{0,5},{1,8},{4,9},{5,12},{8,13},{9,0},{12,1},{13,4},{2,7},{3,10},{... | collective-permute-start | bytes 2312 | tf_op jit(solution)/shard_map/ppermute | solution.py:68
  18.6 12.5 %collective-permute-start.3 = (s32[192]{0:T(256)S(1)}, s32[192]{0:T(256)S(1)}, u32[]{:S(2)}, u32[]{:S(2)}) collective-permute-start(s32[192]{0:T(256)S(1)} %get-tuple-element.14), channel_id=1, source_target_pairs={{0,8},{1,9},{4,12},{5,13},{8,0},{9,1},{12,4},{13,5},{2,10},{3,11},... | collective-permute-start | bytes 2312 | tf_op jit(solution)/shard_map/ppermute | solution.py:68
  19.9 12.0 %collective-permute-start.4 = (s32[192]{0:T(256)S(1)}, s32[192]{0:T(256)S(1)}, u32[]{:S(2)}, u32[]{:S(2)}) collective-permute-start(s32[192]{0:T(256)S(1)} %get-tuple-element.13), channel_id=1, source_target_pairs={{0,9},{1,12},{4,13},{5,0},{8,1},{9,4},{12,5},{13,8},{2,11},{3,14},... | collective-permute-start | bytes 2312 | tf_op jit(solution)/shard_map/ppermute | solution.py:68
  26.8 4.2 %copy-start.7 = (bf16[8,768]{1,0:T(8,128)(2,1)S(1)}, bf16[8,768]{1,0:T(8,128)(2,1)}, u32[]{:S(2)}) copy-start(bf16[8,768]{1,0:T(8,128)(2,1)} %param.13) | copy-start | bytes 36868
  28.2 3.9 %collective-permute-start.5 = (s32[192]{0:T(256)S(1)}, s32[192]{0:T(256)S(1)}, u32[]{:S(2)}, u32[]{:S(2)}) collective-permute-start(s32[192]{0:T(256)S(1)} %get-tuple-element.12), channel_id=1, source_target_pairs={{0,12},{1,13},{4,0},{5,1},{8,4},{9,5},{12,8},{13,9},{2,14},{3,15},... | collective-permute-start | bytes 2312 | tf_op jit(solution)/shard_map/ppermute | solution.py:68
  29.6 6.0 %collective-permute-start.6 = (s32[192]{0:T(256)S(1)}, s32[192]{0:T(256)S(1)}, u32[]{:S(2)}, u32[]{:S(2)}) collective-permute-start(s32[192]{0:T(256)S(1)} %get-tuple-element.11), channel_id=1, source_target_pairs={{0,13},{1,0},{4,1},{5,4},{8,5},{9,8},{12,9},{13,12},{2,15},{3,2},{... | collective-permute-start | bytes 2312 | tf_op jit(solution)/shard_map/ppermute | solution.py:68
  31.1 11.0 %collective-permute-start.7 = (bf16[192,768]{1,0:T(8,128)(2,1)}, bf16[192,768]{1,0:T(8,128)(2,1)S(1)}, u32[]{:S(2)}, u32[]{:S(2)}) collective-permute-start(bf16[192,768]{1,0:T(8,128)(2,1)} %convolution_convert_fusion.8), channel_id=1, source_target_pairs={{0,1},{1,4},{4,5},{5,8},{8,9},{9,12},{12,13},{13,0},{2,3},{3,6},{6... | collective-permute-start | bytes 884744 | tf_op jit(solution)/shard_map/ppermute | solution.py:68
  31.1 12.8 %collective-permute-start.8 = (bf16[192,768]{1,0:T(8,128)(2,1)}, bf16[192,768]{1,0:T(8,128)(2,1)S(1)}, u32[]{:S(2)}, u32[]{:S(2)}) collective-permute-start(bf16[192,768]{1,0:T(8,128)(2,1)} %convolution_convert_fusion.7), channel_id=1, source_target_pairs={{0,4},{1,5},{4,8},{5,9},{8,12},{9,13},{12,0},{13,1},{2,6},{3,7},{6... | collective-permute-start | bytes 884744 | tf_op jit(solution)/shard_map/ppermute | solution.py:68
  31.9 40.5 %collective-permute-start.9 = (bf16[192,768]{1,0:T(8,128)(2,1)S(1)}, bf16[192,768]{1,0:T(8,128)(2,1)S(1)}, u32[]{:S(2)}, u32[]{:S(2)}) collective-permute-start(bf16[192,768]{1,0:T(8,128)(2,1)S(1)} %convolution_convert_fusion.6), channel_id=1, source_target_pairs={{0,5},{1,8},{4,9},{5,12},{8,13},{9,0},{12,1},{13,4},{2,7},{3,10},{... | collective-permute-start | bytes 884744 | tf_op jit(solution)/shard_map/ppermute | solution.py:68
  32.1 41.0 %collective-permute-start.10 = (bf16[192,768]{1,0:T(8,128)(2,1)S(1)}, bf16[192,768]{1,0:T(8,128)(2,1)S(1)}, u32[]{:S(2)}, u32[]{:S(2)}) collective-permute-start(bf16[192,768]{1,0:T(8,128)(2,1)S(1)} %convolution_convert_fusion.5), channel_id=1, source_target_pairs={{0,8},{1,9},{4,12},{5,13},{8,0},{9,1},{12,4},{13,5},{2,10},{3,11},... | collective-permute-start | bytes 884744 | tf_op jit(solution)/shard_map/ppermute | solution.py:68
  35.6 38.3 %collective-permute-start.11 = (bf16[192,768]{1,0:T(8,128)(2,1)S(1)}, bf16[192,768]{1,0:T(8,128)(2,1)S(1)}, u32[]{:S(2)}, u32[]{:S(2)}) collective-permute-start(bf16[192,768]{1,0:T(8,128)(2,1)S(1)} %convolution_convert_fusion.4), channel_id=1, source_target_pairs={{0,9},{1,12},{4,13},{5,0},{8,1},{9,4},{12,5},{13,8},{2,11},{3,14},... | collective-permute-start | bytes 884744 | tf_op jit(solution)/shard_map/ppermute | solution.py:68
  42.0 32.6 %collective-permute-start.12 = (bf16[192,768]{1,0:T(8,128)(2,1)S(1)}, bf16[192,768]{1,0:T(8,128)(2,1)S(1)}, u32[]{:S(2)}, u32[]{:S(2)}) collective-permute-start(bf16[192,768]{1,0:T(8,128)(2,1)S(1)} %convolution_convert_fusion.3), channel_id=1, source_target_pairs={{0,12},{1,13},{4,0},{5,1},{8,4},{9,5},{12,8},{13,9},{2,14},{3,15},... | collective-permute-start | bytes 884744 | tf_op jit(solution)/shard_map/ppermute | solution.py:68
  44.0 31.4 %collective-permute-start.13 = (bf16[192,768]{1,0:T(8,128)(2,1)S(1)}, bf16[192,768]{1,0:T(8,128)(2,1)S(1)}, u32[]{:S(2)}, u32[]{:S(2)}) collective-permute-start(bf16[192,768]{1,0:T(8,128)(2,1)S(1)} %convolution_convert_fusion.2), channel_id=1, source_target_pairs={{0,13},{1,0},{4,1},{5,4},{8,5},{9,8},{12,9},{13,12},{2,15},{3,2},{... | collective-permute-start | bytes 884744 | tf_op jit(solution)/shard_map/ppermute | solution.py:68
  143.1 99.4 %copy-start.3 = (f32[512,768]{1,0:T(8,128)S(1)}, f32[512,768]{1,0:T(8,128)}, u32[]{:S(2)}) copy-start(f32[512,768]{1,0:T(8,128)} %reshape.152) | copy-start | bytes 4718596
  242.5 7.1 %copy-start.8 = (bf16[1536,3072]{1,0:T(8,128)(2,1)S(1)}, bf16[1536,3072]{1,0:T(8,128)(2,1)}, u32[]{:S(2)}) copy-start(bf16[1536,3072]{1,0:T(8,128)(2,1)} %all-gather.9.cloned.1.call-done) | copy-start | bytes 28311556
  307.4 5.5 %copy-start.9 = (bf16[1536,1536]{1,0:T(8,128)(2,1)S(1)}, bf16[1536,1536]{1,0:T(8,128)(2,1)}, u32[]{:S(2)}) copy-start(bf16[1536,1536]{1,0:T(8,128)(2,1)} %all-gather.11.cloned.1.call-done) | copy-start | bytes 14155780
  307.4 6.7 %copy-start.10 = (f32[512,3072]{1,0:T(8,128)S(1)}, f32[512,3072]{1,0:T(8,128)}, u32[]{:S(2)}) copy-start(f32[512,3072]{1,0:T(8,128)} %fusion.2) | copy-start | bytes 18874372
  314.2 1.9 copy-start.4
  314.2 1.9 copy-start.5
  314.2 1.9 copy-start.6
  314.2 3.4 %copy-start.1 = (bf16[192,2,1536]{2,1,0:T(2,128)(2,1)S(1)}, bf16[192,2,1536]{2,1,0:T(2,128)(2,1)}, u32[]{:S(2)}) copy-start(bf16[192,2,1536]{2,1,0:T(2,128)(2,1)} %param.16) | copy-start | bytes 3538948
Sparse Core Ops, SparseCore 0:
  10.3 92.4 all-gather.4
  105.6 52.9 all-gather.6
  161.5 80.9 all-gather.8
  245.2 62.1 all-gather.10

commit v2 on v1

v2 whole, which is shorter than its diff:
```python
import functools

import jax
import jax.numpy as jnp
from jax import lax
from jax.experimental import pallas as pl
from jax.experimental.pallas import tpu as pltpu
from jax.sharding import PartitionSpec as P

HD = 64
TSTEPS = 8
CB = 128
EPS = 1e-06

META_ROWS = 16
CODE = 32
LANES = 128
VMEM_LIMIT = 48 * 1024 * 1024
F32 = jnp.float32
BF16 = jnp.bfloat16
WHOLE = pl.BlockSpec(memory_space=pltpu.VMEM)
SCALARS = pl.BlockSpec(memory_space=pltpu.SMEM)


def iota(shape, axis):
    return lax.broadcasted_iota(jnp.int32, shape, axis)


def dot(left, right):
    return jnp.dot(left, right, preferred_element_type=F32)


def dot_t(left, right):
    return lax.dot_general(left, right, (((1,), (1,)), ((), ())), preferred_element_type=F32)


def params(**extra):
    return pltpu.CompilerParams(vmem_limit_bytes=VMEM_LIMIT, **extra)


def place_kernel(n_owners, capacity, ahead_ref, position_ref, feat_ref, *out_refs):
    rows = feat_ref.shape[0]
    ahead = ahead_ref[...]
    owner_hot = (iota((n_owners, rows), 0) == ahead).astype(F32)
    upper = (iota((rows, rows), 0) <= iota((rows, rows), 1)).astype(BF16)
    running = dot(owner_hot.astype(BF16), upper)
    rank = jnp.sum(running * owner_hot, axis=0, keepdims=True).astype(jnp.int32) - 1
    code = position_ref[...] + 1
    line = iota((META_ROWS, rows), 0)
    meta = jnp.where(line == 0, code // CODE, jnp.where(line == 1, code % CODE, 0))
    meta = meta.astype(F32).astype(BF16)
    feat = feat_ref[...]
    for block in range(n_owners):
        place = jnp.where(ahead == block, rank, -1)
        taken = (iota((capacity, rows), 0) == place).astype(F32).astype(BF16)
        out = out_refs[block]
        out[:capacity, :] = dot(taken, feat).astype(BF16)
        out[capacity:, :] = jnp.zeros((META_ROWS, out.shape[1]), BF16)
        out[capacity:, :capacity] = dot_t(meta, taken).astype(BF16)


def place_rows(ahead, position, obs_feat, n_owners, capacity):
    rows, width = obs_feat.shape
    block = jax.ShapeDtypeStruct((capacity + META_ROWS, width), BF16)
    return pl.pallas_call(
        functools.partial(place_kernel, n_owners, capacity),
        out_shape=[block] * n_owners,
        in_specs=[WHOLE] * 3,
        out_specs=[WHOLE] * n_owners,
        compiler_params=params(),
        cost_estimate=pl.CostEstimate(
            flops=2 * rows * width * n_owners * capacity,
            bytes_accessed=2 * width * (rows + n_owners * capacity),
            transcendentals=0,
        ),
        name="place_rows",
    )(ahead.reshape(1, rows), position.reshape(1, rows), obs_feat)


def pool_kernel(capacity, slot_dev, slot_ref, embed_ref, *refs):
    block_refs, (keep_ref, send_ref) = refs[:-2], refs[-2:]
    half = keep_ref.shape[0]
    places = 2 * half
    mine = slot_ref[0]
    total = jnp.zeros((places, keep_ref.shape[1]), F32)
    seen = jnp.zeros((places, capacity), F32)
    for block in block_refs:
        meta = block[capacity:, :capacity].astype(F32)
        code = (meta[0:1] * CODE + meta[1:2]).astype(jnp.int32) - 1
        turned = jnp.where(code >= half, code - half, code + half)
        code = jnp.where((code >= 0) & (mine == 1), turned, code)
        hot = (iota((places, capacity), 0) == code).astype(F32)
        seen += hot
        total += dot(hot.astype(BF16), block[:capacity, :])
    count = jnp.sum(seen, axis=1, keepdims=True)
    steps = embed_ref.shape[0]
    step_hot = iota((places, steps), 1) == iota((places, steps), 0) % slot_dev + mine * slot_dev
    embed = dot(step_hot.astype(F32).astype(BF16), embed_ref[...])
    tokens = (total / jnp.maximum(count, 1.0) + embed).astype(BF16)
    keep_ref[...] = tokens[:half]
    send_ref[...] = tokens[half:]


def pool_rows(my_slot, time_embed, blocks, capacity, slot_dev):
    width = time_embed.shape[1]
    half = jax.ShapeDtypeStruct((CB * slot_dev // 2, width), BF16)
    return pl.pallas_call(
        functools.partial(pool_kernel, capacity, slot_dev),
        out_shape=[half, half],
        in_specs=[SCALARS] + [WHOLE] * (1 + len(blocks)),
        out_specs=[WHOLE] * 2,
        compiler_params=params(),
        cost_estimate=pl.CostEstimate(
            flops=2 * CB * slot_dev * width * len(blocks) * capacity,
            bytes_accessed=2 * width * (CB * slot_dev + len(blocks) * capacity),
            transcendentals=0,
        ),
        name="pool_rows",
    )(my_slot, time_embed, *blocks)


def weave_kernel(slot_dev, slot_ref, keep_ref, got_ref, out_ref):
    rows, half = out_ref.shape[0], keep_ref.shape[0]
    mine = slot_ref[0]
    row, col = iota((rows, half), 0), iota((rows, half), 1)
    source = col == row // TSTEPS * slot_dev + row % slot_dev
    own = row % TSTEPS // slot_dev == mine
    from_keep = (source & own).astype(F32).astype(BF16)
    from_got = (source & jnp.logical_not(own)).astype(F32).astype(BF16)
    out_ref[...] = (dot(from_keep, keep_ref[...]) + dot(from_got, got_ref[...])).astype(BF16)


def weave_steps(my_slot, keep, got, slot_dev):
    rows, width = 2 * keep.shape[0], keep.shape[1]
    return pl.pallas_call(
        functools.partial(weave_kernel, slot_dev),
        out_shape=jax.ShapeDtypeStruct((rows, width), BF16),
        in_specs=[SCALARS, WHOLE, WHOLE],
        out_specs=WHOLE,
        compiler_params=params(),
        cost_estimate=pl.CostEstimate(
            flops=2 * rows * rows * width, bytes_accessed=4 * rows * width, transcendentals=0
        ),
        name="weave_steps",
    )(my_slot, keep, got)


def head_scale(values, ones):
    square = values * values
    high = square.astype(BF16)
    low = (square - high.astype(F32)).astype(BF16)
    sums = dot(high, ones) + dot(low, ones)
    return (values * lax.rsqrt(sums * (1.0 / HD) + EPS)).astype(BF16)


def layer_kernel(
    heads_width, tok_ref, qkv_ref, out_w_ref, gate_ref, up_ref, down_ref, out_ref, norm_ref, acc_ref, ctx_ref
):
    step = pl.program_id(0)
    rows = tok_ref.shape[0]

    @pl.when(step == 0)
    def attention():
        tokens = tok_ref[...].astype(F32)
        scale = lax.rsqrt(jnp.mean(tokens * tokens, axis=1, keepdims=True) + EPS)
        normed = (tokens * scale).astype(BF16)
        norm_ref[...] = normed
        projected = dot(normed, qkv_ref[...])
        same_head = iota((LANES, LANES), 0) // HD == iota((LANES, LANES), 1) // HD
        ones = same_head.astype(F32).astype(BF16)
        group = LANES
        first = iota((group, LANES), 1) < HD
        row, col = iota((2 * group, group), 0), iota((2 * group, group), 1)
        same_cell = row % group // TSTEPS == col // TSTEPS
        for pair in range(heads_width // LANES):
            at = pair * LANES
            query = head_scale(projected[:, at : at + LANES], ones)
            key = head_scale(projected[:, heads_width + at : heads_width + at + LANES], ones)
            value = projected[:, 2 * heads_width + at : 2 * heads_width + at + LANES].astype(BF16)
            for begin in range(0, rows, group):
                q = query[begin : begin + group]
                k = key[begin : begin + group]
                v = value[begin : begin + group]
                both = jnp.concatenate(
                    [jnp.where(first, q, jnp.zeros_like(q)), jnp.where(first, jnp.zeros_like(q), q)], axis=0
                )
                scores = dot_t(both, k) * HD ** (-0.5)
                expo = jnp.where(same_cell, jnp.exp(scores), 0.0)
                probs = (expo / jnp.sum(expo, axis=1, keepdims=True)).astype(BF16)
                mixed = dot(probs, v)
                ctx = jnp.where(first, mixed[:group], mixed[group:])
                ctx_ref[begin : begin + group, at : at + LANES] = ctx.astype(BF16)
        acc_ref[...] = dot_t(ctx_ref[...], out_w_ref[...])

    @pl.when(step > 0)
    def gated():
        normed = norm_ref[...]
        gate = dot(normed, gate_ref[...])
        up = dot(normed, up_ref[...])
        hidden = (gate / (1.0 + jnp.exp(-gate)) * up).astype(BF16)
        acc_ref[...] += dot_t(hidden, down_ref[...])

    @pl.when(step == pl.num_programs(0) - 1)
    def finish():
        out_ref[...] = acc_ref[...].astype(out_ref.dtype)


def layer(tokens, weights, heads_width, hidden_width, out_type):
    rows, width = tokens.shape
    chunk = heads_width
    steps = hidden_width // chunk
    gate_at = 3
    up_at = gate_at + steps
    out_at = up_at + steps
    down_at = out_at + 1

    def chunk_spec(at):
        return pl.BlockSpec((width, chunk), lambda i: (0, at + jnp.maximum(i - 1, 0)))

    flops = 2 * rows * width * weights.shape[1]
    return pl.pallas_call(
        functools.partial(layer_kernel, heads_width),
        out_shape=jax.ShapeDtypeStruct((rows, width), out_type),
        grid=(1 + steps,),
        in_specs=[
            pl.BlockSpec((rows, width), lambda i: (0, 0)),
            pl.BlockSpec((width, 3 * chunk), lambda i: (0, 0)),
            pl.BlockSpec((width, chunk), lambda i: (0, out_at)),
            chunk_spec(gate_at),
            chunk_spec(up_at),
            chunk_spec(down_at),
        ],
        out_specs=pl.BlockSpec((rows, width), lambda i: (0, 0)),
        scratch_shapes=[
            pltpu.VMEM((rows, width), BF16),
            pltpu.VMEM((rows, width), F32),
            pltpu.VMEM((rows, heads_width), BF16),
        ],
        compiler_params=params(dimension_semantics=("arbitrary",)),
        cost_estimate=pl.CostEstimate(
            flops=flops, bytes_accessed=2 * weights.size + 4 * rows * width, transcendentals=rows * hidden_width
        ),
        name="layer",
    )(tokens, weights, weights, weights, weights, weights)


def gather_weights(w_qkv, w_out, w_gate_up, w_down):
    n_share = lax.axis_size("groups") * lax.axis_size("slots")
    which = lax.axis_index("groups") * lax.axis_size("slots") + lax.axis_index("slots")
    parts = []
    for weight in (w_qkv, w_gate_up, w_out.T, w_down.T):
        share = weight.shape[0] // n_share
        mine = lax.dynamic_slice_in_dim(weight, which * share, share, 0)
        parts.append(mine.reshape(share, -1))
    mine = jnp.concatenate(parts, axis=1)
    return lax.all_gather(mine, ("cells", "groups", "slots"), axis=0, tiled=True)


def tokens_by_permutes(ahead, position, obs_feat, time_embed, my_slot, capacity, slot_dev):
    n_owners = lax.axis_size("cells") * lax.axis_size("mp")
    blocks = place_rows(ahead, position, obs_feat, n_owners, capacity)

    def shift(values, step):
        pairs = [(j, (j + step) % n_owners) for j in range(n_owners)]
        return lax.ppermute(values, ("cells", "mp"), pairs)

    got = [blocks[0]] + [shift(blocks[step], step) for step in range(1, n_owners)]
    keep, send = pool_rows(my_slot.reshape(1), time_embed, got, capacity, slot_dev)
    other = lax.ppermute(send, "slots", [(0, 1), (1, 0)])
    return weave_steps(my_slot.reshape(1), keep, other, slot_dev)


def tokens_by_exchanges(ahead, position, obs_feat, time_embed, my_slot, capacity, slot_dev):
    n_slots = lax.axis_size("slots")
    n_owners = lax.axis_size("cells") * lax.axis_size("mp")
    my_owner = lax.axis_index("cells") * lax.axis_size("mp") + lax.axis_index("mp")
    rows, width = obs_feat.shape
    owners = jnp.arange(n_owners, dtype=jnp.int32)
    owner = jnp.where(ahead < n_owners, (ahead + my_owner) % n_owners, n_owners)
    owner_hot = (owner[:, None] == owners[None, :]).astype(F32)
    row_ids = jnp.arange(rows, dtype=jnp.int32)
    lower = (row_ids[None, :] <= row_ids[:, None]).astype(BF16)
    running = dot(lower, owner_hot.astype(BF16))
    rank = jnp.sum(running * owner_hot, axis=1).astype(jnp.int32) - 1
    place = jnp.where(owner < n_owners, owner * capacity + rank, n_owners * capacity)
    place_ids = jnp.arange(n_owners * capacity, dtype=jnp.int32)
    taken = place_ids[:, None] == place[None, :]
    send_feat = dot(taken.astype(BF16), obs_feat).astype(BF16).reshape(n_owners, capacity, width)
    send_code = jnp.sum(jnp.where(taken, position[None, :] + 1, 0), axis=1).reshape(n_owners, capacity)
    axes = ("cells", "mp")
    got_feat = lax.all_to_all(send_feat, axes, split_axis=0, concat_axis=0, tiled=True).reshape(-1, width)
    got_code = lax.all_to_all(send_code, axes, split_axis=0, concat_axis=0, tiled=True).reshape(-1) - 1
    hot = (jnp.arange(CB * slot_dev, dtype=jnp.int32)[:, None] == got_code[None, :]).astype(BF16)
    count = jnp.sum(hot.astype(F32), axis=1)
    pooled = dot(hot, got_feat) / jnp.maximum(count, 1.0)[:, None]
    embed = lax.dynamic_slice_in_dim(time_embed, my_slot * slot_dev, slot_dev, 0).astype(F32)
    tokens = (pooled.reshape(CB, slot_dev, width) + embed[None]).astype(BF16)
    grid = tokens.reshape(n_slots, CB // n_slots, slot_dev, width)
    grid = lax.all_to_all(grid, "slots", split_axis=0, concat_axis=2, tiled=True)
    return grid.reshape(-1, width)


def on_device(obs_feat, obs_cell, obs_slot, obs_count, time_embed, w_qkv, w_out, w_gate_up, w_down):
    n_cells = lax.axis_size("cells")
    n_slots = lax.axis_size("slots")
    n_mp = lax.axis_size("mp")
    n_owners = n_cells * n_mp
    rows, width = obs_feat.shape
    capacity = 3 * rows // n_owners
    quarter = CB // n_slots
    slot_dev = TSTEPS // n_slots
    my_owner = lax.axis_index("cells") * n_mp + lax.axis_index("mp")
    my_slot = lax.axis_index("slots")
    weights = gather_weights(w_qkv, w_out, w_gate_up, w_down)

    valid = jnp.arange(rows, dtype=jnp.int32) < obs_count[0]
    owner = obs_cell // (quarter * n_mp * n_slots) * n_mp + obs_cell // quarter % n_mp
    ahead = jnp.where(valid, (owner - my_owner + n_owners) % n_owners, n_owners)
    local = obs_cell // (quarter * n_mp) % n_slots * quarter + obs_cell % quarter
    position = local * slot_dev + obs_slot
    route = tokens_by_permutes if n_slots == 2 and capacity % 16 == 0 else tokens_by_exchanges
    tokens = route(ahead, position, obs_feat, time_embed, my_slot, capacity, slot_dev)

    swap = [(0, 1), (1, 0)]
    heads_width, hidden_width = w_qkv.shape[2], w_gate_up.shape[2]
    partner = lax.ppermute(tokens, "mp", swap)
    for_partner = layer(partner, weights, heads_width, hidden_width, BF16)
    from_partner = lax.ppermute(for_partner, "mp", swap)
    own = layer(tokens, weights, heads_width, hidden_width, F32)
    mixed = tokens.astype(F32) + own + from_partner.astype(F32)
    return mixed.astype(BF16).reshape(quarter, TSTEPS, width)


def solution(mesh):
    placed = (
        P(("groups", "cells", "slots", "mp"), None),
        P(("groups", "cells", "slots", "mp")),
        P(("groups", "cells", "slots", "mp")),
        P(("groups", "cells", "slots", "mp")),
        P(),
        P("cells", None, "mp"),
        P("mp", "cells"),
        P("cells", None, "mp"),
        P("mp", "cells"),
    )
    return jax.shard_map(
        on_device,
        mesh=mesh,
        in_specs=placed,
        out_specs=P(("groups", "cells", "slots", "mp"), None, None),
        check_vma=False,
    )
```

time: 325 us -> 209 us (0.64)
  matrix products: 53.1 us -> 0 us
  waiting for transfers between devices: 176 us -> 125 us
  Pallas kernels: 0 us -> 29.4 us
  local copies, waits for them, and re-layouts: 28.7 us -> 4.24 us
  blocking collectives: 18.6 us -> 0 us
  starting transfers between devices: 23.9 us -> 33.8 us
  other arithmetic: 9.85 us -> 2 us
    all_gather x4 -> x1, waiting for transfers between devices: 149 us -> 81.9 us  [gather_weights(): lax.all_gather(mine, ('cells', 'groups', 'slots'), axis=0, tiled=True)]
    dot_general x22 -> x0, matrix products: 53.1 us -> none  [the longest x2 11.7 us: on_device(): jnp.dot(flat_rows, full_qkv[rows], preferred_element_type=jnp.float32)]
    pallas_call x0 -> x5, Pallas kernels: none -> 29.4 us  [the longest x2 24.8 us: layer(): pl.pallas_call(functools.partial(layer_kernel, heads_width), out_shape=ja...]
    all_to_all x1 -> x0, blocking collectives: 18.6 us -> none  [on_device(): lax.all_to_all(token_grid, 'slots', split_axis=0, concat_axis=2, tiled=True)]
    ppermute x0 -> x3, waiting for transfers between devices: none -> 13.1 us  [the longest x1 11.1 us: tokens_by_permutes(): other = lax.ppermute(send, 'slots', [(0, 1), (1, 0)])]
    ppermute x0 -> x3, starting transfers between devices: none -> 6.81 us  [the longest x1 5.18 us: on_device(): partner = lax.ppermute(tokens, 'mp', swap)]
    reduce_sum x7 -> x0, other arithmetic: 6.81 us -> none  [the longest x3 5.86 us: rms_scale(): jnp.mean(values * values, axis=-1, keepdims=True) + EPS]
    dot_general x5 -> x0, local copies, waits for them, and re-layouts: 6.8 us -> none  [the longest x3 5.52 us: on_device(): jnp.dot(flat_rows, full_qkv[rows], preferred_element_type=jnp.float32)]
  transfers between devices with their start and end apart: 18 -> 11, of which waited for: 6 -> 7; matrix products, arithmetic and copies ran while one was open for 25% -> 0% of each run, Pallas kernels for 0% -> 8%
where the time goes in v2:
time: 209 us
  waiting for transfers between devices  125 us (60%)
  starting transfers between devices  33.8 us (16%)
  Pallas kernels  29.4 us (14%)
  between operations  14.2 us (7%)
  local copies, waits for them, and re-layouts  4.24 us (2%)
    all_gather x1, waiting for transfers between devices, gather_weights(): lax.all_gather(mine, ('cells', 'groups', 'slots'), axis=0, tiled=True)  81.9 us
    ppermute x7, waiting for transfers between devices, shift(): return lax.ppermute(values, ('cells', 'mp'), pairs)  30.3 us
    ppermute x7, starting transfers between devices, shift(): return lax.ppermute(values, ('cells', 'mp'), pairs)  27 us
    pallas_call x2, Pallas kernels, layer(): pl.pallas_call(functools.partial(layer_kernel, heads_width), out_shape=ja...  24.8 us
    ppermute x1, waiting for transfers between devices, tokens_by_permutes(): other = lax.ppermute(send, 'slots', [(0, 1), (1, 0)])  11.1 us
    ppermute x1, starting transfers between devices, on_device(): partner = lax.ppermute(tokens, 'mp', swap)  5.18 us
  transfers between devices with their start and end apart: 11, of which 7 were waited for; matrix products, arithmetic and copies ran while one was open for 0% of the time, Pallas kernels for 8%

profile of v2, /device:TPU:0, one launch (start us, length us, event | category | flops | bytes accessed | tf_op | source)
XLA Modules:
  0.0 208.9 jit_solution(5114954192579832587)
XLA Ops:
  6.5 0.0 copy-start
  6.5 0.0 all-gather.2.cloned.1.call-start
  6.5 1.3 copy-done
  7.8 0.2 constant_dynamic-slice_fusion
  8.1 0.9 dynamic-slice_bitcast_fusion.1
  9.0 0.0 copy-start.3
  9.0 0.0 copy-start.4
  9.0 0.0 copy-start.1
  9.0 1.0 dynamic-slice_bitcast_fusion
  10.0 0.8 dynamic-slice_bitcast_fusion.2
  10.8 0.9 pad_maximum_fusion
  11.7 0.0 all-gather.2.cloned.1.call-update
  12.3 0.0 copy-done.3
  12.4 0.0 copy-done.4
  12.4 0.0 copy-done.1
  12.4 0.0 copy-start.2
  12.4 2.0 place_rows.1
  14.4 0.5 collective-permute-start
  14.9 2.6 %collective-permute-start.1 = (bf16[208,768]{1,0:T(8,128)(2,1)S(1)}, bf16[208,768]{1,0:T(8,128)(2,1)S(1)}, u32[]{:S(2)}, u32[]{:S(2)}) collective-permute-start(bf16[208,768]{1,0:T(8,128)(2,1)S(1)} %get-tuple-element.17), channel_id=1, source_target_pairs={{0,4},{1,5},{4,8},{5,9},{8,12},{9,13},{12,0},{13,1},{2,6},{3,7},{6... | collective-permute-start | bytes 958472 | tf_op jit(solution)/shard_map/ppermute | solution.py:265
  17.5 2.5 %collective-permute-start.2 = (bf16[208,768]{1,0:T(8,128)(2,1)S(1)}, bf16[208,768]{1,0:T(8,128)(2,1)S(1)}, u32[]{:S(2)}, u32[]{:S(2)}) collective-permute-start(bf16[208,768]{1,0:T(8,128)(2,1)S(1)} %get-tuple-element.18), channel_id=1, source_target_pairs={{0,5},{1,8},{4,9},{5,12},{8,13},{9,0},{12,1},{13,4},{2,7},{3,10},{... | collective-permute-start | bytes 958472 | tf_op jit(solution)/shard_map/ppermute | solution.py:265
  20.1 1.2 collective-permute-start.3
  21.3 1.2 collective-permute-start.4
  22.5 3.8 %collective-permute-done.refs_1_ = bf16[208,768]{1,0:T(8,128)(2,1)S(1)} collective-permute-done((bf16[208,768]{1,0:T(8,128)(2,1)S(1)}, bf16[208,768]{1,0:T(8,128)(2,1)S(1)}, u32[]{:S(2)}, u32[]{:S(2)}) %collective-permute-start) | collective-permute-done | bytes 319520 | tf_op jit(solution)/shard_map/ppermute | solution.py:265
  26.3 2.4 %collective-permute-start.5 = (bf16[208,768]{1,0:T(8,128)(2,1)S(1)}, bf16[208,768]{1,0:T(8,128)(2,1)S(1)}, u32[]{:S(2)}, u32[]{:S(2)}) collective-permute-start(bf16[208,768]{1,0:T(8,128)(2,1)S(1)} %get-tuple-element.21), channel_id=1, source_target_pairs={{0,12},{1,13},{4,0},{5,1},{8,4},{9,5},{12,8},{13,9},{2,14},{3,15},... | collective-permute-start | bytes 958472 | tf_op jit(solution)/shard_map/ppermute | solution.py:265
  28.7 0.0 collective-permute-done.1.refs_2_
  28.8 16.5 %collective-permute-start.6 = (bf16[208,768]{1,0:T(8,128)(2,1)S(1)}, bf16[208,768]{1,0:T(8,128)(2,1)S(1)}, u32[]{:S(2)}, u32[]{:S(2)}) collective-permute-start(bf16[208,768]{1,0:T(8,128)(2,1)S(1)} %get-tuple-element.22), channel_id=1, source_target_pairs={{0,13},{1,0},{4,1},{5,4},{8,5},{9,8},{12,9},{13,12},{2,15},{3,2},{... | collective-permute-start | bytes 958472 | tf_op jit(solution)/shard_map/ppermute | solution.py:265
  45.2 21.8 %collective-permute-done.2.refs_3_ = bf16[208,768]{1,0:T(8,128)(2,1)S(1)} collective-permute-done((bf16[208,768]{1,0:T(8,128)(2,1)S(1)}, bf16[208,768]{1,0:T(8,128)(2,1)S(1)}, u32[]{:S(2)}, u32[]{:S(2)}) %collective-permute-start.2) | collective-permute-done | bytes 319520 | tf_op jit(solution)/shard_map/ppermute | solution.py:265
  67.0 0.2 collective-permute-done.3.refs_4_
  67.2 0.0 collective-permute-done.4.refs_5_
  67.2 0.0 collective-permute-done.5.refs_6_
  67.2 4.5 %collective-permute-done.6.refs_7_ = bf16[208,768]{1,0:T(8,128)(2,1)S(1)} collective-permute-done((bf16[208,768]{1,0:T(8,128)(2,1)S(1)}, bf16[208,768]{1,0:T(8,128)(2,1)S(1)}, u32[]{:S(2)}, u32[]{:S(2)}) %collective-permute-start.6) | collective-permute-done | bytes 319520 | tf_op jit(solution)/shard_map/ppermute | solution.py:265
  71.7 0.0 copy-done.2
  71.7 2.1 pool_rows.1
  73.8 1.6 collective-permute-start.7
  75.3 11.1 %collective-permute-done.7.got_ref = bf16[256,768]{1,0:T(8,128)(2,1)S(1)} collective-permute-done((bf16[256,768]{1,0:T(8,128)(2,1)S(1)}, bf16[256,768]{1,0:T(8,128)(2,1)S(1)}, u32[]{:S(2)}, u32[]{:S(2)}) %collective-permute-start.7) | collective-permute-done | bytes 393248 | tf_op jit(solution)/shard_map/ppermute | solution.py:269
  86.5 0.6 weave_steps.1.tok_ref
  87.1 5.2 %collective-permute-start.8 = (bf16[512,768]{1,0:T(8,128)(2,1)S(1)}, bf16[512,768]{1,0:T(8,128)(2,1)S(1)}, u32[]{:S(2)}, u32[]{:S(2)}) collective-permute-start(bf16[512,768]{1,0:T(8,128)(2,1)S(1)} %weave_steps.1.tok_ref), channel_id=1, source_target_pairs={{0,1},{1,0},{2,3},{3,2},{4,5},{5,4},{6,7},{7,6},{8,9},{9,8},{10,11... | collective-permute-start | bytes 2359304 | tf_op jit(solution)/shard_map/ppermute | solution.py:326
  92.3 1.9 collective-permute-done.8.tok_ref
  94.2 81.9 %all-gather.2.cloned.1.call-done.qkv_ref.out_w_ref.gate_ref.up_ref.down_ref = bf16[768,6144]{1,0:T(8,128)(2,1)} async-done(((bf16[48,6144]{1,0:T(8,128)(2,1)}), bf16[768,6144]{1,0:T(8,128)(2,1)}) %all-gather.2.cloned.1.call-update) | async-done | bytes 9437200 | tf_op jit(solution)/shard_map/all_gather | solution.py:256
  176.1 12.4 %layer.3 = bf16[512,768]{1,0:T(8,128)(2,1)S(1)} custom-call(bf16[512,768]{1,0:T(8,128)(2,1)S(1)} %collective-permute-done.8.tok_ref, bf16[768,6144]{1,0:T(8,128)(2,1)} %all-gather.2.cloned.1.call-done.qkv_ref.out_w_ref.gate_ref.up_ref.down_ref, bf16[768,6144]{1,0:T(8,128)(2,1)} %all-gather.2.cloned.1.call-done.qkv_ref.out_w_ref.gate_ref.up_ref.down_ref, ...), custom_call_target="tpu_custom_call" | custom-call | flops 4831838208 | bytes 11010048 | tf_op jit(solution)/shard_map/layer/pallas_call | solution.py:221
  188.4 0.1 collective-permute-start.9
  188.5 12.4 %layer.2 = f32[512,768]{1,0:T(8,128)S(1)} custom-call(bf16[512,768]{1,0:T(8,128)(2,1)S(1)} %weave_steps.1.tok_ref, bf16[768,6144]{1,0:T(8,128)(2,1)} %all-gather.2.cloned.1.call-done.qkv_ref.out_w_ref.gate_ref.up_ref.down_ref, bf16[768,6144]{1,0:T(8,128)(2,1)} %all-gather.2.cloned.1.call-done.qkv_ref.out_w_ref.gate_ref.up_ref.down_ref, ...), custom_call_target="tpu_custom_call" | custom-call | flops 4831838208 | bytes 11010048 | tf_op jit(solution)/shard_map/layer/pallas_call | solution.py:221
  200.9 0.0 collective-permute-done.9
  200.9 1.1 fusion
  (3 shorter events, 0.1 us)
Async XLA Ops:
  6.5 1.3 copy-start
  6.5 169.5 %all-gather.2.cloned.1.call-start = ((), (), s32[]{:S(2)}) async-start(), calls=%async_computation | async-start | bytes 10027008 | tf_op jit(solution)/shard_map/all_gather | solution.py:256
  9.0 3.4 %copy-start.3 = (s32[512]{0:T(512)S(1)}, s32[512]{0:T(512)}, u32[]{:S(2)}) copy-start(s32[512]{0:T(512)} %param.11) | copy-start | bytes 6148
  9.0 3.4 %copy-start.4 = (s32[512]{0:T(512)S(1)}, s32[512]{0:T(512)}, u32[]{:S(2)}) copy-start(s32[512]{0:T(512)} %param.10) | copy-start | bytes 6148
  9.0 3.4 %copy-start.1 = (bf16[512,768]{1,0:T(8,128)(2,1)S(1)}, bf16[512,768]{1,0:T(8,128)(2,1)}, u32[]{:S(2)}) copy-start(bf16[512,768]{1,0:T(8,128)(2,1)} %feat_ref.1) | copy-start | bytes 2359300
  12.4 59.3 %copy-start.2 = (bf16[8,768]{1,0:T(8,128)(2,1)S(1)}, bf16[8,768]{1,0:T(8,128)(2,1)}, u32[]{:S(2)}) copy-start(bf16[8,768]{1,0:T(8,128)(2,1)} %embed_ref.1) | copy-start | bytes 36868
  14.4 11.9 %collective-permute-start = (bf16[208,768]{1,0:T(8,128)(2,1)S(1)}, bf16[208,768]{1,0:T(8,128)(2,1)S(1)}, u32[]{:S(2)}, u32[]{:S(2)}) collective-permute-start(bf16[208,768]{1,0:T(8,128)(2,1)S(1)} %get-tuple-element.16), channel_id=1, source_target_pairs={{0,1},{1,4},{4,5},{5,8},{8,9},{9,12},{12,13},{13,0},{2,3},{3,6},{6... | collective-permute-start | bytes 958472 | tf_op jit(solution)/shard_map/ppermute | solution.py:265
  14.9 13.8 %collective-permute-start.1 = (bf16[208,768]{1,0:T(8,128)(2,1)S(1)}, bf16[208,768]{1,0:T(8,128)(2,1)S(1)}, u32[]{:S(2)}, u32[]{:S(2)}) collective-permute-start(bf16[208,768]{1,0:T(8,128)(2,1)S(1)} %get-tuple-element.17), channel_id=1, source_target_pairs={{0,4},{1,5},{4,8},{5,9},{8,12},{9,13},{12,0},{13,1},{2,6},{3,7},{6... | collective-permute-start | bytes 958472 | tf_op jit(solution)/shard_map/ppermute | solution.py:265
  17.5 49.5 %collective-permute-start.2 = (bf16[208,768]{1,0:T(8,128)(2,1)S(1)}, bf16[208,768]{1,0:T(8,128)(2,1)S(1)}, u32[]{:S(2)}, u32[]{:S(2)}) collective-permute-start(bf16[208,768]{1,0:T(8,128)(2,1)S(1)} %get-tuple-element.18), channel_id=1, source_target_pairs={{0,5},{1,8},{4,9},{5,12},{8,13},{9,0},{12,1},{13,4},{2,7},{3,10},{... | collective-permute-start | bytes 958472 | tf_op jit(solution)/shard_map/ppermute | solution.py:265
  20.1 47.1 %collective-permute-start.3 = (bf16[208,768]{1,0:T(8,128)(2,1)S(1)}, bf16[208,768]{1,0:T(8,128)(2,1)S(1)}, u32[]{:S(2)}, u32[]{:S(2)}) collective-permute-start(bf16[208,768]{1,0:T(8,128)(2,1)S(1)} %get-tuple-element.19), channel_id=1, source_target_pairs={{0,8},{1,9},{4,12},{5,13},{8,0},{9,1},{12,4},{13,5},{2,10},{3,11},... | collective-permute-start | bytes 958472 | tf_op jit(solution)/shard_map/ppermute | solution.py:265
  21.3 45.9 %collective-permute-start.4 = (bf16[208,768]{1,0:T(8,128)(2,1)S(1)}, bf16[208,768]{1,0:T(8,128)(2,1)S(1)}, u32[]{:S(2)}, u32[]{:S(2)}) collective-permute-start(bf16[208,768]{1,0:T(8,128)(2,1)S(1)} %get-tuple-element.20), channel_id=1, source_target_pairs={{0,9},{1,12},{4,13},{5,0},{8,1},{9,4},{12,5},{13,8},{2,11},{3,14},... | collective-permute-start | bytes 958472 | tf_op jit(solution)/shard_map/ppermute | solution.py:265
  26.3 40.9 %collective-permute-start.5 = (bf16[208,768]{1,0:T(8,128)(2,1)S(1)}, bf16[208,768]{1,0:T(8,128)(2,1)S(1)}, u32[]{:S(2)}, u32[]{:S(2)}) collective-permute-start(bf16[208,768]{1,0:T(8,128)(2,1)S(1)} %get-tuple-element.21), channel_id=1, source_target_pairs={{0,12},{1,13},{4,0},{5,1},{8,4},{9,5},{12,8},{13,9},{2,14},{3,15},... | collective-permute-start | bytes 958472 | tf_op jit(solution)/shard_map/ppermute | solution.py:265
  28.8 42.9 %collective-permute-start.6 = (bf16[208,768]{1,0:T(8,128)(2,1)S(1)}, bf16[208,768]{1,0:T(8,128)(2,1)S(1)}, u32[]{:S(2)}, u32[]{:S(2)}) collective-permute-start(bf16[208,768]{1,0:T(8,128)(2,1)S(1)} %get-tuple-element.22), channel_id=1, source_target_pairs={{0,13},{1,0},{4,1},{5,4},{8,5},{9,8},{12,9},{13,12},{2,15},{3,2},{... | collective-permute-start | bytes 958472 | tf_op jit(solution)/shard_map/ppermute | solution.py:265
  73.8 12.7 %collective-permute-start.7 = (bf16[256,768]{1,0:T(8,128)(2,1)S(1)}, bf16[256,768]{1,0:T(8,128)(2,1)S(1)}, u32[]{:S(2)}, u32[]{:S(2)}) collective-permute-start(bf16[256,768]{1,0:T(8,128)(2,1)S(1)} %get-tuple-element.24), channel_id=1, source_target_pairs={{0,2},{2,0},{1,3},{3,1},{4,6},{6,4},{5,7},{7,5},{8,10},{10,8},{9,1... | collective-permute-start | bytes 1179656 | tf_op jit(solution)/shard_map/ppermute | solution.py:269
  87.1 7.1 %collective-permute-start.8 = (bf16[512,768]{1,0:T(8,128)(2,1)S(1)}, bf16[512,768]{1,0:T(8,128)(2,1)S(1)}, u32[]{:S(2)}, u32[]{:S(2)}) collective-permute-start(bf16[512,768]{1,0:T(8,128)(2,1)S(1)} %weave_steps.1.tok_ref), channel_id=1, source_target_pairs={{0,1},{1,0},{2,3},{3,2},{4,5},{5,4},{6,7},{7,6},{8,9},{9,8},{10,11... | collective-permute-start | bytes 2359304 | tf_op jit(solution)/shard_map/ppermute | solution.py:326
  188.4 12.5 %collective-permute-start.9 = (bf16[512,768]{1,0:T(8,128)(2,1)S(1)}, bf16[512,768]{1,0:T(8,128)(2,1)S(1)}, u32[]{:S(2)}, u32[]{:S(2)}) collective-permute-start(bf16[512,768]{1,0:T(8,128)(2,1)S(1)} %layer.3), channel_id=1, source_target_pairs={{0,1},{1,0},{2,3},{3,2},{4,5},{5,4},{6,7},{7,6},{8,9},{9,8},{10,11... | collective-permute-start | bytes 2359304 | tf_op jit(solution)/shard_map/ppermute | solution.py:328
Sparse Core Ops, SparseCore 0:
  11.8 164.2 all-gather.1

commit v3 on v2

v3 whole, which is shorter than its diff:
```python
import functools

import jax
import jax.numpy as jnp
from jax import lax
from jax.experimental import pallas as pl
from jax.experimental.pallas import tpu as pltpu
from jax.sharding import PartitionSpec as P

HD = 64
TSTEPS = 8
CB = 128
EPS = 1e-06

META_ROWS = 16
CODE = 32
LANES = 128
VMEM_LIMIT = 48 * 1024 * 1024
F32 = jnp.float32
BF16 = jnp.bfloat16
WHOLE = pl.BlockSpec(memory_space=pltpu.VMEM)
SCALARS = pl.BlockSpec(memory_space=pltpu.SMEM)


def iota(shape, axis):
    return lax.broadcasted_iota(jnp.int32, shape, axis)


def dot(left, right):
    return jnp.dot(left, right, preferred_element_type=F32)


def dot_t(left, right):
    return lax.dot_general(left, right, (((1,), (1,)), ((), ())), preferred_element_type=F32)


def params():
    return pltpu.CompilerParams(vmem_limit_bytes=VMEM_LIMIT)


def place_kernel(capacity, owner_ref, position_ref, feat_ref, out_ref):
    n_owners, rows = out_ref.shape[0], feat_ref.shape[0]
    owner = owner_ref[...]
    owner_hot = (iota((n_owners, rows), 0) == owner).astype(F32)
    upper = (iota((rows, rows), 0) <= iota((rows, rows), 1)).astype(BF16)
    running = dot(owner_hot.astype(BF16), upper)
    rank = jnp.sum(running * owner_hot, axis=0, keepdims=True).astype(jnp.int32) - 1
    code = position_ref[...] + 1
    line = iota((META_ROWS, rows), 0)
    meta = jnp.where(line == 0, code // CODE, jnp.where(line == 1, code % CODE, 0))
    meta = meta.astype(F32).astype(BF16)
    feat = feat_ref[...]
    for block in range(n_owners):
        place = jnp.where(owner == block, rank, -1)
        taken = (iota((capacity, rows), 0) == place).astype(F32).astype(BF16)
        out_ref[block, :capacity, :] = dot(taken, feat).astype(BF16)
        out_ref[block, capacity:, :] = jnp.zeros((META_ROWS, feat.shape[1]), BF16)
        out_ref[block, capacity:, :capacity] = dot_t(meta, taken).astype(BF16)


def place_rows(owner, position, obs_feat, n_owners, capacity):
    rows, width = obs_feat.shape
    return pl.pallas_call(
        functools.partial(place_kernel, capacity),
        out_shape=jax.ShapeDtypeStruct((n_owners, capacity + META_ROWS, width), BF16),
        in_specs=[WHOLE] * 3,
        out_specs=WHOLE,
        compiler_params=params(),
        cost_estimate=pl.CostEstimate(
            flops=2 * rows * width * n_owners * capacity,
            bytes_accessed=2 * width * (rows + n_owners * capacity),
            transcendentals=0,
        ),
        name="place_rows",
    )(owner.reshape(1, rows), position.reshape(1, rows), obs_feat)


def pool_kernel(capacity, slot_dev, slot_ref, embed_ref, got_ref, keep_ref, send_ref):
    half = keep_ref.shape[0]
    places = 2 * half
    mine = slot_ref[0]
    total = jnp.zeros((places, keep_ref.shape[1]), F32)
    seen = jnp.zeros((places, capacity), F32)
    for block in range(got_ref.shape[0]):
        meta = got_ref[block, capacity:, :capacity].astype(F32)
        code = (meta[0:1] * CODE + meta[1:2]).astype(jnp.int32) - 1
        turned = jnp.where(code >= half, code - half, code + half)
        code = jnp.where((code >= 0) & (mine == 1), turned, code)
        hot = (iota((places, capacity), 0) == code).astype(F32)
        seen += hot
        total += dot(hot.astype(BF16), got_ref[block, :capacity, :])
    count = jnp.sum(seen, axis=1, keepdims=True)
    steps = embed_ref.shape[0]
    step_hot = iota((places, steps), 1) == iota((places, steps), 0) % slot_dev + mine * slot_dev
    embed = dot(step_hot.astype(F32).astype(BF16), embed_ref[...])
    tokens = (total / jnp.maximum(count, 1.0) + embed).astype(BF16)
    keep_ref[...] = tokens[:half]
    send_ref[...] = tokens[half:]


def pool_rows(my_slot, time_embed, got, capacity, slot_dev):
    width = time_embed.shape[1]
    half = jax.ShapeDtypeStruct((CB * slot_dev // 2, width), BF16)
    return pl.pallas_call(
        functools.partial(pool_kernel, capacity, slot_dev),
        out_shape=[half, half],
        in_specs=[SCALARS, WHOLE, WHOLE],
        out_specs=[WHOLE] * 2,
        compiler_params=params(),
        cost_estimate=pl.CostEstimate(
            flops=2 * CB * slot_dev * got.size, bytes_accessed=2 * got.size, transcendentals=0
        ),
        name="pool_rows",
    )(my_slot, time_embed, got)


def weave_kernel(slot_dev, slot_ref, order_ref, keep_ref, got_ref, out_ref):
    rows, width = out_ref.shape
    half = keep_ref.shape[0]
    mine = slot_ref[0]
    row, col = iota((rows, half), 0), iota((rows, half), 1)
    source = col == row // TSTEPS * slot_dev + row % slot_dev
    own = row % TSTEPS // slot_dev == mine
    from_keep = (source & own).astype(F32).astype(BF16)
    from_got = (source & jnp.logical_not(own)).astype(F32).astype(BF16)
    tokens = (dot(from_keep, keep_ref[...]) + dot(from_got, got_ref[...])).astype(BF16)
    move = (iota((width, width), 0) == order_ref[...]).astype(F32).astype(BF16)
    out_ref[...] = dot(tokens, move).astype(BF16)


def weave_steps(my_slot, order, keep, got, slot_dev):
    rows, width = 2 * keep.shape[0], keep.shape[1]
    return pl.pallas_call(
        functools.partial(weave_kernel, slot_dev),
        out_shape=jax.ShapeDtypeStruct((rows, width), BF16),
        in_specs=[SCALARS] + [WHOLE] * 3,
        out_specs=WHOLE,
        compiler_params=params(),
        cost_estimate=pl.CostEstimate(
            flops=2 * rows * width * (rows + width), bytes_accessed=4 * rows * width, transcendentals=0
        ),
        name="weave_steps",
    )(my_slot, order.reshape(1, width), keep, got)


def head_scale(values, ones):
    square = values * values
    high = square.astype(BF16)
    low = (square - high.astype(F32)).astype(BF16)
    sums = dot(high, ones) + dot(low, ones)
    return (values * lax.rsqrt(sums * (1.0 / HD) + EPS)).astype(BF16)


def attention(normed, weight, heads_width, ctx_ref):
    rows = normed.shape[0]
    projected = dot(normed, weight)
    same_head = iota((LANES, LANES), 0) // HD == iota((LANES, LANES), 1) // HD
    ones = same_head.astype(F32).astype(BF16)
    group = LANES
    first = iota((group, LANES), 1) < HD
    row, col = iota((2 * group, group), 0), iota((2 * group, group), 1)
    same_cell = row % group // TSTEPS == col // TSTEPS
    for pair in range(heads_width // LANES):
        at = pair * LANES
        query = head_scale(projected[:, at : at + LANES], ones)
        key = head_scale(projected[:, heads_width + at : heads_width + at + LANES], ones)
        value = projected[:, 2 * heads_width + at : 2 * heads_width + at + LANES].astype(BF16)
        for begin in range(0, rows, group):
            q = query[begin : begin + group]
            k = key[begin : begin + group]
            v = value[begin : begin + group]
            none = jnp.zeros_like(q)
            both = jnp.concatenate([jnp.where(first, q, none), jnp.where(first, none, q)], axis=0)
            scores = dot_t(both, k) * HD ** (-0.5)
            expo = jnp.where(same_cell, jnp.exp(scores), 0.0)
            probs = (expo / jnp.sum(expo, axis=1, keepdims=True)).astype(BF16)
            mixed = dot(probs, v)
            ctx = jnp.where(first, mixed[:group], mixed[group:])
            ctx_ref[begin : begin + group, at : at + LANES] = ctx.astype(BF16)


def gated(normed, gate_w, up_w, down_w):
    gate = dot(normed, gate_w)
    up = dot(normed, up_w)
    hidden = (gate / (1.0 + jnp.exp(-gate)) * up).astype(BF16)
    return dot_t(hidden, down_w)


def chunk_kernel(plan, unit, n_units, with_heads, n_sets, n_pieces, *refs):
    refs = list(refs)
    take = lambda count: [refs.pop(0) for _ in range(count)]
    rows_in = take(n_sets)
    sums_in = [None] * n_sets if with_heads else take(n_sets)
    pieces = take(n_pieces)
    norm_out = take(n_sets) if with_heads else rows_in
    sums_out = take(n_sets)
    w_ref, ctx_ref, sems = take(3)
    width = w_ref.shape[0]
    copies = {}
    for number, (section, piece, source_col, row, col, size) in enumerate(plan):
        copy = pltpu.make_async_copy(
            pieces[piece].at[:, pl.ds(source_col, size)],
            w_ref.at[pl.ds(row, pieces[piece].shape[0]), pl.ds(col, size)],
            sems.at[number],
        )
        copy.start()
        copies.setdefault(section, []).append(copy)

    def ready(sections):
        for section in sections:
            for copy in copies.pop(section, []):
                copy.wait()

    def columns(first, count):
        return w_ref[:, first * unit : (first + count) * unit]

    begin = 0
    sums = sums_in
    if with_heads:
        for rows_ref, norm_ref in zip(rows_in, norm_out):
            tokens = rows_ref[...].astype(F32)
            scale = lax.rsqrt(jnp.mean(tokens * tokens, axis=1, keepdims=True) + EPS)
            norm_ref[...] = (tokens * scale).astype(BF16)
        ready(range(4))
        for norm_ref, sum_ref in zip(norm_out, sums_out):
            attention(norm_ref[...], columns(0, 3), unit, ctx_ref)
            sum_ref[...] = dot_t(ctx_ref[...], columns(3, 1))
        begin, sums = 4, sums_out
    for number in range(n_units):
        at = begin + 3 * number
        ready(range(at, at + 3))
        for norm_ref, sum_ref, out_ref in zip(norm_out, sums, sums_out):
            add = gated(norm_ref[...], columns(at, 1), columns(at + 1, 1), columns(at + 2, 1))
            out_ref[...] = (sum_ref[...] + add).astype(out_ref.dtype)
        sums = sums_out


def layer_chunk(rows_in, sums_in, pieces, unit, with_heads, out_type):
    n_sets = len(rows_in)
    rows, width = rows_in[0].shape
    columns = max(at + array.shape[1] for array, _, at in pieces)
    n_units = (columns // unit - 4 * with_heads) // 3
    plan = []
    for section in range(columns // unit):
        left, right = section * unit, (section + 1) * unit
        for number, (array, row, at) in enumerate(pieces):
            low, high = max(left, at), min(right, at + array.shape[1])
            if low < high:
                plan.append((section, number, low - at, row, low, high - low))
    like = lambda kind: jax.ShapeDtypeStruct((rows, width), kind)
    outs = [like(BF16)] * (n_sets * with_heads) + [like(out_type)] * n_sets
    results = pl.pallas_call(
        functools.partial(chunk_kernel, plan, unit, n_units, with_heads, n_sets, len(pieces)),
        out_shape=outs,
        in_specs=[WHOLE] * (len(rows_in) + len(sums_in)) + [pl.BlockSpec(memory_space=pl.ANY)] * len(pieces),
        out_specs=[WHOLE] * len(outs),
        scratch_shapes=[
            pltpu.VMEM((width, columns), BF16),
            pltpu.VMEM((rows, unit), BF16),
            pltpu.SemaphoreType.DMA((len(plan),)),
        ],
        compiler_params=params(),
        cost_estimate=pl.CostEstimate(
            flops=2 * n_sets * rows * width * columns,
            bytes_accessed=2 * width * columns + 8 * n_sets * rows * width,
            transcendentals=n_sets * n_units * rows * unit,
        ),
        name="layer_heads" if with_heads else "layer_gated",
    )(*rows_in, *sums_in, *[array for array, _, _ in pieces])
    return results[: -n_sets] if with_heads else rows_in, results[-n_sets:]


def finish_kernel(tok_ref, sum_ref, got_ref, order_ref, out_ref):
    width = out_ref.shape[1]
    mixed = (tok_ref[...].astype(F32) + sum_ref[...] + got_ref[...].astype(F32)).astype(BF16)
    move = (iota((width, width), 0) == order_ref[...]).astype(F32).astype(BF16)
    out_ref[...] = dot_t(mixed, move).astype(BF16)


def finish(tokens, sums, got, order):
    rows, width = tokens.shape
    return pl.pallas_call(
        finish_kernel,
        out_shape=jax.ShapeDtypeStruct((rows, width), BF16),
        in_specs=[WHOLE] * 4,
        out_specs=WHOLE,
        compiler_params=params(),
        cost_estimate=pl.CostEstimate(
            flops=2 * rows * width * width, bytes_accessed=10 * rows * width, transcendentals=0
        ),
        name="finish",
    )(tokens, sums, got, order.reshape(1, width))


def chunk_columns(w_qkv, w_out, w_gate_up, w_down, units):
    unit = w_qkv.shape[2]
    parts = []
    for number in units:
        if number < 0:
            parts += [w_qkv[:, 0], w_qkv[:, 1], w_qkv[:, 2], w_out]
        else:
            cols = slice(number * unit, (number + 1) * unit)
            parts += [w_gate_up[:, 0, cols], w_gate_up[:, 1, cols], w_down[:, cols]]
    return jnp.concatenate(parts, axis=1)


def chunk_pieces(shard, share_rows):
    n_cells = lax.axis_size("cells")
    rows = shard.shape[0]
    share = share_rows.shape[0]
    mine = lax.axis_index("cells")
    lines = lax.all_gather(share_rows, "cells", axis=0, tiled=True)
    others = jnp.concatenate(
        [
            lax.dynamic_slice_in_dim(lines, (mine + ahead) % n_cells * share, share, 0)
            for ahead in range(1, n_cells)
        ],
        axis=0,
    )
    swap = [(0, 1), (1, 0)]
    by_slot = lax.ppermute(others, "slots", swap)
    by_group = lax.ppermute(others, "groups", swap)
    cut = shard.shape[1] // (2 * LANES) * LANES
    far_a = lax.ppermute(by_slot[:, :cut], "groups", swap)
    far_b = lax.ppermute(by_group[:, cut:], "slots", swap)
    step = others.shape[0]
    return [
        (shard, 0, 0),
        (others, rows, 0),
        (by_slot, rows + step, 0),
        (by_group, rows + 2 * step, 0),
        (far_a, rows + 3 * step, 0),
        (far_b, rows + 3 * step, cut),
    ]


def arrival_order(width, n_cells, n_share):
    mine = lax.axis_index("cells")
    share_id = lax.axis_index("groups") * lax.axis_size("slots") + lax.axis_index("slots")
    rows = width // n_cells
    share = rows // n_share
    step = (n_cells - 1) * share
    place = jnp.arange(width, dtype=jnp.int32)
    past = jnp.maximum(place - rows, 0)
    which = past // step
    cell = (mine + 1 + past % step // share) % n_cells
    far = cell * rows + (which ^ share_id) * share + past % share
    return jnp.where(place < rows, mine * rows + place, far)


def tokens_by_blocks(owner, position, obs_feat, time_embed, my_slot, capacity, slot_dev, order):
    n_owners = lax.axis_size("cells") * lax.axis_size("mp")
    blocks = place_rows(owner, position, obs_feat, n_owners, capacity)
    got = lax.all_to_all(blocks, ("cells", "mp"), split_axis=0, concat_axis=0, tiled=True)
    keep, send = pool_rows(my_slot.reshape(1), time_embed, got, capacity, slot_dev)
    other = lax.ppermute(send, "slots", [(0, 1), (1, 0)])
    return weave_steps(my_slot.reshape(1), order, keep, other, slot_dev)


def tokens_by_exchanges(owner, position, obs_feat, time_embed, my_slot, capacity, slot_dev):
    n_slots = lax.axis_size("slots")
    n_owners = lax.axis_size("cells") * lax.axis_size("mp")
    rows, width = obs_feat.shape
    owners = jnp.arange(n_owners, dtype=jnp.int32)
    owner_hot = (owner[:, None] == owners[None, :]).astype(F32)
    row_ids = jnp.arange(rows, dtype=jnp.int32)
    lower = (row_ids[None, :] <= row_ids[:, None]).astype(BF16)
    running = dot(lower, owner_hot.astype(BF16))
    rank = jnp.sum(running * owner_hot, axis=1).astype(jnp.int32) - 1
    place = jnp.where(owner < n_owners, owner * capacity + rank, n_owners * capacity)
    place_ids = jnp.arange(n_owners * capacity, dtype=jnp.int32)
    taken = place_ids[:, None] == place[None, :]
    send_feat = dot(taken.astype(BF16), obs_feat).astype(BF16).reshape(n_owners, capacity, width)
    send_code = jnp.sum(jnp.where(taken, position[None, :] + 1, 0), axis=1).reshape(n_owners, capacity)
    axes = ("cells", "mp")
    got_feat = lax.all_to_all(send_feat, axes, split_axis=0, concat_axis=0, tiled=True).reshape(-1, width)
    got_code = lax.all_to_all(send_code, axes, split_axis=0, concat_axis=0, tiled=True).reshape(-1) - 1
    hot = (jnp.arange(CB * slot_dev, dtype=jnp.int32)[:, None] == got_code[None, :]).astype(BF16)
    count = jnp.sum(hot.astype(F32), axis=1)
    pooled = dot(hot, got_feat) / jnp.maximum(count, 1.0)[:, None]
    embed = lax.dynamic_slice_in_dim(time_embed, my_slot * slot_dev, slot_dev, 0).astype(F32)
    tokens = (pooled.reshape(CB, slot_dev, width) + embed[None]).astype(BF16)
    grid = tokens.reshape(n_slots, CB // n_slots, slot_dev, width)
    grid = lax.all_to_all(grid, "slots", split_axis=0, concat_axis=2, tiled=True)
    return grid.reshape(-1, width)


def on_device(obs_feat, obs_cell, obs_slot, obs_count, time_embed, w_qkv, w_out, w_gate_up, w_down):
    n_cells = lax.axis_size("cells")
    n_slots = lax.axis_size("slots")
    n_groups = lax.axis_size("groups")
    n_mp = lax.axis_size("mp")
    n_owners = n_cells * n_mp
    rows, width = obs_feat.shape
    capacity = 3 * rows // n_owners
    quarter = CB // n_slots
    slot_dev = TSTEPS // n_slots
    my_slot = lax.axis_index("slots")
    n_share = n_groups * n_slots
    share = w_qkv.shape[0] // n_share
    unit = w_qkv.shape[2]
    n_units = w_gate_up.shape[2] // unit

    valid = jnp.arange(rows, dtype=jnp.int32) < obs_count[0]
    owner = obs_cell // (quarter * n_mp * n_slots) * n_mp + obs_cell // quarter % n_mp
    owner = jnp.where(valid, owner, n_owners)
    local = obs_cell // (quarter * n_mp) % n_slots * quarter + obs_cell % quarter
    position = local * slot_dev + obs_slot

    local_weights = (w_qkv, w_out.T, w_gate_up, w_down.T)
    which = lax.axis_index("groups") * n_slots + my_slot
    share_weights = [lax.dynamic_slice_in_dim(w, which * share, share, 0) for w in local_weights]
    chunks = [[-1, 0], list(range(1, n_units - 1)), [n_units - 1]]
    if n_slots == 2 and n_groups == 2 and share % 16 == 0 and capacity % 16 == 0:
        order = arrival_order(width, n_cells, n_share)
        gathered = [
            chunk_pieces(chunk_columns(*local_weights, units), chunk_columns(*share_weights, units))
            for units in chunks
        ]
        tokens = tokens_by_blocks(owner, position, obs_feat, time_embed, my_slot, capacity, slot_dev, order)
    else:
        order = jnp.arange(width, dtype=jnp.int32)
        axes = ("cells", "groups", "slots")
        gathered = [
            [(lax.all_gather(chunk_columns(*share_weights, units), axes, axis=0, tiled=True), 0, 0)]
            for units in chunks
        ]
        tokens = tokens_by_exchanges(owner, position, obs_feat, time_embed, my_slot, capacity, slot_dev)

    swap = [(0, 1), (1, 0)]
    partner = lax.ppermute(tokens, "mp", swap)
    normed, sums = layer_chunk([partner, tokens], [], gathered[0], unit, True, F32)
    for pieces in gathered[1:-1]:
        _, sums = layer_chunk(normed, sums, pieces, unit, False, F32)
    _, (for_partner,) = layer_chunk(normed[:1], sums[:1], gathered[-1], unit, False, BF16)
    from_partner = lax.ppermute(for_partner, "mp", swap)
    _, (own,) = layer_chunk(normed[1:], sums[1:], gathered[-1], unit, False, F32)
    return finish(tokens, own, from_partner, order).reshape(quarter, TSTEPS, width)


def solution(mesh):
    placed = (
        P(("groups", "cells", "slots", "mp"), None),
        P(("groups", "cells", "slots", "mp")),
        P(("groups", "cells", "slots", "mp")),
        P(("groups", "cells", "slots", "mp")),
        P(),
        P("cells", None, "mp"),
        P("mp", "cells"),
        P("cells", None, "mp"),
        P("mp", "cells"),
    )
    return jax.shard_map(
        on_device,
        mesh=mesh,
        in_specs=placed,
        out_specs=P(("groups", "cells", "slots", "mp"), None, None),
        check_vma=False,
    )
```

time: 209 us -> 212 us (1.014)
  blocking collectives: 0 us -> 102 us
  waiting for transfers between devices: 125 us -> 23.4 us
  local copies, waits for them, and re-layouts: 4.24 us -> 26.4 us
  between operations: 14.2 us -> 1.1 us
  starting transfers between devices: 33.8 us -> 21.4 us
  Pallas kernels: 29.4 us -> 35.1 us
    all_gather x0 -> x3, blocking collectives: none -> 102 us  [chunk_pieces(): lines = lax.all_gather(share_rows, 'cells', axis=0, tiled=True)]
    all_gather x1 -> x0, waiting for transfers between devices: 81.9 us -> none  [gather_weights(): lax.all_gather(mine, ('cells', 'groups', 'slots'), axis=0, tiled=True)]
    ppermute x8 -> x13, waiting for transfers between devices: 41.4 us -> 23 us  [the longest x3 10.6 us: chunk_pieces(): by_slot = lax.ppermute(others, 'slots', swap)]
    ppermute x8 -> x13, starting transfers between devices: 28.6 us -> 14.9 us  [the longest x3 3.62 us: chunk_pieces(): far_a = lax.ppermute(by_slot[:, :cut], 'groups', swap)]
    unnamed x12 -> x60, local copies, waits for them, and re-layouts: 2.25 us -> 14.2 us
    slice x0 -> x10, local copies, waits for them, and re-layouts: none -> 9.08 us  [the longest x4 6.96 us: chunk_columns(): parts += [w_gate_up[:, 0, cols], w_gate_up[:, 1, cols], w_down[:, cols]]]
    all_to_all x0 -> x1, starting transfers between devices: none -> 6.32 us  [tokens_by_blocks(): lax.all_to_all(blocks, ('cells', 'mp'), split_axis=0, concat_axis=0, tile...]
    ppermute x1, starting transfers between devices: 5.18 us -> 0.07 us  [on_device(): partner = lax.ppermute(tokens, 'mp', swap)]
  transfers between devices with their start and end apart: 11 -> 16, of which waited for: 7 -> 4; matrix products, arithmetic and copies ran while one was open for 0% -> 10% of each run, Pallas kernels for 8% -> 14%
where the time goes in v3:
time: 212 us; the launch traced here: 211 us
  blocking collectives  102 us (48%)
  Pallas kernels  35.1 us (17%)
  local copies, waits for them, and re-layouts  26.4 us (12%)
  waiting for transfers between devices  23.4 us (11%)
  starting transfers between devices  21.4 us (10%)
    all_gather x3, blocking collectives, chunk_pieces(): lines = lax.all_gather(share_rows, 'cells', axis=0, tiled=True)  102 us
    pallas_call x4, Pallas kernels, layer_chunk(): pl.pallas_call(functools.partial(chunk_kernel, plan, unit, n_units, with_...  27.8 us
    unnamed x60, local copies, waits for them, and re-layouts  14.2 us
    ppermute x3, waiting for transfers between devices, chunk_pieces(): by_slot = lax.ppermute(others, 'slots', swap)  10.6 us
    slice x4, local copies, waits for them, and re-layouts, chunk_columns(): parts += [w_gate_up[:, 0, cols], w_gate_up[:, 1, cols], w_down[:, cols]]  6.96 us
    all_to_all x1, starting transfers between devices, tokens_by_blocks(): lax.all_to_all(blocks, ('cells', 'mp'), split_axis=0, concat_axis=0, tile...  6.32 us
    ppermute x3, waiting for transfers between devices, chunk_pieces(): far_a = lax.ppermute(by_slot[:, :cut], 'groups', swap)  6.29 us
    ppermute x1, waiting for transfers between devices, tokens_by_blocks(): other = lax.ppermute(send, 'slots', [(0, 1), (1, 0)])  6.14 us
  transfers between devices with their start and end apart: 16, of which 4 were waited for; matrix products, arithmetic and copies ran while one was open for 10% of the time, Pallas kernels for 14%

profile of v3, /device:TPU:0, one launch (start us, length us, event | category | flops | bytes accessed | tf_op | source)
XLA Modules:
  0.0 211.3 jit_solution(9435950188846322364)
XLA Ops:
  0.7 0.7 fusion.20
  1.4 1.1 copy-done.5
  2.5 2.0 place_rows.1
  4.5 1.5 copy-done
  5.9 6.3 %all-to-all-start = ((bf16[8,208,768]{2,1,0:T(8,128)(2,1)}), bf16[8,208,768]{2,1,0:T(8,128)(2,1)S(1)}, u32[]{:S(2)}, u32[]{:S(2)}) async-start(bf16[8,208,768]{2,1,0:T(8,128)(2,1)} %copy-done), calls=%async_computation | async-start | bytes 5111808 | tf_op jit(solution)/shard_map/all_to_all | solution.py:354
  12.3 0.9 dynamic-slice_bitcast_fusion
  13.2 0.8 constant_dynamic-update-slice_fusion.6
  14.0 0.8 constant_dynamic-update-slice_fusion.5
  14.8 1.8 constant_dynamic-slice_fusion
  16.6 0.8 constant_dynamic-update-slice_fusion.4
  17.3 0.8 constant_dynamic-update-slice_fusion.3
  18.3 0.7 copy-done.16
  18.9 68.9 %all_gather.9 = bf16[192,2688]{1,0:T(8,128)(2,1)} all-gather(bf16[48,2688]{1,0:T(8,128)(2,1)S(1)} %get-tuple-element.51), channel_id=1, replica_groups=mesh['groups'=2,'cells'=4,'slots'=2,'mp'=2] {'cells'}, dimensions={0}, use_global_device_ids=true | all-gather | bytes 1290240 | tf_op jit(solution)/shard_map/all_gather | solution.py:312
  87.8 1.3 constant_dynamic-slice_fusion.13
  89.1 1.0 pad_maximum_fusion.refs_3_
  90.1 1.5 collective-permute-start.2
  91.6 1.5 collective-permute-start.3
  93.1 15.2 %all_gather.11 = bf16[192,1152]{1,0:T(8,128)(2,1)S(1)} all-gather(bf16[48,1152]{1,0:T(8,128)(2,1)S(1)} %pad_maximum_fusion.4), channel_id=1, replica_groups=mesh['groups'=2,'cells'=4,'slots'=2,'mp'=2] {'cells'}, dimensions={0}, use_global_device_ids=true | all-gather | bytes 552960 | tf_op jit(solution)/shard_map/all_gather | solution.py:312
  109.5 0.9 bitcast_dynamic-update-slice_fusion.3
  110.5 4.3 %fusion.22 = (bf16[192,1,384]{2,1,0:T(2,128)(2,1)}, bf16[192,1,384]{2,1,0:T(2,128)(2,1)}, bf16[192,1,384]{2,1,0:T(2,128)(2,1)S(1)}, bf16[192,1,384]{2,1,0:T(2,12...) fusion(bf16[192,2,1536]{2,1,0:T(2,128)(2,1)} %param.16), kind=kLoop, calls=%fused_computation.108 | loop fusion | bytes 2359296 | tf_op jit(solution)/shard_map/slice | solution.py:303
  114.8 0.7 fusion.3
  115.6 0.7 fusion.2
  116.3 1.6 slice_dynamic-update-slice_fusion.1
  117.9 0.7 fusion.1
  118.7 17.9 %all_gather.10 = bf16[192,2304]{1,0:T(8,128)(2,1)S(1)} all-gather(bf16[48,2304]{1,0:T(8,128)(2,1)S(1)} %copy-done.17), channel_id=1, replica_groups=mesh['groups'=2,'cells'=4,'slots'=2,'mp'=2] {'cells'}, dimensions={0}, use_global_device_ids=true | all-gather | bytes 1105920 | tf_op jit(solution)/shard_map/all_gather | solution.py:312
  136.6 0.9 constant_dynamic-slice_fusion.10
  137.5 0.7 copy-done.6
  138.2 2.0 pool_rows.1
  140.2 1.6 collective-permute-start
  141.9 6.1 %collective-permute-done.got_ref = bf16[256,768]{1,0:T(8,128)(2,1)S(1)} collective-permute-done((bf16[256,768]{1,0:T(8,128)(2,1)S(1)}, bf16[256,768]{1,0:T(8,128)(2,1)S(1)}, u32[]{:S(2)}, u32[]{:S(2)}) %collective-permute-start) | collective-permute-done | bytes 393248 | tf_op jit(solution)/shard_map/ppermute | solution.py:356
  148.1 1.5 weave_steps.1.refs_1_.tok_ref
  149.7 0.8 fusion
  150.5 1.5 collective-permute-start.6
  152.0 1.5 collective-permute-start.7
  153.5 0.8 fusion.23
  154.3 1.0 slice.146
  155.4 1.0 slice.147
  157.7 10.6 %collective-permute-done.6.refs_6_ = bf16[144,2304]{1,0:T(8,128)(2,1)S(1)} collective-permute-done((bf16[144,2304]{1,0:T(8,128)(2,1)S(1)}, bf16[144,2304]{1,0:T(8,128)(2,1)S(1)}, u32[]{:S(2)}, u32[]{:S(2)}) %collective-permute-start.6) | collective-permute-done | bytes 663584 | tf_op jit(solution)/shard_map/ppermute | solution.py:321
  168.2 1.5 collective-permute-start.12
  169.8 1.6 collective-permute-start.13
  171.4 6.3 %collective-permute-done.4.refs_6_ = bf16[144,1280]{1,0:T(8,128)(2,1)S(1)} collective-permute-done((bf16[144,1280]{1,0:T(8,128)(2,1)S(1)}, bf16[144,1280]{1,0:T(8,128)(2,1)S(1)}, u32[]{:S(2)}, u32[]{:S(2)}) %collective-permute-start.4) | collective-permute-done | bytes 368672 | tf_op jit(solution)/shard_map/ppermute | solution.py:324
  177.7 1.5 collective-permute-start.8
  179.7 14.0 %layer_heads.1 = (bf16[512,768]{1,0:T(8,128)(2,1)S(1)}, bf16[512,768]{1,0:T(8,128)(2,1)S(1)}, f32[512,768]{1,0:T(8,128)}, f32[512,768]{1,0:T(8,128)}) custom-call(bf16[512,768]{1,0:T(8,128)(2,1)S(1)} %collective-permute-done.1.refs_0_, bf16[512,768]{1,0:T(8,128)(2,1)} %copy-done.3, bf16[192,2688]{1,0:T(8,128)(2,1)} %get-tuple-element.45.refs_2_, ...), custom_call_target="tpu_custom_call" | custom-call | flops 4227858432 | bytes 10420224 | tf_op jit(solution)/shard_map/layer_heads/pallas_call | solution.py:252
  193.8 10.0 %layer_gated.3 = (f32[512,768]{1,0:T(8,128)}, f32[512,768]{1,0:T(8,128)}) custom-call(bf16[512,768]{1,0:T(8,128)(2,1)S(1)} %get-tuple-element.16.refs_0_, bf16[512,768]{1,0:T(8,128)(2,1)S(1)} %get-tuple-element.15.refs_1_.refs_0_, f32[512,768]{1,0:T(8,128)} %get-tuple-element.17.refs_2_, f32[512,768]{1,0:T(8,128)} %get-tuple-element.18.refs_3_, ...), custom_call_target="tpu_custom_call" | custom-call | flops 3623878656 | bytes 9830400 | tf_op jit(solution)/shard_map/layer_gated/pallas_call | solution.py:252
  203.8 1.4 copy-done.2
  205.2 1.9 layer_gated.5
  207.2 1.9 layer_gated.4.sum_ref
  209.5 1.8 finish.1
  (78 shorter events, 3.9 us)
Async XLA Ops:
  1.4 1.1 copy-start.5
  4.5 1.5 copy-start
  5.9 131.5 %all-to-all-start = ((bf16[8,208,768]{2,1,0:T(8,128)(2,1)}), bf16[8,208,768]{2,1,0:T(8,128)(2,1)S(1)}, u32[]{:S(2)}, u32[]{:S(2)}) async-start(bf16[8,208,768]{2,1,0:T(8,128)(2,1)} %copy-done), calls=%async_computation | async-start | bytes 5111808 | tf_op jit(solution)/shard_map/all_to_all | solution.py:354
  18.3 0.7 copy-start.16
  90.1 60.4 %collective-permute-start.2 = (bf16[144,2688]{1,0:T(8,128)(2,1)}, bf16[144,2688]{1,0:T(8,128)(2,1)}, u32[]{:S(2)}, u32[]{:S(2)}) collective-permute-start(bf16[144,2688]{1,0:T(8,128)(2,1)} %pad_maximum_fusion.refs_3_), channel_id=1, source_target_pairs={{0,2},{2,0},{1,3},{3,1},{4,6},{6,4},{5,7},{7,5},{8,10},{10,8},{9,1... | collective-permute-start | bytes 2322440 | tf_op jit(solution)/shard_map/ppermute | solution.py:321
  91.6 60.4 %collective-permute-start.3 = (bf16[144,2688]{1,0:T(8,128)(2,1)}, bf16[144,2688]{1,0:T(8,128)(2,1)}, u32[]{:S(2)}, u32[]{:S(2)}) collective-permute-start(bf16[144,2688]{1,0:T(8,128)(2,1)} %pad_maximum_fusion.refs_3_), channel_id=1, source_target_pairs={{0,16},{16,0},{1,17},{17,1},{2,18},{18,2},{3,19},{19,3},{4,20},{20... | collective-permute-start | bytes 2322440 | tf_op jit(solution)/shard_map/ppermute | solution.py:322
  108.4 48.0 %collective-permute-start.10 = (bf16[144,1152]{1,0:T(8,128)(2,1)S(1)}, bf16[144,1152]{1,0:T(8,128)(2,1)S(1)}, u32[]{:S(2)}, u32[]{:S(2)}) collective-permute-start(bf16[144,1152]{1,0:T(8,128)(2,1)S(1)} %pad_maximum_fusion.3.refs_3_), channel_id=1, source_target_pairs={{0,2},{2,0},{1,3},{3,1},{4,6},{6,4},{5,7},{7,5},{8,10},{10,8},{9,1... | collective-permute-start | bytes 995336 | tf_op jit(solution)/shard_map/ppermute | solution.py:321
  109.0 48.0 %collective-permute-start.11 = (bf16[144,1152]{1,0:T(8,128)(2,1)S(1)}, bf16[144,1152]{1,0:T(8,128)(2,1)S(1)}, u32[]{:S(2)}, u32[]{:S(2)}) collective-permute-start(bf16[144,1152]{1,0:T(8,128)(2,1)S(1)} %pad_maximum_fusion.3.refs_3_), channel_id=1, source_target_pairs={{0,16},{16,0},{1,17},{17,1},{2,18},{18,2},{3,19},{19,3},{4,20},{20... | collective-permute-start | bytes 995336 | tf_op jit(solution)/shard_map/ppermute | solution.py:322
  110.4 5.1 %copy-start.15 = (bf16[192,3,384]{2,0,1:T(8,128)(2,1)S(1)}, bf16[192,3,384]{2,0,1:T(8,128)(2,1)}, u32[]{:S(2)}) copy-start(bf16[192,3,384]{2,0,1:T(8,128)(2,1)} %param.14) | copy-start | bytes 1327108
  110.5 5.1 %copy-start.18 = (bf16[384,192]{0,1:T(8,128)(2,1)S(1)}, bf16[384,192]{0,1:T(8,128)(2,1)}, u32[]{:S(2)}) copy-start(bf16[384,192]{0,1:T(8,128)(2,1)} %param.15) | copy-start | bytes 442372
  114.8 3.9 %copy-start.17 = (bf16[48,2304]{1,0:T(8,128)(2,1)S(1)}, bf16[48,2304]{1,0:T(8,128)(2,1)}, u32[]{:S(2)}) copy-start(bf16[48,2304]{1,0:T(8,128)(2,1)} %copy-done.16) | copy-start | bytes 663556
  118.7 17.9 %copy-start.19 = (bf16[192,2688]{1,0:T(8,128)(2,1)}, bf16[192,2688]{1,0:T(8,128)(2,1)S(1)}, u32[]{:S(2)}) copy-start(bf16[192,2688]{1,0:T(8,128)(2,1)S(1)} %fusion.5) | copy-start | bytes 3096580
  137.5 0.7 copy-start.6
  138.2 3.7 %copy-start.12 = (bf16[48,2304]{1,0:T(8,128)(2,1)S(1)}, bf16[48,2304]{1,0:T(8,128)(2,1)}, u32[]{:S(2)}) copy-start(bf16[48,2304]{1,0:T(8,128)(2,1)} %get-tuple-element.40) | copy-start | bytes 663556
  138.2 3.7 %copy-start.13 = (bf16[48,2304]{1,0:T(8,128)(2,1)S(1)}, bf16[48,2304]{1,0:T(8,128)(2,1)}, u32[]{:S(2)}) copy-start(bf16[48,2304]{1,0:T(8,128)(2,1)} %get-tuple-element.41) | copy-start | bytes 663556
  138.2 3.7 %copy-start.14 = (bf16[48,2304]{1,0:T(8,128)(2,1)S(1)}, bf16[48,2304]{1,0:T(8,128)(2,1)}, u32[]{:S(2)}) copy-start(bf16[48,2304]{1,0:T(8,128)(2,1)} %get-tuple-element.42) | copy-start | bytes 663556
  140.2 7.8 %collective-permute-start = (bf16[256,768]{1,0:T(8,128)(2,1)S(1)}, bf16[256,768]{1,0:T(8,128)(2,1)S(1)}, u32[]{:S(2)}, u32[]{:S(2)}) collective-permute-start(bf16[256,768]{1,0:T(8,128)(2,1)S(1)} %get-tuple-element.14), channel_id=1, source_target_pairs={{0,2},{2,0},{1,3},{3,1},{4,6},{6,4},{5,7},{7,5},{8,10},{10,8},{9,1... | collective-permute-start | bytes 1179656 | tf_op jit(solution)/shard_map/ppermute | solution.py:356
  148.1 1.6 copy-start.9
  148.1 1.6 copy-start.10
  148.1 5.4 %copy-start.11 = (bf16[1536,192]{0,1:T(8,128)(2,1)S(1)}, bf16[1536,192]{0,1:T(8,128)(2,1)}, u32[]{:S(2)}) copy-start(bf16[1536,192]{0,1:T(8,128)(2,1)} %param.17) | copy-start | bytes 1769476
  149.6 6.8 %copy-start.3 = (bf16[512,768]{1,0:T(8,128)(2,1)}, bf16[512,768]{1,0:T(8,128)(2,1)S(1)}, u32[]{:S(2)}) copy-start(bf16[512,768]{1,0:T(8,128)(2,1)S(1)} %weave_steps.1.refs_1_.tok_ref) | copy-start | bytes 2359300
  149.6 30.1 %collective-permute-start.1 = (bf16[512,768]{1,0:T(8,128)(2,1)S(1)}, bf16[512,768]{1,0:T(8,128)(2,1)S(1)}, u32[]{:S(2)}, u32[]{:S(2)}) collective-permute-start(bf16[512,768]{1,0:T(8,128)(2,1)S(1)} %weave_steps.1.refs_1_.tok_ref), channel_id=1, source_target_pairs={{0,1},{1,0},{2,3},{3,2},{4,5},{5,4},{6,7},{7,6},{8,9},{9,8},{10,11... | collective-permute-start | bytes 2359304 | tf_op jit(solution)/shard_map/ppermute | solution.py:431
  149.7 7.9 %copy-start.7 = (bf16[192,1,384]{2,1,0:T(2,128)(2,1)S(1)}, bf16[192,1,384]{2,1,0:T(2,128)(2,1)}, u32[]{:S(2)}) copy-start(bf16[192,1,384]{2,1,0:T(2,128)(2,1)} %get-tuple-element.29) | copy-start | bytes 442372
  149.7 7.8 %copy-start.8 = (bf16[192,1,384]{2,1,0:T(2,128)(2,1)S(1)}, bf16[192,1,384]{2,1,0:T(2,128)(2,1)}, u32[]{:S(2)}) copy-start(bf16[192,1,384]{2,1,0:T(2,128)(2,1)} %get-tuple-element.36) | copy-start | bytes 442372
  150.5 17.7 %collective-permute-start.6 = (bf16[144,2304]{1,0:T(8,128)(2,1)S(1)}, bf16[144,2304]{1,0:T(8,128)(2,1)S(1)}, u32[]{:S(2)}, u32[]{:S(2)}) collective-permute-start(bf16[144,2304]{1,0:T(8,128)(2,1)S(1)} %pad_maximum_fusion.1.refs_5_), channel_id=1, source_target_pairs={{0,2},{2,0},{1,3},{3,1},{4,6},{6,4},{5,7},{7,5},{8,10},{10,8},{9,1... | collective-permute-start | bytes 1990664 | tf_op jit(solution)/shard_map/ppermute | solution.py:321
  152.0 17.8 %collective-permute-start.7 = (bf16[144,2304]{1,0:T(8,128)(2,1)S(1)}, bf16[144,2304]{1,0:T(8,128)(2,1)S(1)}, u32[]{:S(2)}, u32[]{:S(2)}) collective-permute-start(bf16[144,2304]{1,0:T(8,128)(2,1)S(1)} %pad_maximum_fusion.1.refs_5_), channel_id=1, source_target_pairs={{0,16},{16,0},{1,17},{17,1},{2,18},{18,2},{3,19},{19,3},{4,20},{20... | collective-permute-start | bytes 1990664 | tf_op jit(solution)/shard_map/ppermute | solution.py:322
  156.4 21.2 %collective-permute-start.4 = (bf16[144,1280]{1,0:T(8,128)(2,1)S(1)}, bf16[144,1280]{1,0:T(8,128)(2,1)S(1)}, u32[]{:S(2)}, u32[]{:S(2)}) collective-permute-start(bf16[144,1280]{1,0:T(8,128)(2,1)S(1)} %slice.146), channel_id=1, source_target_pairs={{0,16},{16,0},{1,17},{17,1},{2,18},{18,2},{3,19},{19,3},{4,20},{20... | collective-permute-start | bytes 1105928 | tf_op jit(solution)/shard_map/ppermute | solution.py:324
  157.0 22.2 %collective-permute-start.5 = (bf16[144,1408]{1,0:T(8,128)(2,1)S(1)}, bf16[144,1408]{1,0:T(8,128)(2,1)S(1)}, u32[]{:S(2)}, u32[]{:S(2)}) collective-permute-start(bf16[144,1408]{1,0:T(8,128)(2,1)S(1)} %slice.147), channel_id=1, source_target_pairs={{0,2},{2,0},{1,3},{3,1},{4,6},{6,4},{5,7},{7,5},{8,10},{10,8},{9,1... | collective-permute-start | bytes 1216520 | tf_op jit(solution)/shard_map/ppermute | solution.py:325
  168.2 35.5 %collective-permute-start.12 = (bf16[144,512]{1,0:T(8,128)(2,1)S(1)}, bf16[144,512]{1,0:T(8,128)(2,1)S(1)}, u32[]{:S(2)}, u32[]{:S(2)}) collective-permute-start(bf16[144,512]{1,0:T(8,128)(2,1)S(1)} %slice.156), channel_id=1, source_target_pairs={{0,16},{16,0},{1,17},{17,1},{2,18},{18,2},{3,19},{19,3},{4,20},{20... | collective-permute-start | bytes 442376 | tf_op jit(solution)/shard_map/ppermute | solution.py:324
  169.8 34.0 %collective-permute-start.13 = (bf16[144,640]{1,0:T(8,128)(2,1)S(1)}, bf16[144,640]{1,0:T(8,128)(2,1)S(1)}, u32[]{:S(2)}, u32[]{:S(2)}) collective-permute-start(bf16[144,640]{1,0:T(8,128)(2,1)S(1)} %slice.157), channel_id=1, source_target_pairs={{0,2},{2,0},{1,3},{3,1},{4,6},{6,4},{5,7},{7,5},{8,10},{10,8},{9,1... | collective-permute-start | bytes 552968 | tf_op jit(solution)/shard_map/ppermute | solution.py:325
  177.7 16.1 %collective-permute-start.8 = (bf16[144,1152]{1,0:T(8,128)(2,1)S(1)}, bf16[144,1152]{1,0:T(8,128)(2,1)S(1)}, u32[]{:S(2)}, u32[]{:S(2)}) collective-permute-start(bf16[144,1152]{1,0:T(8,128)(2,1)S(1)} %slice.152), channel_id=1, source_target_pairs={{0,16},{16,0},{1,17},{17,1},{2,18},{18,2},{3,19},{19,3},{4,20},{20... | collective-permute-start | bytes 995336 | tf_op jit(solution)/shard_map/ppermute | solution.py:324
  179.2 14.6 %collective-permute-start.9 = (bf16[144,1152]{1,0:T(8,128)(2,1)S(1)}, bf16[144,1152]{1,0:T(8,128)(2,1)S(1)}, u32[]{:S(2)}, u32[]{:S(2)}) collective-permute-start(bf16[144,1152]{1,0:T(8,128)(2,1)S(1)} %slice.153), channel_id=1, source_target_pairs={{0,2},{2,0},{1,3},{3,1},{4,6},{6,4},{5,7},{7,5},{8,10},{10,8},{9,1... | collective-permute-start | bytes 995336 | tf_op jit(solution)/shard_map/ppermute | solution.py:325
  203.8 1.4 copy-start.2
  205.2 2.0 copy-start.1
  207.1 2.4 %collective-permute-start.14 = (bf16[512,768]{1,0:T(8,128)(2,1)S(1)}, bf16[512,768]{1,0:T(8,128)(2,1)S(1)}, u32[]{:S(2)}, u32[]{:S(2)}) collective-permute-start(bf16[512,768]{1,0:T(8,128)(2,1)S(1)} %layer_gated.5), channel_id=1, source_target_pairs={{0,1},{1,0},{2,3},{3,2},{4,5},{5,4},{6,7},{7,6},{8,9},{9,8},{10,11... | collective-permute-start | bytes 2359304 | tf_op jit(solution)/shard_map/ppermute | solution.py:436
  207.2 2.3 %copy-start.4 = (bf16[512,768]{1,0:T(8,128)(2,1)S(1)}, bf16[512,768]{1,0:T(8,128)(2,1)}, u32[]{:S(2)}) copy-start(bf16[512,768]{1,0:T(8,128)(2,1)} %copy-done.3) | copy-start | bytes 2359300

commit v4 on v3

--- a/solution.py
+++ b/solution.py
@@ -307,16 +307,14 @@
 def chunk_pieces(shard, share_rows):
     n_cells = lax.axis_size("cells")
     rows = shard.shape[0]
-    share = share_rows.shape[0]
-    mine = lax.axis_index("cells")
-    lines = lax.all_gather(share_rows, "cells", axis=0, tiled=True)
-    others = jnp.concatenate(
-        [
-            lax.dynamic_slice_in_dim(lines, (mine + ahead) % n_cells * share, share, 0)
-            for ahead in range(1, n_cells)
-        ],
-        axis=0,
-    )
+    up = [(j, (j + 1) % n_cells) for j in range(n_cells)]
+    down = [(j, (j - 1) % n_cells) for j in range(n_cells)]
+    below = [lax.ppermute(share_rows, "cells", up)]
+    above = [lax.ppermute(share_rows, "cells", down)]
+    while len(below) + len(above) < n_cells - 1:
+        line, way = (below, up) if len(below) <= len(above) else (above, down)
+        line.append(lax.ppermute(line[-1], "cells", way))
+    others = jnp.concatenate(above + below[::-1], axis=0)
     swap = [(0, 1), (1, 0)]
     by_slot = lax.ppermute(others, "slots", swap)
     by_group = lax.ppermute(others, "groups", swap)

time: 212 us -> 209 us (0.986)
  blocking collectives: 102 us -> 0 us
  waiting for transfers between devices: 23.4 us -> 94.1 us
  starting transfers between devices: 21.4 us -> 45.8 us
  local copies, waits for them, and re-layouts: 26.4 us -> 31.8 us
    all_gather x3 -> x0, blocking collectives: 102 us -> none  [chunk_pieces(): lines = lax.all_gather(share_rows, 'cells', axis=0, tiled=True)]
    ppermute x0 -> x9, waiting for transfers between devices: none -> 54.9 us  [the longest x3 54.9 us: chunk_pieces(): line.append(lax.ppermute(line[-1], 'cells', way))]
    ppermute x0 -> x9, starting transfers between devices: none -> 28.5 us  [the longest x3 15.7 us: chunk_pieces(): line.append(lax.ppermute(line[-1], 'cells', way))]
    ppermute x3, waiting for transfers between devices: 10.6 us -> 23.7 us  [chunk_pieces(): by_slot = lax.ppermute(others, 'slots', swap)]
    unnamed x60 -> x62, local copies, waits for them, and re-layouts: 14.2 us -> 19.4 us
    concatenate x0 -> x3, local copies, waits for them, and re-layouts: none -> 3.86 us  [chunk_pieces(): others = jnp.concatenate(above + below[::-1], axis=0)]
    dynamic_slice x3 -> x0, local copies, waits for them, and re-layouts: 2.15 us -> none  [chunk_pieces(): lax.dynamic_slice_in_dim(lines, (mine + ahead) % n_cells * share, share, 0)]
  transfers between devices with their start and end apart: 16 -> 25, of which waited for: 4 -> 8; matrix products, arithmetic and copies ran while one was open for 10% -> 8% of each run, Pallas kernels for 14% -> 15%
where the time goes in v4:
time: 209 us; the launch traced here: 208 us
  waiting for transfers between devices  94.1 us (45%)
  starting transfers between devices  45.8 us (22%)
  Pallas kernels  34.5 us (17%)
  local copies, waits for them, and re-layouts  31.8 us (15%)
    ppermute x3, waiting for transfers between devices, chunk_pieces(): line.append(lax.ppermute(line[-1], 'cells', way))  54.9 us
    pallas_call x4, Pallas kernels, layer_chunk(): pl.pallas_call(functools.partial(chunk_kernel, plan, unit, n_units, with_...  27.3 us
    ppermute x3, waiting for transfers between devices, chunk_pieces(): by_slot = lax.ppermute(others, 'slots', swap)  23.7 us
    unnamed x62, local copies, waits for them, and re-layouts  19.4 us
    ppermute x3, starting transfers between devices, chunk_pieces(): line.append(lax.ppermute(line[-1], 'cells', way))  15.7 us
    ppermute x3, starting transfers between devices, chunk_pieces(): above = [lax.ppermute(share_rows, 'cells', down)]  12.7 us
    slice x4, local copies, waits for them, and re-layouts, chunk_columns(): parts += [w_gate_up[:, 0, cols], w_gate_up[:, 1, cols], w_down[:, cols]]  7.38 us
    ppermute x3, waiting for transfers between devices, chunk_pieces(): far_a = lax.ppermute(by_slot[:, :cut], 'groups', swap)  7.26 us
  transfers between devices with their start and end apart: 25, of which 8 were waited for; matrix products, arithmetic and copies ran while one was open for 8% of the time, Pallas kernels for 15%

profile of v4, /device:TPU:0, one launch (start us, length us, event | category | flops | bytes accessed | tf_op | source)
XLA Modules:
  0.0 208.1 jit_solution(14314410832275661176)
XLA Ops:
  0.0 1.0 dynamic-slice_bitcast_fusion
  1.0 1.4 constant_dynamic-update-slice_fusion.6
  2.4 1.4 constant_dynamic-update-slice_fusion.5
  3.8 1.8 constant_dynamic-slice_fusion
  5.6 0.6 constant_dynamic-update-slice_fusion.15
  6.2 1.4 constant_dynamic-update-slice_fusion.4
  10.7 0.6 constant_dynamic-update-slice_fusion.1
  11.3 0.6 fusion.24
  12.0 5.1 %collective-permute-start.2 = (bf16[48,2688]{1,0:T(8,128)(2,1)}, bf16[48,2688]{1,0:T(8,128)(2,1)}, u32[]{:S(2)}, u32[]{:S(2)}) collective-permute-start(bf16[48,2688]{1,0:T(8,128)(2,1)} %get-tuple-element.42), channel_id=1, source_target_pairs={{0,12},{4,0},{8,4},{12,8},{1,13},{5,1},{9,5},{13,9},{2,14},{6,2},{... | collective-permute-start | bytes 774152 | tf_op jit(solution)/shard_map/ppermute | solution.py:313
  17.0 0.7 pad_maximum_fusion.1
  17.7 3.8 %collective-permute-start.16 = (bf16[48,1152]{1,0:T(8,128)(2,1)}, bf16[48,1152]{1,0:T(8,128)(2,1)}, u32[]{:S(2)}, u32[]{:S(2)}) collective-permute-start(bf16[48,1152]{1,0:T(8,128)(2,1)} %pad_maximum_fusion.1), channel_id=1, source_target_pairs={{0,12},{4,0},{8,4},{12,8},{1,13},{5,1},{9,5},{13,9},{2,14},{6,2},{... | collective-permute-start | bytes 331784 | tf_op jit(solution)/shard_map/ppermute | solution.py:313
  22.2 2.0 place_rows.1
  24.2 1.5 copy-done
  25.7 5.2 %all-to-all-start = ((bf16[8,208,768]{2,1,0:T(8,128)(2,1)}), bf16[8,208,768]{2,1,0:T(8,128)(2,1)S(1)}, u32[]{:S(2)}, u32[]{:S(2)}) async-start(bf16[8,208,768]{2,1,0:T(8,128)(2,1)} %copy-done), calls=%async_computation | async-start | bytes 5111808 | tf_op jit(solution)/shard_map/all_to_all | solution.py:352
  30.9 3.8 %collective-permute-start.9 = (bf16[48,2304]{1,0:T(8,128)(2,1)}, bf16[48,2304]{1,0:T(8,128)(2,1)}, u32[]{:S(2)}, u32[]{:S(2)}) collective-permute-start(bf16[48,2304]{1,0:T(8,128)(2,1)} %get-tuple-element.41), channel_id=1, source_target_pairs={{0,12},{4,0},{8,4},{12,8},{1,13},{5,1},{9,5},{13,9},{2,14},{6,2},{... | collective-permute-start | bytes 663560 | tf_op jit(solution)/shard_map/ppermute | solution.py:313
  34.8 4.2 %fusion.22 = (bf16[192,1,384]{2,1,0:T(2,128)(2,1)}, bf16[192,1,384]{2,1,0:T(2,128)(2,1)S(1)}, bf16[192,1,384]{2,1,0:T(2,128)(2,1)S(1)}, bf16[192,1,384]{2,1,0:T(...) fusion(bf16[192,2,1536]{2,1,0:T(2,128)(2,1)} %param.16), kind=kLoop, calls=%fused_computation.105 | loop fusion | bytes 2359296 | tf_op jit(solution)/shard_map/slice | solution.py:303
  39.1 0.9 slice_dynamic-update-slice_fusion.1
  40.6 1.0 constant_dynamic-update-slice_fusion.21
  41.6 47.4 %collective-permute-done.18 = bf16[48,1152]{1,0:T(8,128)(2,1)S(1)} collective-permute-done((bf16[48,1152]{1,0:T(8,128)(2,1)}, bf16[48,1152]{1,0:T(8,128)(2,1)S(1)}, u32[]{:S(2)}, u32[]{:S(2)}) %collective-permute-start.18) | collective-permute-done | bytes 110624 | tf_op jit(solution)/shard_map/ppermute | solution.py:316
  89.1 0.9 constant_dynamic-update-slice_fusion.19.refs_3_
  90.0 1.6 collective-permute-start.19
  91.5 1.5 collective-permute-start.20
  93.1 15.5 %collective-permute-start.11 = (bf16[48,2304]{1,0:T(8,128)(2,1)}, bf16[48,2304]{1,0:T(8,128)(2,1)}, u32[]{:S(2)}, u32[]{:S(2)}) collective-permute-start(bf16[48,2304]{1,0:T(8,128)(2,1)} %collective-permute-done.10), channel_id=1, source_target_pairs={{0,4},{4,8},{8,12},{12,0},{1,5},{5,9},{9,13},{13,1},{2,6},{6,10},{... | collective-permute-start | bytes 663560 | tf_op jit(solution)/shard_map/ppermute | solution.py:316
  108.6 1.6 constant_dynamic-update-slice_fusion.18
  110.2 1.7 constant_dynamic-update-slice_fusion.9
  111.9 7.5 %collective-permute-done.4 = bf16[48,2688]{1,0:T(8,128)(2,1)S(1)} collective-permute-done((bf16[48,2688]{1,0:T(8,128)(2,1)}, bf16[48,2688]{1,0:T(8,128)(2,1)S(1)}, u32[]{:S(2)}, u32[]{:S(2)}) %collective-permute-start.4) | collective-permute-done | bytes 258080 | tf_op jit(solution)/shard_map/ppermute | solution.py:316
  119.4 0.7 constant_dynamic-update-slice_fusion.8
  120.2 0.7 copy-done.9
  120.9 2.0 pool_rows.1
  122.9 1.6 collective-permute-start
  124.5 1.7 constant_dynamic-update-slice_fusion.7.refs_3_
  127.2 1.0 constant_dynamic-update-slice_fusion.17
  128.1 6.9 %collective-permute-done.got_ref = bf16[256,768]{1,0:T(8,128)(2,1)S(1)} collective-permute-done((bf16[256,768]{1,0:T(8,128)(2,1)S(1)}, bf16[256,768]{1,0:T(8,128)(2,1)S(1)}, u32[]{:S(2)}, u32[]{:S(2)}) %collective-permute-start) | collective-permute-done | bytes 393248 | tf_op jit(solution)/shard_map/ppermute | solution.py:354
  135.0 1.5 weave_steps.1.refs_1_.tok_ref
  136.6 1.3 constant_dynamic-update-slice_fusion.16.refs_5_
  137.9 11.0 %collective-permute-done.5.refs_4_ = bf16[144,2688]{1,0:T(8,128)(2,1)S(1)} collective-permute-done((bf16[144,2688]{1,0:T(8,128)(2,1)}, bf16[144,2688]{1,0:T(8,128)(2,1)S(1)}, u32[]{:S(2)}, u32[]{:S(2)}) %collective-permute-start.5) | collective-permute-done | bytes 774176 | tf_op jit(solution)/shard_map/ppermute | solution.py:319
  148.9 1.5 collective-permute-start.12
  150.9 0.7 fusion.23
  151.7 1.6 collective-permute-start.7
  154.0 12.7 %collective-permute-done.12.refs_6_ = bf16[144,2304]{1,0:T(8,128)(2,1)S(1)} collective-permute-done((bf16[144,2304]{1,0:T(8,128)(2,1)S(1)}, bf16[144,2304]{1,0:T(8,128)(2,1)S(1)}, u32[]{:S(2)}, u32[]{:S(2)}) %collective-permute-start.12) | collective-permute-done | bytes 663584 | tf_op jit(solution)/shard_map/ppermute | solution.py:319
  167.2 1.0 collective-permute-done.13.refs_7_
  168.8 7.3 %collective-permute-done.7.refs_6_ = bf16[144,1280]{1,0:T(8,128)(2,1)S(1)} collective-permute-done((bf16[144,1280]{1,0:T(8,128)(2,1)S(1)}, bf16[144,1280]{1,0:T(8,128)(2,1)S(1)}, u32[]{:S(2)}, u32[]{:S(2)}) %collective-permute-start.7) | collective-permute-done | bytes 368672 | tf_op jit(solution)/shard_map/ppermute | solution.py:322
  177.2 13.8 %layer_heads.1 = (bf16[512,768]{1,0:T(8,128)(2,1)S(1)}, bf16[512,768]{1,0:T(8,128)(2,1)S(1)}, f32[512,768]{1,0:T(8,128)}, f32[512,768]{1,0:T(8,128)}) custom-call(bf16[512,768]{1,0:T(8,128)(2,1)S(1)} %collective-permute-done.1.refs_0_, bf16[512,768]{1,0:T(8,128)(2,1)} %copy-done.3, bf16[192,2688]{1,0:T(8,128)(2,1)} %get-tuple-element.39.refs_2_, ...), custom_call_target="tpu_custom_call" | custom-call | flops 4227858432 | bytes 10420224 | tf_op jit(solution)/shard_map/layer_heads/pallas_call | solution.py:252
  191.0 9.6 %layer_gated.3 = (f32[512,768]{1,0:T(8,128)}, f32[512,768]{1,0:T(8,128)}) custom-call(bf16[512,768]{1,0:T(8,128)(2,1)S(1)} %get-tuple-element.16.refs_0_, bf16[512,768]{1,0:T(8,128)(2,1)S(1)} %get-tuple-element.15.refs_1_.refs_0_, f32[512,768]{1,0:T(8,128)} %get-tuple-element.17.refs_2_, f32[512,768]{1,0:T(8,128)} %get-tuple-element.18.refs_3_, ...), custom_call_target="tpu_custom_call" | custom-call | flops 3623878656 | bytes 9830400 | tf_op jit(solution)/shard_map/layer_gated/pallas_call | solution.py:252
  200.6 1.4 copy-done.2
  202.1 1.9 layer_gated.5
  204.1 1.9 layer_gated.4.sum_ref
  206.3 1.8 finish.1
  (92 shorter events, 8.8 us)
Async XLA Ops:
  0.0 7.6 %copy-start.14 = (bf16[384,192]{0,1:T(8,128)(2,1)S(1)}, bf16[384,192]{0,1:T(8,128)(2,1)}, u32[]{:S(2)}) copy-start(bf16[384,192]{0,1:T(8,128)(2,1)} %param.15) | copy-start | bytes 442372
  0.0 22.2 %copy-start.16 = (s32[512]{0:T(512)S(1)}, s32[512]{0:T(512)}, u32[]{:S(2)}) copy-start(s32[512]{0:T(512)} %param.11) | copy-start | bytes 6148
  0.0 22.2 %copy-start.17 = (s32[512]{0:T(512)S(1)}, s32[512]{0:T(512)}, u32[]{:S(2)}) copy-start(s32[512]{0:T(512)} %param.10) | copy-start | bytes 6148
  0.0 22.2 %copy-start.8 = (bf16[512,768]{1,0:T(8,128)(2,1)S(1)}, bf16[512,768]{1,0:T(8,128)(2,1)}, u32[]{:S(2)}) copy-start(bf16[512,768]{1,0:T(8,128)(2,1)} %feat_ref.1) | copy-start | bytes 2359300
  12.0 98.3 %collective-permute-start.2 = (bf16[48,2688]{1,0:T(8,128)(2,1)}, bf16[48,2688]{1,0:T(8,128)(2,1)}, u32[]{:S(2)}, u32[]{:S(2)}) collective-permute-start(bf16[48,2688]{1,0:T(8,128)(2,1)} %get-tuple-element.42), channel_id=1, source_target_pairs={{0,12},{4,0},{8,4},{12,8},{1,13},{5,1},{9,5},{13,9},{2,14},{6,2},{... | collective-permute-start | bytes 774152 | tf_op jit(solution)/shard_map/ppermute | solution.py:313
  17.0 93.2 %collective-permute-start.3 = (bf16[48,2688]{1,0:T(8,128)(2,1)}, bf16[48,2688]{1,0:T(8,128)(2,1)}, u32[]{:S(2)}, u32[]{:S(2)}) collective-permute-start(bf16[48,2688]{1,0:T(8,128)(2,1)} %get-tuple-element.42), channel_id=1, source_target_pairs={{0,4},{4,8},{8,12},{12,0},{1,5},{5,9},{9,13},{13,1},{2,6},{6,10},{... | collective-permute-start | bytes 774152 | tf_op jit(solution)/shard_map/ppermute | solution.py:312
  17.7 22.6 %collective-permute-start.16 = (bf16[48,1152]{1,0:T(8,128)(2,1)}, bf16[48,1152]{1,0:T(8,128)(2,1)}, u32[]{:S(2)}, u32[]{:S(2)}) collective-permute-start(bf16[48,1152]{1,0:T(8,128)(2,1)} %pad_maximum_fusion.1), channel_id=1, source_target_pairs={{0,12},{4,0},{8,4},{12,8},{1,13},{5,1},{9,5},{13,9},{2,14},{6,2},{... | collective-permute-start | bytes 331784 | tf_op jit(solution)/shard_map/ppermute | solution.py:313
  21.5 18.9 %collective-permute-start.17 = (bf16[48,1152]{1,0:T(8,128)(2,1)}, bf16[48,1152]{1,0:T(8,128)(2,1)}, u32[]{:S(2)}, u32[]{:S(2)}) collective-permute-start(bf16[48,1152]{1,0:T(8,128)(2,1)} %pad_maximum_fusion.1), channel_id=1, source_target_pairs={{0,4},{4,8},{8,12},{12,0},{1,5},{5,9},{9,13},{13,1},{2,6},{6,10},{... | collective-permute-start | bytes 331784 | tf_op jit(solution)/shard_map/ppermute | solution.py:312
  24.2 1.5 copy-start
  25.7 9.1 %copy-start.13 = (bf16[192,3,384]{2,0,1:T(8,128)(2,1)S(1)}, bf16[192,3,384]{2,0,1:T(8,128)(2,1)}, u32[]{:S(2)}) copy-start(bf16[192,3,384]{2,0,1:T(8,128)(2,1)} %param.14) | copy-start | bytes 1327108
  25.7 94.5 %all-to-all-start = ((bf16[8,208,768]{2,1,0:T(8,128)(2,1)}), bf16[8,208,768]{2,1,0:T(8,128)(2,1)S(1)}, u32[]{:S(2)}, u32[]{:S(2)}) async-start(bf16[8,208,768]{2,1,0:T(8,128)(2,1)} %copy-done), calls=%async_computation | async-start | bytes 5111808 | tf_op jit(solution)/shard_map/all_to_all | solution.py:352
  30.9 60.6 %collective-permute-start.9 = (bf16[48,2304]{1,0:T(8,128)(2,1)}, bf16[48,2304]{1,0:T(8,128)(2,1)}, u32[]{:S(2)}, u32[]{:S(2)}) collective-permute-start(bf16[48,2304]{1,0:T(8,128)(2,1)} %get-tuple-element.41), channel_id=1, source_target_pairs={{0,12},{4,0},{8,4},{12,8},{1,13},{5,1},{9,5},{13,9},{2,14},{6,2},{... | collective-permute-start | bytes 663560 | tf_op jit(solution)/shard_map/ppermute | solution.py:313
  40.2 79.2 %copy-start.6 = (bf16[192,2304]{1,0:T(8,128)(2,1)}, bf16[192,2304]{1,0:T(8,128)(2,1)S(1)}, u32[]{:S(2)}) copy-start(bf16[192,2304]{1,0:T(8,128)(2,1)S(1)} %get-tuple-element.47) | copy-start | bytes 2654212
  40.2 79.2 %copy-start.15 = (bf16[192,2688]{1,0:T(8,128)(2,1)}, bf16[192,2688]{1,0:T(8,128)(2,1)S(1)}, u32[]{:S(2)}) copy-start(bf16[192,2688]{1,0:T(8,128)(2,1)S(1)} %get-tuple-element.48) | copy-start | bytes 3096580
  40.3 52.7 %collective-permute-start.10 = (bf16[48,2304]{1,0:T(8,128)(2,1)}, bf16[48,2304]{1,0:T(8,128)(2,1)}, u32[]{:S(2)}, u32[]{:S(2)}) collective-permute-start(bf16[48,2304]{1,0:T(8,128)(2,1)} %get-tuple-element.41), channel_id=1, source_target_pairs={{0,4},{4,8},{8,12},{12,0},{1,5},{5,9},{9,13},{13,1},{2,6},{6,10},{... | collective-permute-start | bytes 663560 | tf_op jit(solution)/shard_map/ppermute | solution.py:312
  40.4 48.6 %collective-permute-start.18 = (bf16[48,1152]{1,0:T(8,128)(2,1)}, bf16[48,1152]{1,0:T(8,128)(2,1)S(1)}, u32[]{:S(2)}, u32[]{:S(2)}) collective-permute-start(bf16[48,1152]{1,0:T(8,128)(2,1)} %collective-permute-done.17), channel_id=1, source_target_pairs={{0,4},{4,8},{8,12},{12,0},{1,5},{5,9},{9,13},{13,1},{2,6},{6,10},{... | collective-permute-start | bytes 331784 | tf_op jit(solution)/shard_map/ppermute | solution.py:316
  90.0 61.7 %collective-permute-start.19 = (bf16[144,1152]{1,0:T(8,128)(2,1)S(1)}, bf16[144,1152]{1,0:T(8,128)(2,1)S(1)}, u32[]{:S(2)}, u32[]{:S(2)}) collective-permute-start(bf16[144,1152]{1,0:T(8,128)(2,1)S(1)} %constant_dynamic-update-slice_fusion.19.refs_3_), channel_id=1, source_target_pairs={{0,2},{2,0},{1,3},{3,1},{4,6},{6,4},{5,7},{7,5},{8,10},{10,8},{9,1... | collective-permute-start | bytes 995336 | tf_op jit(solution)/shard_map/ppermute | solution.py:319
  91.5 61.7 %collective-permute-start.20 = (bf16[144,1152]{1,0:T(8,128)(2,1)S(1)}, bf16[144,1152]{1,0:T(8,128)(2,1)S(1)}, u32[]{:S(2)}, u32[]{:S(2)}) collective-permute-start(bf16[144,1152]{1,0:T(8,128)(2,1)S(1)} %constant_dynamic-update-slice_fusion.19.refs_3_), channel_id=1, source_target_pairs={{0,16},{16,0},{1,17},{17,1},{2,18},{18,2},{3,19},{19,3},{4,20},{20... | collective-permute-start | bytes 995336 | tf_op jit(solution)/shard_map/ppermute | solution.py:320
  93.1 33.6 %collective-permute-start.11 = (bf16[48,2304]{1,0:T(8,128)(2,1)}, bf16[48,2304]{1,0:T(8,128)(2,1)}, u32[]{:S(2)}, u32[]{:S(2)}) collective-permute-start(bf16[48,2304]{1,0:T(8,128)(2,1)} %collective-permute-done.10), channel_id=1, source_target_pairs={{0,4},{4,8},{8,12},{12,0},{1,5},{5,9},{9,13},{13,1},{2,6},{6,10},{... | collective-permute-start | bytes 663560 | tf_op jit(solution)/shard_map/ppermute | solution.py:316
  110.2 9.2 %collective-permute-start.4 = (bf16[48,2688]{1,0:T(8,128)(2,1)}, bf16[48,2688]{1,0:T(8,128)(2,1)S(1)}, u32[]{:S(2)}, u32[]{:S(2)}) collective-permute-start(bf16[48,2688]{1,0:T(8,128)(2,1)} %collective-permute-done.3), channel_id=1, source_target_pairs={{0,4},{4,8},{8,12},{12,0},{1,5},{5,9},{9,13},{13,1},{2,6},{6,10},{... | collective-permute-start | bytes 774152 | tf_op jit(solution)/shard_map/ppermute | solution.py:316
  120.2 0.7 copy-start.9
  120.9 6.3 %copy-start.5 = (bf16[144,2304]{1,0:T(8,128)(2,1)S(1)}, bf16[144,2304]{1,0:T(8,128)(2,1)}, u32[]{:S(2)}) copy-start(bf16[144,2304]{1,0:T(8,128)(2,1)} %constant_dynamic-update-slice_fusion.18) | copy-start | bytes 1990660
  122.9 12.1 %collective-permute-start = (bf16[256,768]{1,0:T(8,128)(2,1)S(1)}, bf16[256,768]{1,0:T(8,128)(2,1)S(1)}, u32[]{:S(2)}, u32[]{:S(2)}) collective-permute-start(bf16[256,768]{1,0:T(8,128)(2,1)S(1)} %get-tuple-element.14), channel_id=1, source_target_pairs={{0,2},{2,0},{1,3},{3,1},{4,6},{6,4},{5,7},{7,5},{8,10},{10,8},{9,1... | collective-permute-start | bytes 1179656 | tf_op jit(solution)/shard_map/ppermute | solution.py:354
  126.1 22.7 %collective-permute-start.5 = (bf16[144,2688]{1,0:T(8,128)(2,1)}, bf16[144,2688]{1,0:T(8,128)(2,1)S(1)}, u32[]{:S(2)}, u32[]{:S(2)}) collective-permute-start(bf16[144,2688]{1,0:T(8,128)(2,1)} %constant_dynamic-update-slice_fusion.7.refs_3_), channel_id=1, source_target_pairs={{0,2},{2,0},{1,3},{3,1},{4,6},{6,4},{5,7},{7,5},{8,10},{10,8},{9,1... | collective-permute-start | bytes 2322440 | tf_op jit(solution)/shard_map/ppermute | solution.py:319
  126.7 23.7 %collective-permute-start.6 = (bf16[144,2688]{1,0:T(8,128)(2,1)}, bf16[144,2688]{1,0:T(8,128)(2,1)S(1)}, u32[]{:S(2)}, u32[]{:S(2)}) collective-permute-start(bf16[144,2688]{1,0:T(8,128)(2,1)} %constant_dynamic-update-slice_fusion.7.refs_3_), channel_id=1, source_target_pairs={{0,16},{16,0},{1,17},{17,1},{2,18},{18,2},{3,19},{19,3},{4,20},{20... | collective-permute-start | bytes 2322440 | tf_op jit(solution)/shard_map/ppermute | solution.py:320
  135.0 15.8 %copy-start.7 = (bf16[192,2304]{1,0:T(8,128)(2,1)S(1)}, bf16[192,2304]{1,0:T(8,128)(2,1)}, u32[]{:S(2)}) copy-start(bf16[192,2304]{1,0:T(8,128)(2,1)} %copy-done.6) | copy-start | bytes 2654212
  135.0 15.8 %copy-start.12 = (bf16[1536,192]{0,1:T(8,128)(2,1)S(1)}, bf16[1536,192]{0,1:T(8,128)(2,1)}, u32[]{:S(2)}) copy-start(bf16[1536,192]{0,1:T(8,128)(2,1)} %param.17) | copy-start | bytes 1769476
  136.5 17.4 %copy-start.3 = (bf16[512,768]{1,0:T(8,128)(2,1)}, bf16[512,768]{1,0:T(8,128)(2,1)S(1)}, u32[]{:S(2)}) copy-start(bf16[512,768]{1,0:T(8,128)(2,1)S(1)} %weave_steps.1.refs_1_.tok_ref) | copy-start | bytes 2359300
  136.5 17.3 %copy-start.10 = (bf16[192,1,384]{2,1,0:T(2,128)(2,1)S(1)}, bf16[192,1,384]{2,1,0:T(2,128)(2,1)}, u32[]{:S(2)}) copy-start(bf16[192,1,384]{2,1,0:T(2,128)(2,1)} %get-tuple-element.29) | copy-start | bytes 442372
  136.5 17.3 %copy-start.11 = (bf16[192,1,384]{2,1,0:T(2,128)(2,1)S(1)}, bf16[192,1,384]{2,1,0:T(2,128)(2,1)}, u32[]{:S(2)}) copy-start(bf16[192,1,384]{2,1,0:T(2,128)(2,1)} %get-tuple-element.36) | copy-start | bytes 442372
  136.5 40.6 %collective-permute-start.1 = (bf16[512,768]{1,0:T(8,128)(2,1)S(1)}, bf16[512,768]{1,0:T(8,128)(2,1)S(1)}, u32[]{:S(2)}, u32[]{:S(2)}) collective-permute-start(bf16[512,768]{1,0:T(8,128)(2,1)S(1)} %weave_steps.1.refs_1_.tok_ref), channel_id=1, source_target_pairs={{0,1},{1,0},{2,3},{3,2},{4,5},{5,4},{6,7},{7,6},{8,9},{9,8},{10,11... | collective-permute-start | bytes 2359304 | tf_op jit(solution)/shard_map/ppermute | solution.py:429
  148.9 17.8 %collective-permute-start.12 = (bf16[144,2304]{1,0:T(8,128)(2,1)S(1)}, bf16[144,2304]{1,0:T(8,128)(2,1)S(1)}, u32[]{:S(2)}, u32[]{:S(2)}) collective-permute-start(bf16[144,2304]{1,0:T(8,128)(2,1)S(1)} %constant_dynamic-update-slice_fusion.16.refs_5_), channel_id=1, source_target_pairs={{0,2},{2,0},{1,3},{3,1},{4,6},{6,4},{5,7},{7,5},{8,10},{10,8},{9,1... | collective-permute-start | bytes 1990664 | tf_op jit(solution)/shard_map/ppermute | solution.py:319
  150.4 17.8 %collective-permute-start.13 = (bf16[144,2304]{1,0:T(8,128)(2,1)S(1)}, bf16[144,2304]{1,0:T(8,128)(2,1)S(1)}, u32[]{:S(2)}, u32[]{:S(2)}) collective-permute-start(bf16[144,2304]{1,0:T(8,128)(2,1)S(1)} %constant_dynamic-update-slice_fusion.16.refs_5_), channel_id=1, source_target_pairs={{0,16},{16,0},{1,17},{17,1},{2,18},{18,2},{3,19},{19,3},{4,20},{20... | collective-permute-start | bytes 1990664 | tf_op jit(solution)/shard_map/ppermute | solution.py:320
  151.7 24.4 %collective-permute-start.7 = (bf16[144,1280]{1,0:T(8,128)(2,1)S(1)}, bf16[144,1280]{1,0:T(8,128)(2,1)S(1)}, u32[]{:S(2)}, u32[]{:S(2)}) collective-permute-start(bf16[144,1280]{1,0:T(8,128)(2,1)S(1)} %slice.146), channel_id=1, source_target_pairs={{0,16},{16,0},{1,17},{17,1},{2,18},{18,2},{3,19},{19,3},{4,20},{20... | collective-permute-start | bytes 1105928 | tf_op jit(solution)/shard_map/ppermute | solution.py:322
  153.3 23.3 %collective-permute-start.8 = (bf16[144,1408]{1,0:T(8,128)(2,1)S(1)}, bf16[144,1408]{1,0:T(8,128)(2,1)S(1)}, u32[]{:S(2)}, u32[]{:S(2)}) collective-permute-start(bf16[144,1408]{1,0:T(8,128)(2,1)S(1)} %slice.147), channel_id=1, source_target_pairs={{0,2},{2,0},{1,3},{3,1},{4,6},{6,4},{5,7},{7,5},{8,10},{10,8},{9,1... | collective-permute-start | bytes 1216520 | tf_op jit(solution)/shard_map/ppermute | solution.py:323
  166.7 33.9 %collective-permute-start.21 = (bf16[144,512]{1,0:T(8,128)(2,1)S(1)}, bf16[144,512]{1,0:T(8,128)(2,1)S(1)}, u32[]{:S(2)}, u32[]{:S(2)}) collective-permute-start(bf16[144,512]{1,0:T(8,128)(2,1)S(1)} %slice.156), channel_id=1, source_target_pairs={{0,16},{16,0},{1,17},{17,1},{2,18},{18,2},{3,19},{19,3},{4,20},{20... | collective-permute-start | bytes 442376 | tf_op jit(solution)/shard_map/ppermute | solution.py:322
  168.2 32.4 %collective-permute-start.22 = (bf16[144,640]{1,0:T(8,128)(2,1)S(1)}, bf16[144,640]{1,0:T(8,128)(2,1)S(1)}, u32[]{:S(2)}, u32[]{:S(2)}) collective-permute-start(bf16[144,640]{1,0:T(8,128)(2,1)S(1)} %slice.157), channel_id=1, source_target_pairs={{0,2},{2,0},{1,3},{3,1},{4,6},{6,4},{5,7},{7,5},{8,10},{10,8},{9,1... | collective-permute-start | bytes 552968 | tf_op jit(solution)/shard_map/ppermute | solution.py:323
  176.1 14.9 %collective-permute-start.14 = (bf16[144,1152]{1,0:T(8,128)(2,1)S(1)}, bf16[144,1152]{1,0:T(8,128)(2,1)S(1)}, u32[]{:S(2)}, u32[]{:S(2)}) collective-permute-start(bf16[144,1152]{1,0:T(8,128)(2,1)S(1)} %slice.152), channel_id=1, source_target_pairs={{0,16},{16,0},{1,17},{17,1},{2,18},{18,2},{3,19},{19,3},{4,20},{20... | collective-permute-start | bytes 995336 | tf_op jit(solution)/shard_map/ppermute | solution.py:322
  176.6 14.4 %collective-permute-start.15 = (bf16[144,1152]{1,0:T(8,128)(2,1)S(1)}, bf16[144,1152]{1,0:T(8,128)(2,1)S(1)}, u32[]{:S(2)}, u32[]{:S(2)}) collective-permute-start(bf16[144,1152]{1,0:T(8,128)(2,1)S(1)} %slice.153), channel_id=1, source_target_pairs={{0,2},{2,0},{1,3},{3,1},{4,6},{6,4},{5,7},{7,5},{8,10},{10,8},{9,1... | collective-permute-start | bytes 995336 | tf_op jit(solution)/shard_map/ppermute | solution.py:323
  200.6 1.4 copy-start.2
  202.0 2.0 copy-start.1
  204.0 2.4 %collective-permute-start.23 = (bf16[512,768]{1,0:T(8,128)(2,1)S(1)}, bf16[512,768]{1,0:T(8,128)(2,1)S(1)}, u32[]{:S(2)}, u32[]{:S(2)}) collective-permute-start(bf16[512,768]{1,0:T(8,128)(2,1)S(1)} %layer_gated.5), channel_id=1, source_target_pairs={{0,1},{1,0},{2,3},{3,2},{4,5},{5,4},{6,7},{7,6},{8,9},{9,8},{10,11... | collective-permute-start | bytes 2359304 | tf_op jit(solution)/shard_map/ppermute | solution.py:434
  204.1 2.3 %copy-start.4 = (bf16[512,768]{1,0:T(8,128)(2,1)S(1)}, bf16[512,768]{1,0:T(8,128)(2,1)}, u32[]{:S(2)}) copy-start(bf16[512,768]{1,0:T(8,128)(2,1)} %copy-done.3) | copy-start | bytes 2359300

commit v5 on v4

v5 whole, which is shorter than its diff:
```python
import functools

import jax
import jax.numpy as jnp
from jax import lax
from jax.experimental import pallas as pl
from jax.experimental.pallas import tpu as pltpu
from jax.sharding import PartitionSpec as P

HD = 64
TSTEPS = 8
CB = 128
EPS = 1e-06

CODE = 32
UNIT = 512
LANES = 128
VMEM_LIMIT = 48 * 1024 * 1024
F32 = jnp.float32
BF16 = jnp.bfloat16
WHOLE = pl.BlockSpec(memory_space=pltpu.VMEM)
SCALARS = pl.BlockSpec(memory_space=pltpu.SMEM)


def iota(shape, axis):
    return lax.broadcasted_iota(jnp.int32, shape, axis)


def dot(left, right):
    return jnp.dot(left, right, preferred_element_type=F32)


def dot_t(left, right):
    return lax.dot_general(left, right, (((1,), (1,)), ((), ())), preferred_element_type=F32)


def params():
    return pltpu.CompilerParams(vmem_limit_bytes=VMEM_LIMIT)


def place_kernel(capacity, owner_ref, position_ref, feat_ref, out_ref, code_ref):
    n_owners, rows = out_ref.shape[0], feat_ref.shape[0]
    owner = owner_ref[...]
    owner_hot = (iota((n_owners, rows), 0) == owner).astype(F32)
    upper = (iota((rows, rows), 0) <= iota((rows, rows), 1)).astype(BF16)
    running = dot(owner_hot.astype(BF16), upper)
    rank = jnp.sum(running * owner_hot, axis=0, keepdims=True).astype(jnp.int32) - 1
    code = position_ref[...] + 1
    line = iota((8, rows), 0)
    digits = jnp.where(line == 0, code // CODE, jnp.where(line == 1, code % CODE, 0))
    digits = digits.astype(F32).astype(BF16)
    feat = feat_ref[...]
    for block in range(n_owners):
        place = jnp.where(owner == block, rank, -1)
        taken = (iota((capacity, rows), 0) == place).astype(F32).astype(BF16)
        out_ref[block] = dot(taken, feat).astype(BF16)
        sent = dot_t(digits, taken)
        code_ref[block] = (sent[0:1] * CODE + sent[1:2]).astype(jnp.int32) - 1


def place_rows(owner, position, obs_feat, n_owners, capacity):
    rows, width = obs_feat.shape
    return pl.pallas_call(
        functools.partial(place_kernel, capacity),
        out_shape=[
            jax.ShapeDtypeStruct((n_owners, capacity, width), BF16),
            jax.ShapeDtypeStruct((n_owners, 1, capacity), jnp.int32),
        ],
        in_specs=[WHOLE] * 3,
        out_specs=[WHOLE] * 2,
        compiler_params=params(),
        cost_estimate=pl.CostEstimate(
            flops=2 * rows * width * n_owners * capacity,
            bytes_accessed=2 * width * (rows + n_owners * capacity),
            transcendentals=0,
        ),
        name="place_rows",
    )(owner.reshape(1, rows), position.reshape(1, rows), obs_feat)


def pool_kernel(capacity, slot_dev, slot_ref, embed_ref, code_ref, got_ref, keep_ref, send_ref):
    half = keep_ref.shape[0]
    places = 2 * half
    mine = slot_ref[0]
    total = jnp.zeros((places, keep_ref.shape[1]), F32)
    seen = jnp.zeros((places, capacity), F32)
    for block in range(got_ref.shape[0]):
        code = code_ref[block]
        turned = jnp.where(code >= half, code - half, code + half)
        code = jnp.where((code >= 0) & (mine == 1), turned, code)
        hot = (iota((places, capacity), 0) == code).astype(F32)
        seen += hot
        total += dot(hot.astype(BF16), got_ref[block])
    count = jnp.sum(seen, axis=1, keepdims=True)
    steps = embed_ref.shape[0]
    step_hot = iota((places, steps), 1) == iota((places, steps), 0) % slot_dev + mine * slot_dev
    embed = dot(step_hot.astype(F32).astype(BF16), embed_ref[...])
    tokens = (total / jnp.maximum(count, 1.0) + embed).astype(BF16)
    keep_ref[...] = tokens[:half]
    send_ref[...] = tokens[half:]


def pool_rows(my_slot, time_embed, codes, got, capacity, slot_dev):
    width = time_embed.shape[1]
    half = jax.ShapeDtypeStruct((CB * slot_dev // 2, width), BF16)
    return pl.pallas_call(
        functools.partial(pool_kernel, capacity, slot_dev),
        out_shape=[half, half],
        in_specs=[SCALARS] + [WHOLE] * 3,
        out_specs=[WHOLE] * 2,
        compiler_params=params(),
        cost_estimate=pl.CostEstimate(
            flops=2 * CB * slot_dev * got.size, bytes_accessed=2 * got.size, transcendentals=0
        ),
        name="pool_rows",
    )(my_slot, time_embed, codes, got)


def weave_kernel(slot_dev, slot_ref, order_ref, keep_ref, got_ref, out_ref):
    rows, width = out_ref.shape
    half = keep_ref.shape[0]
    mine = slot_ref[0]
    row, col = iota((rows, half), 0), iota((rows, half), 1)
    source = col == row // TSTEPS * slot_dev + row % slot_dev
    own = row % TSTEPS // slot_dev == mine
    from_keep = (source & own).astype(F32).astype(BF16)
    from_got = (source & jnp.logical_not(own)).astype(F32).astype(BF16)
    tokens = (dot(from_keep, keep_ref[...]) + dot(from_got, got_ref[...])).astype(BF16)
    move = (iota((width, width), 0) == order_ref[...]).astype(F32).astype(BF16)
    out_ref[...] = dot(tokens, move).astype(BF16)


def weave_steps(my_slot, order, keep, got, slot_dev):
    rows, width = 2 * keep.shape[0], keep.shape[1]
    return pl.pallas_call(
        functools.partial(weave_kernel, slot_dev),
        out_shape=jax.ShapeDtypeStruct((rows, width), BF16),
        in_specs=[SCALARS] + [WHOLE] * 3,
        out_specs=WHOLE,
        compiler_params=params(),
        cost_estimate=pl.CostEstimate(
            flops=2 * rows * width * (rows + width), bytes_accessed=4 * rows * width, transcendentals=0
        ),
        name="weave_steps",
    )(my_slot, order.reshape(1, width), keep, got)


def head_scale(values, ones):
    sums = dot((values * values).astype(BF16), ones)
    return values * lax.rsqrt(sums * (1.0 / HD) + EPS)


def attention(normed, weight, heads_width, ctx_ref):
    rows = normed.shape[0]
    projected = dot(normed, weight)
    same_head = iota((LANES, LANES), 0) // HD == iota((LANES, LANES), 1) // HD
    ones = same_head.astype(F32).astype(BF16)
    group = LANES
    first = iota((group, LANES), 1) < HD
    row, col = iota((2 * group, group), 0), iota((2 * group, group), 1)
    same_cell = row % group // TSTEPS == col // TSTEPS
    count = jnp.ones((group, LANES), BF16)
    for pair in range(heads_width // LANES):
        at = pair * LANES
        query = (head_scale(projected[:, at : at + LANES], ones) * HD ** (-0.5)).astype(BF16)
        key = head_scale(projected[:, heads_width + at : heads_width + at + LANES], ones).astype(BF16)
        value = projected[:, 2 * heads_width + at : 2 * heads_width + at + LANES].astype(BF16)
        for begin in range(0, rows, group):
            q = query[begin : begin + group]
            k = key[begin : begin + group]
            v = value[begin : begin + group]
            none = jnp.zeros_like(q)
            both = jnp.concatenate([jnp.where(first, q, none), jnp.where(first, none, q)], axis=0)
            expo = jnp.where(same_cell, jnp.exp(dot_t(both, k)), 0.0).astype(BF16)
            mixed = dot(expo, jnp.concatenate([v, count], axis=1))
            top, low = mixed[:group], mixed[group:]
            over = jnp.where(first, top[:, :LANES], low[:, :LANES])
            under = jnp.where(first, top[:, LANES:], low[:, LANES:])
            ctx_ref[begin : begin + group, at : at + LANES] = (over / under).astype(BF16)


def gated(normed, gate_w, up_w, down_w):
    gate = dot(normed, gate_w)
    up = dot(normed, up_w)
    hidden = (gate * (0.5 * jnp.tanh(0.5 * gate) + 0.5) * up).astype(BF16)
    return dot_t(hidden, down_w)


def layer_kernel(plan, sections, tok_ref, *refs):
    pieces, (out_ref, w_ref, norm_ref, ctx_ref, acc_ref, sems) = refs[:-6], refs[-6:]
    copies = {}
    for number, (section, piece, source_col, row, col, size) in enumerate(plan):
        copy = pltpu.make_async_copy(
            pieces[piece].at[:, pl.ds(source_col, size)],
            w_ref.at[pl.ds(row, pieces[piece].shape[0]), pl.ds(col, size)],
            sems.at[number],
        )
        copy.start()
        copies.setdefault(section, []).append(copy)

    def columns(section):
        for copy in copies[section]:
            copy.wait()
        begin, end = sections[section]
        return w_ref[:, begin:end]

    tokens = tok_ref[...].astype(F32)
    scale = lax.rsqrt(jnp.mean(tokens * tokens, axis=1, keepdims=True) + EPS)
    norm_ref[...] = (tokens * scale).astype(BF16)
    attention(norm_ref[...], columns(0), ctx_ref.shape[1], ctx_ref)
    acc_ref[...] = dot_t(ctx_ref[...], columns(1))
    for at in range(2, len(sections), 3):
        add = gated(norm_ref[...], columns(at), columns(at + 1), columns(at + 2))
        if at + 3 < len(sections):
            acc_ref[...] += add
        else:
            out_ref[...] = (acc_ref[...] + add).astype(out_ref.dtype)


def layer(tokens, pieces, heads_width, hidden_width, out_type):
    rows, width = tokens.shape
    gate_at = 3 * heads_width
    up_at = gate_at + hidden_width
    out_at = up_at + hidden_width
    down_at = out_at + heads_width
    columns = down_at + hidden_width
    unit = min(UNIT, hidden_width)
    sections = [(0, gate_at), (out_at, down_at)]
    for begin in range(0, hidden_width, unit):
        sections += [(at + begin, at + begin + unit) for at in (gate_at, up_at, down_at)]
    plan = []
    for section, (left, right) in enumerate(sections):
        for number, (array, row, at) in enumerate(pieces):
            low, high = max(left, at), min(right, at + array.shape[1])
            if low < high:
                plan.append((section, number, low - at, row, low, high - low))
    return pl.pallas_call(
        functools.partial(layer_kernel, plan, sections),
        out_shape=jax.ShapeDtypeStruct((rows, width), out_type),
        in_specs=[WHOLE] + [pl.BlockSpec(memory_space=pl.ANY)] * len(pieces),
        out_specs=WHOLE,
        scratch_shapes=[
            pltpu.VMEM((width, columns), BF16),
            pltpu.VMEM((rows, width), BF16),
            pltpu.VMEM((rows, heads_width), BF16),
            pltpu.VMEM((rows, width), F32),
            pltpu.SemaphoreType.DMA((len(plan),)),
        ],
        compiler_params=params(),
        cost_estimate=pl.CostEstimate(
            flops=2 * rows * width * columns,
            bytes_accessed=2 * width * columns + 6 * rows * width,
            transcendentals=rows * hidden_width,
        ),
        name="layer",
    )(tokens, *[array for array, _, _ in pieces])


def finish_kernel(tok_ref, sum_ref, got_ref, order_ref, out_ref):
    width = out_ref.shape[1]
    mixed = (tok_ref[...].astype(F32) + sum_ref[...] + got_ref[...].astype(F32)).astype(BF16)
    move = (iota((width, width), 0) == order_ref[...]).astype(F32).astype(BF16)
    out_ref[...] = dot_t(mixed, move).astype(BF16)


def finish(tokens, sums, got, order):
    rows, width = tokens.shape
    return pl.pallas_call(
        finish_kernel,
        out_shape=jax.ShapeDtypeStruct((rows, width), BF16),
        in_specs=[WHOLE] * 4,
        out_specs=WHOLE,
        compiler_params=params(),
        cost_estimate=pl.CostEstimate(
            flops=2 * rows * width * width, bytes_accessed=10 * rows * width, transcendentals=0
        ),
        name="finish",
    )(tokens, sums, got, order.reshape(1, width))


def side_by_side(w_qkv, w_out, w_gate_up, w_down):
    rows = w_qkv.shape[0]
    return jnp.concatenate([w_qkv.reshape(rows, -1), w_gate_up.reshape(rows, -1), w_out, w_down], axis=1)


def shares_along_cells(share_rows):
    n_cells = lax.axis_size("cells")
    up = [(j, (j + 1) % n_cells) for j in range(n_cells)]
    down = [(j, (j - 1) % n_cells) for j in range(n_cells)]
    below = [lax.ppermute(share_rows, "cells", up)]
    above = [lax.ppermute(share_rows, "cells", down)]
    while len(below) + len(above) < n_cells - 1:
        line, way = (below, up) if len(below) <= len(above) else (above, down)
        line.append(lax.ppermute(line[-1], "cells", way))
    return above + below[::-1]


def pieces_of_all(shard, shares):
    rows = shard.shape[0]
    others = jnp.concatenate(shares, axis=0)
    swap = [(0, 1), (1, 0)]
    by_slot = lax.ppermute(others, "slots", swap)
    by_group = lax.ppermute(others, "groups", swap)
    cut = shard.shape[1] // (2 * LANES) * LANES
    far_a = lax.ppermute(by_slot[:, :cut], "groups", swap)
    far_b = lax.ppermute(by_group[:, cut:], "slots", swap)
    step = others.shape[0]
    return [
        (shard, 0, 0),
        (others, rows, 0),
        (by_slot, rows + step, 0),
        (by_group, rows + 2 * step, 0),
        (far_a, rows + 3 * step, 0),
        (far_b, rows + 3 * step, cut),
    ]


def arrival_order(width, n_cells, n_share):
    mine = lax.axis_index("cells")
    share_id = lax.axis_index("groups") * lax.axis_size("slots") + lax.axis_index("slots")
    rows = width // n_cells
    share = rows // n_share
    step = (n_cells - 1) * share
    place = jnp.arange(width, dtype=jnp.int32)
    past = jnp.maximum(place - rows, 0)
    which = past // step
    cell = (mine + 1 + past % step // share) % n_cells
    far = cell * rows + (which ^ share_id) * share + past % share
    return jnp.where(place < rows, mine * rows + place, far)


def tokens_by_blocks(owner, position, obs_feat, time_embed, my_slot, capacity, slot_dev, order, shares):
    n_owners = lax.axis_size("cells") * lax.axis_size("mp")
    blocks, codes = place_rows(owner, position, obs_feat, n_owners, capacity)
    codes = lax.all_to_all(codes, ("cells", "mp"), split_axis=0, concat_axis=0, tiled=True)
    blocks, *shares = lax.optimization_barrier((blocks, *shares))
    got = lax.all_to_all(blocks, ("cells", "mp"), split_axis=0, concat_axis=0, tiled=True)
    keep, send = pool_rows(my_slot.reshape(1), time_embed, codes, got, capacity, slot_dev)
    other = lax.ppermute(send, "slots", [(0, 1), (1, 0)])
    return weave_steps(my_slot.reshape(1), order, keep, other, slot_dev), shares


def tokens_by_exchanges(owner, position, obs_feat, time_embed, my_slot, capacity, slot_dev):
    n_slots = lax.axis_size("slots")
    n_owners = lax.axis_size("cells") * lax.axis_size("mp")
    rows, width = obs_feat.shape
    owners = jnp.arange(n_owners, dtype=jnp.int32)
    owner_hot = (owner[:, None] == owners[None, :]).astype(F32)
    row_ids = jnp.arange(rows, dtype=jnp.int32)
    lower = (row_ids[None, :] <= row_ids[:, None]).astype(BF16)
    running = dot(lower, owner_hot.astype(BF16))
    rank = jnp.sum(running * owner_hot, axis=1).astype(jnp.int32) - 1
    place = jnp.where(owner < n_owners, owner * capacity + rank, n_owners * capacity)
    place_ids = jnp.arange(n_owners * capacity, dtype=jnp.int32)
    taken = place_ids[:, None] == place[None, :]
    send_feat = dot(taken.astype(BF16), obs_feat).astype(BF16).reshape(n_owners, capacity, width)
    send_code = jnp.sum(jnp.where(taken, position[None, :] + 1, 0), axis=1).reshape(n_owners, capacity)
    axes = ("cells", "mp")
    got_feat = lax.all_to_all(send_feat, axes, split_axis=0, concat_axis=0, tiled=True).reshape(-1, width)
    got_code = lax.all_to_all(send_code, axes, split_axis=0, concat_axis=0, tiled=True).reshape(-1) - 1
    hot = (jnp.arange(CB * slot_dev, dtype=jnp.int32)[:, None] == got_code[None, :]).astype(BF16)
    count = jnp.sum(hot.astype(F32), axis=1)
    pooled = dot(hot, got_feat) / jnp.maximum(count, 1.0)[:, None]
    embed = lax.dynamic_slice_in_dim(time_embed, my_slot * slot_dev, slot_dev, 0).astype(F32)
    tokens = (pooled.reshape(CB, slot_dev, width) + embed[None]).astype(BF16)
    grid = tokens.reshape(n_slots, CB // n_slots, slot_dev, width)
    grid = lax.all_to_all(grid, "slots", split_axis=0, concat_axis=2, tiled=True)
    return grid.reshape(-1, width)


def on_device(obs_feat, obs_cell, obs_slot, obs_count, time_embed, w_qkv, w_out, w_gate_up, w_down):
    n_cells = lax.axis_size("cells")
    n_slots = lax.axis_size("slots")
    n_groups = lax.axis_size("groups")
    n_mp = lax.axis_size("mp")
    n_owners = n_cells * n_mp
    rows, width = obs_feat.shape
    capacity = 3 * rows // n_owners
    quarter = CB // n_slots
    slot_dev = TSTEPS // n_slots
    my_slot = lax.axis_index("slots")
    n_share = n_groups * n_slots
    share = w_qkv.shape[0] // n_share
    valid = jnp.arange(rows, dtype=jnp.int32) < obs_count[0]
    owner = obs_cell // (quarter * n_mp * n_slots) * n_mp + obs_cell // quarter % n_mp
    owner = jnp.where(valid, owner, n_owners)
    local = obs_cell // (quarter * n_mp) % n_slots * quarter + obs_cell % quarter
    position = local * slot_dev + obs_slot

    local_weights = (w_qkv, w_out.T, w_gate_up, w_down.T)
    which = lax.axis_index("groups") * n_slots + my_slot
    share_rows = side_by_side(*[lax.dynamic_slice_in_dim(w, which * share, share, 0) for w in local_weights])
    if n_slots == 2 and n_groups == 2 and share % 16 == 0 and capacity % 16 == 0:
        order = arrival_order(width, n_cells, n_share)
        shares = shares_along_cells(share_rows)
        tokens, shares = tokens_by_blocks(
            owner, position, obs_feat, time_embed, my_slot, capacity, slot_dev, order, shares
        )
        pieces = pieces_of_all(side_by_side(*local_weights), shares)
    else:
        order = jnp.arange(width, dtype=jnp.int32)
        pieces = [(lax.all_gather(share_rows, ("cells", "groups", "slots"), axis=0, tiled=True), 0, 0)]
        tokens = tokens_by_exchanges(owner, position, obs_feat, time_embed, my_slot, capacity, slot_dev)

    swap = [(0, 1), (1, 0)]
    heads_width, hidden_width = w_qkv.shape[2], w_gate_up.shape[2]
    partner = lax.ppermute(tokens, "mp", swap)
    for_partner = layer(partner, pieces, heads_width, hidden_width, BF16)
    from_partner = lax.ppermute(for_partner, "mp", swap)
    own = layer(tokens, pieces, heads_width, hidden_width, F32)
    return finish(tokens, own, from_partner, order).reshape(quarter, TSTEPS, width)


def solution(mesh):
    placed = (
        P(("groups", "cells", "slots", "mp"), None),
        P(("groups", "cells", "slots", "mp")),
        P(("groups", "cells", "slots", "mp")),
        P(("groups", "cells", "slots", "mp")),
        P(),
        P("cells", None, "mp"),
        P("mp", "cells"),
        P("cells", None, "mp"),
        P("mp", "cells"),
    )
    return jax.shard_map(
        on_device,
        mesh=mesh,
        in_specs=placed,
        out_specs=P(("groups", "cells", "slots", "mp"), None, None),
        check_vma=False,
    )
```

time: 209 us -> 162 us (0.78)
  local copies, waits for them, and re-layouts: 31.8 us -> 12 us
  starting transfers between devices: 45.8 us -> 30.3 us
  waiting for transfers between devices: 94.1 us -> 86.2 us
  Pallas kernels: 34.5 us -> 30.3 us
    ppermute x21 -> x7, waiting for transfers between devices: 86.9 us -> 33.7 us  [the longest x1 14.1 us: shares_along_cells(): below = [lax.ppermute(share_rows, 'cells', up)]]
    all_to_all x1, waiting for transfers between devices: 0.01 us -> 46.7 us  [tokens_by_blocks(): lax.all_to_all(blocks, ('cells', 'mp'), split_axis=0, concat_axis=0, tile...]
    ppermute x21 -> x7, starting transfers between devices: 38.9 us -> 10.4 us  [the longest x1 3.1 us: shares_along_cells(): below = [lax.ppermute(share_rows, 'cells', up)]]
    all_to_all x0 -> x1, starting transfers between devices: none -> 14.4 us  [tokens_by_blocks(): lax.all_to_all(codes, ('cells', 'mp'), split_axis=0, concat_axis=0, tiled...]
    unnamed x62 -> x21, local copies, waits for them, and re-layouts: 19.4 us -> 5.74 us
    slice x10 -> x2, local copies, waits for them, and re-layouts: 7.52 us -> 2.45 us  [the longest x1 1.23 us: pieces_of_all(): far_b = lax.ppermute(by_group[:, cut:], 'slots', swap)]
    pallas_call x5 -> x3, Pallas kernels: 29.2 us -> 25.1 us  [the longest x2 21.7 us: layer(): pl.pallas_call(functools.partial(layer_kernel, plan, sections), out_shape...]
    concatenate x3 -> x1, local copies, waits for them, and re-layouts: 3.86 us -> 0.85 us  [pieces_of_all(): others = jnp.concatenate(shares, axis=0)]
  transfers between devices with their start and end apart: 25 -> 12, of which waited for: 8 -> 5; matrix products, arithmetic and copies ran while one was open for 8% -> 6% of each run, Pallas kernels for 15% -> 11%
where the time goes in v5:
time: 162 us
  waiting for transfers between devices  86.2 us (53%)
  starting transfers between devices  30.3 us (19%)
  Pallas kernels  30.3 us (19%)
  local copies, waits for them, and re-layouts  12 us (7%)
  other arithmetic  1.81 us (1%)
    all_to_all x1, waiting for transfers between devices, tokens_by_blocks(): lax.all_to_all(blocks, ('cells', 'mp'), split_axis=0, concat_axis=0, tile...  46.7 us
    pallas_call x2, Pallas kernels, layer(): pl.pallas_call(functools.partial(layer_kernel, plan, sections), out_shape...  21.7 us
    all_to_all x1, starting transfers between devices, tokens_by_blocks(): lax.all_to_all(codes, ('cells', 'mp'), split_axis=0, concat_axis=0, tiled...  14.4 us
    ppermute x1, waiting for transfers between devices, shares_along_cells(): below = [lax.ppermute(share_rows, 'cells', up)]  14.1 us
    ppermute x1, waiting for transfers between devices, pieces_of_all(): far_b = lax.ppermute(by_group[:, cut:], 'slots', swap)  13.3 us
    ppermute x1, waiting for transfers between devices, shares_along_cells(): line.append(lax.ppermute(line[-1], 'cells', way))  6.19 us
    ppermute x1, waiting for transfers between devices, tokens_by_blocks(): other = lax.ppermute(send, 'slots', [(0, 1), (1, 0)])  5.83 us
    unnamed x21, local copies, waits for them, and re-layouts  5.74 us
  transfers between devices with their start and end apart: 12, of which 5 were waited for; matrix products, arithmetic and copies ran while one was open for 6% of the time, Pallas kernels for 11%

profile of v5, /device:TPU:0, one launch (start us, length us, event | category | flops | bytes accessed | tf_op | source)
XLA Modules:
  0.0 161.5 jit_solution(302756425919942312)
XLA Ops:
  0.0 0.8 dynamic-slice_bitcast_fusion.2
  0.9 0.9 dynamic-slice_bitcast_fusion.1
  1.8 0.9 dynamic-slice_bitcast_fusion
  2.7 1.2 constant_dynamic-slice_fusion
  4.0 3.1 %collective-permute-start.1 = (bf16[48,6144]{1,0:T(8,128)(2,1)S(1)}, bf16[48,6144]{1,0:T(8,128)(2,1)S(1)}, u32[]{:S(2)}, u32[]{:S(2)}) collective-permute-start(bf16[48,6144]{1,0:T(8,128)(2,1)S(1)} %pad_maximum_fusion.1), channel_id=1, source_target_pairs={{0,4},{4,8},{8,12},{12,0},{1,5},{5,9},{9,13},{13,1},{2,6},{6,10},{... | collective-permute-start | bytes 1769480 | tf_op jit(solution)/shard_map/ppermute | solution.py:290
  7.1 2.1 %collective-permute-start = (bf16[48,6144]{1,0:T(8,128)(2,1)S(1)}, bf16[48,6144]{1,0:T(8,128)(2,1)}, u32[]{:S(2)}, u32[]{:S(2)}) collective-permute-start(bf16[48,6144]{1,0:T(8,128)(2,1)S(1)} %pad_maximum_fusion.1), channel_id=1, source_target_pairs={{0,12},{4,0},{8,4},{12,8},{1,13},{5,1},{9,5},{13,9},{2,14},{6,2},{... | collective-permute-start | bytes 1769480 | tf_op jit(solution)/shard_map/ppermute | solution.py:291
  9.2 14.1 %collective-permute-done.1 = bf16[48,6144]{1,0:T(8,128)(2,1)S(1)} collective-permute-done((bf16[48,6144]{1,0:T(8,128)(2,1)S(1)}, bf16[48,6144]{1,0:T(8,128)(2,1)S(1)}, u32[]{:S(2)}, u32[]{:S(2)}) %collective-permute-start.1) | collective-permute-done | bytes 589856 | tf_op jit(solution)/shard_map/ppermute | solution.py:290
  23.3 0.0 collective-permute-start.2
  24.0 3.4 %place_rows.1 = (bf16[8,192,768]{2,1,0:T(8,128)(2,1)}, s32[8,1,192]{2,1,0:T(1,128)}) custom-call(s32[1,512]{1,0:T(1,128)S(1)} %bitcast.22, s32[1,512]{1,0:T(1,128)S(1)} %bitcast.21, bf16[512,768]{1,0:T(8,128)(2,1)S(1)} %copy-done), custom_call_target="tpu_custom_call" | custom-call | flops 1207959552 | bytes 3145728 | tf_op jit(solution)/shard_map/place_rows/pallas_call | solution.py:63
  27.4 14.4 %all-to-all-start = ((s32[8,1,192]{2,1,0:T(1,128)}), s32[8,1,192]{2,1,0:T(1,128)S(1)}, u32[]{:S(2)}, u32[]{:S(2)}) async-start(s32[8,1,192]{2,1,0:T(1,128)} %get-tuple-element.13), calls=%async_computation | async-start | bytes 16384 | tf_op jit(solution)/shard_map/all_to_all | solution.py:335
  41.8 0.0 collective-permute-done
  41.8 6.2 %collective-permute-done.2 = bf16[48,6144]{1,0:T(8,128)(2,1)} collective-permute-done((bf16[48,6144]{1,0:T(8,128)(2,1)S(1)}, bf16[48,6144]{1,0:T(8,128)(2,1)}, u32[]{:S(2)}, u32[]{:S(2)}) %collective-permute-start.2) | collective-permute-done | bytes 589856 | tf_op jit(solution)/shard_map/ppermute | solution.py:294
  48.0 0.0 all-to-all-done.code_ref
  48.0 3.8 %all-to-all-start.1 = ((bf16[8,192,768]{2,1,0:T(8,128)(2,1)}), bf16[8,192,768]{2,1,0:T(8,128)(2,1)S(1)}, u32[]{:S(2)}, u32[]{:S(2)}) async-start(bf16[8,192,768]{2,1,0:T(8,128)(2,1)} %get-tuple-element.15), calls=%async_computation.1 | async-start | bytes 4718592 | tf_op jit(solution)/shard_map/all_to_all | solution.py:337
  51.8 0.0 copy-start.1
  51.8 1.9 %constant_dynamic-update-slice_fusion.2 = bf16[144,6144]{1,0:T(8,128)(2,1)} fusion(bf16[48,6144]{1,0:T(8,128)(2,1)} %collective-permute-done), kind=kLoop, calls=%fused_computation.15 | loop fusion | bytes 1179648
  53.7 1.9 %constant_dynamic-update-slice_fusion.1 = bf16[144,6144]{1,0:T(8,128)(2,1)} fusion(bf16[144,6144]{1,0:T(8,128)(2,1)} %constant_dynamic-update-slice_fusion.2, bf16[48,6144]{1,0:T(8,128)(2,1)} %collective-permute-done.2), kind=kLoop, calls=%fused_computation.14 | loop fusion | bytes 1179648
  55.7 0.9 constant_dynamic-update-slice_fusion.refs_1_
  56.5 1.5 collective-permute-start.5
  58.0 1.5 collective-permute-start.4
  59.5 46.7 %all-to-all-done.1.got_ref = bf16[8,192,768]{2,1,0:T(8,128)(2,1)S(1)} async-done(((bf16[8,192,768]{2,1,0:T(8,128)(2,1)}), bf16[8,192,768]{2,1,0:T(8,128)(2,1)S(1)}, u32[]{:S(2)}, u32[]{:S(2)}) %all-to-all-start.1) | async-done | bytes 2359328 | tf_op jit(solution)/shard_map/all_to_all | solution.py:337
  106.2 2.0 %pool_rows.1 = (bf16[256,768]{1,0:T(8,128)(2,1)S(1)}, bf16[256,768]{1,0:T(8,128)(2,1)S(1)}) custom-call(s32[1]{0:T(128)} %bitcast.slot_ref, bf16[8,768]{1,0:T(8,128)(2,1)S(1)} %copy-done.1, s32[8,1,192]{2,1,0:T(1,128)S(1)} %all-to-all-done.code_ref, bf16[8,192,768]{2,1,0:T(8,128)(2,1)S(1)} %all-to-all-done.1.got_ref), custom_call_target="tpu_custom_call" | custom-call | flops 1207959552 | bytes 2359296 | tf_op jit(solution)/shard_map/pool_rows/pallas_call | solution.py:106
  108.3 1.6 collective-permute-start.3
  109.8 0.0 collective-permute-done.5.refs_3_
  109.8 1.2 slice.9
  111.1 0.6 collective-permute-start.7
  111.7 0.0 collective-permute-done.4.refs_2_
  111.7 1.2 slice.8
  112.9 1.6 collective-permute-start.6
  114.5 0.1 compare_select_fusion.2.order_ref
  114.5 5.8 %collective-permute-done.3.got_ref = bf16[256,768]{1,0:T(8,128)(2,1)S(1)} collective-permute-done((bf16[256,768]{1,0:T(8,128)(2,1)S(1)}, bf16[256,768]{1,0:T(8,128)(2,1)S(1)}, u32[]{:S(2)}, u32[]{:S(2)}) %collective-permute-start.3) | collective-permute-done | bytes 393248 | tf_op jit(solution)/shard_map/ppermute | solution.py:339
  120.4 1.5 weave_steps.1.tok_ref
  121.8 0.0 copy-start.3
  121.9 0.0 copy-start.5
  121.9 0.1 collective-permute-start.8
  122.0 0.0 copy-done.2
  122.0 0.1 copy.17
  122.2 0.7 copy-done.3
  122.9 0.0 copy-done.5
  122.9 1.7 %pad_maximum_fusion.refs_0_ = bf16[192,6144]{1,0:T(8,128)(2,1)} fusion(bf16[192,1536]{1,0:T(8,128)(2,1)S(1)} %bitcast.28, bf16[192,384]{1,0:T(8,128)(2,1)S(1)} %bitcast.31, bf16[192,3072]{1,0:T(8,128)(2,1)S(1)} %bitcast.23, bf16[192,1152]{1,0:T(8,128)(2,1)S(1)} %bitcast.25), kind=kLoop, calls=%fused_computation | loop fusion | flops 9437184 | bytes 4718592 | tf_op jit(solution)/shard_map/concatenate | solution.py:283
  124.6 13.3 %collective-permute-done.7.refs_5_ = bf16[144,3072]{1,0:T(8,128)(2,1)S(1)} collective-permute-done((bf16[144,3072]{1,0:T(8,128)(2,1)S(1)}, bf16[144,3072]{1,0:T(8,128)(2,1)S(1)}, u32[]{:S(2)}, u32[]{:S(2)}) %collective-permute-start.7) | collective-permute-done | bytes 884768 | tf_op jit(solution)/shard_map/ppermute | solution.py:306
  138.0 0.0 collective-permute-done.6.refs_4_
  138.0 0.0 collective-permute-done.8.tok_ref
  138.0 10.8 %layer.3 = bf16[512,768]{1,0:T(8,128)(2,1)S(1)} custom-call(bf16[512,768]{1,0:T(8,128)(2,1)S(1)} %collective-permute-done.8.tok_ref, bf16[192,6144]{1,0:T(8,128)(2,1)} %pad_maximum_fusion.refs_0_, bf16[144,6144]{1,0:T(8,128)(2,1)} %constant_dynamic-update-slice_fusion.refs_1_, bf16[144,6144]{1,0:T(8,128)(2,1)} %collective-permute-done.4.refs_2_, ...), custom_call_target="tpu_custom_call" | custom-call | flops 4831838208 | bytes 11796480 | tf_op jit(solution)/shard_map/layer/pallas_call | solution.py:237
  148.8 0.1 collective-permute-start.9
  148.9 10.8 %layer.2.sum_ref = f32[512,768]{1,0:T(8,128)S(1)} custom-call(bf16[512,768]{1,0:T(8,128)(2,1)S(1)} %weave_steps.1.tok_ref, bf16[192,6144]{1,0:T(8,128)(2,1)} %pad_maximum_fusion.refs_0_, bf16[144,6144]{1,0:T(8,128)(2,1)} %constant_dynamic-update-slice_fusion.refs_1_, bf16[144,6144]{1,0:T(8,128)(2,1)} %collective-permute-done.4.refs_2_, ...), custom_call_target="tpu_custom_call" | custom-call | flops 4831838208 | bytes 11796480 | tf_op jit(solution)/shard_map/layer/pallas_call | solution.py:237
  159.7 0.0 collective-permute-done.9.got_ref
  159.7 1.8 %finish.1 = bf16[512,768]{1,0:T(8,128)(2,1)} custom-call(bf16[512,768]{1,0:T(8,128)(2,1)S(1)} %weave_steps.1.tok_ref, f32[512,768]{1,0:T(8,128)S(1)} %layer.2.sum_ref, bf16[512,768]{1,0:T(8,128)(2,1)S(1)} %collective-permute-done.9.got_ref, s32[1,768]{1,0:T(1,128)S(1)} %compare_select_fusion.2.order_ref), custom_call_target="tpu_custom_call" | custom-call | flops 603979776 | bytes 3932160 | tf_op jit(solution)/shard_map/finish/pallas_call | solution.py:268
  (15 shorter events, 0.2 us)
Async XLA Ops:
  0.0 24.0 %copy-start.6 = (s32[512]{0:T(512)S(1)}, s32[512]{0:T(512)}, u32[]{:S(2)}) copy-start(s32[512]{0:T(512)} %param.11) | copy-start | bytes 6148
  0.0 24.0 %copy-start.7 = (s32[512]{0:T(512)S(1)}, s32[512]{0:T(512)}, u32[]{:S(2)}) copy-start(s32[512]{0:T(512)} %param.10) | copy-start | bytes 6148
  0.0 24.0 %copy-start = (bf16[512,768]{1,0:T(8,128)(2,1)S(1)}, bf16[512,768]{1,0:T(8,128)(2,1)}, u32[]{:S(2)}) copy-start(bf16[512,768]{1,0:T(8,128)(2,1)} %feat_ref.1) | copy-start | bytes 2359300
  4.0 19.3 %collective-permute-start.1 = (bf16[48,6144]{1,0:T(8,128)(2,1)S(1)}, bf16[48,6144]{1,0:T(8,128)(2,1)S(1)}, u32[]{:S(2)}, u32[]{:S(2)}) collective-permute-start(bf16[48,6144]{1,0:T(8,128)(2,1)S(1)} %pad_maximum_fusion.1), channel_id=1, source_target_pairs={{0,4},{4,8},{8,12},{12,0},{1,5},{5,9},{9,13},{13,1},{2,6},{6,10},{... | collective-permute-start | bytes 1769480 | tf_op jit(solution)/shard_map/ppermute | solution.py:290
  7.1 34.7 %collective-permute-start = (bf16[48,6144]{1,0:T(8,128)(2,1)S(1)}, bf16[48,6144]{1,0:T(8,128)(2,1)}, u32[]{:S(2)}, u32[]{:S(2)}) collective-permute-start(bf16[48,6144]{1,0:T(8,128)(2,1)S(1)} %pad_maximum_fusion.1), channel_id=1, source_target_pairs={{0,12},{4,0},{8,4},{12,8},{1,13},{5,1},{9,5},{13,9},{2,14},{6,2},{... | collective-permute-start | bytes 1769480 | tf_op jit(solution)/shard_map/ppermute | solution.py:291
  23.3 24.7 %collective-permute-start.2 = (bf16[48,6144]{1,0:T(8,128)(2,1)S(1)}, bf16[48,6144]{1,0:T(8,128)(2,1)}, u32[]{:S(2)}, u32[]{:S(2)}) collective-permute-start(bf16[48,6144]{1,0:T(8,128)(2,1)S(1)} %collective-permute-done.1), channel_id=1, source_target_pairs={{0,4},{4,8},{8,12},{12,0},{1,5},{5,9},{9,13},{13,1},{2,6},{6,10},{... | collective-permute-start | bytes 1769480 | tf_op jit(solution)/shard_map/ppermute | solution.py:294
  27.4 20.6 %all-to-all-start = ((s32[8,1,192]{2,1,0:T(1,128)}), s32[8,1,192]{2,1,0:T(1,128)S(1)}, u32[]{:S(2)}, u32[]{:S(2)}) async-start(s32[8,1,192]{2,1,0:T(1,128)} %get-tuple-element.13), calls=%async_computation | async-start | bytes 16384 | tf_op jit(solution)/shard_map/all_to_all | solution.py:335
  48.0 58.2 %all-to-all-start.1 = ((bf16[8,192,768]{2,1,0:T(8,128)(2,1)}), bf16[8,192,768]{2,1,0:T(8,128)(2,1)S(1)}, u32[]{:S(2)}, u32[]{:S(2)}) async-start(bf16[8,192,768]{2,1,0:T(8,128)(2,1)} %get-tuple-element.15), calls=%async_computation.1 | async-start | bytes 4718592 | tf_op jit(solution)/shard_map/all_to_all | solution.py:337
  51.8 54.4 %copy-start.1 = (bf16[8,768]{1,0:T(8,128)(2,1)S(1)}, bf16[8,768]{1,0:T(8,128)(2,1)}, u32[]{:S(2)}) copy-start(bf16[8,768]{1,0:T(8,128)(2,1)} %embed_ref.1) | copy-start | bytes 36868
  56.5 53.3 %collective-permute-start.5 = (bf16[144,6144]{1,0:T(8,128)(2,1)}, bf16[144,6144]{1,0:T(8,128)(2,1)}, u32[]{:S(2)}, u32[]{:S(2)}) collective-permute-start(bf16[144,6144]{1,0:T(8,128)(2,1)} %constant_dynamic-update-slice_fusion.refs_1_), channel_id=1, source_target_pairs={{0,16},{16,0},{1,17},{17,1},{2,18},{18,2},{3,19},{19,3},{4,20},{20... | collective-permute-start | bytes 5308424 | tf_op jit(solution)/shard_map/ppermute | solution.py:303
  58.0 53.6 %collective-permute-start.4 = (bf16[144,6144]{1,0:T(8,128)(2,1)}, bf16[144,6144]{1,0:T(8,128)(2,1)}, u32[]{:S(2)}, u32[]{:S(2)}) collective-permute-start(bf16[144,6144]{1,0:T(8,128)(2,1)} %constant_dynamic-update-slice_fusion.refs_1_), channel_id=1, source_target_pairs={{0,2},{2,0},{1,3},{3,1},{4,6},{6,4},{5,7},{7,5},{8,10},{10,8},{9,1... | collective-permute-start | bytes 5308424 | tf_op jit(solution)/shard_map/ppermute | solution.py:302
  108.3 12.1 %collective-permute-start.3 = (bf16[256,768]{1,0:T(8,128)(2,1)S(1)}, bf16[256,768]{1,0:T(8,128)(2,1)S(1)}, u32[]{:S(2)}, u32[]{:S(2)}) collective-permute-start(bf16[256,768]{1,0:T(8,128)(2,1)S(1)} %get-tuple-element.17), channel_id=1, source_target_pairs={{0,2},{2,0},{1,3},{3,1},{4,6},{6,4},{5,7},{7,5},{8,10},{10,8},{9,1... | collective-permute-start | bytes 1179656 | tf_op jit(solution)/shard_map/ppermute | solution.py:339
  111.1 26.9 %collective-permute-start.7 = (bf16[144,3072]{1,0:T(8,128)(2,1)S(1)}, bf16[144,3072]{1,0:T(8,128)(2,1)S(1)}, u32[]{:S(2)}, u32[]{:S(2)}) collective-permute-start(bf16[144,3072]{1,0:T(8,128)(2,1)S(1)} %slice.9), channel_id=1, source_target_pairs={{0,2},{2,0},{1,3},{3,1},{4,6},{6,4},{5,7},{7,5},{8,10},{10,8},{9,1... | collective-permute-start | bytes 2654216 | tf_op jit(solution)/shard_map/ppermute | solution.py:306
  112.9 25.1 %collective-permute-start.6 = (bf16[144,3072]{1,0:T(8,128)(2,1)S(1)}, bf16[144,3072]{1,0:T(8,128)(2,1)S(1)}, u32[]{:S(2)}, u32[]{:S(2)}) collective-permute-start(bf16[144,3072]{1,0:T(8,128)(2,1)S(1)} %slice.8), channel_id=1, source_target_pairs={{0,16},{16,0},{1,17},{17,1},{2,18},{18,2},{3,19},{19,3},{4,20},{20... | collective-permute-start | bytes 2654216 | tf_op jit(solution)/shard_map/ppermute | solution.py:305
  120.4 1.6 copy-start.4
  120.4 1.6 %copy-start.2 = (bf16[192,2,1536]{2,1,0:T(2,128)(2,1)S(1)}, bf16[192,2,1536]{2,1,0:T(2,128)(2,1)}, u32[]{:S(2)}) copy-start(bf16[192,2,1536]{2,1,0:T(2,128)(2,1)} %param.16) | copy-start | bytes 3538948
  121.8 1.1 copy-start.3
  121.9 1.1 copy-start.5
  121.9 16.1 %collective-permute-start.8 = (bf16[512,768]{1,0:T(8,128)(2,1)S(1)}, bf16[512,768]{1,0:T(8,128)(2,1)S(1)}, u32[]{:S(2)}, u32[]{:S(2)}) collective-permute-start(bf16[512,768]{1,0:T(8,128)(2,1)S(1)} %weave_steps.1.tok_ref), channel_id=1, source_target_pairs={{0,1},{1,0},{2,3},{3,2},{4,5},{5,4},{6,7},{7,6},{8,9},{9,8},{10,11... | collective-permute-start | bytes 2359304 | tf_op jit(solution)/shard_map/ppermute | solution.py:407
  148.8 10.9 %collective-permute-start.9 = (bf16[512,768]{1,0:T(8,128)(2,1)S(1)}, bf16[512,768]{1,0:T(8,128)(2,1)S(1)}, u32[]{:S(2)}, u32[]{:S(2)}) collective-permute-start(bf16[512,768]{1,0:T(8,128)(2,1)S(1)} %layer.3), channel_id=1, source_target_pairs={{0,1},{1,0},{2,3},{3,2},{4,5},{5,4},{6,7},{7,6},{8,9},{9,8},{10,11... | collective-permute-start | bytes 2359304 | tf_op jit(solution)/shard_map/ppermute | solution.py:409

commit v6 on v5

--- a/solution.py
+++ b/solution.py
@@ -186,74 +186,88 @@
     return dot_t(hidden, down_w)
 
 
-def layer_kernel(plan, sections, tok_ref, *refs):
-    pieces, (out_ref, w_ref, norm_ref, ctx_ref, acc_ref, sems) = refs[:-6], refs[-6:]
+def layer_kernel(plan, sections, with_heads, n_sets, n_pieces, places, *refs):
+    refs = list(refs)
+    take = lambda count: [refs.pop(0) for _ in range(count)]
+    tokens = take(n_sets)
+    sums = take(0 if with_heads else n_sets)
+    pieces = take(n_pieces)
+    outs = take(n_sets)
+    w_ref, norm_ref, ctx_ref, acc_ref, sems = refs
     copies = {}
-    for number, (section, piece, source_col, row, col, size) in enumerate(plan):
+    for number, (section, piece, slot, n_rows, source_col, row, col, size) in enumerate(plan):
+        source_row = 0 if slot is None else pl.multiple_of(places[slot], 16)
         copy = pltpu.make_async_copy(
-            pieces[piece].at[:, pl.ds(source_col, size)],
-            w_ref.at[pl.ds(row, pieces[piece].shape[0]), pl.ds(col, size)],
+            pieces[piece].at[pl.ds(source_row, n_rows), pl.ds(source_col, size)],
+            w_ref.at[pl.ds(row, n_rows), pl.ds(col, size)],
             sems.at[number],
         )
         copy.start()
         copies.setdefault(section, []).append(copy)
 
     def columns(section):
-        for copy in copies[section]:
+        for copy in copies.pop(section, []):
             copy.wait()
         begin, end = sections[section]
         return w_ref[:, begin:end]
 
-    tokens = tok_ref[...].astype(F32)
-    scale = lax.rsqrt(jnp.mean(tokens * tokens, axis=1, keepdims=True) + EPS)
-    norm_ref[...] = (tokens * scale).astype(BF16)
-    attention(norm_ref[...], columns(0), ctx_ref.shape[1], ctx_ref)
-    acc_ref[...] = dot_t(ctx_ref[...], columns(1))
-    for at in range(2, len(sections), 3):
-        add = gated(norm_ref[...], columns(at), columns(at + 1), columns(at + 2))
-        if at + 3 < len(sections):
-            acc_ref[...] += add
-        else:
-            out_ref[...] = (acc_ref[...] + add).astype(out_ref.dtype)
-
-
-def layer(tokens, pieces, heads_width, hidden_width, out_type):
-    rows, width = tokens.shape
+    for number in range(n_sets):
+        rows = tokens[number][...].astype(F32)
+        scale = lax.rsqrt(jnp.mean(rows * rows, axis=1, keepdims=True) + EPS)
+        norm_ref[number] = (rows * scale).astype(BF16)
+    first = 0
+    if with_heads:
+        for number in range(n_sets):
+            attention(norm_ref[number], columns(0), ctx_ref.shape[1], ctx_ref)
+            acc_ref[number] = dot_t(ctx_ref[...], columns(1))
+        first = 2
+    for at in range(first, len(sections), 3):
+        for number in range(n_sets):
+            add = gated(norm_ref[number], columns(at), columns(at + 1), columns(at + 2))
+            so_far = sums[number][...] if at == 0 else acc_ref[number]
+            if at + 3 < len(sections):
+                acc_ref[number] = so_far + add
+            else:
+                outs[number][...] = (so_far + add).astype(outs[number].dtype)
+
+
+def layer(places, tokens, sums, pieces, heads_width, n_units, out_type):
+    n_sets = len(tokens)
+    rows, width = tokens[0].shape
     gate_at = 3 * heads_width
-    up_at = gate_at + hidden_width
-    out_at = up_at + hidden_width
+    up_at = gate_at + n_units * UNIT
+    out_at = up_at + n_units * UNIT
     down_at = out_at + heads_width
-    columns = down_at + hidden_width
-    unit = min(UNIT, hidden_width)
-    sections = [(0, gate_at), (out_at, down_at)]
-    for begin in range(0, hidden_width, unit):
-        sections += [(at + begin, at + begin + unit) for at in (gate_at, up_at, down_at)]
+    columns = down_at + n_units * UNIT
+    sections = [(0, gate_at), (out_at, down_at)] if heads_width else []
+    for begin in range(0, n_units * UNIT, UNIT):
+        sections += [(at + begin, at + begin + UNIT) for at in (gate_at, up_at, down_at)]
     plan = []
     for section, (left, right) in enumerate(sections):
-        for number, (array, row, at) in enumerate(pieces):
+        for number, (array, slot, row, n_rows, at) in enumerate(pieces):
             low, high = max(left, at), min(right, at + array.shape[1])
             if low < high:
-                plan.append((section, number, low - at, row, low, high - low))
+                plan.append((section, number, slot, n_rows, low - at, row, low, high - low))
     return pl.pallas_call(
-        functools.partial(layer_kernel, plan, sections),
-        out_shape=jax.ShapeDtypeStruct((rows, width), out_type),
-        in_specs=[WHOLE] + [pl.BlockSpec(memory_space=pl.ANY)] * len(pieces),
-        out_specs=WHOLE,
+        functools.partial(layer_kernel, plan, sections, heads_width > 0, n_sets, len(pieces)),
+        out_shape=[jax.ShapeDtypeStruct((rows, width), out_type)] * n_sets,
+        in_specs=[SCALARS] + [WHOLE] * (n_sets + len(sums)) + [pl.BlockSpec(memory_space=pl.ANY)] * len(pieces),
+        out_specs=[WHOLE] * n_sets,
         scratch_shapes=[
             pltpu.VMEM((width, columns), BF16),
-            pltpu.VMEM((rows, width), BF16),
-            pltpu.VMEM((rows, heads_width), BF16),
-            pltpu.VMEM((rows, width), F32),
+            pltpu.VMEM((n_sets, rows, width), BF16),
+            pltpu.VMEM((rows, max(heads_width, LANES)), BF16),
+            pltpu.VMEM((n_sets, rows, width), F32),
             pltpu.SemaphoreType.DMA((len(plan),)),
         ],
         compiler_params=params(),
         cost_estimate=pl.CostEstimate(
-            flops=2 * rows * width * columns,
-            bytes_accessed=2 * width * columns + 6 * rows * width,
-            transcendentals=rows * hidden_width,
+            flops=2 * n_sets * rows * width * columns,
+            bytes_accessed=2 * width * columns + 6 * n_sets * rows * width,
+            transcendentals=n_sets * n_units * rows * UNIT,
         ),
-        name="layer",
-    )(tokens, *[array for array, _, _ in pieces])
+        name="layer_heads" if heads_width else "layer_gated",
+    )(places, *tokens, *sums, *[piece[0] for piece in pieces])
 
 
 def finish_kernel(tok_ref, sum_ref, got_ref, order_ref, out_ref):
@@ -278,9 +292,12 @@
     )(tokens, sums, got, order.reshape(1, width))
 
 
-def side_by_side(w_qkv, w_out, w_gate_up, w_down):
+def side_by_side(w_qkv, w_out, w_gate_up, w_down, first, last, with_heads):
     rows = w_qkv.shape[0]
-    return jnp.concatenate([w_qkv.reshape(rows, -1), w_gate_up.reshape(rows, -1), w_out, w_down], axis=1)
+    gate_up = w_gate_up[:, :, first:last].reshape(rows, -1)
+    down = w_down[:, first:last]
+    parts = [w_qkv.reshape(rows, -1), gate_up, w_out, down] if with_heads else [gate_up, down]
+    return jnp.concatenate(parts, axis=1)
 
 
 def shares_along_cells(share_rows):
@@ -295,23 +312,27 @@
     return above + below[::-1]
 
 
-def pieces_of_all(shard, shares):
-    rows = shard.shape[0]
-    others = jnp.concatenate(shares, axis=0)
+def pieces_by_gather(shard, others, n_share):
+    rows, step = shard.shape[0], others.shape[0]
+    shares = lax.all_gather(others, ("groups", "slots"), axis=0, tiled=True)
+    return [(shard, None, 0, rows, 0)] + [(shares, far, rows + far * step, step, 0) for far in range(n_share)]
+
+
+def pieces_by_permutes(shard, others):
+    rows, step = shard.shape[0], others.shape[0]
     swap = [(0, 1), (1, 0)]
     by_slot = lax.ppermute(others, "slots", swap)
     by_group = lax.ppermute(others, "groups", swap)
     cut = shard.shape[1] // (2 * LANES) * LANES
     far_a = lax.ppermute(by_slot[:, :cut], "groups", swap)
     far_b = lax.ppermute(by_group[:, cut:], "slots", swap)
-    step = others.shape[0]
     return [
-        (shard, 0, 0),
-        (others, rows, 0),
-        (by_slot, rows + step, 0),
-        (by_group, rows + 2 * step, 0),
-        (far_a, rows + 3 * step, 0),
-        (far_b, rows + 3 * step, cut),
+        (shard, None, 0, rows, 0),
+        (others, None, rows, step, 0),
+        (by_slot, None, rows + step, step, 0),
+        (by_group, None, rows + 2 * step, step, 0),
+        (far_a, None, rows + 3 * step, step, 0),
+        (far_b, None, rows + 3 * step, step, cut),
     ]
 
 
@@ -329,15 +350,13 @@
     return jnp.where(place < rows, mine * rows + place, far)
 
 
-def tokens_by_blocks(owner, position, obs_feat, time_embed, my_slot, capacity, slot_dev, order, shares):
-    n_owners = lax.axis_size("cells") * lax.axis_size("mp")
-    blocks, codes = place_rows(owner, position, obs_feat, n_owners, capacity)
-    codes = lax.all_to_all(codes, ("cells", "mp"), split_axis=0, concat_axis=0, tiled=True)
-    blocks, *shares = lax.optimization_barrier((blocks, *shares))
+def tokens_by_blocks(blocks, codes, time_embed, my_slot, slot_dev, order, shares, later):
+    blocks, codes, *shares = lax.optimization_barrier((blocks, codes, *shares))
     got = lax.all_to_all(blocks, ("cells", "mp"), split_axis=0, concat_axis=0, tiled=True)
-    keep, send = pool_rows(my_slot.reshape(1), time_embed, codes, got, capacity, slot_dev)
+    got, later = lax.optimization_barrier((got, later))
+    keep, send = pool_rows(my_slot.reshape(1), time_embed, codes, got, blocks.shape[1], slot_dev)
     other = lax.ppermute(send, "slots", [(0, 1), (1, 0)])
-    return weave_steps(my_slot.reshape(1), order, keep, other, slot_dev), shares
+    return weave_steps(my_slot.reshape(1), order, keep, other, slot_dev), shares, later
 
 
 def tokens_by_exchanges(owner, position, obs_feat, time_embed, my_slot, capacity, slot_dev):
@@ -389,25 +408,39 @@
 
     local_weights = (w_qkv, w_out.T, w_gate_up, w_down.T)
     which = lax.axis_index("groups") * n_slots + my_slot
-    share_rows = side_by_side(*[lax.dynamic_slice_in_dim(w, which * share, share, 0) for w in local_weights])
+    share_weights = [lax.dynamic_slice_in_dim(w, which * share, share, 0) for w in local_weights]
+    heads_width, hidden_width = w_qkv.shape[2], w_gate_up.shape[2]
+    early = hidden_width - UNIT
+    part_a, part_b = (0, early, True), (early, hidden_width, False)
+    share_a, share_b = side_by_side(*share_weights, *part_a), side_by_side(*share_weights, *part_b)
     if n_slots == 2 and n_groups == 2 and share % 16 == 0 and capacity % 16 == 0:
         order = arrival_order(width, n_cells, n_share)
-        shares = shares_along_cells(share_rows)
-        tokens, shares = tokens_by_blocks(
-            owner, position, obs_feat, time_embed, my_slot, capacity, slot_dev, order, shares
+        shares = shares_along_cells(share_a)
+        blocks, codes = place_rows(owner, position, obs_feat, n_owners, capacity)
+        codes = lax.all_to_all(codes, ("cells", "mp"), split_axis=0, concat_axis=0, tiled=True)
+        tokens, shares, share_b = tokens_by_blocks(
+            blocks, codes, time_embed, my_slot, slot_dev, order, shares, share_b
         )
-        pieces = pieces_of_all(side_by_side(*local_weights), shares)
+        others_a = jnp.concatenate(shares, axis=0)
+        pieces_a = pieces_by_gather(side_by_side(*local_weights, *part_a), others_a, n_share)
+        places = (jnp.arange(n_share, dtype=jnp.int32) ^ which) * others_a.shape[0]
+        others_b = jnp.concatenate(shares_along_cells(share_b), axis=0)
+        pieces_b = pieces_by_permutes(side_by_side(*local_weights, *part_b), others_b)
     else:
         order = jnp.arange(width, dtype=jnp.int32)
-        pieces = [(lax.all_gather(share_rows, ("cells", "groups", "slots"), axis=0, tiled=True), 0, 0)]
+        axes = ("cells", "groups", "slots")
+        pieces_a, pieces_b = [
+            [(lax.all_gather(mine, axes, axis=0, tiled=True), None, 0, width, 0)] for mine in (share_a, share_b)
+        ]
+        places = jnp.zeros((n_share,), jnp.int32)
         tokens = tokens_by_exchanges(owner, position, obs_feat, time_embed, my_slot, capacity, slot_dev)
 
     swap = [(0, 1), (1, 0)]
-    heads_width, hidden_width = w_qkv.shape[2], w_gate_up.shape[2]
     partner = lax.ppermute(tokens, "mp", swap)
-    for_partner = layer(partner, pieces, heads_width, hidden_width, BF16)
+    sums = layer(places, [partner, tokens], [], pieces_a, heads_width, early // UNIT, F32)
+    (for_partner,) = layer(places, [partner], sums[:1], pieces_b, 0, 1, BF16)
     from_partner = lax.ppermute(for_partner, "mp", swap)
-    own = layer(tokens, pieces, heads_width, hidden_width, F32)
+    (own,) = layer(places, [tokens], sums[1:], pieces_b, 0, 1, F32)
     return finish(tokens, own, from_partner, order).reshape(quarter, TSTEPS, width)
 
 

time: 162 us -> 176 us (1.086)
  blocking collectives: 0 us -> 16.6 us
  between operations: 0.86 us -> 14.4 us
  starting transfers between devices: 30.3 us -> 20.4 us
  waiting for transfers between devices: 86.2 us -> 78.4 us
    all_to_all x0 -> x1, blocking collectives: none -> 16.6 us  [on_device(): lax.all_to_all(codes, ('cells', 'mp'), split_axis=0, concat_axis=0, tiled...]
    all_to_all x1 -> x0, starting transfers between devices: 14.4 us -> none  [tokens_by_blocks(): lax.all_to_all(codes, ('cells', 'mp'), split_axis=0, concat_axis=0, tiled...]
    all_to_all x1, waiting for transfers between devices: 46.7 us -> 52.3 us  [tokens_by_blocks(): lax.all_to_all(blocks, ('cells', 'mp'), split_axis=0, concat_axis=0, tile...]
    ppermute x4, waiting for transfers between devices: 13.4 us -> 8.18 us  [the longest x1 8.17 us: pieces_by_permutes(): by_slot = lax.ppermute(others, 'slots', swap)]
    ppermute x1, waiting for transfers between devices: 5.83 us -> 0.82 us  [tokens_by_blocks(): other = lax.ppermute(send, 'slots', [(0, 1), (1, 0)])]
    slice x2 -> x13, local copies, waits for them, and re-layouts: 2.45 us -> 4.82 us  [the longest x6 2.09 us: side_by_side(): gate_up = w_gate_up[:, :, first:last].reshape(rows, -1)]
    ppermute x1 -> x2, waiting for transfers between devices: 14.1 us -> 11.8 us  [shares_along_cells(): below = [lax.ppermute(share_rows, 'cells', up)]]
    ppermute x1 -> x2, waiting for transfers between devices: 6.19 us -> 5.24 us  [shares_along_cells(): line.append(lax.ppermute(line[-1], 'cells', way))]
  transfers between devices with their start and end apart: 12 -> 15, of which waited for: 5 -> 6; matrix products, arithmetic and copies ran while one was open for 6% -> 3% of each run, Pallas kernels for 11% -> 15%
where the time goes in v6:
time: 176 us; the launch traced here: 175 us
  waiting for transfers between devices  78.4 us (45%)
  Pallas kernels  31 us (18%)
  starting transfers between devices  20.4 us (12%)
  blocking collectives  16.6 us (9%)
  between operations  14.4 us (8%)
  local copies, waits for them, and re-layouts  11.9 us (7%)
  other arithmetic  2.81 us (2%)
    all_to_all x1, waiting for transfers between devices, tokens_by_blocks(): lax.all_to_all(blocks, ('cells', 'mp'), split_axis=0, concat_axis=0, tile...  52.3 us
    pallas_call x3, Pallas kernels, layer(): pl.pallas_call(functools.partial(layer_kernel, plan, sections, heads_widt...  22.3 us
    all_to_all x1, blocking collectives, on_device(): lax.all_to_all(codes, ('cells', 'mp'), split_axis=0, concat_axis=0, tiled...  16.6 us
    ppermute x2, waiting for transfers between devices, shares_along_cells(): below = [lax.ppermute(share_rows, 'cells', up)]  11.8 us
    ppermute x1, waiting for transfers between devices, pieces_by_permutes(): by_slot = lax.ppermute(others, 'slots', swap)  8.17 us
    unnamed x29, local copies, waits for them, and re-layouts  5.25 us
    ppermute x2, waiting for transfers between devices, shares_along_cells(): line.append(lax.ppermute(line[-1], 'cells', way))  5.24 us
    ppermute x2, starting transfers between devices, shares_along_cells(): below = [lax.ppermute(share_rows, 'cells', up)]  3.86 us
  transfers between devices with their start and end apart: 15, of which 6 were waited for; matrix products, arithmetic and copies ran while one was open for 3% of the time, Pallas kernels for 15%

profile of v6, /device:TPU:0, one launch (start us, length us, event | category | flops | bytes accessed | tf_op | source)
XLA Modules:
  0.0 175.5 jit_solution(9334618393193911283)
XLA Ops:
  6.5 1.0 dynamic-slice_bitcast_fusion
  7.5 0.0 copy-start.7
  7.6 0.8 dynamic-slice_bitcast_fusion.2
  8.4 1.1 constant_dynamic-slice_fusion
  9.5 0.9 dynamic-slice_bitcast_fusion.1
  10.5 3.1 %collective-permute-start.1 = (bf16[48,4608]{1,0:T(8,128)(2,1)S(1)}, bf16[48,4608]{1,0:T(8,128)(2,1)S(1)}, u32[]{:S(2)}, u32[]{:S(2)}) collective-permute-start(bf16[48,4608]{1,0:T(8,128)(2,1)S(1)} %pad_maximum_fusion.3), channel_id=1, source_target_pairs={{0,4},{4,8},{8,12},{12,0},{1,5},{5,9},{9,13},{13,1},{2,6},{6,10},{... | collective-permute-start | bytes 1327112 | tf_op jit(solution)/shard_map/ppermute | solution.py:307
  13.6 2.1 %collective-permute-start = (bf16[48,4608]{1,0:T(8,128)(2,1)S(1)}, bf16[48,4608]{1,0:T(8,128)(2,1)S(1)}, u32[]{:S(2)}, u32[]{:S(2)}) collective-permute-start(bf16[48,4608]{1,0:T(8,128)(2,1)S(1)} %pad_maximum_fusion.3), channel_id=1, source_target_pairs={{0,12},{4,0},{8,4},{12,8},{1,13},{5,1},{9,5},{13,9},{2,14},{6,2},{... | collective-permute-start | bytes 1327112 | tf_op jit(solution)/shard_map/ppermute | solution.py:308
  15.6 11.0 %collective-permute-done.1 = bf16[48,4608]{1,0:T(8,128)(2,1)S(1)} collective-permute-done((bf16[48,4608]{1,0:T(8,128)(2,1)S(1)}, bf16[48,4608]{1,0:T(8,128)(2,1)S(1)}, u32[]{:S(2)}, u32[]{:S(2)}) %collective-permute-start.1) | collective-permute-done | bytes 442400 | tf_op jit(solution)/shard_map/ppermute | solution.py:307
  27.3 3.4 %place_rows.1 = (bf16[8,192,768]{2,1,0:T(8,128)(2,1)}, s32[8,1,192]{2,1,0:T(1,128)S(1)}) custom-call(s32[1,512]{1,0:T(1,128)S(1)} %bitcast.26, s32[1,512]{1,0:T(1,128)S(1)} %bitcast.25, bf16[512,768]{1,0:T(8,128)(2,1)S(1)} %copy-done.4), custom_call_target="tpu_custom_call" | custom-call | flops 1207959552 | bytes 3145728 | tf_op jit(solution)/shard_map/place_rows/pallas_call | solution.py:63
  30.7 16.6 %all_to_all.10.code_ref = s32[8,1,192]{2,1,0:T(1,128)S(1)} all-to-all(s32[8,1,192]{2,1,0:T(1,128)S(1)} %get-tuple-element.19), channel_id=1, replica_groups=mesh['groups'=2,'cells'=4,'slots'=2,'mp'=2] {'cells','mp'}, dimensions={0} | all-to-all | bytes 12288 | tf_op jit(solution)/shard_map/all_to_all | solution.py:420
  47.3 1.3 pad_maximum_fusion.1
  48.6 0.0 all-gather.2.cloned.1.call-update
  48.6 3.6 %all-to-all-start.1 = ((bf16[8,192,768]{2,1,0:T(8,128)(2,1)}), bf16[8,192,768]{2,1,0:T(8,128)(2,1)S(1)}, u32[]{:S(2)}, u32[]{:S(2)}) async-start(bf16[8,192,768]{2,1,0:T(8,128)(2,1)} %get-tuple-element.21), calls=%async_computation.1 | async-start | bytes 4718592 | tf_op jit(solution)/shard_map/all_to_all | solution.py:355
  52.3 0.0 slice-start
  52.3 0.0 slice-start.2
  52.3 1.0 constant_dynamic-slice_fusion.1
  53.3 1.0 slice.43
  54.4 0.1 compare_select_fusion.2.order_ref
  54.5 52.3 %all-to-all-done.1.got_ref = bf16[8,192,768]{2,1,0:T(8,128)(2,1)S(1)} async-done(((bf16[8,192,768]{2,1,0:T(8,128)(2,1)}), bf16[8,192,768]{2,1,0:T(8,128)(2,1)S(1)}, u32[]{:S(2)}, u32[]{:S(2)}) %all-to-all-start.1) | async-done | bytes 2359328 | tf_op jit(solution)/shard_map/all_to_all | solution.py:355
  106.8 1.2 collective-permute-start.5
  108.1 0.8 collective-permute-start.6
  108.9 1.0 slice.42
  109.9 0.0 copy-start.6
  109.9 0.2 copy.18
  110.1 0.8 copy-done.6
  111.0 2.1 %pool_rows.1 = (bf16[256,768]{1,0:T(8,128)(2,1)S(1)}, bf16[256,768]{1,0:T(8,128)(2,1)S(1)}) custom-call(s32[1]{0:T(128)} %bitcast.slot_ref, bf16[8,768]{1,0:T(8,128)(2,1)S(1)} %copy-done.5, s32[8,1,192]{2,1,0:T(1,128)S(1)} %all_to_all.10.code_ref, bf16[8,192,768]{2,1,0:T(8,128)(2,1)S(1)} %all-to-all-done.1.got_ref), custom_call_target="tpu_custom_call" | custom-call | flops 1207959552 | bytes 2359296 | tf_op jit(solution)/shard_map/pool_rows/pallas_call | solution.py:106
  113.0 1.6 collective-permute-start.3
  114.6 0.8 collective-permute-done.6
  115.4 1.7 collective-permute-start.7
  117.1 5.2 %collective-permute-done.7 = bf16[48,1536]{1,0:T(8,128)(2,1)S(1)} collective-permute-done((bf16[48,1536]{1,0:T(8,128)(2,1)S(1)}, bf16[48,1536]{1,0:T(8,128)(2,1)S(1)}, u32[]{:S(2)}, u32[]{:S(2)}) %collective-permute-start.7) | collective-permute-done | bytes 147488 | tf_op jit(solution)/shard_map/ppermute | solution.py:311
  122.4 0.8 collective-permute-done.3.got_ref
  123.2 1.5 weave_steps.1.refs_1_.refs_0_.tok_ref
  124.7 0.1 collective-permute-start.4
  124.8 1.6 collective-permute-start.8
  126.3 1.5 collective-permute-start.9
  127.8 1.4 pad_maximum_fusion.refs_2_
  129.2 8.2 %collective-permute-done.8.refs_4_ = bf16[144,1536]{1,0:T(8,128)(2,1)S(1)} collective-permute-done((bf16[144,1536]{1,0:T(8,128)(2,1)S(1)}, bf16[144,1536]{1,0:T(8,128)(2,1)S(1)}, u32[]{:S(2)}, u32[]{:S(2)}) %collective-permute-start.8) | collective-permute-done | bytes 442400 | tf_op jit(solution)/shard_map/ppermute | solution.py:324
  137.4 1.6 collective-permute-start.10
  139.0 0.7 slice.45
  139.7 1.5 collective-permute-start.11
  141.2 0.9 copy-done.1
  142.1 1.1 copy-done.2
  143.2 15.9 %layer_heads.1 = (f32[512,768]{1,0:T(8,128)S(1)}, f32[512,768]{1,0:T(8,128)S(1)}) custom-call(s32[4]{0:T(128)S(1)} %xor_multiply_fusion.places, bf16[512,768]{1,0:T(8,128)(2,1)S(1)} %copy-done.2, bf16[512,768]{1,0:T(8,128)(2,1)S(1)} %weave_steps.1.refs_1_.refs_0_.tok_ref, bf16[192,4608]{1,0:T(8,128)(2,1)} %pad_maximum_fusion.refs_2_, ...), custom_call_target="tpu_custom_call" | custom-call | flops 7247757312 | bytes 11796480 | tf_op jit(solution)/shard_map/layer_heads/pallas_call | solution.py:251
  159.1 1.2 copy-done
  160.3 2.8 %layer_gated.3 = bf16[512,768]{1,0:T(8,128)(2,1)S(1)} custom-call(s32[4]{0:T(128)S(1)} %xor_multiply_fusion.places, bf16[512,768]{1,0:T(8,128)(2,1)S(1)} %copy-done.3, f32[512,768]{1,0:T(8,128)S(1)} %get-tuple-element.30.refs_1_, bf16[192,1536]{1,0:T(8,128)(2,1)S(1)} %pad_maximum_fusion.2.refs_2_, ...), custom_call_target="tpu_custom_call" | custom-call | flops 1207959552 | bytes 4718592 | tf_op jit(solution)/shard_map/layer_gated/pallas_call | solution.py:251
  163.1 0.1 collective-permute-start.12
  163.2 3.7 %layer_gated.2.sum_ref = f32[512,768]{1,0:T(8,128)S(1)} custom-call(s32[4]{0:T(128)S(1)} %xor_multiply_fusion.places, bf16[512,768]{1,0:T(8,128)(2,1)S(1)} %weave_steps.1.refs_1_.refs_0_.tok_ref, f32[512,768]{1,0:T(8,128)} %copy-done, bf16[192,1536]{1,0:T(8,128)(2,1)S(1)} %pad_maximum_fusion.2.refs_2_, ...), custom_call_target="tpu_custom_call" | custom-call | flops 1207959552 | bytes 4718592 | tf_op jit(solution)/shard_map/layer_gated/pallas_call | solution.py:251
  166.8 1.8 %finish.1 = bf16[512,768]{1,0:T(8,128)(2,1)} custom-call(bf16[512,768]{1,0:T(8,128)(2,1)S(1)} %weave_steps.1.refs_1_.refs_0_.tok_ref, f32[512,768]{1,0:T(8,128)S(1)} %layer_gated.2.sum_ref, bf16[512,768]{1,0:T(8,128)(2,1)S(1)} %collective-permute-done.12.got_ref, s32[1,768]{1,0:T(1,128)S(1)} %compare_select_fusion.2.order_ref), custom_call_target="tpu_custom_call" | custom-call | flops 603979776 | bytes 3932160 | tf_op jit(solution)/shard_map/finish/pallas_call | solution.py:282
  (46 shorter events, 0.4 us)
Async XLA Ops:
  6.5 20.7 %copy-start.9 = (s32[512]{0:T(512)S(1)}, s32[512]{0:T(512)}, u32[]{:S(2)}) copy-start(s32[512]{0:T(512)} %param.11) | copy-start | bytes 6148
  6.5 20.8 %copy-start.10 = (s32[512]{0:T(512)S(1)}, s32[512]{0:T(512)}, u32[]{:S(2)}) copy-start(s32[512]{0:T(512)} %param.10) | copy-start | bytes 6148
  6.5 20.8 %copy-start.4 = (bf16[512,768]{1,0:T(8,128)(2,1)S(1)}, bf16[512,768]{1,0:T(8,128)(2,1)}, u32[]{:S(2)}) copy-start(bf16[512,768]{1,0:T(8,128)(2,1)} %feat_ref.1) | copy-start | bytes 2359300
  6.5 135.5 %all-gather.2.cloned.1.call-start = ((), (), s32[]{:S(2)}) async-start(), calls=%async_computation.2 | async-start | bytes 6635520 | tf_op jit(solution)/shard_map/all_gather | solution.py:317
  7.5 44.7 %copy-start.7 = (bf16[48,1536]{1,0:T(8,128)(2,1)}, bf16[48,1536]{1,0:T(8,128)(2,1)S(1)}, u32[]{:S(2)}) copy-start(bf16[48,1536]{1,0:T(8,128)(2,1)S(1)} %dynamic-slice_bitcast_fusion) | copy-start | bytes 442372
  10.5 16.1 %collective-permute-start.1 = (bf16[48,4608]{1,0:T(8,128)(2,1)S(1)}, bf16[48,4608]{1,0:T(8,128)(2,1)S(1)}, u32[]{:S(2)}, u32[]{:S(2)}) collective-permute-start(bf16[48,4608]{1,0:T(8,128)(2,1)S(1)} %pad_maximum_fusion.3), channel_id=1, source_target_pairs={{0,4},{4,8},{8,12},{12,0},{1,5},{5,9},{9,13},{13,1},{2,6},{6,10},{... | collective-permute-start | bytes 1327112 | tf_op jit(solution)/shard_map/ppermute | solution.py:307
  13.6 33.8 %collective-permute-start = (bf16[48,4608]{1,0:T(8,128)(2,1)S(1)}, bf16[48,4608]{1,0:T(8,128)(2,1)S(1)}, u32[]{:S(2)}, u32[]{:S(2)}) collective-permute-start(bf16[48,4608]{1,0:T(8,128)(2,1)S(1)} %pad_maximum_fusion.3), channel_id=1, source_target_pairs={{0,12},{4,0},{8,4},{12,8},{1,13},{5,1},{9,5},{13,9},{2,14},{6,2},{... | collective-permute-start | bytes 1327112 | tf_op jit(solution)/shard_map/ppermute | solution.py:308
  26.6 20.7 %collective-permute-start.2 = (bf16[48,4608]{1,0:T(8,128)(2,1)S(1)}, bf16[48,4608]{1,0:T(8,128)(2,1)S(1)}, u32[]{:S(2)}, u32[]{:S(2)}) collective-permute-start(bf16[48,4608]{1,0:T(8,128)(2,1)S(1)} %collective-permute-done.1), channel_id=1, source_target_pairs={{0,4},{4,8},{8,12},{12,0},{1,5},{5,9},{9,13},{13,1},{2,6},{6,10},{... | collective-permute-start | bytes 1327112 | tf_op jit(solution)/shard_map/ppermute | solution.py:311
  48.6 58.2 %all-to-all-start.1 = ((bf16[8,192,768]{2,1,0:T(8,128)(2,1)}), bf16[8,192,768]{2,1,0:T(8,128)(2,1)S(1)}, u32[]{:S(2)}, u32[]{:S(2)}) async-start(bf16[8,192,768]{2,1,0:T(8,128)(2,1)} %get-tuple-element.21), calls=%async_computation.1 | async-start | bytes 4718592 | tf_op jit(solution)/shard_map/all_to_all | solution.py:355
  52.3 2.1 %slice-start = ((bf16[192,2,1536]{2,1,0:T(2,128)(2,1)}), bf16[192,2,512]{2,1,0:T(2,128)(2,1)S(1)}, s32[]{:S(2)}) async-start(bf16[192,2,1536]{2,1,0:T(2,128)(2,1)} %param.16), calls=%async_computation.3 | async-start | bytes 786432 | tf_op jit(solution)/shard_map/slice | solution.py:297
  52.3 2.2 %slice-start.2 = ((bf16[48,1536]{1,0:T(8,128)(2,1)}), bf16[48,512]{1,0:T(8,128)(2,1)S(1)}, s32[]{:S(2)}) async-start(bf16[48,1536]{1,0:T(8,128)(2,1)} %copy-done.7), calls=%async_computation.5 | async-start | bytes 98304 | tf_op jit(solution)/shard_map/slice | solution.py:298
  106.8 3.1 %slice-start.1 = ((bf16[192,2,1536]{2,1,0:T(2,128)(2,1)}), bf16[192,2,1024]{2,1,0:T(2,128)(2,1)S(1)}, s32[]{:S(2)}) async-start(bf16[192,2,1536]{2,1,0:T(2,128)(2,1)} %param.16), calls=%async_computation.4 | async-start | bytes 1572864 | tf_op jit(solution)/shard_map/slice | solution.py:297
  106.8 10.3 %collective-permute-start.5 = (bf16[48,1536]{1,0:T(8,128)(2,1)S(1)}, bf16[48,1536]{1,0:T(8,128)(2,1)S(1)}, u32[]{:S(2)}, u32[]{:S(2)}) collective-permute-start(bf16[48,1536]{1,0:T(8,128)(2,1)S(1)} %pad_maximum_fusion.4), channel_id=1, source_target_pairs={{0,12},{4,0},{8,4},{12,8},{1,13},{5,1},{9,5},{13,9},{2,14},{6,2},{... | collective-permute-start | bytes 442376 | tf_op jit(solution)/shard_map/ppermute | solution.py:308
  108.1 7.3 %collective-permute-start.6 = (bf16[48,1536]{1,0:T(8,128)(2,1)S(1)}, bf16[48,1536]{1,0:T(8,128)(2,1)S(1)}, u32[]{:S(2)}, u32[]{:S(2)}) collective-permute-start(bf16[48,1536]{1,0:T(8,128)(2,1)S(1)} %pad_maximum_fusion.4), channel_id=1, source_target_pairs={{0,4},{4,8},{8,12},{12,0},{1,5},{5,9},{9,13},{13,1},{2,6},{6,10},{... | collective-permute-start | bytes 442376 | tf_op jit(solution)/shard_map/ppermute | solution.py:307
  109.9 1.0 copy-start.6
  109.9 1.1 copy-start.5
  113.0 10.2 %collective-permute-start.3 = (bf16[256,768]{1,0:T(8,128)(2,1)S(1)}, bf16[256,768]{1,0:T(8,128)(2,1)S(1)}, u32[]{:S(2)}, u32[]{:S(2)}) collective-permute-start(bf16[256,768]{1,0:T(8,128)(2,1)S(1)} %get-tuple-element.24), channel_id=1, source_target_pairs={{0,2},{2,0},{1,3},{3,1},{4,6},{6,4},{5,7},{7,5},{8,10},{10,8},{9,1... | collective-permute-start | bytes 1179656 | tf_op jit(solution)/shard_map/ppermute | solution.py:358
  115.4 6.9 %collective-permute-start.7 = (bf16[48,1536]{1,0:T(8,128)(2,1)S(1)}, bf16[48,1536]{1,0:T(8,128)(2,1)S(1)}, u32[]{:S(2)}, u32[]{:S(2)}) collective-permute-start(bf16[48,1536]{1,0:T(8,128)(2,1)S(1)} %collective-permute-done.6), channel_id=1, source_target_pairs={{0,4},{4,8},{8,12},{12,0},{1,5},{5,9},{9,13},{13,1},{2,6},{6,10},{... | collective-permute-start | bytes 442376 | tf_op jit(solution)/shard_map/ppermute | solution.py:311
  123.2 4.6 %copy-start.8 = (bf16[384,192]{0,1:T(8,128)(2,1)S(1)}, bf16[384,192]{0,1:T(8,128)(2,1)}, u32[]{:S(2)}) copy-start(bf16[384,192]{0,1:T(8,128)(2,1)} %param.15) | copy-start | bytes 442372
  124.7 16.5 %collective-permute-start.4 = (bf16[512,768]{1,0:T(8,128)(2,1)S(1)}, bf16[512,768]{1,0:T(8,128)(2,1)S(1)}, u32[]{:S(2)}, u32[]{:S(2)}) collective-permute-start(bf16[512,768]{1,0:T(8,128)(2,1)S(1)} %weave_steps.1.refs_1_.refs_0_.tok_ref), channel_id=1, source_target_pairs={{0,1},{1,0},{2,3},{3,2},{4,5},{5,4},{6,7},{7,6},{8,9},{9,8},{10,11... | collective-permute-start | bytes 2359304 | tf_op jit(solution)/shard_map/ppermute | solution.py:439
  124.8 12.6 %collective-permute-start.8 = (bf16[144,1536]{1,0:T(8,128)(2,1)S(1)}, bf16[144,1536]{1,0:T(8,128)(2,1)S(1)}, u32[]{:S(2)}, u32[]{:S(2)}) collective-permute-start(bf16[144,1536]{1,0:T(8,128)(2,1)S(1)} %constant_dynamic-update-slice_fusion.refs_3_), channel_id=1, source_target_pairs={{0,2},{2,0},{1,3},{3,1},{4,6},{6,4},{5,7},{7,5},{8,10},{10,8},{9,1... | collective-permute-start | bytes 1327112 | tf_op jit(solution)/shard_map/ppermute | solution.py:324
  126.3 12.7 %collective-permute-start.9 = (bf16[144,1536]{1,0:T(8,128)(2,1)S(1)}, bf16[144,1536]{1,0:T(8,128)(2,1)S(1)}, u32[]{:S(2)}, u32[]{:S(2)}) collective-permute-start(bf16[144,1536]{1,0:T(8,128)(2,1)S(1)} %constant_dynamic-update-slice_fusion.refs_3_), channel_id=1, source_target_pairs={{0,16},{16,0},{1,17},{17,1},{2,18},{18,2},{3,19},{19,3},{4,20},{20... | collective-permute-start | bytes 1327112 | tf_op jit(solution)/shard_map/ppermute | solution.py:325
  137.4 22.9 %collective-permute-start.10 = (bf16[144,768]{1,0:T(8,128)(2,1)S(1)}, bf16[144,768]{1,0:T(8,128)(2,1)S(1)}, u32[]{:S(2)}, u32[]{:S(2)}) collective-permute-start(bf16[144,768]{1,0:T(8,128)(2,1)S(1)} %slice.44), channel_id=1, source_target_pairs={{0,16},{16,0},{1,17},{17,1},{2,18},{18,2},{3,19},{19,3},{4,20},{20... | collective-permute-start | bytes 663560 | tf_op jit(solution)/shard_map/ppermute | solution.py:327
  139.7 20.6 %collective-permute-start.11 = (bf16[144,768]{1,0:T(8,128)(2,1)}, bf16[144,768]{1,0:T(8,128)(2,1)S(1)}, u32[]{:S(2)}, u32[]{:S(2)}) collective-permute-start(bf16[144,768]{1,0:T(8,128)(2,1)} %slice.45), channel_id=1, source_target_pairs={{0,2},{2,0},{1,3},{3,1},{4,6},{6,4},{5,7},{7,5},{8,10},{10,8},{9,1... | collective-permute-start | bytes 663560 | tf_op jit(solution)/shard_map/ppermute | solution.py:328
  141.2 0.9 copy-start.1
  142.1 1.1 copy-start.2
  143.2 17.1 %copy-start.3 = (bf16[512,768]{1,0:T(8,128)(2,1)S(1)}, bf16[512,768]{1,0:T(8,128)(2,1)}, u32[]{:S(2)}) copy-start(bf16[512,768]{1,0:T(8,128)(2,1)} %copy-done.1) | copy-start | bytes 2359300
  159.1 1.2 copy-start
  163.1 3.7 %collective-permute-start.12 = (bf16[512,768]{1,0:T(8,128)(2,1)S(1)}, bf16[512,768]{1,0:T(8,128)(2,1)S(1)}, u32[]{:S(2)}, u32[]{:S(2)}) collective-permute-start(bf16[512,768]{1,0:T(8,128)(2,1)S(1)} %layer_gated.3), channel_id=1, source_target_pairs={{0,1},{1,0},{2,3},{3,2},{4,5},{5,4},{6,7},{7,6},{8,9},{9,8},{10,11... | collective-permute-start | bytes 2359304 | tf_op jit(solution)/shard_map/ppermute | solution.py:442
Sparse Core Ops, SparseCore 0:
  48.7 60.2 all-gather.1

commit v7 on v6

--- a/solution.py
+++ b/solution.py
@@ -160,20 +160,25 @@
     row, col = iota((2 * group, group), 0), iota((2 * group, group), 1)
     same_cell = row % group // TSTEPS == col // TSTEPS
     count = jnp.ones((group, LANES), BF16)
+    begins = range(0, rows, group)
     for pair in range(heads_width // LANES):
         at = pair * LANES
         query = (head_scale(projected[:, at : at + LANES], ones) * HD ** (-0.5)).astype(BF16)
         key = head_scale(projected[:, heads_width + at : heads_width + at + LANES], ones).astype(BF16)
         value = projected[:, 2 * heads_width + at : 2 * heads_width + at + LANES].astype(BF16)
-        for begin in range(0, rows, group):
-            q = query[begin : begin + group]
-            k = key[begin : begin + group]
-            v = value[begin : begin + group]
-            none = jnp.zeros_like(q)
-            both = jnp.concatenate([jnp.where(first, q, none), jnp.where(first, none, q)], axis=0)
-            expo = jnp.where(same_cell, jnp.exp(dot_t(both, k)), 0.0).astype(BF16)
-            mixed = dot(expo, jnp.concatenate([v, count], axis=1))
-            top, low = mixed[:group], mixed[group:]
+        none = jnp.zeros_like(query)
+        first_rows = iota((rows, LANES), 1) < HD
+        left, right = jnp.where(first_rows, query, none), jnp.where(first_rows, none, query)
+        scores = [
+            dot_t(jnp.concatenate([left[at : at + group], right[at : at + group]], axis=0), key[at : at + group])
+            for at in begins
+        ]
+        expos = [jnp.where(same_cell, jnp.exp(score), 0.0).astype(BF16) for score in scores]
+        mixed = [
+            dot(expo, jnp.concatenate([value[at : at + group], count], axis=1)) for at, expo in zip(begins, expos)
+        ]
+        for begin, both in zip(begins, mixed):
+            top, low = both[:group], both[group:]
             over = jnp.where(first, top[:, :LANES], low[:, :LANES])
             under = jnp.where(first, top[:, LANES:], low[:, LANES:])
             ctx_ref[begin : begin + group, at : at + LANES] = (over / under).astype(BF16)
@@ -186,7 +191,7 @@
     return dot_t(hidden, down_w)
 
 
-def layer_kernel(plan, sections, with_heads, n_sets, n_pieces, places, *refs):
+def layer_kernel(plan, sections, with_heads, n_sets, n_pieces, *refs):
     refs = list(refs)
     take = lambda count: [refs.pop(0) for _ in range(count)]
     tokens = take(n_sets)
@@ -195,11 +200,10 @@
     outs = take(n_sets)
     w_ref, norm_ref, ctx_ref, acc_ref, sems = refs
     copies = {}
-    for number, (section, piece, slot, n_rows, source_col, row, col, size) in enumerate(plan):
-        source_row = 0 if slot is None else pl.multiple_of(places[slot], 16)
+    for number, (section, piece, source_col, row, col, size) in enumerate(plan):
         copy = pltpu.make_async_copy(
-            pieces[piece].at[pl.ds(source_row, n_rows), pl.ds(source_col, size)],
-            w_ref.at[pl.ds(row, n_rows), pl.ds(col, size)],
+            pieces[piece].at[:, pl.ds(source_col, size)],
+            w_ref.at[pl.ds(row, pieces[piece].shape[0]), pl.ds(col, size)],
             sems.at[number],
         )
         copy.start()
@@ -231,7 +235,7 @@
                 outs[number][...] = (so_far + add).astype(outs[number].dtype)
 
 
-def layer(places, tokens, sums, pieces, heads_width, n_units, out_type):
+def layer(tokens, sums, pieces, heads_width, n_units, out_type):
     n_sets = len(tokens)
     rows, width = tokens[0].shape
     gate_at = 3 * heads_width
@@ -244,14 +248,14 @@
         sections += [(at + begin, at + begin + UNIT) for at in (gate_at, up_at, down_at)]
     plan = []
     for section, (left, right) in enumerate(sections):
-        for number, (array, slot, row, n_rows, at) in enumerate(pieces):
+        for number, (array, row, at) in enumerate(pieces):
             low, high = max(left, at), min(right, at + array.shape[1])
             if low < high:
-                plan.append((section, number, slot, n_rows, low - at, row, low, high - low))
+                plan.append((section, number, low - at, row, low, high - low))
     return pl.pallas_call(
         functools.partial(layer_kernel, plan, sections, heads_width > 0, n_sets, len(pieces)),
         out_shape=[jax.ShapeDtypeStruct((rows, width), out_type)] * n_sets,
-        in_specs=[SCALARS] + [WHOLE] * (n_sets + len(sums)) + [pl.BlockSpec(memory_space=pl.ANY)] * len(pieces),
+        in_specs=[WHOLE] * (n_sets + len(sums)) + [pl.BlockSpec(memory_space=pl.ANY)] * len(pieces),
         out_specs=[WHOLE] * n_sets,
         scratch_shapes=[
             pltpu.VMEM((width, columns), BF16),
@@ -267,7 +271,7 @@
             transcendentals=n_sets * n_units * rows * UNIT,
         ),
         name="layer_heads" if heads_width else "layer_gated",
-    )(places, *tokens, *sums, *[piece[0] for piece in pieces])
+    )(*tokens, *sums, *[piece[0] for piece in pieces])
 
 
 def finish_kernel(tok_ref, sum_ref, got_ref, order_ref, out_ref):
@@ -300,40 +304,34 @@
     return jnp.concatenate(parts, axis=1)
 
 
-def shares_along_cells(share_rows):
+def along_cells(values, distance):
     n_cells = lax.axis_size("cells")
-    up = [(j, (j + 1) % n_cells) for j in range(n_cells)]
-    down = [(j, (j - 1) % n_cells) for j in range(n_cells)]
-    below = [lax.ppermute(share_rows, "cells", up)]
-    above = [lax.ppermute(share_rows, "cells", down)]
-    while len(below) + len(above) < n_cells - 1:
-        line, way = (below, up) if len(below) <= len(above) else (above, down)
-        line.append(lax.ppermute(line[-1], "cells", way))
+    return lax.ppermute(values, "cells", [(j, (j - distance) % n_cells) for j in range(n_cells)])
+
+
+def from_neighbours(share_rows):
+    return along_cells(share_rows, 1), along_cells(share_rows, -1)
+
+
+def from_all_cells(above, below):
+    above, below = [above], [below]
+    while len(above) + len(below) < lax.axis_size("cells") - 1:
+        line, way = (below, -1) if len(below) <= len(above) else (above, 1)
+        line.append(along_cells(line[-1], way))
     return above + below[::-1]
 
 
-def pieces_by_gather(shard, others, n_share):
-    rows, step = shard.shape[0], others.shape[0]
-    shares = lax.all_gather(others, ("groups", "slots"), axis=0, tiled=True)
-    return [(shard, None, 0, rows, 0)] + [(shares, far, rows + far * step, step, 0) for far in range(n_share)]
-
-
-def pieces_by_permutes(shard, others):
-    rows, step = shard.shape[0], others.shape[0]
-    swap = [(0, 1), (1, 0)]
-    by_slot = lax.ppermute(others, "slots", swap)
-    by_group = lax.ppermute(others, "groups", swap)
-    cut = shard.shape[1] // (2 * LANES) * LANES
-    far_a = lax.ppermute(by_slot[:, :cut], "groups", swap)
-    far_b = lax.ppermute(by_group[:, cut:], "slots", swap)
-    return [
-        (shard, None, 0, rows, 0),
-        (others, None, rows, step, 0),
-        (by_slot, None, rows + step, step, 0),
-        (by_group, None, rows + 2 * step, step, 0),
-        (far_a, None, rows + 3 * step, step, 0),
-        (far_b, None, rows + 3 * step, step, cut),
-    ]
+def pieces_of_all(shard, shares):
+    rows = shard.shape[0]
+    others = jnp.concatenate(shares, axis=0)
+    step = others.shape[0]
+    n_slots = lax.axis_size("slots")
+    n_share = lax.axis_size("groups") * n_slots
+    pieces = [(shard, 0, 0), (others, rows, 0)]
+    for far in range(1, n_share):
+        pairs = [(place, place ^ far) for place in range(n_share)]
+        pieces.append((lax.ppermute(others, ("groups", "slots"), pairs), rows + far * step, 0))
+    return pieces
 
 
 def arrival_order(width, n_cells, n_share):
@@ -350,13 +348,9 @@
     return jnp.where(place < rows, mine * rows + place, far)
 
 
-def tokens_by_blocks(blocks, codes, time_embed, my_slot, slot_dev, order, shares, later):
-    blocks, codes, *shares = lax.optimization_barrier((blocks, codes, *shares))
+def pooled_blocks(blocks, codes, time_embed, my_slot, slot_dev):
     got = lax.all_to_all(blocks, ("cells", "mp"), split_axis=0, concat_axis=0, tiled=True)
-    got, later = lax.optimization_barrier((got, later))
-    keep, send = pool_rows(my_slot.reshape(1), time_embed, codes, got, blocks.shape[1], slot_dev)
-    other = lax.ppermute(send, "slots", [(0, 1), (1, 0)])
-    return weave_steps(my_slot.reshape(1), order, keep, other, slot_dev), shares, later
+    return pool_rows(my_slot.reshape(1), time_embed, codes, got, blocks.shape[1], slot_dev)
 
 
 def tokens_by_exchanges(owner, position, obs_feat, time_embed, my_slot, capacity, slot_dev):
@@ -415,32 +409,33 @@
     share_a, share_b = side_by_side(*share_weights, *part_a), side_by_side(*share_weights, *part_b)
     if n_slots == 2 and n_groups == 2 and share % 16 == 0 and capacity % 16 == 0:
         order = arrival_order(width, n_cells, n_share)
-        shares = shares_along_cells(share_a)
+        shares = from_all_cells(*from_neighbours(share_a))
         blocks, codes = place_rows(owner, position, obs_feat, n_owners, capacity)
         codes = lax.all_to_all(codes, ("cells", "mp"), split_axis=0, concat_axis=0, tiled=True)
-        tokens, shares, share_b = tokens_by_blocks(
-            blocks, codes, time_embed, my_slot, slot_dev, order, shares, share_b
-        )
-        others_a = jnp.concatenate(shares, axis=0)
-        pieces_a = pieces_by_gather(side_by_side(*local_weights, *part_a), others_a, n_share)
-        places = (jnp.arange(n_share, dtype=jnp.int32) ^ which) * others_a.shape[0]
-        others_b = jnp.concatenate(shares_along_cells(share_b), axis=0)
-        pieces_b = pieces_by_permutes(side_by_side(*local_weights, *part_b), others_b)
+        blocks, codes, *shares = lax.optimization_barrier((blocks, codes, *shares))
+        pieces_a = pieces_of_all(side_by_side(*local_weights, *part_a), shares)
+        keep, send = pooled_blocks(blocks, codes, time_embed, my_slot, slot_dev)
+        arrays, share_b, send = lax.optimization_barrier(([piece[0] for piece in pieces_a], share_b, send))
+        pieces_a = [(array, *place) for array, (_, *place) in zip(arrays, pieces_a)]
+        other = lax.ppermute(send, "slots", [(0, 1), (1, 0)])
+        near_b = from_neighbours(share_b)
+        other, near_b = lax.optimization_barrier((other, near_b))
+        pieces_b = pieces_of_all(side_by_side(*local_weights, *part_b), from_all_cells(*near_b))
+        tokens = weave_steps(my_slot.reshape(1), order, keep, other, slot_dev)
     else:
         order = jnp.arange(width, dtype=jnp.int32)
         axes = ("cells", "groups", "slots")
         pieces_a, pieces_b = [
-            [(lax.all_gather(mine, axes, axis=0, tiled=True), None, 0, width, 0)] for mine in (share_a, share_b)
+            [(lax.all_gather(mine, axes, axis=0, tiled=True), 0, 0)] for mine in (share_a, share_b)
         ]
-        places = jnp.zeros((n_share,), jnp.int32)
         tokens = tokens_by_exchanges(owner, position, obs_feat, time_embed, my_slot, capacity, slot_dev)
 
     swap = [(0, 1), (1, 0)]
     partner = lax.ppermute(tokens, "mp", swap)
-    sums = layer(places, [partner, tokens], [], pieces_a, heads_width, early // UNIT, F32)
-    (for_partner,) = layer(places, [partner], sums[:1], pieces_b, 0, 1, BF16)
+    sums = layer([partner, tokens], [], pieces_a, heads_width, early // UNIT, F32)
+    (for_partner,) = layer([partner], sums[:1], pieces_b, 0, 1, BF16)
     from_partner = lax.ppermute(for_partner, "mp", swap)
-    (own,) = layer(places, [tokens], sums[1:], pieces_b, 0, 1, F32)
+    (own,) = layer([tokens], sums[1:], pieces_b, 0, 1, F32)
     return finish(tokens, own, from_partner, order).reshape(quarter, TSTEPS, width)
 
 

time: 176 us -> 164 us (0.932)
  between operations: 14.4 us -> 0.96 us
  local copies, waits for them, and re-layouts: 11.9 us -> 14.9 us
  waiting for transfers between devices: 78.4 us -> 76.5 us
    all_to_all x1, waiting for transfers between devices: 52.3 us -> 41.1 us  [pooled_blocks(): lax.all_to_all(blocks, ('cells', 'mp'), split_axis=0, concat_axis=0, tile...]
    ppermute x11 -> x13, waiting for transfers between devices: 26 us -> 35.4 us  [the longest x6 23.6 us: along_cells(): lax.ppermute(values, 'cells', [(j, (j - distance) % n_cells) for j in ran...]
    unnamed x29 -> x33, local copies, waits for them, and re-layouts: 5.25 us -> 7.43 us
    ppermute x11 -> x13, starting transfers between devices: 16.6 us -> 18.2 us  [the longest x6 9.91 us: along_cells(): lax.ppermute(values, 'cells', [(j, (j - distance) % n_cells) for j in ran...]
  transfers between devices with their start and end apart: 15 -> 16, of which waited for: 6 -> 7; matrix products, arithmetic and copies ran while one was open for 3% -> 7% of each run, Pallas kernels for 15% -> 15%
where the time goes in v7:
time: 164 us
  waiting for transfers between devices  76.5 us (47%)
  Pallas kernels  30.3 us (18%)
  starting transfers between devices  21.9 us (13%)
  blocking collectives  16.6 us (10%)
  local copies, waits for them, and re-layouts  14.9 us (9%)
  other arithmetic  2.67 us (2%)
    all_to_all x1, waiting for transfers between devices, pooled_blocks(): lax.all_to_all(blocks, ('cells', 'mp'), split_axis=0, concat_axis=0, tile...  41.1 us
    ppermute x6, waiting for transfers between devices, along_cells(): lax.ppermute(values, 'cells', [(j, (j - distance) % n_cells) for j in ran...  23.6 us
    pallas_call x3, Pallas kernels, layer(): pl.pallas_call(functools.partial(layer_kernel, plan, sections, heads_widt...  21.6 us
    all_to_all x1, blocking collectives, on_device(): lax.all_to_all(codes, ('cells', 'mp'), split_axis=0, concat_axis=0, tiled...  16.6 us
    ppermute x6, waiting for transfers between devices, pieces_of_all(): lax.ppermute(others, ('groups', 'slots'), pairs)  11.8 us
    ppermute x6, starting transfers between devices, along_cells(): lax.ppermute(values, 'cells', [(j, (j - distance) % n_cells) for j in ran...  9.91 us
    unnamed x33, local copies, waits for them, and re-layouts  7.43 us
    ppermute x6, starting transfers between devices, pieces_of_all(): lax.ppermute(others, ('groups', 'slots'), pairs)  7.04 us
  transfers between devices with their start and end apart: 16, of which 7 were waited for; matrix products, arithmetic and copies ran while one was open for 7% of the time, Pallas kernels for 15%

profile of v7, /device:TPU:0, one launch (start us, length us, event | category | flops | bytes accessed | tf_op | source)
XLA Modules:
  0.0 163.8 jit_solution(11997269656902973554)
XLA Ops:
  0.0 1.0 dynamic-slice_bitcast_fusion
  1.0 0.8 dynamic-slice_bitcast_fusion.2
  1.8 1.1 constant_dynamic-slice_fusion
  3.0 0.9 dynamic-slice_bitcast_fusion.1
  3.9 3.1 %collective-permute-start.1 = (bf16[48,4608]{1,0:T(8,128)(2,1)S(1)}, bf16[48,4608]{1,0:T(8,128)(2,1)S(1)}, u32[]{:S(2)}, u32[]{:S(2)}) collective-permute-start(bf16[48,4608]{1,0:T(8,128)(2,1)S(1)} %pad_maximum_fusion.2), channel_id=1, source_target_pairs={{0,4},{4,8},{8,12},{12,0},{1,5},{5,9},{9,13},{13,1},{2,6},{6,10},{... | collective-permute-start | bytes 1327112 | tf_op jit(solution)/shard_map/ppermute | solution.py:309
  7.0 2.1 %collective-permute-start = (bf16[48,4608]{1,0:T(8,128)(2,1)S(1)}, bf16[48,4608]{1,0:T(8,128)(2,1)S(1)}, u32[]{:S(2)}, u32[]{:S(2)}) collective-permute-start(bf16[48,4608]{1,0:T(8,128)(2,1)S(1)} %pad_maximum_fusion.2), channel_id=1, source_target_pairs={{0,12},{4,0},{8,4},{12,8},{1,13},{5,1},{9,5},{13,9},{2,14},{6,2},{... | collective-permute-start | bytes 1327112 | tf_op jit(solution)/shard_map/ppermute | solution.py:309
  9.1 11.0 %collective-permute-done.1 = bf16[48,4608]{1,0:T(8,128)(2,1)S(1)} collective-permute-done((bf16[48,4608]{1,0:T(8,128)(2,1)S(1)}, bf16[48,4608]{1,0:T(8,128)(2,1)S(1)}, u32[]{:S(2)}, u32[]{:S(2)}) %collective-permute-start.1) | collective-permute-done | bytes 442400 | tf_op jit(solution)/shard_map/ppermute | solution.py:309
  20.8 3.4 %place_rows.1 = (bf16[8,192,768]{2,1,0:T(8,128)(2,1)}, s32[8,1,192]{2,1,0:T(1,128)S(1)}) custom-call(s32[1,512]{1,0:T(1,128)S(1)} %bitcast.26, s32[1,512]{1,0:T(1,128)S(1)} %bitcast.25, bf16[512,768]{1,0:T(8,128)(2,1)S(1)} %copy-done.1), custom_call_target="tpu_custom_call" | custom-call | flops 1207959552 | bytes 3145728 | tf_op jit(solution)/shard_map/place_rows/pallas_call | solution.py:63
  24.2 16.6 %all_to_all.10.code_ref = s32[8,1,192]{2,1,0:T(1,128)S(1)} all-to-all(s32[8,1,192]{2,1,0:T(1,128)S(1)} %get-tuple-element.27), channel_id=1, replica_groups=mesh['groups'=2,'cells'=4,'slots'=2,'mp'=2] {'cells','mp'}, dimensions={0} | all-to-all | bytes 12288 | tf_op jit(solution)/shard_map/all_to_all | solution.py:414
  40.8 0.7 copy-done.7
  41.6 0.2 copy-done.8
  41.7 3.6 %all-to-all-start.1 = ((bf16[8,192,768]{2,1,0:T(8,128)(2,1)}), bf16[8,192,768]{2,1,0:T(8,128)(2,1)S(1)}, u32[]{:S(2)}, u32[]{:S(2)}) async-start(bf16[8,192,768]{2,1,0:T(8,128)(2,1)} %get-tuple-element.29), calls=%async_computation.1 | async-start | bytes 4718592 | tf_op jit(solution)/shard_map/all_to_all | solution.py:352
  45.4 1.8 %constant_dynamic-update-slice_fusion.2 = bf16[144,4608]{1,0:T(8,128)(2,1)} fusion(bf16[48,4608]{1,0:T(8,128)(2,1)} %copy-done.7), kind=kLoop, calls=%fused_computation.9 | loop fusion | bytes 884736
  47.2 1.9 %constant_dynamic-update-slice_fusion.1 = bf16[144,4608]{1,0:T(8,128)(2,1)} fusion(bf16[144,4608]{1,0:T(8,128)(2,1)} %constant_dynamic-update-slice_fusion.2, bf16[48,4608]{1,0:T(8,128)(2,1)} %copy-done.8), kind=kLoop, calls=%fused_computation.8 | loop fusion | bytes 884736
  49.1 0.8 constant_dynamic-update-slice_fusion.refs_3_
  49.9 1.5 collective-permute-start.3
  51.4 1.5 collective-permute-start.4
  52.9 0.5 collective-permute-start.5
  53.4 0.8 slice.33
  54.2 0.2 copy.17
  54.4 0.1 copy-done.5
  54.5 0.8 copy.15
  55.3 1.0 constant_dynamic-slice_fusion.1
  56.4 2.5 %pad_maximum_fusion.refs_2_ = bf16[192,4608]{1,0:T(8,128)(2,1)} fusion(bf16[192,1024]{1,0:T(8,128)(2,1)} %slice.33, bf16[192,384]{1,0:T(8,128)(2,1)S(1)} %bitcast.40, bf16[192,2048]{1,0:T(8,128)(2,1)S(1)} %bitcast.27, bf16[192,1152]{1,0:T(8,128)(2,1)} %bitcast.29), kind=kLoop, calls=%fused_computation | loop fusion | flops 7077888 | bytes 3538944 | tf_op jit(solution)/shard_map/concatenate | solution.py:304
  58.8 41.1 %all-to-all-done.1.got_ref = bf16[8,192,768]{2,1,0:T(8,128)(2,1)S(1)} async-done(((bf16[8,192,768]{2,1,0:T(8,128)(2,1)}), bf16[8,192,768]{2,1,0:T(8,128)(2,1)S(1)}, u32[]{:S(2)}, u32[]{:S(2)}) %all-to-all-start.1) | async-done | bytes 2359328 | tf_op jit(solution)/shard_map/all_to_all | solution.py:352
  100.0 2.1 %pool_rows.1 = (bf16[256,768]{1,0:T(8,128)(2,1)S(1)}, bf16[256,768]{1,0:T(8,128)(2,1)S(1)}) custom-call(s32[1]{0:T(128)} %bitcast.slot_ref, bf16[8,768]{1,0:T(8,128)(2,1)S(1)} %copy-done.2, s32[8,1,192]{2,1,0:T(1,128)S(1)} %all_to_all.10.code_ref, bf16[8,192,768]{2,1,0:T(8,128)(2,1)S(1)} %all-to-all-done.1.got_ref), custom_call_target="tpu_custom_call" | custom-call | flops 1207959552 | bytes 2359296 | tf_op jit(solution)/shard_map/pool_rows/pallas_call | solution.py:106
  102.1 9.2 %collective-permute-done.4.refs_5_ = bf16[144,4608]{1,0:T(8,128)(2,1)} collective-permute-done((bf16[144,4608]{1,0:T(8,128)(2,1)}, bf16[144,4608]{1,0:T(8,128)(2,1)}, u32[]{:S(2)}, u32[]{:S(2)}) %collective-permute-start.4) | collective-permute-done | bytes 1327136 | tf_op jit(solution)/shard_map/ppermute | solution.py:333
  111.3 1.2 collective-permute-start.6
  112.5 3.5 %collective-permute-start.7 = (bf16[48,1536]{1,0:T(8,128)(2,1)S(1)}, bf16[48,1536]{1,0:T(8,128)(2,1)S(1)}, u32[]{:S(2)}, u32[]{:S(2)}) collective-permute-start(bf16[48,1536]{1,0:T(8,128)(2,1)S(1)} %pad_maximum_fusion.3), channel_id=1, source_target_pairs={{0,12},{4,0},{8,4},{12,8},{1,13},{5,1},{9,5},{13,9},{2,14},{6,2},{... | collective-permute-start | bytes 442376 | tf_op jit(solution)/shard_map/ppermute | solution.py:309
  116.0 0.9 slice.35
  117.0 0.3 slice.30
  117.3 0.1 compare_select_fusion.2.order_ref
  117.4 2.5 %collective-permute-done.7 = bf16[48,1536]{1,0:T(8,128)(2,1)S(1)} collective-permute-done((bf16[48,1536]{1,0:T(8,128)(2,1)S(1)}, bf16[48,1536]{1,0:T(8,128)(2,1)S(1)}, u32[]{:S(2)}, u32[]{:S(2)}) %collective-permute-start.7) | collective-permute-done | bytes 147488 | tf_op jit(solution)/shard_map/ppermute | solution.py:309
  119.9 3.0 %collective-permute-done.8 = bf16[48,1536]{1,0:T(8,128)(2,1)S(1)} collective-permute-done((bf16[48,1536]{1,0:T(8,128)(2,1)S(1)}, bf16[48,1536]{1,0:T(8,128)(2,1)S(1)}, u32[]{:S(2)}, u32[]{:S(2)}) %collective-permute-start.8) | collective-permute-done | bytes 147488 | tf_op jit(solution)/shard_map/ppermute | solution.py:309
  122.9 1.5 weave_steps.1.refs_1_.refs_0_.tok_ref
  124.4 0.1 collective-permute-start.9
  124.5 1.2 collective-permute-start.10
  125.8 7.0 %collective-permute-done.10 = bf16[48,1536]{1,0:T(8,128)(2,1)S(1)} collective-permute-done((bf16[48,1536]{1,0:T(8,128)(2,1)S(1)}, bf16[48,1536]{1,0:T(8,128)(2,1)S(1)}, u32[]{:S(2)}, u32[]{:S(2)}) %collective-permute-start.10) | collective-permute-done | bytes 147488 | tf_op jit(solution)/shard_map/ppermute | solution.py:309
  132.8 0.9 collective-permute-start.11
  133.7 1.5 collective-permute-start.12
  135.2 1.2 collective-permute-start.13
  136.4 15.7 %layer_heads.1 = (f32[512,768]{1,0:T(8,128)}, f32[512,768]{1,0:T(8,128)}) custom-call(bf16[512,768]{1,0:T(8,128)(2,1)S(1)} %collective-permute-done.9.refs_0_, bf16[512,768]{1,0:T(8,128)(2,1)S(1)} %weave_steps.1.refs_1_.refs_0_.tok_ref, bf16[192,4608]{1,0:T(8,128)(2,1)} %pad_maximum_fusion.refs_2_, ...), custom_call_target="tpu_custom_call" | custom-call | flops 7247757312 | bytes 11796480 | tf_op jit(solution)/shard_map/layer_heads/pallas_call | solution.py:255
  152.1 2.6 %collective-permute-done.12.refs_5_ = bf16[144,1536]{1,0:T(8,128)(2,1)S(1)} collective-permute-done((bf16[144,1536]{1,0:T(8,128)(2,1)S(1)}, bf16[144,1536]{1,0:T(8,128)(2,1)S(1)}, u32[]{:S(2)}, u32[]{:S(2)}) %collective-permute-start.12) | collective-permute-done | bytes 442400 | tf_op jit(solution)/shard_map/ppermute | solution.py:333
  154.7 1.4 copy-done
  156.1 2.2 %layer_gated.3 = bf16[512,768]{1,0:T(8,128)(2,1)S(1)} custom-call(bf16[512,768]{1,0:T(8,128)(2,1)S(1)} %collective-permute-done.9.refs_0_, f32[512,768]{1,0:T(8,128)S(1)} %copy-done, bf16[192,1536]{1,0:T(8,128)(2,1)S(1)} %pad_maximum_fusion.1.refs_2_, bf16[144,1536]{1,0:T(8,128)(2,1)S(1)} %constant_dynamic-update-slice_fusion.3.refs_3_, ...), custom_call_target="tpu_custom_call" | custom-call | flops 1207959552 | bytes 4718592 | tf_op jit(solution)/shard_map/layer_gated/pallas_call | solution.py:255
  158.3 0.1 collective-permute-start.14
  158.4 3.6 %layer_gated.2.sum_ref = f32[512,768]{1,0:T(8,128)S(1)} custom-call(bf16[512,768]{1,0:T(8,128)(2,1)S(1)} %weave_steps.1.refs_1_.refs_0_.tok_ref, f32[512,768]{1,0:T(8,128)} %get-tuple-element.43.refs_1_, bf16[192,1536]{1,0:T(8,128)(2,1)S(1)} %pad_maximum_fusion.1.refs_2_, bf16[144,1536]{1,0:T(8,128)(2,1)S(1)} %constant_dynamic-update-slice_fusion.3.refs_3_, ...), custom_call_target="tpu_custom_call" | custom-call | flops 1207959552 | bytes 4718592 | tf_op jit(solution)/shard_map/layer_gated/pallas_call | solution.py:255
  162.1 1.8 %finish.1 = bf16[512,768]{1,0:T(8,128)(2,1)} custom-call(bf16[512,768]{1,0:T(8,128)(2,1)S(1)} %weave_steps.1.refs_1_.refs_0_.tok_ref, f32[512,768]{1,0:T(8,128)S(1)} %layer_gated.2.sum_ref, bf16[512,768]{1,0:T(8,128)(2,1)S(1)} %collective-permute-done.14.got_ref, s32[1,768]{1,0:T(1,128)S(1)} %compare_select_fusion.2.order_ref), custom_call_target="tpu_custom_call" | custom-call | flops 603979776 | bytes 3932160 | tf_op jit(solution)/shard_map/finish/pallas_call | solution.py:286
  (47 shorter events, 0.3 us)
Async XLA Ops:
  0.0 20.8 %copy-start.10 = (s32[512]{0:T(512)S(1)}, s32[512]{0:T(512)}, u32[]{:S(2)}) copy-start(s32[512]{0:T(512)} %param.11) | copy-start | bytes 6148
  0.0 20.8 %copy-start.11 = (s32[512]{0:T(512)S(1)}, s32[512]{0:T(512)}, u32[]{:S(2)}) copy-start(s32[512]{0:T(512)} %param.10) | copy-start | bytes 6148
  0.0 20.8 %copy-start.1 = (bf16[512,768]{1,0:T(8,128)(2,1)S(1)}, bf16[512,768]{1,0:T(8,128)(2,1)}, u32[]{:S(2)}) copy-start(bf16[512,768]{1,0:T(8,128)(2,1)} %feat_ref.1) | copy-start | bytes 2359300
  1.0 52.3 %copy-start.6 = (bf16[48,1536]{1,0:T(8,128)(2,1)}, bf16[48,1536]{1,0:T(8,128)(2,1)S(1)}, u32[]{:S(2)}) copy-start(bf16[48,1536]{1,0:T(8,128)(2,1)S(1)} %dynamic-slice_bitcast_fusion) | copy-start | bytes 442372
  3.9 16.2 %collective-permute-start.1 = (bf16[48,4608]{1,0:T(8,128)(2,1)S(1)}, bf16[48,4608]{1,0:T(8,128)(2,1)S(1)}, u32[]{:S(2)}, u32[]{:S(2)}) collective-permute-start(bf16[48,4608]{1,0:T(8,128)(2,1)S(1)} %pad_maximum_fusion.2), channel_id=1, source_target_pairs={{0,4},{4,8},{8,12},{12,0},{1,5},{5,9},{9,13},{13,1},{2,6},{6,10},{... | collective-permute-start | bytes 1327112 | tf_op jit(solution)/shard_map/ppermute | solution.py:309
  7.0 33.8 %collective-permute-start = (bf16[48,4608]{1,0:T(8,128)(2,1)S(1)}, bf16[48,4608]{1,0:T(8,128)(2,1)S(1)}, u32[]{:S(2)}, u32[]{:S(2)}) collective-permute-start(bf16[48,4608]{1,0:T(8,128)(2,1)S(1)} %pad_maximum_fusion.2), channel_id=1, source_target_pairs={{0,12},{4,0},{8,4},{12,8},{1,13},{5,1},{9,5},{13,9},{2,14},{6,2},{... | collective-permute-start | bytes 1327112 | tf_op jit(solution)/shard_map/ppermute | solution.py:309
  20.1 20.7 %collective-permute-start.2 = (bf16[48,4608]{1,0:T(8,128)(2,1)S(1)}, bf16[48,4608]{1,0:T(8,128)(2,1)S(1)}, u32[]{:S(2)}, u32[]{:S(2)}) collective-permute-start(bf16[48,4608]{1,0:T(8,128)(2,1)S(1)} %collective-permute-done.1), channel_id=1, source_target_pairs={{0,4},{4,8},{8,12},{12,0},{1,5},{5,9},{9,13},{13,1},{2,6},{6,10},{... | collective-permute-start | bytes 1327112 | tf_op jit(solution)/shard_map/ppermute | solution.py:309
  40.8 0.8 copy-start.7
  40.8 0.9 copy-start.8
  41.7 58.2 %all-to-all-start.1 = ((bf16[8,192,768]{2,1,0:T(8,128)(2,1)}), bf16[8,192,768]{2,1,0:T(8,128)(2,1)S(1)}, u32[]{:S(2)}, u32[]{:S(2)}) async-start(bf16[8,192,768]{2,1,0:T(8,128)(2,1)} %get-tuple-element.29), calls=%async_computation.1 | async-start | bytes 4718592 | tf_op jit(solution)/shard_map/all_to_all | solution.py:352
  47.2 6.2 %copy-start.4 = (bf16[1536,192]{0,1:T(8,128)(2,1)S(1)}, bf16[1536,192]{0,1:T(8,128)(2,1)}, u32[]{:S(2)}) copy-start(bf16[1536,192]{0,1:T(8,128)(2,1)} %param.17) | copy-start | bytes 1769476
  49.1 5.1 %slice-start = ((bf16[192,2,1536]{2,1,0:T(2,128)(2,1)}), bf16[192,2,1024]{2,1,0:T(2,128)(2,1)S(1)}, s32[]{:S(2)}) async-start(bf16[192,2,1536]{2,1,0:T(2,128)(2,1)} %param.16), calls=%async_computation.2 | async-start | bytes 1572864 | tf_op jit(solution)/shard_map/slice | solution.py:301
  49.9 52.2 %collective-permute-start.3 = (bf16[144,4608]{1,0:T(8,128)(2,1)}, bf16[144,4608]{1,0:T(8,128)(2,1)}, u32[]{:S(2)}, u32[]{:S(2)}) collective-permute-start(bf16[144,4608]{1,0:T(8,128)(2,1)} %constant_dynamic-update-slice_fusion.refs_3_), channel_id=1, source_target_pairs={{0,2},{2,0},{16,18},{18,16},{1,3},{3,1},{17,19},{19,17},{4,6},{6,4... | collective-permute-start | bytes 3981320 | tf_op jit(solution)/shard_map/ppermute | solution.py:333
  51.4 59.9 %collective-permute-start.4 = (bf16[144,4608]{1,0:T(8,128)(2,1)}, bf16[144,4608]{1,0:T(8,128)(2,1)}, u32[]{:S(2)}, u32[]{:S(2)}) collective-permute-start(bf16[144,4608]{1,0:T(8,128)(2,1)} %constant_dynamic-update-slice_fusion.refs_3_), channel_id=1, source_target_pairs={{0,16},{2,18},{16,0},{18,2},{1,17},{3,19},{17,1},{19,3},{4,20},{6,... | collective-permute-start | bytes 3981320 | tf_op jit(solution)/shard_map/ppermute | solution.py:333
  52.9 58.4 %collective-permute-start.5 = (bf16[144,4608]{1,0:T(8,128)(2,1)}, bf16[144,4608]{1,0:T(8,128)(2,1)}, u32[]{:S(2)}, u32[]{:S(2)}) collective-permute-start(bf16[144,4608]{1,0:T(8,128)(2,1)} %constant_dynamic-update-slice_fusion.refs_3_), channel_id=1, source_target_pairs={{0,18},{2,16},{16,2},{18,0},{1,19},{3,17},{17,3},{19,1},{4,22},{6,... | collective-permute-start | bytes 3981320 | tf_op jit(solution)/shard_map/ppermute | solution.py:333
  53.4 1.2 copy-start.5
  54.2 2.1 %slice-start.1 = ((bf16[48,1536]{1,0:T(8,128)(2,1)}), bf16[48,512]{1,0:T(8,128)(2,1)S(1)}, s32[]{:S(2)}) async-start(bf16[48,1536]{1,0:T(8,128)(2,1)} %copy-done.6), calls=%async_computation.3 | async-start | bytes 98304 | tf_op jit(solution)/shard_map/slice | solution.py:302
  54.2 2.2 %copy-start.9 = (bf16[384,192]{0,1:T(8,128)(2,1)S(1)}, bf16[384,192]{0,1:T(8,128)(2,1)}, u32[]{:S(2)}) copy-start(bf16[384,192]{0,1:T(8,128)(2,1)} %param.15) | copy-start | bytes 442372
  56.3 43.6 %copy-start.2 = (bf16[8,768]{1,0:T(8,128)(2,1)S(1)}, bf16[8,768]{1,0:T(8,128)(2,1)}, u32[]{:S(2)}) copy-start(bf16[8,768]{1,0:T(8,128)(2,1)} %embed_ref.1) | copy-start | bytes 36868
  100.0 17.0 %copy-start.3 = (bf16[192,2,1536]{2,1,0:T(2,128)(2,1)S(1)}, bf16[192,2,1536]{2,1,0:T(2,128)(2,1)}, u32[]{:S(2)}) copy-start(bf16[192,2,1536]{2,1,0:T(2,128)(2,1)} %param.16) | copy-start | bytes 3538948
  111.3 11.6 %collective-permute-start.6 = (bf16[256,768]{1,0:T(8,128)(2,1)S(1)}, bf16[256,768]{1,0:T(8,128)(2,1)S(1)}, u32[]{:S(2)}, u32[]{:S(2)}) collective-permute-start(bf16[256,768]{1,0:T(8,128)(2,1)S(1)} %get-tuple-element.35), channel_id=1, source_target_pairs={{0,2},{2,0},{1,3},{3,1},{4,6},{6,4},{5,7},{7,5},{8,10},{10,8},{9,1... | collective-permute-start | bytes 1179656 | tf_op jit(solution)/shard_map/ppermute | solution.py:420
  112.5 7.4 %collective-permute-start.7 = (bf16[48,1536]{1,0:T(8,128)(2,1)S(1)}, bf16[48,1536]{1,0:T(8,128)(2,1)S(1)}, u32[]{:S(2)}, u32[]{:S(2)}) collective-permute-start(bf16[48,1536]{1,0:T(8,128)(2,1)S(1)} %pad_maximum_fusion.3), channel_id=1, source_target_pairs={{0,12},{4,0},{8,4},{12,8},{1,13},{5,1},{9,5},{13,9},{2,14},{6,2},{... | collective-permute-start | bytes 442376 | tf_op jit(solution)/shard_map/ppermute | solution.py:309
  116.0 6.9 %collective-permute-start.8 = (bf16[48,1536]{1,0:T(8,128)(2,1)S(1)}, bf16[48,1536]{1,0:T(8,128)(2,1)S(1)}, u32[]{:S(2)}, u32[]{:S(2)}) collective-permute-start(bf16[48,1536]{1,0:T(8,128)(2,1)S(1)} %pad_maximum_fusion.3), channel_id=1, source_target_pairs={{0,4},{4,8},{8,12},{12,0},{1,5},{5,9},{9,13},{13,1},{2,6},{6,10},{... | collective-permute-start | bytes 442376 | tf_op jit(solution)/shard_map/ppermute | solution.py:309
  124.4 12.0 %collective-permute-start.9 = (bf16[512,768]{1,0:T(8,128)(2,1)S(1)}, bf16[512,768]{1,0:T(8,128)(2,1)S(1)}, u32[]{:S(2)}, u32[]{:S(2)}) collective-permute-start(bf16[512,768]{1,0:T(8,128)(2,1)S(1)} %weave_steps.1.refs_1_.refs_0_.tok_ref), channel_id=1, source_target_pairs={{0,1},{1,0},{2,3},{3,2},{4,5},{5,4},{6,7},{7,6},{8,9},{9,8},{10,11... | collective-permute-start | bytes 2359304 | tf_op jit(solution)/shard_map/ppermute | solution.py:434
  124.5 8.3 %collective-permute-start.10 = (bf16[48,1536]{1,0:T(8,128)(2,1)S(1)}, bf16[48,1536]{1,0:T(8,128)(2,1)S(1)}, u32[]{:S(2)}, u32[]{:S(2)}) collective-permute-start(bf16[48,1536]{1,0:T(8,128)(2,1)S(1)} %collective-permute-done.8), channel_id=1, source_target_pairs={{0,4},{4,8},{8,12},{12,0},{1,5},{5,9},{9,13},{13,1},{2,6},{6,10},{... | collective-permute-start | bytes 442376 | tf_op jit(solution)/shard_map/ppermute | solution.py:309
  132.8 19.3 %collective-permute-start.11 = (bf16[144,1536]{1,0:T(8,128)(2,1)S(1)}, bf16[144,1536]{1,0:T(8,128)(2,1)S(1)}, u32[]{:S(2)}, u32[]{:S(2)}) collective-permute-start(bf16[144,1536]{1,0:T(8,128)(2,1)S(1)} %constant_dynamic-update-slice_fusion.3.refs_3_), channel_id=1, source_target_pairs={{0,2},{2,0},{16,18},{18,16},{1,3},{3,1},{17,19},{19,17},{4,6},{6,4... | collective-permute-start | bytes 1327112 | tf_op jit(solution)/shard_map/ppermute | solution.py:333
  133.7 21.0 %collective-permute-start.12 = (bf16[144,1536]{1,0:T(8,128)(2,1)S(1)}, bf16[144,1536]{1,0:T(8,128)(2,1)S(1)}, u32[]{:S(2)}, u32[]{:S(2)}) collective-permute-start(bf16[144,1536]{1,0:T(8,128)(2,1)S(1)} %constant_dynamic-update-slice_fusion.3.refs_3_), channel_id=1, source_target_pairs={{0,16},{2,18},{16,0},{18,2},{1,17},{3,19},{17,1},{19,3},{4,20},{6,... | collective-permute-start | bytes 1327112 | tf_op jit(solution)/shard_map/ppermute | solution.py:333
  135.2 19.5 %collective-permute-start.13 = (bf16[144,1536]{1,0:T(8,128)(2,1)S(1)}, bf16[144,1536]{1,0:T(8,128)(2,1)S(1)}, u32[]{:S(2)}, u32[]{:S(2)}) collective-permute-start(bf16[144,1536]{1,0:T(8,128)(2,1)S(1)} %constant_dynamic-update-slice_fusion.3.refs_3_), channel_id=1, source_target_pairs={{0,18},{2,16},{16,2},{18,0},{1,19},{3,17},{17,3},{19,1},{4,22},{6,... | collective-permute-start | bytes 1327112 | tf_op jit(solution)/shard_map/ppermute | solution.py:333
  154.7 1.4 copy-start
  158.3 3.7 %collective-permute-start.14 = (bf16[512,768]{1,0:T(8,128)(2,1)S(1)}, bf16[512,768]{1,0:T(8,128)(2,1)S(1)}, u32[]{:S(2)}, u32[]{:S(2)}) collective-permute-start(bf16[512,768]{1,0:T(8,128)(2,1)S(1)} %layer_gated.3), channel_id=1, source_target_pairs={{0,1},{1,0},{2,3},{3,2},{4,5},{5,4},{6,7},{7,6},{8,9},{9,8},{10,11... | collective-permute-start | bytes 2359304 | tf_op jit(solution)/shard_map/ppermute | solution.py:437

commit v8 on v5

--- a/solution.py
+++ b/solution.py
@@ -145,35 +145,38 @@
     )(my_slot, order.reshape(1, width), keep, got)
 
 
-def head_scale(values, ones):
-    sums = dot((values * values).astype(BF16), ones)
-    return values * lax.rsqrt(sums * (1.0 / HD) + EPS)
-
-
 def attention(normed, weight, heads_width, ctx_ref):
     rows = normed.shape[0]
+    group = LANES
+    lane = iota((1, LANES), 1)
+    first = iota((group, LANES), 1) < HD
+    masks = [(lane < HD).astype(F32).astype(BF16), (lane >= HD).astype(F32).astype(BF16)]
+    ones = (iota((LANES, LANES), 0) // HD == iota((LANES, LANES), 1) // HD).astype(F32)
+    mean = (ones * (1.0 / HD)).astype(BF16)
+    ones = ones.astype(BF16)
+    same_cell = iota((2 * group, group), 0) % group // TSTEPS == iota((2 * group, group), 1) // TSTEPS
+    same_cell = same_cell.astype(F32).astype(BF16)
+    count = jnp.ones((group, LANES), BF16)
     projected = dot(normed, weight)
-    same_head = iota((LANES, LANES), 0) // HD == iota((LANES, LANES), 1) // HD
-    ones = same_head.astype(F32).astype(BF16)
-    group = LANES
-    first = iota((group, LANES), 1) < HD
-    row, col = iota((2 * group, group), 0), iota((2 * group, group), 1)
-    same_cell = row % group // TSTEPS == col // TSTEPS
-    count = jnp.ones((group, LANES), BF16)
-    for pair in range(heads_width // LANES):
-        at = pair * LANES
-        query = (head_scale(projected[:, at : at + LANES], ones) * HD ** (-0.5)).astype(BF16)
-        key = head_scale(projected[:, heads_width + at : heads_width + at + LANES], ones).astype(BF16)
+    begins = range(0, rows, group)
+    for at in range(0, heads_width, LANES):
+        query = projected[:, at : at + LANES]
+        key = projected[:, heads_width + at : heads_width + at + LANES]
         value = projected[:, 2 * heads_width + at : 2 * heads_width + at + LANES].astype(BF16)
-        for begin in range(0, rows, group):
-            q = query[begin : begin + group]
-            k = key[begin : begin + group]
-            v = value[begin : begin + group]
-            none = jnp.zeros_like(q)
-            both = jnp.concatenate([jnp.where(first, q, none), jnp.where(first, none, q)], axis=0)
-            expo = jnp.where(same_cell, jnp.exp(dot_t(both, k)), 0.0).astype(BF16)
-            mixed = dot(expo, jnp.concatenate([v, count], axis=1))
-            top, low = mixed[:group], mixed[group:]
+        query_bf, key_bf = query.astype(BF16), key.astype(BF16)
+        query = (query * lax.rsqrt(dot(query_bf * query_bf, ones) + HD * EPS)).astype(BF16)
+        key = (key * lax.rsqrt(dot(key_bf * key_bf, mean) + EPS)).astype(BF16)
+        left, right = query * masks[0], query * masks[1]
+        scores = [
+            dot_t(jnp.concatenate([left[at : at + group], right[at : at + group]], axis=0), key[at : at + group])
+            for at in begins
+        ]
+        expos = [jnp.exp(score).astype(BF16) * same_cell for score in scores]
+        mixed = [
+            dot(expo, jnp.concatenate([value[at : at + group], count], axis=1)) for at, expo in zip(begins, expos)
+        ]
+        for begin, both in zip(begins, mixed):
+            top, low = both[:group], both[group:]
             over = jnp.where(first, top[:, :LANES], low[:, :LANES])
             under = jnp.where(first, top[:, LANES:], low[:, LANES:])
             ctx_ref[begin : begin + group, at : at + LANES] = (over / under).astype(BF16)
@@ -189,9 +192,9 @@
 def layer_kernel(plan, sections, tok_ref, *refs):
     pieces, (out_ref, w_ref, norm_ref, ctx_ref, acc_ref, sems) = refs[:-6], refs[-6:]
     copies = {}
-    for number, (section, piece, source_col, row, col, size) in enumerate(plan):
+    for number, (section, piece, row, col, size) in enumerate(plan):
         copy = pltpu.make_async_copy(
-            pieces[piece].at[:, pl.ds(source_col, size)],
+            pieces[piece].at[:, pl.ds(col, size)],
             w_ref.at[pl.ds(row, pieces[piece].shape[0]), pl.ds(col, size)],
             sems.at[number],
         )
@@ -224,16 +227,14 @@
     out_at = up_at + hidden_width
     down_at = out_at + heads_width
     columns = down_at + hidden_width
-    unit = min(UNIT, hidden_width)
     sections = [(0, gate_at), (out_at, down_at)]
-    for begin in range(0, hidden_width, unit):
-        sections += [(at + begin, at + begin + unit) for at in (gate_at, up_at, down_at)]
-    plan = []
-    for section, (left, right) in enumerate(sections):
-        for number, (array, row, at) in enumerate(pieces):
-            low, high = max(left, at), min(right, at + array.shape[1])
-            if low < high:
-                plan.append((section, number, low - at, row, low, high - low))
+    for begin in range(0, hidden_width, UNIT):
+        sections += [(at + begin, at + begin + UNIT) for at in (gate_at, up_at, down_at)]
+    plan = [
+        (section, number, row, left, right - left)
+        for section, (left, right) in enumerate(sections)
+        for number, (_, row) in enumerate(pieces)
+    ]
     return pl.pallas_call(
         functools.partial(layer_kernel, plan, sections),
         out_shape=jax.ShapeDtypeStruct((rows, width), out_type),
@@ -253,7 +254,7 @@
             transcendentals=rows * hidden_width,
         ),
         name="layer",
-    )(tokens, *[array for array, _, _ in pieces])
+    )(tokens, *[array for array, _ in pieces])
 
 
 def finish_kernel(tok_ref, sum_ref, got_ref, order_ref, out_ref):
@@ -283,61 +284,38 @@
     return jnp.concatenate([w_qkv.reshape(rows, -1), w_gate_up.reshape(rows, -1), w_out, w_down], axis=1)
 
 
-def shares_along_cells(share_rows):
+def along_cells(values, distance):
     n_cells = lax.axis_size("cells")
-    up = [(j, (j + 1) % n_cells) for j in range(n_cells)]
-    down = [(j, (j - 1) % n_cells) for j in range(n_cells)]
-    below = [lax.ppermute(share_rows, "cells", up)]
-    above = [lax.ppermute(share_rows, "cells", down)]
-    while len(below) + len(above) < n_cells - 1:
-        line, way = (below, up) if len(below) <= len(above) else (above, down)
-        line.append(lax.ppermute(line[-1], "cells", way))
-    return above + below[::-1]
-
-
-def pieces_of_all(shard, shares):
-    rows = shard.shape[0]
-    others = jnp.concatenate(shares, axis=0)
-    swap = [(0, 1), (1, 0)]
-    by_slot = lax.ppermute(others, "slots", swap)
-    by_group = lax.ppermute(others, "groups", swap)
-    cut = shard.shape[1] // (2 * LANES) * LANES
-    far_a = lax.ppermute(by_slot[:, :cut], "groups", swap)
-    far_b = lax.ppermute(by_group[:, cut:], "slots", swap)
-    step = others.shape[0]
-    return [
-        (shard, 0, 0),
-        (others, rows, 0),
-        (by_slot, rows + step, 0),
-        (by_group, rows + 2 * step, 0),
-        (far_a, rows + 3 * step, 0),
-        (far_b, rows + 3 * step, cut),
-    ]
-
-
-def arrival_order(width, n_cells, n_share):
+    return lax.ppermute(values, "cells", [(j, (j - distance) % n_cells) for j in range(n_cells)])
+
+
+def to_other_places(shares):
+    n_slots = lax.axis_size("slots")
+    n_share = lax.axis_size("groups") * n_slots
+    places = [shares]
+    for far in range(1, n_share):
+        pairs = [(place, place ^ far) for place in range(n_share)]
+        places.append(lax.ppermute(shares, ("groups", "slots"), pairs))
+    return places
+
+
+def arrival_order(width, n_share):
+    n_cells = lax.axis_size("cells")
     mine = lax.axis_index("cells")
-    share_id = lax.axis_index("groups") * lax.axis_size("slots") + lax.axis_index("slots")
+    place = lax.axis_index("groups") * lax.axis_size("slots") + lax.axis_index("slots")
     rows = width // n_cells
     share = rows // n_share
-    step = (n_cells - 1) * share
-    place = jnp.arange(width, dtype=jnp.int32)
-    past = jnp.maximum(place - rows, 0)
-    which = past // step
-    cell = (mine + 1 + past % step // share) % n_cells
-    far = cell * rows + (which ^ share_id) * share + past % share
-    return jnp.where(place < rows, mine * rows + place, far)
-
-
-def tokens_by_blocks(owner, position, obs_feat, time_embed, my_slot, capacity, slot_dev, order, shares):
-    n_owners = lax.axis_size("cells") * lax.axis_size("mp")
-    blocks, codes = place_rows(owner, position, obs_feat, n_owners, capacity)
-    codes = lax.all_to_all(codes, ("cells", "mp"), split_axis=0, concat_axis=0, tiled=True)
-    blocks, *shares = lax.optimization_barrier((blocks, *shares))
+    row = jnp.arange(width, dtype=jnp.int32)
+    past = row - 2 * rows
+    far = jnp.where(past < 0, row // share % n_share, past // (2 * share))
+    distance = jnp.where(past < 0, n_cells - 1, 1 + past // share % 2)
+    other = (mine + distance) % n_cells * rows + (far ^ place) * share + row % share
+    return jnp.where(row < rows, mine * rows + row, other)
+
+
+def pooled_blocks(blocks, codes, time_embed, my_slot, slot_dev):
     got = lax.all_to_all(blocks, ("cells", "mp"), split_axis=0, concat_axis=0, tiled=True)
-    keep, send = pool_rows(my_slot.reshape(1), time_embed, codes, got, capacity, slot_dev)
-    other = lax.ppermute(send, "slots", [(0, 1), (1, 0)])
-    return weave_steps(my_slot.reshape(1), order, keep, other, slot_dev), shares
+    return pool_rows(my_slot.reshape(1), time_embed, codes, got, blocks.shape[1], slot_dev)
 
 
 def tokens_by_exchanges(owner, position, obs_feat, time_embed, my_slot, capacity, slot_dev):
@@ -389,17 +367,29 @@
 
     local_weights = (w_qkv, w_out.T, w_gate_up, w_down.T)
     which = lax.axis_index("groups") * n_slots + my_slot
-    share_rows = side_by_side(*[lax.dynamic_slice_in_dim(w, which * share, share, 0) for w in local_weights])
-    if n_slots == 2 and n_groups == 2 and share % 16 == 0 and capacity % 16 == 0:
-        order = arrival_order(width, n_cells, n_share)
-        shares = shares_along_cells(share_rows)
-        tokens, shares = tokens_by_blocks(
-            owner, position, obs_feat, time_embed, my_slot, capacity, slot_dev, order, shares
-        )
-        pieces = pieces_of_all(side_by_side(*local_weights), shares)
+    share_weights = [lax.dynamic_slice_in_dim(w, which * share, share, 0) for w in local_weights]
+    share_rows = side_by_side(*share_weights)
+    if n_slots == 2 and n_groups == 2 and n_cells == 4 and share % 16 == 0 and capacity % 16 == 0:
+        order = arrival_order(width, n_share)
+        below = along_cells(share_rows, -1)
+        blocks, codes = place_rows(owner, position, obs_feat, n_owners, capacity)
+        codes = lax.all_to_all(codes, ("cells", "mp"), split_axis=0, concat_axis=0, tiled=True)
+        below, codes, share_rows = lax.optimization_barrier((below, codes, share_rows))
+        first = to_other_places(below)
+        above, opposite = along_cells(share_rows, 1), along_cells(below, -1)
+        blocks, above, opposite, first = lax.optimization_barrier((blocks, above, opposite, first))
+        second = to_other_places(jnp.concatenate([above, opposite], axis=0))
+        keep, send = pooled_blocks(blocks, codes, time_embed, my_slot, slot_dev)
+        send, second = lax.optimization_barrier((send, second))
+        other = lax.ppermute(send, "slots", [(0, 1), (1, 0)])
+        tokens = weave_steps(my_slot.reshape(1), order, keep, other, slot_dev)
+        pieces, row = [], 0
+        for array in [side_by_side(*local_weights)] + first + second:
+            pieces.append((array, row))
+            row += array.shape[0]
     else:
         order = jnp.arange(width, dtype=jnp.int32)
-        pieces = [(lax.all_gather(share_rows, ("cells", "groups", "slots"), axis=0, tiled=True), 0, 0)]
+        pieces = [(lax.all_gather(share_rows, ("cells", "groups", "slots"), axis=0, tiled=True), 0)]
         tokens = tokens_by_exchanges(owner, position, obs_feat, time_embed, my_slot, capacity, slot_dev)
 
     swap = [(0, 1), (1, 0)]

time: 162 us -> 163 us (level)
  starting transfers between devices: 30.3 us -> 18.1 us
  blocking collectives: 0 us -> 11.5 us
  waiting for transfers between devices: 86.2 us -> 82 us
  local copies, waits for them, and re-layouts: 12 us -> 15.1 us
  Pallas kernels: 30.3 us -> 32.6 us
    all_to_all x2 -> x1, starting transfers between devices: 18.2 us -> 3.8 us  [pooled_blocks(): lax.all_to_all(blocks, ('cells', 'mp'), split_axis=0, concat_axis=0, tile...]
    all_to_all x0 -> x1, blocking collectives: none -> 11.5 us  [on_device(): lax.all_to_all(codes, ('cells', 'mp'), split_axis=0, concat_axis=0, tiled...]
    ppermute x8 -> x10, waiting for transfers between devices: 39.5 us -> 32.4 us  [the longest x6 13.5 us: to_other_places(): places.append(lax.ppermute(shares, ('groups', 'slots'), pairs))]
    unnamed x21 -> x48, local copies, waits for them, and re-layouts: 5.74 us -> 12 us
    all_to_all x2 -> x1, waiting for transfers between devices: 46.7 us -> 49.6 us  [pooled_blocks(): lax.all_to_all(blocks, ('cells', 'mp'), split_axis=0, concat_axis=0, tile...]
    slice x2 -> x0, local copies, waits for them, and re-layouts: 2.45 us -> none  [the longest x1 1.23 us: pieces_of_all(): far_b = lax.ppermute(by_group[:, cut:], 'slots', swap)]
    ppermute x8 -> x10, starting transfers between devices: 11.9 us -> 13.7 us  [the longest x6 7.04 us: to_other_places(): places.append(lax.ppermute(shares, ('groups', 'slots'), pairs))]
  transfers between devices with their start and end apart: 12 -> 13, of which waited for: 5 -> 5; matrix products, arithmetic and copies ran while one was open for 6% -> 2% of each run, Pallas kernels for 11% -> 11%
where the time goes in v8:
time: 163 us; the launch traced here: 162 us
  waiting for transfers between devices  82 us (50%)
  Pallas kernels  32.6 us (20%)
  starting transfers between devices  18.1 us (11%)
  local copies, waits for them, and re-layouts  15.1 us (9%)
  blocking collectives  11.5 us (7%)
  other arithmetic  1.77 us (1%)
    all_to_all x1, waiting for transfers between devices, pooled_blocks(): lax.all_to_all(blocks, ('cells', 'mp'), split_axis=0, concat_axis=0, tile...  49.6 us
    pallas_call x2, Pallas kernels, layer(): pl.pallas_call(functools.partial(layer_kernel, plan, sections), out_shape...  23.1 us
    ppermute x6, waiting for transfers between devices, to_other_places(): places.append(lax.ppermute(shares, ('groups', 'slots'), pairs))  13.5 us
    unnamed x48, local copies, waits for them, and re-layouts  12 us
    all_to_all x1, blocking collectives, on_device(): lax.all_to_all(codes, ('cells', 'mp'), split_axis=0, concat_axis=0, tiled...  11.5 us
    ppermute x3, waiting for transfers between devices, along_cells(): lax.ppermute(values, 'cells', [(j, (j - distance) % n_cells) for j in ran...  9.63 us
    ppermute x1, waiting for transfers between devices, on_device(): other = lax.ppermute(send, 'slots', [(0, 1), (1, 0)])  9.34 us
    ppermute x6, starting transfers between devices, to_other_places(): places.append(lax.ppermute(shares, ('groups', 'slots'), pairs))  7.04 us
  transfers between devices with their start and end apart: 13, of which 5 were waited for; matrix products, arithmetic and copies ran while one was open for 2% of the time, Pallas kernels for 11%

profile of v8, /device:TPU:0, one launch (start us, length us, event | category | flops | bytes accessed | tf_op | source)
XLA Modules:
  0.0 161.9 jit_solution(5975671796859801269)
XLA Ops:
  0.0 0.8 dynamic-slice_bitcast_fusion.2
  0.8 0.9 dynamic-slice_bitcast_fusion.1
  1.7 0.9 dynamic-slice_bitcast_fusion
  2.6 0.0 copy-start.20
  2.6 0.0 copy-start.21
  2.7 1.2 constant_dynamic-slice_fusion
  4.0 3.1 %collective-permute-start = (bf16[48,6144]{1,0:T(8,128)(2,1)S(1)}, bf16[48,6144]{1,0:T(8,128)(2,1)S(1)}, u32[]{:S(2)}, u32[]{:S(2)}) collective-permute-start(bf16[48,6144]{1,0:T(8,128)(2,1)S(1)} %pad_maximum_fusion.1), channel_id=1, source_target_pairs={{0,4},{4,8},{8,12},{12,0},{1,5},{5,9},{9,13},{13,1},{2,6},{6,10},{... | collective-permute-start | bytes 1769480 | tf_op jit(solution)/shard_map/ppermute | solution.py:289
  7.8 3.4 %place_rows.1 = (bf16[8,192,768]{2,1,0:T(8,128)(2,1)}, s32[8,1,192]{2,1,0:T(1,128)S(1)}) custom-call(s32[1,512]{1,0:T(1,128)S(1)} %bitcast.22, s32[1,512]{1,0:T(1,128)S(1)} %bitcast.21, bf16[512,768]{1,0:T(8,128)(2,1)S(1)} %copy-done.1), custom_call_target="tpu_custom_call" | custom-call | flops 1207959552 | bytes 3145728 | tf_op jit(solution)/shard_map/place_rows/pallas_call | solution.py:63
  11.2 11.5 %all_to_all.10.code_ref = s32[8,1,192]{2,1,0:T(1,128)S(1)} all-to-all(s32[8,1,192]{2,1,0:T(1,128)S(1)} %get-tuple-element.24), channel_id=1, replica_groups=mesh['groups'=2,'cells'=4,'slots'=2,'mp'=2] {'cells','mp'}, dimensions={0} | all-to-all | bytes 12288 | tf_op jit(solution)/shard_map/all_to_all | solution.py:376
  22.6 1.7 %collective-permute-start.1 = (bf16[48,6144]{1,0:T(8,128)(2,1)S(1)}, bf16[48,6144]{1,0:T(8,128)(2,1)S(1)}, u32[]{:S(2)}, u32[]{:S(2)}) collective-permute-start(bf16[48,6144]{1,0:T(8,128)(2,1)S(1)} %pad_maximum_fusion.1), channel_id=1, source_target_pairs={{0,12},{4,0},{8,4},{12,8},{1,13},{5,1},{9,5},{13,9},{2,14},{6,2},{... | collective-permute-start | bytes 1769480 | tf_op jit(solution)/shard_map/ppermute | solution.py:289
  24.4 2.4 %collective-permute-start.5 = (bf16[48,6144]{1,0:T(8,128)(2,1)S(1)}, bf16[48,6144]{1,0:T(8,128)(2,1)S(1)}, u32[]{:S(2)}, u32[]{:S(2)}) collective-permute-start(bf16[48,6144]{1,0:T(8,128)(2,1)S(1)} %collective-permute-done.refs_1_), channel_id=1, source_target_pairs={{0,18},{2,16},{16,2},{18,0},{1,19},{3,17},{17,3},{19,1},{4,22},{6,... | collective-permute-start | bytes 1769480 | tf_op jit(solution)/shard_map/ppermute | solution.py:298
  26.8 0.5 collective-permute-start.4
  27.3 0.5 collective-permute-start.3
  27.8 0.3 collective-permute-start.2
  28.2 0.8 copy-done.2
  29.0 9.6 %collective-permute-done.1 = bf16[48,6144]{1,0:T(8,128)(2,1)S(1)} collective-permute-done((bf16[48,6144]{1,0:T(8,128)(2,1)S(1)}, bf16[48,6144]{1,0:T(8,128)(2,1)S(1)}, u32[]{:S(2)}, u32[]{:S(2)}) %collective-permute-start.1) | collective-permute-done | bytes 589856 | tf_op jit(solution)/shard_map/ppermute | solution.py:289
  38.6 2.9 %collective-permute-done.5.refs_4_ = bf16[48,6144]{1,0:T(8,128)(2,1)S(1)} collective-permute-done((bf16[48,6144]{1,0:T(8,128)(2,1)S(1)}, bf16[48,6144]{1,0:T(8,128)(2,1)S(1)}, u32[]{:S(2)}, u32[]{:S(2)}) %collective-permute-start.5) | collective-permute-done | bytes 589856 | tf_op jit(solution)/shard_map/ppermute | solution.py:298
  41.5 0.8 copy-done.4
  42.4 10.5 %collective-permute-done.4.refs_3_ = bf16[48,6144]{1,0:T(8,128)(2,1)S(1)} collective-permute-done((bf16[48,6144]{1,0:T(8,128)(2,1)S(1)}, bf16[48,6144]{1,0:T(8,128)(2,1)S(1)}, u32[]{:S(2)}, u32[]{:S(2)}) %collective-permute-start.4) | collective-permute-done | bytes 589856 | tf_op jit(solution)/shard_map/ppermute | solution.py:298
  52.9 0.9 copy-done.6
  53.8 0.8 copy-done.8
  54.6 0.8 copy-done.17
  55.4 3.8 %all-to-all-start.1 = ((bf16[8,192,768]{2,1,0:T(8,128)(2,1)}), bf16[8,192,768]{2,1,0:T(8,128)(2,1)S(1)}, u32[]{:S(2)}, u32[]{:S(2)}) async-start(bf16[8,192,768]{2,1,0:T(8,128)(2,1)} %get-tuple-element.29), calls=%async_computation.1 | async-start | bytes 4718592 | tf_op jit(solution)/shard_map/all_to_all | solution.py:317
  59.2 1.2 constant_dynamic-update-slice_fusion.1
  60.4 0.1 copy-done.18
  60.5 1.8 %collective-permute-start.8 = (bf16[96,6144]{1,0:T(8,128)(2,1)S(1)}, bf16[96,6144]{1,0:T(8,128)(2,1)}, u32[]{:S(2)}, u32[]{:S(2)}) collective-permute-start(bf16[96,6144]{1,0:T(8,128)(2,1)S(1)} %constant_dynamic-update-slice_fusion.refs_5_), channel_id=1, source_target_pairs={{0,18},{2,16},{16,2},{18,0},{1,19},{3,17},{17,3},{19,1},{4,22},{6,... | collective-permute-start | bytes 3538952 | tf_op jit(solution)/shard_map/ppermute | solution.py:298
  62.3 1.2 collective-permute-start.7
  63.5 0.5 collective-permute-start.6
  64.1 49.6 %all-to-all-done.1.got_ref = bf16[8,192,768]{2,1,0:T(8,128)(2,1)S(1)} async-done(((bf16[8,192,768]{2,1,0:T(8,128)(2,1)}), bf16[8,192,768]{2,1,0:T(8,128)(2,1)S(1)}, u32[]{:S(2)}, u32[]{:S(2)}) %all-to-all-start.1) | async-done | bytes 2359328 | tf_op jit(solution)/shard_map/all_to_all | solution.py:317
  113.6 0.7 copy-done.10
  114.3 2.8 %pool_rows.1 = (bf16[256,768]{1,0:T(8,128)(2,1)S(1)}, bf16[256,768]{1,0:T(8,128)(2,1)}) custom-call(s32[1]{0:T(128)} %bitcast.slot_ref, bf16[8,768]{1,0:T(8,128)(2,1)S(1)} %copy-done.10, s32[8,1,192]{2,1,0:T(1,128)S(1)} %all_to_all.10.code_ref, bf16[8,192,768]{2,1,0:T(8,128)(2,1)S(1)} %all-to-all-done.1.got_ref), custom_call_target="tpu_custom_call" | custom-call | flops 1207959552 | bytes 2359296 | tf_op jit(solution)/shard_map/pool_rows/pallas_call | solution.py:106
  117.2 0.7 copy-done.11
  117.9 1.6 collective-permute-start.9
  119.5 9.3 %collective-permute-done.9.got_ref = bf16[256,768]{1,0:T(8,128)(2,1)S(1)} collective-permute-done((bf16[256,768]{1,0:T(8,128)(2,1)}, bf16[256,768]{1,0:T(8,128)(2,1)S(1)}, u32[]{:S(2)}, u32[]{:S(2)}) %collective-permute-start.9) | collective-permute-done | bytes 393248 | tf_op jit(solution)/shard_map/ppermute | solution.py:384
  128.9 1.0 copy-done.12
  129.9 1.5 weave_steps.1.tok_ref
  131.3 0.1 collective-permute-start.10
  131.5 0.1 copy.17
  131.7 0.9 copy-done.14
  132.6 0.0 copy-done.19
  132.6 1.7 %pad_maximum_fusion.refs_0_ = bf16[192,6144]{1,0:T(8,128)(2,1)} fusion(bf16[192,1536]{1,0:T(8,128)(2,1)S(1)} %bitcast.28, bf16[192,384]{1,0:T(8,128)(2,1)S(1)} %bitcast.31, bf16[192,3072]{1,0:T(8,128)(2,1)S(1)} %bitcast.23, bf16[192,1152]{1,0:T(8,128)(2,1)S(1)} %bitcast.25), kind=kLoop, calls=%fused_computation | loop fusion | flops 9437184 | bytes 4718592 | tf_op jit(solution)/shard_map/concatenate | solution.py:284
  134.3 0.4 copy-done.7
  134.6 0.4 copy-done.9
  135.0 11.0 %layer.3 = bf16[512,768]{1,0:T(8,128)(2,1)S(1)} custom-call(bf16[512,768]{1,0:T(8,128)(2,1)S(1)} %collective-permute-done.10.tok_ref, bf16[192,6144]{1,0:T(8,128)(2,1)} %pad_maximum_fusion.refs_0_, bf16[48,6144]{1,0:T(8,128)(2,1)S(1)} %copy-done.3, bf16[48,6144]{1,0:T(8,128)(2,1)S(1)} %copy-done.9, bf16[48,6144]{1,0:T(8,128)(2,1)S(1)} %copy-done.7, ...), custom_call_target="tpu_custom_call" | custom-call | flops 4831838208 | bytes 11796480 | tf_op jit(solution)/shard_map/layer/pallas_call | solution.py:238
  146.0 0.6 collective-permute-start.11
  146.6 12.2 %layer.2.sum_ref = f32[512,768]{1,0:T(8,128)} custom-call(bf16[512,768]{1,0:T(8,128)(2,1)S(1)} %weave_steps.1.tok_ref, bf16[192,6144]{1,0:T(8,128)(2,1)} %pad_maximum_fusion.refs_0_, bf16[48,6144]{1,0:T(8,128)(2,1)S(1)} %copy-done.3, bf16[48,6144]{1,0:T(8,128)(2,1)S(1)} %copy-done.9, bf16[48,6144]{1,0:T(8,128)(2,1)S(1)} %copy-done.7, ...), custom_call_target="tpu_custom_call" | custom-call | flops 4831838208 | bytes 11796480 | tf_op jit(solution)/shard_map/layer/pallas_call | solution.py:238
  158.8 1.4 copy-done
  160.2 1.8 %finish.1 = bf16[512,768]{1,0:T(8,128)(2,1)} custom-call(bf16[512,768]{1,0:T(8,128)(2,1)S(1)} %weave_steps.1.tok_ref, f32[512,768]{1,0:T(8,128)S(1)} %copy-done, bf16[512,768]{1,0:T(8,128)(2,1)S(1)} %collective-permute-done.11.got_ref, s32[1,768]{1,0:T(1,128)S(1)} %compare_select_fusion.6.order_ref), custom_call_target="tpu_custom_call" | custom-call | flops 603979776 | bytes 3932160 | tf_op jit(solution)/shard_map/finish/pallas_call | solution.py:269
  (43 shorter events, 0.3 us)
Async XLA Ops:
  2.6 5.1 %copy-start.20 = (s32[512]{0:T(512)S(1)}, s32[512]{0:T(512)}, u32[]{:S(2)}) copy-start(s32[512]{0:T(512)} %param.11) | copy-start | bytes 6148
  2.6 5.1 %copy-start.21 = (s32[512]{0:T(512)S(1)}, s32[512]{0:T(512)}, u32[]{:S(2)}) copy-start(s32[512]{0:T(512)} %param.10) | copy-start | bytes 6148
  2.7 5.1 %copy-start.1 = (bf16[512,768]{1,0:T(8,128)(2,1)S(1)}, bf16[512,768]{1,0:T(8,128)(2,1)}, u32[]{:S(2)}) copy-start(bf16[512,768]{1,0:T(8,128)(2,1)} %feat_ref.1) | copy-start | bytes 2359300
  4.0 18.6 %collective-permute-start = (bf16[48,6144]{1,0:T(8,128)(2,1)S(1)}, bf16[48,6144]{1,0:T(8,128)(2,1)S(1)}, u32[]{:S(2)}, u32[]{:S(2)}) collective-permute-start(bf16[48,6144]{1,0:T(8,128)(2,1)S(1)} %pad_maximum_fusion.1), channel_id=1, source_target_pairs={{0,4},{4,8},{8,12},{12,0},{1,5},{5,9},{9,13},{13,1},{2,6},{6,10},{... | collective-permute-start | bytes 1769480 | tf_op jit(solution)/shard_map/ppermute | solution.py:289
  22.6 16.0 %collective-permute-start.1 = (bf16[48,6144]{1,0:T(8,128)(2,1)S(1)}, bf16[48,6144]{1,0:T(8,128)(2,1)S(1)}, u32[]{:S(2)}, u32[]{:S(2)}) collective-permute-start(bf16[48,6144]{1,0:T(8,128)(2,1)S(1)} %pad_maximum_fusion.1), channel_id=1, source_target_pairs={{0,12},{4,0},{8,4},{12,8},{1,13},{5,1},{9,5},{13,9},{2,14},{6,2},{... | collective-permute-start | bytes 1769480 | tf_op jit(solution)/shard_map/ppermute | solution.py:289
  24.4 17.2 %collective-permute-start.5 = (bf16[48,6144]{1,0:T(8,128)(2,1)S(1)}, bf16[48,6144]{1,0:T(8,128)(2,1)S(1)}, u32[]{:S(2)}, u32[]{:S(2)}) collective-permute-start(bf16[48,6144]{1,0:T(8,128)(2,1)S(1)} %collective-permute-done.refs_1_), channel_id=1, source_target_pairs={{0,18},{2,16},{16,2},{18,0},{1,19},{3,17},{17,3},{19,1},{4,22},{6,... | collective-permute-start | bytes 1769480 | tf_op jit(solution)/shard_map/ppermute | solution.py:298
  26.8 26.1 %collective-permute-start.4 = (bf16[48,6144]{1,0:T(8,128)(2,1)S(1)}, bf16[48,6144]{1,0:T(8,128)(2,1)S(1)}, u32[]{:S(2)}, u32[]{:S(2)}) collective-permute-start(bf16[48,6144]{1,0:T(8,128)(2,1)S(1)} %collective-permute-done.refs_1_), channel_id=1, source_target_pairs={{0,16},{2,18},{16,0},{18,2},{1,17},{3,19},{17,1},{19,3},{4,20},{6,... | collective-permute-start | bytes 1769480 | tf_op jit(solution)/shard_map/ppermute | solution.py:298
  27.3 26.5 %collective-permute-start.3 = (bf16[48,6144]{1,0:T(8,128)(2,1)S(1)}, bf16[48,6144]{1,0:T(8,128)(2,1)S(1)}, u32[]{:S(2)}, u32[]{:S(2)}) collective-permute-start(bf16[48,6144]{1,0:T(8,128)(2,1)S(1)} %collective-permute-done.refs_1_), channel_id=1, source_target_pairs={{0,2},{2,0},{16,18},{18,16},{1,3},{3,1},{17,19},{19,17},{4,6},{6,4... | collective-permute-start | bytes 1769480 | tf_op jit(solution)/shard_map/ppermute | solution.py:298
  27.8 26.7 %collective-permute-start.2 = (bf16[48,6144]{1,0:T(8,128)(2,1)S(1)}, bf16[48,6144]{1,0:T(8,128)(2,1)S(1)}, u32[]{:S(2)}, u32[]{:S(2)}) collective-permute-start(bf16[48,6144]{1,0:T(8,128)(2,1)S(1)} %collective-permute-done.refs_1_), channel_id=1, source_target_pairs={{0,4},{4,8},{8,12},{12,0},{1,5},{5,9},{9,13},{13,1},{2,6},{6,10},{... | collective-permute-start | bytes 1769480 | tf_op jit(solution)/shard_map/ppermute | solution.py:289
  28.2 0.8 copy-start.2
  38.6 16.0 %copy-start.16 = (bf16[48,6144]{1,0:T(8,128)(2,1)}, bf16[48,6144]{1,0:T(8,128)(2,1)S(1)}, u32[]{:S(2)}) copy-start(bf16[48,6144]{1,0:T(8,128)(2,1)S(1)} %collective-permute-done.1) | copy-start | bytes 1769476
  41.5 0.8 copy-start.4
  52.9 0.9 copy-start.6
  53.8 0.8 copy-start.8
  54.6 0.8 copy-start.17
  55.4 58.2 %all-to-all-start.1 = ((bf16[8,192,768]{2,1,0:T(8,128)(2,1)}), bf16[8,192,768]{2,1,0:T(8,128)(2,1)S(1)}, u32[]{:S(2)}, u32[]{:S(2)}) async-start(bf16[8,192,768]{2,1,0:T(8,128)(2,1)} %get-tuple-element.29), calls=%async_computation.1 | async-start | bytes 4718592 | tf_op jit(solution)/shard_map/all_to_all | solution.py:317
  59.2 1.2 copy-start.18
  60.5 57.4 %collective-permute-start.8 = (bf16[96,6144]{1,0:T(8,128)(2,1)S(1)}, bf16[96,6144]{1,0:T(8,128)(2,1)}, u32[]{:S(2)}, u32[]{:S(2)}) collective-permute-start(bf16[96,6144]{1,0:T(8,128)(2,1)S(1)} %constant_dynamic-update-slice_fusion.refs_5_), channel_id=1, source_target_pairs={{0,18},{2,16},{16,2},{18,0},{1,19},{3,17},{17,3},{19,1},{4,22},{6,... | collective-permute-start | bytes 3538952 | tf_op jit(solution)/shard_map/ppermute | solution.py:298
  62.3 55.6 %collective-permute-start.7 = (bf16[96,6144]{1,0:T(8,128)(2,1)S(1)}, bf16[96,6144]{1,0:T(8,128)(2,1)}, u32[]{:S(2)}, u32[]{:S(2)}) collective-permute-start(bf16[96,6144]{1,0:T(8,128)(2,1)S(1)} %constant_dynamic-update-slice_fusion.refs_5_), channel_id=1, source_target_pairs={{0,16},{2,18},{16,0},{18,2},{1,17},{3,19},{17,1},{19,3},{4,20},{6,... | collective-permute-start | bytes 3538952 | tf_op jit(solution)/shard_map/ppermute | solution.py:298
  63.5 54.4 %collective-permute-start.6 = (bf16[96,6144]{1,0:T(8,128)(2,1)S(1)}, bf16[96,6144]{1,0:T(8,128)(2,1)}, u32[]{:S(2)}, u32[]{:S(2)}) collective-permute-start(bf16[96,6144]{1,0:T(8,128)(2,1)S(1)} %constant_dynamic-update-slice_fusion.refs_5_), channel_id=1, source_target_pairs={{0,2},{2,0},{16,18},{18,16},{1,3},{3,1},{17,19},{19,17},{4,6},{6,4... | collective-permute-start | bytes 3538952 | tf_op jit(solution)/shard_map/ppermute | solution.py:298
  113.6 0.7 copy-start.10
  117.2 0.7 copy-start.11
  117.9 10.9 %collective-permute-start.9 = (bf16[256,768]{1,0:T(8,128)(2,1)}, bf16[256,768]{1,0:T(8,128)(2,1)S(1)}, u32[]{:S(2)}, u32[]{:S(2)}) collective-permute-start(bf16[256,768]{1,0:T(8,128)(2,1)} %get-tuple-element.34), channel_id=1, source_target_pairs={{0,2},{2,0},{1,3},{3,1},{4,6},{6,4},{5,7},{7,5},{8,10},{10,8},{9,1... | collective-permute-start | bytes 1179656 | tf_op jit(solution)/shard_map/ppermute | solution.py:384
  128.9 1.0 copy-start.12
  129.9 1.5 copy-start.15
  129.9 1.6 copy-start.13
  131.3 2.9 %collective-permute-start.10 = (bf16[512,768]{1,0:T(8,128)(2,1)S(1)}, bf16[512,768]{1,0:T(8,128)(2,1)S(1)}, u32[]{:S(2)}, u32[]{:S(2)}) collective-permute-start(bf16[512,768]{1,0:T(8,128)(2,1)S(1)} %weave_steps.1.tok_ref), channel_id=1, source_target_pairs={{0,1},{1,0},{2,3},{3,2},{4,5},{5,4},{6,7},{7,6},{8,9},{9,8},{10,11... | collective-permute-start | bytes 2359304 | tf_op jit(solution)/shard_map/ppermute | solution.py:397
  131.5 1.1 copy-start.14
  131.5 1.1 copy-start.19
  132.6 1.7 %copy-start.3 = (bf16[48,6144]{1,0:T(8,128)(2,1)S(1)}, bf16[48,6144]{1,0:T(8,128)(2,1)}, u32[]{:S(2)}) copy-start(bf16[48,6144]{1,0:T(8,128)(2,1)} %copy-done.2) | copy-start | bytes 1769476
  132.6 1.7 %copy-start.5 = (bf16[48,6144]{1,0:T(8,128)(2,1)S(1)}, bf16[48,6144]{1,0:T(8,128)(2,1)}, u32[]{:S(2)}) copy-start(bf16[48,6144]{1,0:T(8,128)(2,1)} %copy-done.4) | copy-start | bytes 1769476
  132.6 2.1 %copy-start.7 = (bf16[48,6144]{1,0:T(8,128)(2,1)S(1)}, bf16[48,6144]{1,0:T(8,128)(2,1)}, u32[]{:S(2)}) copy-start(bf16[48,6144]{1,0:T(8,128)(2,1)} %copy-done.6) | copy-start | bytes 1769476
  132.6 2.4 %copy-start.9 = (bf16[48,6144]{1,0:T(8,128)(2,1)S(1)}, bf16[48,6144]{1,0:T(8,128)(2,1)}, u32[]{:S(2)}) copy-start(bf16[48,6144]{1,0:T(8,128)(2,1)} %copy-done.8) | copy-start | bytes 1769476
  146.0 12.7 %collective-permute-start.11 = (bf16[512,768]{1,0:T(8,128)(2,1)S(1)}, bf16[512,768]{1,0:T(8,128)(2,1)S(1)}, u32[]{:S(2)}, u32[]{:S(2)}) collective-permute-start(bf16[512,768]{1,0:T(8,128)(2,1)S(1)} %layer.3), channel_id=1, source_target_pairs={{0,1},{1,0},{2,3},{3,2},{4,5},{5,4},{6,7},{7,6},{8,9},{9,8},{10,11... | collective-permute-start | bytes 2359304 | tf_op jit(solution)/shard_map/ppermute | solution.py:399
  158.7 1.4 copy-start

commit v9 on v8

--- a/solution.py
+++ b/solution.py
@@ -15,7 +15,7 @@
 CODE = 32
 UNIT = 512
 LANES = 128
-VMEM_LIMIT = 48 * 1024 * 1024
+MIB = 1024 * 1024
 F32 = jnp.float32
 BF16 = jnp.bfloat16
 WHOLE = pl.BlockSpec(memory_space=pltpu.VMEM)
@@ -34,8 +34,8 @@
     return lax.dot_general(left, right, (((1,), (1,)), ((), ())), preferred_element_type=F32)
 
 
-def params():
-    return pltpu.CompilerParams(vmem_limit_bytes=VMEM_LIMIT)
+def params(mib):
+    return pltpu.CompilerParams(vmem_limit_bytes=mib * MIB)
 
 
 def place_kernel(capacity, owner_ref, position_ref, feat_ref, out_ref, code_ref):
@@ -68,7 +68,7 @@
         ],
         in_specs=[WHOLE] * 3,
         out_specs=[WHOLE] * 2,
-        compiler_params=params(),
+        compiler_params=params(24),
         cost_estimate=pl.CostEstimate(
             flops=2 * rows * width * n_owners * capacity,
             bytes_accessed=2 * width * (rows + n_owners * capacity),
@@ -108,7 +108,7 @@
         out_shape=[half, half],
         in_specs=[SCALARS] + [WHOLE] * 3,
         out_specs=[WHOLE] * 2,
-        compiler_params=params(),
+        compiler_params=params(24),
         cost_estimate=pl.CostEstimate(
             flops=2 * CB * slot_dev * got.size, bytes_accessed=2 * got.size, transcendentals=0
         ),
@@ -137,7 +137,7 @@
         out_shape=jax.ShapeDtypeStruct((rows, width), BF16),
         in_specs=[SCALARS] + [WHOLE] * 3,
         out_specs=WHOLE,
-        compiler_params=params(),
+        compiler_params=params(16),
         cost_estimate=pl.CostEstimate(
             flops=2 * rows * width * (rows + width), bytes_accessed=4 * rows * width, transcendentals=0
         ),
@@ -189,72 +189,76 @@
     return dot_t(hidden, down_w)
 
 
-def layer_kernel(plan, sections, tok_ref, *refs):
-    pieces, (out_ref, w_ref, norm_ref, ctx_ref, acc_ref, sems) = refs[:-6], refs[-6:]
-    copies = {}
-    for number, (section, piece, row, col, size) in enumerate(plan):
-        copy = pltpu.make_async_copy(
-            pieces[piece].at[:, pl.ds(col, size)],
-            w_ref.at[pl.ds(row, pieces[piece].shape[0]), pl.ds(col, size)],
-            sems.at[number],
-        )
+def put_rows_kernel(firsts, *refs):
+    pieces, (out_ref, sems) = refs[: len(firsts)], refs[-2:]
+    copies = [
+        pltpu.make_async_copy(piece, out_ref.at[pl.ds(first, piece.shape[0]), :], sems.at[number])
+        for number, (first, piece) in enumerate(zip(firsts, pieces))
+    ]
+    for copy in copies:
         copy.start()
-        copies.setdefault(section, []).append(copy)
-
-    def columns(section):
-        for copy in copies[section]:
-            copy.wait()
-        begin, end = sections[section]
-        return w_ref[:, begin:end]
-
-    tokens = tok_ref[...].astype(F32)
-    scale = lax.rsqrt(jnp.mean(tokens * tokens, axis=1, keepdims=True) + EPS)
-    norm_ref[...] = (tokens * scale).astype(BF16)
-    attention(norm_ref[...], columns(0), ctx_ref.shape[1], ctx_ref)
-    acc_ref[...] = dot_t(ctx_ref[...], columns(1))
-    for at in range(2, len(sections), 3):
-        add = gated(norm_ref[...], columns(at), columns(at + 1), columns(at + 2))
-        if at + 3 < len(sections):
-            acc_ref[...] += add
-        else:
-            out_ref[...] = (acc_ref[...] + add).astype(out_ref.dtype)
-
-
-def layer(tokens, pieces, heads_width, hidden_width, out_type):
-    rows, width = tokens.shape
+    for copy in copies:
+        copy.wait()
+
+
+def put_rows(pieces, rows, first, into=None):
+    firsts = [first + sum(piece.shape[0] for piece in pieces[:number]) for number in range(len(pieces))]
+    operands = pieces if into is None else pieces + [into]
+    return pl.pallas_call(
+        functools.partial(put_rows_kernel, firsts),
+        out_shape=jax.ShapeDtypeStruct((rows, pieces[0].shape[1]), BF16),
+        in_specs=[pl.BlockSpec(memory_space=pl.ANY)] * len(operands),
+        out_specs=pl.BlockSpec(memory_space=pl.ANY),
+        scratch_shapes=[pltpu.SemaphoreType.DMA((len(pieces),))],
+        input_output_aliases={} if into is None else {len(pieces): 0},
+        compiler_params=params(2),
+        cost_estimate=pl.CostEstimate(
+            flops=0, bytes_accessed=4 * sum(piece.size for piece in pieces), transcendentals=0
+        ),
+        name="put_rows",
+    )(*operands)
+
+
+def layer_kernel(hidden_width, tok_ref, w_ref, out_ref, norm_ref, ctx_ref, acc_ref):
+    heads_width = ctx_ref.shape[1]
     gate_at = 3 * heads_width
     up_at = gate_at + hidden_width
     out_at = up_at + hidden_width
     down_at = out_at + heads_width
-    columns = down_at + hidden_width
-    sections = [(0, gate_at), (out_at, down_at)]
+    tokens = tok_ref[...].astype(F32)
+    scale = lax.rsqrt(jnp.mean(tokens * tokens, axis=1, keepdims=True) + EPS)
+    norm_ref[...] = (tokens * scale).astype(BF16)
+    attention(norm_ref[...], w_ref[:, :gate_at], heads_width, ctx_ref)
+    acc_ref[...] = dot_t(ctx_ref[...], w_ref[:, out_at:down_at])
     for begin in range(0, hidden_width, UNIT):
-        sections += [(at + begin, at + begin + UNIT) for at in (gate_at, up_at, down_at)]
-    plan = [
-        (section, number, row, left, right - left)
-        for section, (left, right) in enumerate(sections)
-        for number, (_, row) in enumerate(pieces)
-    ]
-    return pl.pallas_call(
-        functools.partial(layer_kernel, plan, sections),
+        gate_w, up_w, down_w = [w_ref[:, at + begin : at + begin + UNIT] for at in (gate_at, up_at, down_at)]
+        add = gated(norm_ref[...], gate_w, up_w, down_w)
+        if begin + UNIT < hidden_width:
+            acc_ref[...] += add
+        else:
+            out_ref[...] = (acc_ref[...] + add).astype(out_ref.dtype)
+
+
+def layer(tokens, weights, heads_width, hidden_width, out_type):
+    rows, width = tokens.shape
+    return pl.pallas_call(
+        functools.partial(layer_kernel, hidden_width),
         out_shape=jax.ShapeDtypeStruct((rows, width), out_type),
-        in_specs=[WHOLE] + [pl.BlockSpec(memory_space=pl.ANY)] * len(pieces),
+        in_specs=[WHOLE] * 2,
         out_specs=WHOLE,
         scratch_shapes=[
-            pltpu.VMEM((width, columns), BF16),
             pltpu.VMEM((rows, width), BF16),
             pltpu.VMEM((rows, heads_width), BF16),
             pltpu.VMEM((rows, width), F32),
-            pltpu.SemaphoreType.DMA((len(plan),)),
         ],
-        compiler_params=params(),
-        cost_estimate=pl.CostEstimate(
-            flops=2 * rows * width * columns,
-            bytes_accessed=2 * width * columns + 6 * rows * width,
+        compiler_params=params(36),
+        cost_estimate=pl.CostEstimate(
+            flops=2 * rows * width * weights.shape[1],
+            bytes_accessed=2 * weights.size + 6 * rows * width,
             transcendentals=rows * hidden_width,
         ),
         name="layer",
-    )(tokens, *[array for array, _ in pieces])
+    )(tokens, weights)
 
 
 def finish_kernel(tok_ref, sum_ref, got_ref, order_ref, out_ref):
@@ -271,7 +275,7 @@
         out_shape=jax.ShapeDtypeStruct((rows, width), BF16),
         in_specs=[WHOLE] * 4,
         out_specs=WHOLE,
-        compiler_params=params(),
+        compiler_params=params(16),
         cost_estimate=pl.CostEstimate(
             flops=2 * rows * width * width, bytes_accessed=10 * rows * width, transcendentals=0
         ),
@@ -311,11 +315,6 @@
     distance = jnp.where(past < 0, n_cells - 1, 1 + past // share % 2)
     other = (mine + distance) % n_cells * rows + (far ^ place) * share + row % share
     return jnp.where(row < rows, mine * rows + row, other)
-
-
-def pooled_blocks(blocks, codes, time_embed, my_slot, slot_dev):
-    got = lax.all_to_all(blocks, ("cells", "mp"), split_axis=0, concat_axis=0, tiled=True)
-    return pool_rows(my_slot.reshape(1), time_embed, codes, got, blocks.shape[1], slot_dev)
 
 
 def tokens_by_exchanges(owner, position, obs_feat, time_embed, my_slot, capacity, slot_dev):
@@ -379,25 +378,26 @@
         above, opposite = along_cells(share_rows, 1), along_cells(below, -1)
         blocks, above, opposite, first = lax.optimization_barrier((blocks, above, opposite, first))
         second = to_other_places(jnp.concatenate([above, opposite], axis=0))
-        keep, send = pooled_blocks(blocks, codes, time_embed, my_slot, slot_dev)
+        weights = put_rows([side_by_side(*local_weights)] + first, width, 0)
+        got = lax.all_to_all(blocks, ("cells", "mp"), split_axis=0, concat_axis=0, tiled=True)
+        got, weights = lax.optimization_barrier((got, weights))
+        keep, send = pool_rows(my_slot.reshape(1), time_embed, codes, got, capacity, slot_dev)
         send, second = lax.optimization_barrier((send, second))
         other = lax.ppermute(send, "slots", [(0, 1), (1, 0)])
+        weights = put_rows(second, width, width // 2, weights)
+        other, weights = lax.optimization_barrier((other, weights))
         tokens = weave_steps(my_slot.reshape(1), order, keep, other, slot_dev)
-        pieces, row = [], 0
-        for array in [side_by_side(*local_weights)] + first + second:
-            pieces.append((array, row))
-            row += array.shape[0]
     else:
         order = jnp.arange(width, dtype=jnp.int32)
-        pieces = [(lax.all_gather(share_rows, ("cells", "groups", "slots"), axis=0, tiled=True), 0)]
+        weights = lax.all_gather(share_rows, ("cells", "groups", "slots"), axis=0, tiled=True)
         tokens = tokens_by_exchanges(owner, position, obs_feat, time_embed, my_slot, capacity, slot_dev)
 
     swap = [(0, 1), (1, 0)]
     heads_width, hidden_width = w_qkv.shape[2], w_gate_up.shape[2]
     partner = lax.ppermute(tokens, "mp", swap)
-    for_partner = layer(partner, pieces, heads_width, hidden_width, BF16)
+    for_partner = layer(partner, weights, heads_width, hidden_width, BF16)
     from_partner = lax.ppermute(for_partner, "mp", swap)
-    own = layer(tokens, pieces, heads_width, hidden_width, F32)
+    own = layer(tokens, weights, heads_width, hidden_width, F32)
     return finish(tokens, own, from_partner, order).reshape(quarter, TSTEPS, width)
 
 

time: 163 us -> 154 us (0.945)
  waiting for transfers between devices: 82 us -> 68.1 us
  local copies, waits for them, and re-layouts: 15.1 us -> 28.2 us
  Pallas kernels: 32.6 us -> 27.1 us
    ppermute x3, waiting for transfers between devices: 9.63 us -> 21.8 us  [along_cells(): lax.ppermute(values, 'cells', [(j, (j - distance) % n_cells) for j in ran...]
    unnamed x48 -> x54, local copies, waits for them, and re-layouts: 12 us -> 24.2 us
    ppermute x6, waiting for transfers between devices: 13.5 us -> 1.62 us  [to_other_places(): places.append(lax.ppermute(shares, ('groups', 'slots'), pairs))]
    ppermute x1, waiting for transfers between devices: 9.34 us -> 0.78 us  [on_device(): other = lax.ppermute(send, 'slots', [(0, 1), (1, 0)])]
    all_to_all x1, waiting for transfers between devices: 49.6 us -> 41.7 us  [on_device(): lax.all_to_all(blocks, ('cells', 'mp'), split_axis=0, concat_axis=0, tile...]
    pallas_call x2 -> x4, Pallas kernels: 23.1 us -> 17.7 us  [the longest x2 14.5 us: layer(): pl.pallas_call(functools.partial(layer_kernel, hidden_width), out_shape=j...]
    ppermute x1, waiting for transfers between devices: 0.01 us -> 2.27 us  [on_device(): partner = lax.ppermute(tokens, 'mp', swap)]
  transfers between devices with their start and end apart: 13 -> 13, of which waited for: 5 -> 6; matrix products, arithmetic and copies ran while one was open for 2% -> 2% of each run, Pallas kernels for 11% -> 11%
where the time goes in v9:
time: 154 us
  waiting for transfers between devices  68.1 us (44%)
  local copies, waits for them, and re-layouts  28.2 us (18%)
  Pallas kernels  27.1 us (18%)
  starting transfers between devices  17.7 us (11%)
  blocking collectives  11.5 us (7%)
    all_to_all x1, waiting for transfers between devices, on_device(): lax.all_to_all(blocks, ('cells', 'mp'), split_axis=0, concat_axis=0, tile...  41.7 us
    unnamed x54, local copies, waits for them, and re-layouts  24.2 us
    ppermute x3, waiting for transfers between devices, along_cells(): lax.ppermute(values, 'cells', [(j, (j - distance) % n_cells) for j in ran...  21.8 us
    pallas_call x2, Pallas kernels, layer(): pl.pallas_call(functools.partial(layer_kernel, hidden_width), out_shape=j...  14.5 us
    all_to_all x1, blocking collectives, on_device(): lax.all_to_all(codes, ('cells', 'mp'), split_axis=0, concat_axis=0, tiled...  11.5 us
    ppermute x6, starting transfers between devices, to_other_places(): places.append(lax.ppermute(shares, ('groups', 'slots'), pairs))  7.04 us
    ppermute x3, starting transfers between devices, along_cells(): lax.ppermute(values, 'cells', [(j, (j - distance) % n_cells) for j in ran...  5.1 us
    all_to_all x1, starting transfers between devices, on_device(): lax.all_to_all(blocks, ('cells', 'mp'), split_axis=0, concat_axis=0, tile...  4.82 us
  transfers between devices with their start and end apart: 13, of which 6 were waited for; matrix products, arithmetic and copies ran while one was open for 2% of the time, Pallas kernels for 11%

profile of v9, /device:TPU:0, one launch (start us, length us, event | category | flops | bytes accessed | tf_op | source)
XLA Modules:
  0.0 153.8 jit_solution(16161415542767277140)
XLA Ops:
  0.0 1.2 constant_dynamic-slice_fusion
  1.2 1.0 dynamic-slice_bitcast_fusion.1
  2.3 0.9 dynamic-slice_bitcast_fusion
  3.2 0.8 dynamic-slice_bitcast_fusion.2
  4.0 3.1 %collective-permute-start = (bf16[48,6144]{1,0:T(8,128)(2,1)S(1)}, bf16[48,6144]{1,0:T(8,128)(2,1)S(1)}, u32[]{:S(2)}, u32[]{:S(2)}) collective-permute-start(bf16[48,6144]{1,0:T(8,128)(2,1)S(1)} %pad_maximum_fusion.1), channel_id=1, source_target_pairs={{0,4},{4,8},{8,12},{12,0},{1,5},{5,9},{9,13},{13,1},{2,6},{6,10},{... | collective-permute-start | bytes 1769480 | tf_op jit(solution)/shard_map/ppermute | solution.py:293
  7.8 3.3 %place_rows.1 = (bf16[8,192,768]{2,1,0:T(8,128)(2,1)}, s32[8,1,192]{2,1,0:T(1,128)S(1)}) custom-call(s32[1,512]{1,0:T(1,128)S(1)} %bitcast.22, s32[1,512]{1,0:T(1,128)S(1)} %bitcast.21, bf16[512,768]{1,0:T(8,128)(2,1)S(1)} %copy-done.13), custom_call_target="tpu_custom_call" | custom-call | flops 1207959552 | bytes 3145728 | tf_op jit(solution)/shard_map/place_rows/pallas_call | solution.py:63
  11.1 11.5 %all_to_all.10.code_ref = s32[8,1,192]{2,1,0:T(1,128)S(1)} all-to-all(s32[8,1,192]{2,1,0:T(1,128)S(1)} %get-tuple-element.28), channel_id=1, replica_groups=mesh['groups'=2,'cells'=4,'slots'=2,'mp'=2] {'cells','mp'}, dimensions={0} | all-to-all | bytes 12288 | tf_op jit(solution)/shard_map/all_to_all | solution.py:375
  22.6 1.7 %collective-permute-start.1 = (bf16[48,6144]{1,0:T(8,128)(2,1)S(1)}, bf16[48,6144]{1,0:T(8,128)(2,1)S(1)}, u32[]{:S(2)}, u32[]{:S(2)}) collective-permute-start(bf16[48,6144]{1,0:T(8,128)(2,1)S(1)} %pad_maximum_fusion.1), channel_id=1, source_target_pairs={{0,12},{4,0},{8,4},{12,8},{1,13},{5,1},{9,5},{13,9},{2,14},{6,2},{... | collective-permute-start | bytes 1769480 | tf_op jit(solution)/shard_map/ppermute | solution.py:293
  24.4 0.3 collective-permute-start.2
  24.7 1.5 collective-permute-start.3
  26.2 1.5 collective-permute-start.4
  27.7 0.5 collective-permute-start.5
  28.2 0.8 copy-done.5
  29.0 9.6 %collective-permute-done.1 = bf16[48,6144]{1,0:T(8,128)(2,1)S(1)} collective-permute-done((bf16[48,6144]{1,0:T(8,128)(2,1)S(1)}, bf16[48,6144]{1,0:T(8,128)(2,1)S(1)}, u32[]{:S(2)}, u32[]{:S(2)}) %collective-permute-start.1) | collective-permute-done | bytes 589856 | tf_op jit(solution)/shard_map/ppermute | solution.py:293
  38.6 12.1 %collective-permute-done.2 = bf16[48,6144]{1,0:T(8,128)(2,1)S(1)} collective-permute-done((bf16[48,6144]{1,0:T(8,128)(2,1)S(1)}, bf16[48,6144]{1,0:T(8,128)(2,1)S(1)}, u32[]{:S(2)}, u32[]{:S(2)}) %collective-permute-start.2) | collective-permute-done | bytes 589856 | tf_op jit(solution)/shard_map/ppermute | solution.py:293
  50.7 0.9 copy-done.7
  51.6 1.6 %collective-permute-done.4.refs_3_ = bf16[48,6144]{1,0:T(8,128)(2,1)S(1)} collective-permute-done((bf16[48,6144]{1,0:T(8,128)(2,1)S(1)}, bf16[48,6144]{1,0:T(8,128)(2,1)S(1)}, u32[]{:S(2)}, u32[]{:S(2)}) %collective-permute-start.4) | collective-permute-done | bytes 589856 | tf_op jit(solution)/shard_map/ppermute | solution.py:302
  53.2 0.8 copy-done.9
  54.1 0.8 copy-done.11
  54.9 4.8 %all-to-all-start.1 = ((bf16[8,192,768]{2,1,0:T(8,128)(2,1)}), bf16[8,192,768]{2,1,0:T(8,128)(2,1)S(1)}, u32[]{:S(2)}, u32[]{:S(2)}) async-start(bf16[8,192,768]{2,1,0:T(8,128)(2,1)} %get-tuple-element.33), calls=%async_computation.1 | async-start | bytes 4718592 | tf_op jit(solution)/shard_map/all_to_all | solution.py:382
  59.7 1.2 constant_dynamic-update-slice_fusion.1
  60.9 1.1 constant_dynamic-update-slice_fusion.refs_0_
  62.0 0.5 collective-permute-start.6
  62.5 1.7 %collective-permute-start.7 = (bf16[96,6144]{1,0:T(8,128)(2,1)S(1)}, bf16[96,6144]{1,0:T(8,128)(2,1)}, u32[]{:S(2)}, u32[]{:S(2)}) collective-permute-start(bf16[96,6144]{1,0:T(8,128)(2,1)S(1)} %constant_dynamic-update-slice_fusion.refs_0_), channel_id=1, source_target_pairs={{0,16},{2,18},{16,0},{18,2},{1,17},{3,19},{17,1},{19,3},{4,20},{6,... | collective-permute-start | bytes 3538952 | tf_op jit(solution)/shard_map/ppermute | solution.py:302
  64.1 1.4 collective-permute-start.8
  65.7 0.9 copy-done.19
  66.8 0.2 pad_maximum_fusion.refs_0_
  67.0 0.8 copy-done.6
  68.0 0.2 copy-done.10
  68.2 0.2 copy-done.12
  68.4 0.7 put_rows.2.refs_4_
  69.1 3.6 %copy-done = bf16[768,6144]{1,0:T(8,128)(2,1)} copy-done((bf16[768,6144]{1,0:T(8,128)(2,1)}, bf16[768,6144]{1,0:T(8,128)(2,1)S(1)}, u32[]{:S(2)}) %copy-start) | copy-done | bytes 9437208
  72.7 41.7 %all-to-all-done.1.got_ref = bf16[8,192,768]{2,1,0:T(8,128)(2,1)S(1)} async-done(((bf16[8,192,768]{2,1,0:T(8,128)(2,1)}), bf16[8,192,768]{2,1,0:T(8,128)(2,1)S(1)}, u32[]{:S(2)}, u32[]{:S(2)}) %all-to-all-start.1) | async-done | bytes 2359328 | tf_op jit(solution)/shard_map/all_to_all | solution.py:382
  114.4 0.7 copy-done.14
  115.1 2.8 %pool_rows.1 = (bf16[256,768]{1,0:T(8,128)(2,1)S(1)}, bf16[256,768]{1,0:T(8,128)(2,1)}) custom-call(s32[1]{0:T(128)} %bitcast.slot_ref, bf16[8,768]{1,0:T(8,128)(2,1)S(1)} %copy-done.14, s32[8,1,192]{2,1,0:T(1,128)S(1)} %all_to_all.10.code_ref, bf16[8,192,768]{2,1,0:T(8,128)(2,1)S(1)} %all-to-all-done.1.got_ref), custom_call_target="tpu_custom_call" | custom-call | flops 1207959552 | bytes 2359296 | tf_op jit(solution)/shard_map/pool_rows/pallas_call | solution.py:106
  117.9 0.7 copy-done.15
  118.7 0.5 collective-permute-start.9
  119.2 3.7 %copy-done.1 = bf16[768,6144]{1,0:T(8,128)(2,1)S(1)} copy-done((bf16[768,6144]{1,0:T(8,128)(2,1)S(1)}, bf16[768,6144]{1,0:T(8,128)(2,1)}, u32[]{:S(2)}) %copy-start.1) | copy-done | bytes 9437208
  122.9 2.4 %put_rows.3.w_ref = bf16[768,6144]{1,0:T(8,128)(2,1)S(1)} custom-call(bf16[96,6144]{1,0:T(8,128)(2,1)S(1)} %constant_dynamic-update-slice_fusion.refs_0_, bf16[96,6144]{1,0:T(8,128)(2,1)} %collective-permute-done.6.refs_1_, bf16[96,6144]{1,0:T(8,128)(2,1)} %collective-permute-done.7.refs_2_, ...), custom_call_target="tpu_custom_call", output_to_operand_aliasing={{}: (4, {})} | custom-call | bytes 9437184 | tf_op jit(solution)/shard_map/put_rows/pallas_call | solution.py:207
  125.3 3.6 %copy-done.2 = bf16[768,6144]{1,0:T(8,128)(2,1)} copy-done((bf16[768,6144]{1,0:T(8,128)(2,1)}, bf16[768,6144]{1,0:T(8,128)(2,1)S(1)}, u32[]{:S(2)}) %copy-start.2) | copy-done | bytes 9437208
  129.0 0.8 collective-permute-done.9.got_ref
  129.7 1.5 weave_steps.1.tok_ref
  131.3 2.3 %collective-permute-done.10.tok_ref = bf16[512,768]{1,0:T(8,128)(2,1)S(1)} collective-permute-done((bf16[512,768]{1,0:T(8,128)(2,1)S(1)}, bf16[512,768]{1,0:T(8,128)(2,1)S(1)}, u32[]{:S(2)}, u32[]{:S(2)}) %collective-permute-start.10) | collective-permute-done | bytes 786464 | tf_op jit(solution)/shard_map/ppermute | solution.py:397
  133.6 3.7 %copy-done.3 = bf16[768,6144]{1,0:T(8,128)(2,1)S(1)} copy-done((bf16[768,6144]{1,0:T(8,128)(2,1)S(1)}, bf16[768,6144]{1,0:T(8,128)(2,1)}, u32[]{:S(2)}) %copy-start.3) | copy-done | bytes 9437208
  137.2 7.3 %layer.3 = bf16[512,768]{1,0:T(8,128)(2,1)S(1)} custom-call(bf16[512,768]{1,0:T(8,128)(2,1)S(1)} %collective-permute-done.10.tok_ref, bf16[768,6144]{1,0:T(8,128)(2,1)S(1)} %copy-done.3), custom_call_target="tpu_custom_call" | custom-call | flops 4831838208 | bytes 11796480 | tf_op jit(solution)/shard_map/layer/pallas_call | solution.py:244
  144.5 0.2 collective-permute-start.11
  144.7 7.3 %layer.2.sum_ref = f32[512,768]{1,0:T(8,128)S(1)} custom-call(bf16[512,768]{1,0:T(8,128)(2,1)S(1)} %weave_steps.1.tok_ref, bf16[768,6144]{1,0:T(8,128)(2,1)S(1)} %copy-done.4), custom_call_target="tpu_custom_call" | custom-call | flops 4831838208 | bytes 11796480 | tf_op jit(solution)/shard_map/layer/pallas_call | solution.py:244
  152.0 1.8 %finish.1 = bf16[512,768]{1,0:T(8,128)(2,1)} custom-call(bf16[512,768]{1,0:T(8,128)(2,1)S(1)} %weave_steps.1.tok_ref, f32[512,768]{1,0:T(8,128)S(1)} %layer.2.sum_ref, bf16[512,768]{1,0:T(8,128)(2,1)S(1)} %collective-permute-done.11.got_ref, s32[1,768]{1,0:T(1,128)S(1)} %compare_select_fusion.6.order_ref), custom_call_target="tpu_custom_call" | custom-call | flops 603979776 | bytes 3932160 | tf_op jit(solution)/shard_map/finish/pallas_call | solution.py:273
  (51 shorter events, 0.8 us)
Async XLA Ops:
  1.2 6.6 %copy-start.23 = (s32[512]{0:T(512)S(1)}, s32[512]{0:T(512)}, u32[]{:S(2)}) copy-start(s32[512]{0:T(512)} %param.11) | copy-start | bytes 6148
  1.2 6.6 %copy-start.24 = (s32[512]{0:T(512)S(1)}, s32[512]{0:T(512)}, u32[]{:S(2)}) copy-start(s32[512]{0:T(512)} %param.10) | copy-start | bytes 6148
  1.2 6.6 %copy-start.13 = (bf16[512,768]{1,0:T(8,128)(2,1)S(1)}, bf16[512,768]{1,0:T(8,128)(2,1)}, u32[]{:S(2)}) copy-start(bf16[512,768]{1,0:T(8,128)(2,1)} %feat_ref.1) | copy-start | bytes 2359300
  4.0 18.6 %collective-permute-start = (bf16[48,6144]{1,0:T(8,128)(2,1)S(1)}, bf16[48,6144]{1,0:T(8,128)(2,1)S(1)}, u32[]{:S(2)}, u32[]{:S(2)}) collective-permute-start(bf16[48,6144]{1,0:T(8,128)(2,1)S(1)} %pad_maximum_fusion.1), channel_id=1, source_target_pairs={{0,4},{4,8},{8,12},{12,0},{1,5},{5,9},{9,13},{13,1},{2,6},{6,10},{... | collective-permute-start | bytes 1769480 | tf_op jit(solution)/shard_map/ppermute | solution.py:293
  22.6 16.0 %collective-permute-start.1 = (bf16[48,6144]{1,0:T(8,128)(2,1)S(1)}, bf16[48,6144]{1,0:T(8,128)(2,1)S(1)}, u32[]{:S(2)}, u32[]{:S(2)}) collective-permute-start(bf16[48,6144]{1,0:T(8,128)(2,1)S(1)} %pad_maximum_fusion.1), channel_id=1, source_target_pairs={{0,12},{4,0},{8,4},{12,8},{1,13},{5,1},{9,5},{13,9},{2,14},{6,2},{... | collective-permute-start | bytes 1769480 | tf_op jit(solution)/shard_map/ppermute | solution.py:293
  24.4 26.4 %collective-permute-start.2 = (bf16[48,6144]{1,0:T(8,128)(2,1)S(1)}, bf16[48,6144]{1,0:T(8,128)(2,1)S(1)}, u32[]{:S(2)}, u32[]{:S(2)}) collective-permute-start(bf16[48,6144]{1,0:T(8,128)(2,1)S(1)} %collective-permute-done.refs_1_), channel_id=1, source_target_pairs={{0,4},{4,8},{8,12},{12,0},{1,5},{5,9},{9,13},{13,1},{2,6},{6,10},{... | collective-permute-start | bytes 1769480 | tf_op jit(solution)/shard_map/ppermute | solution.py:293
  24.7 26.1 %collective-permute-start.3 = (bf16[48,6144]{1,0:T(8,128)(2,1)S(1)}, bf16[48,6144]{1,0:T(8,128)(2,1)S(1)}, u32[]{:S(2)}, u32[]{:S(2)}) collective-permute-start(bf16[48,6144]{1,0:T(8,128)(2,1)S(1)} %collective-permute-done.refs_1_), channel_id=1, source_target_pairs={{0,2},{2,0},{16,18},{18,16},{1,3},{3,1},{17,19},{19,17},{4,6},{6,4... | collective-permute-start | bytes 1769480 | tf_op jit(solution)/shard_map/ppermute | solution.py:302
  26.2 27.1 %collective-permute-start.4 = (bf16[48,6144]{1,0:T(8,128)(2,1)S(1)}, bf16[48,6144]{1,0:T(8,128)(2,1)S(1)}, u32[]{:S(2)}, u32[]{:S(2)}) collective-permute-start(bf16[48,6144]{1,0:T(8,128)(2,1)S(1)} %collective-permute-done.refs_1_), channel_id=1, source_target_pairs={{0,16},{2,18},{16,0},{18,2},{1,17},{3,19},{17,1},{19,3},{4,20},{6,... | collective-permute-start | bytes 1769480 | tf_op jit(solution)/shard_map/ppermute | solution.py:302
  27.7 26.4 %collective-permute-start.5 = (bf16[48,6144]{1,0:T(8,128)(2,1)S(1)}, bf16[48,6144]{1,0:T(8,128)(2,1)S(1)}, u32[]{:S(2)}, u32[]{:S(2)}) collective-permute-start(bf16[48,6144]{1,0:T(8,128)(2,1)S(1)} %collective-permute-done.refs_1_), channel_id=1, source_target_pairs={{0,18},{2,16},{16,2},{18,0},{1,19},{3,17},{17,3},{19,1},{4,22},{6,... | collective-permute-start | bytes 1769480 | tf_op jit(solution)/shard_map/ppermute | solution.py:302
  28.1 0.8 copy-start.5
  38.6 15.5 %copy-start.20 = (bf16[48,6144]{1,0:T(8,128)(2,1)}, bf16[48,6144]{1,0:T(8,128)(2,1)S(1)}, u32[]{:S(2)}) copy-start(bf16[48,6144]{1,0:T(8,128)(2,1)S(1)} %collective-permute-done.1) | copy-start | bytes 1769476
  50.7 3.3 %copy-start.21 = (bf16[48,6144]{1,0:T(8,128)(2,1)}, bf16[48,6144]{1,0:T(8,128)(2,1)S(1)}, u32[]{:S(2)}) copy-start(bf16[48,6144]{1,0:T(8,128)(2,1)S(1)} %collective-permute-done.2) | copy-start | bytes 1769476
  50.7 0.9 copy-start.7
  53.2 0.8 copy-start.9
  54.1 0.8 copy-start.11
  54.9 59.5 %all-to-all-start.1 = ((bf16[8,192,768]{2,1,0:T(8,128)(2,1)}), bf16[8,192,768]{2,1,0:T(8,128)(2,1)S(1)}, u32[]{:S(2)}, u32[]{:S(2)}) async-start(bf16[8,192,768]{2,1,0:T(8,128)(2,1)} %get-tuple-element.33), calls=%async_computation.1 | async-start | bytes 4718592 | tf_op jit(solution)/shard_map/all_to_all | solution.py:382
  59.7 5.9 %copy-start.17 = (bf16[192,2,1536]{2,1,0:T(2,128)(2,1)S(1)}, bf16[192,2,1536]{2,1,0:T(2,128)(2,1)}, u32[]{:S(2)}) copy-start(bf16[192,2,1536]{2,1,0:T(2,128)(2,1)} %param.16) | copy-start | bytes 3538948
  62.0 56.7 %collective-permute-start.6 = (bf16[96,6144]{1,0:T(8,128)(2,1)S(1)}, bf16[96,6144]{1,0:T(8,128)(2,1)}, u32[]{:S(2)}, u32[]{:S(2)}) collective-permute-start(bf16[96,6144]{1,0:T(8,128)(2,1)S(1)} %constant_dynamic-update-slice_fusion.refs_0_), channel_id=1, source_target_pairs={{0,2},{2,0},{16,18},{18,16},{1,3},{3,1},{17,19},{19,17},{4,6},{6,4... | collective-permute-start | bytes 3538952 | tf_op jit(solution)/shard_map/ppermute | solution.py:302
  62.5 56.2 %collective-permute-start.7 = (bf16[96,6144]{1,0:T(8,128)(2,1)S(1)}, bf16[96,6144]{1,0:T(8,128)(2,1)}, u32[]{:S(2)}, u32[]{:S(2)}) collective-permute-start(bf16[96,6144]{1,0:T(8,128)(2,1)S(1)} %constant_dynamic-update-slice_fusion.refs_0_), channel_id=1, source_target_pairs={{0,16},{2,18},{16,0},{18,2},{1,17},{3,19},{17,1},{19,3},{4,20},{6,... | collective-permute-start | bytes 3538952 | tf_op jit(solution)/shard_map/ppermute | solution.py:302
  64.1 54.6 %collective-permute-start.8 = (bf16[96,6144]{1,0:T(8,128)(2,1)S(1)}, bf16[96,6144]{1,0:T(8,128)(2,1)}, u32[]{:S(2)}, u32[]{:S(2)}) collective-permute-start(bf16[96,6144]{1,0:T(8,128)(2,1)S(1)} %constant_dynamic-update-slice_fusion.refs_0_), channel_id=1, source_target_pairs={{0,18},{2,16},{16,2},{18,0},{1,19},{3,17},{17,3},{19,1},{4,22},{6,... | collective-permute-start | bytes 3538952 | tf_op jit(solution)/shard_map/ppermute | solution.py:302
  65.6 1.0 copy-start.19
  65.6 1.2 copy-start.18
  65.6 1.2 copy-start.22
  66.8 1.1 copy-start.6
  66.8 1.2 copy-start.8
  66.8 1.4 copy-start.10
  66.8 1.6 %copy-start.12 = (bf16[48,6144]{1,0:T(8,128)(2,1)S(1)}, bf16[48,6144]{1,0:T(8,128)(2,1)}, u32[]{:S(2)}) copy-start(bf16[48,6144]{1,0:T(8,128)(2,1)} %copy-done.11) | copy-start | bytes 1769476
  69.1 3.6 %copy-start = (bf16[768,6144]{1,0:T(8,128)(2,1)}, bf16[768,6144]{1,0:T(8,128)(2,1)S(1)}, u32[]{:S(2)}) copy-start(bf16[768,6144]{1,0:T(8,128)(2,1)S(1)} %put_rows.2.refs_4_) | copy-start | bytes 28311556
  114.4 0.7 copy-start.14
  117.9 0.7 copy-start.15
  118.7 11.0 %collective-permute-start.9 = (bf16[256,768]{1,0:T(8,128)(2,1)}, bf16[256,768]{1,0:T(8,128)(2,1)S(1)}, u32[]{:S(2)}, u32[]{:S(2)}) collective-permute-start(bf16[256,768]{1,0:T(8,128)(2,1)} %get-tuple-element.43), channel_id=1, source_target_pairs={{0,2},{2,0},{1,3},{3,1},{4,6},{6,4},{5,7},{7,5},{8,10},{10,8},{9,1... | collective-permute-start | bytes 1179656 | tf_op jit(solution)/shard_map/ppermute | solution.py:386
  119.2 3.7 %copy-start.1 = (bf16[768,6144]{1,0:T(8,128)(2,1)S(1)}, bf16[768,6144]{1,0:T(8,128)(2,1)}, u32[]{:S(2)}) copy-start(bf16[768,6144]{1,0:T(8,128)(2,1)} %copy-done) | copy-start | bytes 28311556
  122.9 6.9 %copy-start.16 = (bf16[256,768]{1,0:T(8,128)(2,1)S(1)}, bf16[256,768]{1,0:T(8,128)(2,1)}, u32[]{:S(2)}) copy-start(bf16[256,768]{1,0:T(8,128)(2,1)} %copy-done.15) | copy-start | bytes 1179652
  125.3 3.6 %copy-start.2 = (bf16[768,6144]{1,0:T(8,128)(2,1)}, bf16[768,6144]{1,0:T(8,128)(2,1)S(1)}, u32[]{:S(2)}) copy-start(bf16[768,6144]{1,0:T(8,128)(2,1)S(1)} %put_rows.3.w_ref) | copy-start | bytes 28311556
  131.2 2.4 %collective-permute-start.10 = (bf16[512,768]{1,0:T(8,128)(2,1)S(1)}, bf16[512,768]{1,0:T(8,128)(2,1)S(1)}, u32[]{:S(2)}, u32[]{:S(2)}) collective-permute-start(bf16[512,768]{1,0:T(8,128)(2,1)S(1)} %weave_steps.1.tok_ref), channel_id=1, source_target_pairs={{0,1},{1,0},{2,3},{3,2},{4,5},{5,4},{6,7},{7,6},{8,9},{9,8},{10,11... | collective-permute-start | bytes 2359304 | tf_op jit(solution)/shard_map/ppermute | solution.py:397
  133.6 3.7 %copy-start.3 = (bf16[768,6144]{1,0:T(8,128)(2,1)S(1)}, bf16[768,6144]{1,0:T(8,128)(2,1)}, u32[]{:S(2)}) copy-start(bf16[768,6144]{1,0:T(8,128)(2,1)} %copy-done.2) | copy-start | bytes 28311556
  137.2 7.5 %copy-start.4 = (bf16[768,6144]{1,0:T(8,128)(2,1)S(1)}, bf16[768,6144]{1,0:T(8,128)(2,1)}, u32[]{:S(2)}) copy-start(bf16[768,6144]{1,0:T(8,128)(2,1)} %copy-done.2) | copy-start | bytes 28311556
  144.5 7.5 %collective-permute-start.11 = (bf16[512,768]{1,0:T(8,128)(2,1)S(1)}, bf16[512,768]{1,0:T(8,128)(2,1)S(1)}, u32[]{:S(2)}, u32[]{:S(2)}) collective-permute-start(bf16[512,768]{1,0:T(8,128)(2,1)S(1)} %layer.3), channel_id=1, source_target_pairs={{0,1},{1,0},{2,3},{3,2},{4,5},{5,4},{6,7},{7,6},{8,9},{9,8},{10,11... | collective-permute-start | bytes 2359304 | tf_op jit(solution)/shard_map/ppermute | solution.py:399

commit v10 on v9

--- a/solution.py
+++ b/solution.py
@@ -38,44 +38,75 @@
     return pltpu.CompilerParams(vmem_limit_bytes=mib * MIB)
 
 
-def place_kernel(capacity, owner_ref, position_ref, feat_ref, out_ref, code_ref):
-    n_owners, rows = out_ref.shape[0], feat_ref.shape[0]
-    owner = owner_ref[...]
+def block_places(owner, n_owners):
+    rows = owner.shape[1]
     owner_hot = (iota((n_owners, rows), 0) == owner).astype(F32)
     upper = (iota((rows, rows), 0) <= iota((rows, rows), 1)).astype(BF16)
     running = dot(owner_hot.astype(BF16), upper)
-    rank = jnp.sum(running * owner_hot, axis=0, keepdims=True).astype(jnp.int32) - 1
+    return jnp.sum(running * owner_hot, axis=0, keepdims=True).astype(jnp.int32) - 1
+
+
+def one_hot_rows(owner, rank, block, capacity):
+    place = jnp.where(owner == block, rank, -1)
+    return (iota((capacity, owner.shape[1]), 0) == place).astype(F32).astype(BF16)
+
+
+def code_kernel(owner_ref, position_ref, time_ref, code_ref, embed_ref):
+    n_owners, _, capacity = code_ref.shape
+    embed_ref[...] = time_ref[...]
+    owner = owner_ref[...]
+    rank = block_places(owner, n_owners)
     code = position_ref[...] + 1
-    line = iota((8, rows), 0)
+    line = iota((8, owner.shape[1]), 0)
     digits = jnp.where(line == 0, code // CODE, jnp.where(line == 1, code % CODE, 0))
     digits = digits.astype(F32).astype(BF16)
-    feat = feat_ref[...]
     for block in range(n_owners):
-        place = jnp.where(owner == block, rank, -1)
-        taken = (iota((capacity, rows), 0) == place).astype(F32).astype(BF16)
-        out_ref[block] = dot(taken, feat).astype(BF16)
-        sent = dot_t(digits, taken)
+        sent = dot_t(digits, one_hot_rows(owner, rank, block, capacity))
         code_ref[block] = (sent[0:1] * CODE + sent[1:2]).astype(jnp.int32) - 1
 
 
-def place_rows(owner, position, obs_feat, n_owners, capacity):
-    rows, width = obs_feat.shape
-    return pl.pallas_call(
-        functools.partial(place_kernel, capacity),
+def place_codes(owner, position, time_embed, n_owners, capacity):
+    rows = owner.shape[0]
+    return pl.pallas_call(
+        code_kernel,
         out_shape=[
-            jax.ShapeDtypeStruct((n_owners, capacity, width), BF16),
             jax.ShapeDtypeStruct((n_owners, 1, capacity), jnp.int32),
+            jax.ShapeDtypeStruct(time_embed.shape, BF16),
         ],
         in_specs=[WHOLE] * 3,
         out_specs=[WHOLE] * 2,
-        compiler_params=params(24),
+        compiler_params=params(6),
+        cost_estimate=pl.CostEstimate(
+            flops=16 * rows * n_owners * capacity, bytes_accessed=8 * rows, transcendentals=0
+        ),
+        name="place_codes",
+    )(owner.reshape(1, rows), position.reshape(1, rows), time_embed)
+
+
+def place_kernel(owner_ref, feat_ref, out_ref):
+    n_owners, capacity, _ = out_ref.shape
+    owner = owner_ref[...]
+    rank = block_places(owner, n_owners)
+    feat = feat_ref[...]
+    for block in range(n_owners):
+        out_ref[block] = dot(one_hot_rows(owner, rank, block, capacity), feat).astype(BF16)
+
+
+def place_rows(owner, obs_feat, n_owners, capacity):
+    rows, width = obs_feat.shape
+    return pl.pallas_call(
+        place_kernel,
+        out_shape=jax.ShapeDtypeStruct((n_owners, capacity, width), BF16),
+        in_specs=[WHOLE] * 2,
+        out_specs=WHOLE,
+        compiler_params=params(12),
         cost_estimate=pl.CostEstimate(
             flops=2 * rows * width * n_owners * capacity,
             bytes_accessed=2 * width * (rows + n_owners * capacity),
             transcendentals=0,
         ),
         name="place_rows",
-    )(owner.reshape(1, rows), position.reshape(1, rows), obs_feat)
+    )(owner.reshape(1, rows), obs_feat)
 
 
 def pool_kernel(capacity, slot_dev, slot_ref, embed_ref, code_ref, got_ref, keep_ref, send_ref):
@@ -108,7 +139,7 @@
         out_shape=[half, half],
         in_specs=[SCALARS] + [WHOLE] * 3,
         out_specs=[WHOLE] * 2,
-        compiler_params=params(24),
+        compiler_params=params(12),
         cost_estimate=pl.CostEstimate(
             flops=2 * CB * slot_dev * got.size, bytes_accessed=2 * got.size, transcendentals=0
         ),
@@ -137,7 +168,7 @@
         out_shape=jax.ShapeDtypeStruct((rows, width), BF16),
         in_specs=[SCALARS] + [WHOLE] * 3,
         out_specs=WHOLE,
-        compiler_params=params(16),
+        compiler_params=params(10),
         cost_estimate=pl.CostEstimate(
             flops=2 * rows * width * (rows + width), bytes_accessed=4 * rows * width, transcendentals=0
         ),
@@ -251,7 +282,7 @@
             pltpu.VMEM((rows, heads_width), BF16),
             pltpu.VMEM((rows, width), F32),
         ],
-        compiler_params=params(36),
+        compiler_params=params(26),
         cost_estimate=pl.CostEstimate(
             flops=2 * rows * width * weights.shape[1],
             bytes_accessed=2 * weights.size + 6 * rows * width,
@@ -275,7 +306,7 @@
         out_shape=jax.ShapeDtypeStruct((rows, width), BF16),
         in_specs=[WHOLE] * 4,
         out_specs=WHOLE,
-        compiler_params=params(16),
+        compiler_params=params(10),
         cost_estimate=pl.CostEstimate(
             flops=2 * rows * width * width, bytes_accessed=10 * rows * width, transcendentals=0
         ),
@@ -371,17 +402,18 @@
     if n_slots == 2 and n_groups == 2 and n_cells == 4 and share % 16 == 0 and capacity % 16 == 0:
         order = arrival_order(width, n_share)
         below = along_cells(share_rows, -1)
-        blocks, codes = place_rows(owner, position, obs_feat, n_owners, capacity)
+        codes, embed = place_codes(owner, position, time_embed, n_owners, capacity)
         codes = lax.all_to_all(codes, ("cells", "mp"), split_axis=0, concat_axis=0, tiled=True)
         below, codes, share_rows = lax.optimization_barrier((below, codes, share_rows))
         first = to_other_places(below)
+        blocks = place_rows(owner, obs_feat, n_owners, capacity)
         above, opposite = along_cells(share_rows, 1), along_cells(below, -1)
         blocks, above, opposite, first = lax.optimization_barrier((blocks, above, opposite, first))
         second = to_other_places(jnp.concatenate([above, opposite], axis=0))
         weights = put_rows([side_by_side(*local_weights)] + first, width, 0)
         got = lax.all_to_all(blocks, ("cells", "mp"), split_axis=0, concat_axis=0, tiled=True)
         got, weights = lax.optimization_barrier((got, weights))
-        keep, send = pool_rows(my_slot.reshape(1), time_embed, codes, got, capacity, slot_dev)
+        keep, send = pool_rows(my_slot.reshape(1), embed, codes, got, capacity, slot_dev)
         send, second = lax.optimization_barrier((send, second))
         other = lax.ppermute(send, "slots", [(0, 1), (1, 0)])
         weights = put_rows(second, width, width // 2, weights)

time: 154 us -> 154 us (level)
  blocking collectives: 11.5 us -> 14.1 us
  waiting for transfers between devices: 68.1 us -> 65.9 us
    all_to_all x1, blocking collectives: 11.5 us -> 14.1 us  [on_device(): lax.all_to_all(codes, ('cells', 'mp'), split_axis=0, concat_axis=0, tiled...]
    ppermute x3, waiting for transfers between devices: 21.8 us -> 19.6 us  [along_cells(): lax.ppermute(values, 'cells', [(j, (j - distance) % n_cells) for j in ran...]
    unnamed x54 -> x58, local copies, waits for them, and re-layouts: 24.2 us -> 23.4 us
    pallas_call x1 -> x2, Pallas kernels: 3.33 us -> 3.69 us  [the longest x1 2.98 us: place_rows(): pl.pallas_call(place_kernel, out_shape=jax.ShapeDtypeStruct((n_owners, ca...]
where the time goes in v10:
time: 154 us
  waiting for transfers between devices  65.9 us (43%)
  local copies, waits for them, and re-layouts  27.4 us (18%)
  Pallas kernels  27.4 us (18%)
  starting transfers between devices  17.7 us (11%)
  blocking collectives  14.1 us (9%)
    all_to_all x1, waiting for transfers between devices, on_device(): lax.all_to_all(blocks, ('cells', 'mp'), split_axis=0, concat_axis=0, tile...  41.7 us
    unnamed x58, local copies, waits for them, and re-layouts  23.4 us
    ppermute x3, waiting for transfers between devices, along_cells(): lax.ppermute(values, 'cells', [(j, (j - distance) % n_cells) for j in ran...  19.6 us
    pallas_call x2, Pallas kernels, layer(): pl.pallas_call(functools.partial(layer_kernel, hidden_width), out_shape=j...  14.5 us
    all_to_all x1, blocking collectives, on_device(): lax.all_to_all(codes, ('cells', 'mp'), split_axis=0, concat_axis=0, tiled...  14.1 us
    ppermute x6, starting transfers between devices, to_other_places(): places.append(lax.ppermute(shares, ('groups', 'slots'), pairs))  7.04 us
    ppermute x3, starting transfers between devices, along_cells(): lax.ppermute(values, 'cells', [(j, (j - distance) % n_cells) for j in ran...  5.1 us
    all_to_all x1, starting transfers between devices, on_device(): lax.all_to_all(blocks, ('cells', 'mp'), split_axis=0, concat_axis=0, tile...  4.82 us
  transfers between devices with their start and end apart: 13, of which 6 were waited for; matrix products, arithmetic and copies ran while one was open for 2% of the time, Pallas kernels for 11%

profile of v10, /device:TPU:0, one launch (start us, length us, event | category | flops | bytes accessed | tf_op | source)
XLA Modules:
  0.0 153.8 jit_solution(16130858666553594506)
XLA Ops:
  0.0 1.2 constant_dynamic-slice_fusion
  1.3 1.0 dynamic-slice_bitcast_fusion.1
  2.3 0.9 dynamic-slice_bitcast_fusion
  3.2 0.8 dynamic-slice_bitcast_fusion.2
  4.0 3.1 %collective-permute-start = (bf16[48,6144]{1,0:T(8,128)(2,1)S(1)}, bf16[48,6144]{1,0:T(8,128)(2,1)S(1)}, u32[]{:S(2)}, u32[]{:S(2)}) collective-permute-start(bf16[48,6144]{1,0:T(8,128)(2,1)S(1)} %pad_maximum_fusion.1), channel_id=1, source_target_pairs={{0,4},{4,8},{8,12},{12,0},{1,5},{5,9},{9,13},{13,1},{2,6},{6,10},{... | collective-permute-start | bytes 1769480 | tf_op jit(solution)/shard_map/ppermute | solution.py:324
  7.8 0.7 place_codes.1
  8.5 14.1 %all_to_all.10.code_ref = s32[8,1,192]{2,1,0:T(1,128)S(1)} all-to-all(s32[8,1,192]{2,1,0:T(1,128)S(1)} %get-tuple-element.29), channel_id=1, replica_groups=mesh['groups'=2,'cells'=4,'slots'=2,'mp'=2] {'cells','mp'}, dimensions={0} | all-to-all | bytes 12288 | tf_op jit(solution)/shard_map/all_to_all | solution.py:406
  22.7 1.7 %collective-permute-start.1 = (bf16[48,6144]{1,0:T(8,128)(2,1)S(1)}, bf16[48,6144]{1,0:T(8,128)(2,1)S(1)}, u32[]{:S(2)}, u32[]{:S(2)}) collective-permute-start(bf16[48,6144]{1,0:T(8,128)(2,1)S(1)} %pad_maximum_fusion.1), channel_id=1, source_target_pairs={{0,12},{4,0},{8,4},{12,8},{1,13},{5,1},{9,5},{13,9},{2,14},{6,2},{... | collective-permute-start | bytes 1769480 | tf_op jit(solution)/shard_map/ppermute | solution.py:324
  24.4 0.3 collective-permute-start.2
  24.7 1.5 collective-permute-start.3
  26.2 1.5 collective-permute-start.4
  27.7 0.5 collective-permute-start.5
  28.2 3.0 %place_rows.1 = bf16[8,192,768]{2,1,0:T(8,128)(2,1)} custom-call(s32[1,512]{1,0:T(1,128)S(1)} %bitcast.22, bf16[512,768]{1,0:T(8,128)(2,1)S(1)} %copy-done.13), custom_call_target="tpu_custom_call" | custom-call | flops 1207959552 | bytes 3145728 | tf_op jit(solution)/shard_map/place_rows/pallas_call | solution.py:97
  31.2 7.4 %collective-permute-done.1 = bf16[48,6144]{1,0:T(8,128)(2,1)S(1)} collective-permute-done((bf16[48,6144]{1,0:T(8,128)(2,1)S(1)}, bf16[48,6144]{1,0:T(8,128)(2,1)S(1)}, u32[]{:S(2)}, u32[]{:S(2)}) %collective-permute-start.1) | collective-permute-done | bytes 589856 | tf_op jit(solution)/shard_map/ppermute | solution.py:324
  38.6 12.1 %collective-permute-done.2 = bf16[48,6144]{1,0:T(8,128)(2,1)S(1)} collective-permute-done((bf16[48,6144]{1,0:T(8,128)(2,1)S(1)}, bf16[48,6144]{1,0:T(8,128)(2,1)S(1)}, u32[]{:S(2)}, u32[]{:S(2)}) %collective-permute-start.2) | collective-permute-done | bytes 589856 | tf_op jit(solution)/shard_map/ppermute | solution.py:324
  50.8 0.9 copy-done.7
  51.6 1.6 %collective-permute-done.4.refs_3_ = bf16[48,6144]{1,0:T(8,128)(2,1)S(1)} collective-permute-done((bf16[48,6144]{1,0:T(8,128)(2,1)S(1)}, bf16[48,6144]{1,0:T(8,128)(2,1)S(1)}, u32[]{:S(2)}, u32[]{:S(2)}) %collective-permute-start.4) | collective-permute-done | bytes 589856 | tf_op jit(solution)/shard_map/ppermute | solution.py:333
  53.2 0.8 copy-done.9
  54.1 0.8 copy-done.11
  54.9 4.8 %all-to-all-start.1 = ((bf16[8,192,768]{2,1,0:T(8,128)(2,1)}), bf16[8,192,768]{2,1,0:T(8,128)(2,1)S(1)}, u32[]{:S(2)}, u32[]{:S(2)}) async-start(bf16[8,192,768]{2,1,0:T(8,128)(2,1)} %place_rows.1), calls=%async_computation.1 | async-start | bytes 4718592 | tf_op jit(solution)/shard_map/all_to_all | solution.py:414
  59.7 1.2 constant_dynamic-update-slice_fusion.1
  60.9 1.1 constant_dynamic-update-slice_fusion.refs_0_
  62.0 0.5 collective-permute-start.6
  62.5 1.7 %collective-permute-start.7 = (bf16[96,6144]{1,0:T(8,128)(2,1)S(1)}, bf16[96,6144]{1,0:T(8,128)(2,1)}, u32[]{:S(2)}, u32[]{:S(2)}) collective-permute-start(bf16[96,6144]{1,0:T(8,128)(2,1)S(1)} %constant_dynamic-update-slice_fusion.refs_0_), channel_id=1, source_target_pairs={{0,16},{2,18},{16,0},{18,2},{1,17},{3,19},{17,1},{19,3},{4,20},{6,... | collective-permute-start | bytes 3538952 | tf_op jit(solution)/shard_map/ppermute | solution.py:333
  64.2 1.4 collective-permute-start.8
  65.7 0.9 copy-done.21
  66.8 0.2 pad_maximum_fusion.refs_0_
  67.1 0.8 copy-done.6
  68.1 0.2 copy-done.10
  68.2 0.2 copy-done.12
  68.4 0.7 put_rows.2.refs_4_
  69.1 3.6 %copy-done = bf16[768,6144]{1,0:T(8,128)(2,1)} copy-done((bf16[768,6144]{1,0:T(8,128)(2,1)}, bf16[768,6144]{1,0:T(8,128)(2,1)S(1)}, u32[]{:S(2)}) %copy-start) | copy-done | bytes 9437208
  72.7 41.7 %all-to-all-done.1.got_ref = bf16[8,192,768]{2,1,0:T(8,128)(2,1)S(1)} async-done(((bf16[8,192,768]{2,1,0:T(8,128)(2,1)}), bf16[8,192,768]{2,1,0:T(8,128)(2,1)S(1)}, u32[]{:S(2)}, u32[]{:S(2)}) %all-to-all-start.1) | async-done | bytes 2359328 | tf_op jit(solution)/shard_map/all_to_all | solution.py:414
  114.4 0.7 copy-done.16
  115.1 2.8 %pool_rows.1 = (bf16[256,768]{1,0:T(8,128)(2,1)S(1)}, bf16[256,768]{1,0:T(8,128)(2,1)}) custom-call(s32[1]{0:T(128)} %bitcast.slot_ref, bf16[8,768]{1,0:T(8,128)(2,1)S(1)} %copy-done.16, s32[8,1,192]{2,1,0:T(1,128)S(1)} %all_to_all.10.code_ref, bf16[8,192,768]{2,1,0:T(8,128)(2,1)S(1)} %all-to-all-done.1.got_ref), custom_call_target="tpu_custom_call" | custom-call | flops 1207959552 | bytes 2359296 | tf_op jit(solution)/shard_map/pool_rows/pallas_call | solution.py:137
  118.0 0.7 copy-done.17
  118.7 0.5 collective-permute-start.9
  119.2 3.7 %copy-done.1 = bf16[768,6144]{1,0:T(8,128)(2,1)S(1)} copy-done((bf16[768,6144]{1,0:T(8,128)(2,1)S(1)}, bf16[768,6144]{1,0:T(8,128)(2,1)}, u32[]{:S(2)}) %copy-start.1) | copy-done | bytes 9437208
  122.9 2.4 %put_rows.3.w_ref = bf16[768,6144]{1,0:T(8,128)(2,1)S(1)} custom-call(bf16[96,6144]{1,0:T(8,128)(2,1)S(1)} %constant_dynamic-update-slice_fusion.refs_0_, bf16[96,6144]{1,0:T(8,128)(2,1)} %collective-permute-done.6.refs_1_, bf16[96,6144]{1,0:T(8,128)(2,1)} %collective-permute-done.7.refs_2_, ...), custom_call_target="tpu_custom_call", output_to_operand_aliasing={{}: (4, {})} | custom-call | bytes 9437184 | tf_op jit(solution)/shard_map/put_rows/pallas_call | solution.py:238
  125.3 3.6 %copy-done.2 = bf16[768,6144]{1,0:T(8,128)(2,1)} copy-done((bf16[768,6144]{1,0:T(8,128)(2,1)}, bf16[768,6144]{1,0:T(8,128)(2,1)S(1)}, u32[]{:S(2)}) %copy-start.2) | copy-done | bytes 9437208
  129.0 0.8 collective-permute-done.9.got_ref
  129.8 1.5 weave_steps.1.tok_ref
  131.3 2.3 %collective-permute-done.10.tok_ref = bf16[512,768]{1,0:T(8,128)(2,1)S(1)} collective-permute-done((bf16[512,768]{1,0:T(8,128)(2,1)S(1)}, bf16[512,768]{1,0:T(8,128)(2,1)S(1)}, u32[]{:S(2)}, u32[]{:S(2)}) %collective-permute-start.10) | collective-permute-done | bytes 786464 | tf_op jit(solution)/shard_map/ppermute | solution.py:429
  133.6 3.7 %copy-done.3 = bf16[768,6144]{1,0:T(8,128)(2,1)S(1)} copy-done((bf16[768,6144]{1,0:T(8,128)(2,1)S(1)}, bf16[768,6144]{1,0:T(8,128)(2,1)}, u32[]{:S(2)}) %copy-start.3) | copy-done | bytes 9437208
  137.3 7.3 %layer.3 = bf16[512,768]{1,0:T(8,128)(2,1)S(1)} custom-call(bf16[512,768]{1,0:T(8,128)(2,1)S(1)} %collective-permute-done.10.tok_ref, bf16[768,6144]{1,0:T(8,128)(2,1)S(1)} %copy-done.3), custom_call_target="tpu_custom_call" | custom-call | flops 4831838208 | bytes 11796480 | tf_op jit(solution)/shard_map/layer/pallas_call | solution.py:275
  144.5 0.2 collective-permute-start.11
  144.7 7.3 %layer.2.sum_ref = f32[512,768]{1,0:T(8,128)S(1)} custom-call(bf16[512,768]{1,0:T(8,128)(2,1)S(1)} %weave_steps.1.tok_ref, bf16[768,6144]{1,0:T(8,128)(2,1)S(1)} %copy-done.4), custom_call_target="tpu_custom_call" | custom-call | flops 4831838208 | bytes 11796480 | tf_op jit(solution)/shard_map/layer/pallas_call | solution.py:275
  152.0 1.8 %finish.1 = bf16[512,768]{1,0:T(8,128)(2,1)} custom-call(bf16[512,768]{1,0:T(8,128)(2,1)S(1)} %weave_steps.1.tok_ref, f32[512,768]{1,0:T(8,128)S(1)} %layer.2.sum_ref, bf16[512,768]{1,0:T(8,128)(2,1)S(1)} %collective-permute-done.11.got_ref, s32[1,768]{1,0:T(1,128)S(1)} %compare_select_fusion.6.order_ref), custom_call_target="tpu_custom_call" | custom-call | flops 603979776 | bytes 3932160 | tf_op jit(solution)/shard_map/finish/pallas_call | solution.py:304
  (56 shorter events, 0.8 us)
Async XLA Ops:
  1.2 6.6 %copy-start.25 = (s32[512]{0:T(512)S(1)}, s32[512]{0:T(512)}, u32[]{:S(2)}) copy-start(s32[512]{0:T(512)} %param.11) | copy-start | bytes 6148
  1.2 6.6 %copy-start.26 = (s32[512]{0:T(512)S(1)}, s32[512]{0:T(512)}, u32[]{:S(2)}) copy-start(s32[512]{0:T(512)} %param.10) | copy-start | bytes 6148
  1.2 6.6 %copy-start.14 = (bf16[8,768]{1,0:T(8,128)(2,1)S(1)}, bf16[8,768]{1,0:T(8,128)(2,1)}, u32[]{:S(2)}) copy-start(bf16[8,768]{1,0:T(8,128)(2,1)} %time_ref.1) | copy-start | bytes 36868
  1.2 26.9 %copy-start.13 = (bf16[512,768]{1,0:T(8,128)(2,1)S(1)}, bf16[512,768]{1,0:T(8,128)(2,1)}, u32[]{:S(2)}) copy-start(bf16[512,768]{1,0:T(8,128)(2,1)} %feat_ref.1) | copy-start | bytes 2359300
  4.0 18.6 %collective-permute-start = (bf16[48,6144]{1,0:T(8,128)(2,1)S(1)}, bf16[48,6144]{1,0:T(8,128)(2,1)S(1)}, u32[]{:S(2)}, u32[]{:S(2)}) collective-permute-start(bf16[48,6144]{1,0:T(8,128)(2,1)S(1)} %pad_maximum_fusion.1), channel_id=1, source_target_pairs={{0,4},{4,8},{8,12},{12,0},{1,5},{5,9},{9,13},{13,1},{2,6},{6,10},{... | collective-permute-start | bytes 1769480 | tf_op jit(solution)/shard_map/ppermute | solution.py:324
  8.5 17.6 %copy-start.15 = (bf16[8,768]{1,0:T(8,128)(2,1)}, bf16[8,768]{1,0:T(8,128)(2,1)S(1)}, u32[]{:S(2)}) copy-start(bf16[8,768]{1,0:T(8,128)(2,1)S(1)} %get-tuple-element.28.embed_ref) | copy-start | bytes 36868
  22.7 8.5 %copy-start.5 = (bf16[48,6144]{1,0:T(8,128)(2,1)}, bf16[48,6144]{1,0:T(8,128)(2,1)S(1)}, u32[]{:S(2)}) copy-start(bf16[48,6144]{1,0:T(8,128)(2,1)S(1)} %collective-permute-done.refs_1_) | copy-start | bytes 1769476
  22.7 16.0 %collective-permute-start.1 = (bf16[48,6144]{1,0:T(8,128)(2,1)S(1)}, bf16[48,6144]{1,0:T(8,128)(2,1)S(1)}, u32[]{:S(2)}, u32[]{:S(2)}) collective-permute-start(bf16[48,6144]{1,0:T(8,128)(2,1)S(1)} %pad_maximum_fusion.1), channel_id=1, source_target_pairs={{0,12},{4,0},{8,4},{12,8},{1,13},{5,1},{9,5},{13,9},{2,14},{6,2},{... | collective-permute-start | bytes 1769480 | tf_op jit(solution)/shard_map/ppermute | solution.py:324
  24.4 26.4 %collective-permute-start.2 = (bf16[48,6144]{1,0:T(8,128)(2,1)S(1)}, bf16[48,6144]{1,0:T(8,128)(2,1)S(1)}, u32[]{:S(2)}, u32[]{:S(2)}) collective-permute-start(bf16[48,6144]{1,0:T(8,128)(2,1)S(1)} %collective-permute-done.refs_1_), channel_id=1, source_target_pairs={{0,4},{4,8},{8,12},{12,0},{1,5},{5,9},{9,13},{13,1},{2,6},{6,10},{... | collective-permute-start | bytes 1769480 | tf_op jit(solution)/shard_map/ppermute | solution.py:324
  24.7 26.1 %collective-permute-start.3 = (bf16[48,6144]{1,0:T(8,128)(2,1)S(1)}, bf16[48,6144]{1,0:T(8,128)(2,1)S(1)}, u32[]{:S(2)}, u32[]{:S(2)}) collective-permute-start(bf16[48,6144]{1,0:T(8,128)(2,1)S(1)} %collective-permute-done.refs_1_), channel_id=1, source_target_pairs={{0,2},{2,0},{16,18},{18,16},{1,3},{3,1},{17,19},{19,17},{4,6},{6,4... | collective-permute-start | bytes 1769480 | tf_op jit(solution)/shard_map/ppermute | solution.py:333
  26.2 27.1 %collective-permute-start.4 = (bf16[48,6144]{1,0:T(8,128)(2,1)S(1)}, bf16[48,6144]{1,0:T(8,128)(2,1)S(1)}, u32[]{:S(2)}, u32[]{:S(2)}) collective-permute-start(bf16[48,6144]{1,0:T(8,128)(2,1)S(1)} %collective-permute-done.refs_1_), channel_id=1, source_target_pairs={{0,16},{2,18},{16,0},{18,2},{1,17},{3,19},{17,1},{19,3},{4,20},{6,... | collective-permute-start | bytes 1769480 | tf_op jit(solution)/shard_map/ppermute | solution.py:333
  27.7 26.4 %collective-permute-start.5 = (bf16[48,6144]{1,0:T(8,128)(2,1)S(1)}, bf16[48,6144]{1,0:T(8,128)(2,1)S(1)}, u32[]{:S(2)}, u32[]{:S(2)}) collective-permute-start(bf16[48,6144]{1,0:T(8,128)(2,1)S(1)} %collective-permute-done.refs_1_), channel_id=1, source_target_pairs={{0,18},{2,16},{16,2},{18,0},{1,19},{3,17},{17,3},{19,1},{4,22},{6,... | collective-permute-start | bytes 1769480 | tf_op jit(solution)/shard_map/ppermute | solution.py:333
  38.6 14.6 %copy-start.22 = (bf16[48,6144]{1,0:T(8,128)(2,1)}, bf16[48,6144]{1,0:T(8,128)(2,1)S(1)}, u32[]{:S(2)}) copy-start(bf16[48,6144]{1,0:T(8,128)(2,1)S(1)} %collective-permute-done.1) | copy-start | bytes 1769476
  50.7 2.5 %copy-start.23 = (bf16[48,6144]{1,0:T(8,128)(2,1)}, bf16[48,6144]{1,0:T(8,128)(2,1)S(1)}, u32[]{:S(2)}) copy-start(bf16[48,6144]{1,0:T(8,128)(2,1)S(1)} %collective-permute-done.2) | copy-start | bytes 1769476
  50.8 0.9 copy-start.7
  53.2 0.8 copy-start.9
  54.1 0.8 copy-start.11
  54.9 59.5 %all-to-all-start.1 = ((bf16[8,192,768]{2,1,0:T(8,128)(2,1)}), bf16[8,192,768]{2,1,0:T(8,128)(2,1)S(1)}, u32[]{:S(2)}, u32[]{:S(2)}) async-start(bf16[8,192,768]{2,1,0:T(8,128)(2,1)} %place_rows.1), calls=%async_computation.1 | async-start | bytes 4718592 | tf_op jit(solution)/shard_map/all_to_all | solution.py:414
  59.7 5.9 %copy-start.19 = (bf16[192,2,1536]{2,1,0:T(2,128)(2,1)S(1)}, bf16[192,2,1536]{2,1,0:T(2,128)(2,1)}, u32[]{:S(2)}) copy-start(bf16[192,2,1536]{2,1,0:T(2,128)(2,1)} %param.16) | copy-start | bytes 3538948
  62.0 56.7 %collective-permute-start.6 = (bf16[96,6144]{1,0:T(8,128)(2,1)S(1)}, bf16[96,6144]{1,0:T(8,128)(2,1)}, u32[]{:S(2)}, u32[]{:S(2)}) collective-permute-start(bf16[96,6144]{1,0:T(8,128)(2,1)S(1)} %constant_dynamic-update-slice_fusion.refs_0_), channel_id=1, source_target_pairs={{0,2},{2,0},{16,18},{18,16},{1,3},{3,1},{17,19},{19,17},{4,6},{6,4... | collective-permute-start | bytes 3538952 | tf_op jit(solution)/shard_map/ppermute | solution.py:333
  62.5 56.2 %collective-permute-start.7 = (bf16[96,6144]{1,0:T(8,128)(2,1)S(1)}, bf16[96,6144]{1,0:T(8,128)(2,1)}, u32[]{:S(2)}, u32[]{:S(2)}) collective-permute-start(bf16[96,6144]{1,0:T(8,128)(2,1)S(1)} %constant_dynamic-update-slice_fusion.refs_0_), channel_id=1, source_target_pairs={{0,16},{2,18},{16,0},{18,2},{1,17},{3,19},{17,1},{19,3},{4,20},{6,... | collective-permute-start | bytes 3538952 | tf_op jit(solution)/shard_map/ppermute | solution.py:333
  64.2 54.6 %collective-permute-start.8 = (bf16[96,6144]{1,0:T(8,128)(2,1)S(1)}, bf16[96,6144]{1,0:T(8,128)(2,1)}, u32[]{:S(2)}, u32[]{:S(2)}) collective-permute-start(bf16[96,6144]{1,0:T(8,128)(2,1)S(1)} %constant_dynamic-update-slice_fusion.refs_0_), channel_id=1, source_target_pairs={{0,18},{2,16},{16,2},{18,0},{1,19},{3,17},{17,3},{19,1},{4,22},{6,... | collective-permute-start | bytes 3538952 | tf_op jit(solution)/shard_map/ppermute | solution.py:333
  65.6 1.0 copy-start.21
  65.6 1.2 copy-start.20
  65.6 1.2 copy-start.24
  66.8 1.1 copy-start.6
  66.8 1.2 copy-start.8
  66.8 1.4 copy-start.10
  66.8 1.6 %copy-start.12 = (bf16[48,6144]{1,0:T(8,128)(2,1)S(1)}, bf16[48,6144]{1,0:T(8,128)(2,1)}, u32[]{:S(2)}) copy-start(bf16[48,6144]{1,0:T(8,128)(2,1)} %copy-done.11) | copy-start | bytes 1769476
  69.1 3.6 %copy-start = (bf16[768,6144]{1,0:T(8,128)(2,1)}, bf16[768,6144]{1,0:T(8,128)(2,1)S(1)}, u32[]{:S(2)}) copy-start(bf16[768,6144]{1,0:T(8,128)(2,1)S(1)} %put_rows.2.refs_4_) | copy-start | bytes 28311556
  114.4 0.7 copy-start.16
  118.0 0.7 copy-start.17
  118.7 11.0 %collective-permute-start.9 = (bf16[256,768]{1,0:T(8,128)(2,1)}, bf16[256,768]{1,0:T(8,128)(2,1)S(1)}, u32[]{:S(2)}, u32[]{:S(2)}) collective-permute-start(bf16[256,768]{1,0:T(8,128)(2,1)} %get-tuple-element.43), channel_id=1, source_target_pairs={{0,2},{2,0},{1,3},{3,1},{4,6},{6,4},{5,7},{7,5},{8,10},{10,8},{9,1... | collective-permute-start | bytes 1179656 | tf_op jit(solution)/shard_map/ppermute | solution.py:418
  119.2 3.7 %copy-start.1 = (bf16[768,6144]{1,0:T(8,128)(2,1)S(1)}, bf16[768,6144]{1,0:T(8,128)(2,1)}, u32[]{:S(2)}) copy-start(bf16[768,6144]{1,0:T(8,128)(2,1)} %copy-done) | copy-start | bytes 28311556
  122.9 6.9 %copy-start.18 = (bf16[256,768]{1,0:T(8,128)(2,1)S(1)}, bf16[256,768]{1,0:T(8,128)(2,1)}, u32[]{:S(2)}) copy-start(bf16[256,768]{1,0:T(8,128)(2,1)} %copy-done.17) | copy-start | bytes 1179652
  125.3 3.6 %copy-start.2 = (bf16[768,6144]{1,0:T(8,128)(2,1)}, bf16[768,6144]{1,0:T(8,128)(2,1)S(1)}, u32[]{:S(2)}) copy-start(bf16[768,6144]{1,0:T(8,128)(2,1)S(1)} %put_rows.3.w_ref) | copy-start | bytes 28311556
  131.2 2.4 %collective-permute-start.10 = (bf16[512,768]{1,0:T(8,128)(2,1)S(1)}, bf16[512,768]{1,0:T(8,128)(2,1)S(1)}, u32[]{:S(2)}, u32[]{:S(2)}) collective-permute-start(bf16[512,768]{1,0:T(8,128)(2,1)S(1)} %weave_steps.1.tok_ref), channel_id=1, source_target_pairs={{0,1},{1,0},{2,3},{3,2},{4,5},{5,4},{6,7},{7,6},{8,9},{9,8},{10,11... | collective-permute-start | bytes 2359304 | tf_op jit(solution)/shard_map/ppermute | solution.py:429
  133.6 3.7 %copy-start.3 = (bf16[768,6144]{1,0:T(8,128)(2,1)S(1)}, bf16[768,6144]{1,0:T(8,128)(2,1)}, u32[]{:S(2)}) copy-start(bf16[768,6144]{1,0:T(8,128)(2,1)} %copy-done.2) | copy-start | bytes 28311556
  137.3 7.5 %copy-start.4 = (bf16[768,6144]{1,0:T(8,128)(2,1)S(1)}, bf16[768,6144]{1,0:T(8,128)(2,1)}, u32[]{:S(2)}) copy-start(bf16[768,6144]{1,0:T(8,128)(2,1)} %copy-done.2) | copy-start | bytes 28311556
  144.5 7.5 %collective-permute-start.11 = (bf16[512,768]{1,0:T(8,128)(2,1)S(1)}, bf16[512,768]{1,0:T(8,128)(2,1)S(1)}, u32[]{:S(2)}, u32[]{:S(2)}) collective-permute-start(bf16[512,768]{1,0:T(8,128)(2,1)S(1)} %layer.3), channel_id=1, source_target_pairs={{0,1},{1,0},{2,3},{3,2},{4,5},{5,4},{6,7},{7,6},{8,9},{9,8},{10,11... | collective-permute-start | bytes 2359304 | tf_op jit(solution)/shard_map/ppermute | solution.py:431

commit v11 on v10

--- a/solution.py
+++ b/solution.py
@@ -242,7 +242,7 @@
         out_specs=pl.BlockSpec(memory_space=pl.ANY),
         scratch_shapes=[pltpu.SemaphoreType.DMA((len(pieces),))],
         input_output_aliases={} if into is None else {len(pieces): 0},
-        compiler_params=params(2),
+        compiler_params=params(56),
         cost_estimate=pl.CostEstimate(
             flops=0, bytes_accessed=4 * sum(piece.size for piece in pieces), transcendentals=0
         ),
@@ -250,39 +250,54 @@
     )(*operands)
 
 
-def layer_kernel(hidden_width, tok_ref, w_ref, out_ref, norm_ref, ctx_ref, acc_ref):
-    heads_width = ctx_ref.shape[1]
+def layer_kernel(sections, tok_ref, far_ref, out_ref, w_ref, norm_ref, ctx_ref, acc_ref, sems):
+    copies = [
+        pltpu.make_async_copy(far_ref.at[:, pl.ds(at, size)], w_ref.at[:, pl.ds(at, size)], sems.at[number])
+        for number, (at, size) in enumerate(sections)
+    ]
+    for copy in copies:
+        copy.start()
+
+    def columns(number):
+        copies[number].wait()
+        at, size = sections[number]
+        return w_ref[:, at : at + size]
+
+    tokens = tok_ref[...].astype(F32)
+    scale = lax.rsqrt(jnp.mean(tokens * tokens, axis=1, keepdims=True) + EPS)
+    norm_ref[...] = (tokens * scale).astype(BF16)
+    attention(norm_ref[...], columns(0), ctx_ref.shape[1], ctx_ref)
+    acc_ref[...] = dot_t(ctx_ref[...], columns(1))
+    for at in range(2, len(sections), 3):
+        add = gated(norm_ref[...], columns(at), columns(at + 1), columns(at + 2))
+        if at + 3 < len(sections):
+            acc_ref[...] += add
+        else:
+            out_ref[...] = (acc_ref[...] + add).astype(out_ref.dtype)
+
+
+def layer(tokens, weights, heads_width, hidden_width, out_type):
+    rows, width = tokens.shape
     gate_at = 3 * heads_width
     up_at = gate_at + hidden_width
     out_at = up_at + hidden_width
     down_at = out_at + heads_width
-    tokens = tok_ref[...].astype(F32)
-    scale = lax.rsqrt(jnp.mean(tokens * tokens, axis=1, keepdims=True) + EPS)
-    norm_ref[...] = (tokens * scale).astype(BF16)
-    attention(norm_ref[...], w_ref[:, :gate_at], heads_width, ctx_ref)
-    acc_ref[...] = dot_t(ctx_ref[...], w_ref[:, out_at:down_at])
+    sections = [(0, gate_at), (out_at, heads_width)]
     for begin in range(0, hidden_width, UNIT):
-        gate_w, up_w, down_w = [w_ref[:, at + begin : at + begin + UNIT] for at in (gate_at, up_at, down_at)]
-        add = gated(norm_ref[...], gate_w, up_w, down_w)
-        if begin + UNIT < hidden_width:
-            acc_ref[...] += add
-        else:
-            out_ref[...] = (acc_ref[...] + add).astype(out_ref.dtype)
-
-
-def layer(tokens, weights, heads_width, hidden_width, out_type):
-    rows, width = tokens.shape
-    return pl.pallas_call(
-        functools.partial(layer_kernel, hidden_width),
+        sections += [(at + begin, UNIT) for at in (gate_at, up_at, down_at)]
+    return pl.pallas_call(
+        functools.partial(layer_kernel, sections),
         out_shape=jax.ShapeDtypeStruct((rows, width), out_type),
-        in_specs=[WHOLE] * 2,
+        in_specs=[WHOLE, pl.BlockSpec(memory_space=pl.ANY)],
         out_specs=WHOLE,
         scratch_shapes=[
+            pltpu.VMEM(weights.shape, BF16),
             pltpu.VMEM((rows, width), BF16),
             pltpu.VMEM((rows, heads_width), BF16),
             pltpu.VMEM((rows, width), F32),
+            pltpu.SemaphoreType.DMA((len(sections),)),
         ],
-        compiler_params=params(26),
+        compiler_params=params(56),
         cost_estimate=pl.CostEstimate(
             flops=2 * rows * width * weights.shape[1],
             bytes_accessed=2 * weights.size + 6 * rows * width,

time: 154 us -> 392 us (2.55)
  Pallas kernels: 27.4 us -> 322 us
  waiting for transfers between devices: 65.9 us -> 24.4 us
  local copies, waits for them, and re-layouts: 27.4 us -> 10.5 us
    pallas_call x2, Pallas kernels: 3.12 us -> 288 us  [put_rows(): pl.pallas_call(functools.partial(put_rows_kernel, firsts), out_shape=jax....]
    all_to_all x1, waiting for transfers between devices: 41.7 us -> 0.01 us  [on_device(): lax.all_to_all(blocks, ('cells', 'mp'), split_axis=0, concat_axis=0, tile...]
    unnamed x58 -> x38, local copies, waits for them, and re-layouts: 23.4 us -> 7.24 us
    pallas_call x2, Pallas kernels: 14.5 us -> 25.1 us  [layer(): pl.pallas_call(functools.partial(layer_kernel, sections), out_shape=jax.S...]
  transfers between devices with their start and end apart: 13 -> 13, of which waited for: 6 -> 4; matrix products, arithmetic and copies ran while one was open for 2% -> 2% of each run, Pallas kernels for 11% -> 78%
where the time goes in v11:
time: 392 us
  Pallas kernels  322 us (82%)
  waiting for transfers between devices  24.4 us (6%)
  starting transfers between devices  17.8 us (5%)
  blocking collectives  14.1 us (4%)
  local copies, waits for them, and re-layouts  10.5 us (3%)
    pallas_call x2, Pallas kernels, put_rows(): pl.pallas_call(functools.partial(put_rows_kernel, firsts), out_shape=jax....  288 us
    pallas_call x2, Pallas kernels, layer(): pl.pallas_call(functools.partial(layer_kernel, sections), out_shape=jax.S...  25.1 us
    ppermute x3, waiting for transfers between devices, along_cells(): lax.ppermute(values, 'cells', [(j, (j - distance) % n_cells) for j in ran...  19.6 us
    all_to_all x1, blocking collectives, on_device(): lax.all_to_all(codes, ('cells', 'mp'), split_axis=0, concat_axis=0, tiled...  14.1 us
  transfers between devices with their start and end apart: 13, of which 4 were waited for; matrix products, arithmetic and copies ran while one was open for 2% of the time, Pallas kernels for 78%

profile of v11, /device:TPU:0, one launch (start us, length us, event | category | flops | bytes accessed | tf_op | source)
XLA Modules:
  0.0 391.8 jit_solution(16349341641992483731)
XLA Ops:
  0.0 1.2 constant_dynamic-slice_fusion
  1.2 0.0 copy-start.14
  1.3 0.0 copy-start.15
  1.3 0.0 copy-start.4
  1.3 0.0 copy-start.3
  1.3 1.0 dynamic-slice_bitcast_fusion.1
  2.5 3.1 collective-permute-start
  6.3 0.7 place_codes.1
  7.0 14.1 %all_to_all.10.code_ref = s32[8,1,192]{2,1,0:T(1,128)S(1)} all-to-all(s32[8,1,192]{2,1,0:T(1,128)S(1)} %get-tuple-element.29), channel_id=1, replica_groups=mesh['groups'=2,'cells'=4,'slots'=2,'mp'=2] {'cells','mp'}, dimensions={0} | all-to-all | bytes 12288 | tf_op jit(solution)/shard_map/all_to_all | solution.py:421
  21.1 0.0 collective-permute-done.refs_1_
  21.1 1.7 collective-permute-start.1
  22.8 0.3 collective-permute-start.2
  23.1 1.5 collective-permute-start.3
  24.6 1.5 collective-permute-start.4
  26.1 0.5 collective-permute-start.5
  26.6 3.0 place_rows.1
  29.6 7.4 %collective-permute-done.1 = bf16[48,6144]{1,0:T(8,128)(2,1)S(1)} collective-permute-done((bf16[48,6144]{1,0:T(8,128)(2,1)S(1)}, bf16[48,6144]{1,0:T(8,128)(2,1)S(1)}, u32[]{:S(2)}, u32[]{:S(2)}) %collective-permute-start.1) | collective-permute-done | bytes 589856 | tf_op jit(solution)/shard_map/ppermute | solution.py:339
  37.0 12.1 %collective-permute-done.2 = bf16[48,6144]{1,0:T(8,128)(2,1)S(1)} collective-permute-done((bf16[48,6144]{1,0:T(8,128)(2,1)S(1)}, bf16[48,6144]{1,0:T(8,128)(2,1)S(1)}, u32[]{:S(2)}, u32[]{:S(2)}) %collective-permute-start.2) | collective-permute-done | bytes 589856 | tf_op jit(solution)/shard_map/ppermute | solution.py:339
  49.2 0.0 collective-permute-done.3.refs_2_
  49.2 2.5 collective-permute-done.4.refs_3_
  51.7 0.8 copy-done.10
  52.5 0.0 collective-permute-done.5.refs_4_
  52.5 4.8 %all-to-all-start.1 = ((bf16[8,192,768]{2,1,0:T(8,128)(2,1)}), bf16[8,192,768]{2,1,0:T(8,128)(2,1)S(1)}, u32[]{:S(2)}, u32[]{:S(2)}) async-start(bf16[8,192,768]{2,1,0:T(8,128)(2,1)} %place_rows.1), calls=%async_computation.1 | async-start | bytes 4718592 | tf_op jit(solution)/shard_map/all_to_all | solution.py:429
  57.3 2.0 constant_dynamic-update-slice_fusion.1
  59.4 1.9 constant_dynamic-update-slice_fusion.refs_0_
  61.3 0.5 collective-permute-start.6
  61.8 1.5 collective-permute-start.7
  63.4 1.4 collective-permute-start.8
  64.8 0.1 copy.18
  64.9 0.9 copy-done.7
  65.9 1.7 pad_maximum_fusion.refs_0_
  67.5 144.1 %put_rows.2.refs_4_ = bf16[768,6144]{1,0:T(8,128)(2,1)} custom-call(bf16[192,6144]{1,0:T(8,128)(2,1)} %pad_maximum_fusion.refs_0_, bf16[48,6144]{1,0:T(8,128)(2,1)} %copy-done.8, bf16[48,6144]{1,0:T(8,128)(2,1)} %copy-done.9, bf16[48,6144]{1,0:T(8,128)(2,1)} %copy-done.10, bf16[48,6144]{1,0:T(8,128)(2,1)} %collective-permute-done.5.refs_4_), custom_call_target="tpu_custom_call" | custom-call | bytes 9437184 | tf_op jit(solution)/shard_map/put_rows/pallas_call | solution.py:238
  211.6 0.0 all-to-all-done.1.got_ref
  211.6 2.1 pool_rows.1
  213.7 0.0 collective-permute-done.8.refs_3_
  213.7 0.6 collective-permute-start.9
  214.4 144.1 %put_rows.3.far_ref = bf16[768,6144]{1,0:T(8,128)(2,1)} custom-call(bf16[96,6144]{1,0:T(8,128)(2,1)} %constant_dynamic-update-slice_fusion.refs_0_, bf16[96,6144]{1,0:T(8,128)(2,1)} %collective-permute-done.6.refs_1_, bf16[96,6144]{1,0:T(8,128)(2,1)} %collective-permute-done.7.refs_2_, ...), custom_call_target="tpu_custom_call", output_to_operand_aliasing={{}: (4, {})} | custom-call | bytes 9437184 | tf_op jit(solution)/shard_map/put_rows/pallas_call | solution.py:238
  358.5 1.5 weave_steps.1.tok_ref
  359.9 0.0 copy-start.1
  359.9 0.1 collective-permute-start.10
  360.0 2.3 collective-permute-done.10.tok_ref
  362.3 0.9 copy-done.16
  363.2 12.3 %layer.3 = bf16[512,768]{1,0:T(8,128)(2,1)} custom-call(bf16[512,768]{1,0:T(8,128)(2,1)} %copy-done.16, bf16[768,6144]{1,0:T(8,128)(2,1)} %put_rows.3.far_ref), custom_call_target="tpu_custom_call" | custom-call | flops 4831838208 | bytes 11796480 | tf_op jit(solution)/shard_map/layer/pallas_call | solution.py:288
  375.5 0.2 collective-permute-start.11
  375.7 12.9 %layer.2.sum_ref = f32[512,768]{1,0:T(8,128)} custom-call(bf16[512,768]{1,0:T(8,128)(2,1)} %copy-done.1, bf16[768,6144]{1,0:T(8,128)(2,1)} %put_rows.3.far_ref), custom_call_target="tpu_custom_call" | custom-call | flops 4831838208 | bytes 11796480 | tf_op jit(solution)/shard_map/layer/pallas_call | solution.py:288
  388.6 0.0 collective-permute-done.11.got_ref
  388.6 1.4 copy-done
  390.0 1.8 finish.1
  (36 shorter events, 0.3 us)
Async XLA Ops:
  0.0 2.3 copy-start.6
  0.0 2.4 copy-start.13
  1.2 5.0 %copy-start.14 = (s32[512]{0:T(512)S(1)}, s32[512]{0:T(512)}, u32[]{:S(2)}) copy-start(s32[512]{0:T(512)} %param.11) | copy-start | bytes 6148
  1.3 5.0 %copy-start.15 = (s32[512]{0:T(512)S(1)}, s32[512]{0:T(512)}, u32[]{:S(2)}) copy-start(s32[512]{0:T(512)} %param.10) | copy-start | bytes 6148
  1.3 5.0 %copy-start.4 = (bf16[8,768]{1,0:T(8,128)(2,1)S(1)}, bf16[8,768]{1,0:T(8,128)(2,1)}, u32[]{:S(2)}) copy-start(bf16[8,768]{1,0:T(8,128)(2,1)} %time_ref.1) | copy-start | bytes 36868
  1.3 25.3 %copy-start.3 = (bf16[512,768]{1,0:T(8,128)(2,1)S(1)}, bf16[512,768]{1,0:T(8,128)(2,1)}, u32[]{:S(2)}) copy-start(bf16[512,768]{1,0:T(8,128)(2,1)} %feat_ref.1) | copy-start | bytes 2359300
  2.5 18.6 %collective-permute-start = (bf16[48,6144]{1,0:T(8,128)(2,1)S(1)}, bf16[48,6144]{1,0:T(8,128)(2,1)S(1)}, u32[]{:S(2)}, u32[]{:S(2)}) collective-permute-start(bf16[48,6144]{1,0:T(8,128)(2,1)S(1)} %pad_maximum_fusion.1), channel_id=1, source_target_pairs={{0,4},{4,8},{8,12},{12,0},{1,5},{5,9},{9,13},{13,1},{2,6},{6,10},{... | collective-permute-start | bytes 1769480 | tf_op jit(solution)/shard_map/ppermute | solution.py:339
  21.1 8.5 %copy-start.8 = (bf16[48,6144]{1,0:T(8,128)(2,1)}, bf16[48,6144]{1,0:T(8,128)(2,1)S(1)}, u32[]{:S(2)}) copy-start(bf16[48,6144]{1,0:T(8,128)(2,1)S(1)} %collective-permute-done.refs_1_) | copy-start | bytes 1769476
  21.1 16.0 %collective-permute-start.1 = (bf16[48,6144]{1,0:T(8,128)(2,1)S(1)}, bf16[48,6144]{1,0:T(8,128)(2,1)S(1)}, u32[]{:S(2)}, u32[]{:S(2)}) collective-permute-start(bf16[48,6144]{1,0:T(8,128)(2,1)S(1)} %pad_maximum_fusion.1), channel_id=1, source_target_pairs={{0,12},{4,0},{8,4},{12,8},{1,13},{5,1},{9,5},{13,9},{2,14},{6,2},{... | collective-permute-start | bytes 1769480 | tf_op jit(solution)/shard_map/ppermute | solution.py:339
  22.8 26.4 %collective-permute-start.2 = (bf16[48,6144]{1,0:T(8,128)(2,1)S(1)}, bf16[48,6144]{1,0:T(8,128)(2,1)S(1)}, u32[]{:S(2)}, u32[]{:S(2)}) collective-permute-start(bf16[48,6144]{1,0:T(8,128)(2,1)S(1)} %collective-permute-done.refs_1_), channel_id=1, source_target_pairs={{0,4},{4,8},{8,12},{12,0},{1,5},{5,9},{9,13},{13,1},{2,6},{6,10},{... | collective-permute-start | bytes 1769480 | tf_op jit(solution)/shard_map/ppermute | solution.py:339
  23.1 26.1 %collective-permute-start.3 = (bf16[48,6144]{1,0:T(8,128)(2,1)S(1)}, bf16[48,6144]{1,0:T(8,128)(2,1)S(1)}, u32[]{:S(2)}, u32[]{:S(2)}) collective-permute-start(bf16[48,6144]{1,0:T(8,128)(2,1)S(1)} %collective-permute-done.refs_1_), channel_id=1, source_target_pairs={{0,2},{2,0},{16,18},{18,16},{1,3},{3,1},{17,19},{19,17},{4,6},{6,4... | collective-permute-start | bytes 1769480 | tf_op jit(solution)/shard_map/ppermute | solution.py:348
  24.6 27.1 %collective-permute-start.4 = (bf16[48,6144]{1,0:T(8,128)(2,1)S(1)}, bf16[48,6144]{1,0:T(8,128)(2,1)S(1)}, u32[]{:S(2)}, u32[]{:S(2)}) collective-permute-start(bf16[48,6144]{1,0:T(8,128)(2,1)S(1)} %collective-permute-done.refs_1_), channel_id=1, source_target_pairs={{0,16},{2,18},{16,0},{18,2},{1,17},{3,19},{17,1},{19,3},{4,20},{6,... | collective-permute-start | bytes 1769480 | tf_op jit(solution)/shard_map/ppermute | solution.py:348
  26.1 26.4 %collective-permute-start.5 = (bf16[48,6144]{1,0:T(8,128)(2,1)S(1)}, bf16[48,6144]{1,0:T(8,128)(2,1)}, u32[]{:S(2)}, u32[]{:S(2)}) collective-permute-start(bf16[48,6144]{1,0:T(8,128)(2,1)S(1)} %collective-permute-done.refs_1_), channel_id=1, source_target_pairs={{0,18},{2,16},{16,2},{18,0},{1,19},{3,17},{17,3},{19,1},{4,22},{6,... | collective-permute-start | bytes 1769480 | tf_op jit(solution)/shard_map/ppermute | solution.py:348
  37.0 14.6 %copy-start.11 = (bf16[48,6144]{1,0:T(8,128)(2,1)}, bf16[48,6144]{1,0:T(8,128)(2,1)S(1)}, u32[]{:S(2)}) copy-start(bf16[48,6144]{1,0:T(8,128)(2,1)S(1)} %collective-permute-done.1) | copy-start | bytes 1769476
  49.2 2.5 copy-start.12
  49.2 2.5 copy-start.9
  51.7 0.8 copy-start.10
  52.5 159.1 %all-to-all-start.1 = ((bf16[8,192,768]{2,1,0:T(8,128)(2,1)}), bf16[8,192,768]{2,1,0:T(8,128)(2,1)S(1)}, u32[]{:S(2)}, u32[]{:S(2)}) async-start(bf16[8,192,768]{2,1,0:T(8,128)(2,1)} %place_rows.1), calls=%async_computation.1 | async-start | bytes 4718592 | tf_op jit(solution)/shard_map/all_to_all | solution.py:429
  57.3 7.5 %copy-start.5 = (bf16[192,2,1536]{2,1,0:T(2,128)(2,1)S(1)}, bf16[192,2,1536]{2,1,0:T(2,128)(2,1)}, u32[]{:S(2)}) copy-start(bf16[192,2,1536]{2,1,0:T(2,128)(2,1)} %param.16) | copy-start | bytes 3538948
  61.3 152.4 %collective-permute-start.6 = (bf16[96,6144]{1,0:T(8,128)(2,1)}, bf16[96,6144]{1,0:T(8,128)(2,1)}, u32[]{:S(2)}, u32[]{:S(2)}) collective-permute-start(bf16[96,6144]{1,0:T(8,128)(2,1)} %constant_dynamic-update-slice_fusion.refs_0_), channel_id=1, source_target_pairs={{0,2},{2,0},{16,18},{18,16},{1,3},{3,1},{17,19},{19,17},{4,6},{6,4... | collective-permute-start | bytes 3538952 | tf_op jit(solution)/shard_map/ppermute | solution.py:348
  61.8 151.9 %collective-permute-start.7 = (bf16[96,6144]{1,0:T(8,128)(2,1)}, bf16[96,6144]{1,0:T(8,128)(2,1)}, u32[]{:S(2)}, u32[]{:S(2)}) collective-permute-start(bf16[96,6144]{1,0:T(8,128)(2,1)} %constant_dynamic-update-slice_fusion.refs_0_), channel_id=1, source_target_pairs={{0,16},{2,18},{16,0},{18,2},{1,17},{3,19},{17,1},{19,3},{4,20},{6,... | collective-permute-start | bytes 3538952 | tf_op jit(solution)/shard_map/ppermute | solution.py:348
  63.4 150.4 %collective-permute-start.8 = (bf16[96,6144]{1,0:T(8,128)(2,1)}, bf16[96,6144]{1,0:T(8,128)(2,1)}, u32[]{:S(2)}, u32[]{:S(2)}) collective-permute-start(bf16[96,6144]{1,0:T(8,128)(2,1)} %constant_dynamic-update-slice_fusion.refs_0_), channel_id=1, source_target_pairs={{0,18},{2,16},{16,2},{18,0},{1,19},{3,17},{17,3},{19,1},{4,22},{6,... | collective-permute-start | bytes 3538952 | tf_op jit(solution)/shard_map/ppermute | solution.py:348
  64.8 1.0 copy-start.7
  213.7 144.7 %collective-permute-start.9 = (bf16[256,768]{1,0:T(8,128)(2,1)S(1)}, bf16[256,768]{1,0:T(8,128)(2,1)S(1)}, u32[]{:S(2)}, u32[]{:S(2)}) collective-permute-start(bf16[256,768]{1,0:T(8,128)(2,1)S(1)} %get-tuple-element.43), channel_id=1, source_target_pairs={{0,2},{2,0},{1,3},{3,1},{4,6},{6,4},{5,7},{7,5},{8,10},{10,8},{9,1... | collective-permute-start | bytes 1179656 | tf_op jit(solution)/shard_map/ppermute | solution.py:433
  359.9 15.5 %copy-start.1 = (bf16[512,768]{1,0:T(8,128)(2,1)}, bf16[512,768]{1,0:T(8,128)(2,1)S(1)}, u32[]{:S(2)}) copy-start(bf16[512,768]{1,0:T(8,128)(2,1)S(1)} %weave_steps.1.tok_ref) | copy-start | bytes 2359300
  359.9 2.4 collective-permute-start.10
  362.3 0.9 copy-start.16
  375.5 13.1 %collective-permute-start.11 = (bf16[512,768]{1,0:T(8,128)(2,1)}, bf16[512,768]{1,0:T(8,128)(2,1)S(1)}, u32[]{:S(2)}, u32[]{:S(2)}) collective-permute-start(bf16[512,768]{1,0:T(8,128)(2,1)} %layer.3), channel_id=1, source_target_pairs={{0,1},{1,0},{2,3},{3,2},{4,5},{5,4},{6,7},{7,6},{8,9},{9,8},{10,11... | collective-permute-start | bytes 2359304 | tf_op jit(solution)/shard_map/ppermute | solution.py:446
  375.7 12.9 %copy-start.2 = (bf16[512,768]{1,0:T(8,128)(2,1)S(1)}, bf16[512,768]{1,0:T(8,128)(2,1)}, u32[]{:S(2)}) copy-start(bf16[512,768]{1,0:T(8,128)(2,1)} %copy-done.1) | copy-start | bytes 2359300
  388.6 1.4 copy-start

commit v12 on v10

--- a/solution.py
+++ b/solution.py
@@ -20,6 +20,7 @@
 BF16 = jnp.bfloat16
 WHOLE = pl.BlockSpec(memory_space=pltpu.VMEM)
 SCALARS = pl.BlockSpec(memory_space=pltpu.SMEM)
+FAR = pl.BlockSpec(memory_space=pl.ANY)
 
 
 def iota(shape, axis):
@@ -75,7 +76,7 @@
         ],
         in_specs=[WHOLE] * 3,
         out_specs=[WHOLE] * 2,
-        compiler_params=params(6),
+        compiler_params=params(12),
         cost_estimate=pl.CostEstimate(
             flops=16 * rows * n_owners * capacity, bytes_accessed=8 * rows, transcendentals=0
         ),
@@ -168,7 +169,7 @@
         out_shape=jax.ShapeDtypeStruct((rows, width), BF16),
         in_specs=[SCALARS] + [WHOLE] * 3,
         out_specs=WHOLE,
-        compiler_params=params(10),
+        compiler_params=params(12),
         cost_estimate=pl.CostEstimate(
             flops=2 * rows * width * (rows + width), bytes_accessed=4 * rows * width, transcendentals=0
         ),
@@ -220,46 +221,30 @@
     return dot_t(hidden, down_w)
 
 
-def put_rows_kernel(firsts, *refs):
-    pieces, (out_ref, sems) = refs[: len(firsts)], refs[-2:]
-    copies = [
-        pltpu.make_async_copy(piece, out_ref.at[pl.ds(first, piece.shape[0]), :], sems.at[number])
-        for number, (first, piece) in enumerate(zip(firsts, pieces))
-    ]
-    for copy in copies:
+def layer_kernel(plan, hidden_width, tok_ref, *refs):
+    pieces, (out_ref, w_ref, norm_ref, ctx_ref, acc_ref, sems) = refs[:-6], refs[-6:]
+    copies = {}
+    for number, (section, piece, row, at, size) in enumerate(plan):
+        copy = pltpu.make_async_copy(
+            pieces[piece].at[:, pl.ds(at, size)],
+            w_ref.at[pl.ds(row, pieces[piece].shape[0]), pl.ds(at, size)],
+            sems.at[number],
+        )
         copy.start()
-    for copy in copies:
-        copy.wait()
-
-
-def put_rows(pieces, rows, first, into=None):
-    firsts = [first + sum(piece.shape[0] for piece in pieces[:number]) for number in range(len(pieces))]
-    operands = pieces if into is None else pieces + [into]
-    return pl.pallas_call(
-        functools.partial(put_rows_kernel, firsts),
-        out_shape=jax.ShapeDtypeStruct((rows, pieces[0].shape[1]), BF16),
-        in_specs=[pl.BlockSpec(memory_space=pl.ANY)] * len(operands),
-        out_specs=pl.BlockSpec(memory_space=pl.ANY),
-        scratch_shapes=[pltpu.SemaphoreType.DMA((len(pieces),))],
-        input_output_aliases={} if into is None else {len(pieces): 0},
-        compiler_params=params(2),
-        cost_estimate=pl.CostEstimate(
-            flops=0, bytes_accessed=4 * sum(piece.size for piece in pieces), transcendentals=0
-        ),
-        name="put_rows",
-    )(*operands)
-
-
-def layer_kernel(hidden_width, tok_ref, w_ref, out_ref, norm_ref, ctx_ref, acc_ref):
+        copies.setdefault(section, []).append(copy)
+
+    def ready(section):
+        for copy in copies[section]:
+            copy.wait()
+
     heads_width = ctx_ref.shape[1]
-    gate_at = 3 * heads_width
-    up_at = gate_at + hidden_width
-    out_at = up_at + hidden_width
-    down_at = out_at + heads_width
+    gate_at, up_at, out_at, down_at, _ = layer_columns(heads_width, hidden_width)
     tokens = tok_ref[...].astype(F32)
     scale = lax.rsqrt(jnp.mean(tokens * tokens, axis=1, keepdims=True) + EPS)
     norm_ref[...] = (tokens * scale).astype(BF16)
+    ready(0)
     attention(norm_ref[...], w_ref[:, :gate_at], heads_width, ctx_ref)
+    ready(1)
     acc_ref[...] = dot_t(ctx_ref[...], w_ref[:, out_at:down_at])
     for begin in range(0, hidden_width, UNIT):
         gate_w, up_w, down_w = [w_ref[:, at + begin : at + begin + UNIT] for at in (gate_at, up_at, down_at)]
@@ -270,26 +255,42 @@
             out_ref[...] = (acc_ref[...] + add).astype(out_ref.dtype)
 
 
-def layer(tokens, weights, heads_width, hidden_width, out_type):
+def layer_columns(heads_width, hidden_width):
+    gate_at = 3 * heads_width
+    up_at = gate_at + hidden_width
+    out_at = up_at + hidden_width
+    return gate_at, up_at, out_at, out_at + heads_width, out_at + heads_width + hidden_width
+
+
+def layer(tokens, pieces, heads_width, hidden_width, out_type):
     rows, width = tokens.shape
-    return pl.pallas_call(
-        functools.partial(layer_kernel, hidden_width),
+    gate_at, _, _, _, columns = layer_columns(heads_width, hidden_width)
+    plan = []
+    for section, (left, right) in enumerate([(0, gate_at), (gate_at, columns)]):
+        row = 0
+        for number, piece in enumerate(pieces):
+            plan.append((section, number, row, left, right - left))
+            row += piece.shape[0]
+    return pl.pallas_call(
+        functools.partial(layer_kernel, plan, hidden_width),
         out_shape=jax.ShapeDtypeStruct((rows, width), out_type),
-        in_specs=[WHOLE] * 2,
+        in_specs=[WHOLE] + [FAR] * len(pieces),
         out_specs=WHOLE,
         scratch_shapes=[
+            pltpu.VMEM((width, columns), BF16),
             pltpu.VMEM((rows, width), BF16),
             pltpu.VMEM((rows, heads_width), BF16),
             pltpu.VMEM((rows, width), F32),
+            pltpu.SemaphoreType.DMA((len(plan),)),
         ],
-        compiler_params=params(26),
-        cost_estimate=pl.CostEstimate(
-            flops=2 * rows * width * weights.shape[1],
-            bytes_accessed=2 * weights.size + 6 * rows * width,
+        compiler_params=params(54),
+        cost_estimate=pl.CostEstimate(
+            flops=2 * rows * width * columns,
+            bytes_accessed=2 * width * columns + 6 * rows * width,
             transcendentals=rows * hidden_width,
         ),
         name="layer",
-    )(tokens, weights)
+    )(tokens, *pieces)
 
 
 def finish_kernel(tok_ref, sum_ref, got_ref, order_ref, out_ref):
@@ -306,7 +307,7 @@
         out_shape=jax.ShapeDtypeStruct((rows, width), BF16),
         in_specs=[WHOLE] * 4,
         out_specs=WHOLE,
-        compiler_params=params(10),
+        compiler_params=params(12),
         cost_estimate=pl.CostEstimate(
             flops=2 * rows * width * width, bytes_accessed=10 * rows * width, transcendentals=0
         ),
@@ -410,26 +411,25 @@
         above, opposite = along_cells(share_rows, 1), along_cells(below, -1)
         blocks, above, opposite, first = lax.optimization_barrier((blocks, above, opposite, first))
         second = to_other_places(jnp.concatenate([above, opposite], axis=0))
-        weights = put_rows([side_by_side(*local_weights)] + first, width, 0)
+        shard = side_by_side(*local_weights)
         got = lax.all_to_all(blocks, ("cells", "mp"), split_axis=0, concat_axis=0, tiled=True)
-        got, weights = lax.optimization_barrier((got, weights))
+        got, shard = lax.optimization_barrier((got, shard))
         keep, send = pool_rows(my_slot.reshape(1), embed, codes, got, capacity, slot_dev)
         send, second = lax.optimization_barrier((send, second))
         other = lax.ppermute(send, "slots", [(0, 1), (1, 0)])
-        weights = put_rows(second, width, width // 2, weights)
-        other, weights = lax.optimization_barrier((other, weights))
+        pieces = [shard] + first + second
         tokens = weave_steps(my_slot.reshape(1), order, keep, other, slot_dev)
     else:
         order = jnp.arange(width, dtype=jnp.int32)
-        weights = lax.all_gather(share_rows, ("cells", "groups", "slots"), axis=0, tiled=True)
+        pieces = [lax.all_gather(share_rows, ("cells", "groups", "slots"), axis=0, tiled=True)]
         tokens = tokens_by_exchanges(owner, position, obs_feat, time_embed, my_slot, capacity, slot_dev)
 
     swap = [(0, 1), (1, 0)]
     heads_width, hidden_width = w_qkv.shape[2], w_gate_up.shape[2]
     partner = lax.ppermute(tokens, "mp", swap)
-    for_partner = layer(partner, weights, heads_width, hidden_width, BF16)
+    for_partner = layer(partner, pieces, heads_width, hidden_width, BF16)
     from_partner = lax.ppermute(for_partner, "mp", swap)
-    own = layer(tokens, weights, heads_width, hidden_width, F32)
+    own = layer(tokens, pieces, heads_width, hidden_width, F32)
     return finish(tokens, own, from_partner, order).reshape(quarter, TSTEPS, width)
 
 

time: 154 us -> 157 us (1.019)
  local copies, waits for them, and re-layouts: 27.4 us -> 11.2 us
  waiting for transfers between devices: 65.9 us -> 79.9 us
  Pallas kernels: 27.4 us -> 31.5 us
    unnamed x58 -> x36, local copies, waits for them, and re-layouts: 23.4 us -> 6.19 us
    ppermute x6, waiting for transfers between devices: 1.62 us -> 15.5 us  [to_other_places(): places.append(lax.ppermute(shares, ('groups', 'slots'), pairs))]
    ppermute x3, waiting for transfers between devices: 19.6 us -> 7.39 us  [along_cells(): lax.ppermute(values, 'cells', [(j, (j - distance) % n_cells) for j in ran...]
    ppermute x1, waiting for transfers between devices: 0.79 us -> 9.5 us  [on_device(): other = lax.ppermute(send, 'slots', [(0, 1), (1, 0)])]
    pallas_call x4 -> x2, Pallas kernels: 17.7 us -> 22.5 us  [layer(): pl.pallas_call(functools.partial(layer_kernel, plan, hidden_width), out_s...]
    all_to_all x1, waiting for transfers between devices: 41.7 us -> 45.2 us  [on_device(): lax.all_to_all(blocks, ('cells', 'mp'), split_axis=0, concat_axis=0, tile...]
  transfers between devices with their start and end apart: 13 -> 13, of which waited for: 6 -> 9; matrix products, arithmetic and copies ran while one was open for 2% -> 3% of each run, Pallas kernels for 11% -> 11%
where the time goes in v12:
time: 157 us
  waiting for transfers between devices  79.9 us (51%)
  Pallas kernels  31.5 us (20%)
  starting transfers between devices  17.5 us (11%)
  blocking collectives  14.1 us (9%)
  local copies, waits for them, and re-layouts  11.2 us (7%)
  other arithmetic  1.76 us (1%)
    all_to_all x1, waiting for transfers between devices, on_device(): lax.all_to_all(blocks, ('cells', 'mp'), split_axis=0, concat_axis=0, tile...  45.2 us
    pallas_call x2, Pallas kernels, layer(): pl.pallas_call(functools.partial(layer_kernel, plan, hidden_width), out_s...  22.5 us
    ppermute x6, waiting for transfers between devices, to_other_places(): places.append(lax.ppermute(shares, ('groups', 'slots'), pairs))  15.5 us
    all_to_all x1, blocking collectives, on_device(): lax.all_to_all(codes, ('cells', 'mp'), split_axis=0, concat_axis=0, tiled...  14.1 us
    ppermute x1, waiting for transfers between devices, on_device(): other = lax.ppermute(send, 'slots', [(0, 1), (1, 0)])  9.5 us
    ppermute x3, waiting for transfers between devices, along_cells(): lax.ppermute(values, 'cells', [(j, (j - distance) % n_cells) for j in ran...  7.39 us
    ppermute x6, starting transfers between devices, to_other_places(): places.append(lax.ppermute(shares, ('groups', 'slots'), pairs))  6.98 us
    unnamed x36, local copies, waits for them, and re-layouts  6.19 us
  transfers between devices with their start and end apart: 13, of which 9 were waited for; matrix products, arithmetic and copies ran while one was open for 3% of the time, Pallas kernels for 11%

profile of v12, /device:TPU:0, one launch (start us, length us, event | category | flops | bytes accessed | tf_op | source)
XLA Modules:
  0.0 156.9 jit_solution(17744625193480308904)
XLA Ops:
  0.0 0.8 dynamic-slice_bitcast_fusion.2
  0.8 0.9 dynamic-slice_bitcast_fusion.1
  1.7 0.9 dynamic-slice_bitcast_fusion
  2.6 0.0 copy-start.10
  2.7 0.0 copy-start.4
  2.7 1.2 constant_dynamic-slice_fusion
  4.0 3.1 %collective-permute-start = (bf16[48,6144]{1,0:T(8,128)(2,1)S(1)}, bf16[48,6144]{1,0:T(8,128)(2,1)S(1)}, u32[]{:S(2)}, u32[]{:S(2)}) collective-permute-start(bf16[48,6144]{1,0:T(8,128)(2,1)S(1)} %pad_maximum_fusion.1), channel_id=1, source_target_pairs={{0,4},{4,8},{8,12},{12,0},{1,5},{5,9},{9,13},{13,1},{2,6},{6,10},{... | collective-permute-start | bytes 1769480 | tf_op jit(solution)/shard_map/ppermute | solution.py:325
  7.8 0.7 place_codes.1
  8.5 14.1 %all_to_all.10.code_ref = s32[8,1,192]{2,1,0:T(1,128)S(1)} all-to-all(s32[8,1,192]{2,1,0:T(1,128)S(1)} %get-tuple-element.27), channel_id=1, replica_groups=mesh['groups'=2,'cells'=4,'slots'=2,'mp'=2] {'cells','mp'}, dimensions={0} | all-to-all | bytes 12288 | tf_op jit(solution)/shard_map/all_to_all | solution.py:407
  22.6 1.7 %collective-permute-start.1 = (bf16[48,6144]{1,0:T(8,128)(2,1)S(1)}, bf16[48,6144]{1,0:T(8,128)(2,1)S(1)}, u32[]{:S(2)}, u32[]{:S(2)}) collective-permute-start(bf16[48,6144]{1,0:T(8,128)(2,1)S(1)} %pad_maximum_fusion.1), channel_id=1, source_target_pairs={{0,12},{4,0},{8,4},{12,8},{1,13},{5,1},{9,5},{13,9},{2,14},{6,2},{... | collective-permute-start | bytes 1769480 | tf_op jit(solution)/shard_map/ppermute | solution.py:325
  24.4 2.4 %collective-permute-start.5 = (bf16[48,6144]{1,0:T(8,128)(2,1)S(1)}, bf16[48,6144]{1,0:T(8,128)(2,1)S(1)}, u32[]{:S(2)}, u32[]{:S(2)}) collective-permute-start(bf16[48,6144]{1,0:T(8,128)(2,1)S(1)} %collective-permute-done.refs_1_), channel_id=1, source_target_pairs={{0,18},{2,16},{16,2},{18,0},{1,19},{3,17},{17,3},{19,1},{4,22},{6,... | collective-permute-start | bytes 1769480 | tf_op jit(solution)/shard_map/ppermute | solution.py:334
  26.8 0.5 collective-permute-start.4
  27.3 0.5 collective-permute-start.3
  27.9 0.3 collective-permute-start.2
  28.2 3.0 %place_rows.1 = bf16[8,192,768]{2,1,0:T(8,128)(2,1)} custom-call(s32[1,512]{1,0:T(1,128)S(1)} %bitcast.22, bf16[512,768]{1,0:T(8,128)(2,1)S(1)} %copy-done.3), custom_call_target="tpu_custom_call" | custom-call | flops 1207959552 | bytes 3145728 | tf_op jit(solution)/shard_map/place_rows/pallas_call | solution.py:98
  31.2 7.4 %collective-permute-done.1 = bf16[48,6144]{1,0:T(8,128)(2,1)S(1)} collective-permute-done((bf16[48,6144]{1,0:T(8,128)(2,1)S(1)}, bf16[48,6144]{1,0:T(8,128)(2,1)S(1)}, u32[]{:S(2)}, u32[]{:S(2)}) %collective-permute-start.1) | collective-permute-done | bytes 589856 | tf_op jit(solution)/shard_map/ppermute | solution.py:325
  38.6 2.9 %collective-permute-done.5.refs_4_ = bf16[48,6144]{1,0:T(8,128)(2,1)S(1)} collective-permute-done((bf16[48,6144]{1,0:T(8,128)(2,1)S(1)}, bf16[48,6144]{1,0:T(8,128)(2,1)S(1)}, u32[]{:S(2)}, u32[]{:S(2)}) %collective-permute-start.5) | collective-permute-done | bytes 589856 | tf_op jit(solution)/shard_map/ppermute | solution.py:334
  41.5 11.4 %collective-permute-done.4.refs_3_ = bf16[48,6144]{1,0:T(8,128)(2,1)S(1)} collective-permute-done((bf16[48,6144]{1,0:T(8,128)(2,1)S(1)}, bf16[48,6144]{1,0:T(8,128)(2,1)S(1)}, u32[]{:S(2)}, u32[]{:S(2)}) %collective-permute-start.4) | collective-permute-done | bytes 589856 | tf_op jit(solution)/shard_map/ppermute | solution.py:334
  52.9 0.1 collective-permute-done.3.refs_2_
  53.0 0.7 copy-done.14
  53.7 0.2 copy-done.15
  53.9 3.8 %all-to-all-start.1 = ((bf16[8,192,768]{2,1,0:T(8,128)(2,1)}), bf16[8,192,768]{2,1,0:T(8,128)(2,1)S(1)}, u32[]{:S(2)}, u32[]{:S(2)}) async-start(bf16[8,192,768]{2,1,0:T(8,128)(2,1)} %place_rows.1), calls=%async_computation.1 | async-start | bytes 4718592 | tf_op jit(solution)/shard_map/all_to_all | solution.py:415
  57.8 0.9 constant_dynamic-update-slice_fusion.1
  58.7 2.0 %constant_dynamic-update-slice_fusion.refs_5_ = bf16[96,6144]{1,0:T(8,128)(2,1)} fusion(bf16[96,6144]{1,0:T(8,128)(2,1)} %constant_dynamic-update-slice_fusion.1, bf16[48,6144]{1,0:T(8,128)(2,1)} %collective-permute-done.2), kind=kLoop, calls=%fused_computation.21 | loop fusion | bytes 1179648 | tf_op jit(solution)/shard_map/concatenate | solution.py:413
  60.7 1.7 %collective-permute-start.8 = (bf16[96,6144]{1,0:T(8,128)(2,1)}, bf16[96,6144]{1,0:T(8,128)(2,1)}, u32[]{:S(2)}, u32[]{:S(2)}) collective-permute-start(bf16[96,6144]{1,0:T(8,128)(2,1)} %constant_dynamic-update-slice_fusion.refs_5_), channel_id=1, source_target_pairs={{0,18},{2,16},{16,2},{18,0},{1,19},{3,17},{17,3},{19,1},{4,22},{6,... | collective-permute-start | bytes 3538952 | tf_op jit(solution)/shard_map/ppermute | solution.py:334
  62.5 1.2 collective-permute-start.7
  63.7 0.5 collective-permute-start.6
  64.3 0.0 copy-start.6
  64.3 0.0 copy-start.8
  64.3 0.1 copy.17
  64.4 0.9 copy-done.6
  65.3 0.0 copy-done.8
  65.4 1.7 %pad_maximum_fusion.refs_0_ = bf16[192,6144]{1,0:T(8,128)(2,1)} fusion(bf16[192,1536]{1,0:T(8,128)(2,1)S(1)} %bitcast.29, bf16[192,384]{1,0:T(8,128)(2,1)S(1)} %bitcast.32, bf16[192,3072]{1,0:T(8,128)(2,1)S(1)} %bitcast.24, bf16[192,1152]{1,0:T(8,128)(2,1)S(1)} %bitcast.26), kind=kLoop, calls=%fused_computation | loop fusion | flops 9437184 | bytes 4718592 | tf_op jit(solution)/shard_map/concatenate | solution.py:320
  67.0 45.2 %all-to-all-done.1.got_ref = bf16[8,192,768]{2,1,0:T(8,128)(2,1)S(1)} async-done(((bf16[8,192,768]{2,1,0:T(8,128)(2,1)}), bf16[8,192,768]{2,1,0:T(8,128)(2,1)S(1)}, u32[]{:S(2)}, u32[]{:S(2)}) %all-to-all-start.1) | async-done | bytes 2359328 | tf_op jit(solution)/shard_map/all_to_all | solution.py:415
  112.2 2.1 %pool_rows.1 = (bf16[256,768]{1,0:T(8,128)(2,1)S(1)}, bf16[256,768]{1,0:T(8,128)(2,1)S(1)}) custom-call(s32[1]{0:T(128)} %bitcast.slot_ref, bf16[8,768]{1,0:T(8,128)(2,1)S(1)} %get-tuple-element.26.embed_ref, s32[8,1,192]{2,1,0:T(1,128)S(1)} %all_to_all.10.code_ref, bf16[8,192,768]{2,1,0:T(8,128)(2,1)S(1)} %all-to-all-done.1.got_ref), custom_call_target="tpu_custom_call" | custom-call | flops 1207959552 | bytes 2359296 | tf_op jit(solution)/shard_map/pool_rows/pallas_call | solution.py:138
  114.3 1.0 collective-permute-done.7.refs_7_
  115.3 0.1 collective-permute-done.6.refs_6_
  115.4 1.4 collective-permute-start.9
  116.8 9.5 %collective-permute-done.9.got_ref = bf16[256,768]{1,0:T(8,128)(2,1)S(1)} collective-permute-done((bf16[256,768]{1,0:T(8,128)(2,1)S(1)}, bf16[256,768]{1,0:T(8,128)(2,1)S(1)}, u32[]{:S(2)}, u32[]{:S(2)}) %collective-permute-start.9) | collective-permute-done | bytes 393248 | tf_op jit(solution)/shard_map/ppermute | solution.py:419
  126.3 1.5 weave_steps.1.tok_ref
  127.8 0.1 collective-permute-start.10
  127.9 2.3 %collective-permute-done.10.tok_ref = bf16[512,768]{1,0:T(8,128)(2,1)S(1)} collective-permute-done((bf16[512,768]{1,0:T(8,128)(2,1)S(1)}, bf16[512,768]{1,0:T(8,128)(2,1)S(1)}, u32[]{:S(2)}, u32[]{:S(2)}) %collective-permute-start.10) | collective-permute-done | bytes 786464 | tf_op jit(solution)/shard_map/ppermute | solution.py:429
  130.2 0.9 copy-done.11
  131.0 10.9 %layer.3 = bf16[512,768]{1,0:T(8,128)(2,1)} custom-call(bf16[512,768]{1,0:T(8,128)(2,1)} %copy-done.11, bf16[192,6144]{1,0:T(8,128)(2,1)} %pad_maximum_fusion.refs_0_, bf16[48,6144]{1,0:T(8,128)(2,1)} %copy-done.12, bf16[48,6144]{1,0:T(8,128)(2,1)} %copy-done.15, bf16[48,6144]{1,0:T(8,128)(2,1)} %copy-done.14, bf16[48,6144]{1,0:T(8,128)(2,1)} %copy-done.13, ...), custom_call_target="tpu_custom_call" | custom-call | flops 4831838208 | bytes 11796480 | tf_op jit(solution)/shard_map/layer/pallas_call | solution.py:274
  142.0 0.2 collective-permute-start.11
  142.2 11.5 %layer.2.sum_ref = f32[512,768]{1,0:T(8,128)} custom-call(bf16[512,768]{1,0:T(8,128)(2,1)} %copy-done.1, bf16[192,6144]{1,0:T(8,128)(2,1)} %pad_maximum_fusion.refs_0_, bf16[48,6144]{1,0:T(8,128)(2,1)} %copy-done.12, bf16[48,6144]{1,0:T(8,128)(2,1)} %copy-done.15, bf16[48,6144]{1,0:T(8,128)(2,1)} %copy-done.14, bf16[48,6144]{1,0:T(8,128)(2,1)} %copy-done.13, ...), custom_call_target="tpu_custom_call" | custom-call | flops 4831838208 | bytes 11796480 | tf_op jit(solution)/shard_map/layer/pallas_call | solution.py:274
  153.7 1.4 copy-done
  155.1 1.8 %finish.1 = bf16[512,768]{1,0:T(8,128)(2,1)} custom-call(bf16[512,768]{1,0:T(8,128)(2,1)S(1)} %copy-done.2, f32[512,768]{1,0:T(8,128)S(1)} %copy-done, bf16[512,768]{1,0:T(8,128)(2,1)S(1)} %collective-permute-done.11.got_ref, s32[1,768]{1,0:T(1,128)S(1)} %compare_select_fusion.6.order_ref), custom_call_target="tpu_custom_call" | custom-call | flops 603979776 | bytes 3932160 | tf_op jit(solution)/shard_map/finish/pallas_call | solution.py:305
  (32 shorter events, 0.3 us)
Async XLA Ops:
  2.6 5.1 %copy-start.9 = (s32[512]{0:T(512)S(1)}, s32[512]{0:T(512)}, u32[]{:S(2)}) copy-start(s32[512]{0:T(512)} %param.11) | copy-start | bytes 6148
  2.6 5.1 %copy-start.10 = (s32[512]{0:T(512)S(1)}, s32[512]{0:T(512)}, u32[]{:S(2)}) copy-start(s32[512]{0:T(512)} %param.10) | copy-start | bytes 6148
  2.7 5.1 %copy-start.4 = (bf16[8,768]{1,0:T(8,128)(2,1)S(1)}, bf16[8,768]{1,0:T(8,128)(2,1)}, u32[]{:S(2)}) copy-start(bf16[8,768]{1,0:T(8,128)(2,1)} %time_ref.1) | copy-start | bytes 36868
  2.7 25.5 %copy-start.3 = (bf16[512,768]{1,0:T(8,128)(2,1)S(1)}, bf16[512,768]{1,0:T(8,128)(2,1)}, u32[]{:S(2)}) copy-start(bf16[512,768]{1,0:T(8,128)(2,1)} %feat_ref.1) | copy-start | bytes 2359300
  4.0 18.6 %collective-permute-start = (bf16[48,6144]{1,0:T(8,128)(2,1)S(1)}, bf16[48,6144]{1,0:T(8,128)(2,1)S(1)}, u32[]{:S(2)}, u32[]{:S(2)}) collective-permute-start(bf16[48,6144]{1,0:T(8,128)(2,1)S(1)} %pad_maximum_fusion.1), channel_id=1, source_target_pairs={{0,4},{4,8},{8,12},{12,0},{1,5},{5,9},{9,13},{13,1},{2,6},{6,10},{... | collective-permute-start | bytes 1769480 | tf_op jit(solution)/shard_map/ppermute | solution.py:325
  22.6 8.6 %copy-start.12 = (bf16[48,6144]{1,0:T(8,128)(2,1)}, bf16[48,6144]{1,0:T(8,128)(2,1)S(1)}, u32[]{:S(2)}) copy-start(bf16[48,6144]{1,0:T(8,128)(2,1)S(1)} %collective-permute-done.refs_1_) | copy-start | bytes 1769476
  22.6 16.0 %collective-permute-start.1 = (bf16[48,6144]{1,0:T(8,128)(2,1)S(1)}, bf16[48,6144]{1,0:T(8,128)(2,1)S(1)}, u32[]{:S(2)}, u32[]{:S(2)}) collective-permute-start(bf16[48,6144]{1,0:T(8,128)(2,1)S(1)} %pad_maximum_fusion.1), channel_id=1, source_target_pairs={{0,12},{4,0},{8,4},{12,8},{1,13},{5,1},{9,5},{13,9},{2,14},{6,2},{... | collective-permute-start | bytes 1769480 | tf_op jit(solution)/shard_map/ppermute | solution.py:325
  24.4 17.2 %collective-permute-start.5 = (bf16[48,6144]{1,0:T(8,128)(2,1)S(1)}, bf16[48,6144]{1,0:T(8,128)(2,1)S(1)}, u32[]{:S(2)}, u32[]{:S(2)}) collective-permute-start(bf16[48,6144]{1,0:T(8,128)(2,1)S(1)} %collective-permute-done.refs_1_), channel_id=1, source_target_pairs={{0,18},{2,16},{16,2},{18,0},{1,19},{3,17},{17,3},{19,1},{4,22},{6,... | collective-permute-start | bytes 1769480 | tf_op jit(solution)/shard_map/ppermute | solution.py:334
  26.8 26.1 %collective-permute-start.4 = (bf16[48,6144]{1,0:T(8,128)(2,1)S(1)}, bf16[48,6144]{1,0:T(8,128)(2,1)S(1)}, u32[]{:S(2)}, u32[]{:S(2)}) collective-permute-start(bf16[48,6144]{1,0:T(8,128)(2,1)S(1)} %collective-permute-done.refs_1_), channel_id=1, source_target_pairs={{0,16},{2,18},{16,0},{18,2},{1,17},{3,19},{17,1},{19,3},{4,20},{6,... | collective-permute-start | bytes 1769480 | tf_op jit(solution)/shard_map/ppermute | solution.py:334
  27.3 25.7 %collective-permute-start.3 = (bf16[48,6144]{1,0:T(8,128)(2,1)S(1)}, bf16[48,6144]{1,0:T(8,128)(2,1)S(1)}, u32[]{:S(2)}, u32[]{:S(2)}) collective-permute-start(bf16[48,6144]{1,0:T(8,128)(2,1)S(1)} %collective-permute-done.refs_1_), channel_id=1, source_target_pairs={{0,2},{2,0},{16,18},{18,16},{1,3},{3,1},{17,19},{19,17},{4,6},{6,4... | collective-permute-start | bytes 1769480 | tf_op jit(solution)/shard_map/ppermute | solution.py:334
  27.9 25.2 %collective-permute-start.2 = (bf16[48,6144]{1,0:T(8,128)(2,1)S(1)}, bf16[48,6144]{1,0:T(8,128)(2,1)}, u32[]{:S(2)}, u32[]{:S(2)}) collective-permute-start(bf16[48,6144]{1,0:T(8,128)(2,1)S(1)} %collective-permute-done.refs_1_), channel_id=1, source_target_pairs={{0,4},{4,8},{8,12},{12,0},{1,5},{5,9},{9,13},{13,1},{2,6},{6,10},{... | collective-permute-start | bytes 1769480 | tf_op jit(solution)/shard_map/ppermute | solution.py:325
  41.5 11.5 %copy-start.13 = (bf16[48,6144]{1,0:T(8,128)(2,1)}, bf16[48,6144]{1,0:T(8,128)(2,1)S(1)}, u32[]{:S(2)}) copy-start(bf16[48,6144]{1,0:T(8,128)(2,1)S(1)} %collective-permute-done.5.refs_4_) | copy-start | bytes 1769476
  52.9 0.8 copy-start.14
  53.0 0.9 copy-start.15
  53.9 58.2 %all-to-all-start.1 = ((bf16[8,192,768]{2,1,0:T(8,128)(2,1)}), bf16[8,192,768]{2,1,0:T(8,128)(2,1)S(1)}, u32[]{:S(2)}, u32[]{:S(2)}) async-start(bf16[8,192,768]{2,1,0:T(8,128)(2,1)} %place_rows.1), calls=%async_computation.1 | async-start | bytes 4718592 | tf_op jit(solution)/shard_map/all_to_all | solution.py:415
  57.8 6.4 %copy-start.7 = (bf16[192,3,384]{2,0,1:T(8,128)(2,1)S(1)}, bf16[192,3,384]{2,0,1:T(8,128)(2,1)}, u32[]{:S(2)}) copy-start(bf16[192,3,384]{2,0,1:T(8,128)(2,1)} %param.14) | copy-start | bytes 1327108
  58.7 5.6 %copy-start.5 = (bf16[192,2,1536]{2,1,0:T(2,128)(2,1)S(1)}, bf16[192,2,1536]{2,1,0:T(2,128)(2,1)}, u32[]{:S(2)}) copy-start(bf16[192,2,1536]{2,1,0:T(2,128)(2,1)} %param.16) | copy-start | bytes 3538948
  60.7 53.5 %collective-permute-start.8 = (bf16[96,6144]{1,0:T(8,128)(2,1)}, bf16[96,6144]{1,0:T(8,128)(2,1)}, u32[]{:S(2)}, u32[]{:S(2)}) collective-permute-start(bf16[96,6144]{1,0:T(8,128)(2,1)} %constant_dynamic-update-slice_fusion.refs_5_), channel_id=1, source_target_pairs={{0,18},{2,16},{16,2},{18,0},{1,19},{3,17},{17,3},{19,1},{4,22},{6,... | collective-permute-start | bytes 3538952 | tf_op jit(solution)/shard_map/ppermute | solution.py:334
  62.5 52.8 %collective-permute-start.7 = (bf16[96,6144]{1,0:T(8,128)(2,1)}, bf16[96,6144]{1,0:T(8,128)(2,1)}, u32[]{:S(2)}, u32[]{:S(2)}) collective-permute-start(bf16[96,6144]{1,0:T(8,128)(2,1)} %constant_dynamic-update-slice_fusion.refs_5_), channel_id=1, source_target_pairs={{0,16},{2,18},{16,0},{18,2},{1,17},{3,19},{17,1},{19,3},{4,20},{6,... | collective-permute-start | bytes 3538952 | tf_op jit(solution)/shard_map/ppermute | solution.py:334
  63.7 51.7 %collective-permute-start.6 = (bf16[96,6144]{1,0:T(8,128)(2,1)}, bf16[96,6144]{1,0:T(8,128)(2,1)}, u32[]{:S(2)}, u32[]{:S(2)}) collective-permute-start(bf16[96,6144]{1,0:T(8,128)(2,1)} %constant_dynamic-update-slice_fusion.refs_5_), channel_id=1, source_target_pairs={{0,2},{2,0},{16,18},{18,16},{1,3},{3,1},{17,19},{19,17},{4,6},{6,4... | collective-permute-start | bytes 3538952 | tf_op jit(solution)/shard_map/ppermute | solution.py:334
  64.3 1.1 copy-start.6
  64.3 1.1 copy-start.8
  115.4 10.9 %collective-permute-start.9 = (bf16[256,768]{1,0:T(8,128)(2,1)S(1)}, bf16[256,768]{1,0:T(8,128)(2,1)S(1)}, u32[]{:S(2)}, u32[]{:S(2)}) collective-permute-start(bf16[256,768]{1,0:T(8,128)(2,1)S(1)} %get-tuple-element.37), channel_id=1, source_target_pairs={{0,2},{2,0},{1,3},{3,1},{4,6},{6,4},{5,7},{7,5},{8,10},{10,8},{9,1... | collective-permute-start | bytes 1179656 | tf_op jit(solution)/shard_map/ppermute | solution.py:419
  127.8 14.2 %copy-start.1 = (bf16[512,768]{1,0:T(8,128)(2,1)}, bf16[512,768]{1,0:T(8,128)(2,1)S(1)}, u32[]{:S(2)}) copy-start(bf16[512,768]{1,0:T(8,128)(2,1)S(1)} %weave_steps.1.tok_ref) | copy-start | bytes 2359300
  127.8 2.4 %collective-permute-start.10 = (bf16[512,768]{1,0:T(8,128)(2,1)S(1)}, bf16[512,768]{1,0:T(8,128)(2,1)S(1)}, u32[]{:S(2)}, u32[]{:S(2)}) collective-permute-start(bf16[512,768]{1,0:T(8,128)(2,1)S(1)} %weave_steps.1.tok_ref), channel_id=1, source_target_pairs={{0,1},{1,0},{2,3},{3,2},{4,5},{5,4},{6,7},{7,6},{8,9},{9,8},{10,11... | collective-permute-start | bytes 2359304 | tf_op jit(solution)/shard_map/ppermute | solution.py:429
  130.2 0.9 copy-start.11
  142.0 11.7 %collective-permute-start.11 = (bf16[512,768]{1,0:T(8,128)(2,1)}, bf16[512,768]{1,0:T(8,128)(2,1)S(1)}, u32[]{:S(2)}, u32[]{:S(2)}) collective-permute-start(bf16[512,768]{1,0:T(8,128)(2,1)} %layer.3), channel_id=1, source_target_pairs={{0,1},{1,0},{2,3},{3,2},{4,5},{5,4},{6,7},{7,6},{8,9},{9,8},{10,11... | collective-permute-start | bytes 2359304 | tf_op jit(solution)/shard_map/ppermute | solution.py:431
  142.2 11.5 %copy-start.2 = (bf16[512,768]{1,0:T(8,128)(2,1)S(1)}, bf16[512,768]{1,0:T(8,128)(2,1)}, u32[]{:S(2)}) copy-start(bf16[512,768]{1,0:T(8,128)(2,1)} %copy-done.1) | copy-start | bytes 2359300
  153.7 1.4 copy-start

commit v13 on v12

--- a/solution.py
+++ b/solution.py
@@ -224,25 +224,30 @@
 def layer_kernel(plan, hidden_width, tok_ref, *refs):
     pieces, (out_ref, w_ref, norm_ref, ctx_ref, acc_ref, sems) = refs[:-6], refs[-6:]
     copies = {}
-    for number, (section, piece, row, at, size) in enumerate(plan):
+    for number, (section, piece, source, row, at, size) in enumerate(plan):
         copy = pltpu.make_async_copy(
-            pieces[piece].at[:, pl.ds(at, size)],
+            pieces[piece].at[:, pl.ds(source, size)],
             w_ref.at[pl.ds(row, pieces[piece].shape[0]), pl.ds(at, size)],
             sems.at[number],
         )
-        copy.start()
         copies.setdefault(section, []).append(copy)
+
+    def start(section):
+        for copy in copies[section]:
+            copy.start()
 
     def ready(section):
         for copy in copies[section]:
             copy.wait()
 
+    start(0)
     heads_width = ctx_ref.shape[1]
     gate_at, up_at, out_at, down_at, _ = layer_columns(heads_width, hidden_width)
     tokens = tok_ref[...].astype(F32)
     scale = lax.rsqrt(jnp.mean(tokens * tokens, axis=1, keepdims=True) + EPS)
     norm_ref[...] = (tokens * scale).astype(BF16)
     ready(0)
+    start(1)
     attention(norm_ref[...], w_ref[:, :gate_at], heads_width, ctx_ref)
     ready(1)
     acc_ref[...] = dot_t(ctx_ref[...], w_ref[:, out_at:down_at])
@@ -267,10 +272,10 @@
     gate_at, _, _, _, columns = layer_columns(heads_width, hidden_width)
     plan = []
     for section, (left, right) in enumerate([(0, gate_at), (gate_at, columns)]):
-        row = 0
-        for number, piece in enumerate(pieces):
-            plan.append((section, number, row, left, right - left))
-            row += piece.shape[0]
+        for number, (array, row, at) in enumerate(pieces):
+            low, high = max(left, at), min(right, at + array.shape[1])
+            if low < high:
+                plan.append((section, number, low - at, row, low, high - low))
     return pl.pallas_call(
         functools.partial(layer_kernel, plan, hidden_width),
         out_shape=jax.ShapeDtypeStruct((rows, width), out_type),
@@ -290,7 +295,7 @@
             transcendentals=rows * hidden_width,
         ),
         name="layer",
-    )(tokens, *pieces)
+    )(tokens, *[array for array, _, _ in pieces])
 
 
 def finish_kernel(tok_ref, sum_ref, got_ref, order_ref, out_ref):
@@ -333,6 +338,16 @@
         pairs = [(place, place ^ far) for place in range(n_share)]
         places.append(lax.ppermute(shares, ("groups", "slots"), pairs))
     return places
+
+
+def to_other_places_by_halves(shares):
+    swap = [(0, 1), (1, 0)]
+    by_slot = lax.ppermute(shares, "slots", swap)
+    by_group = lax.ppermute(shares, "groups", swap)
+    cut = shares.shape[1] // 2
+    left = lax.ppermute(by_slot[:, :cut], "groups", swap)
+    right = lax.ppermute(by_group[:, cut:], "slots", swap)
+    return [shares, by_slot, by_group, left, right]
 
 
 def arrival_order(width, n_share):
@@ -410,18 +425,21 @@
         blocks = place_rows(owner, obs_feat, n_owners, capacity)
         above, opposite = along_cells(share_rows, 1), along_cells(below, -1)
         blocks, above, opposite, first = lax.optimization_barrier((blocks, above, opposite, first))
-        second = to_other_places(jnp.concatenate([above, opposite], axis=0))
+        second = to_other_places_by_halves(jnp.concatenate([above, opposite], axis=0))
         shard = side_by_side(*local_weights)
         got = lax.all_to_all(blocks, ("cells", "mp"), split_axis=0, concat_axis=0, tiled=True)
-        got, shard = lax.optimization_barrier((got, shard))
+        got, shard, second = lax.optimization_barrier((got, shard, second))
         keep, send = pool_rows(my_slot.reshape(1), embed, codes, got, capacity, slot_dev)
-        send, second = lax.optimization_barrier((send, second))
         other = lax.ppermute(send, "slots", [(0, 1), (1, 0)])
-        pieces = [shard] + first + second
+        pieces, row = [], 0
+        for array in [shard] + first + second[:3]:
+            pieces.append((array, row, 0))
+            row += array.shape[0]
+        pieces += [(second[3], row, 0), (second[4], row, second[3].shape[1])]
         tokens = weave_steps(my_slot.reshape(1), order, keep, other, slot_dev)
     else:
         order = jnp.arange(width, dtype=jnp.int32)
-        pieces = [lax.all_gather(share_rows, ("cells", "groups", "slots"), axis=0, tiled=True)]
+        pieces = [(lax.all_gather(share_rows, ("cells", "groups", "slots"), axis=0, tiled=True), 0, 0)]
         tokens = tokens_by_exchanges(owner, position, obs_feat, time_embed, my_slot, capacity, slot_dev)
 
     swap = [(0, 1), (1, 0)]

time: 157 us -> 157 us (level)
  local copies, waits for them, and re-layouts: 11.2 us -> 9.47 us
  starting transfers between devices: 17.5 us -> 19.1 us
    ppermute x0 -> x4, waiting for transfers between devices: none -> 36.6 us  [the longest x1 25.5 us: to_other_places_by_halves(): by_group = lax.ppermute(shares, 'groups', swap)]
    all_to_all x1, waiting for transfers between devices: 45.2 us -> 8.8 us  [on_device(): lax.all_to_all(blocks, ('cells', 'mp'), split_axis=0, concat_axis=0, tile...]
    ppermute x0 -> x4, starting transfers between devices: none -> 4.92 us  [the longest x1 1.58 us: to_other_places_by_halves(): by_group = lax.ppermute(shares, 'groups', swap)]
    ppermute x6 -> x3, starting transfers between devices: 6.98 us -> 3.49 us  [to_other_places(): places.append(lax.ppermute(shares, ('groups', 'slots'), pairs))]
    ppermute x6 -> x3, waiting for transfers between devices: 15.5 us -> 14.4 us  [to_other_places(): places.append(lax.ppermute(shares, ('groups', 'slots'), pairs))]
    unnamed x36 -> x44, local copies, waits for them, and re-layouts: 6.19 us -> 5.18 us
  transfers between devices with their start and end apart: 13 -> 14, of which waited for: 9 -> 10; matrix products, arithmetic and copies ran while one was open for 3% -> 2% of each run, Pallas kernels for 11% -> 10%
where the time goes in v13:
time: 157 us; the launch traced here: 156 us
  waiting for transfers between devices  78.6 us (50%)
  Pallas kernels  32.3 us (21%)
  starting transfers between devices  19.1 us (12%)
  blocking collectives  14.1 us (9%)
  local copies, waits for them, and re-layouts  9.47 us (6%)
  other arithmetic  1.75 us (1%)
    ppermute x1, waiting for transfers between devices, to_other_places_by_halves(): by_group = lax.ppermute(shares, 'groups', swap)  25.5 us
    pallas_call x2, Pallas kernels, layer(): pl.pallas_call(functools.partial(layer_kernel, plan, hidden_width), out_s...  23.2 us
    ppermute x3, waiting for transfers between devices, to_other_places(): places.append(lax.ppermute(shares, ('groups', 'slots'), pairs))  14.4 us
    all_to_all x1, blocking collectives, on_device(): lax.all_to_all(codes, ('cells', 'mp'), split_axis=0, concat_axis=0, tiled...  14.1 us
    ppermute x1, waiting for transfers between devices, to_other_places_by_halves(): right = lax.ppermute(by_group[:, cut:], 'slots', swap)  10.4 us
    ppermute x1, waiting for transfers between devices, on_device(): other = lax.ppermute(send, 'slots', [(0, 1), (1, 0)])  9.13 us
    all_to_all x1, waiting for transfers between devices, on_device(): lax.all_to_all(blocks, ('cells', 'mp'), split_axis=0, concat_axis=0, tile...  8.8 us
    ppermute x3, waiting for transfers between devices, along_cells(): lax.ppermute(values, 'cells', [(j, (j - distance) % n_cells) for j in ran...  7.42 us
  transfers between devices with their start and end apart: 14, of which 10 were waited for; matrix products, arithmetic and copies ran while one was open for 2% of the time, Pallas kernels for 10%

profile of v13, /device:TPU:0, one launch (start us, length us, event | category | flops | bytes accessed | tf_op | source)
XLA Modules:
  0.0 156.3 jit_solution(15775493217490203520)
XLA Ops:
  0.0 0.8 dynamic-slice_bitcast_fusion.2
  0.8 0.9 dynamic-slice_bitcast_fusion.1
  1.7 0.9 dynamic-slice_bitcast_fusion
  2.7 0.0 copy-start.4
  2.7 0.0 copy-start.3
  2.7 1.2 constant_dynamic-slice_fusion
  4.0 3.1 %collective-permute-start = (bf16[48,6144]{1,0:T(8,128)(2,1)S(1)}, bf16[48,6144]{1,0:T(8,128)(2,1)S(1)}, u32[]{:S(2)}, u32[]{:S(2)}) collective-permute-start(bf16[48,6144]{1,0:T(8,128)(2,1)S(1)} %pad_maximum_fusion.1), channel_id=1, source_target_pairs={{0,4},{4,8},{8,12},{12,0},{1,5},{5,9},{9,13},{13,1},{2,6},{6,10},{... | collective-permute-start | bytes 1769480 | tf_op jit(solution)/shard_map/ppermute | solution.py:330
  7.8 0.7 place_codes.1
  8.5 14.1 %all_to_all.10.code_ref = s32[8,1,192]{2,1,0:T(1,128)S(1)} all-to-all(s32[8,1,192]{2,1,0:T(1,128)S(1)} %get-tuple-element.27), channel_id=1, replica_groups=mesh['groups'=2,'cells'=4,'slots'=2,'mp'=2] {'cells','mp'}, dimensions={0} | all-to-all | bytes 12288 | tf_op jit(solution)/shard_map/all_to_all | solution.py:422
  22.6 1.7 %collective-permute-start.1 = (bf16[48,6144]{1,0:T(8,128)(2,1)S(1)}, bf16[48,6144]{1,0:T(8,128)(2,1)S(1)}, u32[]{:S(2)}, u32[]{:S(2)}) collective-permute-start(bf16[48,6144]{1,0:T(8,128)(2,1)S(1)} %pad_maximum_fusion.1), channel_id=1, source_target_pairs={{0,12},{4,0},{8,4},{12,8},{1,13},{5,1},{9,5},{13,9},{2,14},{6,2},{... | collective-permute-start | bytes 1769480 | tf_op jit(solution)/shard_map/ppermute | solution.py:330
  24.4 2.4 %collective-permute-start.5 = (bf16[48,6144]{1,0:T(8,128)(2,1)S(1)}, bf16[48,6144]{1,0:T(8,128)(2,1)S(1)}, u32[]{:S(2)}, u32[]{:S(2)}) collective-permute-start(bf16[48,6144]{1,0:T(8,128)(2,1)S(1)} %collective-permute-done.refs_1_), channel_id=1, source_target_pairs={{0,18},{2,16},{16,2},{18,0},{1,19},{3,17},{17,3},{19,1},{4,22},{6,... | collective-permute-start | bytes 1769480 | tf_op jit(solution)/shard_map/ppermute | solution.py:339
  26.8 0.5 collective-permute-start.4
  27.3 0.5 collective-permute-start.3
  27.9 0.3 collective-permute-start.2
  28.2 3.0 %place_rows.1 = bf16[8,192,768]{2,1,0:T(8,128)(2,1)} custom-call(s32[1,512]{1,0:T(1,128)S(1)} %bitcast.22, bf16[512,768]{1,0:T(8,128)(2,1)S(1)} %copy-done.3), custom_call_target="tpu_custom_call" | custom-call | flops 1207959552 | bytes 3145728 | tf_op jit(solution)/shard_map/place_rows/pallas_call | solution.py:98
  31.2 7.4 %collective-permute-done.1 = bf16[48,6144]{1,0:T(8,128)(2,1)S(1)} collective-permute-done((bf16[48,6144]{1,0:T(8,128)(2,1)S(1)}, bf16[48,6144]{1,0:T(8,128)(2,1)S(1)}, u32[]{:S(2)}, u32[]{:S(2)}) %collective-permute-start.1) | collective-permute-done | bytes 589856 | tf_op jit(solution)/shard_map/ppermute | solution.py:330
  38.6 2.9 %collective-permute-done.5.refs_4_ = bf16[48,6144]{1,0:T(8,128)(2,1)S(1)} collective-permute-done((bf16[48,6144]{1,0:T(8,128)(2,1)S(1)}, bf16[48,6144]{1,0:T(8,128)(2,1)S(1)}, u32[]{:S(2)}, u32[]{:S(2)}) %collective-permute-start.5) | collective-permute-done | bytes 589856 | tf_op jit(solution)/shard_map/ppermute | solution.py:339
  41.5 11.4 %collective-permute-done.4.refs_3_ = bf16[48,6144]{1,0:T(8,128)(2,1)S(1)} collective-permute-done((bf16[48,6144]{1,0:T(8,128)(2,1)S(1)}, bf16[48,6144]{1,0:T(8,128)(2,1)S(1)}, u32[]{:S(2)}, u32[]{:S(2)}) %collective-permute-start.4) | collective-permute-done | bytes 589856 | tf_op jit(solution)/shard_map/ppermute | solution.py:339
  52.9 0.1 collective-permute-done.3.refs_2_
  53.0 0.7 copy-done.17
  53.7 0.2 copy-done.18
  53.9 3.8 %all-to-all-start.1 = ((bf16[8,192,768]{2,1,0:T(8,128)(2,1)}), bf16[8,192,768]{2,1,0:T(8,128)(2,1)S(1)}, u32[]{:S(2)}, u32[]{:S(2)}) async-start(bf16[8,192,768]{2,1,0:T(8,128)(2,1)} %place_rows.1), calls=%async_computation.1 | async-start | bytes 4718592 | tf_op jit(solution)/shard_map/all_to_all | solution.py:430
  57.7 0.0 copy-start.7
  57.8 0.0 copy-start.5
  57.8 1.2 constant_dynamic-update-slice_fusion.refs_5_
  59.0 1.6 %collective-permute-start.7 = (bf16[96,6144]{1,0:T(8,128)(2,1)S(1)}, bf16[96,6144]{1,0:T(8,128)(2,1)S(1)}, u32[]{:S(2)}, u32[]{:S(2)}) collective-permute-start(bf16[96,6144]{1,0:T(8,128)(2,1)S(1)} %constant_dynamic-update-slice_fusion.refs_5_), channel_id=1, source_target_pairs={{0,16},{16,0},{1,17},{17,1},{2,18},{18,2},{3,19},{19,3},{4,20},{20... | collective-permute-start | bytes 3538952 | tf_op jit(solution)/shard_map/ppermute | solution.py:346
  60.6 0.8 collective-permute-start.6
  61.5 0.1 copy.17
  61.6 25.5 %collective-permute-done.7.refs_7_ = bf16[96,6144]{1,0:T(8,128)(2,1)S(1)} collective-permute-done((bf16[96,6144]{1,0:T(8,128)(2,1)S(1)}, bf16[96,6144]{1,0:T(8,128)(2,1)S(1)}, u32[]{:S(2)}, u32[]{:S(2)}) %collective-permute-start.7) | collective-permute-done | bytes 1179680 | tf_op jit(solution)/shard_map/ppermute | solution.py:346
  87.2 1.6 collective-permute-start.9
  88.8 1.0 collective-permute-start.8
  89.8 1.6 %pad_maximum_fusion.refs_0_ = bf16[192,6144]{1,0:T(8,128)(2,1)} fusion(bf16[192,1536]{1,0:T(8,128)(2,1)S(1)} %bitcast.29, bf16[192,384]{1,0:T(8,128)(2,1)S(1)} %bitcast.32, bf16[192,3072]{1,0:T(8,128)(2,1)S(1)} %bitcast.24, bf16[192,1152]{1,0:T(8,128)(2,1)S(1)} %bitcast.26), kind=kLoop, calls=%fused_computation | loop fusion | flops 9437184 | bytes 4718592 | tf_op jit(solution)/shard_map/concatenate | solution.py:325
  91.5 10.4 %collective-permute-done.9.refs_9_ = bf16[96,3072]{1,0:T(8,128)(2,1)S(1)} collective-permute-done((bf16[96,3072]{1,0:T(8,128)(2,1)S(1)}, bf16[96,3072]{1,0:T(8,128)(2,1)S(1)}, u32[]{:S(2)}, u32[]{:S(2)}) %collective-permute-start.9) | collective-permute-done | bytes 589856 | tf_op jit(solution)/shard_map/ppermute | solution.py:349
  101.9 0.8 copy-done.19
  102.7 0.6 collective-permute-done.8.refs_8_
  103.3 8.8 %all-to-all-done.1.got_ref = bf16[8,192,768]{2,1,0:T(8,128)(2,1)S(1)} async-done(((bf16[8,192,768]{2,1,0:T(8,128)(2,1)}), bf16[8,192,768]{2,1,0:T(8,128)(2,1)S(1)}, u32[]{:S(2)}, u32[]{:S(2)}) %all-to-all-start.1) | async-done | bytes 2359328 | tf_op jit(solution)/shard_map/all_to_all | solution.py:430
  112.1 2.1 %pool_rows.1 = (bf16[256,768]{1,0:T(8,128)(2,1)S(1)}, bf16[256,768]{1,0:T(8,128)(2,1)S(1)}) custom-call(s32[1]{0:T(128)} %bitcast.slot_ref, bf16[8,768]{1,0:T(8,128)(2,1)S(1)} %get-tuple-element.26.embed_ref, s32[8,1,192]{2,1,0:T(1,128)S(1)} %all_to_all.10.code_ref, bf16[8,192,768]{2,1,0:T(8,128)(2,1)S(1)} %all-to-all-done.1.got_ref), custom_call_target="tpu_custom_call" | custom-call | flops 1207959552 | bytes 2359296 | tf_op jit(solution)/shard_map/pool_rows/pallas_call | solution.py:138
  114.2 1.6 collective-permute-start.10
  115.8 9.1 %collective-permute-done.10.got_ref = bf16[256,768]{1,0:T(8,128)(2,1)S(1)} collective-permute-done((bf16[256,768]{1,0:T(8,128)(2,1)S(1)}, bf16[256,768]{1,0:T(8,128)(2,1)S(1)}, u32[]{:S(2)}, u32[]{:S(2)}) %collective-permute-start.10) | collective-permute-done | bytes 393248 | tf_op jit(solution)/shard_map/ppermute | solution.py:433
  124.9 1.5 weave_steps.1.tok_ref
  126.4 0.1 collective-permute-start.11
  126.5 2.3 %collective-permute-done.11.tok_ref = bf16[512,768]{1,0:T(8,128)(2,1)S(1)} collective-permute-done((bf16[512,768]{1,0:T(8,128)(2,1)S(1)}, bf16[512,768]{1,0:T(8,128)(2,1)S(1)}, u32[]{:S(2)}, u32[]{:S(2)}) %collective-permute-start.11) | collective-permute-done | bytes 786464 | tf_op jit(solution)/shard_map/ppermute | solution.py:447
  128.8 0.9 copy-done.14
  129.6 11.4 %layer.3 = bf16[512,768]{1,0:T(8,128)(2,1)} custom-call(bf16[512,768]{1,0:T(8,128)(2,1)} %copy-done.14, bf16[192,6144]{1,0:T(8,128)(2,1)} %pad_maximum_fusion.refs_0_, bf16[48,6144]{1,0:T(8,128)(2,1)} %copy-done.15, bf16[48,6144]{1,0:T(8,128)(2,1)} %copy-done.18, bf16[48,6144]{1,0:T(8,128)(2,1)} %copy-done.17, bf16[48,6144]{1,0:T(8,128)(2,1)} %copy-done.16, ...), custom_call_target="tpu_custom_call" | custom-call | flops 4831838208 | bytes 11796480 | tf_op jit(solution)/shard_map/layer/pallas_call | solution.py:279
  141.1 0.2 collective-permute-start.12
  141.3 11.8 %layer.2.sum_ref = f32[512,768]{1,0:T(8,128)} custom-call(bf16[512,768]{1,0:T(8,128)(2,1)} %copy-done.1, bf16[192,6144]{1,0:T(8,128)(2,1)} %pad_maximum_fusion.refs_0_, bf16[48,6144]{1,0:T(8,128)(2,1)} %copy-done.15, bf16[48,6144]{1,0:T(8,128)(2,1)} %copy-done.18, bf16[48,6144]{1,0:T(8,128)(2,1)} %copy-done.17, bf16[48,6144]{1,0:T(8,128)(2,1)} %copy-done.16, ...), custom_call_target="tpu_custom_call" | custom-call | flops 4831838208 | bytes 11796480 | tf_op jit(solution)/shard_map/layer/pallas_call | solution.py:279
  153.1 1.4 copy-done
  154.5 1.8 %finish.1 = bf16[512,768]{1,0:T(8,128)(2,1)} custom-call(bf16[512,768]{1,0:T(8,128)(2,1)S(1)} %copy-done.2, f32[512,768]{1,0:T(8,128)S(1)} %copy-done, bf16[512,768]{1,0:T(8,128)(2,1)S(1)} %collective-permute-done.12.got_ref, s32[1,768]{1,0:T(1,128)S(1)} %compare_select_fusion.6.order_ref), custom_call_target="tpu_custom_call" | custom-call | flops 603979776 | bytes 3932160 | tf_op jit(solution)/shard_map/finish/pallas_call | solution.py:310
  (44 shorter events, 0.4 us)
Async XLA Ops:
  2.6 5.1 %copy-start.12 = (s32[512]{0:T(512)S(1)}, s32[512]{0:T(512)}, u32[]{:S(2)}) copy-start(s32[512]{0:T(512)} %param.11) | copy-start | bytes 6148
  2.6 5.1 %copy-start.13 = (s32[512]{0:T(512)S(1)}, s32[512]{0:T(512)}, u32[]{:S(2)}) copy-start(s32[512]{0:T(512)} %param.10) | copy-start | bytes 6148
  2.7 5.1 %copy-start.4 = (bf16[8,768]{1,0:T(8,128)(2,1)S(1)}, bf16[8,768]{1,0:T(8,128)(2,1)}, u32[]{:S(2)}) copy-start(bf16[8,768]{1,0:T(8,128)(2,1)} %time_ref.1) | copy-start | bytes 36868
  2.7 25.5 %copy-start.3 = (bf16[512,768]{1,0:T(8,128)(2,1)S(1)}, bf16[512,768]{1,0:T(8,128)(2,1)}, u32[]{:S(2)}) copy-start(bf16[512,768]{1,0:T(8,128)(2,1)} %feat_ref.1) | copy-start | bytes 2359300
  4.0 18.6 %collective-permute-start = (bf16[48,6144]{1,0:T(8,128)(2,1)S(1)}, bf16[48,6144]{1,0:T(8,128)(2,1)S(1)}, u32[]{:S(2)}, u32[]{:S(2)}) collective-permute-start(bf16[48,6144]{1,0:T(8,128)(2,1)S(1)} %pad_maximum_fusion.1), channel_id=1, source_target_pairs={{0,4},{4,8},{8,12},{12,0},{1,5},{5,9},{9,13},{13,1},{2,6},{6,10},{... | collective-permute-start | bytes 1769480 | tf_op jit(solution)/shard_map/ppermute | solution.py:330
  22.6 8.5 %copy-start.15 = (bf16[48,6144]{1,0:T(8,128)(2,1)}, bf16[48,6144]{1,0:T(8,128)(2,1)S(1)}, u32[]{:S(2)}) copy-start(bf16[48,6144]{1,0:T(8,128)(2,1)S(1)} %collective-permute-done.refs_1_) | copy-start | bytes 1769476
  22.6 16.0 %collective-permute-start.1 = (bf16[48,6144]{1,0:T(8,128)(2,1)S(1)}, bf16[48,6144]{1,0:T(8,128)(2,1)S(1)}, u32[]{:S(2)}, u32[]{:S(2)}) collective-permute-start(bf16[48,6144]{1,0:T(8,128)(2,1)S(1)} %pad_maximum_fusion.1), channel_id=1, source_target_pairs={{0,12},{4,0},{8,4},{12,8},{1,13},{5,1},{9,5},{13,9},{2,14},{6,2},{... | collective-permute-start | bytes 1769480 | tf_op jit(solution)/shard_map/ppermute | solution.py:330
  24.4 17.2 %collective-permute-start.5 = (bf16[48,6144]{1,0:T(8,128)(2,1)S(1)}, bf16[48,6144]{1,0:T(8,128)(2,1)S(1)}, u32[]{:S(2)}, u32[]{:S(2)}) collective-permute-start(bf16[48,6144]{1,0:T(8,128)(2,1)S(1)} %collective-permute-done.refs_1_), channel_id=1, source_target_pairs={{0,18},{2,16},{16,2},{18,0},{1,19},{3,17},{17,3},{19,1},{4,22},{6,... | collective-permute-start | bytes 1769480 | tf_op jit(solution)/shard_map/ppermute | solution.py:339
  26.8 26.1 %collective-permute-start.4 = (bf16[48,6144]{1,0:T(8,128)(2,1)S(1)}, bf16[48,6144]{1,0:T(8,128)(2,1)S(1)}, u32[]{:S(2)}, u32[]{:S(2)}) collective-permute-start(bf16[48,6144]{1,0:T(8,128)(2,1)S(1)} %collective-permute-done.refs_1_), channel_id=1, source_target_pairs={{0,16},{2,18},{16,0},{18,2},{1,17},{3,19},{17,1},{19,3},{4,20},{6,... | collective-permute-start | bytes 1769480 | tf_op jit(solution)/shard_map/ppermute | solution.py:339
  27.3 25.7 %collective-permute-start.3 = (bf16[48,6144]{1,0:T(8,128)(2,1)S(1)}, bf16[48,6144]{1,0:T(8,128)(2,1)S(1)}, u32[]{:S(2)}, u32[]{:S(2)}) collective-permute-start(bf16[48,6144]{1,0:T(8,128)(2,1)S(1)} %collective-permute-done.refs_1_), channel_id=1, source_target_pairs={{0,2},{2,0},{16,18},{18,16},{1,3},{3,1},{17,19},{19,17},{4,6},{6,4... | collective-permute-start | bytes 1769480 | tf_op jit(solution)/shard_map/ppermute | solution.py:339
  27.9 25.2 %collective-permute-start.2 = (bf16[48,6144]{1,0:T(8,128)(2,1)S(1)}, bf16[48,6144]{1,0:T(8,128)(2,1)}, u32[]{:S(2)}, u32[]{:S(2)}) collective-permute-start(bf16[48,6144]{1,0:T(8,128)(2,1)S(1)} %collective-permute-done.refs_1_), channel_id=1, source_target_pairs={{0,4},{4,8},{8,12},{12,0},{1,5},{5,9},{9,13},{13,1},{2,6},{6,10},{... | collective-permute-start | bytes 1769480 | tf_op jit(solution)/shard_map/ppermute | solution.py:330
  41.5 11.5 %copy-start.16 = (bf16[48,6144]{1,0:T(8,128)(2,1)}, bf16[48,6144]{1,0:T(8,128)(2,1)S(1)}, u32[]{:S(2)}) copy-start(bf16[48,6144]{1,0:T(8,128)(2,1)S(1)} %collective-permute-done.5.refs_4_) | copy-start | bytes 1769476
  52.9 0.8 copy-start.17
  53.0 0.9 copy-start.18
  53.9 58.2 %all-to-all-start.1 = ((bf16[8,192,768]{2,1,0:T(8,128)(2,1)}), bf16[8,192,768]{2,1,0:T(8,128)(2,1)S(1)}, u32[]{:S(2)}, u32[]{:S(2)}) async-start(bf16[8,192,768]{2,1,0:T(8,128)(2,1)} %place_rows.1), calls=%async_computation.1 | async-start | bytes 4718592 | tf_op jit(solution)/shard_map/all_to_all | solution.py:430
  57.7 3.7 %copy-start.7 = (bf16[192,3,384]{2,0,1:T(8,128)(2,1)S(1)}, bf16[192,3,384]{2,0,1:T(8,128)(2,1)}, u32[]{:S(2)}) copy-start(bf16[192,3,384]{2,0,1:T(8,128)(2,1)} %param.14) | copy-start | bytes 1327108
  57.8 3.7 %copy-start.5 = (bf16[192,2,1536]{2,1,0:T(2,128)(2,1)S(1)}, bf16[192,2,1536]{2,1,0:T(2,128)(2,1)}, u32[]{:S(2)}) copy-start(bf16[192,2,1536]{2,1,0:T(2,128)(2,1)} %param.16) | copy-start | bytes 3538948
  59.0 2.6 %copy-start.10 = (bf16[96,6144]{1,0:T(8,128)(2,1)}, bf16[96,6144]{1,0:T(8,128)(2,1)S(1)}, u32[]{:S(2)}) copy-start(bf16[96,6144]{1,0:T(8,128)(2,1)S(1)} %constant_dynamic-update-slice_fusion.refs_5_) | copy-start | bytes 3538948
  59.0 28.1 %collective-permute-start.7 = (bf16[96,6144]{1,0:T(8,128)(2,1)S(1)}, bf16[96,6144]{1,0:T(8,128)(2,1)S(1)}, u32[]{:S(2)}, u32[]{:S(2)}) collective-permute-start(bf16[96,6144]{1,0:T(8,128)(2,1)S(1)} %constant_dynamic-update-slice_fusion.refs_5_), channel_id=1, source_target_pairs={{0,16},{16,0},{1,17},{17,1},{2,18},{18,2},{3,19},{19,3},{4,20},{20... | collective-permute-start | bytes 3538952 | tf_op jit(solution)/shard_map/ppermute | solution.py:346
  60.6 28.2 %collective-permute-start.6 = (bf16[96,6144]{1,0:T(8,128)(2,1)S(1)}, bf16[96,6144]{1,0:T(8,128)(2,1)S(1)}, u32[]{:S(2)}, u32[]{:S(2)}) collective-permute-start(bf16[96,6144]{1,0:T(8,128)(2,1)S(1)} %constant_dynamic-update-slice_fusion.refs_5_), channel_id=1, source_target_pairs={{0,2},{2,0},{1,3},{3,1},{4,6},{6,4},{5,7},{7,5},{8,10},{10,8},{9,1... | collective-permute-start | bytes 3538952 | tf_op jit(solution)/shard_map/ppermute | solution.py:345
  61.6 28.2 %copy-start.6 = (bf16[1536,192]{0,1:T(8,128)(2,1)S(1)}, bf16[1536,192]{0,1:T(8,128)(2,1)}, u32[]{:S(2)}) copy-start(bf16[1536,192]{0,1:T(8,128)(2,1)} %param.17) | copy-start | bytes 1769476
  61.6 28.2 %copy-start.11 = (bf16[384,192]{0,1:T(8,128)(2,1)S(1)}, bf16[384,192]{0,1:T(8,128)(2,1)}, u32[]{:S(2)}) copy-start(bf16[384,192]{0,1:T(8,128)(2,1)} %param.15) | copy-start | bytes 442372
  87.2 1.7 %copy-start.8 = (bf16[96,6144]{1,0:T(8,128)(2,1)}, bf16[96,6144]{1,0:T(8,128)(2,1)S(1)}, u32[]{:S(2)}) copy-start(bf16[96,6144]{1,0:T(8,128)(2,1)S(1)} %collective-permute-done.7.refs_7_) | copy-start | bytes 3538948
  87.2 14.7 %collective-permute-start.9 = (bf16[96,3072]{1,0:T(8,128)(2,1)S(1)}, bf16[96,3072]{1,0:T(8,128)(2,1)S(1)}, u32[]{:S(2)}, u32[]{:S(2)}) collective-permute-start(bf16[96,3072]{1,0:T(8,128)(2,1)S(1)} %slice.9), channel_id=1, source_target_pairs={{0,2},{2,0},{1,3},{3,1},{4,6},{6,4},{5,7},{7,5},{8,10},{10,8},{9,1... | collective-permute-start | bytes 1769480 | tf_op jit(solution)/shard_map/ppermute | solution.py:349
  88.8 1.0 copy-start.9
  88.8 14.5 %collective-permute-start.8 = (bf16[96,3072]{1,0:T(8,128)(2,1)S(1)}, bf16[96,3072]{1,0:T(8,128)(2,1)}, u32[]{:S(2)}, u32[]{:S(2)}) collective-permute-start(bf16[96,3072]{1,0:T(8,128)(2,1)S(1)} %slice.8), channel_id=1, source_target_pairs={{0,16},{16,0},{1,17},{17,1},{2,18},{18,2},{3,19},{19,3},{4,20},{20... | collective-permute-start | bytes 1769480 | tf_op jit(solution)/shard_map/ppermute | solution.py:348
  101.9 0.8 copy-start.19
  114.2 10.7 %collective-permute-start.10 = (bf16[256,768]{1,0:T(8,128)(2,1)S(1)}, bf16[256,768]{1,0:T(8,128)(2,1)S(1)}, u32[]{:S(2)}, u32[]{:S(2)}) collective-permute-start(bf16[256,768]{1,0:T(8,128)(2,1)S(1)} %get-tuple-element.36), channel_id=1, source_target_pairs={{0,2},{2,0},{1,3},{3,1},{4,6},{6,4},{5,7},{7,5},{8,10},{10,8},{9,1... | collective-permute-start | bytes 1179656 | tf_op jit(solution)/shard_map/ppermute | solution.py:433
  126.4 14.7 %copy-start.1 = (bf16[512,768]{1,0:T(8,128)(2,1)}, bf16[512,768]{1,0:T(8,128)(2,1)S(1)}, u32[]{:S(2)}) copy-start(bf16[512,768]{1,0:T(8,128)(2,1)S(1)} %weave_steps.1.tok_ref) | copy-start | bytes 2359300
  126.4 2.4 %collective-permute-start.11 = (bf16[512,768]{1,0:T(8,128)(2,1)S(1)}, bf16[512,768]{1,0:T(8,128)(2,1)S(1)}, u32[]{:S(2)}, u32[]{:S(2)}) collective-permute-start(bf16[512,768]{1,0:T(8,128)(2,1)S(1)} %weave_steps.1.tok_ref), channel_id=1, source_target_pairs={{0,1},{1,0},{2,3},{3,2},{4,5},{5,4},{6,7},{7,6},{8,9},{9,8},{10,11... | collective-permute-start | bytes 2359304 | tf_op jit(solution)/shard_map/ppermute | solution.py:447
  128.8 0.9 copy-start.14
  141.1 12.0 %collective-permute-start.12 = (bf16[512,768]{1,0:T(8,128)(2,1)}, bf16[512,768]{1,0:T(8,128)(2,1)S(1)}, u32[]{:S(2)}, u32[]{:S(2)}) collective-permute-start(bf16[512,768]{1,0:T(8,128)(2,1)} %layer.3), channel_id=1, source_target_pairs={{0,1},{1,0},{2,3},{3,2},{4,5},{5,4},{6,7},{7,6},{8,9},{9,8},{10,11... | collective-permute-start | bytes 2359304 | tf_op jit(solution)/shard_map/ppermute | solution.py:449
  141.3 11.8 %copy-start.2 = (bf16[512,768]{1,0:T(8,128)(2,1)S(1)}, bf16[512,768]{1,0:T(8,128)(2,1)}, u32[]{:S(2)}) copy-start(bf16[512,768]{1,0:T(8,128)(2,1)} %copy-done.1) | copy-start | bytes 2359300
  153.1 1.4 copy-start

commit v14 on v10

--- a/solution.py
+++ b/solution.py
@@ -20,6 +20,7 @@
 BF16 = jnp.bfloat16
 WHOLE = pl.BlockSpec(memory_space=pltpu.VMEM)
 SCALARS = pl.BlockSpec(memory_space=pltpu.SMEM)
+FAR = pl.BlockSpec(memory_space=pl.ANY)
 
 
 def iota(shape, axis):
@@ -75,7 +76,7 @@
         ],
         in_specs=[WHOLE] * 3,
         out_specs=[WHOLE] * 2,
-        compiler_params=params(6),
+        compiler_params=params(12),
         cost_estimate=pl.CostEstimate(
             flops=16 * rows * n_owners * capacity, bytes_accessed=8 * rows, transcendentals=0
         ),
@@ -168,7 +169,7 @@
         out_shape=jax.ShapeDtypeStruct((rows, width), BF16),
         in_specs=[SCALARS] + [WHOLE] * 3,
         out_specs=WHOLE,
-        compiler_params=params(10),
+        compiler_params=params(12),
         cost_estimate=pl.CostEstimate(
             flops=2 * rows * width * (rows + width), bytes_accessed=4 * rows * width, transcendentals=0
         ),
@@ -220,34 +221,30 @@
     return dot_t(hidden, down_w)
 
 
-def put_rows_kernel(firsts, *refs):
-    pieces, (out_ref, sems) = refs[: len(firsts)], refs[-2:]
-    copies = [
-        pltpu.make_async_copy(piece, out_ref.at[pl.ds(first, piece.shape[0]), :], sems.at[number])
-        for number, (first, piece) in enumerate(zip(firsts, pieces))
-    ]
+def put_rows_kernel(places, *refs):
+    pieces, (out_ref, sems) = refs[:-2], refs[-2:]
+    copies = []
+    for number, ((row, at), piece) in enumerate(zip(places, pieces)):
+        rows, columns = piece.shape
+        target = out_ref.at[pl.ds(row, rows), pl.ds(at, columns)]
+        copies.append(pltpu.make_async_copy(piece, target, sems.at[number]))
     for copy in copies:
         copy.start()
     for copy in copies:
         copy.wait()
 
 
-def put_rows(pieces, rows, first, into=None):
-    firsts = [first + sum(piece.shape[0] for piece in pieces[:number]) for number in range(len(pieces))]
-    operands = pieces if into is None else pieces + [into]
-    return pl.pallas_call(
-        functools.partial(put_rows_kernel, firsts),
-        out_shape=jax.ShapeDtypeStruct((rows, pieces[0].shape[1]), BF16),
-        in_specs=[pl.BlockSpec(memory_space=pl.ANY)] * len(operands),
-        out_specs=pl.BlockSpec(memory_space=pl.ANY),
+def put_rows(pieces, rows, columns):
+    return pl.pallas_call(
+        functools.partial(put_rows_kernel, [(row, at) for _, row, at in pieces]),
+        out_shape=jax.ShapeDtypeStruct((rows, columns), BF16),
+        in_specs=[FAR] * len(pieces),
+        out_specs=FAR,
         scratch_shapes=[pltpu.SemaphoreType.DMA((len(pieces),))],
-        input_output_aliases={} if into is None else {len(pieces): 0},
         compiler_params=params(2),
-        cost_estimate=pl.CostEstimate(
-            flops=0, bytes_accessed=4 * sum(piece.size for piece in pieces), transcendentals=0
-        ),
+        cost_estimate=pl.CostEstimate(flops=0, bytes_accessed=4 * rows * columns, transcendentals=0),
         name="put_rows",
-    )(*operands)
+    )(*[array for array, _, _ in pieces])
 
 
 def layer_kernel(hidden_width, tok_ref, w_ref, out_ref, norm_ref, ctx_ref, acc_ref):
@@ -306,7 +303,7 @@
         out_shape=jax.ShapeDtypeStruct((rows, width), BF16),
         in_specs=[WHOLE] * 4,
         out_specs=WHOLE,
-        compiler_params=params(10),
+        compiler_params=params(12),
         cost_estimate=pl.CostEstimate(
             flops=2 * rows * width * width, bytes_accessed=10 * rows * width, transcendentals=0
         ),
@@ -332,6 +329,16 @@
         pairs = [(place, place ^ far) for place in range(n_share)]
         places.append(lax.ppermute(shares, ("groups", "slots"), pairs))
     return places
+
+
+def to_other_places_by_halves(shares):
+    swap = [(0, 1), (1, 0)]
+    by_slot = lax.ppermute(shares, "slots", swap)
+    by_group = lax.ppermute(shares, "groups", swap)
+    cut = shares.shape[1] // 2
+    left = lax.ppermute(by_slot[:, :cut], "groups", swap)
+    right = lax.ppermute(by_group[:, cut:], "slots", swap)
+    return [shares, by_slot, by_group, left, right]
 
 
 def arrival_order(width, n_share):
@@ -409,16 +416,20 @@
         blocks = place_rows(owner, obs_feat, n_owners, capacity)
         above, opposite = along_cells(share_rows, 1), along_cells(below, -1)
         blocks, above, opposite, first = lax.optimization_barrier((blocks, above, opposite, first))
-        second = to_other_places(jnp.concatenate([above, opposite], axis=0))
-        weights = put_rows([side_by_side(*local_weights)] + first, width, 0)
+        second = to_other_places_by_halves(jnp.concatenate([above, opposite], axis=0))
+        shard = side_by_side(*local_weights)
         got = lax.all_to_all(blocks, ("cells", "mp"), split_axis=0, concat_axis=0, tiled=True)
-        got, weights = lax.optimization_barrier((got, weights))
+        got, shard, second = lax.optimization_barrier((got, shard, second))
         keep, send = pool_rows(my_slot.reshape(1), embed, codes, got, capacity, slot_dev)
-        send, second = lax.optimization_barrier((send, second))
         other = lax.ppermute(send, "slots", [(0, 1), (1, 0)])
-        weights = put_rows(second, width, width // 2, weights)
-        other, weights = lax.optimization_barrier((other, weights))
+        pieces, row = [], 0
+        for array in [shard] + first + second[:3]:
+            pieces.append((array, row, 0))
+            row += array.shape[0]
+        pieces += [(second[3], row, 0), (second[4], row, second[3].shape[1])]
         tokens = weave_steps(my_slot.reshape(1), order, keep, other, slot_dev)
+        tokens, arrays = lax.optimization_barrier((tokens, [array for array, _, _ in pieces]))
+        weights = put_rows([(array, row, at) for array, (_, row, at) in zip(arrays, pieces)], width, shard.shape[1])
     else:
         order = jnp.arange(width, dtype=jnp.int32)
         weights = lax.all_gather(share_rows, ("cells", "groups", "slots"), axis=0, tiled=True)

time: 154 us -> 158 us (1.026)
  local copies, waits for them, and re-layouts: 27.4 us -> 15.3 us
  waiting for transfers between devices: 65.9 us -> 77.7 us
  starting transfers between devices: 17.7 us -> 19.9 us
    ppermute x0 -> x4, waiting for transfers between devices: none -> 38.3 us  [the longest x1 25.7 us: to_other_places_by_halves(): by_group = lax.ppermute(shares, 'groups', swap)]
    all_to_all x1, waiting for transfers between devices: 41.7 us -> 9.1 us  [on_device(): lax.all_to_all(blocks, ('cells', 'mp'), split_axis=0, concat_axis=0, tile...]
    ppermute x3, waiting for transfers between devices: 19.6 us -> 7.39 us  [along_cells(): lax.ppermute(values, 'cells', [(j, (j - distance) % n_cells) for j in ran...]
    ppermute x6 -> x3, waiting for transfers between devices: 1.62 us -> 13.4 us  [to_other_places(): places.append(lax.ppermute(shares, ('groups', 'slots'), pairs))]
    unnamed x58 -> x60, local copies, waits for them, and re-layouts: 23.4 us -> 12.2 us
    ppermute x1, waiting for transfers between devices: 0.79 us -> 9.44 us  [on_device(): other = lax.ppermute(send, 'slots', [(0, 1), (1, 0)])]
    ppermute x0 -> x4, starting transfers between devices: none -> 4.83 us  [the longest x1 1.6 us: to_other_places_by_halves(): by_group = lax.ppermute(shares, 'groups', swap)]
    ppermute x6 -> x3, starting transfers between devices: 7.04 us -> 3.49 us  [to_other_places(): places.append(lax.ppermute(shares, ('groups', 'slots'), pairs))]
  transfers between devices with their start and end apart: 13 -> 14, of which waited for: 6 -> 8; matrix products, arithmetic and copies ran while one was open for 2% -> 0% of each run, Pallas kernels for 11% -> 8%
where the time goes in v14:
time: 158 us; the launch traced here: 157 us
  waiting for transfers between devices  77.7 us (49%)
  Pallas kernels  28.8 us (18%)
  starting transfers between devices  19.9 us (13%)
  local copies, waits for them, and re-layouts  15.3 us (10%)
  blocking collectives  14.1 us (9%)
    ppermute x1, waiting for transfers between devices, to_other_places_by_halves(): by_group = lax.ppermute(shares, 'groups', swap)  25.7 us
    pallas_call x2, Pallas kernels, layer(): pl.pallas_call(functools.partial(layer_kernel, hidden_width), out_shape=j...  14.5 us
    all_to_all x1, blocking collectives, on_device(): lax.all_to_all(codes, ('cells', 'mp'), split_axis=0, concat_axis=0, tiled...  14.1 us
    ppermute x3, waiting for transfers between devices, to_other_places(): places.append(lax.ppermute(shares, ('groups', 'slots'), pairs))  13.4 us
    unnamed x60, local copies, waits for them, and re-layouts  12.2 us
    ppermute x1, waiting for transfers between devices, to_other_places_by_halves(): right = lax.ppermute(by_group[:, cut:], 'slots', swap)  12.1 us
    ppermute x1, waiting for transfers between devices, on_device(): other = lax.ppermute(send, 'slots', [(0, 1), (1, 0)])  9.44 us
    all_to_all x1, waiting for transfers between devices, on_device(): lax.all_to_all(blocks, ('cells', 'mp'), split_axis=0, concat_axis=0, tile...  9.1 us
  transfers between devices with their start and end apart: 14, of which 8 were waited for; matrix products, arithmetic and copies ran while one was open for 0% of the time, Pallas kernels for 8%

profile of v14, /device:TPU:0, one launch (start us, length us, event | category | flops | bytes accessed | tf_op | source)
XLA Modules:
  0.0 157.1 jit_solution(6656956494223023463)
XLA Ops:
  0.0 0.8 dynamic-slice_bitcast_fusion.2
  0.8 0.9 dynamic-slice_bitcast_fusion.1
  1.7 0.9 dynamic-slice_bitcast_fusion
  2.7 1.2 constant_dynamic-slice_fusion
  4.0 3.1 %collective-permute-start = (bf16[48,6144]{1,0:T(8,128)(2,1)S(1)}, bf16[48,6144]{1,0:T(8,128)(2,1)S(1)}, u32[]{:S(2)}, u32[]{:S(2)}) collective-permute-start(bf16[48,6144]{1,0:T(8,128)(2,1)S(1)} %pad_maximum_fusion.1), channel_id=1, source_target_pairs={{0,4},{4,8},{8,12},{12,0},{1,5},{5,9},{9,13},{13,1},{2,6},{6,10},{... | collective-permute-start | bytes 1769480 | tf_op jit(solution)/shard_map/ppermute | solution.py:321
  7.8 0.7 place_codes.1
  8.5 14.1 %all_to_all.10.code_ref = s32[8,1,192]{2,1,0:T(1,128)S(1)} all-to-all(s32[8,1,192]{2,1,0:T(1,128)S(1)} %get-tuple-element.38), channel_id=1, replica_groups=mesh['groups'=2,'cells'=4,'slots'=2,'mp'=2] {'cells','mp'}, dimensions={0} | all-to-all | bytes 12288 | tf_op jit(solution)/shard_map/all_to_all | solution.py:413
  22.6 1.7 %collective-permute-start.1 = (bf16[48,6144]{1,0:T(8,128)(2,1)S(1)}, bf16[48,6144]{1,0:T(8,128)(2,1)S(1)}, u32[]{:S(2)}, u32[]{:S(2)}) collective-permute-start(bf16[48,6144]{1,0:T(8,128)(2,1)S(1)} %pad_maximum_fusion.1), channel_id=1, source_target_pairs={{0,12},{4,0},{8,4},{12,8},{1,13},{5,1},{9,5},{13,9},{2,14},{6,2},{... | collective-permute-start | bytes 1769480 | tf_op jit(solution)/shard_map/ppermute | solution.py:321
  24.4 2.4 %collective-permute-start.5 = (bf16[48,6144]{1,0:T(8,128)(2,1)S(1)}, bf16[48,6144]{1,0:T(8,128)(2,1)S(1)}, u32[]{:S(2)}, u32[]{:S(2)}) collective-permute-start(bf16[48,6144]{1,0:T(8,128)(2,1)S(1)} %collective-permute-done.refs_1_), channel_id=1, source_target_pairs={{0,18},{2,16},{16,2},{18,0},{1,19},{3,17},{17,3},{19,1},{4,22},{6,... | collective-permute-start | bytes 1769480 | tf_op jit(solution)/shard_map/ppermute | solution.py:330
  26.8 0.5 collective-permute-start.4
  27.3 0.5 collective-permute-start.3
  27.9 0.3 collective-permute-start.2
  28.2 3.0 %place_rows.1 = bf16[8,192,768]{2,1,0:T(8,128)(2,1)} custom-call(s32[1,512]{1,0:T(1,128)S(1)} %bitcast.22, bf16[512,768]{1,0:T(8,128)(2,1)S(1)} %copy-done.16), custom_call_target="tpu_custom_call" | custom-call | flops 1207959552 | bytes 3145728 | tf_op jit(solution)/shard_map/place_rows/pallas_call | solution.py:98
  31.2 7.4 %collective-permute-done.1 = bf16[48,6144]{1,0:T(8,128)(2,1)S(1)} collective-permute-done((bf16[48,6144]{1,0:T(8,128)(2,1)S(1)}, bf16[48,6144]{1,0:T(8,128)(2,1)S(1)}, u32[]{:S(2)}, u32[]{:S(2)}) %collective-permute-start.1) | collective-permute-done | bytes 589856 | tf_op jit(solution)/shard_map/ppermute | solution.py:321
  38.6 2.9 %collective-permute-done.5.refs_4_ = bf16[48,6144]{1,0:T(8,128)(2,1)S(1)} collective-permute-done((bf16[48,6144]{1,0:T(8,128)(2,1)S(1)}, bf16[48,6144]{1,0:T(8,128)(2,1)S(1)}, u32[]{:S(2)}, u32[]{:S(2)}) %collective-permute-start.5) | collective-permute-done | bytes 589856 | tf_op jit(solution)/shard_map/ppermute | solution.py:330
  41.5 0.9 copy-done.6
  42.4 10.5 %collective-permute-done.4.refs_3_ = bf16[48,6144]{1,0:T(8,128)(2,1)S(1)} collective-permute-done((bf16[48,6144]{1,0:T(8,128)(2,1)S(1)}, bf16[48,6144]{1,0:T(8,128)(2,1)S(1)}, u32[]{:S(2)}, u32[]{:S(2)}) %collective-permute-start.4) | collective-permute-done | bytes 589856 | tf_op jit(solution)/shard_map/ppermute | solution.py:330
  52.9 0.9 copy-done.8
  53.8 0.8 copy-done.10
  54.6 4.4 %all-to-all-start.1 = ((bf16[8,192,768]{2,1,0:T(8,128)(2,1)}), bf16[8,192,768]{2,1,0:T(8,128)(2,1)}, u32[]{:S(2)}, u32[]{:S(2)}) async-start(bf16[8,192,768]{2,1,0:T(8,128)(2,1)} %place_rows.1), calls=%async_computation.1 | async-start | bytes 4718592 | tf_op jit(solution)/shard_map/all_to_all | solution.py:421
  59.2 1.6 %collective-permute-start.7 = (bf16[96,6144]{1,0:T(8,128)(2,1)S(1)}, bf16[96,6144]{1,0:T(8,128)(2,1)S(1)}, u32[]{:S(2)}, u32[]{:S(2)}) collective-permute-start(bf16[96,6144]{1,0:T(8,128)(2,1)S(1)} %constant_dynamic-update-slice_fusion.refs_5_), channel_id=1, source_target_pairs={{0,16},{16,0},{1,17},{17,1},{2,18},{18,2},{3,19},{19,3},{4,20},{20... | collective-permute-start | bytes 3538952 | tf_op jit(solution)/shard_map/ppermute | solution.py:337
  60.8 0.8 collective-permute-start.6
  61.6 0.1 copy.17
  61.8 25.7 %collective-permute-done.7.refs_7_ = bf16[96,6144]{1,0:T(8,128)(2,1)S(1)} collective-permute-done((bf16[96,6144]{1,0:T(8,128)(2,1)S(1)}, bf16[96,6144]{1,0:T(8,128)(2,1)S(1)}, u32[]{:S(2)}, u32[]{:S(2)}) %collective-permute-start.7) | collective-permute-done | bytes 1179680 | tf_op jit(solution)/shard_map/ppermute | solution.py:337
  87.5 1.6 collective-permute-start.9
  89.1 0.9 collective-permute-start.8
  90.1 0.2 pad_maximum_fusion.refs_0_
  90.3 12.1 %collective-permute-done.9.refs_9_ = bf16[96,3072]{1,0:T(8,128)(2,1)S(1)} collective-permute-done((bf16[96,3072]{1,0:T(8,128)(2,1)S(1)}, bf16[96,3072]{1,0:T(8,128)(2,1)S(1)}, u32[]{:S(2)}, u32[]{:S(2)}) %collective-permute-start.9) | collective-permute-done | bytes 589856 | tf_op jit(solution)/shard_map/ppermute | solution.py:340
  102.5 0.8 copy-done.12
  103.3 0.5 collective-permute-done.8.refs_8_
  103.8 0.8 copy-done.14
  104.6 9.1 %all-to-all-done.1.got_ref = bf16[8,192,768]{2,1,0:T(8,128)(2,1)} async-done(((bf16[8,192,768]{2,1,0:T(8,128)(2,1)}), bf16[8,192,768]{2,1,0:T(8,128)(2,1)}, u32[]{:S(2)}, u32[]{:S(2)}) %all-to-all-start.1) | async-done | bytes 2359328 | tf_op jit(solution)/shard_map/all_to_all | solution.py:421
  113.7 0.7 copy-done.19
  114.4 4.5 %pool_rows.1 = (bf16[256,768]{1,0:T(8,128)(2,1)S(1)}, bf16[256,768]{1,0:T(8,128)(2,1)}) custom-call(s32[1]{0:T(128)} %bitcast.slot_ref, bf16[8,768]{1,0:T(8,128)(2,1)S(1)} %copy-done.19, s32[8,1,192]{2,1,0:T(1,128)S(1)} %all_to_all.10.code_ref, bf16[8,192,768]{2,1,0:T(8,128)(2,1)} %all-to-all-done.1.got_ref), custom_call_target="tpu_custom_call" | custom-call | flops 1207959552 | bytes 2359296 | tf_op jit(solution)/shard_map/pool_rows/pallas_call | solution.py:138
  118.9 0.7 copy-done.20
  119.6 1.5 collective-permute-start.10
  121.2 9.4 %collective-permute-done.10.got_ref = bf16[256,768]{1,0:T(8,128)(2,1)} collective-permute-done((bf16[256,768]{1,0:T(8,128)(2,1)}, bf16[256,768]{1,0:T(8,128)(2,1)}, u32[]{:S(2)}, u32[]{:S(2)}) %collective-permute-start.10) | collective-permute-done | bytes 393248 | tf_op jit(solution)/shard_map/ppermute | solution.py:424
  130.6 1.0 copy-done.21
  131.6 2.6 %weave_steps.1.tok_ref = bf16[512,768]{1,0:T(8,128)(2,1)S(1)} custom-call(s32[1]{0:T(128)} %bitcast.slot_ref, s32[1,768]{1,0:T(1,128)S(1)} %compare_select_fusion.6.order_ref, bf16[256,768]{1,0:T(8,128)(2,1)S(1)} %copy-done.21, bf16[256,768]{1,0:T(8,128)(2,1)} %collective-permute-done.10.got_ref), custom_call_target="tpu_custom_call" | custom-call | flops 1006632960 | bytes 1572864 | tf_op jit(solution)/shard_map/weave_steps/pallas_call | solution.py:167
  134.4 1.1 copy-done.9
  135.4 1.1 copy-done.11
  136.5 1.1 copy-done.13
  137.6 1.1 copy-done.15
  138.6 1.7 %put_rows.1.w_ref = bf16[768,6144]{1,0:T(8,128)(2,1)S(1)} custom-call(bf16[192,6144]{1,0:T(8,128)(2,1)S(1)} %pad_maximum_fusion.refs_0_, bf16[48,6144]{1,0:T(8,128)(2,1)S(1)} %copy-done.5, bf16[48,6144]{1,0:T(8,128)(2,1)S(1)} %copy-done.11, bf16[48,6144]{1,0:T(8,128)(2,1)S(1)} %copy-done.9, bf16[48,6144]{1,0:T(8,128)(2,1)S(1)} %copy-done.7, ...), custom_call_target="tpu_custom_call" | custom-call | bytes 18874368 | tf_op jit(solution)/shard_map/put_rows/pallas_call | solution.py:238
  140.4 7.2 %layer.3 = bf16[512,768]{1,0:T(8,128)(2,1)S(1)} custom-call(bf16[512,768]{1,0:T(8,128)(2,1)S(1)} %collective-permute-done.11.tok_ref, bf16[768,6144]{1,0:T(8,128)(2,1)S(1)} %put_rows.1.w_ref), custom_call_target="tpu_custom_call" | custom-call | flops 4831838208 | bytes 11796480 | tf_op jit(solution)/shard_map/layer/pallas_call | solution.py:272
  147.6 0.5 collective-permute-start.12
  148.1 7.2 %layer.2.sum_ref = f32[512,768]{1,0:T(8,128)S(1)} custom-call(bf16[512,768]{1,0:T(8,128)(2,1)S(1)} %weave_steps.1.tok_ref, bf16[768,6144]{1,0:T(8,128)(2,1)S(1)} %put_rows.1.w_ref), custom_call_target="tpu_custom_call" | custom-call | flops 4831838208 | bytes 11796480 | tf_op jit(solution)/shard_map/layer/pallas_call | solution.py:272
  155.4 1.8 %finish.1 = bf16[512,768]{1,0:T(8,128)(2,1)} custom-call(bf16[512,768]{1,0:T(8,128)(2,1)S(1)} %weave_steps.1.tok_ref, f32[512,768]{1,0:T(8,128)S(1)} %layer.2.sum_ref, bf16[512,768]{1,0:T(8,128)(2,1)S(1)} %collective-permute-done.12.got_ref, s32[1,768]{1,0:T(1,128)S(1)} %compare_select_fusion.6.order_ref), custom_call_target="tpu_custom_call" | custom-call | flops 603979776 | bytes 3932160 | tf_op jit(solution)/shard_map/finish/pallas_call | solution.py:301
  (61 shorter events, 0.6 us)
Async XLA Ops:
  2.6 5.1 %copy-start.26 = (s32[512]{0:T(512)S(1)}, s32[512]{0:T(512)}, u32[]{:S(2)}) copy-start(s32[512]{0:T(512)} %param.11) | copy-start | bytes 6148
  2.6 5.1 %copy-start.27 = (s32[512]{0:T(512)S(1)}, s32[512]{0:T(512)}, u32[]{:S(2)}) copy-start(s32[512]{0:T(512)} %param.10) | copy-start | bytes 6148
  2.7 5.1 %copy-start.17 = (bf16[8,768]{1,0:T(8,128)(2,1)S(1)}, bf16[8,768]{1,0:T(8,128)(2,1)}, u32[]{:S(2)}) copy-start(bf16[8,768]{1,0:T(8,128)(2,1)} %time_ref.1) | copy-start | bytes 36868
  2.7 25.5 %copy-start.16 = (bf16[512,768]{1,0:T(8,128)(2,1)S(1)}, bf16[512,768]{1,0:T(8,128)(2,1)}, u32[]{:S(2)}) copy-start(bf16[512,768]{1,0:T(8,128)(2,1)} %feat_ref.1) | copy-start | bytes 2359300
  4.0 18.6 %collective-permute-start = (bf16[48,6144]{1,0:T(8,128)(2,1)S(1)}, bf16[48,6144]{1,0:T(8,128)(2,1)S(1)}, u32[]{:S(2)}, u32[]{:S(2)}) collective-permute-start(bf16[48,6144]{1,0:T(8,128)(2,1)S(1)} %pad_maximum_fusion.1), channel_id=1, source_target_pairs={{0,4},{4,8},{8,12},{12,0},{1,5},{5,9},{9,13},{13,1},{2,6},{6,10},{... | collective-permute-start | bytes 1769480 | tf_op jit(solution)/shard_map/ppermute | solution.py:321
  8.5 22.7 %copy-start.18 = (bf16[8,768]{1,0:T(8,128)(2,1)}, bf16[8,768]{1,0:T(8,128)(2,1)S(1)}, u32[]{:S(2)}) copy-start(bf16[8,768]{1,0:T(8,128)(2,1)S(1)} %get-tuple-element.37.embed_ref) | copy-start | bytes 36868
  22.6 8.6 %copy-start.4 = (bf16[48,6144]{1,0:T(8,128)(2,1)}, bf16[48,6144]{1,0:T(8,128)(2,1)S(1)}, u32[]{:S(2)}) copy-start(bf16[48,6144]{1,0:T(8,128)(2,1)S(1)} %collective-permute-done.refs_1_) | copy-start | bytes 1769476
  22.6 16.0 %collective-permute-start.1 = (bf16[48,6144]{1,0:T(8,128)(2,1)S(1)}, bf16[48,6144]{1,0:T(8,128)(2,1)S(1)}, u32[]{:S(2)}, u32[]{:S(2)}) collective-permute-start(bf16[48,6144]{1,0:T(8,128)(2,1)S(1)} %pad_maximum_fusion.1), channel_id=1, source_target_pairs={{0,12},{4,0},{8,4},{12,8},{1,13},{5,1},{9,5},{13,9},{2,14},{6,2},{... | collective-permute-start | bytes 1769480 | tf_op jit(solution)/shard_map/ppermute | solution.py:321
  24.4 17.2 %collective-permute-start.5 = (bf16[48,6144]{1,0:T(8,128)(2,1)S(1)}, bf16[48,6144]{1,0:T(8,128)(2,1)S(1)}, u32[]{:S(2)}, u32[]{:S(2)}) collective-permute-start(bf16[48,6144]{1,0:T(8,128)(2,1)S(1)} %collective-permute-done.refs_1_), channel_id=1, source_target_pairs={{0,18},{2,16},{16,2},{18,0},{1,19},{3,17},{17,3},{19,1},{4,22},{6,... | collective-permute-start | bytes 1769480 | tf_op jit(solution)/shard_map/ppermute | solution.py:330
  26.8 26.1 %collective-permute-start.4 = (bf16[48,6144]{1,0:T(8,128)(2,1)S(1)}, bf16[48,6144]{1,0:T(8,128)(2,1)S(1)}, u32[]{:S(2)}, u32[]{:S(2)}) collective-permute-start(bf16[48,6144]{1,0:T(8,128)(2,1)S(1)} %collective-permute-done.refs_1_), channel_id=1, source_target_pairs={{0,16},{2,18},{16,0},{18,2},{1,17},{3,19},{17,1},{19,3},{4,20},{6,... | collective-permute-start | bytes 1769480 | tf_op jit(solution)/shard_map/ppermute | solution.py:330
  27.3 26.5 %collective-permute-start.3 = (bf16[48,6144]{1,0:T(8,128)(2,1)S(1)}, bf16[48,6144]{1,0:T(8,128)(2,1)S(1)}, u32[]{:S(2)}, u32[]{:S(2)}) collective-permute-start(bf16[48,6144]{1,0:T(8,128)(2,1)S(1)} %collective-permute-done.refs_1_), channel_id=1, source_target_pairs={{0,2},{2,0},{16,18},{18,16},{1,3},{3,1},{17,19},{19,17},{4,6},{6,4... | collective-permute-start | bytes 1769480 | tf_op jit(solution)/shard_map/ppermute | solution.py:330
  27.9 26.8 %collective-permute-start.2 = (bf16[48,6144]{1,0:T(8,128)(2,1)S(1)}, bf16[48,6144]{1,0:T(8,128)(2,1)S(1)}, u32[]{:S(2)}, u32[]{:S(2)}) collective-permute-start(bf16[48,6144]{1,0:T(8,128)(2,1)S(1)} %collective-permute-done.refs_1_), channel_id=1, source_target_pairs={{0,4},{4,8},{8,12},{12,0},{1,5},{5,9},{9,13},{13,1},{2,6},{6,10},{... | collective-permute-start | bytes 1769480 | tf_op jit(solution)/shard_map/ppermute | solution.py:321
  41.5 0.9 copy-start.6
  52.9 0.9 copy-start.8
  53.8 0.8 copy-start.10
  54.6 59.1 %all-to-all-start.1 = ((bf16[8,192,768]{2,1,0:T(8,128)(2,1)}), bf16[8,192,768]{2,1,0:T(8,128)(2,1)}, u32[]{:S(2)}, u32[]{:S(2)}) async-start(bf16[8,192,768]{2,1,0:T(8,128)(2,1)} %place_rows.1), calls=%async_computation.1 | async-start | bytes 4718592 | tf_op jit(solution)/shard_map/all_to_all | solution.py:421
  59.0 2.5 %copy-start.24 = (bf16[192,3,384]{2,0,1:T(8,128)(2,1)S(1)}, bf16[192,3,384]{2,0,1:T(8,128)(2,1)}, u32[]{:S(2)}) copy-start(bf16[192,3,384]{2,0,1:T(8,128)(2,1)} %param.14) | copy-start | bytes 1327108
  59.1 2.5 %copy-start.22 = (bf16[192,2,1536]{2,1,0:T(2,128)(2,1)S(1)}, bf16[192,2,1536]{2,1,0:T(2,128)(2,1)}, u32[]{:S(2)}) copy-start(bf16[192,2,1536]{2,1,0:T(2,128)(2,1)} %param.16) | copy-start | bytes 3538948
  59.2 2.6 %copy-start.2 = (bf16[96,6144]{1,0:T(8,128)(2,1)}, bf16[96,6144]{1,0:T(8,128)(2,1)S(1)}, u32[]{:S(2)}) copy-start(bf16[96,6144]{1,0:T(8,128)(2,1)S(1)} %constant_dynamic-update-slice_fusion.refs_5_) | copy-start | bytes 3538948
  59.2 28.3 %collective-permute-start.7 = (bf16[96,6144]{1,0:T(8,128)(2,1)S(1)}, bf16[96,6144]{1,0:T(8,128)(2,1)S(1)}, u32[]{:S(2)}, u32[]{:S(2)}) collective-permute-start(bf16[96,6144]{1,0:T(8,128)(2,1)S(1)} %constant_dynamic-update-slice_fusion.refs_5_), channel_id=1, source_target_pairs={{0,16},{16,0},{1,17},{17,1},{2,18},{18,2},{3,19},{19,3},{4,20},{20... | collective-permute-start | bytes 3538952 | tf_op jit(solution)/shard_map/ppermute | solution.py:337
  60.8 28.3 %collective-permute-start.6 = (bf16[96,6144]{1,0:T(8,128)(2,1)S(1)}, bf16[96,6144]{1,0:T(8,128)(2,1)S(1)}, u32[]{:S(2)}, u32[]{:S(2)}) collective-permute-start(bf16[96,6144]{1,0:T(8,128)(2,1)S(1)} %constant_dynamic-update-slice_fusion.refs_5_), channel_id=1, source_target_pairs={{0,2},{2,0},{1,3},{3,1},{4,6},{6,4},{5,7},{7,5},{8,10},{10,8},{9,1... | collective-permute-start | bytes 3538952 | tf_op jit(solution)/shard_map/ppermute | solution.py:336
  61.8 28.3 %copy-start.23 = (bf16[1536,192]{0,1:T(8,128)(2,1)S(1)}, bf16[1536,192]{0,1:T(8,128)(2,1)}, u32[]{:S(2)}) copy-start(bf16[1536,192]{0,1:T(8,128)(2,1)} %param.17) | copy-start | bytes 1769476
  61.8 28.3 %copy-start.25 = (bf16[384,192]{0,1:T(8,128)(2,1)S(1)}, bf16[384,192]{0,1:T(8,128)(2,1)}, u32[]{:S(2)}) copy-start(bf16[384,192]{0,1:T(8,128)(2,1)} %param.15) | copy-start | bytes 442372
  87.5 14.9 %collective-permute-start.9 = (bf16[96,3072]{1,0:T(8,128)(2,1)S(1)}, bf16[96,3072]{1,0:T(8,128)(2,1)S(1)}, u32[]{:S(2)}, u32[]{:S(2)}) collective-permute-start(bf16[96,3072]{1,0:T(8,128)(2,1)S(1)} %slice.9), channel_id=1, source_target_pairs={{0,2},{2,0},{1,3},{3,1},{4,6},{6,4},{5,7},{7,5},{8,10},{10,8},{9,1... | collective-permute-start | bytes 1769480 | tf_op jit(solution)/shard_map/ppermute | solution.py:340
  89.1 1.0 copy-start
  89.1 14.7 %collective-permute-start.8 = (bf16[96,3072]{1,0:T(8,128)(2,1)S(1)}, bf16[96,3072]{1,0:T(8,128)(2,1)S(1)}, u32[]{:S(2)}, u32[]{:S(2)}) collective-permute-start(bf16[96,3072]{1,0:T(8,128)(2,1)S(1)} %slice.8), channel_id=1, source_target_pairs={{0,16},{16,0},{1,17},{17,1},{2,18},{18,2},{3,19},{19,3},{4,20},{20... | collective-permute-start | bytes 1769480 | tf_op jit(solution)/shard_map/ppermute | solution.py:339
  102.5 0.8 copy-start.12
  103.8 0.8 copy-start.14
  113.7 0.7 copy-start.19
  118.9 0.7 copy-start.20
  119.6 11.0 %collective-permute-start.10 = (bf16[256,768]{1,0:T(8,128)(2,1)}, bf16[256,768]{1,0:T(8,128)(2,1)}, u32[]{:S(2)}, u32[]{:S(2)}) collective-permute-start(bf16[256,768]{1,0:T(8,128)(2,1)} %get-tuple-element.47), channel_id=1, source_target_pairs={{0,2},{2,0},{1,3},{3,1},{4,6},{6,4},{5,7},{7,5},{8,10},{10,8},{9,1... | collective-permute-start | bytes 1179656 | tf_op jit(solution)/shard_map/ppermute | solution.py:424
  130.6 1.0 copy-start.21
  131.6 2.7 %copy-start.1 = (bf16[96,6144]{1,0:T(8,128)(2,1)S(1)}, bf16[96,6144]{1,0:T(8,128)(2,1)}, u32[]{:S(2)}) copy-start(bf16[96,6144]{1,0:T(8,128)(2,1)} %copy-done) | copy-start | bytes 3538948
  131.6 2.7 %copy-start.3 = (bf16[96,6144]{1,0:T(8,128)(2,1)S(1)}, bf16[96,6144]{1,0:T(8,128)(2,1)}, u32[]{:S(2)}) copy-start(bf16[96,6144]{1,0:T(8,128)(2,1)} %copy-done.2) | copy-start | bytes 3538948
  131.6 2.7 %copy-start.5 = (bf16[48,6144]{1,0:T(8,128)(2,1)S(1)}, bf16[48,6144]{1,0:T(8,128)(2,1)}, u32[]{:S(2)}) copy-start(bf16[48,6144]{1,0:T(8,128)(2,1)} %copy-done.4) | copy-start | bytes 1769476
  131.6 2.7 %copy-start.7 = (bf16[48,6144]{1,0:T(8,128)(2,1)S(1)}, bf16[48,6144]{1,0:T(8,128)(2,1)}, u32[]{:S(2)}) copy-start(bf16[48,6144]{1,0:T(8,128)(2,1)} %copy-done.6) | copy-start | bytes 1769476
  134.2 6.1 %collective-permute-start.11 = (bf16[512,768]{1,0:T(8,128)(2,1)S(1)}, bf16[512,768]{1,0:T(8,128)(2,1)S(1)}, u32[]{:S(2)}, u32[]{:S(2)}) collective-permute-start(bf16[512,768]{1,0:T(8,128)(2,1)S(1)} %weave_steps.1.tok_ref), channel_id=1, source_target_pairs={{0,1},{1,0},{2,3},{3,2},{4,5},{5,4},{6,7},{7,6},{8,9},{9,8},{10,11... | collective-permute-start | bytes 2359304 | tf_op jit(solution)/shard_map/ppermute | solution.py:440
  134.4 1.1 copy-start.9
  135.4 1.1 copy-start.11
  136.5 1.1 copy-start.13
  137.6 1.1 copy-start.15
  147.6 7.8 %collective-permute-start.12 = (bf16[512,768]{1,0:T(8,128)(2,1)S(1)}, bf16[512,768]{1,0:T(8,128)(2,1)S(1)}, u32[]{:S(2)}, u32[]{:S(2)}) collective-permute-start(bf16[512,768]{1,0:T(8,128)(2,1)S(1)} %layer.3), channel_id=1, source_target_pairs={{0,1},{1,0},{2,3},{3,2},{4,5},{5,4},{6,7},{7,6},{8,9},{9,8},{10,11... | collective-permute-start | bytes 2359304 | tf_op jit(solution)/shard_map/ppermute | solution.py:442

commit v15 on v14

--- a/solution.py
+++ b/solution.py
@@ -239,9 +239,9 @@
         functools.partial(put_rows_kernel, [(row, at) for _, row, at in pieces]),
         out_shape=jax.ShapeDtypeStruct((rows, columns), BF16),
         in_specs=[FAR] * len(pieces),
-        out_specs=FAR,
+        out_specs=WHOLE,
         scratch_shapes=[pltpu.SemaphoreType.DMA((len(pieces),))],
-        compiler_params=params(2),
+        compiler_params=params(53),
         cost_estimate=pl.CostEstimate(flops=0, bytes_accessed=4 * rows * columns, transcendentals=0),
         name="put_rows",
     )(*[array for array, _, _ in pieces])

time: 158 us -> 157 us (level)
  waiting for transfers between devices: 77.7 us -> 75.4 us
  Pallas kernels: 28.8 us -> 30.7 us
    pallas_call x1, Pallas kernels: 1.75 us -> 7.31 us  [put_rows(): pl.pallas_call(functools.partial(put_rows_kernel, [(row, at) for _, row,...]
    pallas_call x1, Pallas kernels: 4.48 us -> 2.06 us  [pool_rows(): pl.pallas_call(functools.partial(pool_kernel, capacity, slot_dev), out_sh...]
    unnamed x60 -> x44, local copies, waits for them, and re-layouts: 12.2 us -> 10.2 us
  transfers between devices with their start and end apart: 14 -> 14, of which waited for: 8 -> 9; matrix products, arithmetic and copies ran while one was open for 0% -> 3% of each run, Pallas kernels for 8% -> 12%
where the time goes in v15:
time: 157 us
  waiting for transfers between devices  75.4 us (48%)
  Pallas kernels  30.7 us (20%)
  starting transfers between devices  19.2 us (12%)
  local copies, waits for them, and re-layouts  14.5 us (9%)
  blocking collectives  14.1 us (9%)
  other arithmetic  1.72 us (1%)
    ppermute x1, waiting for transfers between devices, to_other_places_by_halves(): by_group = lax.ppermute(shares, 'groups', swap)  25.7 us
    pallas_call x2, Pallas kernels, layer(): pl.pallas_call(functools.partial(layer_kernel, hidden_width), out_shape=j...  14.4 us
    ppermute x3, waiting for transfers between devices, to_other_places(): places.append(lax.ppermute(shares, ('groups', 'slots'), pairs))  14.4 us
    all_to_all x1, blocking collectives, on_device(): lax.all_to_all(codes, ('cells', 'mp'), split_axis=0, concat_axis=0, tiled...  14.1 us
    ppermute x1, waiting for transfers between devices, to_other_places_by_halves(): right = lax.ppermute(by_group[:, cut:], 'slots', swap)  10.7 us
    unnamed x44, local copies, waits for them, and re-layouts  10.2 us
    ppermute x1, waiting for transfers between devices, on_device(): other = lax.ppermute(send, 'slots', [(0, 1), (1, 0)])  9.12 us
    all_to_all x1, waiting for transfers between devices, on_device(): lax.all_to_all(blocks, ('cells', 'mp'), split_axis=0, concat_axis=0, tile...  7.53 us
  transfers between devices with their start and end apart: 14, of which 9 were waited for; matrix products, arithmetic and copies ran while one was open for 3% of the time, Pallas kernels for 12%

profile of v15, /device:TPU:0, one launch (start us, length us, event | category | flops | bytes accessed | tf_op | source)
XLA Modules:
  0.0 156.6 jit_solution(13804021762344930276)
XLA Ops:
  0.0 0.8 dynamic-slice_bitcast_fusion.2
  0.8 0.9 dynamic-slice_bitcast_fusion.1
  1.7 0.9 dynamic-slice_bitcast_fusion
  2.6 0.0 copy-start.18
  2.7 1.2 constant_dynamic-slice_fusion
  4.0 3.1 %collective-permute-start = (bf16[48,6144]{1,0:T(8,128)(2,1)S(1)}, bf16[48,6144]{1,0:T(8,128)(2,1)S(1)}, u32[]{:S(2)}, u32[]{:S(2)}) collective-permute-start(bf16[48,6144]{1,0:T(8,128)(2,1)S(1)} %pad_maximum_fusion.1), channel_id=1, source_target_pairs={{0,4},{4,8},{8,12},{12,0},{1,5},{5,9},{9,13},{13,1},{2,6},{6,10},{... | collective-permute-start | bytes 1769480 | tf_op jit(solution)/shard_map/ppermute | solution.py:321
  7.8 0.7 place_codes.1
  8.5 14.1 %all_to_all.10.code_ref = s32[8,1,192]{2,1,0:T(1,128)S(1)} all-to-all(s32[8,1,192]{2,1,0:T(1,128)S(1)} %get-tuple-element.38), channel_id=1, replica_groups=mesh['groups'=2,'cells'=4,'slots'=2,'mp'=2] {'cells','mp'}, dimensions={0} | all-to-all | bytes 12288 | tf_op jit(solution)/shard_map/all_to_all | solution.py:413
  22.6 1.7 %collective-permute-start.1 = (bf16[48,6144]{1,0:T(8,128)(2,1)S(1)}, bf16[48,6144]{1,0:T(8,128)(2,1)S(1)}, u32[]{:S(2)}, u32[]{:S(2)}) collective-permute-start(bf16[48,6144]{1,0:T(8,128)(2,1)S(1)} %pad_maximum_fusion.1), channel_id=1, source_target_pairs={{0,12},{4,0},{8,4},{12,8},{1,13},{5,1},{9,5},{13,9},{2,14},{6,2},{... | collective-permute-start | bytes 1769480 | tf_op jit(solution)/shard_map/ppermute | solution.py:321
  24.4 2.4 %collective-permute-start.5 = (bf16[48,6144]{1,0:T(8,128)(2,1)S(1)}, bf16[48,6144]{1,0:T(8,128)(2,1)S(1)}, u32[]{:S(2)}, u32[]{:S(2)}) collective-permute-start(bf16[48,6144]{1,0:T(8,128)(2,1)S(1)} %collective-permute-done.refs_1_), channel_id=1, source_target_pairs={{0,18},{2,16},{16,2},{18,0},{1,19},{3,17},{17,3},{19,1},{4,22},{6,... | collective-permute-start | bytes 1769480 | tf_op jit(solution)/shard_map/ppermute | solution.py:330
  26.8 0.5 collective-permute-start.4
  27.3 0.5 collective-permute-start.3
  27.9 0.3 collective-permute-start.2
  28.2 3.0 %place_rows.1 = bf16[8,192,768]{2,1,0:T(8,128)(2,1)} custom-call(s32[1,512]{1,0:T(1,128)S(1)} %bitcast.22, bf16[512,768]{1,0:T(8,128)(2,1)S(1)} %copy-done.2), custom_call_target="tpu_custom_call" | custom-call | flops 1207959552 | bytes 3145728 | tf_op jit(solution)/shard_map/place_rows/pallas_call | solution.py:98
  31.2 7.4 %collective-permute-done.1 = bf16[48,6144]{1,0:T(8,128)(2,1)S(1)} collective-permute-done((bf16[48,6144]{1,0:T(8,128)(2,1)S(1)}, bf16[48,6144]{1,0:T(8,128)(2,1)S(1)}, u32[]{:S(2)}, u32[]{:S(2)}) %collective-permute-start.1) | collective-permute-done | bytes 589856 | tf_op jit(solution)/shard_map/ppermute | solution.py:321
  38.6 2.9 %collective-permute-done.5.refs_4_ = bf16[48,6144]{1,0:T(8,128)(2,1)S(1)} collective-permute-done((bf16[48,6144]{1,0:T(8,128)(2,1)S(1)}, bf16[48,6144]{1,0:T(8,128)(2,1)S(1)}, u32[]{:S(2)}, u32[]{:S(2)}) %collective-permute-start.5) | collective-permute-done | bytes 589856 | tf_op jit(solution)/shard_map/ppermute | solution.py:330
  41.5 11.4 %collective-permute-done.4.refs_3_ = bf16[48,6144]{1,0:T(8,128)(2,1)S(1)} collective-permute-done((bf16[48,6144]{1,0:T(8,128)(2,1)S(1)}, bf16[48,6144]{1,0:T(8,128)(2,1)S(1)}, u32[]{:S(2)}, u32[]{:S(2)}) %collective-permute-start.4) | collective-permute-done | bytes 589856 | tf_op jit(solution)/shard_map/ppermute | solution.py:330
  52.9 0.1 collective-permute-done.3.refs_2_
  53.0 0.7 copy-done.13
  53.8 0.8 copy-done.14
  54.6 3.6 %all-to-all-start.1 = ((bf16[8,192,768]{2,1,0:T(8,128)(2,1)}), bf16[8,192,768]{2,1,0:T(8,128)(2,1)S(1)}, u32[]{:S(2)}, u32[]{:S(2)}) async-start(bf16[8,192,768]{2,1,0:T(8,128)(2,1)} %place_rows.1), calls=%async_computation.1 | async-start | bytes 4718592 | tf_op jit(solution)/shard_map/all_to_all | solution.py:421
  58.2 1.2 constant_dynamic-update-slice_fusion.1
  59.4 1.2 constant_dynamic-update-slice_fusion.refs_5_
  60.6 1.6 %collective-permute-start.7 = (bf16[96,6144]{1,0:T(8,128)(2,1)S(1)}, bf16[96,6144]{1,0:T(8,128)(2,1)S(1)}, u32[]{:S(2)}, u32[]{:S(2)}) collective-permute-start(bf16[96,6144]{1,0:T(8,128)(2,1)S(1)} %constant_dynamic-update-slice_fusion.refs_5_), channel_id=1, source_target_pairs={{0,16},{16,0},{1,17},{17,1},{2,18},{18,2},{3,19},{19,3},{4,20},{20... | collective-permute-start | bytes 3538952 | tf_op jit(solution)/shard_map/ppermute | solution.py:337
  62.2 0.8 collective-permute-start.6
  63.1 0.1 copy.17
  63.3 25.7 %collective-permute-done.7.refs_7_ = bf16[96,6144]{1,0:T(8,128)(2,1)S(1)} collective-permute-done((bf16[96,6144]{1,0:T(8,128)(2,1)S(1)}, bf16[96,6144]{1,0:T(8,128)(2,1)S(1)}, u32[]{:S(2)}, u32[]{:S(2)}) %collective-permute-start.7) | collective-permute-done | bytes 1179680 | tf_op jit(solution)/shard_map/ppermute | solution.py:337
  89.0 1.6 collective-permute-start.9
  90.6 0.9 collective-permute-start.8
  91.5 0.1 copy-done.7
  91.6 1.6 %pad_maximum_fusion.refs_0_ = bf16[192,6144]{1,0:T(8,128)(2,1)} fusion(bf16[192,1536]{1,0:T(8,128)(2,1)S(1)} %bitcast.29, bf16[192,384]{1,0:T(8,128)(2,1)S(1)} %bitcast.32, bf16[192,3072]{1,0:T(8,128)(2,1)S(1)} %bitcast.24, bf16[192,1152]{1,0:T(8,128)(2,1)S(1)} %bitcast.26), kind=kLoop, calls=%fused_computation | loop fusion | flops 9437184 | bytes 4718592 | tf_op jit(solution)/shard_map/concatenate | solution.py:316
  93.2 10.7 %collective-permute-done.9.refs_9_ = bf16[96,3072]{1,0:T(8,128)(2,1)S(1)} collective-permute-done((bf16[96,3072]{1,0:T(8,128)(2,1)S(1)}, bf16[96,3072]{1,0:T(8,128)(2,1)S(1)}, u32[]{:S(2)}, u32[]{:S(2)}) %collective-permute-start.9) | collective-permute-done | bytes 589856 | tf_op jit(solution)/shard_map/ppermute | solution.py:340
  103.8 0.8 copy-done.15
  104.7 0.6 collective-permute-done.8.refs_8_
  105.3 7.5 %all-to-all-done.1.got_ref = bf16[8,192,768]{2,1,0:T(8,128)(2,1)S(1)} async-done(((bf16[8,192,768]{2,1,0:T(8,128)(2,1)}), bf16[8,192,768]{2,1,0:T(8,128)(2,1)S(1)}, u32[]{:S(2)}, u32[]{:S(2)}) %all-to-all-start.1) | async-done | bytes 2359328 | tf_op jit(solution)/shard_map/all_to_all | solution.py:421
  112.8 2.1 %pool_rows.1 = (bf16[256,768]{1,0:T(8,128)(2,1)S(1)}, bf16[256,768]{1,0:T(8,128)(2,1)S(1)}) custom-call(s32[1]{0:T(128)} %bitcast.slot_ref, bf16[8,768]{1,0:T(8,128)(2,1)S(1)} %get-tuple-element.37.embed_ref, s32[8,1,192]{2,1,0:T(1,128)S(1)} %all_to_all.10.code_ref, bf16[8,192,768]{2,1,0:T(8,128)(2,1)S(1)} %all-to-all-done.1.got_ref), custom_call_target="tpu_custom_call" | custom-call | flops 1207959552 | bytes 2359296 | tf_op jit(solution)/shard_map/pool_rows/pallas_call | solution.py:138
  114.9 0.7 copy-done.4
  115.6 1.5 collective-permute-start.10
  117.2 9.1 %collective-permute-done.10.got_ref = bf16[256,768]{1,0:T(8,128)(2,1)S(1)} collective-permute-done((bf16[256,768]{1,0:T(8,128)(2,1)S(1)}, bf16[256,768]{1,0:T(8,128)(2,1)S(1)}, u32[]{:S(2)}, u32[]{:S(2)}) %collective-permute-start.10) | collective-permute-done | bytes 393248 | tf_op jit(solution)/shard_map/ppermute | solution.py:424
  126.3 1.0 copy-done.5
  127.3 1.5 weave_steps.1.tok_ref
  128.7 0.1 collective-permute-start.11
  128.8 7.3 %put_rows.1.w_ref = bf16[768,6144]{1,0:T(8,128)(2,1)} custom-call(bf16[192,6144]{1,0:T(8,128)(2,1)} %pad_maximum_fusion.refs_0_, bf16[48,6144]{1,0:T(8,128)(2,1)S(1)} %collective-permute-done.refs_1_, bf16[48,6144]{1,0:T(8,128)(2,1)} %copy-done.14, bf16[48,6144]{1,0:T(8,128)(2,1)} %copy-done.13, bf16[48,6144]{1,0:T(8,128)(2,1)} %copy-done.12, ...), custom_call_target="tpu_custom_call" | custom-call | bytes 18874368 | tf_op jit(solution)/shard_map/put_rows/pallas_call | solution.py:238
  136.2 3.7 %copy-done = bf16[768,6144]{1,0:T(8,128)(2,1)S(1)} copy-done((bf16[768,6144]{1,0:T(8,128)(2,1)S(1)}, bf16[768,6144]{1,0:T(8,128)(2,1)}, u32[]{:S(2)}) %copy-start) | copy-done | bytes 9437208
  139.8 7.2 %layer.3 = bf16[512,768]{1,0:T(8,128)(2,1)S(1)} custom-call(bf16[512,768]{1,0:T(8,128)(2,1)S(1)} %collective-permute-done.11.tok_ref, bf16[768,6144]{1,0:T(8,128)(2,1)S(1)} %copy-done), custom_call_target="tpu_custom_call" | custom-call | flops 4831838208 | bytes 11796480 | tf_op jit(solution)/shard_map/layer/pallas_call | solution.py:272
  147.1 0.6 collective-permute-start.12
  147.6 7.2 %layer.2.sum_ref = f32[512,768]{1,0:T(8,128)S(1)} custom-call(bf16[512,768]{1,0:T(8,128)(2,1)S(1)} %weave_steps.1.tok_ref, bf16[768,6144]{1,0:T(8,128)(2,1)S(1)} %copy-done.1), custom_call_target="tpu_custom_call" | custom-call | flops 4831838208 | bytes 11796480 | tf_op jit(solution)/shard_map/layer/pallas_call | solution.py:272
  154.8 1.8 %finish.1 = bf16[512,768]{1,0:T(8,128)(2,1)} custom-call(bf16[512,768]{1,0:T(8,128)(2,1)S(1)} %weave_steps.1.tok_ref, f32[512,768]{1,0:T(8,128)S(1)} %layer.2.sum_ref, bf16[512,768]{1,0:T(8,128)(2,1)S(1)} %collective-permute-done.12.got_ref, s32[1,768]{1,0:T(1,128)S(1)} %compare_select_fusion.6.order_ref), custom_call_target="tpu_custom_call" | custom-call | flops 603979776 | bytes 3932160 | tf_op jit(solution)/shard_map/finish/pallas_call | solution.py:301
  (45 shorter events, 0.4 us)
Async XLA Ops:
  2.6 5.1 %copy-start.18 = (s32[512]{0:T(512)S(1)}, s32[512]{0:T(512)}, u32[]{:S(2)}) copy-start(s32[512]{0:T(512)} %param.11) | copy-start | bytes 6148
  2.6 5.1 %copy-start.19 = (s32[512]{0:T(512)S(1)}, s32[512]{0:T(512)}, u32[]{:S(2)}) copy-start(s32[512]{0:T(512)} %param.10) | copy-start | bytes 6148
  2.7 5.1 %copy-start.3 = (bf16[8,768]{1,0:T(8,128)(2,1)S(1)}, bf16[8,768]{1,0:T(8,128)(2,1)}, u32[]{:S(2)}) copy-start(bf16[8,768]{1,0:T(8,128)(2,1)} %time_ref.1) | copy-start | bytes 36868
  2.7 25.5 %copy-start.2 = (bf16[512,768]{1,0:T(8,128)(2,1)S(1)}, bf16[512,768]{1,0:T(8,128)(2,1)}, u32[]{:S(2)}) copy-start(bf16[512,768]{1,0:T(8,128)(2,1)} %feat_ref.1) | copy-start | bytes 2359300
  4.0 18.6 %collective-permute-start = (bf16[48,6144]{1,0:T(8,128)(2,1)S(1)}, bf16[48,6144]{1,0:T(8,128)(2,1)S(1)}, u32[]{:S(2)}, u32[]{:S(2)}) collective-permute-start(bf16[48,6144]{1,0:T(8,128)(2,1)S(1)} %pad_maximum_fusion.1), channel_id=1, source_target_pairs={{0,4},{4,8},{8,12},{12,0},{1,5},{5,9},{9,13},{13,1},{2,6},{6,10},{... | collective-permute-start | bytes 1769480 | tf_op jit(solution)/shard_map/ppermute | solution.py:321
  22.6 16.0 %collective-permute-start.1 = (bf16[48,6144]{1,0:T(8,128)(2,1)S(1)}, bf16[48,6144]{1,0:T(8,128)(2,1)S(1)}, u32[]{:S(2)}, u32[]{:S(2)}) collective-permute-start(bf16[48,6144]{1,0:T(8,128)(2,1)S(1)} %pad_maximum_fusion.1), channel_id=1, source_target_pairs={{0,12},{4,0},{8,4},{12,8},{1,13},{5,1},{9,5},{13,9},{2,14},{6,2},{... | collective-permute-start | bytes 1769480 | tf_op jit(solution)/shard_map/ppermute | solution.py:321
  24.4 17.2 %collective-permute-start.5 = (bf16[48,6144]{1,0:T(8,128)(2,1)S(1)}, bf16[48,6144]{1,0:T(8,128)(2,1)S(1)}, u32[]{:S(2)}, u32[]{:S(2)}) collective-permute-start(bf16[48,6144]{1,0:T(8,128)(2,1)S(1)} %collective-permute-done.refs_1_), channel_id=1, source_target_pairs={{0,18},{2,16},{16,2},{18,0},{1,19},{3,17},{17,3},{19,1},{4,22},{6,... | collective-permute-start | bytes 1769480 | tf_op jit(solution)/shard_map/ppermute | solution.py:330
  26.8 26.1 %collective-permute-start.4 = (bf16[48,6144]{1,0:T(8,128)(2,1)S(1)}, bf16[48,6144]{1,0:T(8,128)(2,1)S(1)}, u32[]{:S(2)}, u32[]{:S(2)}) collective-permute-start(bf16[48,6144]{1,0:T(8,128)(2,1)S(1)} %collective-permute-done.refs_1_), channel_id=1, source_target_pairs={{0,16},{2,18},{16,0},{18,2},{1,17},{3,19},{17,1},{19,3},{4,20},{6,... | collective-permute-start | bytes 1769480 | tf_op jit(solution)/shard_map/ppermute | solution.py:330
  27.3 25.7 %collective-permute-start.3 = (bf16[48,6144]{1,0:T(8,128)(2,1)S(1)}, bf16[48,6144]{1,0:T(8,128)(2,1)S(1)}, u32[]{:S(2)}, u32[]{:S(2)}) collective-permute-start(bf16[48,6144]{1,0:T(8,128)(2,1)S(1)} %collective-permute-done.refs_1_), channel_id=1, source_target_pairs={{0,2},{2,0},{16,18},{18,16},{1,3},{3,1},{17,19},{19,17},{4,6},{6,4... | collective-permute-start | bytes 1769480 | tf_op jit(solution)/shard_map/ppermute | solution.py:330
  27.9 26.7 %collective-permute-start.2 = (bf16[48,6144]{1,0:T(8,128)(2,1)S(1)}, bf16[48,6144]{1,0:T(8,128)(2,1)}, u32[]{:S(2)}, u32[]{:S(2)}) collective-permute-start(bf16[48,6144]{1,0:T(8,128)(2,1)S(1)} %collective-permute-done.refs_1_), channel_id=1, source_target_pairs={{0,4},{4,8},{8,12},{12,0},{1,5},{5,9},{9,13},{13,1},{2,6},{6,10},{... | collective-permute-start | bytes 1769480 | tf_op jit(solution)/shard_map/ppermute | solution.py:321
  38.6 14.4 %copy-start.16 = (bf16[48,6144]{1,0:T(8,128)(2,1)}, bf16[48,6144]{1,0:T(8,128)(2,1)S(1)}, u32[]{:S(2)}) copy-start(bf16[48,6144]{1,0:T(8,128)(2,1)S(1)} %collective-permute-done.1) | copy-start | bytes 1769476
  41.5 11.5 %copy-start.12 = (bf16[48,6144]{1,0:T(8,128)(2,1)}, bf16[48,6144]{1,0:T(8,128)(2,1)S(1)}, u32[]{:S(2)}) copy-start(bf16[48,6144]{1,0:T(8,128)(2,1)S(1)} %collective-permute-done.5.refs_4_) | copy-start | bytes 1769476
  52.9 0.9 copy-start.13
  53.8 0.8 copy-start.14
  54.6 58.2 %all-to-all-start.1 = ((bf16[8,192,768]{2,1,0:T(8,128)(2,1)}), bf16[8,192,768]{2,1,0:T(8,128)(2,1)S(1)}, u32[]{:S(2)}, u32[]{:S(2)}) async-start(bf16[8,192,768]{2,1,0:T(8,128)(2,1)} %place_rows.1), calls=%async_computation.1 | async-start | bytes 4718592 | tf_op jit(solution)/shard_map/all_to_all | solution.py:421
  58.2 4.8 %copy-start.11 = (bf16[192,3,384]{2,0,1:T(8,128)(2,1)S(1)}, bf16[192,3,384]{2,0,1:T(8,128)(2,1)}, u32[]{:S(2)}) copy-start(bf16[192,3,384]{2,0,1:T(8,128)(2,1)} %param.14) | copy-start | bytes 1327108
  59.4 3.7 %copy-start.9 = (bf16[192,2,1536]{2,1,0:T(2,128)(2,1)S(1)}, bf16[192,2,1536]{2,1,0:T(2,128)(2,1)}, u32[]{:S(2)}) copy-start(bf16[192,2,1536]{2,1,0:T(2,128)(2,1)} %param.16) | copy-start | bytes 3538948
  60.6 2.6 %copy-start.8 = (bf16[96,6144]{1,0:T(8,128)(2,1)}, bf16[96,6144]{1,0:T(8,128)(2,1)S(1)}, u32[]{:S(2)}) copy-start(bf16[96,6144]{1,0:T(8,128)(2,1)S(1)} %constant_dynamic-update-slice_fusion.refs_5_) | copy-start | bytes 3538948
  60.6 28.3 %collective-permute-start.7 = (bf16[96,6144]{1,0:T(8,128)(2,1)S(1)}, bf16[96,6144]{1,0:T(8,128)(2,1)S(1)}, u32[]{:S(2)}, u32[]{:S(2)}) collective-permute-start(bf16[96,6144]{1,0:T(8,128)(2,1)S(1)} %constant_dynamic-update-slice_fusion.refs_5_), channel_id=1, source_target_pairs={{0,16},{16,0},{1,17},{17,1},{2,18},{18,2},{3,19},{19,3},{4,20},{20... | collective-permute-start | bytes 3538952 | tf_op jit(solution)/shard_map/ppermute | solution.py:337
  62.2 28.3 %collective-permute-start.6 = (bf16[96,6144]{1,0:T(8,128)(2,1)S(1)}, bf16[96,6144]{1,0:T(8,128)(2,1)S(1)}, u32[]{:S(2)}, u32[]{:S(2)}) collective-permute-start(bf16[96,6144]{1,0:T(8,128)(2,1)S(1)} %constant_dynamic-update-slice_fusion.refs_5_), channel_id=1, source_target_pairs={{0,2},{2,0},{1,3},{3,1},{4,6},{6,4},{5,7},{7,5},{8,10},{10,8},{9,1... | collective-permute-start | bytes 3538952 | tf_op jit(solution)/shard_map/ppermute | solution.py:336
  63.2 28.3 %copy-start.10 = (bf16[1536,192]{0,1:T(8,128)(2,1)S(1)}, bf16[1536,192]{0,1:T(8,128)(2,1)}, u32[]{:S(2)}) copy-start(bf16[1536,192]{0,1:T(8,128)(2,1)} %param.17) | copy-start | bytes 1769476
  63.2 28.3 %copy-start.17 = (bf16[384,192]{0,1:T(8,128)(2,1)S(1)}, bf16[384,192]{0,1:T(8,128)(2,1)}, u32[]{:S(2)}) copy-start(bf16[384,192]{0,1:T(8,128)(2,1)} %param.15) | copy-start | bytes 442372
  88.9 1.7 %copy-start.6 = (bf16[96,6144]{1,0:T(8,128)(2,1)}, bf16[96,6144]{1,0:T(8,128)(2,1)S(1)}, u32[]{:S(2)}) copy-start(bf16[96,6144]{1,0:T(8,128)(2,1)S(1)} %collective-permute-done.7.refs_7_) | copy-start | bytes 3538948
  89.0 14.9 %collective-permute-start.9 = (bf16[96,3072]{1,0:T(8,128)(2,1)S(1)}, bf16[96,3072]{1,0:T(8,128)(2,1)S(1)}, u32[]{:S(2)}, u32[]{:S(2)}) collective-permute-start(bf16[96,3072]{1,0:T(8,128)(2,1)S(1)} %slice.9), channel_id=1, source_target_pairs={{0,2},{2,0},{1,3},{3,1},{4,6},{6,4},{5,7},{7,5},{8,10},{10,8},{9,1... | collective-permute-start | bytes 1769480 | tf_op jit(solution)/shard_map/ppermute | solution.py:340
  90.5 1.0 copy-start.7
  90.6 14.7 %collective-permute-start.8 = (bf16[96,3072]{1,0:T(8,128)(2,1)S(1)}, bf16[96,3072]{1,0:T(8,128)(2,1)}, u32[]{:S(2)}, u32[]{:S(2)}) collective-permute-start(bf16[96,3072]{1,0:T(8,128)(2,1)S(1)} %slice.8), channel_id=1, source_target_pairs={{0,16},{16,0},{1,17},{17,1},{2,18},{18,2},{3,19},{19,3},{4,20},{20... | collective-permute-start | bytes 1769480 | tf_op jit(solution)/shard_map/ppermute | solution.py:339
  103.8 0.8 copy-start.15
  114.9 0.7 copy-start.4
  115.6 10.7 %collective-permute-start.10 = (bf16[256,768]{1,0:T(8,128)(2,1)S(1)}, bf16[256,768]{1,0:T(8,128)(2,1)S(1)}, u32[]{:S(2)}, u32[]{:S(2)}) collective-permute-start(bf16[256,768]{1,0:T(8,128)(2,1)S(1)} %get-tuple-element.47), channel_id=1, source_target_pairs={{0,2},{2,0},{1,3},{3,1},{4,6},{6,4},{5,7},{7,5},{8,10},{10,8},{9,1... | collective-permute-start | bytes 1179656 | tf_op jit(solution)/shard_map/ppermute | solution.py:424
  126.3 1.0 copy-start.5
  128.7 7.4 %collective-permute-start.11 = (bf16[512,768]{1,0:T(8,128)(2,1)S(1)}, bf16[512,768]{1,0:T(8,128)(2,1)S(1)}, u32[]{:S(2)}, u32[]{:S(2)}) collective-permute-start(bf16[512,768]{1,0:T(8,128)(2,1)S(1)} %weave_steps.1.tok_ref), channel_id=1, source_target_pairs={{0,1},{1,0},{2,3},{3,2},{4,5},{5,4},{6,7},{7,6},{8,9},{9,8},{10,11... | collective-permute-start | bytes 2359304 | tf_op jit(solution)/shard_map/ppermute | solution.py:440
  136.2 3.7 %copy-start = (bf16[768,6144]{1,0:T(8,128)(2,1)S(1)}, bf16[768,6144]{1,0:T(8,128)(2,1)}, u32[]{:S(2)}) copy-start(bf16[768,6144]{1,0:T(8,128)(2,1)} %put_rows.1.w_ref) | copy-start | bytes 28311556
  139.8 7.8 %copy-start.1 = (bf16[768,6144]{1,0:T(8,128)(2,1)S(1)}, bf16[768,6144]{1,0:T(8,128)(2,1)}, u32[]{:S(2)}) copy-start(bf16[768,6144]{1,0:T(8,128)(2,1)} %put_rows.1.w_ref) | copy-start | bytes 28311556
  147.1 7.8 %collective-permute-start.12 = (bf16[512,768]{1,0:T(8,128)(2,1)S(1)}, bf16[512,768]{1,0:T(8,128)(2,1)S(1)}, u32[]{:S(2)}, u32[]{:S(2)}) collective-permute-start(bf16[512,768]{1,0:T(8,128)(2,1)S(1)} %layer.3), channel_id=1, source_target_pairs={{0,1},{1,0},{2,3},{3,2},{4,5},{5,4},{6,7},{7,6},{8,9},{9,8},{10,11... | collective-permute-start | bytes 2359304 | tf_op jit(solution)/shard_map/ppermute | solution.py:442

commit v16 on v15

--- a/solution.py
+++ b/solution.py
@@ -221,45 +221,60 @@
     return dot_t(hidden, down_w)
 
 
-def put_rows_kernel(places, *refs):
-    pieces, (out_ref, sems) = refs[:-2], refs[-2:]
+def put_rows_kernel(plan, *refs):
+    sems, outs, pieces = refs[-1], refs[-3:-1], refs[:-3]
     copies = []
-    for number, ((row, at), piece) in enumerate(zip(places, pieces)):
-        rows, columns = piece.shape
-        target = out_ref.at[pl.ds(row, rows), pl.ds(at, columns)]
-        copies.append(pltpu.make_async_copy(piece, target, sems.at[number]))
+    for number, (piece, out, source, row, at, size) in enumerate(plan):
+        rows = pieces[piece].shape[0]
+        target = outs[out].at[pl.ds(row, rows), pl.ds(at, size)]
+        copies.append(pltpu.make_async_copy(pieces[piece].at[:, pl.ds(source, size)], target, sems.at[number]))
     for copy in copies:
         copy.start()
     for copy in copies:
         copy.wait()
 
 
-def put_rows(pieces, rows, columns):
-    return pl.pallas_call(
-        functools.partial(put_rows_kernel, [(row, at) for _, row, at in pieces]),
-        out_shape=jax.ShapeDtypeStruct((rows, columns), BF16),
+def put_rows(pieces, rows, heads_width, hidden_width):
+    gate_at, out_at = 3 * heads_width, 3 * heads_width + 2 * hidden_width
+    down_at = out_at + heads_width
+    end = down_at + hidden_width
+    runs = [(0, gate_at, 0, 0), (gate_at, out_at, 1, 0), (out_at, down_at, 0, gate_at), (down_at, end, 1, 2 * hidden_width)]
+    plan = []
+    for left, right, out, shift in runs:
+        for number, (array, row, at) in enumerate(pieces):
+            low, high = max(left, at), min(right, at + array.shape[1])
+            if low < high:
+                plan.append((number, out, low - at, row, shift + low - left, high - low))
+    return pl.pallas_call(
+        functools.partial(put_rows_kernel, plan),
+        out_shape=[
+            jax.ShapeDtypeStruct((rows, 4 * heads_width), BF16),
+            jax.ShapeDtypeStruct((rows, 3 * hidden_width), BF16),
+        ],
         in_specs=[FAR] * len(pieces),
-        out_specs=WHOLE,
-        scratch_shapes=[pltpu.SemaphoreType.DMA((len(pieces),))],
+        out_specs=[WHOLE] * 2,
+        scratch_shapes=[pltpu.SemaphoreType.DMA((len(plan),))],
         compiler_params=params(53),
-        cost_estimate=pl.CostEstimate(flops=0, bytes_accessed=4 * rows * columns, transcendentals=0),
+        cost_estimate=pl.CostEstimate(flops=0, bytes_accessed=4 * rows * end, transcendentals=0),
         name="put_rows",
     )(*[array for array, _, _ in pieces])
 
 
-def layer_kernel(hidden_width, tok_ref, w_ref, out_ref, norm_ref, ctx_ref, acc_ref):
+def layer_kernel(tok_ref, heads_ref, far_ref, out_ref, gated_ref, norm_ref, ctx_ref, acc_ref, sem):
+    copy = pltpu.make_async_copy(far_ref, gated_ref, sem)
+    copy.start()
     heads_width = ctx_ref.shape[1]
-    gate_at = 3 * heads_width
-    up_at = gate_at + hidden_width
-    out_at = up_at + hidden_width
-    down_at = out_at + heads_width
+    hidden_width = gated_ref.shape[1] // 3
     tokens = tok_ref[...].astype(F32)
     scale = lax.rsqrt(jnp.mean(tokens * tokens, axis=1, keepdims=True) + EPS)
     norm_ref[...] = (tokens * scale).astype(BF16)
-    attention(norm_ref[...], w_ref[:, :gate_at], heads_width, ctx_ref)
-    acc_ref[...] = dot_t(ctx_ref[...], w_ref[:, out_at:down_at])
+    attention(norm_ref[...], heads_ref[:, : 3 * heads_width], heads_width, ctx_ref)
+    acc_ref[...] = dot_t(ctx_ref[...], heads_ref[:, 3 * heads_width :])
+    copy.wait()
     for begin in range(0, hidden_width, UNIT):
-        gate_w, up_w, down_w = [w_ref[:, at + begin : at + begin + UNIT] for at in (gate_at, up_at, down_at)]
+        gate_w, up_w, down_w = [
+            gated_ref[:, at + begin : at + begin + UNIT] for at in (0, hidden_width, 2 * hidden_width)
+        ]
         add = gated(norm_ref[...], gate_w, up_w, down_w)
         if begin + UNIT < hidden_width:
             acc_ref[...] += add
@@ -267,26 +282,28 @@
             out_ref[...] = (acc_ref[...] + add).astype(out_ref.dtype)
 
 
-def layer(tokens, weights, heads_width, hidden_width, out_type):
+def layer(tokens, heads, hiddens, out_type):
     rows, width = tokens.shape
     return pl.pallas_call(
-        functools.partial(layer_kernel, hidden_width),
+        layer_kernel,
         out_shape=jax.ShapeDtypeStruct((rows, width), out_type),
-        in_specs=[WHOLE] * 2,
+        in_specs=[WHOLE, WHOLE, FAR],
         out_specs=WHOLE,
         scratch_shapes=[
+            pltpu.VMEM(hiddens.shape, BF16),
             pltpu.VMEM((rows, width), BF16),
-            pltpu.VMEM((rows, heads_width), BF16),
+            pltpu.VMEM((rows, heads.shape[1] // 4), BF16),
             pltpu.VMEM((rows, width), F32),
+            pltpu.SemaphoreType.DMA,
         ],
-        compiler_params=params(26),
-        cost_estimate=pl.CostEstimate(
-            flops=2 * rows * width * weights.shape[1],
-            bytes_accessed=2 * weights.size + 6 * rows * width,
-            transcendentals=rows * hidden_width,
+        compiler_params=params(36),
+        cost_estimate=pl.CostEstimate(
+            flops=2 * rows * (heads.size + hiddens.size),
+            bytes_accessed=2 * (heads.size + hiddens.size) + 6 * rows * width,
+            transcendentals=rows * hiddens.shape[1] // 3,
         ),
         name="layer",
-    )(tokens, weights)
+    )(tokens, heads, hiddens)
 
 
 def finish_kernel(tok_ref, sum_ref, got_ref, order_ref, out_ref):
@@ -395,6 +412,7 @@
     slot_dev = TSTEPS // n_slots
     my_slot = lax.axis_index("slots")
     n_share = n_groups * n_slots
+    heads_width, hidden_width = w_qkv.shape[2], w_gate_up.shape[2]
     share = w_qkv.shape[0] // n_share
     valid = jnp.arange(rows, dtype=jnp.int32) < obs_count[0]
     owner = obs_cell // (quarter * n_mp * n_slots) * n_mp + obs_cell // quarter % n_mp
@@ -427,20 +445,20 @@
             pieces.append((array, row, 0))
             row += array.shape[0]
         pieces += [(second[3], row, 0), (second[4], row, second[3].shape[1])]
+        weights = put_rows(pieces, width, heads_width, hidden_width)
+        other, weights = lax.optimization_barrier((other, weights))
         tokens = weave_steps(my_slot.reshape(1), order, keep, other, slot_dev)
-        tokens, arrays = lax.optimization_barrier((tokens, [array for array, _, _ in pieces]))
-        weights = put_rows([(array, row, at) for array, (_, row, at) in zip(arrays, pieces)], width, shard.shape[1])
     else:
         order = jnp.arange(width, dtype=jnp.int32)
-        weights = lax.all_gather(share_rows, ("cells", "groups", "slots"), axis=0, tiled=True)
+        whole = lax.all_gather(share_rows, ("cells", "groups", "slots"), axis=0, tiled=True)
+        weights = put_rows([(whole, 0, 0)], width, heads_width, hidden_width)
         tokens = tokens_by_exchanges(owner, position, obs_feat, time_embed, my_slot, capacity, slot_dev)
 
     swap = [(0, 1), (1, 0)]
-    heads_width, hidden_width = w_qkv.shape[2], w_gate_up.shape[2]
     partner = lax.ppermute(tokens, "mp", swap)
-    for_partner = layer(partner, weights, heads_width, hidden_width, BF16)
+    for_partner = layer(partner, *weights, BF16)
     from_partner = lax.ppermute(for_partner, "mp", swap)
-    own = layer(tokens, weights, heads_width, hidden_width, F32)
+    own = layer(tokens, *weights, F32)
     return finish(tokens, own, from_partner, order).reshape(quarter, TSTEPS, width)
 
 

time: 157 us -> 152 us (0.968)
  waiting for transfers between devices: 75.4 us -> 69.9 us
  Pallas kernels: 30.7 us -> 32.8 us
  local copies, waits for them, and re-layouts: 14.5 us -> 12.8 us
    ppermute x1, waiting for transfers between devices: 9.12 us -> 1.62 us  [on_device(): other = lax.ppermute(send, 'slots', [(0, 1), (1, 0)])]
    ppermute x1, waiting for transfers between devices: 0.01 us -> 2.27 us  [on_device(): partner = lax.ppermute(tokens, 'mp', swap)]
    pallas_call x3, Pallas kernels: 21.7 us -> 23.7 us  [the longest x2 16.2 us: layer(): pl.pallas_call(layer_kernel, out_shape=jax.ShapeDtypeStruct((rows, width)...]
    unnamed x44 -> x46, local copies, waits for them, and re-layouts: 10.2 us -> 8.55 us
  transfers between devices with their start and end apart: 14 -> 14, of which waited for: 9 -> 10; matrix products, arithmetic and copies ran while one was open for 3% -> 3% of each run, Pallas kernels for 12% -> 13%
where the time goes in v16:
time: 152 us; the launch traced here: 151 us
  waiting for transfers between devices  69.9 us (46%)
  Pallas kernels  32.8 us (22%)
  starting transfers between devices  19 us (12%)
  blocking collectives  14.1 us (9%)
  local copies, waits for them, and re-layouts  12.8 us (8%)
  other arithmetic  1.81 us (1%)
    ppermute x1, waiting for transfers between devices, to_other_places_by_halves(): by_group = lax.ppermute(shares, 'groups', swap)  25.5 us
    pallas_call x2, Pallas kernels, layer(): pl.pallas_call(layer_kernel, out_shape=jax.ShapeDtypeStruct((rows, width)...  16.2 us
    ppermute x3, waiting for transfers between devices, to_other_places(): places.append(lax.ppermute(shares, ('groups', 'slots'), pairs))  14.4 us
    all_to_all x1, blocking collectives, on_device(): lax.all_to_all(codes, ('cells', 'mp'), split_axis=0, concat_axis=0, tiled...  14.1 us
    ppermute x1, waiting for transfers between devices, to_other_places_by_halves(): right = lax.ppermute(by_group[:, cut:], 'slots', swap)  10.4 us
    unnamed x46, local copies, waits for them, and re-layouts  8.55 us
    all_to_all x1, waiting for transfers between devices, on_device(): lax.all_to_all(blocks, ('cells', 'mp'), split_axis=0, concat_axis=0, tile...  7.69 us
    pallas_call x1, Pallas kernels, put_rows(): pl.pallas_call(functools.partial(put_rows_kernel, plan), out_shape=[jax.S...  7.49 us
  transfers between devices with their start and end apart: 14, of which 10 were waited for; matrix products, arithmetic and copies ran while one was open for 3% of the time, Pallas kernels for 13%

profile of v16, /device:TPU:0, one launch (start us, length us, event | category | flops | bytes accessed | tf_op | source)
XLA Modules:
  0.0 151.4 jit_solution(1987710009313904766)
XLA Ops:
  0.0 0.8 dynamic-slice_bitcast_fusion.2
  0.8 0.9 dynamic-slice_bitcast_fusion.1
  1.7 0.9 dynamic-slice_bitcast_fusion
  2.6 0.0 copy-start.20
  2.7 1.2 constant_dynamic-slice_fusion
  4.0 3.1 %collective-permute-start = (bf16[48,6144]{1,0:T(8,128)(2,1)S(1)}, bf16[48,6144]{1,0:T(8,128)(2,1)S(1)}, u32[]{:S(2)}, u32[]{:S(2)}) collective-permute-start(bf16[48,6144]{1,0:T(8,128)(2,1)S(1)} %pad_maximum_fusion.1), channel_id=1, source_target_pairs={{0,4},{4,8},{8,12},{12,0},{1,5},{5,9},{9,13},{13,1},{2,6},{6,10},{... | collective-permute-start | bytes 1769480 | tf_op jit(solution)/shard_map/ppermute | solution.py:338
  7.8 0.7 place_codes.1
  8.5 14.1 %all_to_all.10.code_ref = s32[8,1,192]{2,1,0:T(1,128)S(1)} all-to-all(s32[8,1,192]{2,1,0:T(1,128)S(1)} %get-tuple-element.32), channel_id=1, replica_groups=mesh['groups'=2,'cells'=4,'slots'=2,'mp'=2] {'cells','mp'}, dimensions={0} | all-to-all | bytes 12288 | tf_op jit(solution)/shard_map/all_to_all | solution.py:431
  22.6 1.7 %collective-permute-start.1 = (bf16[48,6144]{1,0:T(8,128)(2,1)S(1)}, bf16[48,6144]{1,0:T(8,128)(2,1)S(1)}, u32[]{:S(2)}, u32[]{:S(2)}) collective-permute-start(bf16[48,6144]{1,0:T(8,128)(2,1)S(1)} %pad_maximum_fusion.1), channel_id=1, source_target_pairs={{0,12},{4,0},{8,4},{12,8},{1,13},{5,1},{9,5},{13,9},{2,14},{6,2},{... | collective-permute-start | bytes 1769480 | tf_op jit(solution)/shard_map/ppermute | solution.py:338
  24.4 2.4 %collective-permute-start.5 = (bf16[48,6144]{1,0:T(8,128)(2,1)S(1)}, bf16[48,6144]{1,0:T(8,128)(2,1)S(1)}, u32[]{:S(2)}, u32[]{:S(2)}) collective-permute-start(bf16[48,6144]{1,0:T(8,128)(2,1)S(1)} %collective-permute-done.refs_1_), channel_id=1, source_target_pairs={{0,18},{2,16},{16,2},{18,0},{1,19},{3,17},{17,3},{19,1},{4,22},{6,... | collective-permute-start | bytes 1769480 | tf_op jit(solution)/shard_map/ppermute | solution.py:347
  26.8 0.5 collective-permute-start.4
  27.3 0.5 collective-permute-start.3
  27.9 0.3 collective-permute-start.2
  28.2 3.0 %place_rows.1 = bf16[8,192,768]{2,1,0:T(8,128)(2,1)} custom-call(s32[1,512]{1,0:T(1,128)S(1)} %bitcast.22, bf16[512,768]{1,0:T(8,128)(2,1)S(1)} %copy-done.3), custom_call_target="tpu_custom_call" | custom-call | flops 1207959552 | bytes 3145728 | tf_op jit(solution)/shard_map/place_rows/pallas_call | solution.py:98
  31.2 7.4 %collective-permute-done.1 = bf16[48,6144]{1,0:T(8,128)(2,1)S(1)} collective-permute-done((bf16[48,6144]{1,0:T(8,128)(2,1)S(1)}, bf16[48,6144]{1,0:T(8,128)(2,1)S(1)}, u32[]{:S(2)}, u32[]{:S(2)}) %collective-permute-start.1) | collective-permute-done | bytes 589856 | tf_op jit(solution)/shard_map/ppermute | solution.py:338
  38.6 2.9 %collective-permute-done.5.refs_4_ = bf16[48,6144]{1,0:T(8,128)(2,1)S(1)} collective-permute-done((bf16[48,6144]{1,0:T(8,128)(2,1)S(1)}, bf16[48,6144]{1,0:T(8,128)(2,1)S(1)}, u32[]{:S(2)}, u32[]{:S(2)}) %collective-permute-start.5) | collective-permute-done | bytes 589856 | tf_op jit(solution)/shard_map/ppermute | solution.py:347
  41.5 11.4 %collective-permute-done.4.refs_3_ = bf16[48,6144]{1,0:T(8,128)(2,1)S(1)} collective-permute-done((bf16[48,6144]{1,0:T(8,128)(2,1)S(1)}, bf16[48,6144]{1,0:T(8,128)(2,1)S(1)}, u32[]{:S(2)}, u32[]{:S(2)}) %collective-permute-start.4) | collective-permute-done | bytes 589856 | tf_op jit(solution)/shard_map/ppermute | solution.py:347
  52.9 0.1 collective-permute-done.3.refs_2_
  53.0 0.7 copy-done.14
  53.8 0.8 copy-done.15
  54.6 3.8 %all-to-all-start.1 = ((bf16[8,192,768]{2,1,0:T(8,128)(2,1)}), bf16[8,192,768]{2,1,0:T(8,128)(2,1)S(1)}, u32[]{:S(2)}, u32[]{:S(2)}) async-start(bf16[8,192,768]{2,1,0:T(8,128)(2,1)} %place_rows.1), calls=%async_computation.1 | async-start | bytes 4718592 | tf_op jit(solution)/shard_map/all_to_all | solution.py:439
  58.4 1.2 constant_dynamic-update-slice_fusion.1
  59.6 1.2 constant_dynamic-update-slice_fusion.refs_5_
  60.8 1.6 %collective-permute-start.7 = (bf16[96,6144]{1,0:T(8,128)(2,1)S(1)}, bf16[96,6144]{1,0:T(8,128)(2,1)S(1)}, u32[]{:S(2)}, u32[]{:S(2)}) collective-permute-start(bf16[96,6144]{1,0:T(8,128)(2,1)S(1)} %constant_dynamic-update-slice_fusion.refs_5_), channel_id=1, source_target_pairs={{0,16},{16,0},{1,17},{17,1},{2,18},{18,2},{3,19},{19,3},{4,20},{20... | collective-permute-start | bytes 3538952 | tf_op jit(solution)/shard_map/ppermute | solution.py:354
  62.4 0.8 collective-permute-start.6
  63.2 0.1 copy.17
  63.4 25.5 %collective-permute-done.7.refs_7_ = bf16[96,6144]{1,0:T(8,128)(2,1)S(1)} collective-permute-done((bf16[96,6144]{1,0:T(8,128)(2,1)S(1)}, bf16[96,6144]{1,0:T(8,128)(2,1)S(1)}, u32[]{:S(2)}, u32[]{:S(2)}) %collective-permute-start.7) | collective-permute-done | bytes 1179680 | tf_op jit(solution)/shard_map/ppermute | solution.py:354
  89.0 1.6 %collective-permute-start.9 = (bf16[96,3072]{1,0:T(8,128)(2,1)S(1)}, bf16[96,3072]{1,0:T(8,128)(2,1)S(1)}, u32[]{:S(2)}, u32[]{:S(2)}) collective-permute-start(bf16[96,3072]{1,0:T(8,128)(2,1)S(1)} %slice.9), channel_id=1, source_target_pairs={{0,2},{2,0},{1,3},{3,1},{4,6},{6,4},{5,7},{7,5},{8,10},{10,8},{9,1... | collective-permute-start | bytes 1769480 | tf_op jit(solution)/shard_map/ppermute | solution.py:357
  90.6 0.9 collective-permute-start.8
  91.5 0.1 copy-done.8
  91.6 1.7 %pad_maximum_fusion.refs_0_ = bf16[192,6144]{1,0:T(8,128)(2,1)} fusion(bf16[192,1536]{1,0:T(8,128)(2,1)S(1)} %bitcast.29, bf16[192,384]{1,0:T(8,128)(2,1)S(1)} %bitcast.32, bf16[192,3072]{1,0:T(8,128)(2,1)S(1)} %bitcast.24, bf16[192,1152]{1,0:T(8,128)(2,1)S(1)} %bitcast.26), kind=kLoop, calls=%fused_computation | loop fusion | flops 9437184 | bytes 4718592 | tf_op jit(solution)/shard_map/concatenate | solution.py:333
  93.3 10.4 %collective-permute-done.9.refs_9_ = bf16[96,3072]{1,0:T(8,128)(2,1)S(1)} collective-permute-done((bf16[96,3072]{1,0:T(8,128)(2,1)S(1)}, bf16[96,3072]{1,0:T(8,128)(2,1)S(1)}, u32[]{:S(2)}, u32[]{:S(2)}) %collective-permute-start.9) | collective-permute-done | bytes 589856 | tf_op jit(solution)/shard_map/ppermute | solution.py:357
  103.7 0.8 copy-done.16
  104.5 0.6 collective-permute-done.8.refs_8_
  105.1 7.7 %all-to-all-done.1.got_ref = bf16[8,192,768]{2,1,0:T(8,128)(2,1)S(1)} async-done(((bf16[8,192,768]{2,1,0:T(8,128)(2,1)}), bf16[8,192,768]{2,1,0:T(8,128)(2,1)S(1)}, u32[]{:S(2)}, u32[]{:S(2)}) %all-to-all-start.1) | async-done | bytes 2359328 | tf_op jit(solution)/shard_map/all_to_all | solution.py:439
  112.8 2.1 %pool_rows.1 = (bf16[256,768]{1,0:T(8,128)(2,1)S(1)}, bf16[256,768]{1,0:T(8,128)(2,1)S(1)}) custom-call(s32[1]{0:T(128)} %bitcast.slot_ref, bf16[8,768]{1,0:T(8,128)(2,1)S(1)} %get-tuple-element.31.embed_ref, s32[8,1,192]{2,1,0:T(1,128)S(1)} %all_to_all.10.code_ref, bf16[8,192,768]{2,1,0:T(8,128)(2,1)S(1)} %all-to-all-done.1.got_ref), custom_call_target="tpu_custom_call" | custom-call | flops 1207959552 | bytes 2359296 | tf_op jit(solution)/shard_map/pool_rows/pallas_call | solution.py:138
  114.9 0.7 copy-done.5
  115.6 1.5 collective-permute-start.10
  117.2 7.5 %put_rows.1 = (bf16[768,1536]{1,0:T(8,128)(2,1)}, bf16[768,4608]{1,0:T(8,128)(2,1)}) custom-call(bf16[192,6144]{1,0:T(8,128)(2,1)} %pad_maximum_fusion.refs_0_, bf16[48,6144]{1,0:T(8,128)(2,1)S(1)} %collective-permute-done.refs_1_, bf16[48,6144]{1,0:T(8,128)(2,1)} %copy-done.15, bf16[48,6144]{1,0:T(8,128)(2,1)} %copy-done.14, bf16[48,6144]{1,0:T(8,128)(2,1)} %copy-done.13, ...), custom_call_target="tpu_custom_call" | custom-call | bytes 18874368 | tf_op jit(solution)/shard_map/put_rows/pallas_call | solution.py:248
  124.7 1.6 %collective-permute-done.10.got_ref = bf16[256,768]{1,0:T(8,128)(2,1)S(1)} collective-permute-done((bf16[256,768]{1,0:T(8,128)(2,1)S(1)}, bf16[256,768]{1,0:T(8,128)(2,1)S(1)}, u32[]{:S(2)}, u32[]{:S(2)}) %collective-permute-start.10) | collective-permute-done | bytes 393248 | tf_op jit(solution)/shard_map/ppermute | solution.py:442
  126.3 1.5 weave_steps.1.tok_ref
  127.7 0.1 collective-permute-start.11
  127.8 2.3 %collective-permute-done.11.tok_ref = bf16[512,768]{1,0:T(8,128)(2,1)S(1)} collective-permute-done((bf16[512,768]{1,0:T(8,128)(2,1)S(1)}, bf16[512,768]{1,0:T(8,128)(2,1)S(1)}, u32[]{:S(2)}, u32[]{:S(2)}) %collective-permute-start.11) | collective-permute-done | bytes 786464 | tf_op jit(solution)/shard_map/ppermute | solution.py:458
  130.1 3.0 %copy-done = bf16[768,4608]{1,0:T(8,128)(2,1)S(1)} copy-done((bf16[768,4608]{1,0:T(8,128)(2,1)S(1)}, bf16[768,4608]{1,0:T(8,128)(2,1)}, u32[]{:S(2)}) %copy-start) | copy-done | bytes 7077912
  133.1 8.0 %layer.3 = bf16[512,768]{1,0:T(8,128)(2,1)S(1)} custom-call(bf16[512,768]{1,0:T(8,128)(2,1)S(1)} %collective-permute-done.11.tok_ref, bf16[768,1536]{1,0:T(8,128)(2,1)S(1)} %copy-done.2, bf16[768,4608]{1,0:T(8,128)(2,1)S(1)} %copy-done), custom_call_target="tpu_custom_call" | custom-call | flops 4831838208 | bytes 11796480 | tf_op jit(solution)/shard_map/layer/pallas_call | solution.py:287
  141.1 0.2 collective-permute-start.12
  141.3 8.2 %layer.2.sum_ref = f32[512,768]{1,0:T(8,128)S(1)} custom-call(bf16[512,768]{1,0:T(8,128)(2,1)S(1)} %weave_steps.1.tok_ref, bf16[768,1536]{1,0:T(8,128)(2,1)S(1)} %copy-done.2, bf16[768,4608]{1,0:T(8,128)(2,1)S(1)} %copy-done.1), custom_call_target="tpu_custom_call" | custom-call | flops 4831838208 | bytes 11796480 | tf_op jit(solution)/shard_map/layer/pallas_call | solution.py:287
  149.6 1.8 %finish.1 = bf16[512,768]{1,0:T(8,128)(2,1)} custom-call(bf16[512,768]{1,0:T(8,128)(2,1)S(1)} %weave_steps.1.tok_ref, f32[512,768]{1,0:T(8,128)S(1)} %layer.2.sum_ref, bf16[512,768]{1,0:T(8,128)(2,1)S(1)} %collective-permute-done.12.got_ref, s32[1,768]{1,0:T(1,128)S(1)} %compare_select_fusion.6.order_ref), custom_call_target="tpu_custom_call" | custom-call | flops 603979776 | bytes 3932160 | tf_op jit(solution)/shard_map/finish/pallas_call | solution.py:318
  (47 shorter events, 0.4 us)
Async XLA Ops:
  2.6 5.1 %copy-start.19 = (s32[512]{0:T(512)S(1)}, s32[512]{0:T(512)}, u32[]{:S(2)}) copy-start(s32[512]{0:T(512)} %param.11) | copy-start | bytes 6148
  2.6 5.1 %copy-start.20 = (s32[512]{0:T(512)S(1)}, s32[512]{0:T(512)}, u32[]{:S(2)}) copy-start(s32[512]{0:T(512)} %param.10) | copy-start | bytes 6148
  2.7 5.1 %copy-start.4 = (bf16[8,768]{1,0:T(8,128)(2,1)S(1)}, bf16[8,768]{1,0:T(8,128)(2,1)}, u32[]{:S(2)}) copy-start(bf16[8,768]{1,0:T(8,128)(2,1)} %time_ref.1) | copy-start | bytes 36868
  2.7 25.5 %copy-start.3 = (bf16[512,768]{1,0:T(8,128)(2,1)S(1)}, bf16[512,768]{1,0:T(8,128)(2,1)}, u32[]{:S(2)}) copy-start(bf16[512,768]{1,0:T(8,128)(2,1)} %feat_ref.1) | copy-start | bytes 2359300
  4.0 18.6 %collective-permute-start = (bf16[48,6144]{1,0:T(8,128)(2,1)S(1)}, bf16[48,6144]{1,0:T(8,128)(2,1)S(1)}, u32[]{:S(2)}, u32[]{:S(2)}) collective-permute-start(bf16[48,6144]{1,0:T(8,128)(2,1)S(1)} %pad_maximum_fusion.1), channel_id=1, source_target_pairs={{0,4},{4,8},{8,12},{12,0},{1,5},{5,9},{9,13},{13,1},{2,6},{6,10},{... | collective-permute-start | bytes 1769480 | tf_op jit(solution)/shard_map/ppermute | solution.py:338
  22.6 16.0 %collective-permute-start.1 = (bf16[48,6144]{1,0:T(8,128)(2,1)S(1)}, bf16[48,6144]{1,0:T(8,128)(2,1)S(1)}, u32[]{:S(2)}, u32[]{:S(2)}) collective-permute-start(bf16[48,6144]{1,0:T(8,128)(2,1)S(1)} %pad_maximum_fusion.1), channel_id=1, source_target_pairs={{0,12},{4,0},{8,4},{12,8},{1,13},{5,1},{9,5},{13,9},{2,14},{6,2},{... | collective-permute-start | bytes 1769480 | tf_op jit(solution)/shard_map/ppermute | solution.py:338
  24.4 17.2 %collective-permute-start.5 = (bf16[48,6144]{1,0:T(8,128)(2,1)S(1)}, bf16[48,6144]{1,0:T(8,128)(2,1)S(1)}, u32[]{:S(2)}, u32[]{:S(2)}) collective-permute-start(bf16[48,6144]{1,0:T(8,128)(2,1)S(1)} %collective-permute-done.refs_1_), channel_id=1, source_target_pairs={{0,18},{2,16},{16,2},{18,0},{1,19},{3,17},{17,3},{19,1},{4,22},{6,... | collective-permute-start | bytes 1769480 | tf_op jit(solution)/shard_map/ppermute | solution.py:347
  26.8 26.1 %collective-permute-start.4 = (bf16[48,6144]{1,0:T(8,128)(2,1)S(1)}, bf16[48,6144]{1,0:T(8,128)(2,1)S(1)}, u32[]{:S(2)}, u32[]{:S(2)}) collective-permute-start(bf16[48,6144]{1,0:T(8,128)(2,1)S(1)} %collective-permute-done.refs_1_), channel_id=1, source_target_pairs={{0,16},{2,18},{16,0},{18,2},{1,17},{3,19},{17,1},{19,3},{4,20},{6,... | collective-permute-start | bytes 1769480 | tf_op jit(solution)/shard_map/ppermute | solution.py:347
  27.3 25.7 %collective-permute-start.3 = (bf16[48,6144]{1,0:T(8,128)(2,1)S(1)}, bf16[48,6144]{1,0:T(8,128)(2,1)S(1)}, u32[]{:S(2)}, u32[]{:S(2)}) collective-permute-start(bf16[48,6144]{1,0:T(8,128)(2,1)S(1)} %collective-permute-done.refs_1_), channel_id=1, source_target_pairs={{0,2},{2,0},{16,18},{18,16},{1,3},{3,1},{17,19},{19,17},{4,6},{6,4... | collective-permute-start | bytes 1769480 | tf_op jit(solution)/shard_map/ppermute | solution.py:347
  27.9 26.7 %collective-permute-start.2 = (bf16[48,6144]{1,0:T(8,128)(2,1)S(1)}, bf16[48,6144]{1,0:T(8,128)(2,1)}, u32[]{:S(2)}, u32[]{:S(2)}) collective-permute-start(bf16[48,6144]{1,0:T(8,128)(2,1)S(1)} %collective-permute-done.refs_1_), channel_id=1, source_target_pairs={{0,4},{4,8},{8,12},{12,0},{1,5},{5,9},{9,13},{13,1},{2,6},{6,10},{... | collective-permute-start | bytes 1769480 | tf_op jit(solution)/shard_map/ppermute | solution.py:338
  38.6 14.4 %copy-start.17 = (bf16[48,6144]{1,0:T(8,128)(2,1)}, bf16[48,6144]{1,0:T(8,128)(2,1)S(1)}, u32[]{:S(2)}) copy-start(bf16[48,6144]{1,0:T(8,128)(2,1)S(1)} %collective-permute-done.1) | copy-start | bytes 1769476
  41.5 11.5 %copy-start.13 = (bf16[48,6144]{1,0:T(8,128)(2,1)}, bf16[48,6144]{1,0:T(8,128)(2,1)S(1)}, u32[]{:S(2)}) copy-start(bf16[48,6144]{1,0:T(8,128)(2,1)S(1)} %collective-permute-done.5.refs_4_) | copy-start | bytes 1769476
  52.9 0.8 copy-start.14
  53.8 0.8 copy-start.15
  54.6 58.2 %all-to-all-start.1 = ((bf16[8,192,768]{2,1,0:T(8,128)(2,1)}), bf16[8,192,768]{2,1,0:T(8,128)(2,1)S(1)}, u32[]{:S(2)}, u32[]{:S(2)}) async-start(bf16[8,192,768]{2,1,0:T(8,128)(2,1)} %place_rows.1), calls=%async_computation.1 | async-start | bytes 4718592 | tf_op jit(solution)/shard_map/all_to_all | solution.py:439
  58.4 4.8 %copy-start.12 = (bf16[192,3,384]{2,0,1:T(8,128)(2,1)S(1)}, bf16[192,3,384]{2,0,1:T(8,128)(2,1)}, u32[]{:S(2)}) copy-start(bf16[192,3,384]{2,0,1:T(8,128)(2,1)} %param.14) | copy-start | bytes 1327108
  59.6 3.7 %copy-start.10 = (bf16[192,2,1536]{2,1,0:T(2,128)(2,1)S(1)}, bf16[192,2,1536]{2,1,0:T(2,128)(2,1)}, u32[]{:S(2)}) copy-start(bf16[192,2,1536]{2,1,0:T(2,128)(2,1)} %param.16) | copy-start | bytes 3538948
  60.8 2.6 %copy-start.9 = (bf16[96,6144]{1,0:T(8,128)(2,1)}, bf16[96,6144]{1,0:T(8,128)(2,1)S(1)}, u32[]{:S(2)}) copy-start(bf16[96,6144]{1,0:T(8,128)(2,1)S(1)} %constant_dynamic-update-slice_fusion.refs_5_) | copy-start | bytes 3538948
  60.8 28.2 %collective-permute-start.7 = (bf16[96,6144]{1,0:T(8,128)(2,1)S(1)}, bf16[96,6144]{1,0:T(8,128)(2,1)S(1)}, u32[]{:S(2)}, u32[]{:S(2)}) collective-permute-start(bf16[96,6144]{1,0:T(8,128)(2,1)S(1)} %constant_dynamic-update-slice_fusion.refs_5_), channel_id=1, source_target_pairs={{0,16},{16,0},{1,17},{17,1},{2,18},{18,2},{3,19},{19,3},{4,20},{20... | collective-permute-start | bytes 3538952 | tf_op jit(solution)/shard_map/ppermute | solution.py:354
  62.4 28.2 %collective-permute-start.6 = (bf16[96,6144]{1,0:T(8,128)(2,1)S(1)}, bf16[96,6144]{1,0:T(8,128)(2,1)S(1)}, u32[]{:S(2)}, u32[]{:S(2)}) collective-permute-start(bf16[96,6144]{1,0:T(8,128)(2,1)S(1)} %constant_dynamic-update-slice_fusion.refs_5_), channel_id=1, source_target_pairs={{0,2},{2,0},{1,3},{3,1},{4,6},{6,4},{5,7},{7,5},{8,10},{10,8},{9,1... | collective-permute-start | bytes 3538952 | tf_op jit(solution)/shard_map/ppermute | solution.py:353
  63.4 28.2 %copy-start.11 = (bf16[1536,192]{0,1:T(8,128)(2,1)S(1)}, bf16[1536,192]{0,1:T(8,128)(2,1)}, u32[]{:S(2)}) copy-start(bf16[1536,192]{0,1:T(8,128)(2,1)} %param.17) | copy-start | bytes 1769476
  63.4 28.2 %copy-start.18 = (bf16[384,192]{0,1:T(8,128)(2,1)S(1)}, bf16[384,192]{0,1:T(8,128)(2,1)}, u32[]{:S(2)}) copy-start(bf16[384,192]{0,1:T(8,128)(2,1)} %param.15) | copy-start | bytes 442372
  88.9 1.7 %copy-start.7 = (bf16[96,6144]{1,0:T(8,128)(2,1)}, bf16[96,6144]{1,0:T(8,128)(2,1)S(1)}, u32[]{:S(2)}) copy-start(bf16[96,6144]{1,0:T(8,128)(2,1)S(1)} %collective-permute-done.7.refs_7_) | copy-start | bytes 3538948
  89.0 14.7 %collective-permute-start.9 = (bf16[96,3072]{1,0:T(8,128)(2,1)S(1)}, bf16[96,3072]{1,0:T(8,128)(2,1)S(1)}, u32[]{:S(2)}, u32[]{:S(2)}) collective-permute-start(bf16[96,3072]{1,0:T(8,128)(2,1)S(1)} %slice.9), channel_id=1, source_target_pairs={{0,2},{2,0},{1,3},{3,1},{4,6},{6,4},{5,7},{7,5},{8,10},{10,8},{9,1... | collective-permute-start | bytes 1769480 | tf_op jit(solution)/shard_map/ppermute | solution.py:357
  90.5 1.0 copy-start.8
  90.6 14.5 %collective-permute-start.8 = (bf16[96,3072]{1,0:T(8,128)(2,1)S(1)}, bf16[96,3072]{1,0:T(8,128)(2,1)}, u32[]{:S(2)}, u32[]{:S(2)}) collective-permute-start(bf16[96,3072]{1,0:T(8,128)(2,1)S(1)} %slice.8), channel_id=1, source_target_pairs={{0,16},{16,0},{1,17},{17,1},{2,18},{18,2},{3,19},{19,3},{4,20},{20... | collective-permute-start | bytes 1769480 | tf_op jit(solution)/shard_map/ppermute | solution.py:356
  103.7 0.8 copy-start.16
  114.9 0.8 copy-start.5
  115.6 10.7 %collective-permute-start.10 = (bf16[256,768]{1,0:T(8,128)(2,1)S(1)}, bf16[256,768]{1,0:T(8,128)(2,1)S(1)}, u32[]{:S(2)}, u32[]{:S(2)}) collective-permute-start(bf16[256,768]{1,0:T(8,128)(2,1)S(1)} %get-tuple-element.41), channel_id=1, source_target_pairs={{0,2},{2,0},{1,3},{3,1},{4,6},{6,4},{5,7},{7,5},{8,10},{10,8},{9,1... | collective-permute-start | bytes 1179656 | tf_op jit(solution)/shard_map/ppermute | solution.py:442
  117.2 9.1 %copy-start.6 = (bf16[256,768]{1,0:T(8,128)(2,1)S(1)}, bf16[256,768]{1,0:T(8,128)(2,1)}, u32[]{:S(2)}) copy-start(bf16[256,768]{1,0:T(8,128)(2,1)} %copy-done.5) | copy-start | bytes 1179652
  126.3 3.8 %copy-start.2 = (bf16[768,1536]{1,0:T(8,128)(2,1)S(1)}, bf16[768,1536]{1,0:T(8,128)(2,1)}, u32[]{:S(2)}) copy-start(bf16[768,1536]{1,0:T(8,128)(2,1)} %get-tuple-element.55.heads_ref) | copy-start | bytes 7077892
  127.7 2.4 %collective-permute-start.11 = (bf16[512,768]{1,0:T(8,128)(2,1)S(1)}, bf16[512,768]{1,0:T(8,128)(2,1)S(1)}, u32[]{:S(2)}, u32[]{:S(2)}) collective-permute-start(bf16[512,768]{1,0:T(8,128)(2,1)S(1)} %weave_steps.1.tok_ref), channel_id=1, source_target_pairs={{0,1},{1,0},{2,3},{3,2},{4,5},{5,4},{6,7},{7,6},{8,9},{9,8},{10,11... | collective-permute-start | bytes 2359304 | tf_op jit(solution)/shard_map/ppermute | solution.py:458
  130.1 3.0 %copy-start = (bf16[768,4608]{1,0:T(8,128)(2,1)S(1)}, bf16[768,4608]{1,0:T(8,128)(2,1)}, u32[]{:S(2)}) copy-start(bf16[768,4608]{1,0:T(8,128)(2,1)} %get-tuple-element.56.far_ref) | copy-start | bytes 21233668
  133.1 8.2 %copy-start.1 = (bf16[768,4608]{1,0:T(8,128)(2,1)S(1)}, bf16[768,4608]{1,0:T(8,128)(2,1)}, u32[]{:S(2)}) copy-start(bf16[768,4608]{1,0:T(8,128)(2,1)} %get-tuple-element.56.far_ref) | copy-start | bytes 21233668
  141.1 8.5 %collective-permute-start.12 = (bf16[512,768]{1,0:T(8,128)(2,1)S(1)}, bf16[512,768]{1,0:T(8,128)(2,1)S(1)}, u32[]{:S(2)}, u32[]{:S(2)}) collective-permute-start(bf16[512,768]{1,0:T(8,128)(2,1)S(1)} %layer.3), channel_id=1, source_target_pairs={{0,1},{1,0},{2,3},{3,2},{4,5},{5,4},{6,7},{7,6},{8,9},{9,8},{10,11... | collective-permute-start | bytes 2359304 | tf_op jit(solution)/shard_map/ppermute | solution.py:460

commit v17 on v16

--- a/solution.py
+++ b/solution.py
@@ -296,7 +296,7 @@
             pltpu.VMEM((rows, width), F32),
             pltpu.SemaphoreType.DMA,
         ],
-        compiler_params=params(36),
+        compiler_params=params(58),
         cost_estimate=pl.CostEstimate(
             flops=2 * rows * (heads.size + hiddens.size),
             bytes_accessed=2 * (heads.size + hiddens.size) + 6 * rows * width,
@@ -428,12 +428,12 @@
         order = arrival_order(width, n_share)
         below = along_cells(share_rows, -1)
         codes, embed = place_codes(owner, position, time_embed, n_owners, capacity)
+        below, codes, share_rows = lax.optimization_barrier((below, codes, share_rows))
         codes = lax.all_to_all(codes, ("cells", "mp"), split_axis=0, concat_axis=0, tiled=True)
-        below, codes, share_rows = lax.optimization_barrier((below, codes, share_rows))
         first = to_other_places(below)
         blocks = place_rows(owner, obs_feat, n_owners, capacity)
         above, opposite = along_cells(share_rows, 1), along_cells(below, -1)
-        blocks, above, opposite, first = lax.optimization_barrier((blocks, above, opposite, first))
+        blocks, codes, above, opposite, first = lax.optimization_barrier((blocks, codes, above, opposite, first))
         second = to_other_places_by_halves(jnp.concatenate([above, opposite], axis=0))
         shard = side_by_side(*local_weights)
         got = lax.all_to_all(blocks, ("cells", "mp"), split_axis=0, concat_axis=0, tiled=True)

time: 152 us -> 155 us (1.020)
  blocking collectives: 14.1 us -> 0 us
  waiting for transfers between devices: 69.9 us -> 77.6 us
  Pallas kernels: 32.8 us -> 38.1 us
  starting transfers between devices: 19 us -> 23.9 us
  local copies, waits for them, and re-layouts: 12.8 us -> 11.1 us
    all_to_all x0 -> x1, waiting for transfers between devices: none -> 14.2 us  [on_device(): lax.all_to_all(codes, ('cells', 'mp'), split_axis=0, concat_axis=0, tiled...]
    all_to_all x1 -> x0, blocking collectives: 14.1 us -> none  [on_device(): lax.all_to_all(codes, ('cells', 'mp'), split_axis=0, concat_axis=0, tiled...]
    ppermute x3, waiting for transfers between devices: 14.4 us -> 1.81 us  [to_other_places(): places.append(lax.ppermute(shares, ('groups', 'slots'), pairs))]
    ppermute x3, waiting for transfers between devices: 7.42 us -> 13.5 us  [along_cells(): lax.ppermute(values, 'cells', [(j, (j - distance) % n_cells) for j in ran...]
    all_to_all x0 -> x1, starting transfers between devices: none -> 4.82 us  [on_device(): lax.all_to_all(codes, ('cells', 'mp'), split_axis=0, concat_axis=0, tiled...]
    pallas_call x2, Pallas kernels: 16.2 us -> 20.9 us  [layer(): pl.pallas_call(layer_kernel, out_shape=jax.ShapeDtypeStruct((rows, width)...]
    unnamed x46 -> x44, local copies, waits for them, and re-layouts: 8.55 us -> 6.8 us
  transfers between devices with their start and end apart: 14 -> 15, of which waited for: 10 -> 10; matrix products, arithmetic and copies ran while one was open for 3% -> 3% of each run, Pallas kernels for 13% -> 15%
where the time goes in v17:
time: 155 us; the launch traced here: 154 us
  waiting for transfers between devices  77.6 us (50%)
  Pallas kernels  38.1 us (25%)
  starting transfers between devices  23.9 us (15%)
  local copies, waits for them, and re-layouts  11.1 us (7%)
  other arithmetic  2.53 us (2%)
    ppermute x1, waiting for transfers between devices, to_other_places_by_halves(): by_group = lax.ppermute(shares, 'groups', swap)  25.6 us
    pallas_call x2, Pallas kernels, layer(): pl.pallas_call(layer_kernel, out_shape=jax.ShapeDtypeStruct((rows, width)...  20.9 us
    all_to_all x1, waiting for transfers between devices, on_device(): lax.all_to_all(codes, ('cells', 'mp'), split_axis=0, concat_axis=0, tiled...  14.2 us
    ppermute x3, waiting for transfers between devices, along_cells(): lax.ppermute(values, 'cells', [(j, (j - distance) % n_cells) for j in ran...  13.5 us
    ppermute x1, waiting for transfers between devices, to_other_places_by_halves(): right = lax.ppermute(by_group[:, cut:], 'slots', swap)  10.5 us
    pallas_call x1, Pallas kernels, put_rows(): pl.pallas_call(functools.partial(put_rows_kernel, plan), out_shape=[jax.S...  7.54 us
    all_to_all x1, waiting for transfers between devices, on_device(): lax.all_to_all(blocks, ('cells', 'mp'), split_axis=0, concat_axis=0, tile...  7.53 us
    unnamed x44, local copies, waits for them, and re-layouts  6.8 us
  transfers between devices with their start and end apart: 15, of which 10 were waited for; matrix products, arithmetic and copies ran while one was open for 3% of the time, Pallas kernels for 15%

profile of v17, /device:TPU:0, one launch (start us, length us, event | category | flops | bytes accessed | tf_op | source)
XLA Modules:
  0.0 154.3 jit_solution(8549398918277253148)
XLA Ops:
  0.0 0.8 dynamic-slice_bitcast_fusion.2
  0.8 0.9 dynamic-slice_bitcast_fusion.1
  1.7 0.9 dynamic-slice_bitcast_fusion
  2.6 0.0 copy-start.17
  2.7 1.2 constant_dynamic-slice_fusion
  4.0 0.9 pad_maximum_fusion.1
  4.8 3.0 %collective-permute-start = (bf16[48,6144]{1,0:T(8,128)(2,1)}, bf16[48,6144]{1,0:T(8,128)(2,1)S(1)}, u32[]{:S(2)}, u32[]{:S(2)}) collective-permute-start(bf16[48,6144]{1,0:T(8,128)(2,1)} %pad_maximum_fusion.1), channel_id=1, source_target_pairs={{0,4},{4,8},{8,12},{12,0},{1,5},{5,9},{9,13},{13,1},{2,6},{6,10},{... | collective-permute-start | bytes 1769480 | tf_op jit(solution)/shard_map/ppermute | solution.py:338
  8.6 1.3 place_codes.1
  9.9 13.5 %collective-permute-done.refs_1_ = bf16[48,6144]{1,0:T(8,128)(2,1)S(1)} collective-permute-done((bf16[48,6144]{1,0:T(8,128)(2,1)}, bf16[48,6144]{1,0:T(8,128)(2,1)S(1)}, u32[]{:S(2)}, u32[]{:S(2)}) %collective-permute-start) | collective-permute-done | bytes 589856 | tf_op jit(solution)/shard_map/ppermute | solution.py:338
  23.4 1.7 %collective-permute-start.1 = (bf16[48,6144]{1,0:T(8,128)(2,1)}, bf16[48,6144]{1,0:T(8,128)(2,1)}, u32[]{:S(2)}, u32[]{:S(2)}) collective-permute-start(bf16[48,6144]{1,0:T(8,128)(2,1)} %pad_maximum_fusion.1), channel_id=1, source_target_pairs={{0,12},{4,0},{8,4},{12,8},{1,13},{5,1},{9,5},{13,9},{2,14},{6,2},{... | collective-permute-start | bytes 1769480 | tf_op jit(solution)/shard_map/ppermute | solution.py:338
  25.2 2.4 %collective-permute-start.5 = (bf16[48,6144]{1,0:T(8,128)(2,1)S(1)}, bf16[48,6144]{1,0:T(8,128)(2,1)S(1)}, u32[]{:S(2)}, u32[]{:S(2)}) collective-permute-start(bf16[48,6144]{1,0:T(8,128)(2,1)S(1)} %collective-permute-done.refs_1_), channel_id=1, source_target_pairs={{0,18},{2,16},{16,2},{18,0},{1,19},{3,17},{17,3},{19,1},{4,22},{6,... | collective-permute-start | bytes 1769480 | tf_op jit(solution)/shard_map/ppermute | solution.py:347
  27.6 0.5 collective-permute-start.4
  28.1 0.5 collective-permute-start.3
  28.6 0.3 collective-permute-start.2
  28.9 4.8 %all-to-all-start = ((s32[8,1,192]{2,1,0:T(1,128)}), s32[8,1,192]{2,1,0:T(1,128)S(1)}, u32[]{:S(2)}, u32[]{:S(2)}) async-start(s32[8,1,192]{2,1,0:T(1,128)} %get-tuple-element.34), calls=%async_computation | async-start | bytes 16384 | tf_op jit(solution)/shard_map/all_to_all | solution.py:432
  33.8 3.0 %place_rows.1 = bf16[8,192,768]{2,1,0:T(8,128)(2,1)} custom-call(s32[1,512]{1,0:T(1,128)S(1)} %bitcast.22, bf16[512,768]{1,0:T(8,128)(2,1)S(1)} %copy-done.3), custom_call_target="tpu_custom_call" | custom-call | flops 1207959552 | bytes 3145728 | tf_op jit(solution)/shard_map/place_rows/pallas_call | solution.py:98
  36.8 14.2 %all-to-all-done.code_ref = s32[8,1,192]{2,1,0:T(1,128)S(1)} async-done(((s32[8,1,192]{2,1,0:T(1,128)}), s32[8,1,192]{2,1,0:T(1,128)S(1)}, u32[]{:S(2)}, u32[]{:S(2)}) %all-to-all-start) | async-done | bytes 6176 | tf_op jit(solution)/shard_map/all_to_all | solution.py:432
  51.0 1.6 %collective-permute-done.4.refs_3_ = bf16[48,6144]{1,0:T(8,128)(2,1)S(1)} collective-permute-done((bf16[48,6144]{1,0:T(8,128)(2,1)S(1)}, bf16[48,6144]{1,0:T(8,128)(2,1)S(1)}, u32[]{:S(2)}, u32[]{:S(2)}) %collective-permute-start.4) | collective-permute-done | bytes 589856 | tf_op jit(solution)/shard_map/ppermute | solution.py:347
  52.6 0.2 collective-permute-done.3.refs_2_
  52.8 0.6 copy-done.14
  53.4 3.6 %all-to-all-start.1 = ((bf16[8,192,768]{2,1,0:T(8,128)(2,1)}), bf16[8,192,768]{2,1,0:T(8,128)(2,1)S(1)}, u32[]{:S(2)}, u32[]{:S(2)}) async-start(bf16[8,192,768]{2,1,0:T(8,128)(2,1)} %place_rows.1), calls=%async_computation.1 | async-start | bytes 4718592 | tf_op jit(solution)/shard_map/all_to_all | solution.py:439
  57.1 1.2 constant_dynamic-update-slice_fusion.1
  58.2 1.2 constant_dynamic-update-slice_fusion.refs_5_
  59.4 1.6 %collective-permute-start.7 = (bf16[96,6144]{1,0:T(8,128)(2,1)S(1)}, bf16[96,6144]{1,0:T(8,128)(2,1)S(1)}, u32[]{:S(2)}, u32[]{:S(2)}) collective-permute-start(bf16[96,6144]{1,0:T(8,128)(2,1)S(1)} %constant_dynamic-update-slice_fusion.refs_5_), channel_id=1, source_target_pairs={{0,16},{16,0},{1,17},{17,1},{2,18},{18,2},{3,19},{19,3},{4,20},{20... | collective-permute-start | bytes 3538952 | tf_op jit(solution)/shard_map/ppermute | solution.py:354
  61.1 0.9 collective-permute-start.6
  62.0 0.1 copy.17
  62.2 25.6 %collective-permute-done.7.refs_7_ = bf16[96,6144]{1,0:T(8,128)(2,1)S(1)} collective-permute-done((bf16[96,6144]{1,0:T(8,128)(2,1)S(1)}, bf16[96,6144]{1,0:T(8,128)(2,1)S(1)}, u32[]{:S(2)}, u32[]{:S(2)}) %collective-permute-start.7) | collective-permute-done | bytes 1179680 | tf_op jit(solution)/shard_map/ppermute | solution.py:354
  87.8 1.6 %collective-permute-start.9 = (bf16[96,3072]{1,0:T(8,128)(2,1)S(1)}, bf16[96,3072]{1,0:T(8,128)(2,1)S(1)}, u32[]{:S(2)}, u32[]{:S(2)}) collective-permute-start(bf16[96,3072]{1,0:T(8,128)(2,1)S(1)} %slice.9), channel_id=1, source_target_pairs={{0,2},{2,0},{1,3},{3,1},{4,6},{6,4},{5,7},{7,5},{8,10},{10,8},{9,1... | collective-permute-start | bytes 1769480 | tf_op jit(solution)/shard_map/ppermute | solution.py:357
  89.4 1.1 collective-permute-start.8
  90.6 1.6 %pad_maximum_fusion.refs_0_ = bf16[192,6144]{1,0:T(8,128)(2,1)} fusion(bf16[192,1536]{1,0:T(8,128)(2,1)S(1)} %bitcast.29, bf16[192,384]{1,0:T(8,128)(2,1)S(1)} %bitcast.32, bf16[192,3072]{1,0:T(8,128)(2,1)S(1)} %bitcast.24, bf16[192,1152]{1,0:T(8,128)(2,1)S(1)} %bitcast.26), kind=kLoop, calls=%fused_computation | loop fusion | flops 9437184 | bytes 4718592 | tf_op jit(solution)/shard_map/concatenate | solution.py:333
  92.2 10.5 %collective-permute-done.9.refs_9_ = bf16[96,3072]{1,0:T(8,128)(2,1)S(1)} collective-permute-done((bf16[96,3072]{1,0:T(8,128)(2,1)S(1)}, bf16[96,3072]{1,0:T(8,128)(2,1)S(1)}, u32[]{:S(2)}, u32[]{:S(2)}) %collective-permute-start.9) | collective-permute-done | bytes 589856 | tf_op jit(solution)/shard_map/ppermute | solution.py:357
  102.7 0.8 copy-done.15
  103.5 0.6 collective-permute-done.8.refs_8_
  104.1 7.5 %all-to-all-done.1.got_ref = bf16[8,192,768]{2,1,0:T(8,128)(2,1)S(1)} async-done(((bf16[8,192,768]{2,1,0:T(8,128)(2,1)}), bf16[8,192,768]{2,1,0:T(8,128)(2,1)S(1)}, u32[]{:S(2)}, u32[]{:S(2)}) %all-to-all-start.1) | async-done | bytes 2359328 | tf_op jit(solution)/shard_map/all_to_all | solution.py:439
  111.7 2.1 %pool_rows.1 = (bf16[256,768]{1,0:T(8,128)(2,1)S(1)}, bf16[256,768]{1,0:T(8,128)(2,1)S(1)}) custom-call(s32[1]{0:T(128)} %bitcast.slot_ref, bf16[8,768]{1,0:T(8,128)(2,1)S(1)} %get-tuple-element.32.embed_ref, s32[8,1,192]{2,1,0:T(1,128)S(1)} %all-to-all-done.code_ref, bf16[8,192,768]{2,1,0:T(8,128)(2,1)S(1)} %all-to-all-done.1.got_ref), custom_call_target="tpu_custom_call" | custom-call | flops 1207959552 | bytes 2359296 | tf_op jit(solution)/shard_map/pool_rows/pallas_call | solution.py:138
  113.7 0.7 copy-done.5
  114.5 1.5 collective-permute-start.10
  116.0 7.5 %put_rows.1 = (bf16[768,1536]{1,0:T(8,128)(2,1)}, bf16[768,4608]{1,0:T(8,128)(2,1)}) custom-call(bf16[192,6144]{1,0:T(8,128)(2,1)} %pad_maximum_fusion.refs_0_, bf16[48,6144]{1,0:T(8,128)(2,1)S(1)} %collective-permute-done.refs_1_, bf16[48,6144]{1,0:T(8,128)(2,1)} %collective-permute-done.3.refs_2_, bf16[48,6144]{1,0:T(8,128)(2,1)} %copy-done.14, ...), custom_call_target="tpu_custom_call" | custom-call | bytes 18874368 | tf_op jit(solution)/shard_map/put_rows/pallas_call | solution.py:248
  123.6 1.6 %collective-permute-done.10.got_ref = bf16[256,768]{1,0:T(8,128)(2,1)S(1)} collective-permute-done((bf16[256,768]{1,0:T(8,128)(2,1)S(1)}, bf16[256,768]{1,0:T(8,128)(2,1)S(1)}, u32[]{:S(2)}, u32[]{:S(2)}) %collective-permute-start.10) | collective-permute-done | bytes 393248 | tf_op jit(solution)/shard_map/ppermute | solution.py:442
  125.1 1.5 weave_steps.1.tok_ref
  126.6 0.1 collective-permute-start.11
  126.7 2.3 %collective-permute-done.11.tok_ref = bf16[512,768]{1,0:T(8,128)(2,1)S(1)} collective-permute-done((bf16[512,768]{1,0:T(8,128)(2,1)S(1)}, bf16[512,768]{1,0:T(8,128)(2,1)S(1)}, u32[]{:S(2)}, u32[]{:S(2)}) %collective-permute-start.11) | collective-permute-done | bytes 786464 | tf_op jit(solution)/shard_map/ppermute | solution.py:458
  129.0 0.9 copy-done.19
  129.9 10.3 %layer.3 = bf16[512,768]{1,0:T(8,128)(2,1)} custom-call(bf16[512,768]{1,0:T(8,128)(2,1)} %copy-done.19, bf16[768,1536]{1,0:T(8,128)(2,1)} %get-tuple-element.57.heads_ref, bf16[768,4608]{1,0:T(8,128)(2,1)} %get-tuple-element.58.far_ref), custom_call_target="tpu_custom_call" | custom-call | flops 4831838208 | bytes 11796480 | tf_op jit(solution)/shard_map/layer/pallas_call | solution.py:287
  140.2 0.2 collective-permute-start.12
  140.4 10.6 %layer.2.sum_ref = f32[512,768]{1,0:T(8,128)} custom-call(bf16[512,768]{1,0:T(8,128)(2,1)} %copy-done.1, bf16[768,1536]{1,0:T(8,128)(2,1)} %get-tuple-element.57.heads_ref, bf16[768,4608]{1,0:T(8,128)(2,1)} %get-tuple-element.58.far_ref), custom_call_target="tpu_custom_call" | custom-call | flops 4831838208 | bytes 11796480 | tf_op jit(solution)/shard_map/layer/pallas_call | solution.py:287
  151.1 1.4 copy-done
  152.5 1.8 %finish.1 = bf16[512,768]{1,0:T(8,128)(2,1)} custom-call(bf16[512,768]{1,0:T(8,128)(2,1)S(1)} %copy-done.2, f32[512,768]{1,0:T(8,128)S(1)} %copy-done, bf16[512,768]{1,0:T(8,128)(2,1)S(1)} %collective-permute-done.12.got_ref, s32[1,768]{1,0:T(1,128)S(1)} %compare_select_fusion.6.order_ref), custom_call_target="tpu_custom_call" | custom-call | flops 603979776 | bytes 3932160 | tf_op jit(solution)/shard_map/finish/pallas_call | solution.py:318
  (46 shorter events, 0.3 us)
Async XLA Ops:
  2.6 5.9 %copy-start.17 = (s32[512]{0:T(512)S(1)}, s32[512]{0:T(512)}, u32[]{:S(2)}) copy-start(s32[512]{0:T(512)} %param.11) | copy-start | bytes 6148
  2.6 5.9 %copy-start.18 = (s32[512]{0:T(512)S(1)}, s32[512]{0:T(512)}, u32[]{:S(2)}) copy-start(s32[512]{0:T(512)} %param.10) | copy-start | bytes 6148
  2.7 5.9 %copy-start.4 = (bf16[8,768]{1,0:T(8,128)(2,1)S(1)}, bf16[8,768]{1,0:T(8,128)(2,1)}, u32[]{:S(2)}) copy-start(bf16[8,768]{1,0:T(8,128)(2,1)} %time_ref.1) | copy-start | bytes 36868
  2.7 31.1 %copy-start.3 = (bf16[512,768]{1,0:T(8,128)(2,1)S(1)}, bf16[512,768]{1,0:T(8,128)(2,1)}, u32[]{:S(2)}) copy-start(bf16[512,768]{1,0:T(8,128)(2,1)} %feat_ref.1) | copy-start | bytes 2359300
  4.8 18.6 %collective-permute-start = (bf16[48,6144]{1,0:T(8,128)(2,1)}, bf16[48,6144]{1,0:T(8,128)(2,1)S(1)}, u32[]{:S(2)}, u32[]{:S(2)}) collective-permute-start(bf16[48,6144]{1,0:T(8,128)(2,1)} %pad_maximum_fusion.1), channel_id=1, source_target_pairs={{0,4},{4,8},{8,12},{12,0},{1,5},{5,9},{9,13},{13,1},{2,6},{6,10},{... | collective-permute-start | bytes 1769480 | tf_op jit(solution)/shard_map/ppermute | solution.py:338
  23.4 27.6 %collective-permute-start.1 = (bf16[48,6144]{1,0:T(8,128)(2,1)}, bf16[48,6144]{1,0:T(8,128)(2,1)}, u32[]{:S(2)}, u32[]{:S(2)}) collective-permute-start(bf16[48,6144]{1,0:T(8,128)(2,1)} %pad_maximum_fusion.1), channel_id=1, source_target_pairs={{0,12},{4,0},{8,4},{12,8},{1,13},{5,1},{9,5},{13,9},{2,14},{6,2},{... | collective-permute-start | bytes 1769480 | tf_op jit(solution)/shard_map/ppermute | solution.py:338
  25.2 25.8 %collective-permute-start.5 = (bf16[48,6144]{1,0:T(8,128)(2,1)S(1)}, bf16[48,6144]{1,0:T(8,128)(2,1)S(1)}, u32[]{:S(2)}, u32[]{:S(2)}) collective-permute-start(bf16[48,6144]{1,0:T(8,128)(2,1)S(1)} %collective-permute-done.refs_1_), channel_id=1, source_target_pairs={{0,18},{2,16},{16,2},{18,0},{1,19},{3,17},{17,3},{19,1},{4,22},{6,... | collective-permute-start | bytes 1769480 | tf_op jit(solution)/shard_map/ppermute | solution.py:347
  27.6 25.0 %collective-permute-start.4 = (bf16[48,6144]{1,0:T(8,128)(2,1)S(1)}, bf16[48,6144]{1,0:T(8,128)(2,1)S(1)}, u32[]{:S(2)}, u32[]{:S(2)}) collective-permute-start(bf16[48,6144]{1,0:T(8,128)(2,1)S(1)} %collective-permute-done.refs_1_), channel_id=1, source_target_pairs={{0,16},{2,18},{16,0},{18,2},{1,17},{3,19},{17,1},{19,3},{4,20},{6,... | collective-permute-start | bytes 1769480 | tf_op jit(solution)/shard_map/ppermute | solution.py:347
  28.1 24.7 %collective-permute-start.3 = (bf16[48,6144]{1,0:T(8,128)(2,1)S(1)}, bf16[48,6144]{1,0:T(8,128)(2,1)}, u32[]{:S(2)}, u32[]{:S(2)}) collective-permute-start(bf16[48,6144]{1,0:T(8,128)(2,1)S(1)} %collective-permute-done.refs_1_), channel_id=1, source_target_pairs={{0,2},{2,0},{16,18},{18,16},{1,3},{3,1},{17,19},{19,17},{4,6},{6,4... | collective-permute-start | bytes 1769480 | tf_op jit(solution)/shard_map/ppermute | solution.py:347
  28.6 24.2 %collective-permute-start.2 = (bf16[48,6144]{1,0:T(8,128)(2,1)S(1)}, bf16[48,6144]{1,0:T(8,128)(2,1)}, u32[]{:S(2)}, u32[]{:S(2)}) collective-permute-start(bf16[48,6144]{1,0:T(8,128)(2,1)S(1)} %collective-permute-done.refs_1_), channel_id=1, source_target_pairs={{0,4},{4,8},{8,12},{12,0},{1,5},{5,9},{9,13},{13,1},{2,6},{6,10},{... | collective-permute-start | bytes 1769480 | tf_op jit(solution)/shard_map/ppermute | solution.py:338
  28.9 22.1 %all-to-all-start = ((s32[8,1,192]{2,1,0:T(1,128)}), s32[8,1,192]{2,1,0:T(1,128)S(1)}, u32[]{:S(2)}, u32[]{:S(2)}) async-start(s32[8,1,192]{2,1,0:T(1,128)} %get-tuple-element.34), calls=%async_computation | async-start | bytes 16384 | tf_op jit(solution)/shard_map/all_to_all | solution.py:432
  51.0 1.8 %copy-start.13 = (bf16[48,6144]{1,0:T(8,128)(2,1)}, bf16[48,6144]{1,0:T(8,128)(2,1)S(1)}, u32[]{:S(2)}) copy-start(bf16[48,6144]{1,0:T(8,128)(2,1)S(1)} %collective-permute-done.5.refs_4_) | copy-start | bytes 1769476
  52.6 0.8 copy-start.14
  53.4 58.2 %all-to-all-start.1 = ((bf16[8,192,768]{2,1,0:T(8,128)(2,1)}), bf16[8,192,768]{2,1,0:T(8,128)(2,1)S(1)}, u32[]{:S(2)}, u32[]{:S(2)}) async-start(bf16[8,192,768]{2,1,0:T(8,128)(2,1)} %place_rows.1), calls=%async_computation.1 | async-start | bytes 4718592 | tf_op jit(solution)/shard_map/all_to_all | solution.py:439
  57.1 4.9 %copy-start.12 = (bf16[192,3,384]{2,0,1:T(8,128)(2,1)S(1)}, bf16[192,3,384]{2,0,1:T(8,128)(2,1)}, u32[]{:S(2)}) copy-start(bf16[192,3,384]{2,0,1:T(8,128)(2,1)} %param.14) | copy-start | bytes 1327108
  58.2 3.8 %copy-start.10 = (bf16[192,2,1536]{2,1,0:T(2,128)(2,1)S(1)}, bf16[192,2,1536]{2,1,0:T(2,128)(2,1)}, u32[]{:S(2)}) copy-start(bf16[192,2,1536]{2,1,0:T(2,128)(2,1)} %param.16) | copy-start | bytes 3538948
  59.4 2.7 %copy-start.9 = (bf16[96,6144]{1,0:T(8,128)(2,1)}, bf16[96,6144]{1,0:T(8,128)(2,1)S(1)}, u32[]{:S(2)}) copy-start(bf16[96,6144]{1,0:T(8,128)(2,1)S(1)} %constant_dynamic-update-slice_fusion.refs_5_) | copy-start | bytes 3538948
  59.4 28.3 %collective-permute-start.7 = (bf16[96,6144]{1,0:T(8,128)(2,1)S(1)}, bf16[96,6144]{1,0:T(8,128)(2,1)S(1)}, u32[]{:S(2)}, u32[]{:S(2)}) collective-permute-start(bf16[96,6144]{1,0:T(8,128)(2,1)S(1)} %constant_dynamic-update-slice_fusion.refs_5_), channel_id=1, source_target_pairs={{0,16},{16,0},{1,17},{17,1},{2,18},{18,2},{3,19},{19,3},{4,20},{20... | collective-permute-start | bytes 3538952 | tf_op jit(solution)/shard_map/ppermute | solution.py:354
  61.1 28.3 %collective-permute-start.6 = (bf16[96,6144]{1,0:T(8,128)(2,1)S(1)}, bf16[96,6144]{1,0:T(8,128)(2,1)S(1)}, u32[]{:S(2)}, u32[]{:S(2)}) collective-permute-start(bf16[96,6144]{1,0:T(8,128)(2,1)S(1)} %constant_dynamic-update-slice_fusion.refs_5_), channel_id=1, source_target_pairs={{0,2},{2,0},{1,3},{3,1},{4,6},{6,4},{5,7},{7,5},{8,10},{10,8},{9,1... | collective-permute-start | bytes 3538952 | tf_op jit(solution)/shard_map/ppermute | solution.py:353
  62.2 28.4 %copy-start.11 = (bf16[1536,192]{0,1:T(8,128)(2,1)S(1)}, bf16[1536,192]{0,1:T(8,128)(2,1)}, u32[]{:S(2)}) copy-start(bf16[1536,192]{0,1:T(8,128)(2,1)} %param.17) | copy-start | bytes 1769476
  62.2 28.4 %copy-start.16 = (bf16[384,192]{0,1:T(8,128)(2,1)S(1)}, bf16[384,192]{0,1:T(8,128)(2,1)}, u32[]{:S(2)}) copy-start(bf16[384,192]{0,1:T(8,128)(2,1)} %param.15) | copy-start | bytes 442372
  87.8 1.7 %copy-start.7 = (bf16[96,6144]{1,0:T(8,128)(2,1)}, bf16[96,6144]{1,0:T(8,128)(2,1)S(1)}, u32[]{:S(2)}) copy-start(bf16[96,6144]{1,0:T(8,128)(2,1)S(1)} %collective-permute-done.7.refs_7_) | copy-start | bytes 3538948
  87.8 14.9 %collective-permute-start.9 = (bf16[96,3072]{1,0:T(8,128)(2,1)S(1)}, bf16[96,3072]{1,0:T(8,128)(2,1)S(1)}, u32[]{:S(2)}, u32[]{:S(2)}) collective-permute-start(bf16[96,3072]{1,0:T(8,128)(2,1)S(1)} %slice.9), channel_id=1, source_target_pairs={{0,2},{2,0},{1,3},{3,1},{4,6},{6,4},{5,7},{7,5},{8,10},{10,8},{9,1... | collective-permute-start | bytes 1769480 | tf_op jit(solution)/shard_map/ppermute | solution.py:357
  89.4 1.2 copy-start.8
  89.4 14.7 %collective-permute-start.8 = (bf16[96,3072]{1,0:T(8,128)(2,1)S(1)}, bf16[96,3072]{1,0:T(8,128)(2,1)}, u32[]{:S(2)}, u32[]{:S(2)}) collective-permute-start(bf16[96,3072]{1,0:T(8,128)(2,1)S(1)} %slice.8), channel_id=1, source_target_pairs={{0,16},{16,0},{1,17},{17,1},{2,18},{18,2},{3,19},{19,3},{4,20},{20... | collective-permute-start | bytes 1769480 | tf_op jit(solution)/shard_map/ppermute | solution.py:356
  102.7 0.8 copy-start.15
  113.7 0.7 copy-start.5
  114.5 10.7 %collective-permute-start.10 = (bf16[256,768]{1,0:T(8,128)(2,1)S(1)}, bf16[256,768]{1,0:T(8,128)(2,1)S(1)}, u32[]{:S(2)}, u32[]{:S(2)}) collective-permute-start(bf16[256,768]{1,0:T(8,128)(2,1)S(1)} %get-tuple-element.43), channel_id=1, source_target_pairs={{0,2},{2,0},{1,3},{3,1},{4,6},{6,4},{5,7},{7,5},{8,10},{10,8},{9,1... | collective-permute-start | bytes 1179656 | tf_op jit(solution)/shard_map/ppermute | solution.py:442
  116.0 9.1 %copy-start.6 = (bf16[256,768]{1,0:T(8,128)(2,1)S(1)}, bf16[256,768]{1,0:T(8,128)(2,1)}, u32[]{:S(2)}) copy-start(bf16[256,768]{1,0:T(8,128)(2,1)} %copy-done.5) | copy-start | bytes 1179652
  126.6 13.6 %copy-start.1 = (bf16[512,768]{1,0:T(8,128)(2,1)}, bf16[512,768]{1,0:T(8,128)(2,1)S(1)}, u32[]{:S(2)}) copy-start(bf16[512,768]{1,0:T(8,128)(2,1)S(1)} %weave_steps.1.tok_ref) | copy-start | bytes 2359300
  126.6 2.4 %collective-permute-start.11 = (bf16[512,768]{1,0:T(8,128)(2,1)S(1)}, bf16[512,768]{1,0:T(8,128)(2,1)S(1)}, u32[]{:S(2)}, u32[]{:S(2)}) collective-permute-start(bf16[512,768]{1,0:T(8,128)(2,1)S(1)} %weave_steps.1.tok_ref), channel_id=1, source_target_pairs={{0,1},{1,0},{2,3},{3,2},{4,5},{5,4},{6,7},{7,6},{8,9},{9,8},{10,11... | collective-permute-start | bytes 2359304 | tf_op jit(solution)/shard_map/ppermute | solution.py:458
  129.0 0.9 copy-start.19
  140.2 10.8 %collective-permute-start.12 = (bf16[512,768]{1,0:T(8,128)(2,1)}, bf16[512,768]{1,0:T(8,128)(2,1)S(1)}, u32[]{:S(2)}, u32[]{:S(2)}) collective-permute-start(bf16[512,768]{1,0:T(8,128)(2,1)} %layer.3), channel_id=1, source_target_pairs={{0,1},{1,0},{2,3},{3,2},{4,5},{5,4},{6,7},{7,6},{8,9},{9,8},{10,11... | collective-permute-start | bytes 2359304 | tf_op jit(solution)/shard_map/ppermute | solution.py:460
  140.4 10.6 %copy-start.2 = (bf16[512,768]{1,0:T(8,128)(2,1)S(1)}, bf16[512,768]{1,0:T(8,128)(2,1)}, u32[]{:S(2)}) copy-start(bf16[512,768]{1,0:T(8,128)(2,1)} %copy-done.1) | copy-start | bytes 2359300
  151.1 1.4 copy-start

commit v18 on v17

--- a/solution.py
+++ b/solution.py
@@ -222,7 +222,7 @@
 
 
 def put_rows_kernel(plan, *refs):
-    sems, outs, pieces = refs[-1], refs[-3:-1], refs[:-3]
+    sems, outs, pieces = refs[-1], refs[-4:-1], refs[:-4]
     copies = []
     for number, (piece, out, source, row, at, size) in enumerate(plan):
         rows = pieces[piece].shape[0]
@@ -238,7 +238,7 @@
     gate_at, out_at = 3 * heads_width, 3 * heads_width + 2 * hidden_width
     down_at = out_at + heads_width
     end = down_at + hidden_width
-    runs = [(0, gate_at, 0, 0), (gate_at, out_at, 1, 0), (out_at, down_at, 0, gate_at), (down_at, end, 1, 2 * hidden_width)]
+    runs = [(0, gate_at, 0, 0), (gate_at, out_at, 1, 0), (out_at, down_at, 0, gate_at), (down_at, end, 2, 0)]
     plan = []
     for left, right, out, shift in runs:
         for number, (array, row, at) in enumerate(pieces):
@@ -249,10 +249,11 @@
         functools.partial(put_rows_kernel, plan),
         out_shape=[
             jax.ShapeDtypeStruct((rows, 4 * heads_width), BF16),
-            jax.ShapeDtypeStruct((rows, 3 * hidden_width), BF16),
+            jax.ShapeDtypeStruct((rows, 2 * hidden_width), BF16),
+            jax.ShapeDtypeStruct((rows, hidden_width), BF16),
         ],
         in_specs=[FAR] * len(pieces),
-        out_specs=[WHOLE] * 2,
+        out_specs=[WHOLE] * 3,
         scratch_shapes=[pltpu.SemaphoreType.DMA((len(plan),))],
         compiler_params=params(53),
         cost_estimate=pl.CostEstimate(flops=0, bytes_accessed=4 * rows * end, transcendentals=0),
@@ -260,50 +261,45 @@
     )(*[array for array, _, _ in pieces])
 
 
-def layer_kernel(tok_ref, heads_ref, far_ref, out_ref, gated_ref, norm_ref, ctx_ref, acc_ref, sem):
-    copy = pltpu.make_async_copy(far_ref, gated_ref, sem)
-    copy.start()
+def layer_kernel(tok_ref, heads_ref, gate_up_ref, down_ref, out_ref, norm_ref, ctx_ref, acc_ref):
     heads_width = ctx_ref.shape[1]
-    hidden_width = gated_ref.shape[1] // 3
+    hidden_width = down_ref.shape[1]
     tokens = tok_ref[...].astype(F32)
     scale = lax.rsqrt(jnp.mean(tokens * tokens, axis=1, keepdims=True) + EPS)
     norm_ref[...] = (tokens * scale).astype(BF16)
     attention(norm_ref[...], heads_ref[:, : 3 * heads_width], heads_width, ctx_ref)
     acc_ref[...] = dot_t(ctx_ref[...], heads_ref[:, 3 * heads_width :])
-    copy.wait()
     for begin in range(0, hidden_width, UNIT):
-        gate_w, up_w, down_w = [
-            gated_ref[:, at + begin : at + begin + UNIT] for at in (0, hidden_width, 2 * hidden_width)
-        ]
-        add = gated(norm_ref[...], gate_w, up_w, down_w)
-        if begin + UNIT < hidden_width:
+        end = begin + UNIT
+        gate_w, up_w = gate_up_ref[:, begin:end], gate_up_ref[:, hidden_width + begin : hidden_width + end]
+        add = gated(norm_ref[...], gate_w, up_w, down_ref[:, begin:end])
+        if end < hidden_width:
             acc_ref[...] += add
         else:
             out_ref[...] = (acc_ref[...] + add).astype(out_ref.dtype)
 
 
-def layer(tokens, heads, hiddens, out_type):
+def layer(tokens, heads, gate_up, down, out_type):
     rows, width = tokens.shape
+    size = heads.size + gate_up.size + down.size
     return pl.pallas_call(
         layer_kernel,
         out_shape=jax.ShapeDtypeStruct((rows, width), out_type),
-        in_specs=[WHOLE, WHOLE, FAR],
+        in_specs=[WHOLE] * 4,
         out_specs=WHOLE,
         scratch_shapes=[
-            pltpu.VMEM(hiddens.shape, BF16),
             pltpu.VMEM((rows, width), BF16),
             pltpu.VMEM((rows, heads.shape[1] // 4), BF16),
             pltpu.VMEM((rows, width), F32),
-            pltpu.SemaphoreType.DMA,
         ],
-        compiler_params=params(58),
-        cost_estimate=pl.CostEstimate(
-            flops=2 * rows * (heads.size + hiddens.size),
-            bytes_accessed=2 * (heads.size + hiddens.size) + 6 * rows * width,
-            transcendentals=rows * hiddens.shape[1] // 3,
+        compiler_params=params(28),
+        cost_estimate=pl.CostEstimate(
+            flops=2 * rows * size,
+            bytes_accessed=2 * size + 6 * rows * width,
+            transcendentals=rows * down.shape[1],
         ),
         name="layer",
-    )(tokens, heads, hiddens)
+    )(tokens, heads, gate_up, down)
 
 
 def finish_kernel(tok_ref, sum_ref, got_ref, order_ref, out_ref):

time: 155 us -> 150 us (0.968)
  Pallas kernels: 38.1 us -> 31.8 us
  local copies, waits for them, and re-layouts: 11.1 us -> 14.8 us
  waiting for transfers between devices: 77.6 us -> 75.5 us
    pallas_call x2, Pallas kernels: 20.9 us -> 14.6 us  [layer(): pl.pallas_call(layer_kernel, out_shape=jax.ShapeDtypeStruct((rows, width)...]
    unnamed x44 -> x46, local copies, waits for them, and re-layouts: 6.8 us -> 10.7 us
    all_to_all x1, waiting for transfers between devices: 7.53 us -> 5.52 us  [on_device(): lax.all_to_all(blocks, ('cells', 'mp'), split_axis=0, concat_axis=0, tile...]
  transfers between devices with their start and end apart: 15 -> 15, of which waited for: 10 -> 10; matrix products, arithmetic and copies ran while one was open for 3% -> 3% of each run, Pallas kernels for 15% -> 13%
where the time goes in v18:
time: 150 us
  waiting for transfers between devices  75.5 us (50%)
  Pallas kernels  31.8 us (21%)
  starting transfers between devices  23.9 us (16%)
  local copies, waits for them, and re-layouts  14.8 us (10%)
  other arithmetic  2.6 us (2%)
    ppermute x1, waiting for transfers between devices, to_other_places_by_halves(): by_group = lax.ppermute(shares, 'groups', swap)  25.6 us
    pallas_call x2, Pallas kernels, layer(): pl.pallas_call(layer_kernel, out_shape=jax.ShapeDtypeStruct((rows, width)...  14.6 us
    all_to_all x1, waiting for transfers between devices, on_device(): lax.all_to_all(codes, ('cells', 'mp'), split_axis=0, concat_axis=0, tiled...  14.2 us
    ppermute x3, waiting for transfers between devices, along_cells(): lax.ppermute(values, 'cells', [(j, (j - distance) % n_cells) for j in ran...  13.5 us
    unnamed x46, local copies, waits for them, and re-layouts  10.7 us
    ppermute x1, waiting for transfers between devices, to_other_places_by_halves(): right = lax.ppermute(by_group[:, cut:], 'slots', swap)  9.45 us
    pallas_call x1, Pallas kernels, put_rows(): pl.pallas_call(functools.partial(put_rows_kernel, plan), out_shape=[jax.S...  7.59 us
    all_to_all x1, waiting for transfers between devices, on_device(): lax.all_to_all(blocks, ('cells', 'mp'), split_axis=0, concat_axis=0, tile...  5.52 us
  transfers between devices with their start and end apart: 15, of which 10 were waited for; matrix products, arithmetic and copies ran while one was open for 3% of the time, Pallas kernels for 13%

profile of v18, /device:TPU:0, one launch (start us, length us, event | category | flops | bytes accessed | tf_op | source)
XLA Modules:
  0.0 149.6 jit_solution(10620955136596137518)
XLA Ops:
  0.0 0.8 dynamic-slice_bitcast_fusion.2
  0.8 1.0 dynamic-slice_bitcast_fusion.1
  1.8 0.9 dynamic-slice_bitcast_fusion
  2.8 1.2 constant_dynamic-slice_fusion
  4.0 0.9 pad_maximum_fusion.1
  4.8 3.0 %collective-permute-start = (bf16[48,6144]{1,0:T(8,128)(2,1)}, bf16[48,6144]{1,0:T(8,128)(2,1)S(1)}, u32[]{:S(2)}, u32[]{:S(2)}) collective-permute-start(bf16[48,6144]{1,0:T(8,128)(2,1)} %pad_maximum_fusion.1), channel_id=1, source_target_pairs={{0,4},{4,8},{8,12},{12,0},{1,5},{5,9},{9,13},{13,1},{2,6},{6,10},{... | collective-permute-start | bytes 1769480 | tf_op jit(solution)/shard_map/ppermute | solution.py:334
  8.6 1.3 place_codes.1
  9.9 13.5 %collective-permute-done.refs_1_ = bf16[48,6144]{1,0:T(8,128)(2,1)S(1)} collective-permute-done((bf16[48,6144]{1,0:T(8,128)(2,1)}, bf16[48,6144]{1,0:T(8,128)(2,1)S(1)}, u32[]{:S(2)}, u32[]{:S(2)}) %collective-permute-start) | collective-permute-done | bytes 589856 | tf_op jit(solution)/shard_map/ppermute | solution.py:334
  23.4 1.7 %collective-permute-start.1 = (bf16[48,6144]{1,0:T(8,128)(2,1)}, bf16[48,6144]{1,0:T(8,128)(2,1)}, u32[]{:S(2)}, u32[]{:S(2)}) collective-permute-start(bf16[48,6144]{1,0:T(8,128)(2,1)} %pad_maximum_fusion.1), channel_id=1, source_target_pairs={{0,12},{4,0},{8,4},{12,8},{1,13},{5,1},{9,5},{13,9},{2,14},{6,2},{... | collective-permute-start | bytes 1769480 | tf_op jit(solution)/shard_map/ppermute | solution.py:334
  25.2 2.4 %collective-permute-start.5 = (bf16[48,6144]{1,0:T(8,128)(2,1)S(1)}, bf16[48,6144]{1,0:T(8,128)(2,1)S(1)}, u32[]{:S(2)}, u32[]{:S(2)}) collective-permute-start(bf16[48,6144]{1,0:T(8,128)(2,1)S(1)} %collective-permute-done.refs_1_), channel_id=1, source_target_pairs={{0,18},{2,16},{16,2},{18,0},{1,19},{3,17},{17,3},{19,1},{4,22},{6,... | collective-permute-start | bytes 1769480 | tf_op jit(solution)/shard_map/ppermute | solution.py:343
  27.6 0.5 collective-permute-start.4
  28.1 0.5 collective-permute-start.3
  28.6 0.3 collective-permute-start.2
  28.9 4.8 %all-to-all-start = ((s32[8,1,192]{2,1,0:T(1,128)}), s32[8,1,192]{2,1,0:T(1,128)S(1)}, u32[]{:S(2)}, u32[]{:S(2)}) async-start(s32[8,1,192]{2,1,0:T(1,128)} %get-tuple-element.36), calls=%async_computation | async-start | bytes 16384 | tf_op jit(solution)/shard_map/all_to_all | solution.py:428
  33.8 3.0 %place_rows.1 = bf16[8,192,768]{2,1,0:T(8,128)(2,1)} custom-call(s32[1,512]{1,0:T(1,128)S(1)} %bitcast.22, bf16[512,768]{1,0:T(8,128)(2,1)S(1)} %copy-done.5), custom_call_target="tpu_custom_call" | custom-call | flops 1207959552 | bytes 3145728 | tf_op jit(solution)/shard_map/place_rows/pallas_call | solution.py:98
  36.8 14.2 %all-to-all-done.code_ref = s32[8,1,192]{2,1,0:T(1,128)S(1)} async-done(((s32[8,1,192]{2,1,0:T(1,128)}), s32[8,1,192]{2,1,0:T(1,128)S(1)}, u32[]{:S(2)}, u32[]{:S(2)}) %all-to-all-start) | async-done | bytes 6176 | tf_op jit(solution)/shard_map/all_to_all | solution.py:428
  51.0 1.6 %collective-permute-done.4.refs_3_ = bf16[48,6144]{1,0:T(8,128)(2,1)S(1)} collective-permute-done((bf16[48,6144]{1,0:T(8,128)(2,1)S(1)}, bf16[48,6144]{1,0:T(8,128)(2,1)S(1)}, u32[]{:S(2)}, u32[]{:S(2)}) %collective-permute-start.4) | collective-permute-done | bytes 589856 | tf_op jit(solution)/shard_map/ppermute | solution.py:343
  52.6 0.2 collective-permute-done.3.refs_2_
  52.8 0.6 copy-done.16
  53.4 3.6 %all-to-all-start.1 = ((bf16[8,192,768]{2,1,0:T(8,128)(2,1)}), bf16[8,192,768]{2,1,0:T(8,128)(2,1)S(1)}, u32[]{:S(2)}, u32[]{:S(2)}) async-start(bf16[8,192,768]{2,1,0:T(8,128)(2,1)} %place_rows.1), calls=%async_computation.1 | async-start | bytes 4718592 | tf_op jit(solution)/shard_map/all_to_all | solution.py:435
  57.1 1.2 constant_dynamic-update-slice_fusion.1
  58.3 1.1 constant_dynamic-update-slice_fusion.refs_5_
  59.4 1.6 %collective-permute-start.7 = (bf16[96,6144]{1,0:T(8,128)(2,1)S(1)}, bf16[96,6144]{1,0:T(8,128)(2,1)S(1)}, u32[]{:S(2)}, u32[]{:S(2)}) collective-permute-start(bf16[96,6144]{1,0:T(8,128)(2,1)S(1)} %constant_dynamic-update-slice_fusion.refs_5_), channel_id=1, source_target_pairs={{0,16},{16,0},{1,17},{17,1},{2,18},{18,2},{3,19},{19,3},{4,20},{20... | collective-permute-start | bytes 3538952 | tf_op jit(solution)/shard_map/ppermute | solution.py:350
  61.0 0.9 collective-permute-start.6
  62.0 0.1 copy.17
  62.1 25.6 %collective-permute-done.7.refs_7_ = bf16[96,6144]{1,0:T(8,128)(2,1)S(1)} collective-permute-done((bf16[96,6144]{1,0:T(8,128)(2,1)S(1)}, bf16[96,6144]{1,0:T(8,128)(2,1)S(1)}, u32[]{:S(2)}, u32[]{:S(2)}) %collective-permute-start.7) | collective-permute-done | bytes 1179680 | tf_op jit(solution)/shard_map/ppermute | solution.py:350
  87.7 1.0 copy-done.9
  88.8 1.6 %collective-permute-start.9 = (bf16[96,3072]{1,0:T(8,128)(2,1)S(1)}, bf16[96,3072]{1,0:T(8,128)(2,1)S(1)}, u32[]{:S(2)}, u32[]{:S(2)}) collective-permute-start(bf16[96,3072]{1,0:T(8,128)(2,1)S(1)} %slice.9), channel_id=1, source_target_pairs={{0,2},{2,0},{1,3},{3,1},{4,6},{6,4},{5,7},{7,5},{8,10},{10,8},{9,1... | collective-permute-start | bytes 1769480 | tf_op jit(solution)/shard_map/ppermute | solution.py:353
  90.4 1.0 copy-done.10
  91.4 1.1 collective-permute-start.8
  92.6 1.7 %pad_maximum_fusion.refs_0_ = bf16[192,6144]{1,0:T(8,128)(2,1)} fusion(bf16[192,1536]{1,0:T(8,128)(2,1)S(1)} %bitcast.29, bf16[192,384]{1,0:T(8,128)(2,1)S(1)} %bitcast.32, bf16[192,3072]{1,0:T(8,128)(2,1)S(1)} %bitcast.24, bf16[192,1152]{1,0:T(8,128)(2,1)S(1)} %bitcast.26), kind=kLoop, calls=%fused_computation | loop fusion | flops 9437184 | bytes 4718592 | tf_op jit(solution)/shard_map/concatenate | solution.py:329
  94.2 9.4 %collective-permute-done.9.refs_9_ = bf16[96,3072]{1,0:T(8,128)(2,1)S(1)} collective-permute-done((bf16[96,3072]{1,0:T(8,128)(2,1)S(1)}, bf16[96,3072]{1,0:T(8,128)(2,1)S(1)}, u32[]{:S(2)}, u32[]{:S(2)}) %collective-permute-start.9) | collective-permute-done | bytes 589856 | tf_op jit(solution)/shard_map/ppermute | solution.py:353
  103.7 0.8 copy-done.17
  104.5 1.6 %collective-permute-done.8.refs_8_ = bf16[96,3072]{1,0:T(8,128)(2,1)} collective-permute-done((bf16[96,3072]{1,0:T(8,128)(2,1)S(1)}, bf16[96,3072]{1,0:T(8,128)(2,1)}, u32[]{:S(2)}, u32[]{:S(2)}) %collective-permute-start.8) | collective-permute-done | bytes 589856 | tf_op jit(solution)/shard_map/ppermute | solution.py:352
  106.1 5.5 %all-to-all-done.1.got_ref = bf16[8,192,768]{2,1,0:T(8,128)(2,1)S(1)} async-done(((bf16[8,192,768]{2,1,0:T(8,128)(2,1)}), bf16[8,192,768]{2,1,0:T(8,128)(2,1)S(1)}, u32[]{:S(2)}, u32[]{:S(2)}) %all-to-all-start.1) | async-done | bytes 2359328 | tf_op jit(solution)/shard_map/all_to_all | solution.py:435
  111.7 2.0 %pool_rows.1 = (bf16[256,768]{1,0:T(8,128)(2,1)S(1)}, bf16[256,768]{1,0:T(8,128)(2,1)S(1)}) custom-call(s32[1]{0:T(128)} %bitcast.slot_ref, bf16[8,768]{1,0:T(8,128)(2,1)S(1)} %get-tuple-element.34.embed_ref, s32[8,1,192]{2,1,0:T(1,128)S(1)} %all-to-all-done.code_ref, bf16[8,192,768]{2,1,0:T(8,128)(2,1)S(1)} %all-to-all-done.1.got_ref), custom_call_target="tpu_custom_call" | custom-call | flops 1207959552 | bytes 2359296 | tf_op jit(solution)/shard_map/pool_rows/pallas_call | solution.py:138
  113.7 0.7 copy-done.7
  114.5 1.5 collective-permute-start.10
  116.0 7.6 %put_rows.1 = (bf16[768,1536]{1,0:T(8,128)(2,1)}, bf16[768,3072]{1,0:T(8,128)(2,1)}, bf16[768,1536]{1,0:T(8,128)(2,1)}) custom-call(bf16[192,6144]{1,0:T(8,128)(2,1)} %pad_maximum_fusion.refs_0_, bf16[48,6144]{1,0:T(8,128)(2,1)S(1)} %collective-permute-done.refs_1_, bf16[48,6144]{1,0:T(8,128)(2,1)} %collective-permute-done.3.refs_2_, ...), custom_call_target="tpu_custom_call" | custom-call | bytes 18874368 | tf_op jit(solution)/shard_map/put_rows/pallas_call | solution.py:248
  123.6 1.5 %collective-permute-done.10.got_ref = bf16[256,768]{1,0:T(8,128)(2,1)S(1)} collective-permute-done((bf16[256,768]{1,0:T(8,128)(2,1)S(1)}, bf16[256,768]{1,0:T(8,128)(2,1)S(1)}, u32[]{:S(2)}, u32[]{:S(2)}) %collective-permute-start.10) | collective-permute-done | bytes 393248 | tf_op jit(solution)/shard_map/ppermute | solution.py:438
  125.1 1.5 weave_steps.1.tok_ref
  126.7 2.3 %collective-permute-done.11.tok_ref = bf16[512,768]{1,0:T(8,128)(2,1)S(1)} collective-permute-done((bf16[512,768]{1,0:T(8,128)(2,1)S(1)}, bf16[512,768]{1,0:T(8,128)(2,1)S(1)}, u32[]{:S(2)}, u32[]{:S(2)}) %collective-permute-start.11) | collective-permute-done | bytes 786464 | tf_op jit(solution)/shard_map/ppermute | solution.py:454
  128.9 2.3 %copy-done = bf16[768,3072]{1,0:T(8,128)(2,1)S(1)} copy-done((bf16[768,3072]{1,0:T(8,128)(2,1)S(1)}, bf16[768,3072]{1,0:T(8,128)(2,1)}, u32[]{:S(2)}) %copy-start) | copy-done | bytes 4718616
  131.3 1.7 %copy-done.3 = bf16[768,1536]{1,0:T(8,128)(2,1)S(1)} copy-done((bf16[768,1536]{1,0:T(8,128)(2,1)S(1)}, bf16[768,1536]{1,0:T(8,128)(2,1)}, u32[]{:S(2)}) %copy-start.3) | copy-done | bytes 2359320
  133.0 7.2 %layer.3 = bf16[512,768]{1,0:T(8,128)(2,1)S(1)} custom-call(bf16[512,768]{1,0:T(8,128)(2,1)S(1)} %collective-permute-done.11.tok_ref, bf16[768,1536]{1,0:T(8,128)(2,1)S(1)} %copy-done.2, bf16[768,3072]{1,0:T(8,128)(2,1)S(1)} %copy-done, bf16[768,1536]{1,0:T(8,128)(2,1)S(1)} %copy-done.3), custom_call_target="tpu_custom_call" | custom-call | flops 4831838208 | bytes 11796480 | tf_op jit(solution)/shard_map/layer/pallas_call | solution.py:285
  140.2 0.2 collective-permute-start.12
  140.4 7.4 %layer.2.sum_ref = f32[512,768]{1,0:T(8,128)S(1)} custom-call(bf16[512,768]{1,0:T(8,128)(2,1)S(1)} %weave_steps.1.tok_ref, bf16[768,1536]{1,0:T(8,128)(2,1)S(1)} %copy-done.2, bf16[768,3072]{1,0:T(8,128)(2,1)S(1)} %copy-done.1, bf16[768,1536]{1,0:T(8,128)(2,1)S(1)} %copy-done.4), custom_call_target="tpu_custom_call" | custom-call | flops 4831838208 | bytes 11796480 | tf_op jit(solution)/shard_map/layer/pallas_call | solution.py:285
  147.8 1.8 %finish.1 = bf16[512,768]{1,0:T(8,128)(2,1)} custom-call(bf16[512,768]{1,0:T(8,128)(2,1)S(1)} %weave_steps.1.tok_ref, f32[512,768]{1,0:T(8,128)S(1)} %layer.2.sum_ref, bf16[512,768]{1,0:T(8,128)(2,1)S(1)} %collective-permute-done.12.got_ref, s32[1,768]{1,0:T(1,128)S(1)} %compare_select_fusion.6.order_ref), custom_call_target="tpu_custom_call" | custom-call | flops 603979776 | bytes 3932160 | tf_op jit(solution)/shard_map/finish/pallas_call | solution.py:314
  (48 shorter events, 0.4 us)
Async XLA Ops:
  0.0 8.5 %copy-start.19 = (s32[512]{0:T(512)S(1)}, s32[512]{0:T(512)}, u32[]{:S(2)}) copy-start(s32[512]{0:T(512)} %param.11) | copy-start | bytes 6148
  0.0 8.5 %copy-start.20 = (s32[512]{0:T(512)S(1)}, s32[512]{0:T(512)}, u32[]{:S(2)}) copy-start(s32[512]{0:T(512)} %param.10) | copy-start | bytes 6148
  0.8 7.7 %copy-start.6 = (bf16[8,768]{1,0:T(8,128)(2,1)S(1)}, bf16[8,768]{1,0:T(8,128)(2,1)}, u32[]{:S(2)}) copy-start(bf16[8,768]{1,0:T(8,128)(2,1)} %time_ref.1) | copy-start | bytes 36868
  0.8 32.9 %copy-start.5 = (bf16[512,768]{1,0:T(8,128)(2,1)S(1)}, bf16[512,768]{1,0:T(8,128)(2,1)}, u32[]{:S(2)}) copy-start(bf16[512,768]{1,0:T(8,128)(2,1)} %feat_ref.1) | copy-start | bytes 2359300
  4.8 18.6 %collective-permute-start = (bf16[48,6144]{1,0:T(8,128)(2,1)}, bf16[48,6144]{1,0:T(8,128)(2,1)S(1)}, u32[]{:S(2)}, u32[]{:S(2)}) collective-permute-start(bf16[48,6144]{1,0:T(8,128)(2,1)} %pad_maximum_fusion.1), channel_id=1, source_target_pairs={{0,4},{4,8},{8,12},{12,0},{1,5},{5,9},{9,13},{13,1},{2,6},{6,10},{... | collective-permute-start | bytes 1769480 | tf_op jit(solution)/shard_map/ppermute | solution.py:334
  23.4 27.6 %collective-permute-start.1 = (bf16[48,6144]{1,0:T(8,128)(2,1)}, bf16[48,6144]{1,0:T(8,128)(2,1)}, u32[]{:S(2)}, u32[]{:S(2)}) collective-permute-start(bf16[48,6144]{1,0:T(8,128)(2,1)} %pad_maximum_fusion.1), channel_id=1, source_target_pairs={{0,12},{4,0},{8,4},{12,8},{1,13},{5,1},{9,5},{13,9},{2,14},{6,2},{... | collective-permute-start | bytes 1769480 | tf_op jit(solution)/shard_map/ppermute | solution.py:334
  25.2 25.8 %collective-permute-start.5 = (bf16[48,6144]{1,0:T(8,128)(2,1)S(1)}, bf16[48,6144]{1,0:T(8,128)(2,1)S(1)}, u32[]{:S(2)}, u32[]{:S(2)}) collective-permute-start(bf16[48,6144]{1,0:T(8,128)(2,1)S(1)} %collective-permute-done.refs_1_), channel_id=1, source_target_pairs={{0,18},{2,16},{16,2},{18,0},{1,19},{3,17},{17,3},{19,1},{4,22},{6,... | collective-permute-start | bytes 1769480 | tf_op jit(solution)/shard_map/ppermute | solution.py:343
  27.6 25.0 %collective-permute-start.4 = (bf16[48,6144]{1,0:T(8,128)(2,1)S(1)}, bf16[48,6144]{1,0:T(8,128)(2,1)S(1)}, u32[]{:S(2)}, u32[]{:S(2)}) collective-permute-start(bf16[48,6144]{1,0:T(8,128)(2,1)S(1)} %collective-permute-done.refs_1_), channel_id=1, source_target_pairs={{0,16},{2,18},{16,0},{18,2},{1,17},{3,19},{17,1},{19,3},{4,20},{6,... | collective-permute-start | bytes 1769480 | tf_op jit(solution)/shard_map/ppermute | solution.py:343
  28.1 24.7 %collective-permute-start.3 = (bf16[48,6144]{1,0:T(8,128)(2,1)S(1)}, bf16[48,6144]{1,0:T(8,128)(2,1)}, u32[]{:S(2)}, u32[]{:S(2)}) collective-permute-start(bf16[48,6144]{1,0:T(8,128)(2,1)S(1)} %collective-permute-done.refs_1_), channel_id=1, source_target_pairs={{0,2},{2,0},{16,18},{18,16},{1,3},{3,1},{17,19},{19,17},{4,6},{6,4... | collective-permute-start | bytes 1769480 | tf_op jit(solution)/shard_map/ppermute | solution.py:343
  28.6 24.2 %collective-permute-start.2 = (bf16[48,6144]{1,0:T(8,128)(2,1)S(1)}, bf16[48,6144]{1,0:T(8,128)(2,1)}, u32[]{:S(2)}, u32[]{:S(2)}) collective-permute-start(bf16[48,6144]{1,0:T(8,128)(2,1)S(1)} %collective-permute-done.refs_1_), channel_id=1, source_target_pairs={{0,4},{4,8},{8,12},{12,0},{1,5},{5,9},{9,13},{13,1},{2,6},{6,10},{... | collective-permute-start | bytes 1769480 | tf_op jit(solution)/shard_map/ppermute | solution.py:334
  28.9 22.1 %all-to-all-start = ((s32[8,1,192]{2,1,0:T(1,128)}), s32[8,1,192]{2,1,0:T(1,128)S(1)}, u32[]{:S(2)}, u32[]{:S(2)}) async-start(s32[8,1,192]{2,1,0:T(1,128)} %get-tuple-element.36), calls=%async_computation | async-start | bytes 16384 | tf_op jit(solution)/shard_map/all_to_all | solution.py:428
  51.0 1.8 %copy-start.15 = (bf16[48,6144]{1,0:T(8,128)(2,1)}, bf16[48,6144]{1,0:T(8,128)(2,1)S(1)}, u32[]{:S(2)}) copy-start(bf16[48,6144]{1,0:T(8,128)(2,1)S(1)} %collective-permute-done.5.refs_4_) | copy-start | bytes 1769476
  52.6 0.8 copy-start.16
  53.4 58.2 %all-to-all-start.1 = ((bf16[8,192,768]{2,1,0:T(8,128)(2,1)}), bf16[8,192,768]{2,1,0:T(8,128)(2,1)S(1)}, u32[]{:S(2)}, u32[]{:S(2)}) async-start(bf16[8,192,768]{2,1,0:T(8,128)(2,1)} %place_rows.1), calls=%async_computation.1 | async-start | bytes 4718592 | tf_op jit(solution)/shard_map/all_to_all | solution.py:435
  57.0 4.9 %copy-start.14 = (bf16[192,3,384]{2,0,1:T(8,128)(2,1)S(1)}, bf16[192,3,384]{2,0,1:T(8,128)(2,1)}, u32[]{:S(2)}) copy-start(bf16[192,3,384]{2,0,1:T(8,128)(2,1)} %param.14) | copy-start | bytes 1327108
  57.1 4.9 %copy-start.12 = (bf16[192,2,1536]{2,1,0:T(2,128)(2,1)S(1)}, bf16[192,2,1536]{2,1,0:T(2,128)(2,1)}, u32[]{:S(2)}) copy-start(bf16[192,2,1536]{2,1,0:T(2,128)(2,1)} %param.16) | copy-start | bytes 3538948
  59.4 2.7 %copy-start.11 = (bf16[96,6144]{1,0:T(8,128)(2,1)}, bf16[96,6144]{1,0:T(8,128)(2,1)S(1)}, u32[]{:S(2)}) copy-start(bf16[96,6144]{1,0:T(8,128)(2,1)S(1)} %constant_dynamic-update-slice_fusion.refs_5_) | copy-start | bytes 3538948
  59.4 28.3 %collective-permute-start.7 = (bf16[96,6144]{1,0:T(8,128)(2,1)S(1)}, bf16[96,6144]{1,0:T(8,128)(2,1)S(1)}, u32[]{:S(2)}, u32[]{:S(2)}) collective-permute-start(bf16[96,6144]{1,0:T(8,128)(2,1)S(1)} %constant_dynamic-update-slice_fusion.refs_5_), channel_id=1, source_target_pairs={{0,16},{16,0},{1,17},{17,1},{2,18},{18,2},{3,19},{19,3},{4,20},{20... | collective-permute-start | bytes 3538952 | tf_op jit(solution)/shard_map/ppermute | solution.py:350
  61.0 29.4 %collective-permute-start.6 = (bf16[96,6144]{1,0:T(8,128)(2,1)S(1)}, bf16[96,6144]{1,0:T(8,128)(2,1)S(1)}, u32[]{:S(2)}, u32[]{:S(2)}) collective-permute-start(bf16[96,6144]{1,0:T(8,128)(2,1)S(1)} %constant_dynamic-update-slice_fusion.refs_5_), channel_id=1, source_target_pairs={{0,2},{2,0},{1,3},{3,1},{4,6},{6,4},{5,7},{7,5},{8,10},{10,8},{9,1... | collective-permute-start | bytes 3538952 | tf_op jit(solution)/shard_map/ppermute | solution.py:349
  62.1 30.4 %copy-start.13 = (bf16[1536,192]{0,1:T(8,128)(2,1)S(1)}, bf16[1536,192]{0,1:T(8,128)(2,1)}, u32[]{:S(2)}) copy-start(bf16[1536,192]{0,1:T(8,128)(2,1)} %param.17) | copy-start | bytes 1769476
  62.1 30.4 %copy-start.18 = (bf16[384,192]{0,1:T(8,128)(2,1)S(1)}, bf16[384,192]{0,1:T(8,128)(2,1)}, u32[]{:S(2)}) copy-start(bf16[384,192]{0,1:T(8,128)(2,1)} %param.15) | copy-start | bytes 442372
  87.7 1.0 copy-start.9
  88.8 14.9 %collective-permute-start.9 = (bf16[96,3072]{1,0:T(8,128)(2,1)S(1)}, bf16[96,3072]{1,0:T(8,128)(2,1)S(1)}, u32[]{:S(2)}, u32[]{:S(2)}) collective-permute-start(bf16[96,3072]{1,0:T(8,128)(2,1)S(1)} %slice.9), channel_id=1, source_target_pairs={{0,2},{2,0},{1,3},{3,1},{4,6},{6,4},{5,7},{7,5},{8,10},{10,8},{9,1... | collective-permute-start | bytes 1769480 | tf_op jit(solution)/shard_map/ppermute | solution.py:353
  90.4 1.0 copy-start.10
  91.4 14.7 %collective-permute-start.8 = (bf16[96,3072]{1,0:T(8,128)(2,1)S(1)}, bf16[96,3072]{1,0:T(8,128)(2,1)}, u32[]{:S(2)}, u32[]{:S(2)}) collective-permute-start(bf16[96,3072]{1,0:T(8,128)(2,1)S(1)} %slice.8), channel_id=1, source_target_pairs={{0,16},{16,0},{1,17},{17,1},{2,18},{18,2},{3,19},{19,3},{4,20},{20... | collective-permute-start | bytes 1769480 | tf_op jit(solution)/shard_map/ppermute | solution.py:352
  103.7 0.8 copy-start.17
  113.7 0.8 copy-start.7
  114.5 10.7 %collective-permute-start.10 = (bf16[256,768]{1,0:T(8,128)(2,1)S(1)}, bf16[256,768]{1,0:T(8,128)(2,1)S(1)}, u32[]{:S(2)}, u32[]{:S(2)}) collective-permute-start(bf16[256,768]{1,0:T(8,128)(2,1)S(1)} %get-tuple-element.45), channel_id=1, source_target_pairs={{0,2},{2,0},{1,3},{3,1},{4,6},{6,4},{5,7},{7,5},{8,10},{10,8},{9,1... | collective-permute-start | bytes 1179656 | tf_op jit(solution)/shard_map/ppermute | solution.py:438
  116.0 9.1 %copy-start.8 = (bf16[256,768]{1,0:T(8,128)(2,1)S(1)}, bf16[256,768]{1,0:T(8,128)(2,1)}, u32[]{:S(2)}) copy-start(bf16[256,768]{1,0:T(8,128)(2,1)} %copy-done.7) | copy-start | bytes 1179652
  125.1 3.8 %copy-start.2 = (bf16[768,1536]{1,0:T(8,128)(2,1)S(1)}, bf16[768,1536]{1,0:T(8,128)(2,1)}, u32[]{:S(2)}) copy-start(bf16[768,1536]{1,0:T(8,128)(2,1)} %get-tuple-element.60.heads_ref) | copy-start | bytes 7077892
  126.6 2.4 %collective-permute-start.11 = (bf16[512,768]{1,0:T(8,128)(2,1)S(1)}, bf16[512,768]{1,0:T(8,128)(2,1)S(1)}, u32[]{:S(2)}, u32[]{:S(2)}) collective-permute-start(bf16[512,768]{1,0:T(8,128)(2,1)S(1)} %weave_steps.1.tok_ref), channel_id=1, source_target_pairs={{0,1},{1,0},{2,3},{3,2},{4,5},{5,4},{6,7},{7,6},{8,9},{9,8},{10,11... | collective-permute-start | bytes 2359304 | tf_op jit(solution)/shard_map/ppermute | solution.py:454
  128.9 2.3 %copy-start = (bf16[768,3072]{1,0:T(8,128)(2,1)S(1)}, bf16[768,3072]{1,0:T(8,128)(2,1)}, u32[]{:S(2)}) copy-start(bf16[768,3072]{1,0:T(8,128)(2,1)} %get-tuple-element.61.gate_up_ref) | copy-start | bytes 14155780
  131.3 1.7 %copy-start.3 = (bf16[768,1536]{1,0:T(8,128)(2,1)S(1)}, bf16[768,1536]{1,0:T(8,128)(2,1)}, u32[]{:S(2)}) copy-start(bf16[768,1536]{1,0:T(8,128)(2,1)} %get-tuple-element.62.down_ref) | copy-start | bytes 7077892
  132.9 7.4 %copy-start.1 = (bf16[768,3072]{1,0:T(8,128)(2,1)S(1)}, bf16[768,3072]{1,0:T(8,128)(2,1)}, u32[]{:S(2)}) copy-start(bf16[768,3072]{1,0:T(8,128)(2,1)} %get-tuple-element.61.gate_up_ref) | copy-start | bytes 14155780
  133.0 7.4 %copy-start.4 = (bf16[768,1536]{1,0:T(8,128)(2,1)S(1)}, bf16[768,1536]{1,0:T(8,128)(2,1)}, u32[]{:S(2)}) copy-start(bf16[768,1536]{1,0:T(8,128)(2,1)} %get-tuple-element.62.down_ref) | copy-start | bytes 7077892
  140.2 7.6 %collective-permute-start.12 = (bf16[512,768]{1,0:T(8,128)(2,1)S(1)}, bf16[512,768]{1,0:T(8,128)(2,1)S(1)}, u32[]{:S(2)}, u32[]{:S(2)}) collective-permute-start(bf16[512,768]{1,0:T(8,128)(2,1)S(1)} %layer.3), channel_id=1, source_target_pairs={{0,1},{1,0},{2,3},{3,2},{4,5},{5,4},{6,7},{7,6},{8,9},{9,8},{10,11... | collective-permute-start | bytes 2359304 | tf_op jit(solution)/shard_map/ppermute | solution.py:456

commit v19 on v18

--- a/solution.py
+++ b/solution.py
@@ -335,16 +335,6 @@
 
 
 def to_other_places(shares):
-    n_slots = lax.axis_size("slots")
-    n_share = lax.axis_size("groups") * n_slots
-    places = [shares]
-    for far in range(1, n_share):
-        pairs = [(place, place ^ far) for place in range(n_share)]
-        places.append(lax.ppermute(shares, ("groups", "slots"), pairs))
-    return places
-
-
-def to_other_places_by_halves(shares):
     swap = [(0, 1), (1, 0)]
     by_slot = lax.ppermute(shares, "slots", swap)
     by_group = lax.ppermute(shares, "groups", swap)
@@ -429,18 +419,20 @@
         first = to_other_places(below)
         blocks = place_rows(owner, obs_feat, n_owners, capacity)
         above, opposite = along_cells(share_rows, 1), along_cells(below, -1)
-        blocks, codes, above, opposite, first = lax.optimization_barrier((blocks, codes, above, opposite, first))
-        second = to_other_places_by_halves(jnp.concatenate([above, opposite], axis=0))
+        blocks, codes, above, first = lax.optimization_barrier((blocks, codes, above, first))
+        second = to_other_places(jnp.concatenate([above, opposite], axis=0))
         shard = side_by_side(*local_weights)
         got = lax.all_to_all(blocks, ("cells", "mp"), split_axis=0, concat_axis=0, tiled=True)
         got, shard, second = lax.optimization_barrier((got, shard, second))
         keep, send = pool_rows(my_slot.reshape(1), embed, codes, got, capacity, slot_dev)
         other = lax.ppermute(send, "slots", [(0, 1), (1, 0)])
-        pieces, row = [], 0
-        for array in [shard] + first + second[:3]:
-            pieces.append((array, row, 0))
-            row += array.shape[0]
-        pieces += [(second[3], row, 0), (second[4], row, second[3].shape[1])]
+        pieces, row = [(shard, 0, 0)], shard.shape[0]
+        for own, by_slot, by_group, left, right in (first, second):
+            for array in (own, by_slot, by_group):
+                pieces.append((array, row, 0))
+                row += array.shape[0]
+            pieces += [(left, row, 0), (right, row, left.shape[1])]
+            row += own.shape[0]
         weights = put_rows(pieces, width, heads_width, hidden_width)
         other, weights = lax.optimization_barrier((other, weights))
         tokens = weave_steps(my_slot.reshape(1), order, keep, other, slot_dev)

time: 150 us -> 201 us (1.34)
  the two profiles are of different devices: /device:TPU:0 before, /device:TPU:17 now
where the time goes in v19:
time: 201 us; the launch traced here: 200 us
  waiting for transfers between devices  121 us (60%)
  Pallas kernels  31.9 us (16%)
  starting transfers between devices  29.6 us (15%)
  local copies, waits for them, and re-layouts  15.3 us (8%)
    ppermute x3, waiting for transfers between devices, along_cells(): lax.ppermute(values, 'cells', [(j, (j - distance) % n_cells) for j in ran...  73.3 us
    ppermute x2, waiting for transfers between devices, to_other_places(): by_group = lax.ppermute(shares, 'groups', swap)  36 us
    pallas_call x2, Pallas kernels, layer(): pl.pallas_call(layer_kernel, out_shape=jax.ShapeDtypeStruct((rows, width)...  14.6 us
    unnamed x50, local copies, waits for them, and re-layouts  11.5 us
    ppermute x2, waiting for transfers between devices, to_other_places(): right = lax.ppermute(by_group[:, cut:], 'slots', swap)  9.38 us
    all_to_all x1, starting transfers between devices, on_device(): lax.all_to_all(codes, ('cells', 'mp'), split_axis=0, concat_axis=0, tiled...  8.19 us
    pallas_call x1, Pallas kernels, put_rows(): pl.pallas_call(functools.partial(put_rows_kernel, plan), out_shape=[jax.S...  7.65 us
    all_to_all x1, starting transfers between devices, on_device(): lax.all_to_all(blocks, ('cells', 'mp'), split_axis=0, concat_axis=0, tile...  6.12 us
  transfers between devices with their start and end apart: 16, of which 7 were waited for; matrix products, arithmetic and copies ran while one was open for 2% of the time, Pallas kernels for 10%

profile of v19, /device:TPU:17, one launch (start us, length us, event | category | flops | bytes accessed | tf_op | source)
XLA Modules:
  0.0 200.4 jit_solution(5726664875558438637)
XLA Ops:
  0.0 0.8 dynamic-slice_bitcast_fusion.2
  0.8 0.9 dynamic-slice_bitcast_fusion.1
  1.8 0.9 dynamic-slice_bitcast_fusion
  2.7 1.2 constant_dynamic-slice_fusion
  4.0 1.3 collective-permute-start
  6.0 1.3 place_codes.1
  7.3 10.9 %collective-permute-done.refs_1_ = bf16[48,6144]{1,0:T(8,128)(2,1)S(1)} collective-permute-done((bf16[48,6144]{1,0:T(8,128)(2,1)S(1)}, bf16[48,6144]{1,0:T(8,128)(2,1)S(1)}, u32[]{:S(2)}, u32[]{:S(2)}) %collective-permute-start) | collective-permute-done | bytes 589856 | tf_op jit(solution)/shard_map/ppermute | solution.py:334
  18.2 1.2 collective-permute-start.3
  19.5 1.2 collective-permute-start.2
  20.7 0.2 collective-permute-start.1
  20.8 10.7 %collective-permute-done.3.refs_3_ = bf16[48,6144]{1,0:T(8,128)(2,1)S(1)} collective-permute-done((bf16[48,6144]{1,0:T(8,128)(2,1)S(1)}, bf16[48,6144]{1,0:T(8,128)(2,1)S(1)}, u32[]{:S(2)}, u32[]{:S(2)}) %collective-permute-start.3) | collective-permute-done | bytes 589856 | tf_op jit(solution)/shard_map/ppermute | solution.py:340
  31.5 1.3 collective-permute-start.5
  32.8 0.8 copy-done.14
  33.6 0.7 slice.16
  34.3 1.2 collective-permute-start.4
  35.6 8.2 %all-to-all-start = ((s32[8,1,192]{2,1,0:T(1,128)}), s32[8,1,192]{2,1,0:T(1,128)S(1)}, u32[]{:S(2)}, u32[]{:S(2)}) async-start(s32[8,1,192]{2,1,0:T(1,128)} %get-tuple-element.36), calls=%async_computation | async-start | bytes 16384 | tf_op jit(solution)/shard_map/all_to_all | solution.py:418
  43.8 3.0 %place_rows.1 = bf16[8,192,768]{2,1,0:T(8,128)(2,1)} custom-call(s32[1,512]{1,0:T(1,128)S(1)} %bitcast.22, bf16[512,768]{1,0:T(8,128)(2,1)S(1)} %copy-done.5), custom_call_target="tpu_custom_call" | custom-call | flops 1207959552 | bytes 3145728 | tf_op jit(solution)/shard_map/place_rows/pallas_call | solution.py:98
  46.8 0.8 copy-done.19
  47.6 6.1 %all-to-all-start.1 = ((bf16[8,192,768]{2,1,0:T(8,128)(2,1)}), bf16[8,192,768]{2,1,0:T(8,128)(2,1)S(1)}, u32[]{:S(2)}, u32[]{:S(2)}) async-start(bf16[8,192,768]{2,1,0:T(8,128)(2,1)} %place_rows.1), calls=%async_computation.1 | async-start | bytes 4718592 | tf_op jit(solution)/shard_map/all_to_all | solution.py:425
  53.8 1.2 collective-permute-start.6
  55.0 1.1 constant_dynamic-update-slice_fusion.1
  56.1 62.4 %collective-permute-done.6 = bf16[48,6144]{1,0:T(8,128)(2,1)S(1)} collective-permute-done((bf16[48,6144]{1,0:T(8,128)(2,1)}, bf16[48,6144]{1,0:T(8,128)(2,1)S(1)}, u32[]{:S(2)}, u32[]{:S(2)}) %collective-permute-start.6) | collective-permute-done | bytes 589856 | tf_op jit(solution)/shard_map/ppermute | solution.py:334
  118.5 0.3 collective-permute-start.8
  118.8 1.2 collective-permute-start.7
  120.1 0.1 copy.17
  120.3 0.0 copy-start.15
  120.3 25.4 %collective-permute-done.8.refs_8_ = bf16[96,6144]{1,0:T(8,128)(2,1)S(1)} collective-permute-done((bf16[96,6144]{1,0:T(8,128)(2,1)S(1)}, bf16[96,6144]{1,0:T(8,128)(2,1)S(1)}, u32[]{:S(2)}, u32[]{:S(2)}) %collective-permute-start.8) | collective-permute-done | bytes 1179680 | tf_op jit(solution)/shard_map/ppermute | solution.py:340
  145.7 1.0 copy-done.9
  146.8 0.3 collective-permute-start.10
  147.1 1.0 copy-done.10
  148.1 1.3 collective-permute-start.9
  149.4 1.7 pad_maximum_fusion.refs_0_
  151.1 9.4 %collective-permute-done.10.refs_10_ = bf16[96,3072]{1,0:T(8,128)(2,1)S(1)} collective-permute-done((bf16[96,3072]{1,0:T(8,128)(2,1)S(1)}, bf16[96,3072]{1,0:T(8,128)(2,1)S(1)}, u32[]{:S(2)}, u32[]{:S(2)}) %collective-permute-start.10) | collective-permute-done | bytes 589856 | tf_op jit(solution)/shard_map/ppermute | solution.py:343
  160.5 0.8 copy-done.18
  161.3 0.3 collective-permute-done.9.refs_9_
  161.6 2.1 %pool_rows.1 = (bf16[256,768]{1,0:T(8,128)(2,1)S(1)}, bf16[256,768]{1,0:T(8,128)(2,1)S(1)}) custom-call(s32[1]{0:T(128)} %bitcast.slot_ref, bf16[8,768]{1,0:T(8,128)(2,1)S(1)} %get-tuple-element.34.embed_ref, s32[8,1,192]{2,1,0:T(1,128)S(1)} %all-to-all-done.code_ref, bf16[8,192,768]{2,1,0:T(8,128)(2,1)S(1)} %all-to-all-done.1.got_ref), custom_call_target="tpu_custom_call" | custom-call | flops 1207959552 | bytes 2359296 | tf_op jit(solution)/shard_map/pool_rows/pallas_call | solution.py:138
  163.7 0.7 copy-done.7
  164.4 1.2 collective-permute-start.11
  165.7 7.6 %put_rows.1 = (bf16[768,1536]{1,0:T(8,128)(2,1)}, bf16[768,3072]{1,0:T(8,128)(2,1)}, bf16[768,1536]{1,0:T(8,128)(2,1)}) custom-call(bf16[192,6144]{1,0:T(8,128)(2,1)} %pad_maximum_fusion.refs_0_, bf16[48,6144]{1,0:T(8,128)(2,1)} %copy-done.17, bf16[48,6144]{1,0:T(8,128)(2,1)} %copy-done.14, bf16[48,6144]{1,0:T(8,128)(2,1)} %copy-done.13, ...), custom_call_target="tpu_custom_call" | custom-call | bytes 18874368 | tf_op jit(solution)/shard_map/put_rows/pallas_call | solution.py:248
  173.4 1.5 weave_steps.1.tok_ref
  174.8 2.8 %collective-permute-start.12 = (bf16[512,768]{1,0:T(8,128)(2,1)S(1)}, bf16[512,768]{1,0:T(8,128)(2,1)S(1)}, u32[]{:S(2)}, u32[]{:S(2)}) collective-permute-start(bf16[512,768]{1,0:T(8,128)(2,1)S(1)} %weave_steps.1.tok_ref), channel_id=1, source_target_pairs={{0,1},{1,0},{2,3},{3,2},{4,5},{5,4},{6,7},{7,6},{8,9},{9,8},{10,11... | collective-permute-start | bytes 2359304 | tf_op jit(solution)/shard_map/ppermute | solution.py:446
  177.6 1.9 collective-permute-done.12.tok_ref
  179.6 2.3 %copy-done = bf16[768,3072]{1,0:T(8,128)(2,1)S(1)} copy-done((bf16[768,3072]{1,0:T(8,128)(2,1)S(1)}, bf16[768,3072]{1,0:T(8,128)(2,1)}, u32[]{:S(2)}) %copy-start) | copy-done | bytes 4718616
  181.9 1.7 copy-done.3
  183.6 7.2 %layer.3 = bf16[512,768]{1,0:T(8,128)(2,1)S(1)} custom-call(bf16[512,768]{1,0:T(8,128)(2,1)S(1)} %collective-permute-done.12.tok_ref, bf16[768,1536]{1,0:T(8,128)(2,1)S(1)} %copy-done.2, bf16[768,3072]{1,0:T(8,128)(2,1)S(1)} %copy-done, bf16[768,1536]{1,0:T(8,128)(2,1)S(1)} %copy-done.3), custom_call_target="tpu_custom_call" | custom-call | flops 4831838208 | bytes 11796480 | tf_op jit(solution)/shard_map/layer/pallas_call | solution.py:285
  190.8 0.4 collective-permute-start.13
  191.2 7.4 %layer.2.sum_ref = f32[512,768]{1,0:T(8,128)S(1)} custom-call(bf16[512,768]{1,0:T(8,128)(2,1)S(1)} %weave_steps.1.tok_ref, bf16[768,1536]{1,0:T(8,128)(2,1)S(1)} %copy-done.2, bf16[768,3072]{1,0:T(8,128)(2,1)S(1)} %copy-done.1, bf16[768,1536]{1,0:T(8,128)(2,1)S(1)} %copy-done.4), custom_call_target="tpu_custom_call" | custom-call | flops 4831838208 | bytes 11796480 | tf_op jit(solution)/shard_map/layer/pallas_call | solution.py:285
  198.6 1.8 finish.1
  (56 shorter events, 0.4 us)
Async XLA Ops:
  0.0 6.0 %copy-start.21 = (s32[512]{0:T(512)S(1)}, s32[512]{0:T(512)}, u32[]{:S(2)}) copy-start(s32[512]{0:T(512)} %param.11) | copy-start | bytes 6148
  0.0 6.0 %copy-start.22 = (s32[512]{0:T(512)S(1)}, s32[512]{0:T(512)}, u32[]{:S(2)}) copy-start(s32[512]{0:T(512)} %param.10) | copy-start | bytes 6148
  0.8 5.2 %copy-start.6 = (bf16[8,768]{1,0:T(8,128)(2,1)S(1)}, bf16[8,768]{1,0:T(8,128)(2,1)}, u32[]{:S(2)}) copy-start(bf16[8,768]{1,0:T(8,128)(2,1)} %time_ref.1) | copy-start | bytes 36868
  3.9 39.9 %copy-start.5 = (bf16[512,768]{1,0:T(8,128)(2,1)S(1)}, bf16[512,768]{1,0:T(8,128)(2,1)}, u32[]{:S(2)}) copy-start(bf16[512,768]{1,0:T(8,128)(2,1)} %feat_ref.1) | copy-start | bytes 2359300
  4.0 14.2 %collective-permute-start = (bf16[48,6144]{1,0:T(8,128)(2,1)S(1)}, bf16[48,6144]{1,0:T(8,128)(2,1)S(1)}, u32[]{:S(2)}, u32[]{:S(2)}) collective-permute-start(bf16[48,6144]{1,0:T(8,128)(2,1)S(1)} %pad_maximum_fusion.1), channel_id=1, source_target_pairs={{0,4},{4,8},{8,12},{12,0},{1,5},{5,9},{9,13},{13,1},{2,6},{6,10},{... | collective-permute-start | bytes 1769480 | tf_op jit(solution)/shard_map/ppermute | solution.py:334
  18.2 16.1 %copy-start.17 = (bf16[48,6144]{1,0:T(8,128)(2,1)}, bf16[48,6144]{1,0:T(8,128)(2,1)S(1)}, u32[]{:S(2)}) copy-start(bf16[48,6144]{1,0:T(8,128)(2,1)S(1)} %collective-permute-done.refs_1_) | copy-start | bytes 1769476
  18.2 13.3 %collective-permute-start.3 = (bf16[48,6144]{1,0:T(8,128)(2,1)S(1)}, bf16[48,6144]{1,0:T(8,128)(2,1)S(1)}, u32[]{:S(2)}, u32[]{:S(2)}) collective-permute-start(bf16[48,6144]{1,0:T(8,128)(2,1)S(1)} %collective-permute-done.refs_1_), channel_id=1, source_target_pairs={{0,16},{16,0},{1,17},{17,1},{2,18},{18,2},{3,19},{19,3},{4,20},{20... | collective-permute-start | bytes 1769480 | tf_op jit(solution)/shard_map/ppermute | solution.py:340
  19.5 13.3 %collective-permute-start.2 = (bf16[48,6144]{1,0:T(8,128)(2,1)S(1)}, bf16[48,6144]{1,0:T(8,128)(2,1)S(1)}, u32[]{:S(2)}, u32[]{:S(2)}) collective-permute-start(bf16[48,6144]{1,0:T(8,128)(2,1)S(1)} %collective-permute-done.refs_1_), channel_id=1, source_target_pairs={{0,2},{2,0},{1,3},{3,1},{4,6},{6,4},{5,7},{7,5},{8,10},{10,8},{9,1... | collective-permute-start | bytes 1769480 | tf_op jit(solution)/shard_map/ppermute | solution.py:339
  20.7 26.1 %collective-permute-start.1 = (bf16[48,6144]{1,0:T(8,128)(2,1)S(1)}, bf16[48,6144]{1,0:T(8,128)(2,1)S(1)}, u32[]{:S(2)}, u32[]{:S(2)}) collective-permute-start(bf16[48,6144]{1,0:T(8,128)(2,1)S(1)} %pad_maximum_fusion.1), channel_id=1, source_target_pairs={{0,12},{4,0},{8,4},{12,8},{1,13},{5,1},{9,5},{13,9},{2,14},{6,2},{... | collective-permute-start | bytes 1769480 | tf_op jit(solution)/shard_map/ppermute | solution.py:334
  31.5 15.3 %copy-start.13 = (bf16[48,6144]{1,0:T(8,128)(2,1)}, bf16[48,6144]{1,0:T(8,128)(2,1)S(1)}, u32[]{:S(2)}) copy-start(bf16[48,6144]{1,0:T(8,128)(2,1)S(1)} %collective-permute-done.3.refs_3_) | copy-start | bytes 1769476
  31.5 15.3 %collective-permute-start.5 = (bf16[48,3072]{1,0:T(8,128)(2,1)S(1)}, bf16[48,3072]{1,0:T(8,128)(2,1)S(1)}, u32[]{:S(2)}, u32[]{:S(2)}) collective-permute-start(bf16[48,3072]{1,0:T(8,128)(2,1)S(1)} %slice.17), channel_id=1, source_target_pairs={{0,2},{2,0},{1,3},{3,1},{4,6},{6,4},{5,7},{7,5},{8,10},{10,8},{9,1... | collective-permute-start | bytes 884744 | tf_op jit(solution)/shard_map/ppermute | solution.py:343
  32.8 0.8 copy-start.14
  34.3 12.5 %collective-permute-start.4 = (bf16[48,3072]{1,0:T(8,128)(2,1)}, bf16[48,3072]{1,0:T(8,128)(2,1)S(1)}, u32[]{:S(2)}, u32[]{:S(2)}) collective-permute-start(bf16[48,3072]{1,0:T(8,128)(2,1)} %slice.16), channel_id=1, source_target_pairs={{0,16},{16,0},{1,17},{17,1},{2,18},{18,2},{3,19},{19,3},{4,20},{20... | collective-permute-start | bytes 884744 | tf_op jit(solution)/shard_map/ppermute | solution.py:342
  35.6 11.2 %all-to-all-start = ((s32[8,1,192]{2,1,0:T(1,128)}), s32[8,1,192]{2,1,0:T(1,128)S(1)}, u32[]{:S(2)}, u32[]{:S(2)}) async-start(s32[8,1,192]{2,1,0:T(1,128)} %get-tuple-element.36), calls=%async_computation | async-start | bytes 16384 | tf_op jit(solution)/shard_map/all_to_all | solution.py:418
  46.8 0.8 copy-start.19
  47.6 113.9 %all-to-all-start.1 = ((bf16[8,192,768]{2,1,0:T(8,128)(2,1)}), bf16[8,192,768]{2,1,0:T(8,128)(2,1)S(1)}, u32[]{:S(2)}, u32[]{:S(2)}) async-start(bf16[8,192,768]{2,1,0:T(8,128)(2,1)} %place_rows.1), calls=%async_computation.1 | async-start | bytes 4718592 | tf_op jit(solution)/shard_map/all_to_all | solution.py:425
  53.8 66.3 %copy-start.16 = (bf16[192,3,384]{2,0,1:T(8,128)(2,1)S(1)}, bf16[192,3,384]{2,0,1:T(8,128)(2,1)}, u32[]{:S(2)}) copy-start(bf16[192,3,384]{2,0,1:T(8,128)(2,1)} %param.14) | copy-start | bytes 1327108
  53.8 66.3 %copy-start.12 = (bf16[192,2,1536]{2,1,0:T(2,128)(2,1)S(1)}, bf16[192,2,1536]{2,1,0:T(2,128)(2,1)}, u32[]{:S(2)}) copy-start(bf16[192,2,1536]{2,1,0:T(2,128)(2,1)} %param.16) | copy-start | bytes 3538948
  53.8 64.7 %collective-permute-start.6 = (bf16[48,6144]{1,0:T(8,128)(2,1)}, bf16[48,6144]{1,0:T(8,128)(2,1)S(1)}, u32[]{:S(2)}, u32[]{:S(2)}) collective-permute-start(bf16[48,6144]{1,0:T(8,128)(2,1)} %copy-done.17), channel_id=1, source_target_pairs={{0,4},{4,8},{8,12},{12,0},{1,5},{5,9},{9,13},{13,1},{2,6},{6,10},{... | collective-permute-start | bytes 1769480 | tf_op jit(solution)/shard_map/ppermute | solution.py:334
  118.5 1.8 copy-start.11
  118.5 27.2 %collective-permute-start.8 = (bf16[96,6144]{1,0:T(8,128)(2,1)S(1)}, bf16[96,6144]{1,0:T(8,128)(2,1)S(1)}, u32[]{:S(2)}, u32[]{:S(2)}) collective-permute-start(bf16[96,6144]{1,0:T(8,128)(2,1)S(1)} %constant_dynamic-update-slice_fusion.refs_6_), channel_id=1, source_target_pairs={{0,16},{16,0},{1,17},{17,1},{2,18},{18,2},{3,19},{19,3},{4,20},{20... | collective-permute-start | bytes 3538952 | tf_op jit(solution)/shard_map/ppermute | solution.py:340
  118.8 28.3 %collective-permute-start.7 = (bf16[96,6144]{1,0:T(8,128)(2,1)S(1)}, bf16[96,6144]{1,0:T(8,128)(2,1)S(1)}, u32[]{:S(2)}, u32[]{:S(2)}) collective-permute-start(bf16[96,6144]{1,0:T(8,128)(2,1)S(1)} %constant_dynamic-update-slice_fusion.refs_6_), channel_id=1, source_target_pairs={{0,2},{2,0},{1,3},{3,1},{4,6},{6,4},{5,7},{7,5},{8,10},{10,8},{9,1... | collective-permute-start | bytes 3538952 | tf_op jit(solution)/shard_map/ppermute | solution.py:339
  120.3 29.2 %copy-start.15 = (bf16[1536,192]{0,1:T(8,128)(2,1)S(1)}, bf16[1536,192]{0,1:T(8,128)(2,1)}, u32[]{:S(2)}) copy-start(bf16[1536,192]{0,1:T(8,128)(2,1)} %param.17) | copy-start | bytes 1769476
  120.3 29.1 %copy-start.20 = (bf16[384,192]{0,1:T(8,128)(2,1)S(1)}, bf16[384,192]{0,1:T(8,128)(2,1)}, u32[]{:S(2)}) copy-start(bf16[384,192]{0,1:T(8,128)(2,1)} %param.15) | copy-start | bytes 442372
  145.7 1.0 copy-start.9
  146.8 13.7 %collective-permute-start.10 = (bf16[96,3072]{1,0:T(8,128)(2,1)S(1)}, bf16[96,3072]{1,0:T(8,128)(2,1)S(1)}, u32[]{:S(2)}, u32[]{:S(2)}) collective-permute-start(bf16[96,3072]{1,0:T(8,128)(2,1)S(1)} %slice.19), channel_id=1, source_target_pairs={{0,2},{2,0},{1,3},{3,1},{4,6},{6,4},{5,7},{7,5},{8,10},{10,8},{9,1... | collective-permute-start | bytes 1769480 | tf_op jit(solution)/shard_map/ppermute | solution.py:343
  147.1 1.0 copy-start.10
  148.1 13.4 %collective-permute-start.9 = (bf16[96,3072]{1,0:T(8,128)(2,1)S(1)}, bf16[96,3072]{1,0:T(8,128)(2,1)}, u32[]{:S(2)}, u32[]{:S(2)}) collective-permute-start(bf16[96,3072]{1,0:T(8,128)(2,1)S(1)} %slice.18), channel_id=1, source_target_pairs={{0,16},{16,0},{1,17},{17,1},{2,18},{18,2},{3,19},{19,3},{4,20},{20... | collective-permute-start | bytes 1769480 | tf_op jit(solution)/shard_map/ppermute | solution.py:342
  160.5 0.8 copy-start.18
  163.6 0.8 copy-start.7
  164.4 8.9 %collective-permute-start.11 = (bf16[256,768]{1,0:T(8,128)(2,1)S(1)}, bf16[256,768]{1,0:T(8,128)(2,1)S(1)}, u32[]{:S(2)}, u32[]{:S(2)}) collective-permute-start(bf16[256,768]{1,0:T(8,128)(2,1)S(1)} %get-tuple-element.44), channel_id=1, source_target_pairs={{0,2},{2,0},{1,3},{3,1},{4,6},{6,4},{5,7},{7,5},{8,10},{10,8},{9,1... | collective-permute-start | bytes 1179656 | tf_op jit(solution)/shard_map/ppermute | solution.py:428
  165.7 7.7 %copy-start.8 = (bf16[256,768]{1,0:T(8,128)(2,1)S(1)}, bf16[256,768]{1,0:T(8,128)(2,1)}, u32[]{:S(2)}) copy-start(bf16[256,768]{1,0:T(8,128)(2,1)} %copy-done.7) | copy-start | bytes 1179652
  173.3 6.2 %copy-start.2 = (bf16[768,1536]{1,0:T(8,128)(2,1)S(1)}, bf16[768,1536]{1,0:T(8,128)(2,1)}, u32[]{:S(2)}) copy-start(bf16[768,1536]{1,0:T(8,128)(2,1)} %get-tuple-element.60.heads_ref) | copy-start | bytes 7077892
  174.8 4.7 %collective-permute-start.12 = (bf16[512,768]{1,0:T(8,128)(2,1)S(1)}, bf16[512,768]{1,0:T(8,128)(2,1)S(1)}, u32[]{:S(2)}, u32[]{:S(2)}) collective-permute-start(bf16[512,768]{1,0:T(8,128)(2,1)S(1)} %weave_steps.1.tok_ref), channel_id=1, source_target_pairs={{0,1},{1,0},{2,3},{3,2},{4,5},{5,4},{6,7},{7,6},{8,9},{9,8},{10,11... | collective-permute-start | bytes 2359304 | tf_op jit(solution)/shard_map/ppermute | solution.py:446
  179.6 2.3 %copy-start = (bf16[768,3072]{1,0:T(8,128)(2,1)S(1)}, bf16[768,3072]{1,0:T(8,128)(2,1)}, u32[]{:S(2)}) copy-start(bf16[768,3072]{1,0:T(8,128)(2,1)} %get-tuple-element.61.gate_up_ref) | copy-start | bytes 14155780
  181.9 1.7 copy-start.3
  183.6 7.7 %copy-start.1 = (bf16[768,3072]{1,0:T(8,128)(2,1)S(1)}, bf16[768,3072]{1,0:T(8,128)(2,1)}, u32[]{:S(2)}) copy-start(bf16[768,3072]{1,0:T(8,128)(2,1)} %get-tuple-element.61.gate_up_ref) | copy-start | bytes 14155780
  183.6 7.7 %copy-start.4 = (bf16[768,1536]{1,0:T(8,128)(2,1)S(1)}, bf16[768,1536]{1,0:T(8,128)(2,1)}, u32[]{:S(2)}) copy-start(bf16[768,1536]{1,0:T(8,128)(2,1)} %get-tuple-element.62.down_ref) | copy-start | bytes 7077892
  190.8 7.9 %collective-permute-start.13 = (bf16[512,768]{1,0:T(8,128)(2,1)S(1)}, bf16[512,768]{1,0:T(8,128)(2,1)S(1)}, u32[]{:S(2)}, u32[]{:S(2)}) collective-permute-start(bf16[512,768]{1,0:T(8,128)(2,1)S(1)} %layer.3), channel_id=1, source_target_pairs={{0,1},{1,0},{2,3},{3,2},{4,5},{5,4},{6,7},{7,6},{8,9},{9,8},{10,11... | collective-permute-start | bytes 2359304 | tf_op jit(solution)/shard_map/ppermute | solution.py:448

commit v20 on v19

--- a/solution.py
+++ b/solution.py
@@ -222,7 +222,7 @@
 
 
 def put_rows_kernel(plan, *refs):
-    sems, outs, pieces = refs[-1], refs[-4:-1], refs[:-4]
+    sems, outs, pieces = refs[-1], refs[-5:-1], refs[:-5]
     copies = []
     for number, (piece, out, source, row, at, size) in enumerate(plan):
         rows = pieces[piece].shape[0]
@@ -238,7 +238,9 @@
     gate_at, out_at = 3 * heads_width, 3 * heads_width + 2 * hidden_width
     down_at = out_at + heads_width
     end = down_at + hidden_width
-    runs = [(0, gate_at, 0, 0), (gate_at, out_at, 1, 0), (out_at, down_at, 0, gate_at), (down_at, end, 2, 0)]
+    up_at = gate_at + hidden_width
+    runs = [(0, gate_at, 0, 0), (gate_at, up_at, 1, 0), (up_at, out_at, 2, 0)]
+    runs += [(out_at, down_at, 0, gate_at), (down_at, end, 3, 0)]
     plan = []
     for left, right, out, shift in runs:
         for number, (array, row, at) in enumerate(pieces):
@@ -248,12 +250,11 @@
     return pl.pallas_call(
         functools.partial(put_rows_kernel, plan),
         out_shape=[
-            jax.ShapeDtypeStruct((rows, 4 * heads_width), BF16),
-            jax.ShapeDtypeStruct((rows, 2 * hidden_width), BF16),
-            jax.ShapeDtypeStruct((rows, hidden_width), BF16),
+            jax.ShapeDtypeStruct((rows, columns), BF16)
+            for columns in (4 * heads_width, hidden_width, hidden_width, hidden_width)
         ],
         in_specs=[FAR] * len(pieces),
-        out_specs=[WHOLE] * 3,
+        out_specs=[WHOLE] * 4,
         scratch_shapes=[pltpu.SemaphoreType.DMA((len(plan),))],
         compiler_params=params(53),
         cost_estimate=pl.CostEstimate(flops=0, bytes_accessed=4 * rows * end, transcendentals=0),
@@ -261,7 +262,7 @@
     )(*[array for array, _, _ in pieces])
 
 
-def layer_kernel(tok_ref, heads_ref, gate_up_ref, down_ref, out_ref, norm_ref, ctx_ref, acc_ref):
+def layer_kernel(tok_ref, heads_ref, gate_ref, up_ref, down_ref, out_ref, norm_ref, ctx_ref, acc_ref):
     heads_width = ctx_ref.shape[1]
     hidden_width = down_ref.shape[1]
     tokens = tok_ref[...].astype(F32)
@@ -271,21 +272,20 @@
     acc_ref[...] = dot_t(ctx_ref[...], heads_ref[:, 3 * heads_width :])
     for begin in range(0, hidden_width, UNIT):
         end = begin + UNIT
-        gate_w, up_w = gate_up_ref[:, begin:end], gate_up_ref[:, hidden_width + begin : hidden_width + end]
-        add = gated(norm_ref[...], gate_w, up_w, down_ref[:, begin:end])
+        add = gated(norm_ref[...], gate_ref[:, begin:end], up_ref[:, begin:end], down_ref[:, begin:end])
         if end < hidden_width:
             acc_ref[...] += add
         else:
             out_ref[...] = (acc_ref[...] + add).astype(out_ref.dtype)
 
 
-def layer(tokens, heads, gate_up, down, out_type):
+def layer(tokens, heads, gate, up, down, out_type):
     rows, width = tokens.shape
-    size = heads.size + gate_up.size + down.size
+    size = heads.size + 3 * down.size
     return pl.pallas_call(
         layer_kernel,
         out_shape=jax.ShapeDtypeStruct((rows, width), out_type),
-        in_specs=[WHOLE] * 4,
+        in_specs=[WHOLE] * 5,
         out_specs=WHOLE,
         scratch_shapes=[
             pltpu.VMEM((rows, width), BF16),
@@ -299,7 +299,7 @@
             transcendentals=rows * down.shape[1],
         ),
         name="layer",
-    )(tokens, heads, gate_up, down)
+    )(tokens, heads, gate, up, down)
 
 
 def finish_kernel(tok_ref, sum_ref, got_ref, order_ref, out_ref):
@@ -419,7 +419,7 @@
         first = to_other_places(below)
         blocks = place_rows(owner, obs_feat, n_owners, capacity)
         above, opposite = along_cells(share_rows, 1), along_cells(below, -1)
-        blocks, codes, above, first = lax.optimization_barrier((blocks, codes, above, first))
+        blocks, codes, above, opposite, first = lax.optimization_barrier((blocks, codes, above, opposite, first))
         second = to_other_places(jnp.concatenate([above, opposite], axis=0))
         shard = side_by_side(*local_weights)
         got = lax.all_to_all(blocks, ("cells", "mp"), split_axis=0, concat_axis=0, tiled=True)

time: 201 us -> 152 us (0.76)
  the two profiles are of different devices: /device:TPU:17 before, /device:TPU:0 now
where the time goes in v20:
time: 152 us; the launch traced here: 151 us
  waiting for transfers between devices  77.4 us (51%)
  Pallas kernels  31.8 us (21%)
  starting transfers between devices  21.9 us (14%)
  local copies, waits for them, and re-layouts  16.7 us (11%)
  other arithmetic  2.6 us (2%)
    ppermute x2, waiting for transfers between devices, to_other_places(): by_group = lax.ppermute(shares, 'groups', swap)  36.6 us
    pallas_call x2, Pallas kernels, layer(): pl.pallas_call(layer_kernel, out_shape=jax.ShapeDtypeStruct((rows, width)...  14.4 us
    ppermute x3, waiting for transfers between devices, along_cells(): lax.ppermute(values, 'cells', [(j, (j - distance) % n_cells) for j in ran...  13.5 us
    unnamed x48, local copies, waits for them, and re-layouts  11.8 us
    ppermute x2, waiting for transfers between devices, to_other_places(): right = lax.ppermute(by_group[:, cut:], 'slots', swap)  11.1 us
    pallas_call x1, Pallas kernels, put_rows(): pl.pallas_call(functools.partial(put_rows_kernel, plan), out_shape=[jax.S...  7.74 us
    all_to_all x1, waiting for transfers between devices, on_device(): lax.all_to_all(blocks, ('cells', 'mp'), split_axis=0, concat_axis=0, tile...  6.32 us
    ppermute x3, starting transfers between devices, along_cells(): lax.ppermute(values, 'cells', [(j, (j - distance) % n_cells) for j in ran...  5.05 us
  transfers between devices with their start and end apart: 16, of which 9 were waited for; matrix products, arithmetic and copies ran while one was open for 3% of the time, Pallas kernels for 13%

profile of v20, /device:TPU:0, one launch (start us, length us, event | category | flops | bytes accessed | tf_op | source)
XLA Modules:
  0.0 151.2 jit_solution(588156127282264986)
XLA Ops:
  0.0 0.8 dynamic-slice_bitcast_fusion.2
  0.8 0.9 dynamic-slice_bitcast_fusion.1
  1.8 0.9 dynamic-slice_bitcast_fusion
  2.7 1.2 constant_dynamic-slice_fusion
  3.9 0.9 pad_maximum_fusion.1
  4.8 3.0 %collective-permute-start = (bf16[48,6144]{1,0:T(8,128)(2,1)}, bf16[48,6144]{1,0:T(8,128)(2,1)S(1)}, u32[]{:S(2)}, u32[]{:S(2)}) collective-permute-start(bf16[48,6144]{1,0:T(8,128)(2,1)} %pad_maximum_fusion.1), channel_id=1, source_target_pairs={{0,4},{4,8},{8,12},{12,0},{1,5},{5,9},{9,13},{13,1},{2,6},{6,10},{... | collective-permute-start | bytes 1769480 | tf_op jit(solution)/shard_map/ppermute | solution.py:334
  8.5 1.3 place_codes.1
  9.8 13.5 %collective-permute-done.refs_1_ = bf16[48,6144]{1,0:T(8,128)(2,1)S(1)} collective-permute-done((bf16[48,6144]{1,0:T(8,128)(2,1)}, bf16[48,6144]{1,0:T(8,128)(2,1)S(1)}, u32[]{:S(2)}, u32[]{:S(2)}) %collective-permute-start) | collective-permute-done | bytes 589856 | tf_op jit(solution)/shard_map/ppermute | solution.py:334
  23.4 1.5 %collective-permute-start.4 = (bf16[48,6144]{1,0:T(8,128)(2,1)S(1)}, bf16[48,6144]{1,0:T(8,128)(2,1)S(1)}, u32[]{:S(2)}, u32[]{:S(2)}) collective-permute-start(bf16[48,6144]{1,0:T(8,128)(2,1)S(1)} %collective-permute-done.refs_1_), channel_id=1, source_target_pairs={{0,16},{16,0},{1,17},{17,1},{2,18},{18,2},{3,19},{19,3},{4,20},{20... | collective-permute-start | bytes 1769480 | tf_op jit(solution)/shard_map/ppermute | solution.py:340
  24.9 1.5 collective-permute-start.3
  26.4 1.7 %collective-permute-start.1 = (bf16[48,6144]{1,0:T(8,128)(2,1)}, bf16[48,6144]{1,0:T(8,128)(2,1)}, u32[]{:S(2)}, u32[]{:S(2)}) collective-permute-start(bf16[48,6144]{1,0:T(8,128)(2,1)} %pad_maximum_fusion.1), channel_id=1, source_target_pairs={{0,12},{4,0},{8,4},{12,8},{1,13},{5,1},{9,5},{13,9},{2,14},{6,2},{... | collective-permute-start | bytes 1769480 | tf_op jit(solution)/shard_map/ppermute | solution.py:334
  28.1 0.3 collective-permute-start.2
  28.4 9.5 %collective-permute-done.4.refs_3_ = bf16[48,6144]{1,0:T(8,128)(2,1)S(1)} collective-permute-done((bf16[48,6144]{1,0:T(8,128)(2,1)S(1)}, bf16[48,6144]{1,0:T(8,128)(2,1)S(1)}, u32[]{:S(2)}, u32[]{:S(2)}) %collective-permute-start.4) | collective-permute-done | bytes 589856 | tf_op jit(solution)/shard_map/ppermute | solution.py:340
  37.9 1.3 collective-permute-start.6
  39.2 0.8 copy-done.14
  40.0 0.7 slice.16
  40.8 1.5 %collective-permute-start.5 = (bf16[48,3072]{1,0:T(8,128)(2,1)}, bf16[48,3072]{1,0:T(8,128)(2,1)S(1)}, u32[]{:S(2)}, u32[]{:S(2)}) collective-permute-start(bf16[48,3072]{1,0:T(8,128)(2,1)} %slice.16), channel_id=1, source_target_pairs={{0,16},{16,0},{1,17},{17,1},{2,18},{18,2},{3,19},{19,3},{4,20},{20... | collective-permute-start | bytes 884744 | tf_op jit(solution)/shard_map/ppermute | solution.py:342
  42.3 3.3 %all-to-all-start = ((s32[8,1,192]{2,1,0:T(1,128)}), s32[8,1,192]{2,1,0:T(1,128)S(1)}, u32[]{:S(2)}, u32[]{:S(2)}) async-start(s32[8,1,192]{2,1,0:T(1,128)} %get-tuple-element.39), calls=%async_computation | async-start | bytes 16384 | tf_op jit(solution)/shard_map/all_to_all | solution.py:418
  45.6 3.0 %place_rows.1 = bf16[8,192,768]{2,1,0:T(8,128)(2,1)} custom-call(s32[1,512]{1,0:T(1,128)S(1)} %bitcast.22, bf16[512,768]{1,0:T(8,128)(2,1)S(1)} %copy-done.5), custom_call_target="tpu_custom_call" | custom-call | flops 1207959552 | bytes 3145728 | tf_op jit(solution)/shard_map/place_rows/pallas_call | solution.py:98
  48.7 4.6 %all-to-all-done.code_ref = s32[8,1,192]{2,1,0:T(1,128)S(1)} async-done(((s32[8,1,192]{2,1,0:T(1,128)}), s32[8,1,192]{2,1,0:T(1,128)S(1)}, u32[]{:S(2)}, u32[]{:S(2)}) %all-to-all-start) | async-done | bytes 6176 | tf_op jit(solution)/shard_map/all_to_all | solution.py:418
  53.3 4.6 %all-to-all-start.1 = ((bf16[8,192,768]{2,1,0:T(8,128)(2,1)}), bf16[8,192,768]{2,1,0:T(8,128)(2,1)S(1)}, u32[]{:S(2)}, u32[]{:S(2)}) async-start(bf16[8,192,768]{2,1,0:T(8,128)(2,1)} %place_rows.1), calls=%async_computation.1 | async-start | bytes 4718592 | tf_op jit(solution)/shard_map/all_to_all | solution.py:425
  57.9 1.2 constant_dynamic-update-slice_fusion.1
  59.1 1.1 constant_dynamic-update-slice_fusion.refs_6_
  60.2 0.6 collective-permute-start.8
  60.8 0.5 collective-permute-start.7
  61.6 27.1 %collective-permute-done.8.refs_8_ = bf16[96,6144]{1,0:T(8,128)(2,1)S(1)} collective-permute-done((bf16[96,6144]{1,0:T(8,128)(2,1)S(1)}, bf16[96,6144]{1,0:T(8,128)(2,1)S(1)}, u32[]{:S(2)}, u32[]{:S(2)}) %collective-permute-start.8) | collective-permute-done | bytes 1179680 | tf_op jit(solution)/shard_map/ppermute | solution.py:340
  88.7 1.0 copy-done.9
  89.7 0.6 collective-permute-start.10
  90.3 1.0 copy-done.10
  91.4 0.6 collective-permute-start.9
  92.0 1.7 %pad_maximum_fusion.refs_0_ = bf16[192,6144]{1,0:T(8,128)(2,1)} fusion(bf16[192,1536]{1,0:T(8,128)(2,1)S(1)} %bitcast.29, bf16[192,384]{1,0:T(8,128)(2,1)S(1)} %bitcast.32, bf16[192,3072]{1,0:T(8,128)(2,1)S(1)} %bitcast.24, bf16[192,1152]{1,0:T(8,128)(2,1)S(1)} %bitcast.26), kind=kLoop, calls=%fused_computation | loop fusion | flops 9437184 | bytes 4718592 | tf_op jit(solution)/shard_map/concatenate | solution.py:329
  93.6 11.1 %collective-permute-done.10.refs_10_ = bf16[96,3072]{1,0:T(8,128)(2,1)S(1)} collective-permute-done((bf16[96,3072]{1,0:T(8,128)(2,1)S(1)}, bf16[96,3072]{1,0:T(8,128)(2,1)S(1)}, u32[]{:S(2)}, u32[]{:S(2)}) %collective-permute-start.10) | collective-permute-done | bytes 589856 | tf_op jit(solution)/shard_map/ppermute | solution.py:343
  104.7 0.8 copy-done.18
  105.6 0.7 collective-permute-done.9.refs_9_
  106.2 6.3 %all-to-all-done.1.got_ref = bf16[8,192,768]{2,1,0:T(8,128)(2,1)S(1)} async-done(((bf16[8,192,768]{2,1,0:T(8,128)(2,1)}), bf16[8,192,768]{2,1,0:T(8,128)(2,1)S(1)}, u32[]{:S(2)}, u32[]{:S(2)}) %all-to-all-start.1) | async-done | bytes 2359328 | tf_op jit(solution)/shard_map/all_to_all | solution.py:425
  112.5 2.0 %pool_rows.1 = (bf16[256,768]{1,0:T(8,128)(2,1)S(1)}, bf16[256,768]{1,0:T(8,128)(2,1)S(1)}) custom-call(s32[1]{0:T(128)} %bitcast.slot_ref, bf16[8,768]{1,0:T(8,128)(2,1)S(1)} %get-tuple-element.37.embed_ref, s32[8,1,192]{2,1,0:T(1,128)S(1)} %all-to-all-done.code_ref, bf16[8,192,768]{2,1,0:T(8,128)(2,1)S(1)} %all-to-all-done.1.got_ref), custom_call_target="tpu_custom_call" | custom-call | flops 1207959552 | bytes 2359296 | tf_op jit(solution)/shard_map/pool_rows/pallas_call | solution.py:138
  114.6 0.7 copy-done.7
  115.3 0.5 collective-permute-start.11
  115.9 7.7 %put_rows.1 = (bf16[768,1536]{1,0:T(8,128)(2,1)}, bf16[768,1536]{1,0:T(8,128)(2,1)}, bf16[768,1536]{1,0:T(8,128)(2,1)}, bf16[768,1536]{1,0:T(8,128)(2,1)}) custom-call(bf16[192,6144]{1,0:T(8,128)(2,1)} %pad_maximum_fusion.refs_0_, bf16[48,6144]{1,0:T(8,128)(2,1)} %copy-done.17, bf16[48,6144]{1,0:T(8,128)(2,1)} %copy-done.14, bf16[48,6144]{1,0:T(8,128)(2,1)} %copy-done.13, ...), custom_call_target="tpu_custom_call" | custom-call | bytes 18874368 | tf_op jit(solution)/shard_map/put_rows/pallas_call | solution.py:250
  123.7 2.3 %collective-permute-done.11.got_ref = bf16[256,768]{1,0:T(8,128)(2,1)S(1)} collective-permute-done((bf16[256,768]{1,0:T(8,128)(2,1)S(1)}, bf16[256,768]{1,0:T(8,128)(2,1)S(1)}, u32[]{:S(2)}, u32[]{:S(2)}) %collective-permute-start.11) | collective-permute-done | bytes 393248 | tf_op jit(solution)/shard_map/ppermute | solution.py:428
  126.0 1.5 weave_steps.1.tok_ref
  127.5 2.3 %collective-permute-done.12.tok_ref = bf16[512,768]{1,0:T(8,128)(2,1)S(1)} collective-permute-done((bf16[512,768]{1,0:T(8,128)(2,1)S(1)}, bf16[512,768]{1,0:T(8,128)(2,1)S(1)}, u32[]{:S(2)}, u32[]{:S(2)}) %collective-permute-start.12) | collective-permute-done | bytes 786464 | tf_op jit(solution)/shard_map/ppermute | solution.py:446
  129.8 1.7 %copy-done.1 = bf16[768,1536]{1,0:T(8,128)(2,1)S(1)} copy-done((bf16[768,1536]{1,0:T(8,128)(2,1)S(1)}, bf16[768,1536]{1,0:T(8,128)(2,1)}, u32[]{:S(2)}) %copy-start.1) | copy-done | bytes 2359320
  131.5 1.7 %copy-done.3 = bf16[768,1536]{1,0:T(8,128)(2,1)S(1)} copy-done((bf16[768,1536]{1,0:T(8,128)(2,1)S(1)}, bf16[768,1536]{1,0:T(8,128)(2,1)}, u32[]{:S(2)}) %copy-start.3) | copy-done | bytes 2359320
  133.2 1.7 %copy-done.4 = bf16[768,1536]{1,0:T(8,128)(2,1)S(1)} copy-done((bf16[768,1536]{1,0:T(8,128)(2,1)S(1)}, bf16[768,1536]{1,0:T(8,128)(2,1)}, u32[]{:S(2)}) %copy-start.4) | copy-done | bytes 2359320
  134.8 7.2 %layer.3 = bf16[512,768]{1,0:T(8,128)(2,1)S(1)} custom-call(bf16[512,768]{1,0:T(8,128)(2,1)S(1)} %collective-permute-done.12.tok_ref, bf16[768,1536]{1,0:T(8,128)(2,1)S(1)} %copy-done, bf16[768,1536]{1,0:T(8,128)(2,1)S(1)} %copy-done.1, bf16[768,1536]{1,0:T(8,128)(2,1)S(1)} %copy-done.3, bf16[768,1536]{1,0:T(8,128)(2,1)S(1)} %copy-done.4), custom_call_target="tpu_custom_call" | custom-call | flops 4831838208 | bytes 11796480 | tf_op jit(solution)/shard_map/layer/pallas_call | solution.py:285
  142.2 7.2 %layer.2.sum_ref = f32[512,768]{1,0:T(8,128)S(1)} custom-call(bf16[512,768]{1,0:T(8,128)(2,1)S(1)} %weave_steps.1.tok_ref, bf16[768,1536]{1,0:T(8,128)(2,1)S(1)} %copy-done, bf16[768,1536]{1,0:T(8,128)(2,1)S(1)} %copy-done.2, bf16[768,1536]{1,0:T(8,128)(2,1)S(1)} %copy-done.3, bf16[768,1536]{1,0:T(8,128)(2,1)S(1)} %copy-done.4), custom_call_target="tpu_custom_call" | custom-call | flops 4831838208 | bytes 11796480 | tf_op jit(solution)/shard_map/layer/pallas_call | solution.py:285
  149.5 1.8 %finish.1 = bf16[512,768]{1,0:T(8,128)(2,1)} custom-call(bf16[512,768]{1,0:T(8,128)(2,1)S(1)} %weave_steps.1.tok_ref, f32[512,768]{1,0:T(8,128)S(1)} %layer.2.sum_ref, bf16[512,768]{1,0:T(8,128)(2,1)S(1)} %collective-permute-done.13.got_ref, s32[1,768]{1,0:T(1,128)S(1)} %compare_select_fusion.6.order_ref), custom_call_target="tpu_custom_call" | custom-call | flops 603979776 | bytes 3932160 | tf_op jit(solution)/shard_map/finish/pallas_call | solution.py:314
  (54 shorter events, 0.8 us)
Async XLA Ops:
  0.0 8.4 %copy-start.20 = (s32[512]{0:T(512)S(1)}, s32[512]{0:T(512)}, u32[]{:S(2)}) copy-start(s32[512]{0:T(512)} %param.11) | copy-start | bytes 6148
  0.0 8.5 %copy-start.21 = (s32[512]{0:T(512)S(1)}, s32[512]{0:T(512)}, u32[]{:S(2)}) copy-start(s32[512]{0:T(512)} %param.10) | copy-start | bytes 6148
  0.8 7.7 %copy-start.6 = (bf16[8,768]{1,0:T(8,128)(2,1)S(1)}, bf16[8,768]{1,0:T(8,128)(2,1)}, u32[]{:S(2)}) copy-start(bf16[8,768]{1,0:T(8,128)(2,1)} %time_ref.1) | copy-start | bytes 36868
  3.9 41.7 %copy-start.5 = (bf16[512,768]{1,0:T(8,128)(2,1)S(1)}, bf16[512,768]{1,0:T(8,128)(2,1)}, u32[]{:S(2)}) copy-start(bf16[512,768]{1,0:T(8,128)(2,1)} %feat_ref.1) | copy-start | bytes 2359300
  4.8 18.6 %collective-permute-start = (bf16[48,6144]{1,0:T(8,128)(2,1)}, bf16[48,6144]{1,0:T(8,128)(2,1)S(1)}, u32[]{:S(2)}, u32[]{:S(2)}) collective-permute-start(bf16[48,6144]{1,0:T(8,128)(2,1)} %pad_maximum_fusion.1), channel_id=1, source_target_pairs={{0,4},{4,8},{8,12},{12,0},{1,5},{5,9},{9,13},{13,1},{2,6},{6,10},{... | collective-permute-start | bytes 1769480 | tf_op jit(solution)/shard_map/ppermute | solution.py:334
  23.4 29.9 %copy-start.17 = (bf16[48,6144]{1,0:T(8,128)(2,1)}, bf16[48,6144]{1,0:T(8,128)(2,1)S(1)}, u32[]{:S(2)}) copy-start(bf16[48,6144]{1,0:T(8,128)(2,1)S(1)} %collective-permute-done.refs_1_) | copy-start | bytes 1769476
  23.4 14.5 %collective-permute-start.4 = (bf16[48,6144]{1,0:T(8,128)(2,1)S(1)}, bf16[48,6144]{1,0:T(8,128)(2,1)S(1)}, u32[]{:S(2)}, u32[]{:S(2)}) collective-permute-start(bf16[48,6144]{1,0:T(8,128)(2,1)S(1)} %collective-permute-done.refs_1_), channel_id=1, source_target_pairs={{0,16},{16,0},{1,17},{17,1},{2,18},{18,2},{3,19},{19,3},{4,20},{20... | collective-permute-start | bytes 1769480 | tf_op jit(solution)/shard_map/ppermute | solution.py:340
  24.9 14.3 %collective-permute-start.3 = (bf16[48,6144]{1,0:T(8,128)(2,1)S(1)}, bf16[48,6144]{1,0:T(8,128)(2,1)S(1)}, u32[]{:S(2)}, u32[]{:S(2)}) collective-permute-start(bf16[48,6144]{1,0:T(8,128)(2,1)S(1)} %collective-permute-done.refs_1_), channel_id=1, source_target_pairs={{0,2},{2,0},{1,3},{3,1},{4,6},{6,4},{5,7},{7,5},{8,10},{10,8},{9,1... | collective-permute-start | bytes 1769480 | tf_op jit(solution)/shard_map/ppermute | solution.py:339
  26.4 26.9 %collective-permute-start.1 = (bf16[48,6144]{1,0:T(8,128)(2,1)}, bf16[48,6144]{1,0:T(8,128)(2,1)}, u32[]{:S(2)}, u32[]{:S(2)}) collective-permute-start(bf16[48,6144]{1,0:T(8,128)(2,1)} %pad_maximum_fusion.1), channel_id=1, source_target_pairs={{0,12},{4,0},{8,4},{12,8},{1,13},{5,1},{9,5},{13,9},{2,14},{6,2},{... | collective-permute-start | bytes 1769480 | tf_op jit(solution)/shard_map/ppermute | solution.py:334
  28.1 25.2 %collective-permute-start.2 = (bf16[48,6144]{1,0:T(8,128)(2,1)S(1)}, bf16[48,6144]{1,0:T(8,128)(2,1)}, u32[]{:S(2)}, u32[]{:S(2)}) collective-permute-start(bf16[48,6144]{1,0:T(8,128)(2,1)S(1)} %collective-permute-done.refs_1_), channel_id=1, source_target_pairs={{0,4},{4,8},{8,12},{12,0},{1,5},{5,9},{9,13},{13,1},{2,6},{6,10},{... | collective-permute-start | bytes 1769480 | tf_op jit(solution)/shard_map/ppermute | solution.py:334
  37.9 10.8 %copy-start.13 = (bf16[48,6144]{1,0:T(8,128)(2,1)}, bf16[48,6144]{1,0:T(8,128)(2,1)S(1)}, u32[]{:S(2)}) copy-start(bf16[48,6144]{1,0:T(8,128)(2,1)S(1)} %collective-permute-done.4.refs_3_) | copy-start | bytes 1769476
  37.9 15.4 %collective-permute-start.6 = (bf16[48,3072]{1,0:T(8,128)(2,1)S(1)}, bf16[48,3072]{1,0:T(8,128)(2,1)S(1)}, u32[]{:S(2)}, u32[]{:S(2)}) collective-permute-start(bf16[48,3072]{1,0:T(8,128)(2,1)S(1)} %slice.17), channel_id=1, source_target_pairs={{0,2},{2,0},{1,3},{3,1},{4,6},{6,4},{5,7},{7,5},{8,10},{10,8},{9,1... | collective-permute-start | bytes 884744 | tf_op jit(solution)/shard_map/ppermute | solution.py:343
  39.2 0.8 copy-start.14
  40.8 12.5 %collective-permute-start.5 = (bf16[48,3072]{1,0:T(8,128)(2,1)}, bf16[48,3072]{1,0:T(8,128)(2,1)S(1)}, u32[]{:S(2)}, u32[]{:S(2)}) collective-permute-start(bf16[48,3072]{1,0:T(8,128)(2,1)} %slice.16), channel_id=1, source_target_pairs={{0,16},{16,0},{1,17},{17,1},{2,18},{18,2},{3,19},{19,3},{4,20},{20... | collective-permute-start | bytes 884744 | tf_op jit(solution)/shard_map/ppermute | solution.py:342
  42.3 11.0 %all-to-all-start = ((s32[8,1,192]{2,1,0:T(1,128)}), s32[8,1,192]{2,1,0:T(1,128)S(1)}, u32[]{:S(2)}, u32[]{:S(2)}) async-start(s32[8,1,192]{2,1,0:T(1,128)} %get-tuple-element.39), calls=%async_computation | async-start | bytes 16384 | tf_op jit(solution)/shard_map/all_to_all | solution.py:418
  53.3 59.2 %all-to-all-start.1 = ((bf16[8,192,768]{2,1,0:T(8,128)(2,1)}), bf16[8,192,768]{2,1,0:T(8,128)(2,1)S(1)}, u32[]{:S(2)}, u32[]{:S(2)}) async-start(bf16[8,192,768]{2,1,0:T(8,128)(2,1)} %place_rows.1), calls=%async_computation.1 | async-start | bytes 4718592 | tf_op jit(solution)/shard_map/all_to_all | solution.py:425
  57.9 3.5 %copy-start.16 = (bf16[192,3,384]{2,0,1:T(8,128)(2,1)S(1)}, bf16[192,3,384]{2,0,1:T(8,128)(2,1)}, u32[]{:S(2)}) copy-start(bf16[192,3,384]{2,0,1:T(8,128)(2,1)} %param.14) | copy-start | bytes 1327108
  57.9 3.5 %copy-start.12 = (bf16[192,2,1536]{2,1,0:T(2,128)(2,1)S(1)}, bf16[192,2,1536]{2,1,0:T(2,128)(2,1)}, u32[]{:S(2)}) copy-start(bf16[192,2,1536]{2,1,0:T(2,128)(2,1)} %param.16) | copy-start | bytes 3538948
  60.2 1.3 copy-start.11
  60.2 28.4 %collective-permute-start.8 = (bf16[96,6144]{1,0:T(8,128)(2,1)S(1)}, bf16[96,6144]{1,0:T(8,128)(2,1)S(1)}, u32[]{:S(2)}, u32[]{:S(2)}) collective-permute-start(bf16[96,6144]{1,0:T(8,128)(2,1)S(1)} %constant_dynamic-update-slice_fusion.refs_6_), channel_id=1, source_target_pairs={{0,16},{16,0},{1,17},{17,1},{2,18},{18,2},{3,19},{19,3},{4,20},{20... | collective-permute-start | bytes 3538952 | tf_op jit(solution)/shard_map/ppermute | solution.py:340
  60.8 29.5 %collective-permute-start.7 = (bf16[96,6144]{1,0:T(8,128)(2,1)S(1)}, bf16[96,6144]{1,0:T(8,128)(2,1)S(1)}, u32[]{:S(2)}, u32[]{:S(2)}) collective-permute-start(bf16[96,6144]{1,0:T(8,128)(2,1)S(1)} %constant_dynamic-update-slice_fusion.refs_6_), channel_id=1, source_target_pairs={{0,2},{2,0},{1,3},{3,1},{4,6},{6,4},{5,7},{7,5},{8,10},{10,8},{9,1... | collective-permute-start | bytes 3538952 | tf_op jit(solution)/shard_map/ppermute | solution.py:339
  61.5 30.4 %copy-start.15 = (bf16[1536,192]{0,1:T(8,128)(2,1)S(1)}, bf16[1536,192]{0,1:T(8,128)(2,1)}, u32[]{:S(2)}) copy-start(bf16[1536,192]{0,1:T(8,128)(2,1)} %param.17) | copy-start | bytes 1769476
  61.6 30.4 %copy-start.19 = (bf16[384,192]{0,1:T(8,128)(2,1)S(1)}, bf16[384,192]{0,1:T(8,128)(2,1)}, u32[]{:S(2)}) copy-start(bf16[384,192]{0,1:T(8,128)(2,1)} %param.15) | copy-start | bytes 442372
  88.6 1.0 copy-start.9
  89.7 15.0 %collective-permute-start.10 = (bf16[96,3072]{1,0:T(8,128)(2,1)S(1)}, bf16[96,3072]{1,0:T(8,128)(2,1)S(1)}, u32[]{:S(2)}, u32[]{:S(2)}) collective-permute-start(bf16[96,3072]{1,0:T(8,128)(2,1)S(1)} %slice.19), channel_id=1, source_target_pairs={{0,2},{2,0},{1,3},{3,1},{4,6},{6,4},{5,7},{7,5},{8,10},{10,8},{9,1... | collective-permute-start | bytes 1769480 | tf_op jit(solution)/shard_map/ppermute | solution.py:343
  90.3 1.0 copy-start.10
  91.4 14.8 %collective-permute-start.9 = (bf16[96,3072]{1,0:T(8,128)(2,1)S(1)}, bf16[96,3072]{1,0:T(8,128)(2,1)}, u32[]{:S(2)}, u32[]{:S(2)}) collective-permute-start(bf16[96,3072]{1,0:T(8,128)(2,1)S(1)} %slice.18), channel_id=1, source_target_pairs={{0,16},{16,0},{1,17},{17,1},{2,18},{18,2},{3,19},{19,3},{4,20},{20... | collective-permute-start | bytes 1769480 | tf_op jit(solution)/shard_map/ppermute | solution.py:342
  104.7 0.8 copy-start.18
  114.6 0.7 copy-start.7
  115.3 10.7 %collective-permute-start.11 = (bf16[256,768]{1,0:T(8,128)(2,1)S(1)}, bf16[256,768]{1,0:T(8,128)(2,1)S(1)}, u32[]{:S(2)}, u32[]{:S(2)}) collective-permute-start(bf16[256,768]{1,0:T(8,128)(2,1)S(1)} %get-tuple-element.48), channel_id=1, source_target_pairs={{0,2},{2,0},{1,3},{3,1},{4,6},{6,4},{5,7},{7,5},{8,10},{10,8},{9,1... | collective-permute-start | bytes 1179656 | tf_op jit(solution)/shard_map/ppermute | solution.py:428
  115.9 10.1 %copy-start.8 = (bf16[256,768]{1,0:T(8,128)(2,1)S(1)}, bf16[256,768]{1,0:T(8,128)(2,1)}, u32[]{:S(2)}) copy-start(bf16[256,768]{1,0:T(8,128)(2,1)} %copy-done.7) | copy-start | bytes 1179652
  126.0 3.8 %copy-start = (bf16[768,1536]{1,0:T(8,128)(2,1)S(1)}, bf16[768,1536]{1,0:T(8,128)(2,1)}, u32[]{:S(2)}) copy-start(bf16[768,1536]{1,0:T(8,128)(2,1)} %get-tuple-element.65.heads_ref) | copy-start | bytes 7077892
  127.5 2.4 %collective-permute-start.12 = (bf16[512,768]{1,0:T(8,128)(2,1)S(1)}, bf16[512,768]{1,0:T(8,128)(2,1)S(1)}, u32[]{:S(2)}, u32[]{:S(2)}) collective-permute-start(bf16[512,768]{1,0:T(8,128)(2,1)S(1)} %weave_steps.1.tok_ref), channel_id=1, source_target_pairs={{0,1},{1,0},{2,3},{3,2},{4,5},{5,4},{6,7},{7,6},{8,9},{9,8},{10,11... | collective-permute-start | bytes 2359304 | tf_op jit(solution)/shard_map/ppermute | solution.py:446
  129.8 1.7 %copy-start.1 = (bf16[768,1536]{1,0:T(8,128)(2,1)S(1)}, bf16[768,1536]{1,0:T(8,128)(2,1)}, u32[]{:S(2)}) copy-start(bf16[768,1536]{1,0:T(8,128)(2,1)} %get-tuple-element.66.gate_ref) | copy-start | bytes 7077892
  131.5 1.7 %copy-start.3 = (bf16[768,1536]{1,0:T(8,128)(2,1)S(1)}, bf16[768,1536]{1,0:T(8,128)(2,1)}, u32[]{:S(2)}) copy-start(bf16[768,1536]{1,0:T(8,128)(2,1)} %get-tuple-element.67.up_ref) | copy-start | bytes 7077892
  133.2 1.7 %copy-start.4 = (bf16[768,1536]{1,0:T(8,128)(2,1)S(1)}, bf16[768,1536]{1,0:T(8,128)(2,1)}, u32[]{:S(2)}) copy-start(bf16[768,1536]{1,0:T(8,128)(2,1)} %get-tuple-element.68.down_ref) | copy-start | bytes 7077892
  134.8 7.4 %copy-start.2 = (bf16[768,1536]{1,0:T(8,128)(2,1)S(1)}, bf16[768,1536]{1,0:T(8,128)(2,1)}, u32[]{:S(2)}) copy-start(bf16[768,1536]{1,0:T(8,128)(2,1)} %get-tuple-element.66.gate_ref) | copy-start | bytes 7077892
  142.0 7.4 %collective-permute-start.13 = (bf16[512,768]{1,0:T(8,128)(2,1)S(1)}, bf16[512,768]{1,0:T(8,128)(2,1)S(1)}, u32[]{:S(2)}, u32[]{:S(2)}) collective-permute-start(bf16[512,768]{1,0:T(8,128)(2,1)S(1)} %layer.3), channel_id=1, source_target_pairs={{0,1},{1,0},{2,3},{3,2},{4,5},{5,4},{6,7},{7,6},{8,9},{9,8},{10,11... | collective-permute-start | bytes 2359304 | tf_op jit(solution)/shard_map/ppermute | solution.py:448

commit v21 on v18

--- a/solution.py
+++ b/solution.py
@@ -255,7 +255,7 @@
         in_specs=[FAR] * len(pieces),
         out_specs=[WHOLE] * 3,
         scratch_shapes=[pltpu.SemaphoreType.DMA((len(plan),))],
-        compiler_params=params(53),
+        compiler_params=params(40),
         cost_estimate=pl.CostEstimate(flops=0, bytes_accessed=4 * rows * end, transcendentals=0),
         name="put_rows",
     )(*[array for array, _, _ in pieces])

time: 150 us -> 158 us (1.053)
  local copies, waits for them, and re-layouts: 14.8 us -> 22.5 us
    unnamed x46 -> x64, local copies, waits for them, and re-layouts: 10.7 us -> 18.4 us
    pallas_call x1, Pallas kernels: 7.59 us -> 3.86 us  [put_rows(): pl.pallas_call(functools.partial(put_rows_kernel, plan), out_shape=[jax.S...]
    ppermute x1, waiting for transfers between devices: 9.45 us -> 12.1 us  [to_other_places_by_halves(): right = lax.ppermute(by_group[:, cut:], 'slots', swap)]
    pallas_call x1, Pallas kernels: 2.05 us -> 4.5 us  [pool_rows(): pl.pallas_call(functools.partial(pool_kernel, capacity, slot_dev), out_sh...]
  transfers between devices with their start and end apart: 15 -> 15, of which waited for: 10 -> 9; matrix products, arithmetic and copies ran while one was open for 3% -> 2% of each run, Pallas kernels for 13% -> 10%
where the time goes in v21:
time: 158 us; the launch traced here: 157 us
  waiting for transfers between devices  76.3 us (48%)
  Pallas kernels  31.4 us (20%)
  starting transfers between devices  24.3 us (15%)
  local copies, waits for them, and re-layouts  22.5 us (14%)
    ppermute x1, waiting for transfers between devices, to_other_places_by_halves(): by_group = lax.ppermute(shares, 'groups', swap)  25.7 us
    unnamed x64, local copies, waits for them, and re-layouts  18.4 us
    pallas_call x2, Pallas kernels, layer(): pl.pallas_call(layer_kernel, out_shape=jax.ShapeDtypeStruct((rows, width)...  14.5 us
    all_to_all x1, waiting for transfers between devices, on_device(): lax.all_to_all(codes, ('cells', 'mp'), split_axis=0, concat_axis=0, tiled...  14.2 us
    ppermute x3, waiting for transfers between devices, along_cells(): lax.ppermute(values, 'cells', [(j, (j - distance) % n_cells) for j in ran...  12.9 us
    ppermute x1, waiting for transfers between devices, to_other_places_by_halves(): right = lax.ppermute(by_group[:, cut:], 'slots', swap)  12.1 us
    all_to_all x1, waiting for transfers between devices, on_device(): lax.all_to_all(blocks, ('cells', 'mp'), split_axis=0, concat_axis=0, tile...  6.87 us
    ppermute x3, starting transfers between devices, along_cells(): lax.ppermute(values, 'cells', [(j, (j - distance) % n_cells) for j in ran...  5.05 us
  transfers between devices with their start and end apart: 15, of which 9 were waited for; matrix products, arithmetic and copies ran while one was open for 2% of the time, Pallas kernels for 10%

profile of v21, /device:TPU:0, one launch (start us, length us, event | category | flops | bytes accessed | tf_op | source)
XLA Modules:
  0.0 156.6 jit_solution(13668376877583724443)
XLA Ops:
  0.0 0.8 dynamic-slice_bitcast_fusion.2
  0.8 1.0 dynamic-slice_bitcast_fusion.1
  1.8 0.9 dynamic-slice_bitcast_fusion
  2.8 1.2 constant_dynamic-slice_fusion
  4.0 0.9 pad_maximum_fusion.1
  4.8 3.0 %collective-permute-start = (bf16[48,6144]{1,0:T(8,128)(2,1)}, bf16[48,6144]{1,0:T(8,128)(2,1)S(1)}, u32[]{:S(2)}, u32[]{:S(2)}) collective-permute-start(bf16[48,6144]{1,0:T(8,128)(2,1)} %pad_maximum_fusion.1), channel_id=1, source_target_pairs={{0,4},{4,8},{8,12},{12,0},{1,5},{5,9},{9,13},{13,1},{2,6},{6,10},{... | collective-permute-start | bytes 1769480 | tf_op jit(solution)/shard_map/ppermute | solution.py:334
  8.6 1.3 place_codes.1
  9.9 0.6 copy-done.20
  10.5 12.9 %collective-permute-done.refs_1_ = bf16[48,6144]{1,0:T(8,128)(2,1)S(1)} collective-permute-done((bf16[48,6144]{1,0:T(8,128)(2,1)}, bf16[48,6144]{1,0:T(8,128)(2,1)S(1)}, u32[]{:S(2)}, u32[]{:S(2)}) %collective-permute-start) | collective-permute-done | bytes 589856 | tf_op jit(solution)/shard_map/ppermute | solution.py:334
  23.4 1.7 %collective-permute-start.1 = (bf16[48,6144]{1,0:T(8,128)(2,1)}, bf16[48,6144]{1,0:T(8,128)(2,1)}, u32[]{:S(2)}, u32[]{:S(2)}) collective-permute-start(bf16[48,6144]{1,0:T(8,128)(2,1)} %pad_maximum_fusion.1), channel_id=1, source_target_pairs={{0,12},{4,0},{8,4},{12,8},{1,13},{5,1},{9,5},{13,9},{2,14},{6,2},{... | collective-permute-start | bytes 1769480 | tf_op jit(solution)/shard_map/ppermute | solution.py:334
  25.2 2.4 %collective-permute-start.5 = (bf16[48,6144]{1,0:T(8,128)(2,1)S(1)}, bf16[48,6144]{1,0:T(8,128)(2,1)S(1)}, u32[]{:S(2)}, u32[]{:S(2)}) collective-permute-start(bf16[48,6144]{1,0:T(8,128)(2,1)S(1)} %collective-permute-done.refs_1_), channel_id=1, source_target_pairs={{0,18},{2,16},{16,2},{18,0},{1,19},{3,17},{17,3},{19,1},{4,22},{6,... | collective-permute-start | bytes 1769480 | tf_op jit(solution)/shard_map/ppermute | solution.py:343
  28.1 0.5 collective-permute-start.3
  28.9 4.8 %all-to-all-start = ((s32[8,1,192]{2,1,0:T(1,128)}), s32[8,1,192]{2,1,0:T(1,128)S(1)}, u32[]{:S(2)}, u32[]{:S(2)}) async-start(s32[8,1,192]{2,1,0:T(1,128)} %get-tuple-element.36), calls=%async_computation | async-start | bytes 16384 | tf_op jit(solution)/shard_map/all_to_all | solution.py:428
  33.8 3.0 %place_rows.1 = bf16[8,192,768]{2,1,0:T(8,128)(2,1)} custom-call(s32[1,512]{1,0:T(1,128)S(1)} %bitcast.22, bf16[512,768]{1,0:T(8,128)(2,1)S(1)} %copy-done.18), custom_call_target="tpu_custom_call" | custom-call | flops 1207959552 | bytes 3145728 | tf_op jit(solution)/shard_map/place_rows/pallas_call | solution.py:98
  36.8 14.2 %all-to-all-done.code_ref = s32[8,1,192]{2,1,0:T(1,128)S(1)} async-done(((s32[8,1,192]{2,1,0:T(1,128)}), s32[8,1,192]{2,1,0:T(1,128)S(1)}, u32[]{:S(2)}, u32[]{:S(2)}) %all-to-all-start) | async-done | bytes 6176 | tf_op jit(solution)/shard_map/all_to_all | solution.py:428
  51.0 1.6 %collective-permute-done.4.refs_3_ = bf16[48,6144]{1,0:T(8,128)(2,1)S(1)} collective-permute-done((bf16[48,6144]{1,0:T(8,128)(2,1)S(1)}, bf16[48,6144]{1,0:T(8,128)(2,1)S(1)}, u32[]{:S(2)}, u32[]{:S(2)}) %collective-permute-start.4) | collective-permute-done | bytes 589856 | tf_op jit(solution)/shard_map/ppermute | solution.py:343
  52.7 0.7 copy-done.8
  53.6 4.4 %all-to-all-start.1 = ((bf16[8,192,768]{2,1,0:T(8,128)(2,1)}), bf16[8,192,768]{2,1,0:T(8,128)(2,1)}, u32[]{:S(2)}, u32[]{:S(2)}) async-start(bf16[8,192,768]{2,1,0:T(8,128)(2,1)} %place_rows.1), calls=%async_computation.1 | async-start | bytes 4718592 | tf_op jit(solution)/shard_map/all_to_all | solution.py:435
  58.0 1.2 constant_dynamic-update-slice_fusion.1
  59.2 1.1 constant_dynamic-update-slice_fusion.refs_5_
  60.4 1.6 %collective-permute-start.7 = (bf16[96,6144]{1,0:T(8,128)(2,1)S(1)}, bf16[96,6144]{1,0:T(8,128)(2,1)S(1)}, u32[]{:S(2)}, u32[]{:S(2)}) collective-permute-start(bf16[96,6144]{1,0:T(8,128)(2,1)S(1)} %constant_dynamic-update-slice_fusion.refs_5_), channel_id=1, source_target_pairs={{0,16},{16,0},{1,17},{17,1},{2,18},{18,2},{3,19},{19,3},{4,20},{20... | collective-permute-start | bytes 3538952 | tf_op jit(solution)/shard_map/ppermute | solution.py:350
  62.0 0.8 collective-permute-start.6
  63.0 25.7 %collective-permute-done.7.refs_7_ = bf16[96,6144]{1,0:T(8,128)(2,1)S(1)} collective-permute-done((bf16[96,6144]{1,0:T(8,128)(2,1)S(1)}, bf16[96,6144]{1,0:T(8,128)(2,1)S(1)}, u32[]{:S(2)}, u32[]{:S(2)}) %collective-permute-start.7) | collective-permute-done | bytes 1179680 | tf_op jit(solution)/shard_map/ppermute | solution.py:350
  88.7 1.6 collective-permute-start.9
  90.3 0.9 collective-permute-start.8
  91.5 12.1 %collective-permute-done.9.refs_9_ = bf16[96,3072]{1,0:T(8,128)(2,1)S(1)} collective-permute-done((bf16[96,3072]{1,0:T(8,128)(2,1)S(1)}, bf16[96,3072]{1,0:T(8,128)(2,1)S(1)}, u32[]{:S(2)}, u32[]{:S(2)}) %collective-permute-start.9) | collective-permute-done | bytes 589856 | tf_op jit(solution)/shard_map/ppermute | solution.py:353
  103.7 0.8 copy-done.12
  105.0 0.8 copy-done.14
  105.8 6.9 %all-to-all-done.1.got_ref = bf16[8,192,768]{2,1,0:T(8,128)(2,1)} async-done(((bf16[8,192,768]{2,1,0:T(8,128)(2,1)}), bf16[8,192,768]{2,1,0:T(8,128)(2,1)}, u32[]{:S(2)}, u32[]{:S(2)}) %all-to-all-start.1) | async-done | bytes 2359328 | tf_op jit(solution)/shard_map/all_to_all | solution.py:435
  112.7 0.7 copy-done.21
  113.4 4.5 %pool_rows.1 = (bf16[256,768]{1,0:T(8,128)(2,1)S(1)}, bf16[256,768]{1,0:T(8,128)(2,1)}) custom-call(s32[1]{0:T(128)} %bitcast.slot_ref, bf16[8,768]{1,0:T(8,128)(2,1)S(1)} %copy-done.21, s32[8,1,192]{2,1,0:T(1,128)S(1)} %all-to-all-done.code_ref, bf16[8,192,768]{2,1,0:T(8,128)(2,1)} %all-to-all-done.1.got_ref), custom_call_target="tpu_custom_call" | custom-call | flops 1207959552 | bytes 2359296 | tf_op jit(solution)/shard_map/pool_rows/pallas_call | solution.py:138
  117.9 0.7 copy-done.22
  118.6 1.5 collective-permute-start.10
  120.2 1.3 copy-done.1
  121.4 1.3 copy-done.3
  122.7 1.1 copy-done.5
  123.8 1.1 copy-done.7
  124.8 1.1 copy-done.9
  125.9 1.1 copy-done.11
  127.0 1.1 copy-done.13
  128.0 1.1 copy-done.15
  129.1 3.9 %put_rows.1 = (bf16[768,1536]{1,0:T(8,128)(2,1)S(1)}, bf16[768,3072]{1,0:T(8,128)(2,1)}, bf16[768,1536]{1,0:T(8,128)(2,1)S(1)}) custom-call(bf16[192,6144]{1,0:T(8,128)(2,1)S(1)} %pad_maximum_fusion.refs_0_, bf16[48,6144]{1,0:T(8,128)(2,1)S(1)} %copy-done.5, bf16[48,6144]{1,0:T(8,128)(2,1)S(1)} %copy-done.11, bf16[48,6144]{1,0:T(8,128)(2,1)S(1)} %copy-done.9, ...), custom_call_target="tpu_custom_call" | custom-call | bytes 18874368 | tf_op jit(solution)/shard_map/put_rows/pallas_call | solution.py:248
  133.0 2.5 %weave_steps.1.tok_ref = bf16[512,768]{1,0:T(8,128)(2,1)S(1)} custom-call(s32[1]{0:T(128)} %bitcast.slot_ref, s32[1,768]{1,0:T(1,128)S(1)} %compare_select_fusion.6.order_ref, bf16[256,768]{1,0:T(8,128)(2,1)S(1)} %copy-done.23, bf16[256,768]{1,0:T(8,128)(2,1)} %collective-permute-done.10.got_ref), custom_call_target="tpu_custom_call" | custom-call | flops 1006632960 | bytes 1572864 | tf_op jit(solution)/shard_map/weave_steps/pallas_call | solution.py:167
  135.5 2.3 %collective-permute-done.11.tok_ref = bf16[512,768]{1,0:T(8,128)(2,1)S(1)} collective-permute-done((bf16[512,768]{1,0:T(8,128)(2,1)S(1)}, bf16[512,768]{1,0:T(8,128)(2,1)S(1)}, u32[]{:S(2)}, u32[]{:S(2)}) %collective-permute-start.11) | collective-permute-done | bytes 786464 | tf_op jit(solution)/shard_map/ppermute | solution.py:454
  137.8 2.3 %copy-done.16 = bf16[768,3072]{1,0:T(8,128)(2,1)S(1)} copy-done((bf16[768,3072]{1,0:T(8,128)(2,1)S(1)}, bf16[768,3072]{1,0:T(8,128)(2,1)}, u32[]{:S(2)}) %copy-start.16) | copy-done | bytes 4718616
  140.1 7.2 %layer.3 = bf16[512,768]{1,0:T(8,128)(2,1)S(1)} custom-call(bf16[512,768]{1,0:T(8,128)(2,1)S(1)} %collective-permute-done.11.tok_ref, bf16[768,1536]{1,0:T(8,128)(2,1)S(1)} %get-tuple-element.60.heads_ref, bf16[768,3072]{1,0:T(8,128)(2,1)S(1)} %copy-done.16, bf16[768,1536]{1,0:T(8,128)(2,1)S(1)} %get-tuple-element.62.down_ref), custom_call_target="tpu_custom_call" | custom-call | flops 4831838208 | bytes 11796480 | tf_op jit(solution)/shard_map/layer/pallas_call | solution.py:285
  147.6 7.3 %layer.2.sum_ref = f32[512,768]{1,0:T(8,128)S(1)} custom-call(bf16[512,768]{1,0:T(8,128)(2,1)S(1)} %weave_steps.1.tok_ref, bf16[768,1536]{1,0:T(8,128)(2,1)S(1)} %get-tuple-element.60.heads_ref, bf16[768,3072]{1,0:T(8,128)(2,1)S(1)} %copy-done.17, bf16[768,1536]{1,0:T(8,128)(2,1)S(1)} %get-tuple-element.62.down_ref), custom_call_target="tpu_custom_call" | custom-call | flops 4831838208 | bytes 11796480 | tf_op jit(solution)/shard_map/layer/pallas_call | solution.py:285
  154.9 1.8 %finish.1 = bf16[512,768]{1,0:T(8,128)(2,1)} custom-call(bf16[512,768]{1,0:T(8,128)(2,1)S(1)} %weave_steps.1.tok_ref, f32[512,768]{1,0:T(8,128)S(1)} %layer.2.sum_ref, bf16[512,768]{1,0:T(8,128)(2,1)S(1)} %collective-permute-done.12.got_ref, s32[1,768]{1,0:T(1,128)S(1)} %compare_select_fusion.6.order_ref), custom_call_target="tpu_custom_call" | custom-call | flops 603979776 | bytes 3932160 | tf_op jit(solution)/shard_map/finish/pallas_call | solution.py:314
  (66 shorter events, 2.6 us)
Async XLA Ops:
  0.0 8.5 %copy-start.28 = (s32[512]{0:T(512)S(1)}, s32[512]{0:T(512)}, u32[]{:S(2)}) copy-start(s32[512]{0:T(512)} %param.11) | copy-start | bytes 6148
  0.0 8.5 %copy-start.29 = (s32[512]{0:T(512)S(1)}, s32[512]{0:T(512)}, u32[]{:S(2)}) copy-start(s32[512]{0:T(512)} %param.10) | copy-start | bytes 6148
  0.8 7.7 %copy-start.19 = (bf16[8,768]{1,0:T(8,128)(2,1)S(1)}, bf16[8,768]{1,0:T(8,128)(2,1)}, u32[]{:S(2)}) copy-start(bf16[8,768]{1,0:T(8,128)(2,1)} %time_ref.1) | copy-start | bytes 36868
  0.8 32.9 %copy-start.18 = (bf16[512,768]{1,0:T(8,128)(2,1)S(1)}, bf16[512,768]{1,0:T(8,128)(2,1)}, u32[]{:S(2)}) copy-start(bf16[512,768]{1,0:T(8,128)(2,1)} %feat_ref.1) | copy-start | bytes 2359300
  4.8 18.6 %collective-permute-start = (bf16[48,6144]{1,0:T(8,128)(2,1)}, bf16[48,6144]{1,0:T(8,128)(2,1)S(1)}, u32[]{:S(2)}, u32[]{:S(2)}) collective-permute-start(bf16[48,6144]{1,0:T(8,128)(2,1)} %pad_maximum_fusion.1), channel_id=1, source_target_pairs={{0,4},{4,8},{8,12},{12,0},{1,5},{5,9},{9,13},{13,1},{2,6},{6,10},{... | collective-permute-start | bytes 1769480 | tf_op jit(solution)/shard_map/ppermute | solution.py:334
  9.9 0.6 copy-start.20
  23.4 13.4 %copy-start.4 = (bf16[48,6144]{1,0:T(8,128)(2,1)}, bf16[48,6144]{1,0:T(8,128)(2,1)S(1)}, u32[]{:S(2)}) copy-start(bf16[48,6144]{1,0:T(8,128)(2,1)S(1)} %collective-permute-done.refs_1_) | copy-start | bytes 1769476
  23.4 27.6 %collective-permute-start.1 = (bf16[48,6144]{1,0:T(8,128)(2,1)}, bf16[48,6144]{1,0:T(8,128)(2,1)}, u32[]{:S(2)}, u32[]{:S(2)}) collective-permute-start(bf16[48,6144]{1,0:T(8,128)(2,1)} %pad_maximum_fusion.1), channel_id=1, source_target_pairs={{0,12},{4,0},{8,4},{12,8},{1,13},{5,1},{9,5},{13,9},{2,14},{6,2},{... | collective-permute-start | bytes 1769480 | tf_op jit(solution)/shard_map/ppermute | solution.py:334
  25.2 25.8 %collective-permute-start.5 = (bf16[48,6144]{1,0:T(8,128)(2,1)S(1)}, bf16[48,6144]{1,0:T(8,128)(2,1)S(1)}, u32[]{:S(2)}, u32[]{:S(2)}) collective-permute-start(bf16[48,6144]{1,0:T(8,128)(2,1)S(1)} %collective-permute-done.refs_1_), channel_id=1, source_target_pairs={{0,18},{2,16},{16,2},{18,0},{1,19},{3,17},{17,3},{19,1},{4,22},{6,... | collective-permute-start | bytes 1769480 | tf_op jit(solution)/shard_map/ppermute | solution.py:343
  27.6 25.0 %collective-permute-start.4 = (bf16[48,6144]{1,0:T(8,128)(2,1)S(1)}, bf16[48,6144]{1,0:T(8,128)(2,1)S(1)}, u32[]{:S(2)}, u32[]{:S(2)}) collective-permute-start(bf16[48,6144]{1,0:T(8,128)(2,1)S(1)} %collective-permute-done.refs_1_), channel_id=1, source_target_pairs={{0,16},{2,18},{16,0},{18,2},{1,17},{3,19},{17,1},{19,3},{4,20},{6,... | collective-permute-start | bytes 1769480 | tf_op jit(solution)/shard_map/ppermute | solution.py:343
  28.1 24.6 %collective-permute-start.3 = (bf16[48,6144]{1,0:T(8,128)(2,1)S(1)}, bf16[48,6144]{1,0:T(8,128)(2,1)S(1)}, u32[]{:S(2)}, u32[]{:S(2)}) collective-permute-start(bf16[48,6144]{1,0:T(8,128)(2,1)S(1)} %collective-permute-done.refs_1_), channel_id=1, source_target_pairs={{0,2},{2,0},{16,18},{18,16},{1,3},{3,1},{17,19},{19,17},{4,6},{6,4... | collective-permute-start | bytes 1769480 | tf_op jit(solution)/shard_map/ppermute | solution.py:343
  28.6 24.1 %collective-permute-start.2 = (bf16[48,6144]{1,0:T(8,128)(2,1)S(1)}, bf16[48,6144]{1,0:T(8,128)(2,1)}, u32[]{:S(2)}, u32[]{:S(2)}) collective-permute-start(bf16[48,6144]{1,0:T(8,128)(2,1)S(1)} %collective-permute-done.refs_1_), channel_id=1, source_target_pairs={{0,4},{4,8},{8,12},{12,0},{1,5},{5,9},{9,13},{13,1},{2,6},{6,10},{... | collective-permute-start | bytes 1769480 | tf_op jit(solution)/shard_map/ppermute | solution.py:334
  28.9 22.1 %all-to-all-start = ((s32[8,1,192]{2,1,0:T(1,128)}), s32[8,1,192]{2,1,0:T(1,128)S(1)}, u32[]{:S(2)}, u32[]{:S(2)}) async-start(s32[8,1,192]{2,1,0:T(1,128)} %get-tuple-element.36), calls=%async_computation | async-start | bytes 16384 | tf_op jit(solution)/shard_map/all_to_all | solution.py:428
  51.0 1.7 %copy-start.6 = (bf16[48,6144]{1,0:T(8,128)(2,1)}, bf16[48,6144]{1,0:T(8,128)(2,1)S(1)}, u32[]{:S(2)}) copy-start(bf16[48,6144]{1,0:T(8,128)(2,1)S(1)} %collective-permute-done.5.refs_4_) | copy-start | bytes 1769476
  52.6 0.8 copy-start.8
  52.7 0.9 copy-start.10
  53.6 59.1 %all-to-all-start.1 = ((bf16[8,192,768]{2,1,0:T(8,128)(2,1)}), bf16[8,192,768]{2,1,0:T(8,128)(2,1)}, u32[]{:S(2)}, u32[]{:S(2)}) async-start(bf16[8,192,768]{2,1,0:T(8,128)(2,1)} %place_rows.1), calls=%async_computation.1 | async-start | bytes 4718592 | tf_op jit(solution)/shard_map/all_to_all | solution.py:435
  58.0 4.8 %copy-start.26 = (bf16[192,3,384]{2,0,1:T(8,128)(2,1)S(1)}, bf16[192,3,384]{2,0,1:T(8,128)(2,1)}, u32[]{:S(2)}) copy-start(bf16[192,3,384]{2,0,1:T(8,128)(2,1)} %param.14) | copy-start | bytes 1327108
  58.0 4.8 %copy-start.24 = (bf16[192,2,1536]{2,1,0:T(2,128)(2,1)S(1)}, bf16[192,2,1536]{2,1,0:T(2,128)(2,1)}, u32[]{:S(2)}) copy-start(bf16[192,2,1536]{2,1,0:T(2,128)(2,1)} %param.16) | copy-start | bytes 3538948
  60.4 2.6 %copy-start.2 = (bf16[96,6144]{1,0:T(8,128)(2,1)}, bf16[96,6144]{1,0:T(8,128)(2,1)S(1)}, u32[]{:S(2)}) copy-start(bf16[96,6144]{1,0:T(8,128)(2,1)S(1)} %constant_dynamic-update-slice_fusion.refs_5_) | copy-start | bytes 3538948
  60.4 28.3 %collective-permute-start.7 = (bf16[96,6144]{1,0:T(8,128)(2,1)S(1)}, bf16[96,6144]{1,0:T(8,128)(2,1)S(1)}, u32[]{:S(2)}, u32[]{:S(2)}) collective-permute-start(bf16[96,6144]{1,0:T(8,128)(2,1)S(1)} %constant_dynamic-update-slice_fusion.refs_5_), channel_id=1, source_target_pairs={{0,16},{16,0},{1,17},{17,1},{2,18},{18,2},{3,19},{19,3},{4,20},{20... | collective-permute-start | bytes 3538952 | tf_op jit(solution)/shard_map/ppermute | solution.py:350
  62.0 28.3 %collective-permute-start.6 = (bf16[96,6144]{1,0:T(8,128)(2,1)S(1)}, bf16[96,6144]{1,0:T(8,128)(2,1)S(1)}, u32[]{:S(2)}, u32[]{:S(2)}) collective-permute-start(bf16[96,6144]{1,0:T(8,128)(2,1)S(1)} %constant_dynamic-update-slice_fusion.refs_5_), channel_id=1, source_target_pairs={{0,2},{2,0},{1,3},{3,1},{4,6},{6,4},{5,7},{7,5},{8,10},{10,8},{9,1... | collective-permute-start | bytes 3538952 | tf_op jit(solution)/shard_map/ppermute | solution.py:349
  63.0 28.3 %copy-start.25 = (bf16[1536,192]{0,1:T(8,128)(2,1)S(1)}, bf16[1536,192]{0,1:T(8,128)(2,1)}, u32[]{:S(2)}) copy-start(bf16[1536,192]{0,1:T(8,128)(2,1)} %param.17) | copy-start | bytes 1769476
  63.0 28.3 %copy-start.27 = (bf16[384,192]{0,1:T(8,128)(2,1)S(1)}, bf16[384,192]{0,1:T(8,128)(2,1)}, u32[]{:S(2)}) copy-start(bf16[384,192]{0,1:T(8,128)(2,1)} %param.15) | copy-start | bytes 442372
  88.7 14.9 %collective-permute-start.9 = (bf16[96,3072]{1,0:T(8,128)(2,1)S(1)}, bf16[96,3072]{1,0:T(8,128)(2,1)S(1)}, u32[]{:S(2)}, u32[]{:S(2)}) collective-permute-start(bf16[96,3072]{1,0:T(8,128)(2,1)S(1)} %slice.9), channel_id=1, source_target_pairs={{0,2},{2,0},{1,3},{3,1},{4,6},{6,4},{5,7},{7,5},{8,10},{10,8},{9,1... | collective-permute-start | bytes 1769480 | tf_op jit(solution)/shard_map/ppermute | solution.py:353
  90.3 1.0 copy-start
  90.3 14.7 %collective-permute-start.8 = (bf16[96,3072]{1,0:T(8,128)(2,1)S(1)}, bf16[96,3072]{1,0:T(8,128)(2,1)S(1)}, u32[]{:S(2)}, u32[]{:S(2)}) collective-permute-start(bf16[96,3072]{1,0:T(8,128)(2,1)S(1)} %slice.8), channel_id=1, source_target_pairs={{0,16},{16,0},{1,17},{17,1},{2,18},{18,2},{3,19},{19,3},{4,20},{20... | collective-permute-start | bytes 1769480 | tf_op jit(solution)/shard_map/ppermute | solution.py:352
  103.7 0.8 copy-start.12
  105.0 0.8 copy-start.14
  112.7 0.7 copy-start.21
  117.9 0.8 copy-start.22
  118.6 14.3 %collective-permute-start.10 = (bf16[256,768]{1,0:T(8,128)(2,1)}, bf16[256,768]{1,0:T(8,128)(2,1)}, u32[]{:S(2)}, u32[]{:S(2)}) collective-permute-start(bf16[256,768]{1,0:T(8,128)(2,1)} %get-tuple-element.45), channel_id=1, source_target_pairs={{0,2},{2,0},{1,3},{3,1},{4,6},{6,4},{5,7},{7,5},{8,10},{10,8},{9,1... | collective-permute-start | bytes 1179656 | tf_op jit(solution)/shard_map/ppermute | solution.py:438
  120.2 1.3 copy-start.1
  121.4 1.3 copy-start.3
  122.7 1.1 copy-start.5
  123.8 1.1 copy-start.7
  124.8 1.1 copy-start.9
  125.9 1.1 copy-start.11
  127.0 1.1 copy-start.13
  128.0 1.1 copy-start.15
  129.1 3.9 %copy-start.23 = (bf16[256,768]{1,0:T(8,128)(2,1)S(1)}, bf16[256,768]{1,0:T(8,128)(2,1)}, u32[]{:S(2)}) copy-start(bf16[256,768]{1,0:T(8,128)(2,1)} %copy-done.22) | copy-start | bytes 1179652
  135.5 2.4 %collective-permute-start.11 = (bf16[512,768]{1,0:T(8,128)(2,1)S(1)}, bf16[512,768]{1,0:T(8,128)(2,1)S(1)}, u32[]{:S(2)}, u32[]{:S(2)}) collective-permute-start(bf16[512,768]{1,0:T(8,128)(2,1)S(1)} %weave_steps.1.tok_ref), channel_id=1, source_target_pairs={{0,1},{1,0},{2,3},{3,2},{4,5},{5,4},{6,7},{7,6},{8,9},{9,8},{10,11... | collective-permute-start | bytes 2359304 | tf_op jit(solution)/shard_map/ppermute | solution.py:454
  137.8 2.3 %copy-start.16 = (bf16[768,3072]{1,0:T(8,128)(2,1)S(1)}, bf16[768,3072]{1,0:T(8,128)(2,1)}, u32[]{:S(2)}) copy-start(bf16[768,3072]{1,0:T(8,128)(2,1)} %get-tuple-element.61.gate_up_ref) | copy-start | bytes 14155780
  140.1 7.5 %copy-start.17 = (bf16[768,3072]{1,0:T(8,128)(2,1)S(1)}, bf16[768,3072]{1,0:T(8,128)(2,1)}, u32[]{:S(2)}) copy-start(bf16[768,3072]{1,0:T(8,128)(2,1)} %get-tuple-element.61.gate_up_ref) | copy-start | bytes 14155780
  147.4 7.5 %collective-permute-start.12 = (bf16[512,768]{1,0:T(8,128)(2,1)S(1)}, bf16[512,768]{1,0:T(8,128)(2,1)S(1)}, u32[]{:S(2)}, u32[]{:S(2)}) collective-permute-start(bf16[512,768]{1,0:T(8,128)(2,1)S(1)} %layer.3), channel_id=1, source_target_pairs={{0,1},{1,0},{2,3},{3,2},{4,5},{5,4},{6,7},{7,6},{8,9},{9,8},{10,11... | collective-permute-start | bytes 2359304 | tf_op jit(solution)/shard_map/ppermute | solution.py:456

commit v22 on v19

--- a/solution.py
+++ b/solution.py
@@ -171,7 +171,7 @@
         out_specs=WHOLE,
         compiler_params=params(12),
         cost_estimate=pl.CostEstimate(
-            flops=2 * rows * width * (rows + width), bytes_accessed=4 * rows * width, transcendentals=0
+            flops=16 * rows * width * (rows + width), bytes_accessed=4 * rows * width, transcendentals=0
         ),
         name="weave_steps",
     )(my_slot, order.reshape(1, width), keep, got)
@@ -419,7 +419,7 @@
         first = to_other_places(below)
         blocks = place_rows(owner, obs_feat, n_owners, capacity)
         above, opposite = along_cells(share_rows, 1), along_cells(below, -1)
-        blocks, codes, above, first = lax.optimization_barrier((blocks, codes, above, first))
+        blocks, codes, above, opposite, first = lax.optimization_barrier((blocks, codes, above, opposite, first))
         second = to_other_places(jnp.concatenate([above, opposite], axis=0))
         shard = side_by_side(*local_weights)
         got = lax.all_to_all(blocks, ("cells", "mp"), split_axis=0, concat_axis=0, tiled=True)

time: 201 us -> 147 us (0.73)
  the two profiles are of different devices: /device:TPU:17 before, /device:TPU:0 now
where the time goes in v22:
time: 147 us; the launch traced here: 146 us
  waiting for transfers between devices  77.5 us (53%)
  Pallas kernels  31.6 us (21%)
  starting transfers between devices  21.9 us (15%)
  local copies, waits for them, and re-layouts  11.7 us (8%)
  other arithmetic  2.6 us (2%)
    ppermute x2, waiting for transfers between devices, to_other_places(): by_group = lax.ppermute(shares, 'groups', swap)  36.6 us
    pallas_call x2, Pallas kernels, layer(): pl.pallas_call(layer_kernel, out_shape=jax.ShapeDtypeStruct((rows, width)...  14.4 us
    ppermute x3, waiting for transfers between devices, along_cells(): lax.ppermute(values, 'cells', [(j, (j - distance) % n_cells) for j in ran...  13.5 us
    ppermute x2, waiting for transfers between devices, to_other_places(): right = lax.ppermute(by_group[:, cut:], 'slots', swap)  11.1 us
    pallas_call x1, Pallas kernels, put_rows(): pl.pallas_call(functools.partial(put_rows_kernel, plan), out_shape=[jax.S...  7.61 us
    unnamed x44, local copies, waits for them, and re-layouts  6.83 us
    all_to_all x1, waiting for transfers between devices, on_device(): lax.all_to_all(blocks, ('cells', 'mp'), split_axis=0, concat_axis=0, tile...  6.3 us
    ppermute x3, starting transfers between devices, along_cells(): lax.ppermute(values, 'cells', [(j, (j - distance) % n_cells) for j in ran...  5.05 us
  transfers between devices with their start and end apart: 16, of which 9 were waited for; matrix products, arithmetic and copies ran while one was open for 3% of the time, Pallas kernels for 13%

profile of v22, /device:TPU:0, one launch (start us, length us, event | category | flops | bytes accessed | tf_op | source)
XLA Modules:
  0.0 146.2 jit_solution(10943027808137650498)
XLA Ops:
  0.0 0.8 dynamic-slice_bitcast_fusion.2
  0.8 0.9 dynamic-slice_bitcast_fusion.1
  1.8 0.9 dynamic-slice_bitcast_fusion
  2.7 1.2 constant_dynamic-slice_fusion
  3.9 0.9 pad_maximum_fusion.1
  4.8 3.0 %collective-permute-start = (bf16[48,6144]{1,0:T(8,128)(2,1)}, bf16[48,6144]{1,0:T(8,128)(2,1)S(1)}, u32[]{:S(2)}, u32[]{:S(2)}) collective-permute-start(bf16[48,6144]{1,0:T(8,128)(2,1)} %pad_maximum_fusion.1), channel_id=1, source_target_pairs={{0,4},{4,8},{8,12},{12,0},{1,5},{5,9},{9,13},{13,1},{2,6},{6,10},{... | collective-permute-start | bytes 1769480 | tf_op jit(solution)/shard_map/ppermute | solution.py:334
  8.5 1.3 place_codes.1
  9.8 13.5 %collective-permute-done.refs_1_ = bf16[48,6144]{1,0:T(8,128)(2,1)S(1)} collective-permute-done((bf16[48,6144]{1,0:T(8,128)(2,1)}, bf16[48,6144]{1,0:T(8,128)(2,1)S(1)}, u32[]{:S(2)}, u32[]{:S(2)}) %collective-permute-start) | collective-permute-done | bytes 589856 | tf_op jit(solution)/shard_map/ppermute | solution.py:334
  23.4 1.5 %collective-permute-start.4 = (bf16[48,6144]{1,0:T(8,128)(2,1)S(1)}, bf16[48,6144]{1,0:T(8,128)(2,1)S(1)}, u32[]{:S(2)}, u32[]{:S(2)}) collective-permute-start(bf16[48,6144]{1,0:T(8,128)(2,1)S(1)} %collective-permute-done.refs_1_), channel_id=1, source_target_pairs={{0,16},{16,0},{1,17},{17,1},{2,18},{18,2},{3,19},{19,3},{4,20},{20... | collective-permute-start | bytes 1769480 | tf_op jit(solution)/shard_map/ppermute | solution.py:340
  24.9 1.5 %collective-permute-start.3 = (bf16[48,6144]{1,0:T(8,128)(2,1)S(1)}, bf16[48,6144]{1,0:T(8,128)(2,1)S(1)}, u32[]{:S(2)}, u32[]{:S(2)}) collective-permute-start(bf16[48,6144]{1,0:T(8,128)(2,1)S(1)} %collective-permute-done.refs_1_), channel_id=1, source_target_pairs={{0,2},{2,0},{1,3},{3,1},{4,6},{6,4},{5,7},{7,5},{8,10},{10,8},{9,1... | collective-permute-start | bytes 1769480 | tf_op jit(solution)/shard_map/ppermute | solution.py:339
  26.4 1.7 %collective-permute-start.1 = (bf16[48,6144]{1,0:T(8,128)(2,1)}, bf16[48,6144]{1,0:T(8,128)(2,1)}, u32[]{:S(2)}, u32[]{:S(2)}) collective-permute-start(bf16[48,6144]{1,0:T(8,128)(2,1)} %pad_maximum_fusion.1), channel_id=1, source_target_pairs={{0,12},{4,0},{8,4},{12,8},{1,13},{5,1},{9,5},{13,9},{2,14},{6,2},{... | collective-permute-start | bytes 1769480 | tf_op jit(solution)/shard_map/ppermute | solution.py:334
  28.1 0.3 collective-permute-start.2
  28.4 9.5 %collective-permute-done.4.refs_3_ = bf16[48,6144]{1,0:T(8,128)(2,1)S(1)} collective-permute-done((bf16[48,6144]{1,0:T(8,128)(2,1)S(1)}, bf16[48,6144]{1,0:T(8,128)(2,1)S(1)}, u32[]{:S(2)}, u32[]{:S(2)}) %collective-permute-start.4) | collective-permute-done | bytes 589856 | tf_op jit(solution)/shard_map/ppermute | solution.py:340
  37.9 1.3 collective-permute-start.6
  39.2 0.8 copy-done.12
  40.0 0.7 slice.16
  40.8 1.5 %collective-permute-start.5 = (bf16[48,3072]{1,0:T(8,128)(2,1)}, bf16[48,3072]{1,0:T(8,128)(2,1)S(1)}, u32[]{:S(2)}, u32[]{:S(2)}) collective-permute-start(bf16[48,3072]{1,0:T(8,128)(2,1)} %slice.16), channel_id=1, source_target_pairs={{0,16},{16,0},{1,17},{17,1},{2,18},{18,2},{3,19},{19,3},{4,20},{20... | collective-permute-start | bytes 884744 | tf_op jit(solution)/shard_map/ppermute | solution.py:342
  42.3 3.3 %all-to-all-start = ((s32[8,1,192]{2,1,0:T(1,128)}), s32[8,1,192]{2,1,0:T(1,128)S(1)}, u32[]{:S(2)}, u32[]{:S(2)}) async-start(s32[8,1,192]{2,1,0:T(1,128)} %get-tuple-element.37), calls=%async_computation | async-start | bytes 16384 | tf_op jit(solution)/shard_map/all_to_all | solution.py:418
  45.6 3.0 %place_rows.1 = bf16[8,192,768]{2,1,0:T(8,128)(2,1)} custom-call(s32[1,512]{1,0:T(1,128)S(1)} %bitcast.22, bf16[512,768]{1,0:T(8,128)(2,1)S(1)} %copy-done.3), custom_call_target="tpu_custom_call" | custom-call | flops 1207959552 | bytes 3145728 | tf_op jit(solution)/shard_map/place_rows/pallas_call | solution.py:98
  48.6 4.6 %all-to-all-done.code_ref = s32[8,1,192]{2,1,0:T(1,128)S(1)} async-done(((s32[8,1,192]{2,1,0:T(1,128)}), s32[8,1,192]{2,1,0:T(1,128)S(1)}, u32[]{:S(2)}, u32[]{:S(2)}) %all-to-all-start) | async-done | bytes 6176 | tf_op jit(solution)/shard_map/all_to_all | solution.py:418
  53.3 4.6 %all-to-all-start.1 = ((bf16[8,192,768]{2,1,0:T(8,128)(2,1)}), bf16[8,192,768]{2,1,0:T(8,128)(2,1)S(1)}, u32[]{:S(2)}, u32[]{:S(2)}) async-start(bf16[8,192,768]{2,1,0:T(8,128)(2,1)} %place_rows.1), calls=%async_computation.1 | async-start | bytes 4718592 | tf_op jit(solution)/shard_map/all_to_all | solution.py:425
  57.9 1.2 constant_dynamic-update-slice_fusion.1
  59.1 1.1 constant_dynamic-update-slice_fusion.refs_6_
  60.2 0.6 collective-permute-start.8
  60.8 0.5 collective-permute-start.7
  61.4 0.1 copy.17
  61.6 27.1 %collective-permute-done.8.refs_8_ = bf16[96,6144]{1,0:T(8,128)(2,1)S(1)} collective-permute-done((bf16[96,6144]{1,0:T(8,128)(2,1)S(1)}, bf16[96,6144]{1,0:T(8,128)(2,1)S(1)}, u32[]{:S(2)}, u32[]{:S(2)}) %collective-permute-start.8) | collective-permute-done | bytes 1179680 | tf_op jit(solution)/shard_map/ppermute | solution.py:340
  88.7 1.0 copy-done.7
  89.7 0.6 collective-permute-start.10
  90.3 1.0 copy-done.8
  91.4 0.6 collective-permute-start.9
  92.0 1.7 %pad_maximum_fusion.refs_0_ = bf16[192,6144]{1,0:T(8,128)(2,1)} fusion(bf16[192,1536]{1,0:T(8,128)(2,1)S(1)} %bitcast.29, bf16[192,384]{1,0:T(8,128)(2,1)S(1)} %bitcast.32, bf16[192,3072]{1,0:T(8,128)(2,1)S(1)} %bitcast.24, bf16[192,1152]{1,0:T(8,128)(2,1)S(1)} %bitcast.26), kind=kLoop, calls=%fused_computation | loop fusion | flops 9437184 | bytes 4718592 | tf_op jit(solution)/shard_map/concatenate | solution.py:329
  93.7 11.1 %collective-permute-done.10.refs_10_ = bf16[96,3072]{1,0:T(8,128)(2,1)S(1)} collective-permute-done((bf16[96,3072]{1,0:T(8,128)(2,1)S(1)}, bf16[96,3072]{1,0:T(8,128)(2,1)S(1)}, u32[]{:S(2)}, u32[]{:S(2)}) %collective-permute-start.10) | collective-permute-done | bytes 589856 | tf_op jit(solution)/shard_map/ppermute | solution.py:343
  104.7 0.8 copy-done.16
  105.6 0.7 collective-permute-done.9.refs_9_
  106.2 6.3 %all-to-all-done.1.got_ref = bf16[8,192,768]{2,1,0:T(8,128)(2,1)S(1)} async-done(((bf16[8,192,768]{2,1,0:T(8,128)(2,1)}), bf16[8,192,768]{2,1,0:T(8,128)(2,1)S(1)}, u32[]{:S(2)}, u32[]{:S(2)}) %all-to-all-start.1) | async-done | bytes 2359328 | tf_op jit(solution)/shard_map/all_to_all | solution.py:425
  112.5 2.0 %pool_rows.1 = (bf16[256,768]{1,0:T(8,128)(2,1)S(1)}, bf16[256,768]{1,0:T(8,128)(2,1)S(1)}) custom-call(s32[1]{0:T(128)} %bitcast.slot_ref, bf16[8,768]{1,0:T(8,128)(2,1)S(1)} %get-tuple-element.35.embed_ref, s32[8,1,192]{2,1,0:T(1,128)S(1)} %all-to-all-done.code_ref, bf16[8,192,768]{2,1,0:T(8,128)(2,1)S(1)} %all-to-all-done.1.got_ref), custom_call_target="tpu_custom_call" | custom-call | flops 1207959552 | bytes 2359296 | tf_op jit(solution)/shard_map/pool_rows/pallas_call | solution.py:138
  114.6 0.7 copy-done.5
  115.4 0.5 collective-permute-start.11
  115.9 7.6 %put_rows.1 = (bf16[768,1536]{1,0:T(8,128)(2,1)}, bf16[768,3072]{1,0:T(8,128)(2,1)}, bf16[768,1536]{1,0:T(8,128)(2,1)}) custom-call(bf16[192,6144]{1,0:T(8,128)(2,1)} %pad_maximum_fusion.refs_0_, bf16[48,6144]{1,0:T(8,128)(2,1)} %copy-done.15, bf16[48,6144]{1,0:T(8,128)(2,1)} %copy-done.12, bf16[48,6144]{1,0:T(8,128)(2,1)} %copy-done.11, ...), custom_call_target="tpu_custom_call" | custom-call | bytes 18874368 | tf_op jit(solution)/shard_map/put_rows/pallas_call | solution.py:248
  123.6 2.5 %collective-permute-done.11.got_ref = bf16[256,768]{1,0:T(8,128)(2,1)S(1)} collective-permute-done((bf16[256,768]{1,0:T(8,128)(2,1)S(1)}, bf16[256,768]{1,0:T(8,128)(2,1)S(1)}, u32[]{:S(2)}, u32[]{:S(2)}) %collective-permute-start.11) | collective-permute-done | bytes 393248 | tf_op jit(solution)/shard_map/ppermute | solution.py:428
  126.0 1.5 weave_steps.1.tok_ref
  127.5 0.1 collective-permute-start.12
  127.6 2.3 %collective-permute-done.12.tok_ref = bf16[512,768]{1,0:T(8,128)(2,1)S(1)} collective-permute-done((bf16[512,768]{1,0:T(8,128)(2,1)S(1)}, bf16[512,768]{1,0:T(8,128)(2,1)S(1)}, u32[]{:S(2)}, u32[]{:S(2)}) %collective-permute-start.12) | collective-permute-done | bytes 786464 | tf_op jit(solution)/shard_map/ppermute | solution.py:446
  129.9 7.2 %layer.3 = bf16[512,768]{1,0:T(8,128)(2,1)S(1)} custom-call(bf16[512,768]{1,0:T(8,128)(2,1)S(1)} %collective-permute-done.12.tok_ref, bf16[768,1536]{1,0:T(8,128)(2,1)S(1)} %copy-done.1, bf16[768,3072]{1,0:T(8,128)(2,1)S(1)} %copy-done, bf16[768,1536]{1,0:T(8,128)(2,1)S(1)} %copy-done.2), custom_call_target="tpu_custom_call" | custom-call | flops 4831838208 | bytes 11796480 | tf_op jit(solution)/shard_map/layer/pallas_call | solution.py:285
  137.1 0.2 collective-permute-start.13
  137.3 7.2 %layer.2.sum_ref = f32[512,768]{1,0:T(8,128)S(1)} custom-call(bf16[512,768]{1,0:T(8,128)(2,1)S(1)} %weave_steps.1.tok_ref, bf16[768,1536]{1,0:T(8,128)(2,1)S(1)} %copy-done.1, bf16[768,3072]{1,0:T(8,128)(2,1)S(1)} %copy-done, bf16[768,1536]{1,0:T(8,128)(2,1)S(1)} %copy-done.2), custom_call_target="tpu_custom_call" | custom-call | flops 4831838208 | bytes 11796480 | tf_op jit(solution)/shard_map/layer/pallas_call | solution.py:285
  144.5 1.8 %finish.1 = bf16[512,768]{1,0:T(8,128)(2,1)} custom-call(bf16[512,768]{1,0:T(8,128)(2,1)S(1)} %weave_steps.1.tok_ref, f32[512,768]{1,0:T(8,128)S(1)} %layer.2.sum_ref, bf16[512,768]{1,0:T(8,128)(2,1)S(1)} %collective-permute-done.13.got_ref, s32[1,768]{1,0:T(1,128)S(1)} %compare_select_fusion.6.order_ref), custom_call_target="tpu_custom_call" | custom-call | flops 603979776 | bytes 3932160 | tf_op jit(solution)/shard_map/finish/pallas_call | solution.py:314
  (50 shorter events, 0.3 us)
Async XLA Ops:
  0.0 8.4 %copy-start.18 = (s32[512]{0:T(512)S(1)}, s32[512]{0:T(512)}, u32[]{:S(2)}) copy-start(s32[512]{0:T(512)} %param.11) | copy-start | bytes 6148
  0.0 8.5 %copy-start.19 = (s32[512]{0:T(512)S(1)}, s32[512]{0:T(512)}, u32[]{:S(2)}) copy-start(s32[512]{0:T(512)} %param.10) | copy-start | bytes 6148
  0.8 7.7 %copy-start.4 = (bf16[8,768]{1,0:T(8,128)(2,1)S(1)}, bf16[8,768]{1,0:T(8,128)(2,1)}, u32[]{:S(2)}) copy-start(bf16[8,768]{1,0:T(8,128)(2,1)} %time_ref.1) | copy-start | bytes 36868
  3.9 41.7 %copy-start.3 = (bf16[512,768]{1,0:T(8,128)(2,1)S(1)}, bf16[512,768]{1,0:T(8,128)(2,1)}, u32[]{:S(2)}) copy-start(bf16[512,768]{1,0:T(8,128)(2,1)} %feat_ref.1) | copy-start | bytes 2359300
  4.8 18.6 %collective-permute-start = (bf16[48,6144]{1,0:T(8,128)(2,1)}, bf16[48,6144]{1,0:T(8,128)(2,1)S(1)}, u32[]{:S(2)}, u32[]{:S(2)}) collective-permute-start(bf16[48,6144]{1,0:T(8,128)(2,1)} %pad_maximum_fusion.1), channel_id=1, source_target_pairs={{0,4},{4,8},{8,12},{12,0},{1,5},{5,9},{9,13},{13,1},{2,6},{6,10},{... | collective-permute-start | bytes 1769480 | tf_op jit(solution)/shard_map/ppermute | solution.py:334
  23.4 29.9 %copy-start.15 = (bf16[48,6144]{1,0:T(8,128)(2,1)}, bf16[48,6144]{1,0:T(8,128)(2,1)S(1)}, u32[]{:S(2)}) copy-start(bf16[48,6144]{1,0:T(8,128)(2,1)S(1)} %collective-permute-done.refs_1_) | copy-start | bytes 1769476
  23.4 14.5 %collective-permute-start.4 = (bf16[48,6144]{1,0:T(8,128)(2,1)S(1)}, bf16[48,6144]{1,0:T(8,128)(2,1)S(1)}, u32[]{:S(2)}, u32[]{:S(2)}) collective-permute-start(bf16[48,6144]{1,0:T(8,128)(2,1)S(1)} %collective-permute-done.refs_1_), channel_id=1, source_target_pairs={{0,16},{16,0},{1,17},{17,1},{2,18},{18,2},{3,19},{19,3},{4,20},{20... | collective-permute-start | bytes 1769480 | tf_op jit(solution)/shard_map/ppermute | solution.py:340
  24.9 14.3 %collective-permute-start.3 = (bf16[48,6144]{1,0:T(8,128)(2,1)S(1)}, bf16[48,6144]{1,0:T(8,128)(2,1)S(1)}, u32[]{:S(2)}, u32[]{:S(2)}) collective-permute-start(bf16[48,6144]{1,0:T(8,128)(2,1)S(1)} %collective-permute-done.refs_1_), channel_id=1, source_target_pairs={{0,2},{2,0},{1,3},{3,1},{4,6},{6,4},{5,7},{7,5},{8,10},{10,8},{9,1... | collective-permute-start | bytes 1769480 | tf_op jit(solution)/shard_map/ppermute | solution.py:339
  26.4 26.9 %collective-permute-start.1 = (bf16[48,6144]{1,0:T(8,128)(2,1)}, bf16[48,6144]{1,0:T(8,128)(2,1)}, u32[]{:S(2)}, u32[]{:S(2)}) collective-permute-start(bf16[48,6144]{1,0:T(8,128)(2,1)} %pad_maximum_fusion.1), channel_id=1, source_target_pairs={{0,12},{4,0},{8,4},{12,8},{1,13},{5,1},{9,5},{13,9},{2,14},{6,2},{... | collective-permute-start | bytes 1769480 | tf_op jit(solution)/shard_map/ppermute | solution.py:334
  28.1 25.2 %collective-permute-start.2 = (bf16[48,6144]{1,0:T(8,128)(2,1)S(1)}, bf16[48,6144]{1,0:T(8,128)(2,1)}, u32[]{:S(2)}, u32[]{:S(2)}) collective-permute-start(bf16[48,6144]{1,0:T(8,128)(2,1)S(1)} %collective-permute-done.refs_1_), channel_id=1, source_target_pairs={{0,4},{4,8},{8,12},{12,0},{1,5},{5,9},{9,13},{13,1},{2,6},{6,10},{... | collective-permute-start | bytes 1769480 | tf_op jit(solution)/shard_map/ppermute | solution.py:334
  37.9 10.8 %copy-start.11 = (bf16[48,6144]{1,0:T(8,128)(2,1)}, bf16[48,6144]{1,0:T(8,128)(2,1)S(1)}, u32[]{:S(2)}) copy-start(bf16[48,6144]{1,0:T(8,128)(2,1)S(1)} %collective-permute-done.4.refs_3_) | copy-start | bytes 1769476
  37.9 15.4 %collective-permute-start.6 = (bf16[48,3072]{1,0:T(8,128)(2,1)S(1)}, bf16[48,3072]{1,0:T(8,128)(2,1)S(1)}, u32[]{:S(2)}, u32[]{:S(2)}) collective-permute-start(bf16[48,3072]{1,0:T(8,128)(2,1)S(1)} %slice.17), channel_id=1, source_target_pairs={{0,2},{2,0},{1,3},{3,1},{4,6},{6,4},{5,7},{7,5},{8,10},{10,8},{9,1... | collective-permute-start | bytes 884744 | tf_op jit(solution)/shard_map/ppermute | solution.py:343
  39.2 0.8 copy-start.12
  40.8 12.5 %collective-permute-start.5 = (bf16[48,3072]{1,0:T(8,128)(2,1)}, bf16[48,3072]{1,0:T(8,128)(2,1)S(1)}, u32[]{:S(2)}, u32[]{:S(2)}) collective-permute-start(bf16[48,3072]{1,0:T(8,128)(2,1)} %slice.16), channel_id=1, source_target_pairs={{0,16},{16,0},{1,17},{17,1},{2,18},{18,2},{3,19},{19,3},{4,20},{20... | collective-permute-start | bytes 884744 | tf_op jit(solution)/shard_map/ppermute | solution.py:342
  42.3 11.0 %all-to-all-start = ((s32[8,1,192]{2,1,0:T(1,128)}), s32[8,1,192]{2,1,0:T(1,128)S(1)}, u32[]{:S(2)}, u32[]{:S(2)}) async-start(s32[8,1,192]{2,1,0:T(1,128)} %get-tuple-element.37), calls=%async_computation | async-start | bytes 16384 | tf_op jit(solution)/shard_map/all_to_all | solution.py:418
  53.3 59.2 %all-to-all-start.1 = ((bf16[8,192,768]{2,1,0:T(8,128)(2,1)}), bf16[8,192,768]{2,1,0:T(8,128)(2,1)S(1)}, u32[]{:S(2)}, u32[]{:S(2)}) async-start(bf16[8,192,768]{2,1,0:T(8,128)(2,1)} %place_rows.1), calls=%async_computation.1 | async-start | bytes 4718592 | tf_op jit(solution)/shard_map/all_to_all | solution.py:425
  57.9 3.5 %copy-start.14 = (bf16[192,3,384]{2,0,1:T(8,128)(2,1)S(1)}, bf16[192,3,384]{2,0,1:T(8,128)(2,1)}, u32[]{:S(2)}) copy-start(bf16[192,3,384]{2,0,1:T(8,128)(2,1)} %param.14) | copy-start | bytes 1327108
  57.9 3.5 %copy-start.10 = (bf16[192,2,1536]{2,1,0:T(2,128)(2,1)S(1)}, bf16[192,2,1536]{2,1,0:T(2,128)(2,1)}, u32[]{:S(2)}) copy-start(bf16[192,2,1536]{2,1,0:T(2,128)(2,1)} %param.16) | copy-start | bytes 3538948
  60.2 1.3 copy-start.9
  60.2 28.4 %collective-permute-start.8 = (bf16[96,6144]{1,0:T(8,128)(2,1)S(1)}, bf16[96,6144]{1,0:T(8,128)(2,1)S(1)}, u32[]{:S(2)}, u32[]{:S(2)}) collective-permute-start(bf16[96,6144]{1,0:T(8,128)(2,1)S(1)} %constant_dynamic-update-slice_fusion.refs_6_), channel_id=1, source_target_pairs={{0,16},{16,0},{1,17},{17,1},{2,18},{18,2},{3,19},{19,3},{4,20},{20... | collective-permute-start | bytes 3538952 | tf_op jit(solution)/shard_map/ppermute | solution.py:340
  60.8 29.5 %collective-permute-start.7 = (bf16[96,6144]{1,0:T(8,128)(2,1)S(1)}, bf16[96,6144]{1,0:T(8,128)(2,1)S(1)}, u32[]{:S(2)}, u32[]{:S(2)}) collective-permute-start(bf16[96,6144]{1,0:T(8,128)(2,1)S(1)} %constant_dynamic-update-slice_fusion.refs_6_), channel_id=1, source_target_pairs={{0,2},{2,0},{1,3},{3,1},{4,6},{6,4},{5,7},{7,5},{8,10},{10,8},{9,1... | collective-permute-start | bytes 3538952 | tf_op jit(solution)/shard_map/ppermute | solution.py:339
  61.5 30.4 %copy-start.13 = (bf16[1536,192]{0,1:T(8,128)(2,1)S(1)}, bf16[1536,192]{0,1:T(8,128)(2,1)}, u32[]{:S(2)}) copy-start(bf16[1536,192]{0,1:T(8,128)(2,1)} %param.17) | copy-start | bytes 1769476
  61.6 30.4 %copy-start.17 = (bf16[384,192]{0,1:T(8,128)(2,1)S(1)}, bf16[384,192]{0,1:T(8,128)(2,1)}, u32[]{:S(2)}) copy-start(bf16[384,192]{0,1:T(8,128)(2,1)} %param.15) | copy-start | bytes 442372
  88.6 1.0 copy-start.7
  89.7 15.0 %collective-permute-start.10 = (bf16[96,3072]{1,0:T(8,128)(2,1)S(1)}, bf16[96,3072]{1,0:T(8,128)(2,1)S(1)}, u32[]{:S(2)}, u32[]{:S(2)}) collective-permute-start(bf16[96,3072]{1,0:T(8,128)(2,1)S(1)} %slice.19), channel_id=1, source_target_pairs={{0,2},{2,0},{1,3},{3,1},{4,6},{6,4},{5,7},{7,5},{8,10},{10,8},{9,1... | collective-permute-start | bytes 1769480 | tf_op jit(solution)/shard_map/ppermute | solution.py:343
  90.3 1.0 copy-start.8
  91.4 14.8 %collective-permute-start.9 = (bf16[96,3072]{1,0:T(8,128)(2,1)S(1)}, bf16[96,3072]{1,0:T(8,128)(2,1)}, u32[]{:S(2)}, u32[]{:S(2)}) collective-permute-start(bf16[96,3072]{1,0:T(8,128)(2,1)S(1)} %slice.18), channel_id=1, source_target_pairs={{0,16},{16,0},{1,17},{17,1},{2,18},{18,2},{3,19},{19,3},{4,20},{20... | collective-permute-start | bytes 1769480 | tf_op jit(solution)/shard_map/ppermute | solution.py:342
  104.7 0.8 copy-start.16
  114.6 0.8 copy-start.5
  115.4 10.7 %collective-permute-start.11 = (bf16[256,768]{1,0:T(8,128)(2,1)S(1)}, bf16[256,768]{1,0:T(8,128)(2,1)S(1)}, u32[]{:S(2)}, u32[]{:S(2)}) collective-permute-start(bf16[256,768]{1,0:T(8,128)(2,1)S(1)} %get-tuple-element.46), channel_id=1, source_target_pairs={{0,2},{2,0},{1,3},{3,1},{4,6},{6,4},{5,7},{7,5},{8,10},{10,8},{9,1... | collective-permute-start | bytes 1179656 | tf_op jit(solution)/shard_map/ppermute | solution.py:428
  115.9 10.1 %copy-start.6 = (bf16[256,768]{1,0:T(8,128)(2,1)S(1)}, bf16[256,768]{1,0:T(8,128)(2,1)}, u32[]{:S(2)}) copy-start(bf16[256,768]{1,0:T(8,128)(2,1)} %copy-done.5) | copy-start | bytes 1179652
  126.0 3.8 %copy-start = (bf16[768,3072]{1,0:T(8,128)(2,1)S(1)}, bf16[768,3072]{1,0:T(8,128)(2,1)}, u32[]{:S(2)}) copy-start(bf16[768,3072]{1,0:T(8,128)(2,1)} %get-tuple-element.63.gate_up_ref) | copy-start | bytes 14155780
  126.0 3.8 %copy-start.1 = (bf16[768,1536]{1,0:T(8,128)(2,1)S(1)}, bf16[768,1536]{1,0:T(8,128)(2,1)}, u32[]{:S(2)}) copy-start(bf16[768,1536]{1,0:T(8,128)(2,1)} %get-tuple-element.62.heads_ref) | copy-start | bytes 7077892
  126.0 3.8 %copy-start.2 = (bf16[768,1536]{1,0:T(8,128)(2,1)S(1)}, bf16[768,1536]{1,0:T(8,128)(2,1)}, u32[]{:S(2)}) copy-start(bf16[768,1536]{1,0:T(8,128)(2,1)} %get-tuple-element.64.down_ref) | copy-start | bytes 7077892
  127.5 2.4 %collective-permute-start.12 = (bf16[512,768]{1,0:T(8,128)(2,1)S(1)}, bf16[512,768]{1,0:T(8,128)(2,1)S(1)}, u32[]{:S(2)}, u32[]{:S(2)}) collective-permute-start(bf16[512,768]{1,0:T(8,128)(2,1)S(1)} %weave_steps.1.tok_ref), channel_id=1, source_target_pairs={{0,1},{1,0},{2,3},{3,2},{4,5},{5,4},{6,7},{7,6},{8,9},{9,8},{10,11... | collective-permute-start | bytes 2359304 | tf_op jit(solution)/shard_map/ppermute | solution.py:446
  137.1 7.4 %collective-permute-start.13 = (bf16[512,768]{1,0:T(8,128)(2,1)S(1)}, bf16[512,768]{1,0:T(8,128)(2,1)S(1)}, u32[]{:S(2)}, u32[]{:S(2)}) collective-permute-start(bf16[512,768]{1,0:T(8,128)(2,1)S(1)} %layer.3), channel_id=1, source_target_pairs={{0,1},{1,0},{2,3},{3,2},{4,5},{5,4},{6,7},{7,6},{8,9},{9,8},{10,11... | collective-permute-start | bytes 2359304 | tf_op jit(solution)/shard_map/ppermute | solution.py:448

commit v23 on v22

--- a/solution.py
+++ b/solution.py
@@ -13,7 +13,7 @@
 EPS = 1e-06
 
 CODE = 32
-UNIT = 512
+UNIT = 768
 LANES = 128
 MIB = 1024 * 1024
 F32 = jnp.float32

time: 147 us -> 146 us (level)
  no operation moved by 1% of the time
where the time goes in v23:
time: 146 us
  waiting for transfers between devices  77.5 us (53%)
  Pallas kernels  31.2 us (21%)
  starting transfers between devices  21.9 us (15%)
  local copies, waits for them, and re-layouts  11.7 us (8%)
  other arithmetic  2.6 us (2%)
    ppermute x2, waiting for transfers between devices, to_other_places(): by_group = lax.ppermute(shares, 'groups', swap)  36.6 us
    pallas_call x2, Pallas kernels, layer(): pl.pallas_call(layer_kernel, out_shape=jax.ShapeDtypeStruct((rows, width)...  13.9 us
    ppermute x3, waiting for transfers between devices, along_cells(): lax.ppermute(values, 'cells', [(j, (j - distance) % n_cells) for j in ran...  13.5 us
    ppermute x2, waiting for transfers between devices, to_other_places(): right = lax.ppermute(by_group[:, cut:], 'slots', swap)  11.1 us
    pallas_call x1, Pallas kernels, put_rows(): pl.pallas_call(functools.partial(put_rows_kernel, plan), out_shape=[jax.S...  7.61 us
    unnamed x44, local copies, waits for them, and re-layouts  6.83 us
    all_to_all x1, waiting for transfers between devices, on_device(): lax.all_to_all(blocks, ('cells', 'mp'), split_axis=0, concat_axis=0, tile...  6.3 us
    ppermute x3, starting transfers between devices, along_cells(): lax.ppermute(values, 'cells', [(j, (j - distance) % n_cells) for j in ran...  5.05 us
  transfers between devices with their start and end apart: 16, of which 9 were waited for; matrix products, arithmetic and copies ran while one was open for 3% of the time, Pallas kernels for 13%

profile of v23, /device:TPU:0, one launch (start us, length us, event | category | flops | bytes accessed | tf_op | source)
XLA Modules:
  0.0 145.8 jit_solution(7983237145649515896)
XLA Ops:
  0.0 0.8 dynamic-slice_bitcast_fusion.2
  0.8 0.9 dynamic-slice_bitcast_fusion.1
  1.8 0.9 dynamic-slice_bitcast_fusion
  2.7 1.2 constant_dynamic-slice_fusion
  3.9 0.9 pad_maximum_fusion.1
  4.8 3.0 %collective-permute-start = (bf16[48,6144]{1,0:T(8,128)(2,1)}, bf16[48,6144]{1,0:T(8,128)(2,1)S(1)}, u32[]{:S(2)}, u32[]{:S(2)}) collective-permute-start(bf16[48,6144]{1,0:T(8,128)(2,1)} %pad_maximum_fusion.1), channel_id=1, source_target_pairs={{0,4},{4,8},{8,12},{12,0},{1,5},{5,9},{9,13},{13,1},{2,6},{6,10},{... | collective-permute-start | bytes 1769480 | tf_op jit(solution)/shard_map/ppermute | solution.py:334
  8.5 1.3 place_codes.1
  9.8 13.5 %collective-permute-done.refs_1_ = bf16[48,6144]{1,0:T(8,128)(2,1)S(1)} collective-permute-done((bf16[48,6144]{1,0:T(8,128)(2,1)}, bf16[48,6144]{1,0:T(8,128)(2,1)S(1)}, u32[]{:S(2)}, u32[]{:S(2)}) %collective-permute-start) | collective-permute-done | bytes 589856 | tf_op jit(solution)/shard_map/ppermute | solution.py:334
  23.4 1.5 %collective-permute-start.4 = (bf16[48,6144]{1,0:T(8,128)(2,1)S(1)}, bf16[48,6144]{1,0:T(8,128)(2,1)S(1)}, u32[]{:S(2)}, u32[]{:S(2)}) collective-permute-start(bf16[48,6144]{1,0:T(8,128)(2,1)S(1)} %collective-permute-done.refs_1_), channel_id=1, source_target_pairs={{0,16},{16,0},{1,17},{17,1},{2,18},{18,2},{3,19},{19,3},{4,20},{20... | collective-permute-start | bytes 1769480 | tf_op jit(solution)/shard_map/ppermute | solution.py:340
  24.9 1.5 %collective-permute-start.3 = (bf16[48,6144]{1,0:T(8,128)(2,1)S(1)}, bf16[48,6144]{1,0:T(8,128)(2,1)S(1)}, u32[]{:S(2)}, u32[]{:S(2)}) collective-permute-start(bf16[48,6144]{1,0:T(8,128)(2,1)S(1)} %collective-permute-done.refs_1_), channel_id=1, source_target_pairs={{0,2},{2,0},{1,3},{3,1},{4,6},{6,4},{5,7},{7,5},{8,10},{10,8},{9,1... | collective-permute-start | bytes 1769480 | tf_op jit(solution)/shard_map/ppermute | solution.py:339
  26.4 1.7 %collective-permute-start.1 = (bf16[48,6144]{1,0:T(8,128)(2,1)}, bf16[48,6144]{1,0:T(8,128)(2,1)}, u32[]{:S(2)}, u32[]{:S(2)}) collective-permute-start(bf16[48,6144]{1,0:T(8,128)(2,1)} %pad_maximum_fusion.1), channel_id=1, source_target_pairs={{0,12},{4,0},{8,4},{12,8},{1,13},{5,1},{9,5},{13,9},{2,14},{6,2},{... | collective-permute-start | bytes 1769480 | tf_op jit(solution)/shard_map/ppermute | solution.py:334
  28.1 0.3 collective-permute-start.2
  28.4 9.5 %collective-permute-done.4.refs_3_ = bf16[48,6144]{1,0:T(8,128)(2,1)S(1)} collective-permute-done((bf16[48,6144]{1,0:T(8,128)(2,1)S(1)}, bf16[48,6144]{1,0:T(8,128)(2,1)S(1)}, u32[]{:S(2)}, u32[]{:S(2)}) %collective-permute-start.4) | collective-permute-done | bytes 589856 | tf_op jit(solution)/shard_map/ppermute | solution.py:340
  37.9 1.3 collective-permute-start.6
  39.2 0.8 copy-done.12
  40.0 0.7 slice.16
  40.8 1.5 %collective-permute-start.5 = (bf16[48,3072]{1,0:T(8,128)(2,1)}, bf16[48,3072]{1,0:T(8,128)(2,1)S(1)}, u32[]{:S(2)}, u32[]{:S(2)}) collective-permute-start(bf16[48,3072]{1,0:T(8,128)(2,1)} %slice.16), channel_id=1, source_target_pairs={{0,16},{16,0},{1,17},{17,1},{2,18},{18,2},{3,19},{19,3},{4,20},{20... | collective-permute-start | bytes 884744 | tf_op jit(solution)/shard_map/ppermute | solution.py:342
  42.3 3.3 %all-to-all-start = ((s32[8,1,192]{2,1,0:T(1,128)}), s32[8,1,192]{2,1,0:T(1,128)S(1)}, u32[]{:S(2)}, u32[]{:S(2)}) async-start(s32[8,1,192]{2,1,0:T(1,128)} %get-tuple-element.37), calls=%async_computation | async-start | bytes 16384 | tf_op jit(solution)/shard_map/all_to_all | solution.py:418
  45.6 3.0 %place_rows.1 = bf16[8,192,768]{2,1,0:T(8,128)(2,1)} custom-call(s32[1,512]{1,0:T(1,128)S(1)} %bitcast.22, bf16[512,768]{1,0:T(8,128)(2,1)S(1)} %copy-done.3), custom_call_target="tpu_custom_call" | custom-call | flops 1207959552 | bytes 3145728 | tf_op jit(solution)/shard_map/place_rows/pallas_call | solution.py:98
  48.6 4.6 %all-to-all-done.code_ref = s32[8,1,192]{2,1,0:T(1,128)S(1)} async-done(((s32[8,1,192]{2,1,0:T(1,128)}), s32[8,1,192]{2,1,0:T(1,128)S(1)}, u32[]{:S(2)}, u32[]{:S(2)}) %all-to-all-start) | async-done | bytes 6176 | tf_op jit(solution)/shard_map/all_to_all | solution.py:418
  53.3 4.6 %all-to-all-start.1 = ((bf16[8,192,768]{2,1,0:T(8,128)(2,1)}), bf16[8,192,768]{2,1,0:T(8,128)(2,1)S(1)}, u32[]{:S(2)}, u32[]{:S(2)}) async-start(bf16[8,192,768]{2,1,0:T(8,128)(2,1)} %place_rows.1), calls=%async_computation.1 | async-start | bytes 4718592 | tf_op jit(solution)/shard_map/all_to_all | solution.py:425
  57.9 1.2 constant_dynamic-update-slice_fusion.1
  59.1 1.1 constant_dynamic-update-slice_fusion.refs_6_
  60.2 0.6 collective-permute-start.8
  60.8 0.5 collective-permute-start.7
  61.4 0.1 copy.17
  61.6 27.1 %collective-permute-done.8.refs_8_ = bf16[96,6144]{1,0:T(8,128)(2,1)S(1)} collective-permute-done((bf16[96,6144]{1,0:T(8,128)(2,1)S(1)}, bf16[96,6144]{1,0:T(8,128)(2,1)S(1)}, u32[]{:S(2)}, u32[]{:S(2)}) %collective-permute-start.8) | collective-permute-done | bytes 1179680 | tf_op jit(solution)/shard_map/ppermute | solution.py:340
  88.7 1.0 copy-done.7
  89.7 0.6 collective-permute-start.10
  90.3 1.0 copy-done.8
  91.4 0.6 collective-permute-start.9
  92.0 1.7 %pad_maximum_fusion.refs_0_ = bf16[192,6144]{1,0:T(8,128)(2,1)} fusion(bf16[192,1536]{1,0:T(8,128)(2,1)S(1)} %bitcast.29, bf16[192,384]{1,0:T(8,128)(2,1)S(1)} %bitcast.32, bf16[192,3072]{1,0:T(8,128)(2,1)S(1)} %bitcast.24, bf16[192,1152]{1,0:T(8,128)(2,1)S(1)} %bitcast.26), kind=kLoop, calls=%fused_computation | loop fusion | flops 9437184 | bytes 4718592 | tf_op jit(solution)/shard_map/concatenate | solution.py:329
  93.7 11.1 %collective-permute-done.10.refs_10_ = bf16[96,3072]{1,0:T(8,128)(2,1)S(1)} collective-permute-done((bf16[96,3072]{1,0:T(8,128)(2,1)S(1)}, bf16[96,3072]{1,0:T(8,128)(2,1)S(1)}, u32[]{:S(2)}, u32[]{:S(2)}) %collective-permute-start.10) | collective-permute-done | bytes 589856 | tf_op jit(solution)/shard_map/ppermute | solution.py:343
  104.7 0.8 copy-done.16
  105.6 0.7 collective-permute-done.9.refs_9_
  106.2 6.3 %all-to-all-done.1.got_ref = bf16[8,192,768]{2,1,0:T(8,128)(2,1)S(1)} async-done(((bf16[8,192,768]{2,1,0:T(8,128)(2,1)}), bf16[8,192,768]{2,1,0:T(8,128)(2,1)S(1)}, u32[]{:S(2)}, u32[]{:S(2)}) %all-to-all-start.1) | async-done | bytes 2359328 | tf_op jit(solution)/shard_map/all_to_all | solution.py:425
  112.5 2.0 %pool_rows.1 = (bf16[256,768]{1,0:T(8,128)(2,1)S(1)}, bf16[256,768]{1,0:T(8,128)(2,1)S(1)}) custom-call(s32[1]{0:T(128)} %bitcast.slot_ref, bf16[8,768]{1,0:T(8,128)(2,1)S(1)} %get-tuple-element.35.embed_ref, s32[8,1,192]{2,1,0:T(1,128)S(1)} %all-to-all-done.code_ref, bf16[8,192,768]{2,1,0:T(8,128)(2,1)S(1)} %all-to-all-done.1.got_ref), custom_call_target="tpu_custom_call" | custom-call | flops 1207959552 | bytes 2359296 | tf_op jit(solution)/shard_map/pool_rows/pallas_call | solution.py:138
  114.6 0.7 copy-done.5
  115.4 0.5 collective-permute-start.11
  115.9 7.6 %put_rows.1 = (bf16[768,1536]{1,0:T(8,128)(2,1)}, bf16[768,3072]{1,0:T(8,128)(2,1)}, bf16[768,1536]{1,0:T(8,128)(2,1)}) custom-call(bf16[192,6144]{1,0:T(8,128)(2,1)} %pad_maximum_fusion.refs_0_, bf16[48,6144]{1,0:T(8,128)(2,1)} %copy-done.15, bf16[48,6144]{1,0:T(8,128)(2,1)} %copy-done.12, bf16[48,6144]{1,0:T(8,128)(2,1)} %copy-done.11, ...), custom_call_target="tpu_custom_call" | custom-call | bytes 18874368 | tf_op jit(solution)/shard_map/put_rows/pallas_call | solution.py:248
  123.6 2.5 %collective-permute-done.11.got_ref = bf16[256,768]{1,0:T(8,128)(2,1)S(1)} collective-permute-done((bf16[256,768]{1,0:T(8,128)(2,1)S(1)}, bf16[256,768]{1,0:T(8,128)(2,1)S(1)}, u32[]{:S(2)}, u32[]{:S(2)}) %collective-permute-start.11) | collective-permute-done | bytes 393248 | tf_op jit(solution)/shard_map/ppermute | solution.py:428
  126.0 1.5 weave_steps.1.tok_ref
  127.5 0.1 collective-permute-start.12
  127.6 2.3 %collective-permute-done.12.tok_ref = bf16[512,768]{1,0:T(8,128)(2,1)S(1)} collective-permute-done((bf16[512,768]{1,0:T(8,128)(2,1)S(1)}, bf16[512,768]{1,0:T(8,128)(2,1)S(1)}, u32[]{:S(2)}, u32[]{:S(2)}) %collective-permute-start.12) | collective-permute-done | bytes 786464 | tf_op jit(solution)/shard_map/ppermute | solution.py:446
  129.9 7.0 %layer.3 = bf16[512,768]{1,0:T(8,128)(2,1)S(1)} custom-call(bf16[512,768]{1,0:T(8,128)(2,1)S(1)} %collective-permute-done.12.tok_ref, bf16[768,1536]{1,0:T(8,128)(2,1)S(1)} %copy-done.1, bf16[768,3072]{1,0:T(8,128)(2,1)S(1)} %copy-done, bf16[768,1536]{1,0:T(8,128)(2,1)S(1)} %copy-done.2), custom_call_target="tpu_custom_call" | custom-call | flops 4831838208 | bytes 11796480 | tf_op jit(solution)/shard_map/layer/pallas_call | solution.py:285
  136.8 0.2 collective-permute-start.13
  137.0 7.0 %layer.2.sum_ref = f32[512,768]{1,0:T(8,128)S(1)} custom-call(bf16[512,768]{1,0:T(8,128)(2,1)S(1)} %weave_steps.1.tok_ref, bf16[768,1536]{1,0:T(8,128)(2,1)S(1)} %copy-done.1, bf16[768,3072]{1,0:T(8,128)(2,1)S(1)} %copy-done, bf16[768,1536]{1,0:T(8,128)(2,1)S(1)} %copy-done.2), custom_call_target="tpu_custom_call" | custom-call | flops 4831838208 | bytes 11796480 | tf_op jit(solution)/shard_map/layer/pallas_call | solution.py:285
  144.0 1.8 %finish.1 = bf16[512,768]{1,0:T(8,128)(2,1)} custom-call(bf16[512,768]{1,0:T(8,128)(2,1)S(1)} %weave_steps.1.tok_ref, f32[512,768]{1,0:T(8,128)S(1)} %layer.2.sum_ref, bf16[512,768]{1,0:T(8,128)(2,1)S(1)} %collective-permute-done.13.got_ref, s32[1,768]{1,0:T(1,128)S(1)} %compare_select_fusion.6.order_ref), custom_call_target="tpu_custom_call" | custom-call | flops 603979776 | bytes 3932160 | tf_op jit(solution)/shard_map/finish/pallas_call | solution.py:314
  (50 shorter events, 0.3 us)
Async XLA Ops:
  0.0 8.4 %copy-start.18 = (s32[512]{0:T(512)S(1)}, s32[512]{0:T(512)}, u32[]{:S(2)}) copy-start(s32[512]{0:T(512)} %param.11) | copy-start | bytes 6148
  0.0 8.5 %copy-start.19 = (s32[512]{0:T(512)S(1)}, s32[512]{0:T(512)}, u32[]{:S(2)}) copy-start(s32[512]{0:T(512)} %param.10) | copy-start | bytes 6148
  0.8 7.7 %copy-start.4 = (bf16[8,768]{1,0:T(8,128)(2,1)S(1)}, bf16[8,768]{1,0:T(8,128)(2,1)}, u32[]{:S(2)}) copy-start(bf16[8,768]{1,0:T(8,128)(2,1)} %time_ref.1) | copy-start | bytes 36868
  3.9 41.7 %copy-start.3 = (bf16[512,768]{1,0:T(8,128)(2,1)S(1)}, bf16[512,768]{1,0:T(8,128)(2,1)}, u32[]{:S(2)}) copy-start(bf16[512,768]{1,0:T(8,128)(2,1)} %feat_ref.1) | copy-start | bytes 2359300
  4.8 18.6 %collective-permute-start = (bf16[48,6144]{1,0:T(8,128)(2,1)}, bf16[48,6144]{1,0:T(8,128)(2,1)S(1)}, u32[]{:S(2)}, u32[]{:S(2)}) collective-permute-start(bf16[48,6144]{1,0:T(8,128)(2,1)} %pad_maximum_fusion.1), channel_id=1, source_target_pairs={{0,4},{4,8},{8,12},{12,0},{1,5},{5,9},{9,13},{13,1},{2,6},{6,10},{... | collective-permute-start | bytes 1769480 | tf_op jit(solution)/shard_map/ppermute | solution.py:334
  23.4 29.9 %copy-start.15 = (bf16[48,6144]{1,0:T(8,128)(2,1)}, bf16[48,6144]{1,0:T(8,128)(2,1)S(1)}, u32[]{:S(2)}) copy-start(bf16[48,6144]{1,0:T(8,128)(2,1)S(1)} %collective-permute-done.refs_1_) | copy-start | bytes 1769476
  23.4 14.5 %collective-permute-start.4 = (bf16[48,6144]{1,0:T(8,128)(2,1)S(1)}, bf16[48,6144]{1,0:T(8,128)(2,1)S(1)}, u32[]{:S(2)}, u32[]{:S(2)}) collective-permute-start(bf16[48,6144]{1,0:T(8,128)(2,1)S(1)} %collective-permute-done.refs_1_), channel_id=1, source_target_pairs={{0,16},{16,0},{1,17},{17,1},{2,18},{18,2},{3,19},{19,3},{4,20},{20... | collective-permute-start | bytes 1769480 | tf_op jit(solution)/shard_map/ppermute | solution.py:340
  24.9 14.3 %collective-permute-start.3 = (bf16[48,6144]{1,0:T(8,128)(2,1)S(1)}, bf16[48,6144]{1,0:T(8,128)(2,1)S(1)}, u32[]{:S(2)}, u32[]{:S(2)}) collective-permute-start(bf16[48,6144]{1,0:T(8,128)(2,1)S(1)} %collective-permute-done.refs_1_), channel_id=1, source_target_pairs={{0,2},{2,0},{1,3},{3,1},{4,6},{6,4},{5,7},{7,5},{8,10},{10,8},{9,1... | collective-permute-start | bytes 1769480 | tf_op jit(solution)/shard_map/ppermute | solution.py:339
  26.4 26.9 %collective-permute-start.1 = (bf16[48,6144]{1,0:T(8,128)(2,1)}, bf16[48,6144]{1,0:T(8,128)(2,1)}, u32[]{:S(2)}, u32[]{:S(2)}) collective-permute-start(bf16[48,6144]{1,0:T(8,128)(2,1)} %pad_maximum_fusion.1), channel_id=1, source_target_pairs={{0,12},{4,0},{8,4},{12,8},{1,13},{5,1},{9,5},{13,9},{2,14},{6,2},{... | collective-permute-start | bytes 1769480 | tf_op jit(solution)/shard_map/ppermute | solution.py:334
  28.1 25.2 %collective-permute-start.2 = (bf16[48,6144]{1,0:T(8,128)(2,1)S(1)}, bf16[48,6144]{1,0:T(8,128)(2,1)}, u32[]{:S(2)}, u32[]{:S(2)}) collective-permute-start(bf16[48,6144]{1,0:T(8,128)(2,1)S(1)} %collective-permute-done.refs_1_), channel_id=1, source_target_pairs={{0,4},{4,8},{8,12},{12,0},{1,5},{5,9},{9,13},{13,1},{2,6},{6,10},{... | collective-permute-start | bytes 1769480 | tf_op jit(solution)/shard_map/ppermute | solution.py:334
  37.9 10.8 %copy-start.11 = (bf16[48,6144]{1,0:T(8,128)(2,1)}, bf16[48,6144]{1,0:T(8,128)(2,1)S(1)}, u32[]{:S(2)}) copy-start(bf16[48,6144]{1,0:T(8,128)(2,1)S(1)} %collective-permute-done.4.refs_3_) | copy-start | bytes 1769476
  37.9 15.4 %collective-permute-start.6 = (bf16[48,3072]{1,0:T(8,128)(2,1)S(1)}, bf16[48,3072]{1,0:T(8,128)(2,1)S(1)}, u32[]{:S(2)}, u32[]{:S(2)}) collective-permute-start(bf16[48,3072]{1,0:T(8,128)(2,1)S(1)} %slice.17), channel_id=1, source_target_pairs={{0,2},{2,0},{1,3},{3,1},{4,6},{6,4},{5,7},{7,5},{8,10},{10,8},{9,1... | collective-permute-start | bytes 884744 | tf_op jit(solution)/shard_map/ppermute | solution.py:343
  39.2 0.8 copy-start.12
  40.8 12.5 %collective-permute-start.5 = (bf16[48,3072]{1,0:T(8,128)(2,1)}, bf16[48,3072]{1,0:T(8,128)(2,1)S(1)}, u32[]{:S(2)}, u32[]{:S(2)}) collective-permute-start(bf16[48,3072]{1,0:T(8,128)(2,1)} %slice.16), channel_id=1, source_target_pairs={{0,16},{16,0},{1,17},{17,1},{2,18},{18,2},{3,19},{19,3},{4,20},{20... | collective-permute-start | bytes 884744 | tf_op jit(solution)/shard_map/ppermute | solution.py:342
  42.3 11.0 %all-to-all-start = ((s32[8,1,192]{2,1,0:T(1,128)}), s32[8,1,192]{2,1,0:T(1,128)S(1)}, u32[]{:S(2)}, u32[]{:S(2)}) async-start(s32[8,1,192]{2,1,0:T(1,128)} %get-tuple-element.37), calls=%async_computation | async-start | bytes 16384 | tf_op jit(solution)/shard_map/all_to_all | solution.py:418
  53.3 59.2 %all-to-all-start.1 = ((bf16[8,192,768]{2,1,0:T(8,128)(2,1)}), bf16[8,192,768]{2,1,0:T(8,128)(2,1)S(1)}, u32[]{:S(2)}, u32[]{:S(2)}) async-start(bf16[8,192,768]{2,1,0:T(8,128)(2,1)} %place_rows.1), calls=%async_computation.1 | async-start | bytes 4718592 | tf_op jit(solution)/shard_map/all_to_all | solution.py:425
  57.9 3.5 %copy-start.14 = (bf16[192,3,384]{2,0,1:T(8,128)(2,1)S(1)}, bf16[192,3,384]{2,0,1:T(8,128)(2,1)}, u32[]{:S(2)}) copy-start(bf16[192,3,384]{2,0,1:T(8,128)(2,1)} %param.14) | copy-start | bytes 1327108
  57.9 3.5 %copy-start.10 = (bf16[192,2,1536]{2,1,0:T(2,128)(2,1)S(1)}, bf16[192,2,1536]{2,1,0:T(2,128)(2,1)}, u32[]{:S(2)}) copy-start(bf16[192,2,1536]{2,1,0:T(2,128)(2,1)} %param.16) | copy-start | bytes 3538948
  60.2 1.3 copy-start.9
  60.2 28.4 %collective-permute-start.8 = (bf16[96,6144]{1,0:T(8,128)(2,1)S(1)}, bf16[96,6144]{1,0:T(8,128)(2,1)S(1)}, u32[]{:S(2)}, u32[]{:S(2)}) collective-permute-start(bf16[96,6144]{1,0:T(8,128)(2,1)S(1)} %constant_dynamic-update-slice_fusion.refs_6_), channel_id=1, source_target_pairs={{0,16},{16,0},{1,17},{17,1},{2,18},{18,2},{3,19},{19,3},{4,20},{20... | collective-permute-start | bytes 3538952 | tf_op jit(solution)/shard_map/ppermute | solution.py:340
  60.8 29.5 %collective-permute-start.7 = (bf16[96,6144]{1,0:T(8,128)(2,1)S(1)}, bf16[96,6144]{1,0:T(8,128)(2,1)S(1)}, u32[]{:S(2)}, u32[]{:S(2)}) collective-permute-start(bf16[96,6144]{1,0:T(8,128)(2,1)S(1)} %constant_dynamic-update-slice_fusion.refs_6_), channel_id=1, source_target_pairs={{0,2},{2,0},{1,3},{3,1},{4,6},{6,4},{5,7},{7,5},{8,10},{10,8},{9,1... | collective-permute-start | bytes 3538952 | tf_op jit(solution)/shard_map/ppermute | solution.py:339
  61.5 30.4 %copy-start.13 = (bf16[1536,192]{0,1:T(8,128)(2,1)S(1)}, bf16[1536,192]{0,1:T(8,128)(2,1)}, u32[]{:S(2)}) copy-start(bf16[1536,192]{0,1:T(8,128)(2,1)} %param.17) | copy-start | bytes 1769476
  61.6 30.4 %copy-start.17 = (bf16[384,192]{0,1:T(8,128)(2,1)S(1)}, bf16[384,192]{0,1:T(8,128)(2,1)}, u32[]{:S(2)}) copy-start(bf16[384,192]{0,1:T(8,128)(2,1)} %param.15) | copy-start | bytes 442372
  88.6 1.0 copy-start.7
  89.7 15.0 %collective-permute-start.10 = (bf16[96,3072]{1,0:T(8,128)(2,1)S(1)}, bf16[96,3072]{1,0:T(8,128)(2,1)S(1)}, u32[]{:S(2)}, u32[]{:S(2)}) collective-permute-start(bf16[96,3072]{1,0:T(8,128)(2,1)S(1)} %slice.19), channel_id=1, source_target_pairs={{0,2},{2,0},{1,3},{3,1},{4,6},{6,4},{5,7},{7,5},{8,10},{10,8},{9,1... | collective-permute-start | bytes 1769480 | tf_op jit(solution)/shard_map/ppermute | solution.py:343
  90.3 1.0 copy-start.8
  91.4 14.8 %collective-permute-start.9 = (bf16[96,3072]{1,0:T(8,128)(2,1)S(1)}, bf16[96,3072]{1,0:T(8,128)(2,1)}, u32[]{:S(2)}, u32[]{:S(2)}) collective-permute-start(bf16[96,3072]{1,0:T(8,128)(2,1)S(1)} %slice.18), channel_id=1, source_target_pairs={{0,16},{16,0},{1,17},{17,1},{2,18},{18,2},{3,19},{19,3},{4,20},{20... | collective-permute-start | bytes 1769480 | tf_op jit(solution)/shard_map/ppermute | solution.py:342
  104.7 0.8 copy-start.16
  114.6 0.8 copy-start.5
  115.4 10.7 %collective-permute-start.11 = (bf16[256,768]{1,0:T(8,128)(2,1)S(1)}, bf16[256,768]{1,0:T(8,128)(2,1)S(1)}, u32[]{:S(2)}, u32[]{:S(2)}) collective-permute-start(bf16[256,768]{1,0:T(8,128)(2,1)S(1)} %get-tuple-element.46), channel_id=1, source_target_pairs={{0,2},{2,0},{1,3},{3,1},{4,6},{6,4},{5,7},{7,5},{8,10},{10,8},{9,1... | collective-permute-start | bytes 1179656 | tf_op jit(solution)/shard_map/ppermute | solution.py:428
  115.9 10.1 %copy-start.6 = (bf16[256,768]{1,0:T(8,128)(2,1)S(1)}, bf16[256,768]{1,0:T(8,128)(2,1)}, u32[]{:S(2)}) copy-start(bf16[256,768]{1,0:T(8,128)(2,1)} %copy-done.5) | copy-start | bytes 1179652
  126.0 3.8 %copy-start = (bf16[768,3072]{1,0:T(8,128)(2,1)S(1)}, bf16[768,3072]{1,0:T(8,128)(2,1)}, u32[]{:S(2)}) copy-start(bf16[768,3072]{1,0:T(8,128)(2,1)} %get-tuple-element.63.gate_up_ref) | copy-start | bytes 14155780
  126.0 3.8 %copy-start.1 = (bf16[768,1536]{1,0:T(8,128)(2,1)S(1)}, bf16[768,1536]{1,0:T(8,128)(2,1)}, u32[]{:S(2)}) copy-start(bf16[768,1536]{1,0:T(8,128)(2,1)} %get-tuple-element.62.heads_ref) | copy-start | bytes 7077892
  126.0 3.8 %copy-start.2 = (bf16[768,1536]{1,0:T(8,128)(2,1)S(1)}, bf16[768,1536]{1,0:T(8,128)(2,1)}, u32[]{:S(2)}) copy-start(bf16[768,1536]{1,0:T(8,128)(2,1)} %get-tuple-element.64.down_ref) | copy-start | bytes 7077892
  127.5 2.4 %collective-permute-start.12 = (bf16[512,768]{1,0:T(8,128)(2,1)S(1)}, bf16[512,768]{1,0:T(8,128)(2,1)S(1)}, u32[]{:S(2)}, u32[]{:S(2)}) collective-permute-start(bf16[512,768]{1,0:T(8,128)(2,1)S(1)} %weave_steps.1.tok_ref), channel_id=1, source_target_pairs={{0,1},{1,0},{2,3},{3,2},{4,5},{5,4},{6,7},{7,6},{8,9},{9,8},{10,11... | collective-permute-start | bytes 2359304 | tf_op jit(solution)/shard_map/ppermute | solution.py:446
  136.8 7.2 %collective-permute-start.13 = (bf16[512,768]{1,0:T(8,128)(2,1)S(1)}, bf16[512,768]{1,0:T(8,128)(2,1)S(1)}, u32[]{:S(2)}, u32[]{:S(2)}) collective-permute-start(bf16[512,768]{1,0:T(8,128)(2,1)S(1)} %layer.3), channel_id=1, source_target_pairs={{0,1},{1,0},{2,3},{3,2},{4,5},{5,4},{6,7},{7,6},{8,9},{9,8},{10,11... | collective-permute-start | bytes 2359304 | tf_op jit(solution)/shard_map/ppermute | solution.py:448

commit v24 on v23

--- a/solution.py
+++ b/solution.py
@@ -13,7 +13,7 @@
 EPS = 1e-06
 
 CODE = 32
-UNIT = 768
+UNIT = 1536
 LANES = 128
 MIB = 1024 * 1024
 F32 = jnp.float32

time: 146 us -> 148 us (1.014)
  Pallas kernels: 31.2 us -> 33 us
    pallas_call x2, Pallas kernels: 13.9 us -> 15.8 us  [layer(): pl.pallas_call(layer_kernel, out_shape=jax.ShapeDtypeStruct((rows, width)...]
  transfers between devices with their start and end apart: 16 -> 16, of which waited for: 9 -> 9; matrix products, arithmetic and copies ran while one was open for 3% -> 3% of each run, Pallas kernels for 13% -> 14%
where the time goes in v24:
time: 148 us
  waiting for transfers between devices  77.5 us (52%)
  Pallas kernels  33 us (22%)
  starting transfers between devices  21.8 us (15%)
  local copies, waits for them, and re-layouts  11.7 us (8%)
  other arithmetic  2.6 us (2%)
    ppermute x2, waiting for transfers between devices, to_other_places(): by_group = lax.ppermute(shares, 'groups', swap)  36.6 us
    pallas_call x2, Pallas kernels, layer(): pl.pallas_call(layer_kernel, out_shape=jax.ShapeDtypeStruct((rows, width)...  15.8 us
    ppermute x3, waiting for transfers between devices, along_cells(): lax.ppermute(values, 'cells', [(j, (j - distance) % n_cells) for j in ran...  13.5 us
    ppermute x2, waiting for transfers between devices, to_other_places(): right = lax.ppermute(by_group[:, cut:], 'slots', swap)  11.1 us
    pallas_call x1, Pallas kernels, put_rows(): pl.pallas_call(functools.partial(put_rows_kernel, plan), out_shape=[jax.S...  7.61 us
    unnamed x44, local copies, waits for them, and re-layouts  6.83 us
    all_to_all x1, waiting for transfers between devices, on_device(): lax.all_to_all(blocks, ('cells', 'mp'), split_axis=0, concat_axis=0, tile...  6.3 us
    ppermute x3, starting transfers between devices, along_cells(): lax.ppermute(values, 'cells', [(j, (j - distance) % n_cells) for j in ran...  5.05 us
  transfers between devices with their start and end apart: 16, of which 9 were waited for; matrix products, arithmetic and copies ran while one was open for 3% of the time, Pallas kernels for 14%

profile of v24, /device:TPU:0, one launch (start us, length us, event | category | flops | bytes accessed | tf_op | source)
XLA Modules:
  0.0 147.6 jit_solution(972990079876206989)
XLA Ops:
  0.0 0.8 dynamic-slice_bitcast_fusion.2
  0.8 0.9 dynamic-slice_bitcast_fusion.1
  1.8 0.9 dynamic-slice_bitcast_fusion
  2.7 1.2 constant_dynamic-slice_fusion
  3.9 0.9 pad_maximum_fusion.1
  4.8 3.0 %collective-permute-start = (bf16[48,6144]{1,0:T(8,128)(2,1)}, bf16[48,6144]{1,0:T(8,128)(2,1)S(1)}, u32[]{:S(2)}, u32[]{:S(2)}) collective-permute-start(bf16[48,6144]{1,0:T(8,128)(2,1)} %pad_maximum_fusion.1), channel_id=1, source_target_pairs={{0,4},{4,8},{8,12},{12,0},{1,5},{5,9},{9,13},{13,1},{2,6},{6,10},{... | collective-permute-start | bytes 1769480 | tf_op jit(solution)/shard_map/ppermute | solution.py:334
  8.5 1.3 place_codes.1
  9.8 13.5 %collective-permute-done.refs_1_ = bf16[48,6144]{1,0:T(8,128)(2,1)S(1)} collective-permute-done((bf16[48,6144]{1,0:T(8,128)(2,1)}, bf16[48,6144]{1,0:T(8,128)(2,1)S(1)}, u32[]{:S(2)}, u32[]{:S(2)}) %collective-permute-start) | collective-permute-done | bytes 589856 | tf_op jit(solution)/shard_map/ppermute | solution.py:334
  23.4 1.5 %collective-permute-start.4 = (bf16[48,6144]{1,0:T(8,128)(2,1)S(1)}, bf16[48,6144]{1,0:T(8,128)(2,1)S(1)}, u32[]{:S(2)}, u32[]{:S(2)}) collective-permute-start(bf16[48,6144]{1,0:T(8,128)(2,1)S(1)} %collective-permute-done.refs_1_), channel_id=1, source_target_pairs={{0,16},{16,0},{1,17},{17,1},{2,18},{18,2},{3,19},{19,3},{4,20},{20... | collective-permute-start | bytes 1769480 | tf_op jit(solution)/shard_map/ppermute | solution.py:340
  24.9 1.5 %collective-permute-start.3 = (bf16[48,6144]{1,0:T(8,128)(2,1)S(1)}, bf16[48,6144]{1,0:T(8,128)(2,1)S(1)}, u32[]{:S(2)}, u32[]{:S(2)}) collective-permute-start(bf16[48,6144]{1,0:T(8,128)(2,1)S(1)} %collective-permute-done.refs_1_), channel_id=1, source_target_pairs={{0,2},{2,0},{1,3},{3,1},{4,6},{6,4},{5,7},{7,5},{8,10},{10,8},{9,1... | collective-permute-start | bytes 1769480 | tf_op jit(solution)/shard_map/ppermute | solution.py:339
  26.4 1.7 %collective-permute-start.1 = (bf16[48,6144]{1,0:T(8,128)(2,1)}, bf16[48,6144]{1,0:T(8,128)(2,1)}, u32[]{:S(2)}, u32[]{:S(2)}) collective-permute-start(bf16[48,6144]{1,0:T(8,128)(2,1)} %pad_maximum_fusion.1), channel_id=1, source_target_pairs={{0,12},{4,0},{8,4},{12,8},{1,13},{5,1},{9,5},{13,9},{2,14},{6,2},{... | collective-permute-start | bytes 1769480 | tf_op jit(solution)/shard_map/ppermute | solution.py:334
  28.1 0.3 collective-permute-start.2
  28.4 9.5 %collective-permute-done.4.refs_3_ = bf16[48,6144]{1,0:T(8,128)(2,1)S(1)} collective-permute-done((bf16[48,6144]{1,0:T(8,128)(2,1)S(1)}, bf16[48,6144]{1,0:T(8,128)(2,1)S(1)}, u32[]{:S(2)}, u32[]{:S(2)}) %collective-permute-start.4) | collective-permute-done | bytes 589856 | tf_op jit(solution)/shard_map/ppermute | solution.py:340
  37.9 1.3 collective-permute-start.6
  39.2 0.8 copy-done.12
  40.0 0.7 slice.16
  40.8 1.5 %collective-permute-start.5 = (bf16[48,3072]{1,0:T(8,128)(2,1)}, bf16[48,3072]{1,0:T(8,128)(2,1)S(1)}, u32[]{:S(2)}, u32[]{:S(2)}) collective-permute-start(bf16[48,3072]{1,0:T(8,128)(2,1)} %slice.16), channel_id=1, source_target_pairs={{0,16},{16,0},{1,17},{17,1},{2,18},{18,2},{3,19},{19,3},{4,20},{20... | collective-permute-start | bytes 884744 | tf_op jit(solution)/shard_map/ppermute | solution.py:342
  42.3 3.3 %all-to-all-start = ((s32[8,1,192]{2,1,0:T(1,128)}), s32[8,1,192]{2,1,0:T(1,128)S(1)}, u32[]{:S(2)}, u32[]{:S(2)}) async-start(s32[8,1,192]{2,1,0:T(1,128)} %get-tuple-element.37), calls=%async_computation | async-start | bytes 16384 | tf_op jit(solution)/shard_map/all_to_all | solution.py:418
  45.6 3.0 %place_rows.1 = bf16[8,192,768]{2,1,0:T(8,128)(2,1)} custom-call(s32[1,512]{1,0:T(1,128)S(1)} %bitcast.22, bf16[512,768]{1,0:T(8,128)(2,1)S(1)} %copy-done.3), custom_call_target="tpu_custom_call" | custom-call | flops 1207959552 | bytes 3145728 | tf_op jit(solution)/shard_map/place_rows/pallas_call | solution.py:98
  48.6 4.6 %all-to-all-done.code_ref = s32[8,1,192]{2,1,0:T(1,128)S(1)} async-done(((s32[8,1,192]{2,1,0:T(1,128)}), s32[8,1,192]{2,1,0:T(1,128)S(1)}, u32[]{:S(2)}, u32[]{:S(2)}) %all-to-all-start) | async-done | bytes 6176 | tf_op jit(solution)/shard_map/all_to_all | solution.py:418
  53.3 4.6 %all-to-all-start.1 = ((bf16[8,192,768]{2,1,0:T(8,128)(2,1)}), bf16[8,192,768]{2,1,0:T(8,128)(2,1)S(1)}, u32[]{:S(2)}, u32[]{:S(2)}) async-start(bf16[8,192,768]{2,1,0:T(8,128)(2,1)} %place_rows.1), calls=%async_computation.1 | async-start | bytes 4718592 | tf_op jit(solution)/shard_map/all_to_all | solution.py:425
  57.9 1.2 constant_dynamic-update-slice_fusion.1
  59.1 1.1 constant_dynamic-update-slice_fusion.refs_6_
  60.2 0.6 collective-permute-start.8
  60.8 0.5 collective-permute-start.7
  61.4 0.1 copy.17
  61.6 27.1 %collective-permute-done.8.refs_8_ = bf16[96,6144]{1,0:T(8,128)(2,1)S(1)} collective-permute-done((bf16[96,6144]{1,0:T(8,128)(2,1)S(1)}, bf16[96,6144]{1,0:T(8,128)(2,1)S(1)}, u32[]{:S(2)}, u32[]{:S(2)}) %collective-permute-start.8) | collective-permute-done | bytes 1179680 | tf_op jit(solution)/shard_map/ppermute | solution.py:340
  88.7 1.0 copy-done.7
  89.7 0.6 collective-permute-start.10
  90.3 1.0 copy-done.8
  91.4 0.6 collective-permute-start.9
  92.0 1.7 %pad_maximum_fusion.refs_0_ = bf16[192,6144]{1,0:T(8,128)(2,1)} fusion(bf16[192,1536]{1,0:T(8,128)(2,1)S(1)} %bitcast.29, bf16[192,384]{1,0:T(8,128)(2,1)S(1)} %bitcast.32, bf16[192,3072]{1,0:T(8,128)(2,1)S(1)} %bitcast.24, bf16[192,1152]{1,0:T(8,128)(2,1)S(1)} %bitcast.26), kind=kLoop, calls=%fused_computation | loop fusion | flops 9437184 | bytes 4718592 | tf_op jit(solution)/shard_map/concatenate | solution.py:329
  93.7 11.1 %collective-permute-done.10.refs_10_ = bf16[96,3072]{1,0:T(8,128)(2,1)S(1)} collective-permute-done((bf16[96,3072]{1,0:T(8,128)(2,1)S(1)}, bf16[96,3072]{1,0:T(8,128)(2,1)S(1)}, u32[]{:S(2)}, u32[]{:S(2)}) %collective-permute-start.10) | collective-permute-done | bytes 589856 | tf_op jit(solution)/shard_map/ppermute | solution.py:343
  104.7 0.8 copy-done.16
  105.6 0.7 collective-permute-done.9.refs_9_
  106.2 6.3 %all-to-all-done.1.got_ref = bf16[8,192,768]{2,1,0:T(8,128)(2,1)S(1)} async-done(((bf16[8,192,768]{2,1,0:T(8,128)(2,1)}), bf16[8,192,768]{2,1,0:T(8,128)(2,1)S(1)}, u32[]{:S(2)}, u32[]{:S(2)}) %all-to-all-start.1) | async-done | bytes 2359328 | tf_op jit(solution)/shard_map/all_to_all | solution.py:425
  112.5 2.0 %pool_rows.1 = (bf16[256,768]{1,0:T(8,128)(2,1)S(1)}, bf16[256,768]{1,0:T(8,128)(2,1)S(1)}) custom-call(s32[1]{0:T(128)} %bitcast.slot_ref, bf16[8,768]{1,0:T(8,128)(2,1)S(1)} %get-tuple-element.35.embed_ref, s32[8,1,192]{2,1,0:T(1,128)S(1)} %all-to-all-done.code_ref, bf16[8,192,768]{2,1,0:T(8,128)(2,1)S(1)} %all-to-all-done.1.got_ref), custom_call_target="tpu_custom_call" | custom-call | flops 1207959552 | bytes 2359296 | tf_op jit(solution)/shard_map/pool_rows/pallas_call | solution.py:138
  114.6 0.7 copy-done.5
  115.4 0.5 collective-permute-start.11
  115.9 7.6 %put_rows.1 = (bf16[768,1536]{1,0:T(8,128)(2,1)}, bf16[768,3072]{1,0:T(8,128)(2,1)}, bf16[768,1536]{1,0:T(8,128)(2,1)}) custom-call(bf16[192,6144]{1,0:T(8,128)(2,1)} %pad_maximum_fusion.refs_0_, bf16[48,6144]{1,0:T(8,128)(2,1)} %copy-done.15, bf16[48,6144]{1,0:T(8,128)(2,1)} %copy-done.12, bf16[48,6144]{1,0:T(8,128)(2,1)} %copy-done.11, ...), custom_call_target="tpu_custom_call" | custom-call | bytes 18874368 | tf_op jit(solution)/shard_map/put_rows/pallas_call | solution.py:248
  123.6 2.5 %collective-permute-done.11.got_ref = bf16[256,768]{1,0:T(8,128)(2,1)S(1)} collective-permute-done((bf16[256,768]{1,0:T(8,128)(2,1)S(1)}, bf16[256,768]{1,0:T(8,128)(2,1)S(1)}, u32[]{:S(2)}, u32[]{:S(2)}) %collective-permute-start.11) | collective-permute-done | bytes 393248 | tf_op jit(solution)/shard_map/ppermute | solution.py:428
  126.0 1.5 weave_steps.1.tok_ref
  127.5 0.1 collective-permute-start.12
  127.6 2.3 %collective-permute-done.12.tok_ref = bf16[512,768]{1,0:T(8,128)(2,1)S(1)} collective-permute-done((bf16[512,768]{1,0:T(8,128)(2,1)S(1)}, bf16[512,768]{1,0:T(8,128)(2,1)S(1)}, u32[]{:S(2)}, u32[]{:S(2)}) %collective-permute-start.12) | collective-permute-done | bytes 786464 | tf_op jit(solution)/shard_map/ppermute | solution.py:446
  129.9 7.8 %layer.3 = bf16[512,768]{1,0:T(8,128)(2,1)S(1)} custom-call(bf16[512,768]{1,0:T(8,128)(2,1)S(1)} %collective-permute-done.12.tok_ref, bf16[768,1536]{1,0:T(8,128)(2,1)S(1)} %copy-done.1, bf16[768,3072]{1,0:T(8,128)(2,1)S(1)} %copy-done, bf16[768,1536]{1,0:T(8,128)(2,1)S(1)} %copy-done.2), custom_call_target="tpu_custom_call" | custom-call | flops 4831838208 | bytes 11796480 | tf_op jit(solution)/shard_map/layer/pallas_call | solution.py:285
  137.6 0.2 collective-permute-start.13
  137.8 8.0 %layer.2.sum_ref = f32[512,768]{1,0:T(8,128)S(1)} custom-call(bf16[512,768]{1,0:T(8,128)(2,1)S(1)} %weave_steps.1.tok_ref, bf16[768,1536]{1,0:T(8,128)(2,1)S(1)} %copy-done.1, bf16[768,3072]{1,0:T(8,128)(2,1)S(1)} %copy-done, bf16[768,1536]{1,0:T(8,128)(2,1)S(1)} %copy-done.2), custom_call_target="tpu_custom_call" | custom-call | flops 4831838208 | bytes 11796480 | tf_op jit(solution)/shard_map/layer/pallas_call | solution.py:285
  145.9 1.8 %finish.1 = bf16[512,768]{1,0:T(8,128)(2,1)} custom-call(bf16[512,768]{1,0:T(8,128)(2,1)S(1)} %weave_steps.1.tok_ref, f32[512,768]{1,0:T(8,128)S(1)} %layer.2.sum_ref, bf16[512,768]{1,0:T(8,128)(2,1)S(1)} %collective-permute-done.13.got_ref, s32[1,768]{1,0:T(1,128)S(1)} %compare_select_fusion.6.order_ref), custom_call_target="tpu_custom_call" | custom-call | flops 603979776 | bytes 3932160 | tf_op jit(solution)/shard_map/finish/pallas_call | solution.py:314
  (50 shorter events, 0.3 us)
Async XLA Ops:
  0.0 8.4 %copy-start.18 = (s32[512]{0:T(512)S(1)}, s32[512]{0:T(512)}, u32[]{:S(2)}) copy-start(s32[512]{0:T(512)} %param.11) | copy-start | bytes 6148
  0.0 8.5 %copy-start.19 = (s32[512]{0:T(512)S(1)}, s32[512]{0:T(512)}, u32[]{:S(2)}) copy-start(s32[512]{0:T(512)} %param.10) | copy-start | bytes 6148
  0.8 7.7 %copy-start.4 = (bf16[8,768]{1,0:T(8,128)(2,1)S(1)}, bf16[8,768]{1,0:T(8,128)(2,1)}, u32[]{:S(2)}) copy-start(bf16[8,768]{1,0:T(8,128)(2,1)} %time_ref.1) | copy-start | bytes 36868
  3.9 41.7 %copy-start.3 = (bf16[512,768]{1,0:T(8,128)(2,1)S(1)}, bf16[512,768]{1,0:T(8,128)(2,1)}, u32[]{:S(2)}) copy-start(bf16[512,768]{1,0:T(8,128)(2,1)} %feat_ref.1) | copy-start | bytes 2359300
  4.8 18.6 %collective-permute-start = (bf16[48,6144]{1,0:T(8,128)(2,1)}, bf16[48,6144]{1,0:T(8,128)(2,1)S(1)}, u32[]{:S(2)}, u32[]{:S(2)}) collective-permute-start(bf16[48,6144]{1,0:T(8,128)(2,1)} %pad_maximum_fusion.1), channel_id=1, source_target_pairs={{0,4},{4,8},{8,12},{12,0},{1,5},{5,9},{9,13},{13,1},{2,6},{6,10},{... | collective-permute-start | bytes 1769480 | tf_op jit(solution)/shard_map/ppermute | solution.py:334
  23.4 29.9 %copy-start.15 = (bf16[48,6144]{1,0:T(8,128)(2,1)}, bf16[48,6144]{1,0:T(8,128)(2,1)S(1)}, u32[]{:S(2)}) copy-start(bf16[48,6144]{1,0:T(8,128)(2,1)S(1)} %collective-permute-done.refs_1_) | copy-start | bytes 1769476
  23.4 14.5 %collective-permute-start.4 = (bf16[48,6144]{1,0:T(8,128)(2,1)S(1)}, bf16[48,6144]{1,0:T(8,128)(2,1)S(1)}, u32[]{:S(2)}, u32[]{:S(2)}) collective-permute-start(bf16[48,6144]{1,0:T(8,128)(2,1)S(1)} %collective-permute-done.refs_1_), channel_id=1, source_target_pairs={{0,16},{16,0},{1,17},{17,1},{2,18},{18,2},{3,19},{19,3},{4,20},{20... | collective-permute-start | bytes 1769480 | tf_op jit(solution)/shard_map/ppermute | solution.py:340
  24.9 14.3 %collective-permute-start.3 = (bf16[48,6144]{1,0:T(8,128)(2,1)S(1)}, bf16[48,6144]{1,0:T(8,128)(2,1)S(1)}, u32[]{:S(2)}, u32[]{:S(2)}) collective-permute-start(bf16[48,6144]{1,0:T(8,128)(2,1)S(1)} %collective-permute-done.refs_1_), channel_id=1, source_target_pairs={{0,2},{2,0},{1,3},{3,1},{4,6},{6,4},{5,7},{7,5},{8,10},{10,8},{9,1... | collective-permute-start | bytes 1769480 | tf_op jit(solution)/shard_map/ppermute | solution.py:339
  26.4 26.9 %collective-permute-start.1 = (bf16[48,6144]{1,0:T(8,128)(2,1)}, bf16[48,6144]{1,0:T(8,128)(2,1)}, u32[]{:S(2)}, u32[]{:S(2)}) collective-permute-start(bf16[48,6144]{1,0:T(8,128)(2,1)} %pad_maximum_fusion.1), channel_id=1, source_target_pairs={{0,12},{4,0},{8,4},{12,8},{1,13},{5,1},{9,5},{13,9},{2,14},{6,2},{... | collective-permute-start | bytes 1769480 | tf_op jit(solution)/shard_map/ppermute | solution.py:334
  28.1 25.2 %collective-permute-start.2 = (bf16[48,6144]{1,0:T(8,128)(2,1)S(1)}, bf16[48,6144]{1,0:T(8,128)(2,1)}, u32[]{:S(2)}, u32[]{:S(2)}) collective-permute-start(bf16[48,6144]{1,0:T(8,128)(2,1)S(1)} %collective-permute-done.refs_1_), channel_id=1, source_target_pairs={{0,4},{4,8},{8,12},{12,0},{1,5},{5,9},{9,13},{13,1},{2,6},{6,10},{... | collective-permute-start | bytes 1769480 | tf_op jit(solution)/shard_map/ppermute | solution.py:334
  37.9 10.8 %copy-start.11 = (bf16[48,6144]{1,0:T(8,128)(2,1)}, bf16[48,6144]{1,0:T(8,128)(2,1)S(1)}, u32[]{:S(2)}) copy-start(bf16[48,6144]{1,0:T(8,128)(2,1)S(1)} %collective-permute-done.4.refs_3_) | copy-start | bytes 1769476
  37.9 15.4 %collective-permute-start.6 = (bf16[48,3072]{1,0:T(8,128)(2,1)S(1)}, bf16[48,3072]{1,0:T(8,128)(2,1)S(1)}, u32[]{:S(2)}, u32[]{:S(2)}) collective-permute-start(bf16[48,3072]{1,0:T(8,128)(2,1)S(1)} %slice.17), channel_id=1, source_target_pairs={{0,2},{2,0},{1,3},{3,1},{4,6},{6,4},{5,7},{7,5},{8,10},{10,8},{9,1... | collective-permute-start | bytes 884744 | tf_op jit(solution)/shard_map/ppermute | solution.py:343
  39.2 0.8 copy-start.12
  40.8 12.5 %collective-permute-start.5 = (bf16[48,3072]{1,0:T(8,128)(2,1)}, bf16[48,3072]{1,0:T(8,128)(2,1)S(1)}, u32[]{:S(2)}, u32[]{:S(2)}) collective-permute-start(bf16[48,3072]{1,0:T(8,128)(2,1)} %slice.16), channel_id=1, source_target_pairs={{0,16},{16,0},{1,17},{17,1},{2,18},{18,2},{3,19},{19,3},{4,20},{20... | collective-permute-start | bytes 884744 | tf_op jit(solution)/shard_map/ppermute | solution.py:342
  42.3 11.0 %all-to-all-start = ((s32[8,1,192]{2,1,0:T(1,128)}), s32[8,1,192]{2,1,0:T(1,128)S(1)}, u32[]{:S(2)}, u32[]{:S(2)}) async-start(s32[8,1,192]{2,1,0:T(1,128)} %get-tuple-element.37), calls=%async_computation | async-start | bytes 16384 | tf_op jit(solution)/shard_map/all_to_all | solution.py:418
  53.3 59.2 %all-to-all-start.1 = ((bf16[8,192,768]{2,1,0:T(8,128)(2,1)}), bf16[8,192,768]{2,1,0:T(8,128)(2,1)S(1)}, u32[]{:S(2)}, u32[]{:S(2)}) async-start(bf16[8,192,768]{2,1,0:T(8,128)(2,1)} %place_rows.1), calls=%async_computation.1 | async-start | bytes 4718592 | tf_op jit(solution)/shard_map/all_to_all | solution.py:425
  57.9 3.5 %copy-start.14 = (bf16[192,3,384]{2,0,1:T(8,128)(2,1)S(1)}, bf16[192,3,384]{2,0,1:T(8,128)(2,1)}, u32[]{:S(2)}) copy-start(bf16[192,3,384]{2,0,1:T(8,128)(2,1)} %param.14) | copy-start | bytes 1327108
  57.9 3.5 %copy-start.10 = (bf16[192,2,1536]{2,1,0:T(2,128)(2,1)S(1)}, bf16[192,2,1536]{2,1,0:T(2,128)(2,1)}, u32[]{:S(2)}) copy-start(bf16[192,2,1536]{2,1,0:T(2,128)(2,1)} %param.16) | copy-start | bytes 3538948
  60.2 1.3 copy-start.9
  60.2 28.4 %collective-permute-start.8 = (bf16[96,6144]{1,0:T(8,128)(2,1)S(1)}, bf16[96,6144]{1,0:T(8,128)(2,1)S(1)}, u32[]{:S(2)}, u32[]{:S(2)}) collective-permute-start(bf16[96,6144]{1,0:T(8,128)(2,1)S(1)} %constant_dynamic-update-slice_fusion.refs_6_), channel_id=1, source_target_pairs={{0,16},{16,0},{1,17},{17,1},{2,18},{18,2},{3,19},{19,3},{4,20},{20... | collective-permute-start | bytes 3538952 | tf_op jit(solution)/shard_map/ppermute | solution.py:340
  60.8 29.5 %collective-permute-start.7 = (bf16[96,6144]{1,0:T(8,128)(2,1)S(1)}, bf16[96,6144]{1,0:T(8,128)(2,1)S(1)}, u32[]{:S(2)}, u32[]{:S(2)}) collective-permute-start(bf16[96,6144]{1,0:T(8,128)(2,1)S(1)} %constant_dynamic-update-slice_fusion.refs_6_), channel_id=1, source_target_pairs={{0,2},{2,0},{1,3},{3,1},{4,6},{6,4},{5,7},{7,5},{8,10},{10,8},{9,1... | collective-permute-start | bytes 3538952 | tf_op jit(solution)/shard_map/ppermute | solution.py:339
  61.5 30.4 %copy-start.13 = (bf16[1536,192]{0,1:T(8,128)(2,1)S(1)}, bf16[1536,192]{0,1:T(8,128)(2,1)}, u32[]{:S(2)}) copy-start(bf16[1536,192]{0,1:T(8,128)(2,1)} %param.17) | copy-start | bytes 1769476
  61.6 30.4 %copy-start.17 = (bf16[384,192]{0,1:T(8,128)(2,1)S(1)}, bf16[384,192]{0,1:T(8,128)(2,1)}, u32[]{:S(2)}) copy-start(bf16[384,192]{0,1:T(8,128)(2,1)} %param.15) | copy-start | bytes 442372
  88.6 1.0 copy-start.7
  89.7 15.0 %collective-permute-start.10 = (bf16[96,3072]{1,0:T(8,128)(2,1)S(1)}, bf16[96,3072]{1,0:T(8,128)(2,1)S(1)}, u32[]{:S(2)}, u32[]{:S(2)}) collective-permute-start(bf16[96,3072]{1,0:T(8,128)(2,1)S(1)} %slice.19), channel_id=1, source_target_pairs={{0,2},{2,0},{1,3},{3,1},{4,6},{6,4},{5,7},{7,5},{8,10},{10,8},{9,1... | collective-permute-start | bytes 1769480 | tf_op jit(solution)/shard_map/ppermute | solution.py:343
  90.3 1.0 copy-start.8
  91.4 14.8 %collective-permute-start.9 = (bf16[96,3072]{1,0:T(8,128)(2,1)S(1)}, bf16[96,3072]{1,0:T(8,128)(2,1)}, u32[]{:S(2)}, u32[]{:S(2)}) collective-permute-start(bf16[96,3072]{1,0:T(8,128)(2,1)S(1)} %slice.18), channel_id=1, source_target_pairs={{0,16},{16,0},{1,17},{17,1},{2,18},{18,2},{3,19},{19,3},{4,20},{20... | collective-permute-start | bytes 1769480 | tf_op jit(solution)/shard_map/ppermute | solution.py:342
  104.7 0.8 copy-start.16
  114.6 0.8 copy-start.5
  115.4 10.7 %collective-permute-start.11 = (bf16[256,768]{1,0:T(8,128)(2,1)S(1)}, bf16[256,768]{1,0:T(8,128)(2,1)S(1)}, u32[]{:S(2)}, u32[]{:S(2)}) collective-permute-start(bf16[256,768]{1,0:T(8,128)(2,1)S(1)} %get-tuple-element.46), channel_id=1, source_target_pairs={{0,2},{2,0},{1,3},{3,1},{4,6},{6,4},{5,7},{7,5},{8,10},{10,8},{9,1... | collective-permute-start | bytes 1179656 | tf_op jit(solution)/shard_map/ppermute | solution.py:428
  115.9 10.1 %copy-start.6 = (bf16[256,768]{1,0:T(8,128)(2,1)S(1)}, bf16[256,768]{1,0:T(8,128)(2,1)}, u32[]{:S(2)}) copy-start(bf16[256,768]{1,0:T(8,128)(2,1)} %copy-done.5) | copy-start | bytes 1179652
  126.0 3.8 %copy-start = (bf16[768,3072]{1,0:T(8,128)(2,1)S(1)}, bf16[768,3072]{1,0:T(8,128)(2,1)}, u32[]{:S(2)}) copy-start(bf16[768,3072]{1,0:T(8,128)(2,1)} %get-tuple-element.63.gate_up_ref) | copy-start | bytes 14155780
  126.0 3.8 %copy-start.1 = (bf16[768,1536]{1,0:T(8,128)(2,1)S(1)}, bf16[768,1536]{1,0:T(8,128)(2,1)}, u32[]{:S(2)}) copy-start(bf16[768,1536]{1,0:T(8,128)(2,1)} %get-tuple-element.62.heads_ref) | copy-start | bytes 7077892
  126.0 3.8 %copy-start.2 = (bf16[768,1536]{1,0:T(8,128)(2,1)S(1)}, bf16[768,1536]{1,0:T(8,128)(2,1)}, u32[]{:S(2)}) copy-start(bf16[768,1536]{1,0:T(8,128)(2,1)} %get-tuple-element.64.down_ref) | copy-start | bytes 7077892
  127.5 2.4 %collective-permute-start.12 = (bf16[512,768]{1,0:T(8,128)(2,1)S(1)}, bf16[512,768]{1,0:T(8,128)(2,1)S(1)}, u32[]{:S(2)}, u32[]{:S(2)}) collective-permute-start(bf16[512,768]{1,0:T(8,128)(2,1)S(1)} %weave_steps.1.tok_ref), channel_id=1, source_target_pairs={{0,1},{1,0},{2,3},{3,2},{4,5},{5,4},{6,7},{7,6},{8,9},{9,8},{10,11... | collective-permute-start | bytes 2359304 | tf_op jit(solution)/shard_map/ppermute | solution.py:446
  137.6 8.2 %collective-permute-start.13 = (bf16[512,768]{1,0:T(8,128)(2,1)S(1)}, bf16[512,768]{1,0:T(8,128)(2,1)S(1)}, u32[]{:S(2)}, u32[]{:S(2)}) collective-permute-start(bf16[512,768]{1,0:T(8,128)(2,1)S(1)} %layer.3), channel_id=1, source_target_pairs={{0,1},{1,0},{2,3},{3,2},{4,5},{5,4},{6,7},{7,6},{8,9},{9,8},{10,11... | collective-permute-start | bytes 2359304 | tf_op jit(solution)/shard_map/ppermute | solution.py:448
